TPU v7x, 32 devices: a whole 2x2x4 slice. The times are simulated.
32 devices in a mesh: stn: 16 (over z, x, core), tm: 2 (over y).
Axes of the slice: x: 2, y: 2, z: 4, core: 2. Of those that a mesh axis runs over, the one named last changes fastest.
Arguments:
- voltage: bfloat16 [128, 64, 2, 4096], P('stn', 'tm'), may hold values from -6 to 6
- fir_taps: float32 [16, 4096], replicated, may hold values from -1.5 to 1.5
Outputs:
- visibilities: float32 [2, 128, 32, 2048], P(None, 'stn', None, 'tm')
All inputs are finite; a program needn't handle non-finite values.
Results may differ from a plain program's by a relative error of at most 0.0014.
Values may be sent and summed in bfloat16 or wider, within the bound.
No kernel may reach another device: no remote copies, remote signals or barrier semaphores. Data moves between devices by JAX's collectives and lax.ppermute only.
A program may use at most 192 MiB of HBM per device.

v0:
```python
import math

import jax
import jax.numpy as jnp
from jax import lax
from jax.sharding import PartitionSpec as P

NCH = 4096
ROOT = 64
CHANS = 2048
VISITS = 4


def passed_along(block, axis, distance):
    devices = range(lax.axis_size(axis))
    route = [((i - distance) % len(devices), i) for i in devices]
    return lax.ppermute(block, axis, route)


def passed_along_2(shard, axis, by):
    peers = lax.axis_size(axis)
    pairs = [(i, i + by) for i in range(peers) if 0 <= i + by < peers]
    return lax.ppermute(shard, axis, pairs)


def tables(size_a, size_b, modulus, factor):
    left_index = lax.iota(jnp.int32, size_a)[:, None]
    right_index = lax.iota(jnp.int32, size_b)[None, :]
    angles = (left_index * right_index % modulus).astype(jnp.float32) * (2.0 * math.pi / modulus)
    return (jnp.cos(angles) * factor, jnp.sin(angles) * factor)


def real_form(cosine, sine_part):
    from_real = jnp.stack([cosine, -sine_part], axis=1)
    from_imag = jnp.stack([sine_part, cosine], axis=1)
    return jnp.stack([from_real, from_imag], axis=0)


def channelise(voltage, history, fir_taps):
    count_frames = voltage.shape[1]
    signals = voltage.shape[0]
    width_all = 2 * voltage.shape[3]
    extended = jnp.concatenate([history, voltage], 1)
    extended = extended.reshape(signals, extended.shape[1], width_all).astype(jnp.float32)
    kernel = jnp.tile(fir_taps, (1, 2))[:, None, :]
    filtered = lax.conv_general_dilated(
        extended,
        kernel,
        (1,),
        "VALID",
        dimension_numbers=("NHC", "HIO", "NHC"),
        feature_group_count=width_all,
        precision=lax.Precision.HIGHEST,
    )
    grid_form = filtered.reshape(signals, count_frames, 2, ROOT, ROOT)
    cos_one, sin_one = tables(ROOT, ROOT, ROOT, 1.0)
    section_one = jnp.einsum(
        "sfrab,rapk->sfbpk", grid_form, real_form(cos_one, sin_one), precision=lax.Precision.HIGHEST
    )
    cos_turn, sin_turn = tables(ROOT, ROOT, NCH, 1.0)
    real_part = section_one[:, :, :, 0]
    imag_part = section_one[:, :, :, 1]
    turned = jnp.stack(
        [real_part * cos_turn + imag_part * sin_turn, imag_part * cos_turn - real_part * sin_turn],
        3,
    )
    keep_count = CHANS // ROOT
    cos_two, sin_two = tables(ROOT, keep_count, ROOT, 1.0 / math.sqrt(NCH))
    spectrum = jnp.einsum(
        "sfbpk,pbqj->sfqjk", turned, real_form(cos_two, sin_two), precision=lax.Precision.HIGHEST
    )
    return spectrum.reshape(signals, count_frames, 2, CHANS).astype(jnp.bfloat16)


def correlate(own_block, other_block):
    products = jnp.einsum(
        "sfrc,tfqc->rsqtc", own_block, other_block, preferred_element_type=jnp.float32
    )
    real_part = products[0, :, 0] + products[1, :, 1]
    imag_part = products[1, :, 0] - products[0, :, 1]
    return jnp.stack([real_part, imag_part], 0)


def partner_blocks(local_block):
    blocks = [local_block]
    current = local_block
    for visit_index in range(1, VISITS):
        current = passed_along(current, "stn", 1)
        blocks.append(current)
    return blocks


def local(voltage, fir_taps):
    frames_here = voltage.shape[1]
    tail_frames = voltage[:, frames_here - (fir_taps.shape[0] - 1) :]
    history = passed_along_2(tail_frames, "tm", 1)
    spectrum = channelise(voltage, history, fir_taps)
    local_block = lax.all_to_all(spectrum, "tm", split_axis=3, concat_axis=1, tiled=True)
    blocks = partner_blocks(local_block)
    partial_value = jnp.concatenate(
        [correlate(local_block, visiting_block) for visiting_block in blocks], 2
    )
    return partial_value / float(lax.axis_size("tm") * frames_here)


def solution(mesh):
    return jax.shard_map(
        local,
        mesh=mesh,
        in_specs=(P("stn", "tm", None, None), P()),
        out_specs=P(None, "stn", None, "tm"),
        check_vma=False,
    )
```

profile of v0, /device:TPU:1, one launch (start us, length us, event | category | flops | bytes accessed | tf_op | source)
XLA Modules:
  0.0 472.2 jit_solution(12561633343237202046)
XLA Ops:
  0.0 5.2 %slice.57 = bf16[8,15,2,4096]{3,2,1,0:T(2,128)(2,1)} slice(bf16[8,32,2,4096]{3,2,1,0:T(2,128)(2,1)} %param.2), slice={[0:8], [17:32], [0:2], [0:4096]} | slice | bytes 3932160 | tf_op jit(solution)/shard_map/slice | solution.py:95
  5.2 4.1 collective-permute-start
  9.3 1.2 tile.8
  10.5 0.8 tile.9
  11.3 0.1 fusion.44
  11.4 0.1 fusion.43
  11.6 0.1 sine_multiply_fusion
  11.7 0.1 fusion.38
  11.8 0.1 fusion.36
  12.0 39.0 %collective-permute-done = bf16[8,15,2,4096]{3,2,1,0:T(2,128)(2,1)S(1)} collective-permute-done((bf16[8,15,2,4096]{3,2,1,0:T(2,128)(2,1)}, bf16[8,15,2,4096]{3,2,1,0:T(2,128)(2,1)S(1)}, u32[]{:S(2)}, u32[]{:S(2)}) %collective-permute-start) | collective-permute-done | bytes 1966112 | tf_op jit(solution)/shard_map/ppermute | solution.py:23
  51.0 18.0 %pad_maximum_fusion = bf16[8,47,2,4096]{3,2,1,0:T(2,128)(2,1)S(1)} fusion(bf16[8,32,2,4096]{3,2,1,0:T(2,128)(2,1)} %param.2, bf16[8,15,2,4096]{3,2,1,0:T(2,128)(2,1)S(1)} %collective-permute-done), kind=kLoop, calls=%fused_computation.14 | loop fusion | flops 3080192 | bytes 12320768 | tf_op jit(solution)/shard_map/concatenate | solution.py:43
  69.0 7.0 %copy.49 = bf16[8,47,2,4096]{3,0,2,1:T(8,128)(2,1)S(1)} copy(bf16[8,47,2,4096]{3,2,1,0:T(2,128)(2,1)S(1)} %pad_maximum_fusion) | data formatting | bytes 12320768 | tf_op jit(solution)/shard_map/concatenate | solution.py:43
  76.0 10.3 %fusion.47 = f32[8,32,8192]{2,0,1:T(8,128)} fusion(bf16[8,47,8192]{2,0,1:T(8,128)(2,1)S(1)} %bitcast.100, f32[16,1,8192]{2,1,0:T(1,128)S(1)} %tile.9), kind=kOutput, calls=%fused_computation.80 | convolution fusion | flops 402653184 | bytes 15073280 | tf_op jit(solution)/shard_map/conv_general_dilated | solution.py:46
  86.4 14.2 %reshape.351 = f32[8,32,2,64,64]{4,3,2,0,1:T(8,128)} reshape(f32[8,32,8192]{2,0,1:T(8,128)} %fusion.47) | data formatting | bytes 16777216 | tf_op jit(solution)/shard_map/reshape | solution.py:55
  100.5 33.6 %fusion.5 = f32[8,32,64,2,64]{4,2,3,1,0:T(8,128)} fusion(f32[1,64,2,64]{3,1,0,2:T(8,128)S(1)} %get-tuple-element.16, f32[1,64,2,64]{3,1,0,2:T(8,128)S(1)} %get-tuple-element.15, f32[8,32,2,64,64]{4,3,2,0,1:T(8,128)} %reshape.351), kind=kOutput, calls=%fused_computation.10 | convolution fusion | flops 3221241856 | bytes 16842752 | tf_op jit(solution)/shard_map/sfrab,rapk->sfbpk/dot_general | solution.py:57
  134.1 7.2 %multiply_add_fusion = (f32[8,32,64,1,64]{4,2,3,1,0:T(8,128)S(1)}, f32[8,32,64,1,64]{4,2,3,1,0:T(8,128)S(1)}) fusion(f32[8,32,64,2,64]{4,2,3,1,0:T(8,128)} %fusion.5, f32[64,64]{1,0:T(8,128)S(1)} %get-tuple-element.21, f32[64,64]{1,0:T(8,128)S(1)} %get-tuple-element.22), kind=kLoop, calls=%fused_computation.13 | loop fusion | flops 6291456 | bytes 16809984 | tf_op jit(solution)/shard_map/add | solution.py:64
  141.3 12.6 %fusion.8 = bf16[8,32,2,32,64]{4,3,1,0,2:T(8,128)(2,1)} fusion(f32[8,32,64,1,64]{4,2,3,1,0:T(8,128)S(1)} %get-tuple-element.6, f32[8,32,64,1,64]{4,2,3,1,0:T(8,128)S(1)} %get-tuple-element.5, f32[1,64,2,32]{1,3,0,2:T(8,128)S(1)} %get-tuple-element.18, f32[1,64,2,32]{1,3,0,2:T(8,128)S(1)} %get-tuple-element.17), kind=kOutput, calls=%fused_computation.15 | convolution fusion | flops 1613766656 | bytes 10518528 | tf_op jit(solution)/shard_map/sfbpk,pbqj->sfqjk/dot_general | solution.py:69
  154.0 22.4 %copy.86 = bf16[8,32,2,32,64]{1,2,0,4,3:T(2,128)(2,1)} copy(bf16[8,32,2,32,64]{4,3,1,0,2:T(8,128)(2,1)} %fusion.8) | data formatting | bytes 4194304 | tf_op jit(solution)/shard_map/convert_element_type | solution.py:72
  176.3 10.2 %reshape.366 = bf16[2,2,262144]{2,1,0:T(2,128)(2,1)S(1)} reshape(bf16[2048,8,2,32]{3,2,1,0:T(2,128)(2,1)} %bitcast.95) | data formatting | bytes 4194304
  186.5 27.6 %all_to_all.18 = bf16[2,2,262144]{2,1,0:T(2,128)(2,1)} all-to-all(bf16[2,2,262144]{2,1,0:T(2,128)(2,1)S(1)} %reshape.366), channel_id=1, replica_groups=mesh['stn'=16,'tm'=2] {'tm'}, dimensions={0} | all-to-all | bytes 4194304 | tf_op jit(solution)/shard_map/all_to_all | solution.py:98
  214.2 7.6 %reshape.367 = bf16[2048,8,2,32]{3,2,1,0:T(2,128)(2,1)} reshape(bf16[2,2,262144]{2,1,0:T(2,128)(2,1)} %all_to_all.18) | data formatting | bytes 4194304
  221.8 17.8 %copy.54 = bf16[8,2,32,2,1024]{4,2,1,3,0:T(8,128)(2,1)S(1)} copy(bf16[8,2,32,2,1024]{2,3,0,4,1:T(2,128)(2,1)} %bitcast.96) | data formatting | bytes 4194304 | tf_op jit(solution)/shard_map/all_to_all | solution.py:98
  239.6 3.3 collective-permute-start.1
  242.9 23.0 %collective-permute-done.1 = bf16[8,64,2,1024]{3,1,2,0:T(8,128)(2,1)} collective-permute-done((bf16[8,64,2,1024]{3,1,2,0:T(8,128)(2,1)S(1)}, bf16[8,64,2,1024]{3,1,2,0:T(8,128)(2,1)}, u32[]{:S(2)}, u32[]{:S(2)}) %collective-permute-start.1) | collective-permute-done | bytes 2097184 | tf_op jit(solution)/shard_map/ppermute | solution.py:17
  265.9 2.6 collective-permute-start.2
  268.5 5.1 %copy.77 = bf16[8,64,2,1024,1]{1,0,2,4,3:T(8,128)(2,1)} copy(bf16[8,64,2,1024,1]{3,1,2,0,4:T(8,128)(2,1)S(1)} %bitcast.98) | data formatting | bytes 4194304 | tf_op jit(solution)/shard_map/all_to_all | solution.py:98
  273.5 4.9 %copy.76 = bf16[8,64,2,1024,1]{1,0,4,2,3:T(8,128)(2,1)} copy(bf16[8,64,2,1024,1]{3,1,2,0,4:T(8,128)(2,1)S(1)} %bitcast.99) | data formatting | bytes 4194304 | tf_op jit(solution)/shard_map/all_to_all | solution.py:98
  278.4 27.7 %convolution_bitcast_fusion.3 = f32[2,8,2,8,1024]{3,1,0,2,4:T(8,128)} fusion(bf16[8,64,2,1024,1]{1,0,4,2,3:T(8,128)(2,1)} %copy.76, bf16[8,64,2,1024,1]{1,0,2,4,3:T(8,128)(2,1)} %copy.77), kind=kOutput, calls=%fused_computation.9 | convolution fusion | flops 33554432 | bytes 5242880 | tf_op jit(solution)/shard_map/sfrc,tfqc->rsqtc/dot_general | solution.py:76
  306.2 10.0 %fusion.16 = (f32[1,8,8,1024]{2,1,3,0:T(8,128)}, f32[1,8,8,1024]{2,1,3,0:T(8,128)}) fusion(f32[2,8,2,8,1024]{3,1,0,2,4:T(8,128)} %convolution_bitcast_fusion.3), kind=kLoop, calls=%fused_computation.31 | loop fusion | flops 131072 | bytes 1572864 | tf_op jit(solution)/shard_map/add | solution.py:79
  316.2 2.8 copy.57
  319.0 2.8 copy.58
  321.8 6.6 %copy.78 = bf16[8,64,2,1024,1]{1,0,4,2,3:T(8,128)(2,1)} copy(bf16[8,64,2,1024,1]{3,1,2,0,4:T(8,128)(2,1)} %bitcast.29) | data formatting | bytes 4194304 | tf_op jit(solution)/shard_map/ppermute | solution.py:17
  328.4 0.0 collective-permute-done.2
  328.4 0.0 collective-permute-start.3
  328.4 27.7 %convolution_bitcast_fusion.2 = f32[2,8,2,8,1024]{3,1,0,2,4:T(8,128)} fusion(bf16[8,64,2,1024,1]{1,0,4,2,3:T(8,128)(2,1)} %copy.78, bf16[8,64,2,1024,1]{1,0,2,4,3:T(8,128)(2,1)} %copy.77), kind=kOutput, calls=%fused_computation.8 | convolution fusion | flops 33554432 | bytes 5242880 | tf_op jit(solution)/shard_map/sfrc,tfqc->rsqtc/dot_general | solution.py:76
  356.1 10.0 %fusion.14 = (f32[1,8,8,1024]{2,1,3,0:T(8,128)}, f32[1,8,8,1024]{2,1,3,0:T(8,128)}) fusion(f32[2,8,2,8,1024]{3,1,0,2,4:T(8,128)} %convolution_bitcast_fusion.2), kind=kLoop, calls=%fused_computation.27 | loop fusion | flops 131072 | bytes 1572864 | tf_op jit(solution)/shard_map/add | solution.py:79
  366.1 2.9 copy.61
  369.1 2.8 copy.62
  371.9 6.2 %copy.80 = bf16[8,64,2,1024,1]{1,0,4,2,3:T(8,128)(2,1)} copy(bf16[8,64,2,1024,1]{3,1,2,0,4:T(8,128)(2,1)} %bitcast.34) | data formatting | bytes 4194304 | tf_op jit(solution)/shard_map/ppermute | solution.py:17
  378.1 27.7 %convolution_bitcast_fusion.1 = f32[2,8,2,8,1024]{3,1,0,2,4:T(8,128)} fusion(bf16[8,64,2,1024,1]{1,0,4,2,3:T(8,128)(2,1)} %copy.80, bf16[8,64,2,1024,1]{1,0,2,4,3:T(8,128)(2,1)} %copy.77), kind=kOutput, calls=%fused_computation.7 | convolution fusion | flops 33554432 | bytes 5242880 | tf_op jit(solution)/shard_map/sfrc,tfqc->rsqtc/dot_general | solution.py:76
  405.8 10.0 %fusion.12 = (f32[1,8,8,1024]{2,1,3,0:T(8,128)}, f32[1,8,8,1024]{2,1,3,0:T(8,128)}) fusion(f32[2,8,2,8,1024]{3,1,0,2,4:T(8,128)} %convolution_bitcast_fusion.1), kind=kLoop, calls=%fused_computation.23 | loop fusion | flops 131072 | bytes 1572864 | tf_op jit(solution)/shard_map/add | solution.py:79
  415.8 2.8 copy.65
  418.6 3.5 copy.66
  422.1 0.0 collective-permute-done.3
  422.1 5.1 %copy.82 = bf16[8,64,2,1024,1]{1,0,4,2,3:T(8,128)(2,1)} copy(bf16[8,64,2,1024,1]{3,1,2,0,4:T(8,128)(2,1)S(1)} %bitcast.101) | data formatting | bytes 4194304 | tf_op jit(solution)/shard_map/ppermute | solution.py:17
  427.2 27.7 %convolution_bitcast_fusion = f32[2,8,2,8,1024]{3,1,0,2,4:T(8,128)} fusion(bf16[8,64,2,1024,1]{1,0,4,2,3:T(8,128)(2,1)} %copy.82, bf16[8,64,2,1024,1]{1,0,2,4,3:T(8,128)(2,1)} %copy.77), kind=kOutput, calls=%fused_computation.6 | convolution fusion | flops 33554432 | bytes 5242880 | tf_op jit(solution)/shard_map/sfrc,tfqc->rsqtc/dot_general | solution.py:76
  454.9 10.0 %fusion.10 = (f32[1,8,8,1024]{2,1,3,0:T(8,128)}, f32[1,8,8,1024]{2,1,3,0:T(8,128)}) fusion(f32[2,8,2,8,1024]{3,1,0,2,4:T(8,128)} %convolution_bitcast_fusion), kind=kLoop, calls=%fused_computation.19 | loop fusion | flops 131072 | bytes 1572864 | tf_op jit(solution)/shard_map/add | solution.py:79
  464.8 0.0 copy-start
  464.8 2.8 copy.69
  467.7 2.8 copy.70
  470.5 0.0 copy-done
  470.5 1.5 maximum_multiply_fusion
  (2 shorter events, 0.0 us)
Async XLA Ops:
  5.2 45.8 %collective-permute-start = (bf16[8,15,2,4096]{3,2,1,0:T(2,128)(2,1)}, bf16[8,15,2,4096]{3,2,1,0:T(2,128)(2,1)S(1)}, u32[]{:S(2)}, u32[]{:S(2)}) collective-permute-start(bf16[8,15,2,4096]{3,2,1,0:T(2,128)(2,1)} %slice.57), channel_id=1, source_target_pairs={{0,1},{2,3},{4,5},{6,7},{8,9},{10,11},{12,13},{14,15},{16,17},{18,... | collective-permute-start | bytes 5898248 | tf_op jit(solution)/shard_map/ppermute | solution.py:23
  239.6 26.3 %collective-permute-start.1 = (bf16[8,64,2,1024]{3,1,2,0:T(8,128)(2,1)S(1)}, bf16[8,64,2,1024]{3,1,2,0:T(8,128)(2,1)}, u32[]{:S(2)}, u32[]{:S(2)}) collective-permute-start(bf16[8,64,2,1024]{3,1,2,0:T(8,128)(2,1)S(1)} %bitcast.97), channel_id=1, source_target_pairs={{30,0},{0,2},{2,4},{4,6},{6,8},{8,10},{10,12},{12,14},{14,16},{16,... | collective-permute-start | bytes 6291464 | tf_op jit(solution)/shard_map/ppermute | solution.py:17
  265.9 62.5 %collective-permute-start.2 = (bf16[8,64,2,1024]{3,1,2,0:T(8,128)(2,1)}, bf16[8,64,2,1024]{3,1,2,0:T(8,128)(2,1)}, u32[]{:S(2)}, u32[]{:S(2)}) collective-permute-start(bf16[8,64,2,1024]{3,1,2,0:T(8,128)(2,1)} %collective-permute-done.1), channel_id=1, source_target_pairs={{30,0},{0,2},{2,4},{4,6},{6,8},{8,10},{10,12},{12,14},{14,16},{16,... | collective-permute-start | bytes 6291464 | tf_op jit(solution)/shard_map/ppermute | solution.py:17
  328.4 93.7 %collective-permute-start.3 = (bf16[8,64,2,1024]{3,1,2,0:T(8,128)(2,1)}, bf16[8,64,2,1024]{3,1,2,0:T(8,128)(2,1)S(1)}, u32[]{:S(2)}, u32[]{:S(2)}) collective-permute-start(bf16[8,64,2,1024]{3,1,2,0:T(8,128)(2,1)} %collective-permute-done.2), channel_id=1, source_target_pairs={{30,0},{0,2},{2,4},{4,6},{6,8},{8,10},{10,12},{12,14},{14,16},{16,... | collective-permute-start | bytes 6291464 | tf_op jit(solution)/shard_map/ppermute | solution.py:17
  464.8 5.6 %copy-start = (f32[1,8,8,1024]{3,2,1,0:T(8,128)S(1)}, f32[1,8,8,1024]{3,2,1,0:T(8,128)}, u32[]{:S(2)}) copy-start(f32[1,8,8,1024]{3,2,1,0:T(8,128)} %copy.66) | copy-start | bytes 786436
where the time goes:
time: 479 us; the launch traced here: 472 us
  matrix products  167 us (35%)
  local copies, waits for them, and re-layouts  137 us (29%)
  other arithmetic  67.4 us (14%)
  waiting for transfers between devices  61.9 us (13%)
  blocking collectives  27.6 us (6%)
  starting transfers between devices  10 us (2%)
    dot_general x4, matrix products, correlate(): jnp.einsum('sfrc,tfqc->rsqtc', own_block, other_block, preferred_element_...  111 us
    add x4, other arithmetic, correlate(): real_part = products[0, :, 0] + products[1, :, 1]  40 us
    ppermute x1, waiting for transfers between devices, passed_along_2(): return lax.ppermute(shard, axis, pairs)  39 us
    dot_general x1, matrix products, channelise(): jnp.einsum('sfrab,rapk->sfbpk', grid_form, real_form(cos_one, sin_one), p...  33.6 us
    all_to_all x3, local copies, waits for them, and re-layouts, local(): lax.all_to_all(spectrum, 'tm', split_axis=3, concat_axis=1, tiled=True)  27.8 us
    all_to_all x1, blocking collectives, local(): lax.all_to_all(spectrum, 'tm', split_axis=3, concat_axis=1, tiled=True)  27.6 us
    ppermute x3, waiting for transfers between devices, passed_along(): return lax.ppermute(block, axis, route)  23 us
    convert_element_type x1, local copies, waits for them, and re-layouts, channelise(): spectrum.reshape(signals, count_frames, 2, CHANS).astype(jnp.bfloat16)  22.4 us
  transfers between devices with their start and end apart: 4, of which 2 were waited for; matrix products, arithmetic and copies ran while one was open for 33% of the time, Pallas kernels for 0%

commit v1 on v0

v1 whole, which is shorter than its diff:
```python
import functools
import math

import jax
import jax.numpy as jnp
import ml_dtypes
import numpy as np
from jax import lax
from jax.experimental import pallas as pl
from jax.experimental.pallas import tpu as pltpu
from jax.sharding import PartitionSpec as P

NCH = 4096
CHANS = 2048
TAPS = 16
VISITS = 4
H = 32
LANES = 128
ROWS = 2 * H
K2 = CHANS // H
GROUP = 4
SUB = 8
BF16 = jnp.bfloat16
F32 = jnp.float32


def split(table):
    high = table.astype(ml_dtypes.bfloat16)
    low = (table - high.astype(np.float64)).astype(ml_dtypes.bfloat16)
    return high, low


def angles(rows, columns, modulus):
    turns = np.outer(rows, columns) % modulus
    return turns.astype(np.float64) * (2.0 * math.pi / modulus)


def stage_one_table():
    theta = angles(np.arange(H), np.arange(H), H)
    cosine, sine = np.cos(theta), np.sin(theta)
    table = np.zeros((2, H, H, 2))
    table[0, :, :, 0], table[0, :, :, 1] = cosine, sine
    table[1, :, :, 0], table[1, :, :, 1] = -sine, cosine
    high, low = split(table.reshape(ROWS, ROWS))
    return np.concatenate([high, high, low], axis=1)


def turn_table():
    theta = angles(np.arange(H), np.arange(LANES), NCH)
    return np.stack([np.cos(theta), np.sin(theta)]).astype(np.float32)


def stage_two_table(groups):
    per_group = K2 // groups
    row = np.arange(per_group)
    inner = per_group // 4
    k2_of_row = 4 * (row % inner) + row // inner
    k2 = (np.arange(groups)[:, None] * per_group + k2_of_row[None]).reshape(-1)
    theta = angles(k2, np.arange(LANES), LANES)
    cosine, sine = np.cos(theta) / math.sqrt(NCH), np.sin(theta) / math.sqrt(NCH)
    slots = per_group // SUB
    shape = (groups, slots, 1, SUB, LANES)
    real = np.concatenate([cosine.reshape(shape), sine.reshape(shape)], -1)
    imag = np.concatenate([-sine.reshape(shape), cosine.reshape(shape)], -1)
    table = np.concatenate([real, imag], 2).reshape(2 * K2, 2 * LANES)
    return split(table)


def halves(value):
    high = value.astype(BF16)
    return high, (value - high.astype(F32)).astype(BF16)


def dot(left, right):
    return lax.dot_general(left, right, (((1,), (0,)), ((), ())), preferred_element_type=F32)


def dot_nt(left, right):
    return lax.dot_general(left, right, (((1,), (1,)), ((), ())), preferred_element_type=F32)


def spectra_kernel(parts, out_frames, place, *refs):
    part_refs, refs = refs[: len(parts)], refs[len(parts) :]
    taps_ref, one_ref, turn_ref, high_ref, low_ref = refs[:5]
    outs, (taps, ext, filtered) = refs[5:-3], refs[-3:]

    @pl.when(pl.program_id(0) == 0)
    def _():
        for h in range(H):
            for half in range(TAPS // SUB):
                tile = taps_ref[pl.ds(half * SUB, SUB), pl.ds(h * LANES, LANES)]
                for r in range(2):
                    taps[pl.ds(half * SUB * ROWS + 2 * h + r, SUB, stride=ROWS), :] = tile

    for number, (frames, ref) in enumerate(zip(parts, part_refs)):
        start = place[3 * number + 1]
        valid = place[3 * number + 2]

        @pl.when(valid == 1)
        def _():
            for f in range(frames):
                ext[start + f] = ref[0, f].astype(F32)

        @pl.when(valid == 0)
        def _():
            for f in range(frames):
                ext[start + f] = jnp.zeros((ROWS, LANES), F32)

    def fir(q, carry):
        rows = pl.ds(pl.multiple_of(q * SUB, SUB), SUB)
        tap = [taps[pl.ds(pl.multiple_of(m * ROWS + q * SUB, SUB), SUB), :] for m in range(TAPS)]
        for f in range(out_frames):
            total = tap[0] * ext[f + 1, rows]
            for m in range(1, TAPS):
                total = total + tap[m] * ext[f + 1 + m, rows]
            filtered[f, rows] = total
        return carry

    lax.fori_loop(0, ROWS // SUB, fir, 0)

    cosine = turn_ref[0]
    sine = turn_ref[1]
    step = 2 * GROUP
    for g in range(out_frames // step):
        block = jnp.concatenate([filtered[g * step + f] for f in range(step)], axis=1)
        high, low = halves(block)
        first = dot(one_ref[...], jnp.concatenate([high, low, high], axis=0))
        turned = []
        for f in range(step):
            real = first[:H, f * LANES : (f + 1) * LANES]
            imag = first[H:, f * LANES : (f + 1) * LANES]
            turned.append(
                jnp.concatenate([real * cosine + imag * sine, imag * cosine - real * sine], axis=1)
            )
        high, low = halves(jnp.concatenate(turned, axis=0))
        spectrum = dot_nt(high_ref[...], high) + dot_nt(low_ref[...], high) + dot_nt(high_ref[...], low)
        spectrum = spectrum.astype(BF16)
        for j in range(2):
            tile = spectrum[:, j * LANES : (j + 1) * LANES]
            at = 0
            for out in outs:
                slots = out.shape[2]
                out[0, 2 * g + j] = tile[at : at + slots * 16].reshape(slots, 16, LANES)
                at += slots * 16


def spectra(parts, out_frames, fir_taps, table, group_sizes):
    signals = parts[0][0].shape[0]
    place = jnp.stack([jnp.asarray(v, jnp.int32) for part in parts for v in part[2:]])
    whole = lambda shape: pl.BlockSpec(shape, lambda s, place: (0,) * len(shape))
    in_specs = [
        pl.BlockSpec(
            (1, part[1], ROWS, LANES), functools.partial(lambda n, s, place: (s, place[3 * n], 0, 0), n)
        )
        for n, part in enumerate(parts)
    ]
    one, turn, (high, low) = stage_one_table(), turn_table(), table
    in_specs += [whole((TAPS, NCH)), whole(one.shape), whole(turn.shape), whole(high.shape), whole(low.shape)]
    groups = out_frames // GROUP
    out_specs = [
        pl.BlockSpec((1, groups, n, 16, LANES), lambda s, place: (s, 0, 0, 0, 0)) for n in group_sizes
    ]
    out_shape = [jax.ShapeDtypeStruct((signals, groups, n, 16, LANES), BF16) for n in group_sizes]
    return pl.pallas_call(
        functools.partial(spectra_body, tuple(p[1] for p in parts), out_frames),
        grid_spec=pltpu.PrefetchScalarGridSpec(
            num_scalar_prefetch=1,
            grid=(signals,),
            in_specs=in_specs,
            out_specs=out_specs,
            scratch_shapes=[
                pltpu.VMEM((TAPS * ROWS, LANES), F32),
                pltpu.VMEM((TAPS + out_frames, ROWS, LANES), F32),
                pltpu.VMEM((out_frames, ROWS, LANES), F32),
            ],
        ),
        out_shape=out_shape,
        compiler_params=pltpu.CompilerParams(vmem_limit_bytes=32 << 20),
        cost_estimate=pl.CostEstimate(
            flops=signals * out_frames * NCH * 8 * 64, bytes_accessed=signals * out_frames * NCH * 8, transcendentals=0
        ),
    )(place, *[part[0] for part in parts], fir_taps, one, turn, high, low)


def spectra_body(parts, out_frames, place, *refs):
    spectra_kernel(parts, out_frames, place, *refs)


def correlate_kernel(jobs, scale, add, place, *refs):
    refs = list(refs)
    raw = refs.pop()
    out = refs.pop()
    before = refs.pop() if add else None
    signals, slots = raw.shape[1], raw.shape[3]
    block = 4
    across = signals // block
    lane = lax.broadcasted_iota(jnp.int32, (SUB, LANES), 1)
    low_half = lane < LANES // 2
    even = lane % (LANES // 2) < LANES // 4
    for number, (own_list, other_list) in enumerate(jobs):
        pairs = [(refs[a], refs[b]) for a, b in zip(own_list, other_list)]

        def tile(index, carry):
            slot = index % slots
            rest = index // slots
            first = rest % across * block
            second = rest // across * block
            totals = tuple(jnp.zeros((SUB, LANES), F32) for _ in range(2 * block * block))
            for a_ref, b_ref in pairs:

                def frames(f, totals):
                    a = [a_ref[first + i, f, slot].astype(F32) for i in range(block)]
                    b = [b_ref[second + i, f, slot].astype(F32) for i in range(block)]
                    new = []
                    for i in range(block):
                        ar, ai = a[i][:SUB], a[i][SUB:]
                        for k in range(block):
                            br, bi = b[k][:SUB], b[k][SUB:]
                            at = 2 * (i * block + k)
                            new.append(totals[at] + (ar * br + ai * bi))
                            new.append(totals[at + 1] + (ai * br - ar * bi))
                    return tuple(new)

                totals = lax.fori_loop(0, a_ref.shape[1], frames, totals)
            for i in range(block):
                for k in range(block):
                    at = 2 * (i * block + k)
                    raw[0, first + i, second + k, slot] = totals[at]
                    raw[1, first + i, second + k, slot] = totals[at + 1]
            return carry

        lax.fori_loop(0, slots * across * across, tile, 0)
        visit = place[number]

        def finish(index, carry):
            part = index // signals
            own = index % signals
            for t in range(signals):
                value = [raw[part, own, t, s] for s in range(slots)]
                if slots == 4:
                    pair = []
                    for x, y in ((value[0], value[2]), (value[1], value[3])):
                        pair.append(
                            jnp.where(low_half, x, y)
                            + pltpu.roll(jnp.where(low_half, y, x), LANES // 2, 1)
                        )
                    merged = jnp.where(even, pair[0], pair[1]) + jnp.where(
                        even, pltpu.roll(pair[0], LANES - LANES // 4, 1), pltpu.roll(pair[1], LANES // 4, 1)
                    )
                else:
                    sums = []
                    for x in value:
                        x = x + pltpu.roll(x, LANES // 2, 1)
                        sums.append(x + pltpu.roll(x, LANES // 4, 1))
                    sums = jnp.concatenate(sums, axis=0) if slots > 1 else sums[0]
                    inner = slots * SUB // 4
                    merged = jnp.zeros((inner, LANES), F32)
                    for j in range(4):
                        mine = lane[:inner] // (LANES // 4) == j
                        merged = jnp.where(mine, sums[j * inner : (j + 1) * inner], merged)
                inner = merged.shape[0]
                rows = pl.ds(t, inner, stride=signals)
                merged = merged * scale
                if add:
                    merged = merged + before[part, own, visit, rows, :]
                out[part, own, visit, rows, :] = merged
            return carry

        lax.fori_loop(0, 2 * signals, finish, 0)


def correlate(arrays, jobs, place, scale, before=None):
    signals, _, slots = arrays[0].shape[:3]
    rows = slots * SUB // 4 * signals
    shape = (2, signals, VISITS, rows, LANES)
    operands = list(arrays) + ([] if before is None else [before])
    vmem = pl.BlockSpec(memory_space=pltpu.VMEM)
    work = sum(arrays[a].shape[1] for own, _ in jobs for a in own)
    return pl.pallas_call(
        functools.partial(correlate_body, jobs, scale, before is not None),
        grid_spec=pltpu.PrefetchScalarGridSpec(
            num_scalar_prefetch=1,
            grid=(1,),
            in_specs=[pl.BlockSpec(x.shape, functools.partial(lambda n, i, place: (0,) * n, x.ndim)) for x in operands],
            out_specs=pl.BlockSpec(shape, lambda i, place: (0,) * len(shape)),
            scratch_shapes=[pltpu.VMEM((2, signals, signals, slots, SUB, LANES), F32)],
        ),
        out_shape=jax.ShapeDtypeStruct(shape, F32),
        compiler_params=pltpu.CompilerParams(vmem_limit_bytes=48 << 20),
        input_output_aliases={} if before is None else {len(operands): 0},
        cost_estimate=pl.CostEstimate(
            flops=work * signals * signals * slots * 1024 * 64, bytes_accessed=8 << 20, transcendentals=0
        ),
    )(place, *operands)


def correlate_body(jobs, scale, add, place, *refs):
    correlate_kernel(jobs, scale, add, place, *refs)


def stacked(voltage):
    s, f = voltage.shape[:2]
    return voltage.reshape(s, f, 2, H, LANES).transpose(0, 1, 3, 2, 4).reshape(s, f, ROWS, LANES)


def natural(out, channels):
    parts, s, visits, rows, lanes = out.shape
    i = channels // lanes
    out = out.reshape(parts, s, visits, i, rows // i, lanes)
    return out.transpose(0, 1, 2, 4, 3, 5).reshape(parts, s, visits * (rows // i), channels)


def shifted(block, axis, distance):
    size = lax.axis_size(axis)
    return lax.ppermute(block, axis, [(i, (i + distance) % size) for i in range(size)])


def neighbours(block):
    size = lax.axis_size("stn")
    two = shifted(block, "stn", 2)
    swapped = lax.ppermute(two, "stn", [(i, i ^ 1) for i in range(size)])
    rest = lax.ppermute(block, "stn", [(i, (i + 1 if i % 2 == 0 else i + 3) % size) for i in range(size)])
    return [swapped, two, rest]


def local(voltage, fir_taps):
    groups = lax.axis_size("tm")
    frames = voltage.shape[1]
    volts = stacked(voltage)
    me = lax.axis_index("tm")
    history = lax.ppermute(volts[:, frames - TAPS :], "tm", [(i, i + 1) for i in range(groups - 1)])
    table = stage_two_table(groups)
    slots = K2 // groups // SUB
    first = spectra(
        [(history, TAPS, 0, 0, 1), (volts, TAPS, 0, TAPS, 1)], TAPS, fir_taps, table, [slots * groups]
    )[0]
    later = spectra(
        [(volts, TAPS, 0, 0, 1), (volts, TAPS, 1, TAPS, 1)], TAPS, fir_taps, table, [slots * groups]
    )[0]
    blocks = []
    for piece in (first, later):
        block = lax.all_to_all(piece, "tm", split_axis=2, concat_axis=1, tiled=True)
        blocks.append([block] + neighbours(block))
    even = lax.axis_index("stn") % 2 == 0
    place = jnp.where(even, jnp.array([0, 1, 2, 3]), jnp.array([0, 3, 2, 1])).astype(jnp.int32)
    arrays = [x for blk in blocks for x in blk]
    jobs = [((0, 4), (v, v + 4)) for v in range(VISITS)]
    out = correlate(arrays, jobs, place, 1.0 / (groups * frames))
    return natural(out, CHANS // groups)


def solution(mesh):
    return jax.shard_map(
        local,
        mesh=mesh,
        in_specs=(P("stn", "tm", None, None), P()),
        out_specs=P(None, "stn", None, "tm"),
        check_vma=False,
    )
```

time: 479 us -> 193 us (0.40)
  the two profiles are of different devices: /device:TPU:1 before, /device:TPU:6 now
where the time goes in v1:
time: 193 us
  waiting for transfers between devices  90 us (47%)
  Pallas kernels  72 us (37%)
  starting transfers between devices  15.7 us (8%)
  local copies, waits for them, and re-layouts  14.6 us (8%)
    pallas_call x1, Pallas kernels, correlate(): pl.pallas_call(functools.partial(correlate_body, jobs, scale, before is n...  48.4 us
    ppermute x2, waiting for transfers between devices, shifted(): lax.ppermute(block, axis, [(i, (i + distance) % size) for i in range(size)])  37.1 us
    ppermute x1, waiting for transfers between devices, local(): lax.ppermute(volts[:, frames - TAPS:], 'tm', [(i, i + 1) for i in range(g...  24.2 us
    pallas_call x2, Pallas kernels, spectra(): pl.pallas_call(functools.partial(spectra_body, tuple((p[1] for p in parts...  23.6 us
    ppermute x2, waiting for transfers between devices, neighbours(): lax.ppermute(block, 'stn', [(i, (i + 1 if i % 2 == 0 else i + 3) % size)...  22.1 us
    all_to_all x2, starting transfers between devices, local(): block = lax.all_to_all(piece, 'tm', split_axis=2, concat_axis=1, tiled=True)  10.8 us
    unnamed x30, local copies, waits for them, and re-layouts  7.03 us
    all_to_all x2, waiting for transfers between devices, local(): block = lax.all_to_all(piece, 'tm', split_axis=2, concat_axis=1, tiled=True)  6.63 us
  transfers between devices with their start and end apart: 9, of which 6 were waited for; matrix products, arithmetic and copies ran while one was open for 2% of the time, Pallas kernels for 12%

profile of v1, /device:TPU:6, one launch (start us, length us, event | category | flops | bytes accessed | tf_op | source)
XLA Modules:
  0.0 192.5 jit_solution(16731430940465115004)
XLA Ops:
  0.0 0.0 copy-start
  0.0 3.2 %slice.4 = bf16[8,16,64,128]{3,2,1,0:T(8,128)(2,1)} slice(bf16[8,32,64,128]{3,2,1,0:T(8,128)(2,1)} %bitcast.18), slice={[0:8], [16:32], [0:64], [0:128]} | slice | bytes 4194304 | tf_op jit(solution)/shard_map/slice | solution.py:331
  3.2 1.3 collective-permute-start
  4.5 0.0 copy-done
  4.5 0.0 copy-start.2
  4.5 0.9 copy-done.2
  5.5 0.0 copy-start.4
  5.5 0.8 copy-done.4
  6.3 0.0 copy-start.6
  6.3 0.8 copy-done.6
  7.2 0.0 copy-start.8
  7.2 0.8 copy-done.8
  7.9 0.0 copy-start.10
  7.9 0.8 copy-done.10
  8.7 0.0 copy-start.13
  8.7 0.7 copy-done.13
  9.3 11.8 %shard_map.101 = bf16[8,4,8,16,128]{4,3,2,1,0:T(8,128)(2,1)S(1)} custom-call(s32[6]{0:T(128)S(1)} %copy-done.13, bf16[8,32,64,128]{3,2,1,0:T(8,128)(2,1)S(1)} %bitcast.19, bf16[8,32,64,128]{3,2,1,0:T(8,128)(2,1)S(1)} %bitcast.20, f32[16,4096]{1,0:T(8,128)S(1)} %copy-done.2, bf16[64,192]{1,0:T(8,128)(2,1)S(1)} %copy-done.10, f32[2,32,128]{2,1,0:T(8,128)S(1)} %copy-done.8, ...), custom_call_target="tpu_custom_call" | custom-call | flops 268435456 | bytes 4194304 | tf_op jit(solution)/shard_map/pallas_call | solution.py:164
  21.1 0.0 copy-start.3
  21.2 0.0 copy-start.5
  21.2 0.0 copy-start.7
  21.2 0.0 copy-start.9
  21.2 0.0 copy-start.11
  21.2 0.0 copy-start.12
  21.2 1.3 copy.17
  22.5 7.2 %all-to-all-start.1 = ((bf16[8,4,8,16,128]{4,3,1,0,2:T(8,128)(2,1)}), bf16[8,4,8,16,128]{4,3,1,0,2:T(8,128)(2,1)}, u32[]{:S(2)}, u32[]{:S(2)}) async-start(bf16[8,4,8,16,128]{4,3,1,0,2:T(8,128)(2,1)} %copy.17), calls=%async_computation.1 | async-start | bytes 2097152 | tf_op jit(solution)/shard_map/all_to_all | solution.py:342
  29.7 24.2 %collective-permute-done.refs_0_ = bf16[8,16,64,128]{3,2,1,0:T(8,128)(2,1)S(1)} collective-permute-done((bf16[8,16,64,128]{3,2,1,0:T(8,128)(2,1)}, bf16[8,16,64,128]{3,2,1,0:T(8,128)(2,1)S(1)}, u32[]{:S(2)}, u32[]{:S(2)}) %collective-permute-start) | collective-permute-done | bytes 2097184 | tf_op jit(solution)/shard_map/ppermute | solution.py:331
  53.8 0.0 copy-done.3
  53.9 0.0 copy-done.5
  53.9 0.0 copy-done.7
  53.9 0.0 copy-done.9
  53.9 0.0 copy-done.11
  53.9 0.0 copy-done.12
  53.9 0.0 copy-start.1
  53.9 2.2 %copy-done.1 = bf16[8,32,2,4096]{3,2,1,0:T(2,128)(2,1)S(1)} copy-done((bf16[8,32,2,4096]{3,2,1,0:T(2,128)(2,1)S(1)}, bf16[8,32,2,4096]{3,2,1,0:T(2,128)(2,1)}, u32[]{:S(2)}) %copy-start.1) | copy-done | bytes 4194328
  56.1 11.8 %shard_map.100 = bf16[8,4,8,16,128]{4,3,2,1,0:T(8,128)(2,1)S(1)} custom-call(s32[6]{0:T(128)S(1)} %copy-done.12, bf16[8,16,64,128]{3,2,1,0:T(8,128)(2,1)S(1)} %collective-permute-done.refs_0_, bf16[8,32,64,128]{3,2,1,0:T(8,128)(2,1)S(1)} %bitcast.21, f32[16,4096]{1,0:T(8,128)S(1)} %copy-done.3, bf16[64,192]{1,0:T(8,128)(2,1)S(1)} %copy-done.11, ...), custom_call_target="tpu_custom_call" | custom-call | flops 268435456 | bytes 4194304 | tf_op jit(solution)/shard_map/pallas_call | solution.py:164
  67.9 1.3 copy.15
  69.2 0.0 all-to-all-done.1
  69.2 3.6 %all-to-all-start = ((bf16[8,4,8,16,128]{4,3,1,0,2:T(8,128)(2,1)}), bf16[8,4,8,16,128]{4,3,1,0,2:T(8,128)(2,1)S(1)}, u32[]{:S(2)}, u32[]{:S(2)}) async-start(bf16[8,4,8,16,128]{4,3,1,0,2:T(8,128)(2,1)} %copy.15), calls=%async_computation | async-start | bytes 2097152 | tf_op jit(solution)/shard_map/all_to_all | solution.py:342
  72.7 0.0 copy-start.14
  72.8 1.5 copy.18
  74.3 1.6 collective-permute-start.4
  75.9 6.6 %all-to-all-done = bf16[8,4,8,16,128]{4,3,1,0,2:T(8,128)(2,1)S(1)} async-done(((bf16[8,4,8,16,128]{4,3,1,0,2:T(8,128)(2,1)}), bf16[8,4,8,16,128]{4,3,1,0,2:T(8,128)(2,1)S(1)}, u32[]{:S(2)}, u32[]{:S(2)}) %all-to-all-start) | async-done | bytes 1048608 | tf_op jit(solution)/shard_map/all_to_all | solution.py:342
  82.5 0.3 copy.16
  82.8 1.6 collective-permute-start.1
  84.4 0.0 collective-permute-start.6
  84.4 16.1 %collective-permute-done.4.refs_6_ = bf16[8,8,4,16,128]{4,3,2,1,0:T(8,128)(2,1)} collective-permute-done((bf16[8,8,4,16,128]{4,3,2,1,0:T(8,128)(2,1)S(1)}, bf16[8,8,4,16,128]{4,3,2,1,0:T(8,128)(2,1)}, u32[]{:S(2)}, u32[]{:S(2)}) %collective-permute-start.4) | collective-permute-done | bytes 1048608 | tf_op jit(solution)/shard_map/ppermute | solution.py:315
  100.5 0.0 collective-permute-start.5
  100.5 0.5 collective-permute-start.3
  101.0 20.9 %collective-permute-done.1.refs_2_ = bf16[8,8,4,16,128]{4,3,2,1,0:T(8,128)(2,1)S(1)} collective-permute-done((bf16[8,8,4,16,128]{4,3,2,1,0:T(8,128)(2,1)S(1)}, bf16[8,8,4,16,128]{4,3,2,1,0:T(8,128)(2,1)S(1)}, u32[]{:S(2)}, u32[]{:S(2)}) %collective-permute-start.1) | collective-permute-done | bytes 1048608 | tf_op jit(solution)/shard_map/ppermute | solution.py:315
  121.9 0.0 collective-permute-start.2
  122.0 0.0 copy-done.14
  122.0 10.9 %collective-permute-done.6.refs_7_ = bf16[8,8,4,16,128]{4,3,2,1,0:T(8,128)(2,1)} collective-permute-done((bf16[8,8,4,16,128]{4,3,2,1,0:T(8,128)(2,1)S(1)}, bf16[8,8,4,16,128]{4,3,2,1,0:T(8,128)(2,1)}, u32[]{:S(2)}, u32[]{:S(2)}) %collective-permute-start.6) | collective-permute-done | bytes 1048608 | tf_op jit(solution)/shard_map/ppermute | solution.py:322
  132.9 0.0 collective-permute-done.5.refs_5_
  132.9 11.2 %collective-permute-done.3.refs_3_ = bf16[8,8,4,16,128]{4,3,2,1,0:T(8,128)(2,1)} collective-permute-done((bf16[8,8,4,16,128]{4,3,2,1,0:T(8,128)(2,1)S(1)}, bf16[8,8,4,16,128]{4,3,2,1,0:T(8,128)(2,1)}, u32[]{:S(2)}, u32[]{:S(2)}) %collective-permute-start.3) | collective-permute-done | bytes 1048608 | tf_op jit(solution)/shard_map/ppermute | solution.py:322
  144.1 0.0 collective-permute-done.2.refs_1_
  144.1 48.4 %shard_map.102 = f32[2,8,4,64,128]{4,3,2,1,0:T(8,128)} custom-call(s32[4]{0:T(128)S(1)} %broadcast_select_fusion.place, bf16[8,8,4,16,128]{4,3,2,1,0:T(8,128)(2,1)S(1)} %bitcast.27, bf16[8,8,4,16,128]{4,3,2,1,0:T(8,128)(2,1)} %collective-permute-done.2.refs_1_, bf16[8,8,4,16,128]{4,3,2,1,0:T(8,128)(2,1)S(1)} %collective-permute-done.1.refs_2_, ...), custom_call_target="tpu_custom_call" | custom-call | flops 1073741824 | bytes 8388608 | tf_op jit(solution)/shard_map/pallas_call | solution.py:279
  (1 shorter events, 0.0 us)
Async XLA Ops:
  0.0 4.5 %copy-start = (bf16[8,32,2,4096]{3,2,1,0:T(2,128)(2,1)S(1)}, bf16[8,32,2,4096]{3,2,1,0:T(2,128)(2,1)}, u32[]{:S(2)}) copy-start(bf16[8,32,2,4096]{3,2,1,0:T(2,128)(2,1)} %param.10) | copy-start | bytes 12582916
  3.2 50.6 %collective-permute-start = (bf16[8,16,64,128]{3,2,1,0:T(8,128)(2,1)}, bf16[8,16,64,128]{3,2,1,0:T(8,128)(2,1)S(1)}, u32[]{:S(2)}, u32[]{:S(2)}) collective-permute-start(bf16[8,16,64,128]{3,2,1,0:T(8,128)(2,1)} %slice.4), channel_id=1, source_target_pairs={{0,1},{2,3},{4,5},{6,7},{8,9},{10,11},{12,13},{14,15},{16,17},{18,... | collective-permute-start | bytes 6291464 | tf_op jit(solution)/shard_map/ppermute | solution.py:331
  4.5 1.0 copy-start.2
  5.5 0.8 copy-start.4
  6.3 0.8 copy-start.6
  7.2 0.8 copy-start.8
  7.9 0.8 copy-start.10
  8.7 0.7 copy-start.13
  21.1 32.7 %copy-start.3 = (f32[16,4096]{1,0:T(8,128)S(1)}, f32[16,4096]{1,0:T(8,128)}, u32[]{:S(2)}) copy-start(f32[16,4096]{1,0:T(8,128)} %refs_2_.3) | copy-start | bytes 786436
  21.2 32.7 %copy-start.5 = (bf16[128,256]{1,0:T(8,128)(2,1)S(1)}, bf16[128,256]{1,0:T(8,128)(2,1)}, u32[]{:S(2)}) copy-start(bf16[128,256]{1,0:T(8,128)(2,1)} %constant.39.clone.refs_6_) | copy-start | bytes 196612
  21.2 32.7 %copy-start.7 = (bf16[128,256]{1,0:T(8,128)(2,1)S(1)}, bf16[128,256]{1,0:T(8,128)(2,1)}, u32[]{:S(2)}) copy-start(bf16[128,256]{1,0:T(8,128)(2,1)} %constant.38.clone.refs_5_) | copy-start | bytes 196612
  21.2 32.7 %copy-start.9 = (f32[2,32,128]{2,1,0:T(8,128)S(1)}, f32[2,32,128]{2,1,0:T(8,128)}, u32[]{:S(2)}) copy-start(f32[2,32,128]{2,1,0:T(8,128)} %constant.37.clone.refs_4_) | copy-start | bytes 98308
  21.2 32.7 %copy-start.11 = (bf16[64,192]{1,0:T(8,128)(2,1)S(1)}, bf16[64,192]{1,0:T(8,128)(2,1)}, u32[]{:S(2)}) copy-start(bf16[64,192]{1,0:T(8,128)(2,1)} %constant.36.clone.refs_3_) | copy-start | bytes 73732
  21.2 32.7 %copy-start.12 = (s32[6]{0:T(128)S(1)}, s32[6]{0:T(128)}, u32[]{:S(2)}) copy-start(s32[6]{0:T(128)} %constant.34.clone.1.place) | copy-start | bytes 76
  22.5 46.7 %all-to-all-start.1 = ((bf16[8,4,8,16,128]{4,3,1,0,2:T(8,128)(2,1)}), bf16[8,4,8,16,128]{4,3,1,0,2:T(8,128)(2,1)}, u32[]{:S(2)}, u32[]{:S(2)}) async-start(bf16[8,4,8,16,128]{4,3,1,0,2:T(8,128)(2,1)} %copy.17), calls=%async_computation.1 | async-start | bytes 2097152 | tf_op jit(solution)/shard_map/all_to_all | solution.py:342
  53.9 2.2 %copy-start.1 = (bf16[8,32,2,4096]{3,2,1,0:T(2,128)(2,1)S(1)}, bf16[8,32,2,4096]{3,2,1,0:T(2,128)(2,1)}, u32[]{:S(2)}) copy-start(bf16[8,32,2,4096]{3,2,1,0:T(2,128)(2,1)} %param.10) | copy-start | bytes 12582916
  69.2 13.3 %all-to-all-start = ((bf16[8,4,8,16,128]{4,3,1,0,2:T(8,128)(2,1)}), bf16[8,4,8,16,128]{4,3,1,0,2:T(8,128)(2,1)S(1)}, u32[]{:S(2)}, u32[]{:S(2)}) async-start(bf16[8,4,8,16,128]{4,3,1,0,2:T(8,128)(2,1)} %copy.15), calls=%async_computation | async-start | bytes 2097152 | tf_op jit(solution)/shard_map/all_to_all | solution.py:342
  72.7 49.2 %copy-start.14 = (s32[4]{0:T(128)S(1)}, s32[4]{0:T(128)}, u32[]{:S(2)}) copy-start(s32[4]{0:T(128)} %constant.40.clone) | copy-start | bytes 52
  74.3 26.3 %collective-permute-start.4 = (bf16[8,8,4,16,128]{4,3,2,1,0:T(8,128)(2,1)S(1)}, bf16[8,8,4,16,128]{4,3,2,1,0:T(8,128)(2,1)}, u32[]{:S(2)}, u32[]{:S(2)}) collective-permute-start(bf16[8,8,4,16,128]{4,3,2,1,0:T(8,128)(2,1)S(1)} %bitcast.22), channel_id=1, source_target_pairs={{0,4},{2,6},{4,8},{6,10},{8,12},{10,14},{12,16},{14,18},{16,20},{1... | collective-permute-start | bytes 3145736 | tf_op jit(solution)/shard_map/ppermute | solution.py:315
  82.8 39.2 %collective-permute-start.1 = (bf16[8,8,4,16,128]{4,3,2,1,0:T(8,128)(2,1)S(1)}, bf16[8,8,4,16,128]{4,3,2,1,0:T(8,128)(2,1)S(1)}, u32[]{:S(2)}, u32[]{:S(2)}) collective-permute-start(bf16[8,8,4,16,128]{4,3,2,1,0:T(8,128)(2,1)S(1)} %bitcast.25), channel_id=1, source_target_pairs={{0,4},{2,6},{4,8},{6,10},{8,12},{10,14},{12,16},{14,18},{16,20},{1... | collective-permute-start | bytes 3145736 | tf_op jit(solution)/shard_map/ppermute | solution.py:315
  84.4 48.5 %collective-permute-start.6 = (bf16[8,8,4,16,128]{4,3,2,1,0:T(8,128)(2,1)S(1)}, bf16[8,8,4,16,128]{4,3,2,1,0:T(8,128)(2,1)}, u32[]{:S(2)}, u32[]{:S(2)}) collective-permute-start(bf16[8,8,4,16,128]{4,3,2,1,0:T(8,128)(2,1)S(1)} %bitcast.23), channel_id=1, source_target_pairs={{0,2},{2,8},{4,6},{6,12},{8,10},{10,16},{12,14},{14,20},{16,18},{1... | collective-permute-start | bytes 3145736 | tf_op jit(solution)/shard_map/ppermute | solution.py:322
  100.5 32.4 %collective-permute-start.5 = (bf16[8,8,4,16,128]{4,3,2,1,0:T(8,128)(2,1)}, bf16[8,8,4,16,128]{4,3,2,1,0:T(8,128)(2,1)}, u32[]{:S(2)}, u32[]{:S(2)}) collective-permute-start(bf16[8,8,4,16,128]{4,3,2,1,0:T(8,128)(2,1)} %collective-permute-done.4.refs_6_), channel_id=1, source_target_pairs={{0,2},{2,0},{4,6},{6,4},{8,10},{10,8},{12,14},{14,12},{16,18},{18,... | collective-permute-start | bytes 3145736 | tf_op jit(solution)/shard_map/ppermute | solution.py:321
  100.5 43.6 %collective-permute-start.3 = (bf16[8,8,4,16,128]{4,3,2,1,0:T(8,128)(2,1)S(1)}, bf16[8,8,4,16,128]{4,3,2,1,0:T(8,128)(2,1)}, u32[]{:S(2)}, u32[]{:S(2)}) collective-permute-start(bf16[8,8,4,16,128]{4,3,2,1,0:T(8,128)(2,1)S(1)} %bitcast.26), channel_id=1, source_target_pairs={{0,2},{2,8},{4,6},{6,12},{8,10},{10,16},{12,14},{14,20},{16,18},{1... | collective-permute-start | bytes 3145736 | tf_op jit(solution)/shard_map/ppermute | solution.py:322
  121.9 22.2 %collective-permute-start.2 = (bf16[8,8,4,16,128]{4,3,2,1,0:T(8,128)(2,1)S(1)}, bf16[8,8,4,16,128]{4,3,2,1,0:T(8,128)(2,1)}, u32[]{:S(2)}, u32[]{:S(2)}) collective-permute-start(bf16[8,8,4,16,128]{4,3,2,1,0:T(8,128)(2,1)S(1)} %collective-permute-done.1.refs_2_), channel_id=1, source_target_pairs={{0,2},{2,0},{4,6},{6,4},{8,10},{10,8},{12,14},{14,12},{16,18},{18,... | collective-permute-start | bytes 3145736 | tf_op jit(solution)/shard_map/ppermute | solution.py:321

commit v2 on v1

--- a/solution.py
+++ b/solution.py
@@ -3,7 +3,6 @@
 
 import jax
 import jax.numpy as jnp
-import ml_dtypes
 import numpy as np
 from jax import lax
 from jax.experimental import pallas as pl
@@ -24,12 +23,6 @@
 F32 = jnp.float32
 
 
-def split(table):
-    high = table.astype(ml_dtypes.bfloat16)
-    low = (table - high.astype(np.float64)).astype(ml_dtypes.bfloat16)
-    return high, low
-
-
 def angles(rows, columns, modulus):
     turns = np.outer(rows, columns) % modulus
     return turns.astype(np.float64) * (2.0 * math.pi / modulus)
@@ -41,13 +34,12 @@
     table = np.zeros((2, H, H, 2))
     table[0, :, :, 0], table[0, :, :, 1] = cosine, sine
     table[1, :, :, 0], table[1, :, :, 1] = -sine, cosine
-    high, low = split(table.reshape(ROWS, ROWS))
-    return np.concatenate([high, high, low], axis=1)
+    return np.pad(table.reshape(ROWS, ROWS), ((0, 0), (0, 2 * LANES - ROWS)))
 
 
 def turn_table():
     theta = angles(np.arange(H), np.arange(LANES), NCH)
-    return np.stack([np.cos(theta), np.sin(theta)]).astype(np.float32)
+    return np.concatenate([np.cos(theta), np.sin(theta)], axis=1)
 
 
 def stage_two_table(groups):
@@ -58,12 +50,16 @@
     k2 = (np.arange(groups)[:, None] * per_group + k2_of_row[None]).reshape(-1)
     theta = angles(k2, np.arange(LANES), LANES)
     cosine, sine = np.cos(theta) / math.sqrt(NCH), np.sin(theta) / math.sqrt(NCH)
-    slots = per_group // SUB
-    shape = (groups, slots, 1, SUB, LANES)
+    shape = (groups, per_group // SUB, 1, SUB, LANES)
     real = np.concatenate([cosine.reshape(shape), sine.reshape(shape)], -1)
     imag = np.concatenate([-sine.reshape(shape), cosine.reshape(shape)], -1)
-    table = np.concatenate([real, imag], 2).reshape(2 * K2, 2 * LANES)
-    return split(table)
+    return np.concatenate([real, imag], 2).reshape(2 * K2, 2 * LANES)
+
+
+def tables(groups):
+    two = stage_two_table(groups)
+    rolled = np.roll(two, K2, axis=0)
+    return np.concatenate([stage_one_table(), turn_table(), two, rolled]).astype(np.float32)
 
 
 def halves(value):
@@ -81,8 +77,8 @@
 
 def spectra_kernel(parts, out_frames, place, *refs):
     part_refs, refs = refs[: len(parts)], refs[len(parts) :]
-    taps_ref, one_ref, turn_ref, high_ref, low_ref = refs[:5]
-    outs, (taps, ext, filtered) = refs[5:-3], refs[-3:]
+    taps_ref, table_ref = refs[:2]
+    outs, (taps, one, two, ext, filtered) = refs[2:-5], refs[-5:]
 
     @pl.when(pl.program_id(0) == 0)
     def _():
@@ -91,78 +87,86 @@
                 tile = taps_ref[pl.ds(half * SUB, SUB), pl.ds(h * LANES, LANES)]
                 for r in range(2):
                     taps[pl.ds(half * SUB * ROWS + 2 * h + r, SUB, stride=ROWS), :] = tile
-
-    for number, (frames, ref) in enumerate(zip(parts, part_refs)):
-        start = place[3 * number + 1]
-        valid = place[3 * number + 2]
-
-        @pl.when(valid == 1)
-        def _():
-            for f in range(frames):
-                ext[start + f] = ref[0, f].astype(F32)
-
-        @pl.when(valid == 0)
-        def _():
-            for f in range(frames):
-                ext[start + f] = jnp.zeros((ROWS, LANES), F32)
-
-    def fir(q, carry):
-        rows = pl.ds(pl.multiple_of(q * SUB, SUB), SUB)
-        tap = [taps[pl.ds(pl.multiple_of(m * ROWS + q * SUB, SUB), SUB), :] for m in range(TAPS)]
-        for f in range(out_frames):
-            total = tap[0] * ext[f + 1, rows]
-            for m in range(1, TAPS):
-                total = total + tap[m] * ext[f + 1 + m, rows]
-            filtered[f, rows] = total
-        return carry
-
-    lax.fori_loop(0, ROWS // SUB, fir, 0)
-
-    cosine = turn_ref[0]
-    sine = turn_ref[1]
-    step = 2 * GROUP
-    for g in range(out_frames // step):
-        block = jnp.concatenate([filtered[g * step + f] for f in range(step)], axis=1)
-        high, low = halves(block)
-        first = dot(one_ref[...], jnp.concatenate([high, low, high], axis=0))
-        turned = []
-        for f in range(step):
-            real = first[:H, f * LANES : (f + 1) * LANES]
-            imag = first[H:, f * LANES : (f + 1) * LANES]
-            turned.append(
-                jnp.concatenate([real * cosine + imag * sine, imag * cosine - real * sine], axis=1)
-            )
-        high, low = halves(jnp.concatenate(turned, axis=0))
-        spectrum = dot_nt(high_ref[...], high) + dot_nt(low_ref[...], high) + dot_nt(high_ref[...], low)
-        spectrum = spectrum.astype(BF16)
-        for j in range(2):
-            tile = spectrum[:, j * LANES : (j + 1) * LANES]
-            at = 0
-            for out in outs:
-                slots = out.shape[2]
-                out[0, 2 * g + j] = tile[at : at + slots * 16].reshape(slots, 16, LANES)
-                at += slots * 16
-
-
-def spectra(parts, out_frames, fir_taps, table, group_sizes):
+        high, low = halves(table_ref[:ROWS, :ROWS])
+        one[...] = jnp.concatenate([high, high, low], axis=1)
+        start = pl.multiple_of(ROWS + H + place[1] * 2 * K2, SUB)
+        high, low = halves(table_ref[pl.ds(start, 2 * K2), :])
+        two[0] = high
+        two[1] = low
+
+    def body():
+        for number, (frames, ref) in enumerate(zip(parts, part_refs)):
+            start = place[2 + 3 * number + 1]
+            valid = place[2 + 3 * number + 2]
+
+            @pl.when(valid == 1)
+            def _():
+                for f in range(frames):
+                    ext[start + f] = ref[0, f].astype(F32)
+
+            @pl.when(valid == 0)
+            def _():
+                for f in range(frames):
+                    ext[start + f] = jnp.zeros((ROWS, LANES), F32)
+
+        def fir(q, carry):
+            rows = pl.ds(pl.multiple_of(q * SUB, SUB), SUB)
+            tap = [taps[pl.ds(pl.multiple_of(m * ROWS + q * SUB, SUB), SUB), :] for m in range(TAPS)]
+            for f in range(out_frames):
+                total = tap[0] * ext[f + 1, rows]
+                for m in range(1, TAPS):
+                    total = total + tap[m] * ext[f + 1 + m, rows]
+                filtered[f, rows] = total
+            return carry
+
+        lax.fori_loop(0, ROWS // SUB, fir, 0)
+
+        cosine = table_ref[ROWS : ROWS + H, :LANES]
+        sine = table_ref[ROWS : ROWS + H, LANES:]
+        step = 2 * GROUP
+        for g in range(out_frames // step):
+            block = jnp.concatenate([filtered[g * step + f] for f in range(step)], axis=1)
+            high, low = halves(block)
+            first = dot(one[...], jnp.concatenate([high, low, high], axis=0))
+            turned = []
+            for f in range(step):
+                real = first[:H, f * LANES : (f + 1) * LANES]
+                imag = first[H:, f * LANES : (f + 1) * LANES]
+                turned.append(
+                    jnp.concatenate([real * cosine + imag * sine, imag * cosine - real * sine], axis=1)
+                )
+            high, low = halves(jnp.concatenate(turned, axis=0))
+            spectrum = dot_nt(two[0], high) + dot_nt(two[1], high) + dot_nt(two[0], low)
+            spectrum = spectrum.astype(BF16)
+            for j in range(2):
+                tile = spectrum[:, j * LANES : (j + 1) * LANES]
+                at = 0
+                for out in outs:
+                    slots = out.shape[2]
+                    out[0, 2 * g + j] = tile[at : at + slots * 16].reshape(slots, 16, LANES)
+                    at += slots * 16
+
+    pl.when(place[0] == 1)(body)
+
+
+def spectra(parts, out_frames, fir_taps, groups, group_sizes, run=1, order=0):
     signals = parts[0][0].shape[0]
-    place = jnp.stack([jnp.asarray(v, jnp.int32) for part in parts for v in part[2:]])
+    numbers = [run, order] + [v for part in parts for v in part[2:]]
+    place = jnp.stack([jnp.asarray(v, jnp.int32) for v in numbers])
+    table = tables(groups)
     whole = lambda shape: pl.BlockSpec(shape, lambda s, place: (0,) * len(shape))
     in_specs = [
         pl.BlockSpec(
-            (1, part[1], ROWS, LANES), functools.partial(lambda n, s, place: (s, place[3 * n], 0, 0), n)
+            (1, part[1], ROWS, LANES), functools.partial(lambda n, s, place: (s, place[2 + 3 * n], 0, 0), n)
         )
         for n, part in enumerate(parts)
     ]
-    one, turn, (high, low) = stage_one_table(), turn_table(), table
-    in_specs += [whole((TAPS, NCH)), whole(one.shape), whole(turn.shape), whole(high.shape), whole(low.shape)]
-    groups = out_frames // GROUP
-    out_specs = [
-        pl.BlockSpec((1, groups, n, 16, LANES), lambda s, place: (s, 0, 0, 0, 0)) for n in group_sizes
-    ]
-    out_shape = [jax.ShapeDtypeStruct((signals, groups, n, 16, LANES), BF16) for n in group_sizes]
+    in_specs += [whole((TAPS, NCH)), whole(table.shape)]
+    tiles = out_frames // GROUP
+    out_specs = [pl.BlockSpec((1, tiles, n, 16, LANES), lambda s, place: (s, 0, 0, 0, 0)) for n in group_sizes]
+    out_shape = [jax.ShapeDtypeStruct((signals, tiles, n, 16, LANES), BF16) for n in group_sizes]
     return pl.pallas_call(
-        functools.partial(spectra_body, tuple(p[1] for p in parts), out_frames),
+        functools.partial(spectra_kernel, tuple(p[1] for p in parts), out_frames),
         grid_spec=pltpu.PrefetchScalarGridSpec(
             num_scalar_prefetch=1,
             grid=(signals,),
@@ -170,6 +174,8 @@
             out_specs=out_specs,
             scratch_shapes=[
                 pltpu.VMEM((TAPS * ROWS, LANES), F32),
+                pltpu.VMEM((ROWS, 3 * ROWS), BF16),
+                pltpu.VMEM((2, 2 * K2, 2 * LANES), BF16),
                 pltpu.VMEM((TAPS + out_frames, ROWS, LANES), F32),
                 pltpu.VMEM((out_frames, ROWS, LANES), F32),
             ],
@@ -179,11 +185,7 @@
         cost_estimate=pl.CostEstimate(
             flops=signals * out_frames * NCH * 8 * 64, bytes_accessed=signals * out_frames * NCH * 8, transcendentals=0
         ),
-    )(place, *[part[0] for part in parts], fir_taps, one, turn, high, low)
-
-
-def spectra_body(parts, out_frames, place, *refs):
-    spectra_kernel(parts, out_frames, place, *refs)
+    )(place, *[part[0] for part in parts], fir_taps, table)
 
 
 def correlate_kernel(jobs, scale, add, place, *refs):
@@ -221,7 +223,7 @@
                             new.append(totals[at + 1] + (ai * br - ar * bi))
                     return tuple(new)
 
-                totals = lax.fori_loop(0, a_ref.shape[1], frames, totals)
+                totals = lax.fori_loop(0, a_ref.shape[1], frames, totals, unroll=4)
             for i in range(block):
                 for k in range(block):
                     at = 2 * (i * block + k)
@@ -277,7 +279,7 @@
     vmem = pl.BlockSpec(memory_space=pltpu.VMEM)
     work = sum(arrays[a].shape[1] for own, _ in jobs for a in own)
     return pl.pallas_call(
-        functools.partial(correlate_body, jobs, scale, before is not None),
+        functools.partial(correlate_kernel, jobs, scale, before is not None),
         grid_spec=pltpu.PrefetchScalarGridSpec(
             num_scalar_prefetch=1,
             grid=(1,),
@@ -294,10 +296,6 @@
     )(place, *operands)
 
 
-def correlate_body(jobs, scale, add, place, *refs):
-    correlate_kernel(jobs, scale, add, place, *refs)
-
-
 def stacked(voltage):
     s, f = voltage.shape[:2]
     return voltage.reshape(s, f, 2, H, LANES).transpose(0, 1, 3, 2, 4).reshape(s, f, ROWS, LANES)
@@ -320,32 +318,67 @@
     two = shifted(block, "stn", 2)
     swapped = lax.ppermute(two, "stn", [(i, i ^ 1) for i in range(size)])
     rest = lax.ppermute(block, "stn", [(i, (i + 1 if i % 2 == 0 else i + 3) % size) for i in range(size)])
-    return [swapped, two, rest]
+    return [block, swapped, two, rest]
+
+
+def general(volts, fir_taps):
+    groups = lax.axis_size("tm")
+    frames = volts.shape[1]
+    slots = K2 // groups // SUB
+    history = lax.ppermute(volts[:, frames - TAPS :], "tm", [(i, i + 1) for i in range(groups - 1)])
+    pieces = []
+    for block in range(frames // TAPS):
+        if block:
+            before = (volts, TAPS, block - 1, 0, 1)
+        else:
+            before = (history, TAPS, 0, 0, 1)
+        piece = spectra([before, (volts, TAPS, block, TAPS, 1)], TAPS, fir_taps, groups, [slots * groups])[0]
+        pieces.append(lax.all_to_all(piece, "tm", split_axis=2, concat_axis=1, tiled=True))
+    return [[piece] for piece in pieces]
+
+
+def paired(volts, fir_taps):
+    frames = volts.shape[1]
+    me = lax.axis_index("tm")
+    slots = K2 // 2 // SUB
+    sizes = [slots, slots]
+    swap = [(0, 1), (1, 0)]
+    edge = TAPS // 2
+    last = frames // edge
+    edge_frames = lax.dynamic_slice_in_dim(volts, jnp.where(me == 0, frames - edge, 0), edge, 1)
+    visiting = lax.ppermute(edge_frames, "tm", swap)
+    own_a, away_a = spectra(
+        [(volts, TAPS, 0, 0, me), (volts, TAPS, me, TAPS, 1)], TAPS, fir_taps, 2, sizes, 1, me
+    )
+    own_b, away_b = spectra(
+        [(volts, TAPS, 0, 0, 1), (volts, TAPS, 1, TAPS, 1)], TAPS, fir_taps, 2, sizes, 1 - me, me
+    )
+    own_c, away_c = spectra(
+        [
+            (volts, edge, jnp.where(me == 0, last - 2, 0), edge * me, 1),
+            (volts, edge, jnp.where(me == 0, last - 1, 1), edge * me + edge, 1),
+            (visiting, edge, 0, 2 * edge * (1 - me), 1),
+        ],
+        edge, fir_taps, 2, sizes, 1, me,
+    )
+    got_a = lax.ppermute(away_a, "tm", swap)
+    got_b = lax.ppermute(away_b, "tm", [(0, 1)])
+    got_c = lax.ppermute(away_c, "tm", swap)
+    return [[own_a, got_a], [jnp.where(me == 0, own_b, got_b)], [own_c, got_c]]
 
 
 def local(voltage, fir_taps):
     groups = lax.axis_size("tm")
-    frames = voltage.shape[1]
     volts = stacked(voltage)
-    me = lax.axis_index("tm")
-    history = lax.ppermute(volts[:, frames - TAPS :], "tm", [(i, i + 1) for i in range(groups - 1)])
-    table = stage_two_table(groups)
-    slots = K2 // groups // SUB
-    first = spectra(
-        [(history, TAPS, 0, 0, 1), (volts, TAPS, 0, TAPS, 1)], TAPS, fir_taps, table, [slots * groups]
-    )[0]
-    later = spectra(
-        [(volts, TAPS, 0, 0, 1), (volts, TAPS, 1, TAPS, 1)], TAPS, fir_taps, table, [slots * groups]
-    )[0]
-    blocks = []
-    for piece in (first, later):
-        block = lax.all_to_all(piece, "tm", split_axis=2, concat_axis=1, tiled=True)
-        blocks.append([block] + neighbours(block))
+    stages = paired(volts, fir_taps) if groups == 2 else general(volts, fir_taps)
     even = lax.axis_index("stn") % 2 == 0
     place = jnp.where(even, jnp.array([0, 1, 2, 3]), jnp.array([0, 3, 2, 1])).astype(jnp.int32)
-    arrays = [x for blk in blocks for x in blk]
-    jobs = [((0, 4), (v, v + 4)) for v in range(VISITS)]
-    out = correlate(arrays, jobs, place, 1.0 / (groups * frames))
+    out = None
+    for pieces in stages:
+        arrays = [x for piece in pieces for x in neighbours(piece)]
+        own = tuple(range(0, len(arrays), VISITS))
+        jobs = [(own, tuple(v + o for o in own)) for v in range(VISITS)]
+        out = correlate(arrays, jobs, place, 1.0 / (groups * voltage.shape[1]), out)
     return natural(out, CHANS // groups)
 
 

time: 193 us -> 162 us (0.84)
  the two profiles are of different devices: /device:TPU:6 before, /device:TPU:1 now
where the time goes in v2:
time: 162 us; the launch traced here: 161 us
  Pallas kernels  101 us (62%)
  waiting for transfers between devices  29.9 us (18%)
  starting transfers between devices  21.2 us (13%)
  local copies, waits for them, and re-layouts  9.15 us (6%)
    pallas_call x3, Pallas kernels, correlate(): pl.pallas_call(functools.partial(correlate_kernel, jobs, scale, before is...  67.6 us
    pallas_call x3, Pallas kernels, spectra(): pl.pallas_call(functools.partial(spectra_kernel, tuple((p[1] for p in par...  33.2 us
    ppermute x5, waiting for transfers between devices, shifted(): lax.ppermute(block, axis, [(i, (i + distance) % size) for i in range(size)])  18.3 us
    ppermute x5, starting transfers between devices, shifted(): lax.ppermute(block, axis, [(i, (i + distance) % size) for i in range(size)])  7.24 us
    ppermute x1, waiting for transfers between devices, paired(): got_b = lax.ppermute(away_b, 'tm', [(0, 1)])  6.94 us
    unnamed x12, local copies, waits for them, and re-layouts  6.58 us
    ppermute x5, starting transfers between devices, neighbours(): lax.ppermute(block, 'stn', [(i, (i + 1 if i % 2 == 0 else i + 3) % size)...  5.81 us
    ppermute x1, waiting for transfers between devices, paired(): got_c = lax.ppermute(away_c, 'tm', swap)  4.57 us
  transfers between devices with their start and end apart: 19, of which 5 were waited for; matrix products, arithmetic and copies ran while one was open for 0% of the time, Pallas kernels for 48%

profile of v2, /device:TPU:1, one launch (start us, length us, event | category | flops | bytes accessed | tf_op | source)
XLA Modules:
  0.0 161.2 jit_solution(3877773438102931575)
XLA Ops:
  0.0 0.0 copy-start.3
  0.0 0.0 copy-start.4
  0.0 2.3 %constant_dynamic-slice_fusion = bf16[8,8,64,128]{3,2,1,0:T(8,128)(2,1)} fusion(bf16[8,32,64,128]{3,2,1,0:T(8,128)(2,1)} %bitcast.17, s32[]{:T(128)S(6)} %select_n.39), kind=kLoop, calls=%fused_computation.2 | loop fusion | bytes 2097156 | tf_op jit(solution)/shard_map/dynamic_slice | solution.py:348
  2.3 2.1 %collective-permute-start = (bf16[8,8,64,128]{3,2,1,0:T(8,128)(2,1)}, bf16[8,8,64,128]{3,2,1,0:T(8,128)(2,1)S(1)}, u32[]{:S(2)}, u32[]{:S(2)}) collective-permute-start(bf16[8,8,64,128]{3,2,1,0:T(8,128)(2,1)} %constant_dynamic-slice_fusion), channel_id=1, source_target_pairs={{0,1},{1,0},{2,3},{3,2},{4,5},{5,4},{6,7},{7,6},{8,9},{9,8},{10,11... | collective-permute-start | bytes 3145736 | tf_op jit(solution)/shard_map/ppermute | solution.py:349
  4.4 0.1 stack.43.place
  4.5 0.0 copy-done.3
  4.5 0.0 copy-done.4
  4.5 0.0 copy-start
  4.5 2.2 %copy-done = bf16[8,32,2,4096]{3,2,1,0:T(2,128)(2,1)S(1)} copy-done((bf16[8,32,2,4096]{3,2,1,0:T(2,128)(2,1)S(1)}, bf16[8,32,2,4096]{3,2,1,0:T(2,128)(2,1)}, u32[]{:S(2)}) %copy-start) | copy-done | bytes 4194328
  6.7 12.6 %shard_map.75 = (bf16[8,4,4,16,128]{4,3,2,1,0:T(8,128)(2,1)S(1)}, bf16[8,4,4,16,128]{4,3,2,1,0:T(8,128)(2,1)}) custom-call(s32[8]{0:T(128)S(1)} %stack.43.place, bf16[8,32,64,128]{3,2,1,0:T(8,128)(2,1)S(1)} %bitcast.18, bf16[8,32,64,128]{3,2,1,0:T(8,128)(2,1)S(1)} %bitcast.19, f32[16,4096]{1,0:T(8,128)S(1)} %copy-done.4, f32[352,256]{1,0:T(8,128)S(1)} %copy-done.3), custom_call_target="tpu_custom_call" | custom-call | flops 268435456 | bytes 4194304 | tf_op jit(solution)/shard_map/pallas_call | solution.py:168
  19.3 0.0 collective-permute-start.15
  19.3 1.4 collective-permute-start.12
  20.7 0.1 stack.42.place
  20.8 0.0 copy-start.1
  20.8 2.2 %copy-done.1 = bf16[8,32,2,4096]{3,2,1,0:T(2,128)(2,1)S(1)} copy-done((bf16[8,32,2,4096]{3,2,1,0:T(2,128)(2,1)S(1)}, bf16[8,32,2,4096]{3,2,1,0:T(2,128)(2,1)}, u32[]{:S(2)}) %copy-start.1) | copy-done | bytes 4194328
  23.0 11.9 %shard_map.74 = (bf16[8,4,4,16,128]{4,3,2,1,0:T(8,128)(2,1)S(1)}, bf16[8,4,4,16,128]{4,3,2,1,0:T(8,128)(2,1)S(1)}) custom-call(s32[8]{0:T(128)S(1)} %stack.42.place, bf16[8,32,64,128]{3,2,1,0:T(8,128)(2,1)S(1)} %bitcast.20, bf16[8,32,64,128]{3,2,1,0:T(8,128)(2,1)S(1)} %bitcast.21, f32[16,4096]{1,0:T(8,128)S(1)} %copy-done.4, f32[352,256]{1,0:T(8,128)S(1)} %copy-done.3), custom_call_target="tpu_custom_call" | custom-call | flops 268435456 | bytes 4194304 | tf_op jit(solution)/shard_map/pallas_call | solution.py:168
  34.9 1.3 collective-permute-start.8
  36.2 2.7 %collective-permute-start.14 = (bf16[8,4,4,16,128]{4,3,2,1,0:T(8,128)(2,1)S(1)}, bf16[8,4,4,16,128]{4,3,2,1,0:T(8,128)(2,1)}, u32[]{:S(2)}, u32[]{:S(2)}) collective-permute-start(bf16[8,4,4,16,128]{4,3,2,1,0:T(8,128)(2,1)S(1)} %get-tuple-element.15.refs_0_), channel_id=1, source_target_pairs={{0,2},{2,8},{4,6},{6,12},{8,10},{10,16},{12,14},{14,20},{16,18},{1... | collective-permute-start | bytes 1572872 | tf_op jit(solution)/shard_map/ppermute | solution.py:320
  38.9 0.0 collective-permute-done.15.refs_4_
  38.9 1.3 collective-permute-start.16
  40.2 0.0 collective-permute-done.12.refs_2_
  40.2 1.8 %collective-permute-start.13 = (bf16[8,4,4,16,128]{4,3,2,1,0:T(8,128)(2,1)}, bf16[8,4,4,16,128]{4,3,2,1,0:T(8,128)(2,1)}, u32[]{:S(2)}, u32[]{:S(2)}) collective-permute-start(bf16[8,4,4,16,128]{4,3,2,1,0:T(8,128)(2,1)} %collective-permute-done.12.refs_2_), channel_id=1, source_target_pairs={{0,2},{2,0},{4,6},{6,4},{8,10},{10,8},{12,14},{14,12},{16,18},{18,... | collective-permute-start | bytes 1572872 | tf_op jit(solution)/shard_map/ppermute | solution.py:319
  42.0 6.9 %collective-permute-done.8 = bf16[8,4,4,16,128]{4,3,2,1,0:T(8,128)(2,1)S(1)} collective-permute-done((bf16[8,4,4,16,128]{4,3,2,1,0:T(8,128)(2,1)S(1)}, bf16[8,4,4,16,128]{4,3,2,1,0:T(8,128)(2,1)S(1)}, u32[]{:S(2)}, u32[]{:S(2)}) %collective-permute-start.8) | collective-permute-done | bytes 524320 | tf_op jit(solution)/shard_map/ppermute | solution.py:365
  48.9 2.7 %collective-permute-start.18 = (bf16[8,4,4,16,128]{4,3,2,1,0:T(8,128)(2,1)S(1)}, bf16[8,4,4,16,128]{4,3,2,1,0:T(8,128)(2,1)}, u32[]{:S(2)}, u32[]{:S(2)}) collective-permute-start(bf16[8,4,4,16,128]{4,3,2,1,0:T(8,128)(2,1)S(1)} %collective-permute-done.15.refs_4_), channel_id=1, source_target_pairs={{0,2},{2,8},{4,6},{6,12},{8,10},{10,16},{12,14},{14,20},{16,18},{1... | collective-permute-start | bytes 1572872 | tf_op jit(solution)/shard_map/ppermute | solution.py:320
  51.6 0.1 broadcast_select_fusion.refs_0_
  51.7 0.0 collective-permute-done.refs_2_
  51.7 1.3 collective-permute-start.9
  53.0 0.1 stack.40.place
  53.1 0.0 copy-start.2
  53.1 2.2 %copy-done.2 = bf16[8,32,2,4096]{3,2,1,0:T(2,128)(2,1)S(1)} copy-done((bf16[8,32,2,4096]{3,2,1,0:T(2,128)(2,1)S(1)}, bf16[8,32,2,4096]{3,2,1,0:T(2,128)(2,1)}, u32[]{:S(2)}) %copy-start.2) | copy-done | bytes 4194328
  55.3 0.0 copy-start.5
  55.3 8.7 %shard_map.73 = (bf16[8,2,4,16,128]{4,3,2,1,0:T(8,128)(2,1)S(1)}, bf16[8,2,4,16,128]{4,3,2,1,0:T(8,128)(2,1)S(1)}) custom-call(s32[11]{0:T(128)S(1)} %stack.40.place, bf16[8,32,64,128]{3,2,1,0:T(8,128)(2,1)S(1)} %bitcast.22, bf16[8,32,64,128]{3,2,1,0:T(8,128)(2,1)S(1)} %bitcast.23, bf16[8,8,64,128]{3,2,1,0:T(8,128)(2,1)S(1)} %collective-permute-done.refs_2_, ...), custom_call_target="tpu_custom_call" | custom-call | flops 134217728 | bytes 2097152 | tf_op jit(solution)/shard_map/pallas_call | solution.py:168
  64.0 0.0 collective-permute-done.14.refs_3_
  64.0 0.3 collective-permute-start.11
  64.4 0.0 collective-permute-done.16.refs_6_
  64.4 0.2 collective-permute-start.17
  64.6 0.0 collective-permute-done.13.refs_1_
  64.6 2.2 %collective-permute-start.4 = (bf16[8,2,4,16,128]{4,3,2,1,0:T(8,128)(2,1)S(1)}, bf16[8,2,4,16,128]{4,3,2,1,0:T(8,128)(2,1)}, u32[]{:S(2)}, u32[]{:S(2)}) collective-permute-start(bf16[8,2,4,16,128]{4,3,2,1,0:T(8,128)(2,1)S(1)} %get-tuple-element.12), channel_id=1, source_target_pairs={{0,1},{1,0},{2,3},{3,2},{4,5},{5,4},{6,7},{7,6},{8,9},{9,8},{10,11... | collective-permute-start | bytes 786440 | tf_op jit(solution)/shard_map/ppermute | solution.py:366
  66.8 0.0 collective-permute-done.18.refs_7_
  66.8 2.0 %collective-permute-start.1 = (bf16[8,2,4,16,128]{4,3,2,1,0:T(8,128)(2,1)S(1)}, bf16[8,2,4,16,128]{4,3,2,1,0:T(8,128)(2,1)}, u32[]{:S(2)}, u32[]{:S(2)}) collective-permute-start(bf16[8,2,4,16,128]{4,3,2,1,0:T(8,128)(2,1)S(1)} %get-tuple-element.11.refs_0_), channel_id=1, source_target_pairs={{0,4},{2,6},{4,8},{6,10},{8,12},{10,14},{12,16},{14,18},{16,20},{1... | collective-permute-start | bytes 786440 | tf_op jit(solution)/shard_map/ppermute | solution.py:313
  68.8 4.6 %collective-permute-done.4.refs_4_ = bf16[8,2,4,16,128]{4,3,2,1,0:T(8,128)(2,1)} collective-permute-done((bf16[8,2,4,16,128]{4,3,2,1,0:T(8,128)(2,1)S(1)}, bf16[8,2,4,16,128]{4,3,2,1,0:T(8,128)(2,1)}, u32[]{:S(2)}, u32[]{:S(2)}) %collective-permute-start.4) | collective-permute-done | bytes 262176 | tf_op jit(solution)/shard_map/ppermute | solution.py:366
  73.4 1.3 collective-permute-start.5
  74.6 4.8 %collective-permute-done.9.refs_2_ = bf16[8,4,4,16,128]{4,3,2,1,0:T(8,128)(2,1)} collective-permute-done((bf16[8,4,4,16,128]{4,3,2,1,0:T(8,128)(2,1)S(1)}, bf16[8,4,4,16,128]{4,3,2,1,0:T(8,128)(2,1)}, u32[]{:S(2)}, u32[]{:S(2)}) %collective-permute-start.9) | collective-permute-done | bytes 524320 | tf_op jit(solution)/shard_map/ppermute | solution.py:313
  79.5 0.0 collective-permute-start.10
  79.5 0.0 collective-permute-done.11.refs_3_
  79.5 0.0 collective-permute-start.3
  79.5 11.2 %collective-permute-done.1.refs_2_ = bf16[8,2,4,16,128]{4,3,2,1,0:T(8,128)(2,1)} collective-permute-done((bf16[8,2,4,16,128]{4,3,2,1,0:T(8,128)(2,1)S(1)}, bf16[8,2,4,16,128]{4,3,2,1,0:T(8,128)(2,1)}, u32[]{:S(2)}, u32[]{:S(2)}) %collective-permute-start.1) | collective-permute-done | bytes 262176 | tf_op jit(solution)/shard_map/ppermute | solution.py:313
  90.7 0.0 collective-permute-start.7
  90.7 0.0 collective-permute-done.17.refs_5_
  90.7 0.5 collective-permute-start.2
  91.2 2.3 %collective-permute-done.5.refs_6_ = bf16[8,2,4,16,128]{4,3,2,1,0:T(8,128)(2,1)} collective-permute-done((bf16[8,2,4,16,128]{4,3,2,1,0:T(8,128)(2,1)}, bf16[8,2,4,16,128]{4,3,2,1,0:T(8,128)(2,1)}, u32[]{:S(2)}, u32[]{:S(2)}) %collective-permute-start.5) | collective-permute-done | bytes 262176 | tf_op jit(solution)/shard_map/ppermute | solution.py:313
  93.5 0.0 collective-permute-start.6
  93.5 0.0 copy-done.5
  93.5 24.5 %shard_map.76.refs_4_ = f32[2,8,4,64,128]{4,3,2,1,0:T(8,128)} custom-call(s32[4]{0:T(128)S(1)} %broadcast_select_fusion.1.place, bf16[8,4,4,16,128]{4,3,2,1,0:T(8,128)(2,1)S(1)} %get-tuple-element.15.refs_0_, bf16[8,4,4,16,128]{4,3,2,1,0:T(8,128)(2,1)} %collective-permute-done.13.refs_1_, bf16[8,4,4,16,128]{4,3,2,1,0:T(8,128)(2,1)} %collective-permute-done.12.refs_2_, ...), custom_call_target="tpu_custom_call" | custom-call | flops 536870912 | bytes 8388608 | tf_op jit(solution)/shard_map/pallas_call | solution.py:281
  118.0 0.0 collective-permute-done.10.refs_1_
  118.0 19.8 %shard_map.77.refs_8_ = f32[2,8,4,64,128]{4,3,2,1,0:T(8,128)} custom-call(s32[4]{0:T(128)S(1)} %broadcast_select_fusion.1.place, bf16[8,4,4,16,128]{4,3,2,1,0:T(8,128)(2,1)S(1)} %broadcast_select_fusion.refs_0_, bf16[8,4,4,16,128]{4,3,2,1,0:T(8,128)(2,1)S(1)} %collective-permute-done.10.refs_1_, ...), custom_call_target="tpu_custom_call", output_to_operand_aliasing={{}: (5, {})} | custom-call | flops 268435456 | bytes 8388608 | tf_op jit(solution)/shard_map/pallas_call | solution.py:281
  137.8 0.0 collective-permute-done.3.refs_3_
  137.8 0.0 collective-permute-done.2.refs_1_
  137.8 0.0 collective-permute-done.7.refs_7_
  137.8 0.0 collective-permute-done.6.refs_5_
  137.8 23.3 %shard_map.78 = f32[2,8,4,64,128]{4,3,2,1,0:T(8,128)} custom-call(s32[4]{0:T(128)S(1)} %broadcast_select_fusion.1.place, bf16[8,2,4,16,128]{4,3,2,1,0:T(8,128)(2,1)S(1)} %get-tuple-element.11.refs_0_, bf16[8,2,4,16,128]{4,3,2,1,0:T(8,128)(2,1)S(1)} %collective-permute-done.2.refs_1_, ...), custom_call_target="tpu_custom_call", output_to_operand_aliasing={{}: (9, {})} | custom-call | flops 268435456 | bytes 8388608 | tf_op jit(solution)/shard_map/pallas_call | solution.py:281
  (3 shorter events, 0.0 us)
Async XLA Ops:
  0.0 4.5 %copy-start.3 = (f32[352,256]{1,0:T(8,128)S(1)}, f32[352,256]{1,0:T(8,128)}, u32[]{:S(2)}) copy-start(f32[352,256]{1,0:T(8,128)} %constant.47.clone.refs_4_.refs_3_) | copy-start | bytes 1081348
  0.0 4.5 %copy-start.4 = (f32[16,4096]{1,0:T(8,128)S(1)}, f32[16,4096]{1,0:T(8,128)}, u32[]{:S(2)}) copy-start(f32[16,4096]{1,0:T(8,128)} %refs_2_.3) | copy-start | bytes 786436
  2.3 49.4 %collective-permute-start = (bf16[8,8,64,128]{3,2,1,0:T(8,128)(2,1)}, bf16[8,8,64,128]{3,2,1,0:T(8,128)(2,1)S(1)}, u32[]{:S(2)}, u32[]{:S(2)}) collective-permute-start(bf16[8,8,64,128]{3,2,1,0:T(8,128)(2,1)} %constant_dynamic-slice_fusion), channel_id=1, source_target_pairs={{0,1},{1,0},{2,3},{3,2},{4,5},{5,4},{6,7},{7,6},{8,9},{9,8},{10,11... | collective-permute-start | bytes 3145736 | tf_op jit(solution)/shard_map/ppermute | solution.py:349
  4.5 2.2 %copy-start = (bf16[8,32,2,4096]{3,2,1,0:T(2,128)(2,1)S(1)}, bf16[8,32,2,4096]{3,2,1,0:T(2,128)(2,1)}, u32[]{:S(2)}) copy-start(bf16[8,32,2,4096]{3,2,1,0:T(2,128)(2,1)} %param.7) | copy-start | bytes 12582916
  19.3 19.7 %collective-permute-start.15 = (bf16[8,4,4,16,128]{4,3,2,1,0:T(8,128)(2,1)}, bf16[8,4,4,16,128]{4,3,2,1,0:T(8,128)(2,1)S(1)}, u32[]{:S(2)}, u32[]{:S(2)}) collective-permute-start(bf16[8,4,4,16,128]{4,3,2,1,0:T(8,128)(2,1)} %get-tuple-element.16), channel_id=1, source_target_pairs={{0,1},{1,0},{2,3},{3,2},{4,5},{5,4},{6,7},{7,6},{8,9},{9,8},{10,11... | collective-permute-start | bytes 1572872 | tf_op jit(solution)/shard_map/ppermute | solution.py:364
  19.3 20.9 %collective-permute-start.12 = (bf16[8,4,4,16,128]{4,3,2,1,0:T(8,128)(2,1)S(1)}, bf16[8,4,4,16,128]{4,3,2,1,0:T(8,128)(2,1)}, u32[]{:S(2)}, u32[]{:S(2)}) collective-permute-start(bf16[8,4,4,16,128]{4,3,2,1,0:T(8,128)(2,1)S(1)} %get-tuple-element.15.refs_0_), channel_id=1, source_target_pairs={{0,4},{2,6},{4,8},{6,10},{8,12},{10,14},{12,16},{14,18},{16,20},{1... | collective-permute-start | bytes 1572872 | tf_op jit(solution)/shard_map/ppermute | solution.py:313
  20.8 2.2 %copy-start.1 = (bf16[8,32,2,4096]{3,2,1,0:T(2,128)(2,1)S(1)}, bf16[8,32,2,4096]{3,2,1,0:T(2,128)(2,1)}, u32[]{:S(2)}) copy-start(bf16[8,32,2,4096]{3,2,1,0:T(2,128)(2,1)} %param.7) | copy-start | bytes 12582916
  34.9 14.1 %collective-permute-start.8 = (bf16[8,4,4,16,128]{4,3,2,1,0:T(8,128)(2,1)S(1)}, bf16[8,4,4,16,128]{4,3,2,1,0:T(8,128)(2,1)S(1)}, u32[]{:S(2)}, u32[]{:S(2)}) collective-permute-start(bf16[8,4,4,16,128]{4,3,2,1,0:T(8,128)(2,1)S(1)} %get-tuple-element.14), channel_id=1, source_target_pairs={{0,1},{2,3},{4,5},{6,7},{8,9},{10,11},{12,13},{14,15},{16,17},{18,... | collective-permute-start | bytes 1572872 | tf_op jit(solution)/shard_map/ppermute | solution.py:365
  36.2 27.8 %collective-permute-start.14 = (bf16[8,4,4,16,128]{4,3,2,1,0:T(8,128)(2,1)S(1)}, bf16[8,4,4,16,128]{4,3,2,1,0:T(8,128)(2,1)}, u32[]{:S(2)}, u32[]{:S(2)}) collective-permute-start(bf16[8,4,4,16,128]{4,3,2,1,0:T(8,128)(2,1)S(1)} %get-tuple-element.15.refs_0_), channel_id=1, source_target_pairs={{0,2},{2,8},{4,6},{6,12},{8,10},{10,16},{12,14},{14,20},{16,18},{1... | collective-permute-start | bytes 1572872 | tf_op jit(solution)/shard_map/ppermute | solution.py:320
  38.9 25.4 %collective-permute-start.16 = (bf16[8,4,4,16,128]{4,3,2,1,0:T(8,128)(2,1)S(1)}, bf16[8,4,4,16,128]{4,3,2,1,0:T(8,128)(2,1)}, u32[]{:S(2)}, u32[]{:S(2)}) collective-permute-start(bf16[8,4,4,16,128]{4,3,2,1,0:T(8,128)(2,1)S(1)} %collective-permute-done.15.refs_4_), channel_id=1, source_target_pairs={{0,4},{2,6},{4,8},{6,10},{8,12},{10,14},{12,16},{14,18},{16,20},{1... | collective-permute-start | bytes 1572872 | tf_op jit(solution)/shard_map/ppermute | solution.py:313
  40.2 24.4 %collective-permute-start.13 = (bf16[8,4,4,16,128]{4,3,2,1,0:T(8,128)(2,1)}, bf16[8,4,4,16,128]{4,3,2,1,0:T(8,128)(2,1)}, u32[]{:S(2)}, u32[]{:S(2)}) collective-permute-start(bf16[8,4,4,16,128]{4,3,2,1,0:T(8,128)(2,1)} %collective-permute-done.12.refs_2_), channel_id=1, source_target_pairs={{0,2},{2,0},{4,6},{6,4},{8,10},{10,8},{12,14},{14,12},{16,18},{18,... | collective-permute-start | bytes 1572872 | tf_op jit(solution)/shard_map/ppermute | solution.py:319
  48.9 17.9 %collective-permute-start.18 = (bf16[8,4,4,16,128]{4,3,2,1,0:T(8,128)(2,1)S(1)}, bf16[8,4,4,16,128]{4,3,2,1,0:T(8,128)(2,1)}, u32[]{:S(2)}, u32[]{:S(2)}) collective-permute-start(bf16[8,4,4,16,128]{4,3,2,1,0:T(8,128)(2,1)S(1)} %collective-permute-done.15.refs_4_), channel_id=1, source_target_pairs={{0,2},{2,8},{4,6},{6,12},{8,10},{10,16},{12,14},{14,20},{16,18},{1... | collective-permute-start | bytes 1572872 | tf_op jit(solution)/shard_map/ppermute | solution.py:320
  51.7 27.7 %collective-permute-start.9 = (bf16[8,4,4,16,128]{4,3,2,1,0:T(8,128)(2,1)S(1)}, bf16[8,4,4,16,128]{4,3,2,1,0:T(8,128)(2,1)}, u32[]{:S(2)}, u32[]{:S(2)}) collective-permute-start(bf16[8,4,4,16,128]{4,3,2,1,0:T(8,128)(2,1)S(1)} %broadcast_select_fusion.refs_0_), channel_id=1, source_target_pairs={{0,4},{2,6},{4,8},{6,10},{8,12},{10,14},{12,16},{14,18},{16,20},{1... | collective-permute-start | bytes 1572872 | tf_op jit(solution)/shard_map/ppermute | solution.py:313
  53.1 2.2 %copy-start.2 = (bf16[8,32,2,4096]{3,2,1,0:T(2,128)(2,1)S(1)}, bf16[8,32,2,4096]{3,2,1,0:T(2,128)(2,1)}, u32[]{:S(2)}) copy-start(bf16[8,32,2,4096]{3,2,1,0:T(2,128)(2,1)} %param.7) | copy-start | bytes 12582916
  55.3 38.3 %copy-start.5 = (s32[4]{0:T(128)S(1)}, s32[4]{0:T(128)}, u32[]{:S(2)}) copy-start(s32[4]{0:T(128)} %constant.48.clone) | copy-start | bytes 52
  64.0 15.4 %collective-permute-start.11 = (bf16[8,4,4,16,128]{4,3,2,1,0:T(8,128)(2,1)S(1)}, bf16[8,4,4,16,128]{4,3,2,1,0:T(8,128)(2,1)S(1)}, u32[]{:S(2)}, u32[]{:S(2)}) collective-permute-start(bf16[8,4,4,16,128]{4,3,2,1,0:T(8,128)(2,1)S(1)} %broadcast_select_fusion.refs_0_), channel_id=1, source_target_pairs={{0,2},{2,8},{4,6},{6,12},{8,10},{10,16},{12,14},{14,20},{16,18},{1... | collective-permute-start | bytes 1572872 | tf_op jit(solution)/shard_map/ppermute | solution.py:320
  64.4 26.3 %collective-permute-start.17 = (bf16[8,4,4,16,128]{4,3,2,1,0:T(8,128)(2,1)}, bf16[8,4,4,16,128]{4,3,2,1,0:T(8,128)(2,1)S(1)}, u32[]{:S(2)}, u32[]{:S(2)}) collective-permute-start(bf16[8,4,4,16,128]{4,3,2,1,0:T(8,128)(2,1)} %collective-permute-done.16.refs_6_), channel_id=1, source_target_pairs={{0,2},{2,0},{4,6},{6,4},{8,10},{10,8},{12,14},{14,12},{16,18},{18,... | collective-permute-start | bytes 1572872 | tf_op jit(solution)/shard_map/ppermute | solution.py:319
  64.6 8.8 %collective-permute-start.4 = (bf16[8,2,4,16,128]{4,3,2,1,0:T(8,128)(2,1)S(1)}, bf16[8,2,4,16,128]{4,3,2,1,0:T(8,128)(2,1)}, u32[]{:S(2)}, u32[]{:S(2)}) collective-permute-start(bf16[8,2,4,16,128]{4,3,2,1,0:T(8,128)(2,1)S(1)} %get-tuple-element.12), channel_id=1, source_target_pairs={{0,1},{1,0},{2,3},{3,2},{4,5},{5,4},{6,7},{7,6},{8,9},{9,8},{10,11... | collective-permute-start | bytes 786440 | tf_op jit(solution)/shard_map/ppermute | solution.py:366
  66.8 23.9 %collective-permute-start.1 = (bf16[8,2,4,16,128]{4,3,2,1,0:T(8,128)(2,1)S(1)}, bf16[8,2,4,16,128]{4,3,2,1,0:T(8,128)(2,1)}, u32[]{:S(2)}, u32[]{:S(2)}) collective-permute-start(bf16[8,2,4,16,128]{4,3,2,1,0:T(8,128)(2,1)S(1)} %get-tuple-element.11.refs_0_), channel_id=1, source_target_pairs={{0,4},{2,6},{4,8},{6,10},{8,12},{10,14},{12,16},{14,18},{16,20},{1... | collective-permute-start | bytes 786440 | tf_op jit(solution)/shard_map/ppermute | solution.py:313
  73.4 20.1 %collective-permute-start.5 = (bf16[8,2,4,16,128]{4,3,2,1,0:T(8,128)(2,1)}, bf16[8,2,4,16,128]{4,3,2,1,0:T(8,128)(2,1)}, u32[]{:S(2)}, u32[]{:S(2)}) collective-permute-start(bf16[8,2,4,16,128]{4,3,2,1,0:T(8,128)(2,1)} %collective-permute-done.4.refs_4_), channel_id=1, source_target_pairs={{0,4},{2,6},{4,8},{6,10},{8,12},{10,14},{12,16},{14,18},{16,20},{1... | collective-permute-start | bytes 786440 | tf_op jit(solution)/shard_map/ppermute | solution.py:313
  79.5 38.5 %collective-permute-start.10 = (bf16[8,4,4,16,128]{4,3,2,1,0:T(8,128)(2,1)}, bf16[8,4,4,16,128]{4,3,2,1,0:T(8,128)(2,1)S(1)}, u32[]{:S(2)}, u32[]{:S(2)}) collective-permute-start(bf16[8,4,4,16,128]{4,3,2,1,0:T(8,128)(2,1)} %collective-permute-done.9.refs_2_), channel_id=1, source_target_pairs={{0,2},{2,0},{4,6},{6,4},{8,10},{10,8},{12,14},{14,12},{16,18},{18,... | collective-permute-start | bytes 1572872 | tf_op jit(solution)/shard_map/ppermute | solution.py:319
  79.5 58.4 %collective-permute-start.3 = (bf16[8,2,4,16,128]{4,3,2,1,0:T(8,128)(2,1)S(1)}, bf16[8,2,4,16,128]{4,3,2,1,0:T(8,128)(2,1)S(1)}, u32[]{:S(2)}, u32[]{:S(2)}) collective-permute-start(bf16[8,2,4,16,128]{4,3,2,1,0:T(8,128)(2,1)S(1)} %get-tuple-element.11.refs_0_), channel_id=1, source_target_pairs={{0,2},{2,8},{4,6},{6,12},{8,10},{10,16},{12,14},{14,20},{16,18},{1... | collective-permute-start | bytes 786440 | tf_op jit(solution)/shard_map/ppermute | solution.py:320
  90.7 47.1 %collective-permute-start.7 = (bf16[8,2,4,16,128]{4,3,2,1,0:T(8,128)(2,1)}, bf16[8,2,4,16,128]{4,3,2,1,0:T(8,128)(2,1)S(1)}, u32[]{:S(2)}, u32[]{:S(2)}) collective-permute-start(bf16[8,2,4,16,128]{4,3,2,1,0:T(8,128)(2,1)} %collective-permute-done.4.refs_4_), channel_id=1, source_target_pairs={{0,2},{2,8},{4,6},{6,12},{8,10},{10,16},{12,14},{14,20},{16,18},{1... | collective-permute-start | bytes 786440 | tf_op jit(solution)/shard_map/ppermute | solution.py:320
  90.7 47.1 %collective-permute-start.2 = (bf16[8,2,4,16,128]{4,3,2,1,0:T(8,128)(2,1)}, bf16[8,2,4,16,128]{4,3,2,1,0:T(8,128)(2,1)S(1)}, u32[]{:S(2)}, u32[]{:S(2)}) collective-permute-start(bf16[8,2,4,16,128]{4,3,2,1,0:T(8,128)(2,1)} %collective-permute-done.1.refs_2_), channel_id=1, source_target_pairs={{0,2},{2,0},{4,6},{6,4},{8,10},{10,8},{12,14},{14,12},{16,18},{18,... | collective-permute-start | bytes 786440 | tf_op jit(solution)/shard_map/ppermute | solution.py:319
  93.5 44.3 %collective-permute-start.6 = (bf16[8,2,4,16,128]{4,3,2,1,0:T(8,128)(2,1)}, bf16[8,2,4,16,128]{4,3,2,1,0:T(8,128)(2,1)S(1)}, u32[]{:S(2)}, u32[]{:S(2)}) collective-permute-start(bf16[8,2,4,16,128]{4,3,2,1,0:T(8,128)(2,1)} %collective-permute-done.5.refs_6_), channel_id=1, source_target_pairs={{0,2},{2,0},{4,6},{6,4},{8,10},{10,8},{12,14},{14,12},{16,18},{18,... | collective-permute-start | bytes 786440 | tf_op jit(solution)/shard_map/ppermute | solution.py:319

commit v3 on v2

v3 whole, which is shorter than its diff:
```python
import functools
import math

import jax
import jax.numpy as jnp
import numpy as np
from jax import lax
from jax.experimental import pallas as pl
from jax.experimental.pallas import tpu as pltpu
from jax.sharding import PartitionSpec as P

NCH = 4096
CHANS = 2048
TAPS = 16
VISITS = 4
H = 32
LANES = 128
ROWS = 2 * H
K2 = CHANS // H
STEP = 8
TILE = 16
SUB = 8
BF16 = jnp.bfloat16
F32 = jnp.float32


def angles(rows, columns, modulus):
    turns = np.outer(rows, columns) % modulus
    return turns.astype(np.float64) * (2.0 * math.pi / modulus)


def stage_one_table():
    theta = angles(np.arange(H), np.arange(H), H)
    cosine, sine = np.cos(theta), np.sin(theta)
    table = np.zeros((2, H, H, 2))
    table[0, :, :, 0], table[0, :, :, 1] = cosine, sine
    table[1, :, :, 0], table[1, :, :, 1] = -sine, cosine
    return np.pad(table.reshape(ROWS, ROWS), ((0, 0), (0, 2 * LANES - ROWS)))


def turn_table():
    theta = angles(np.arange(H), np.arange(LANES), NCH)
    return np.concatenate([np.cos(theta), np.sin(theta)], axis=1)


def stage_two_table(groups):
    theta = angles(np.arange(K2), np.arange(LANES), LANES)
    cosine, sine = np.cos(theta) / math.sqrt(NCH), np.sin(theta) / math.sqrt(NCH)
    real = np.concatenate([cosine, sine], 1).reshape(groups, 1, K2 // groups, 2 * LANES)
    imag = np.concatenate([-sine, cosine], 1).reshape(groups, 1, K2 // groups, 2 * LANES)
    return np.concatenate([real, imag], 1).reshape(2 * K2, 2 * LANES)


def tables(groups):
    two = stage_two_table(groups)
    rolled = np.roll(two, K2, axis=0)
    return np.concatenate([stage_one_table(), turn_table(), two, rolled]).astype(np.float32)


def halves(value):
    high = value.astype(BF16)
    return high, (value - high.astype(F32)).astype(BF16)


def dot(left, right):
    return lax.dot_general(left, right, (((1,), (0,)), ((), ())), preferred_element_type=F32)


def dot_nt(left, right):
    return lax.dot_general(left, right, (((1,), (1,)), ((), ())), preferred_element_type=F32)


def spectra_kernel(groups, parts, out_frames, place, *refs):
    part_refs, refs = refs[: len(parts)], refs[len(parts) :]
    taps_ref, table_ref = refs[:2]
    outs, (taps, one, two, ext, filtered, turned, staged) = refs[2:-7], refs[-7:]
    signal, signals = pl.program_id(0), pl.num_programs(0)
    per_group = K2 // groups
    share = LANES // out_frames
    tiles = H // share

    @pl.when(signal == 0)
    def _():
        for h in range(H):
            for half in range(TAPS // SUB):
                tile = taps_ref[pl.ds(half * SUB, SUB), pl.ds(h * LANES, LANES)]
                for r in range(2):
                    taps[pl.ds(half * SUB * ROWS + 2 * h + r, SUB, stride=ROWS), :] = tile
        high, low = halves(table_ref[:ROWS, :ROWS])
        one[...] = jnp.concatenate([high, high, low], axis=1)
        start = pl.multiple_of(ROWS + H + place[1] * 2 * K2, SUB)
        high, low = halves(table_ref[pl.ds(start, 2 * K2), :])
        two[0] = high
        two[1] = low

    def body():
        for number, (frames, ref) in enumerate(zip(parts, part_refs)):
            start = place[2 + 3 * number + 1]
            valid = place[2 + 3 * number + 2]

            @pl.when(valid == 1)
            def _():
                for f in range(frames):
                    ext[start + f] = ref[0, f].astype(F32)

            @pl.when(valid == 0)
            def _():
                for f in range(frames):
                    ext[start + f] = jnp.zeros((ROWS, LANES), F32)

        def fir(q, carry):
            rows = pl.ds(pl.multiple_of(q * SUB, SUB), SUB)
            tap = [taps[pl.ds(pl.multiple_of(m * ROWS + q * SUB, SUB), SUB), :] for m in range(TAPS)]
            for f in range(out_frames):
                total = tap[0] * ext[f + 1, rows]
                for m in range(1, TAPS):
                    total = total + tap[m] * ext[f + 1 + m, rows]
                filtered[f, rows] = total
            return carry

        lax.fori_loop(0, ROWS // SUB, fir, 0)

        cosine = table_ref[ROWS : ROWS + H, :LANES]
        sine = table_ref[ROWS : ROWS + H, LANES:]
        for g in range(out_frames // STEP):
            block = jnp.concatenate([filtered[g * STEP + f] for f in range(STEP)], axis=1)
            high, low = halves(block)
            first = dot(one[...], jnp.concatenate([high, low, high], axis=0))
            for f in range(STEP):
                real = first[:H, f * LANES : (f + 1) * LANES]
                imag = first[H:, f * LANES : (f + 1) * LANES]
                at = (g * STEP + f) * ROWS
                turned[at : at + H, :] = real * cosine + imag * sine
                turned[at + H : at + ROWS, :] = imag * cosine - real * sine
        for pair in range(tiles // 2):
            rows = []
            for k1 in range(2 * pair * share, 2 * (pair + 1) * share):
                for f in range(0, out_frames, SUB):
                    rows.append(
                        jnp.concatenate(
                            [turned[pl.ds(f * ROWS + p * H + k1, SUB, stride=ROWS), :] for p in range(2)], axis=1
                        )
                    )
            high, low = halves(jnp.concatenate(rows, axis=0))
            spectrum = dot_nt(two[0], high) + dot_nt(two[1], high) + dot_nt(two[0], low)
            for k in range(2):
                for t in range(groups):
                    for p in range(2):
                        for k2 in range(0, per_group, SUB):
                            row = (t * 2 + p) * per_group + k2
                            start = ((t * per_group + k2) * tiles + 2 * pair + k) * TILE + p * SUB
                            staged[pl.ds(start + signal, SUB, stride=tiles * TILE), :] = spectrum[
                                row : row + SUB, k * LANES : (k + 1) * LANES
                            ]

        @pl.when(signal == signals - 1)
        def _():
            at = 0
            for out in outs:

                def write(k2, carry):
                    for k in range(tiles):
                        start = pl.multiple_of((at + k2) * tiles * TILE + k * TILE, TILE)
                        out[k2, k] = staged[pl.ds(start, TILE), :].astype(BF16)
                    return carry

                lax.fori_loop(0, out.shape[0], write, 0)
                at += out.shape[0]

    pl.when(place[0] == 1)(body)


def spectra(parts, out_frames, fir_taps, groups, sizes, run=1, order=0):
    signals = parts[0][0].shape[0]
    numbers = [run, order] + [v for part in parts for v in part[2:]]
    place = jnp.stack([jnp.asarray(v, jnp.int32) for v in numbers])
    table = tables(groups)
    tiles = H * out_frames // LANES
    whole = lambda shape: pl.BlockSpec(shape, lambda s, place: (0,) * len(shape))
    in_specs = [
        pl.BlockSpec(
            (1, part[1], ROWS, LANES), functools.partial(lambda n, s, place: (s, place[2 + 3 * n], 0, 0), n)
        )
        for n, part in enumerate(parts)
    ]
    in_specs += [whole((TAPS, NCH)), whole(table.shape)]
    shapes = [(n, tiles, TILE, LANES) for n in sizes]
    return pl.pallas_call(
        functools.partial(spectra_kernel, groups, tuple(p[1] for p in parts), out_frames),
        grid_spec=pltpu.PrefetchScalarGridSpec(
            num_scalar_prefetch=1,
            grid=(signals,),
            in_specs=in_specs,
            out_specs=[whole(shape) for shape in shapes],
            scratch_shapes=[
                pltpu.VMEM((TAPS * ROWS, LANES), F32),
                pltpu.VMEM((ROWS, 3 * ROWS), BF16),
                pltpu.VMEM((2, 2 * K2, 2 * LANES), BF16),
                pltpu.VMEM((TAPS + out_frames, ROWS, LANES), F32),
                pltpu.VMEM((out_frames, ROWS, LANES), F32),
                pltpu.VMEM((out_frames * ROWS, LANES), F32),
                pltpu.VMEM((K2 * tiles * TILE, LANES), F32),
            ],
        ),
        out_shape=[jax.ShapeDtypeStruct(shape, BF16) for shape in shapes],
        compiler_params=pltpu.CompilerParams(vmem_limit_bytes=32 << 20),
        cost_estimate=pl.CostEstimate(
            flops=signals * out_frames * NCH * 8 * 64, bytes_accessed=signals * out_frames * NCH * 8, transcendentals=0
        ),
    )(place, *[part[0] for part in parts], fir_taps, table)


def correlate_kernel(pieces, per_group, scale, add, last, place, *refs):
    refs = list(refs)
    sums = refs.pop() if last else None
    out = refs.pop()
    before = refs.pop() if add else None
    if not last:
        sums = out
    half = per_group // 2
    lane = lax.broadcasted_iota(jnp.int32, (SUB, LANES), 1)
    first_tile = lane < LANES // 2
    real_lane = lane % TILE < SUB
    sign = jnp.where(real_lane, 1.0, -1.0).astype(F32)
    for number, piece in enumerate(pieces):
        tiles = refs[piece[0][0][0]].shape[1]
        share = H // tiles
        where = lax.broadcasted_iota(jnp.int32, (TILE, LANES), 1) // (LANES // share)

        def pair(index, carry):
            k2 = index // tiles
            k1 = index % tiles
            own, other = [], []
            for position in range(len(piece[0])):
                rows = []
                for tile in range(2):
                    array, start = piece[0][position]
                    a = refs[array][start + tile * half + k2, k1]
                    rows += [jnp.where(where == c, a, jnp.zeros_like(a)) for c in range(share)]
                own.append(jnp.concatenate(rows, axis=0))
                rows = []
                for tile in range(2):
                    for visit in range(VISITS):
                        array, start = piece[visit][position]
                        rows.append(refs[array][start + tile * half + k2, k1])
                other.append(jnp.concatenate(rows, axis=0))
            product = dot_nt(jnp.concatenate(own, axis=1), jnp.concatenate(other, axis=1))
            for c in range(share):
                value = []
                for p in range(2):
                    at = [((tile * share + c) * 2 + p) * SUB for tile in range(2)]
                    value.append(
                        jnp.where(first_tile, product[at[0] : at[0] + SUB], product[at[1] : at[1] + SUB])
                    )
                turned = jnp.where(
                    real_lane, pltpu.roll(value[1], LANES - SUB, 1), pltpu.roll(value[1], SUB, 1)
                )
                total = value[0] * sign + turned
                channel = k2 // 4 * LANES + k2 % 4 * H + k1 * share + c
                rows = pl.ds(pl.multiple_of(channel * SUB, SUB), SUB)
                if number:
                    total = total + sums[rows, :]
                elif add:
                    total = total + before[rows, :]
                sums[rows, :] = total
            return carry

        lax.fori_loop(0, half * tiles, pair, 0, unroll=2)
    if not last:
        return

    def finish(index, carry):
        block = index // SUB
        signal = index % SUB
        value = sums[pl.ds(block * LANES * SUB + signal, LANES, stride=SUB), :]
        value = jnp.transpose(value * scale)
        at = 0
        for tile in range(2):
            for visit in range(VISITS):
                for part in range(2):
                    out[part, signal, place[visit], tile * (half // 4) + block] = value[at : at + SUB]
                    at += SUB
        return carry

    lax.fori_loop(0, half // 4 * SUB, finish, 0)


def correlate(arrays, pieces, per_group, place, scale, before, last):
    signals = TILE // 2
    rows = per_group // 2 * H * SUB
    shape = (2, signals, VISITS, per_group // 4, SUB, LANES) if last else (rows, LANES)
    operands = list(arrays) + ([] if before is None else [before])
    whole = lambda shape: pl.BlockSpec(shape, lambda i, place: (0,) * len(shape))
    return pl.pallas_call(
        functools.partial(correlate_kernel, pieces, per_group, scale, before is not None, last),
        grid_spec=pltpu.PrefetchScalarGridSpec(
            num_scalar_prefetch=1,
            grid=(1,),
            in_specs=[whole(x.shape) for x in operands],
            out_specs=whole(shape),
            scratch_shapes=[pltpu.VMEM((rows, LANES), F32)] if last else [],
        ),
        out_shape=jax.ShapeDtypeStruct(shape, F32),
        compiler_params=pltpu.CompilerParams(vmem_limit_bytes=48 << 20),
        input_output_aliases={} if before is None or last else {len(operands): 0},
        cost_estimate=pl.CostEstimate(flops=8 << 30, bytes_accessed=8 << 20, transcendentals=0),
    )(place, *operands)


def stacked(voltage):
    s, f = voltage.shape[:2]
    return voltage.reshape(s, f, 2, H, LANES).transpose(0, 1, 3, 2, 4).reshape(s, f, ROWS, LANES)


def natural(out):
    parts, s, visits, i, t, lanes = out.shape
    return out.transpose(0, 1, 2, 4, 3, 5).reshape(parts, s, visits * t, i * lanes)


def shifted(block, axis, distance):
    size = lax.axis_size(axis)
    return lax.ppermute(block, axis, [(i, (i + distance) % size) for i in range(size)])


def neighbours(block):
    size = lax.axis_size("stn")
    two = shifted(block, "stn", 2)
    swapped = lax.ppermute(two, "stn", [(i, i ^ 1) for i in range(size)])
    rest = lax.ppermute(block, "stn", [(i, (i + 1 if i % 2 == 0 else i + 3) % size) for i in range(size)])
    return [block, swapped, two, rest]


def general(volts, fir_taps):
    groups = lax.axis_size("tm")
    frames = volts.shape[1]
    history = lax.ppermute(volts[:, frames - TAPS :], "tm", [(i, i + 1) for i in range(groups - 1)])
    parts = [(history, TAPS, 0, 0, 1)] + [(volts, TAPS, i, TAPS * (i + 1), 1) for i in range(frames // TAPS)]
    spectrum = spectra(parts, frames, fir_taps, groups, [K2])[0]
    return [[lax.all_to_all(spectrum, "tm", split_axis=0, concat_axis=0, tiled=True)]]


def paired(volts, fir_taps):
    frames = volts.shape[1]
    me = lax.axis_index("tm")
    sizes = [K2 // 2, K2 // 2]
    swap = [(0, 1), (1, 0)]
    edge = TAPS // 2
    last = frames // edge
    edge_frames = lax.dynamic_slice_in_dim(volts, jnp.where(me == 0, frames - edge, 0), edge, 1)
    visiting = lax.ppermute(edge_frames, "tm", swap)
    own_a, away_a = spectra(
        [(volts, TAPS, 0, 0, me), (volts, TAPS, me, TAPS, 1)], TAPS, fir_taps, 2, sizes, 1, me
    )
    own_b, away_b = spectra(
        [(volts, TAPS, 0, 0, 1), (volts, TAPS, 1, TAPS, 1)], TAPS, fir_taps, 2, sizes, 1 - me, me
    )
    own_c, away_c = spectra(
        [
            (volts, edge, jnp.where(me == 0, last - 2, 0), edge * me, 1),
            (volts, edge, jnp.where(me == 0, last - 1, 1), edge * me + edge, 1),
            (visiting, edge, 0, 2 * edge * (1 - me), 1),
        ],
        edge, fir_taps, 2, sizes, 1, me,
    )
    got_a = lax.ppermute(away_a, "tm", swap)
    got_b = lax.ppermute(away_b, "tm", [(0, 1)])
    got_c = lax.ppermute(away_c, "tm", swap)
    return [[own_a, got_a], [jnp.where(me == 0, own_b, got_b)], [own_c, got_c]]


def local(voltage, fir_taps):
    groups = lax.axis_size("tm")
    per_group = K2 // groups
    volts = stacked(voltage)
    stages = paired(volts, fir_taps) if groups == 2 else general(volts, fir_taps)
    even = lax.axis_index("stn") % 2 == 0
    place = jnp.where(even, jnp.array([0, 1, 2, 3]), jnp.array([0, 3, 2, 1])).astype(jnp.int32)
    scale = 1.0 / (groups * voltage.shape[1])
    out = None
    for number, pieces in enumerate(stages):
        arrays = [x for piece in pieces for x in neighbours(piece)]
        starts = range(0, arrays[0].shape[0], per_group)
        laid = tuple(
            tuple((VISITS * n + visit, start) for n in range(len(pieces)) for start in starts)
            for visit in range(VISITS)
        )
        out = correlate(arrays, [laid], per_group, place, scale, out, number == len(stages) - 1)
    return natural(out)


def solution(mesh):
    return jax.shard_map(
        local,
        mesh=mesh,
        in_specs=(P("stn", "tm", None, None), P()),
        out_specs=P(None, "stn", None, "tm"),
        check_vma=False,
    )
```

time: 162 us -> 135 us (0.83)
  Pallas kernels: 101 us -> 78.3 us
  waiting for transfers between devices: 29.9 us -> 22 us
  local copies, waits for them, and re-layouts: 9.15 us -> 12.6 us
    pallas_call x6, Pallas kernels: 101 us -> 78.3 us  [the longest x3 42 us: spectra(): pl.pallas_call(functools.partial(spectra_kernel, groups, tuple((p[1] for...]
    ppermute x5, waiting for transfers between devices: 18.3 us -> 1.3 us  [shifted(): lax.ppermute(block, axis, [(i, (i + distance) % size) for i in range(size)])]
    ppermute x1, waiting for transfers between devices: 6.94 us -> 17.3 us  [paired(): got_b = lax.ppermute(away_b, 'tm', [(0, 1)])]
    unnamed x12 -> x18, local copies, waits for them, and re-layouts: 6.58 us -> 10.1 us
    ppermute x1, starting transfers between devices: 0.01 us -> 2.14 us  [paired(): got_a = lax.ppermute(away_a, 'tm', swap)]
    ppermute x1, starting transfers between devices: 2.07 us -> 0.09 us  [paired(): visiting = lax.ppermute(edge_frames, 'tm', swap)]
  transfers between devices with their start and end apart: 19 -> 19, of which waited for: 5 -> 3; matrix products, arithmetic and copies ran while one was open for 0% -> 2% of each run, Pallas kernels for 48% -> 38%
where the time goes in v3:
time: 135 us; the launch traced here: 134 us
  Pallas kernels  78.3 us (58%)
  waiting for transfers between devices  22 us (16%)
  starting transfers between devices  21.3 us (16%)
  local copies, waits for them, and re-layouts  12.6 us (9%)
    pallas_call x3, Pallas kernels, spectra(): pl.pallas_call(functools.partial(spectra_kernel, groups, tuple((p[1] for...  42 us
    pallas_call x3, Pallas kernels, correlate(): pl.pallas_call(functools.partial(correlate_kernel, pieces, per_group, sca...  36.3 us
    ppermute x1, waiting for transfers between devices, paired(): got_b = lax.ppermute(away_b, 'tm', [(0, 1)])  17.3 us
    unnamed x18, local copies, waits for them, and re-layouts  10.1 us
    ppermute x5, starting transfers between devices, neighbours(): lax.ppermute(block, 'stn', [(i, (i + 1 if i % 2 == 0 else i + 3) % size)...  6.56 us
    ppermute x5, starting transfers between devices, shifted(): lax.ppermute(block, axis, [(i, (i + distance) % size) for i in range(size)])  6.48 us
    ppermute x1, waiting for transfers between devices, paired(): got_c = lax.ppermute(away_c, 'tm', swap)  3.38 us
  transfers between devices with their start and end apart: 19, of which 3 were waited for; matrix products, arithmetic and copies ran while one was open for 2% of the time, Pallas kernels for 38%

profile of v3, /device:TPU:1, one launch (start us, length us, event | category | flops | bytes accessed | tf_op | source)
XLA Modules:
  0.0 134.4 jit_solution(4100576653671110840)
XLA Ops:
  0.0 0.1 stack.43.place
  0.1 0.0 copy-start
  0.1 2.2 %copy-done = bf16[8,32,2,4096]{3,2,1,0:T(2,128)(2,1)S(1)} copy-done((bf16[8,32,2,4096]{3,2,1,0:T(2,128)(2,1)S(1)}, bf16[8,32,2,4096]{3,2,1,0:T(2,128)(2,1)}, u32[]{:S(2)}) %copy-start) | copy-done | bytes 4194328
  2.3 0.0 copy-start.3
  2.3 1.0 copy-done.3
  3.3 0.0 copy-start.5
  3.3 0.9 copy-done.5
  4.2 15.4 %shard_map.75 = (bf16[32,4,16,128]{3,2,1,0:T(8,128)(2,1)S(1)}, bf16[32,4,16,128]{3,2,1,0:T(8,128)(2,1)S(1)}) custom-call(s32[8]{0:T(128)S(1)} %stack.43.place, bf16[8,32,64,128]{3,2,1,0:T(8,128)(2,1)S(1)} %bitcast.16, bf16[8,32,64,128]{3,2,1,0:T(8,128)(2,1)S(1)} %bitcast.17, f32[16,4096]{1,0:T(8,128)S(1)} %copy-done.5, f32[352,256]{1,0:T(8,128)S(1)} %copy-done.3), custom_call_target="tpu_custom_call" | custom-call | flops 268435456 | bytes 4194304 | tf_op jit(solution)/shard_map/pallas_call | solution.py:188
  19.6 0.0 copy-start.4
  19.6 0.0 copy-start.6
  19.6 2.1 %collective-permute-start.15 = (bf16[32,4,16,128]{3,2,1,0:T(8,128)(2,1)S(1)}, bf16[32,4,16,128]{3,2,1,0:T(8,128)(2,1)S(1)}, u32[]{:S(2)}, u32[]{:S(2)}) collective-permute-start(bf16[32,4,16,128]{3,2,1,0:T(8,128)(2,1)S(1)} %get-tuple-element.16), channel_id=1, source_target_pairs={{0,1},{1,0},{2,3},{3,2},{4,5},{5,4},{6,7},{7,6},{8,9},{9,8},{10,11... | collective-permute-start | bytes 1572872 | tf_op jit(solution)/shard_map/ppermute | solution.py:365
  21.7 2.3 %constant_dynamic-slice_fusion = bf16[8,8,64,128]{3,2,1,0:T(8,128)(2,1)} fusion(bf16[8,32,64,128]{3,2,1,0:T(8,128)(2,1)} %bitcast.15, s32[]{:T(128)S(6)} %select_n.39), kind=kLoop, calls=%fused_computation.2 | loop fusion | bytes 2097156 | tf_op jit(solution)/shard_map/dynamic_slice | solution.py:349
  24.0 0.1 collective-permute-start
  24.1 1.3 collective-permute-start.12
  25.4 0.1 stack.42.place
  25.5 0.0 copy-done.4
  25.5 0.0 copy-done.6
  25.5 0.0 copy-start.1
  25.5 2.2 %copy-done.1 = bf16[8,32,2,4096]{3,2,1,0:T(2,128)(2,1)S(1)} copy-done((bf16[8,32,2,4096]{3,2,1,0:T(2,128)(2,1)S(1)}, bf16[8,32,2,4096]{3,2,1,0:T(2,128)(2,1)}, u32[]{:S(2)}) %copy-start.1) | copy-done | bytes 4194328
  27.7 15.4 %shard_map.74 = (bf16[32,4,16,128]{3,2,1,0:T(8,128)(2,1)S(1)}, bf16[32,4,16,128]{3,2,1,0:T(8,128)(2,1)S(1)}) custom-call(s32[8]{0:T(128)S(1)} %stack.42.place, bf16[8,32,64,128]{3,2,1,0:T(8,128)(2,1)S(1)} %bitcast.18, bf16[8,32,64,128]{3,2,1,0:T(8,128)(2,1)S(1)} %bitcast.19, f32[16,4096]{1,0:T(8,128)S(1)} %copy-done.6, f32[352,256]{1,0:T(8,128)S(1)} %copy-done.4), custom_call_target="tpu_custom_call" | custom-call | flops 268435456 | bytes 4194304 | tf_op jit(solution)/shard_map/pallas_call | solution.py:188
  43.1 1.3 collective-permute-start.8
  44.4 0.0 collective-permute-done.15.refs_4_
  44.4 1.3 collective-permute-start.16
  45.8 3.0 %collective-permute-start.14 = (bf16[32,4,16,128]{3,2,1,0:T(8,128)(2,1)S(1)}, bf16[32,4,16,128]{3,2,1,0:T(8,128)(2,1)}, u32[]{:S(2)}, u32[]{:S(2)}) collective-permute-start(bf16[32,4,16,128]{3,2,1,0:T(8,128)(2,1)S(1)} %get-tuple-element.15.refs_0_), channel_id=1, source_target_pairs={{0,2},{2,8},{4,6},{6,12},{8,10},{10,16},{12,14},{14,20},{16,18},{1... | collective-permute-start | bytes 1572872 | tf_op jit(solution)/shard_map/ppermute | solution.py:329
  48.7 0.0 collective-permute-done.12.refs_2_
  48.7 0.0 collective-permute-start.18
  48.8 17.3 %collective-permute-done.8 = bf16[32,4,16,128]{3,2,1,0:T(8,128)(2,1)S(1)} collective-permute-done((bf16[32,4,16,128]{3,2,1,0:T(8,128)(2,1)S(1)}, bf16[32,4,16,128]{3,2,1,0:T(8,128)(2,1)S(1)}, u32[]{:S(2)}, u32[]{:S(2)}) %collective-permute-start.8) | collective-permute-done | bytes 524320 | tf_op jit(solution)/shard_map/ppermute | solution.py:366
  66.0 1.5 %collective-permute-start.13 = (bf16[32,4,16,128]{3,2,1,0:T(8,128)(2,1)}, bf16[32,4,16,128]{3,2,1,0:T(8,128)(2,1)}, u32[]{:S(2)}, u32[]{:S(2)}) collective-permute-start(bf16[32,4,16,128]{3,2,1,0:T(8,128)(2,1)} %collective-permute-done.12.refs_2_), channel_id=1, source_target_pairs={{0,2},{2,0},{4,6},{6,4},{8,10},{10,8},{12,14},{14,12},{16,18},{18,... | collective-permute-start | bytes 1572872 | tf_op jit(solution)/shard_map/ppermute | solution.py:328
  67.6 0.1 broadcast_select_fusion.refs_0_
  67.6 0.0 collective-permute-done.16.refs_6_
  67.7 1.3 collective-permute-start.9
  68.9 0.0 collective-permute-done.refs_2_
  68.9 0.3 collective-permute-start.17
  69.2 0.1 stack.40.place
  69.3 2.2 %copy-done.2 = bf16[8,32,2,4096]{3,2,1,0:T(2,128)(2,1)S(1)} copy-done((bf16[8,32,2,4096]{3,2,1,0:T(2,128)(2,1)S(1)}, bf16[8,32,2,4096]{3,2,1,0:T(2,128)(2,1)}, u32[]{:S(2)}) %copy-start.2) | copy-done | bytes 4194328
  71.5 11.3 %shard_map.73 = (bf16[32,2,16,128]{3,2,1,0:T(8,128)(2,1)S(1)}, bf16[32,2,16,128]{3,2,1,0:T(8,128)(2,1)}) custom-call(s32[11]{0:T(128)S(1)} %stack.40.place, bf16[8,32,64,128]{3,2,1,0:T(8,128)(2,1)S(1)} %bitcast.20, bf16[8,32,64,128]{3,2,1,0:T(8,128)(2,1)S(1)} %bitcast.21, bf16[8,8,64,128]{3,2,1,0:T(8,128)(2,1)S(1)} %collective-permute-done.refs_2_, ...), custom_call_target="tpu_custom_call" | custom-call | flops 134217728 | bytes 2097152 | tf_op jit(solution)/shard_map/pallas_call | solution.py:188
  82.8 0.0 collective-permute-done.14.refs_3_
  82.8 2.2 %collective-permute-start.4 = (bf16[32,2,16,128]{3,2,1,0:T(8,128)(2,1)}, bf16[32,2,16,128]{3,2,1,0:T(8,128)(2,1)S(1)}, u32[]{:S(2)}, u32[]{:S(2)}) collective-permute-start(bf16[32,2,16,128]{3,2,1,0:T(8,128)(2,1)} %get-tuple-element.12), channel_id=1, source_target_pairs={{0,1},{1,0},{2,3},{3,2},{4,5},{5,4},{6,7},{7,6},{8,9},{9,8},{10,11... | collective-permute-start | bytes 786440 | tf_op jit(solution)/shard_map/ppermute | solution.py:367
  85.0 0.0 copy-done.8
  85.0 0.0 collective-permute-done.13.refs_1_
  85.0 1.7 %collective-permute-start.11 = (bf16[32,4,16,128]{3,2,1,0:T(8,128)(2,1)S(1)}, bf16[32,4,16,128]{3,2,1,0:T(8,128)(2,1)S(1)}, u32[]{:S(2)}, u32[]{:S(2)}) collective-permute-start(bf16[32,4,16,128]{3,2,1,0:T(8,128)(2,1)S(1)} %broadcast_select_fusion.refs_0_), channel_id=1, source_target_pairs={{0,2},{2,8},{4,6},{6,12},{8,10},{10,16},{12,14},{14,20},{16,18},{1... | collective-permute-start | bytes 1572872 | tf_op jit(solution)/shard_map/ppermute | solution.py:329
  86.7 0.0 collective-permute-done.18.refs_7_
  86.7 1.3 collective-permute-start.1
  88.0 0.0 collective-permute-done.9.refs_2_
  88.0 0.4 collective-permute-start.3
  88.3 3.4 %collective-permute-done.4.refs_4_ = bf16[32,2,16,128]{3,2,1,0:T(8,128)(2,1)S(1)} collective-permute-done((bf16[32,2,16,128]{3,2,1,0:T(8,128)(2,1)}, bf16[32,2,16,128]{3,2,1,0:T(8,128)(2,1)S(1)}, u32[]{:S(2)}, u32[]{:S(2)}) %collective-permute-start.4) | collective-permute-done | bytes 262176 | tf_op jit(solution)/shard_map/ppermute | solution.py:367
  91.7 0.7 collective-permute-start.10
  92.4 0.0 collective-permute-done.17.refs_5_
  92.4 1.3 collective-permute-start.5
  93.7 13.8 %shard_map.76.refs_4_ = f32[4096,128]{1,0:T(8,128)} custom-call(s32[4]{0:T(128)S(1)} %broadcast_select_fusion.1.place, bf16[32,4,16,128]{3,2,1,0:T(8,128)(2,1)S(1)} %get-tuple-element.15.refs_0_, bf16[32,4,16,128]{3,2,1,0:T(8,128)(2,1)} %collective-permute-done.13.refs_1_, bf16[32,4,16,128]{3,2,1,0:T(8,128)(2,1)} %collective-permute-done.12.refs_2_, ...), custom_call_target="tpu_custom_call" | custom-call | flops 8589934592 | bytes 8388608 | tf_op jit(solution)/shard_map/pallas_call | solution.py:294
  107.5 0.0 collective-permute-done.11.refs_3_
  107.5 1.5 %collective-permute-start.7 = (bf16[32,2,16,128]{3,2,1,0:T(8,128)(2,1)S(1)}, bf16[32,2,16,128]{3,2,1,0:T(8,128)(2,1)S(1)}, u32[]{:S(2)}, u32[]{:S(2)}) collective-permute-start(bf16[32,2,16,128]{3,2,1,0:T(8,128)(2,1)S(1)} %collective-permute-done.4.refs_4_), channel_id=1, source_target_pairs={{0,2},{2,8},{4,6},{6,12},{8,10},{10,16},{12,14},{14,20},{16,18},{1... | collective-permute-start | bytes 786440 | tf_op jit(solution)/shard_map/ppermute | solution.py:329
  109.0 0.0 collective-permute-done.1.refs_2_
  109.0 0.0 collective-permute-start.2
  109.0 1.3 collective-permute-done.5.refs_6_
  110.3 0.0 collective-permute-start.6
  110.3 0.0 collective-permute-done.10.refs_1_
  110.3 1.6 %copy-done.7 = f32[4096,128]{1,0:T(8,128)S(1)} copy-done((f32[4096,128]{1,0:T(8,128)S(1)}, f32[4096,128]{1,0:T(8,128)}, u32[]{:S(2)}) %copy-start.7) | copy-done | bytes 2097176
  111.9 11.2 %shard_map.77.refs_8_ = f32[4096,128]{1,0:T(8,128)S(1)} custom-call(s32[4]{0:T(128)S(1)} %broadcast_select_fusion.1.place, bf16[32,4,16,128]{3,2,1,0:T(8,128)(2,1)S(1)} %broadcast_select_fusion.refs_0_, bf16[32,4,16,128]{3,2,1,0:T(8,128)(2,1)S(1)} %collective-permute-done.10.refs_1_, ...), custom_call_target="tpu_custom_call", output_to_operand_aliasing={{}: (5, {})} | custom-call | flops 8589934592 | bytes 8388608 | tf_op jit(solution)/shard_map/pallas_call | solution.py:294
  123.1 0.0 collective-permute-done.3.refs_3_
  123.1 0.0 collective-permute-done.2.refs_1_
  123.1 0.0 collective-permute-done.7.refs_7_
  123.1 0.0 collective-permute-done.6.refs_5_
  123.1 11.3 %shard_map.78 = f32[2,8,4,8,8,128]{5,4,3,2,1,0:T(8,128)} custom-call(s32[4]{0:T(128)S(1)} %broadcast_select_fusion.1.place, bf16[32,2,16,128]{3,2,1,0:T(8,128)(2,1)S(1)} %get-tuple-element.11.refs_0_, bf16[32,2,16,128]{3,2,1,0:T(8,128)(2,1)S(1)} %collective-permute-done.2.refs_1_, bf16[32,2,16,128]{3,2,1,0:T(8,128)(2,1)S(1)} %collective-permute-done.1.refs_2_, ...), custom_call_target="tpu_custom_call" | custom-call | flops 8589934592 | bytes 8388608 | tf_op jit(solution)/shard_map/pallas_call | solution.py:294
  (6 shorter events, 0.0 us)
Async XLA Ops:
  0.1 2.2 %copy-start = (bf16[8,32,2,4096]{3,2,1,0:T(2,128)(2,1)S(1)}, bf16[8,32,2,4096]{3,2,1,0:T(2,128)(2,1)}, u32[]{:S(2)}) copy-start(bf16[8,32,2,4096]{3,2,1,0:T(2,128)(2,1)} %param.7) | copy-start | bytes 12582916
  2.3 1.0 copy-start.3
  3.3 0.9 copy-start.5
  19.6 5.9 %copy-start.4 = (f32[352,256]{1,0:T(8,128)S(1)}, f32[352,256]{1,0:T(8,128)}, u32[]{:S(2)}) copy-start(f32[352,256]{1,0:T(8,128)} %constant.47.clone.refs_4_.refs_3_) | copy-start | bytes 1081348
  19.6 5.9 %copy-start.6 = (f32[16,4096]{1,0:T(8,128)S(1)}, f32[16,4096]{1,0:T(8,128)}, u32[]{:S(2)}) copy-start(f32[16,4096]{1,0:T(8,128)} %refs_2_.3) | copy-start | bytes 786436
  19.6 24.8 %collective-permute-start.15 = (bf16[32,4,16,128]{3,2,1,0:T(8,128)(2,1)S(1)}, bf16[32,4,16,128]{3,2,1,0:T(8,128)(2,1)S(1)}, u32[]{:S(2)}, u32[]{:S(2)}) collective-permute-start(bf16[32,4,16,128]{3,2,1,0:T(8,128)(2,1)S(1)} %get-tuple-element.16), channel_id=1, source_target_pairs={{0,1},{1,0},{2,3},{3,2},{4,5},{5,4},{6,7},{7,6},{8,9},{9,8},{10,11... | collective-permute-start | bytes 1572872 | tf_op jit(solution)/shard_map/ppermute | solution.py:365
  24.0 44.9 %collective-permute-start = (bf16[8,8,64,128]{3,2,1,0:T(8,128)(2,1)}, bf16[8,8,64,128]{3,2,1,0:T(8,128)(2,1)S(1)}, u32[]{:S(2)}, u32[]{:S(2)}) collective-permute-start(bf16[8,8,64,128]{3,2,1,0:T(8,128)(2,1)} %constant_dynamic-slice_fusion), channel_id=1, source_target_pairs={{0,1},{1,0},{2,3},{3,2},{4,5},{5,4},{6,7},{7,6},{8,9},{9,8},{10,11... | collective-permute-start | bytes 3145736 | tf_op jit(solution)/shard_map/ppermute | solution.py:350
  24.1 24.6 %collective-permute-start.12 = (bf16[32,4,16,128]{3,2,1,0:T(8,128)(2,1)S(1)}, bf16[32,4,16,128]{3,2,1,0:T(8,128)(2,1)}, u32[]{:S(2)}, u32[]{:S(2)}) collective-permute-start(bf16[32,4,16,128]{3,2,1,0:T(8,128)(2,1)S(1)} %get-tuple-element.15.refs_0_), channel_id=1, source_target_pairs={{0,4},{2,6},{4,8},{6,10},{8,12},{10,14},{12,16},{14,18},{16,20},{1... | collective-permute-start | bytes 1572872 | tf_op jit(solution)/shard_map/ppermute | solution.py:322
  25.5 2.2 %copy-start.1 = (bf16[8,32,2,4096]{3,2,1,0:T(2,128)(2,1)S(1)}, bf16[8,32,2,4096]{3,2,1,0:T(2,128)(2,1)}, u32[]{:S(2)}) copy-start(bf16[8,32,2,4096]{3,2,1,0:T(2,128)(2,1)} %param.7) | copy-start | bytes 12582916
  43.1 22.9 %collective-permute-start.8 = (bf16[32,4,16,128]{3,2,1,0:T(8,128)(2,1)S(1)}, bf16[32,4,16,128]{3,2,1,0:T(8,128)(2,1)S(1)}, u32[]{:S(2)}, u32[]{:S(2)}) collective-permute-start(bf16[32,4,16,128]{3,2,1,0:T(8,128)(2,1)S(1)} %get-tuple-element.14), channel_id=1, source_target_pairs={{0,1},{2,3},{4,5},{6,7},{8,9},{10,11},{12,13},{14,15},{16,17},{18,... | collective-permute-start | bytes 1572872 | tf_op jit(solution)/shard_map/ppermute | solution.py:366
  44.4 23.2 %collective-permute-start.16 = (bf16[32,4,16,128]{3,2,1,0:T(8,128)(2,1)S(1)}, bf16[32,4,16,128]{3,2,1,0:T(8,128)(2,1)}, u32[]{:S(2)}, u32[]{:S(2)}) collective-permute-start(bf16[32,4,16,128]{3,2,1,0:T(8,128)(2,1)S(1)} %collective-permute-done.15.refs_4_), channel_id=1, source_target_pairs={{0,4},{2,6},{4,8},{6,10},{8,12},{10,14},{12,16},{14,18},{16,20},{1... | collective-permute-start | bytes 1572872 | tf_op jit(solution)/shard_map/ppermute | solution.py:322
  45.8 37.0 %collective-permute-start.14 = (bf16[32,4,16,128]{3,2,1,0:T(8,128)(2,1)S(1)}, bf16[32,4,16,128]{3,2,1,0:T(8,128)(2,1)}, u32[]{:S(2)}, u32[]{:S(2)}) collective-permute-start(bf16[32,4,16,128]{3,2,1,0:T(8,128)(2,1)S(1)} %get-tuple-element.15.refs_0_), channel_id=1, source_target_pairs={{0,2},{2,8},{4,6},{6,12},{8,10},{10,16},{12,14},{14,20},{16,18},{1... | collective-permute-start | bytes 1572872 | tf_op jit(solution)/shard_map/ppermute | solution.py:329
  48.7 38.0 %collective-permute-start.18 = (bf16[32,4,16,128]{3,2,1,0:T(8,128)(2,1)S(1)}, bf16[32,4,16,128]{3,2,1,0:T(8,128)(2,1)}, u32[]{:S(2)}, u32[]{:S(2)}) collective-permute-start(bf16[32,4,16,128]{3,2,1,0:T(8,128)(2,1)S(1)} %collective-permute-done.15.refs_4_), channel_id=1, source_target_pairs={{0,2},{2,8},{4,6},{6,12},{8,10},{10,16},{12,14},{14,20},{16,18},{1... | collective-permute-start | bytes 1572872 | tf_op jit(solution)/shard_map/ppermute | solution.py:329
  66.0 18.9 %collective-permute-start.13 = (bf16[32,4,16,128]{3,2,1,0:T(8,128)(2,1)}, bf16[32,4,16,128]{3,2,1,0:T(8,128)(2,1)}, u32[]{:S(2)}, u32[]{:S(2)}) collective-permute-start(bf16[32,4,16,128]{3,2,1,0:T(8,128)(2,1)} %collective-permute-done.12.refs_2_), channel_id=1, source_target_pairs={{0,2},{2,0},{4,6},{6,4},{8,10},{10,8},{12,14},{14,12},{16,18},{18,... | collective-permute-start | bytes 1572872 | tf_op jit(solution)/shard_map/ppermute | solution.py:328
  67.7 20.3 %collective-permute-start.9 = (bf16[32,4,16,128]{3,2,1,0:T(8,128)(2,1)S(1)}, bf16[32,4,16,128]{3,2,1,0:T(8,128)(2,1)}, u32[]{:S(2)}, u32[]{:S(2)}) collective-permute-start(bf16[32,4,16,128]{3,2,1,0:T(8,128)(2,1)S(1)} %broadcast_select_fusion.refs_0_), channel_id=1, source_target_pairs={{0,4},{2,6},{4,8},{6,10},{8,12},{10,14},{12,16},{14,18},{16,20},{1... | collective-permute-start | bytes 1572872 | tf_op jit(solution)/shard_map/ppermute | solution.py:322
  68.9 23.5 %collective-permute-start.17 = (bf16[32,4,16,128]{3,2,1,0:T(8,128)(2,1)}, bf16[32,4,16,128]{3,2,1,0:T(8,128)(2,1)}, u32[]{:S(2)}, u32[]{:S(2)}) collective-permute-start(bf16[32,4,16,128]{3,2,1,0:T(8,128)(2,1)} %collective-permute-done.16.refs_6_), channel_id=1, source_target_pairs={{0,2},{2,0},{4,6},{6,4},{8,10},{10,8},{12,14},{14,12},{16,18},{18,... | collective-permute-start | bytes 1572872 | tf_op jit(solution)/shard_map/ppermute | solution.py:328
  69.3 2.2 %copy-start.2 = (bf16[8,32,2,4096]{3,2,1,0:T(2,128)(2,1)S(1)}, bf16[8,32,2,4096]{3,2,1,0:T(2,128)(2,1)}, u32[]{:S(2)}) copy-start(bf16[8,32,2,4096]{3,2,1,0:T(2,128)(2,1)} %param.7) | copy-start | bytes 12582916
  71.5 13.5 %copy-start.8 = (s32[4]{0:T(128)S(1)}, s32[4]{0:T(128)}, u32[]{:S(2)}) copy-start(s32[4]{0:T(128)} %constant.48.clone) | copy-start | bytes 52
  82.8 9.0 %collective-permute-start.4 = (bf16[32,2,16,128]{3,2,1,0:T(8,128)(2,1)}, bf16[32,2,16,128]{3,2,1,0:T(8,128)(2,1)S(1)}, u32[]{:S(2)}, u32[]{:S(2)}) collective-permute-start(bf16[32,2,16,128]{3,2,1,0:T(8,128)(2,1)} %get-tuple-element.12), channel_id=1, source_target_pairs={{0,1},{1,0},{2,3},{3,2},{4,5},{5,4},{6,7},{7,6},{8,9},{9,8},{10,11... | collective-permute-start | bytes 786440 | tf_op jit(solution)/shard_map/ppermute | solution.py:367
  85.0 22.5 %collective-permute-start.11 = (bf16[32,4,16,128]{3,2,1,0:T(8,128)(2,1)S(1)}, bf16[32,4,16,128]{3,2,1,0:T(8,128)(2,1)S(1)}, u32[]{:S(2)}, u32[]{:S(2)}) collective-permute-start(bf16[32,4,16,128]{3,2,1,0:T(8,128)(2,1)S(1)} %broadcast_select_fusion.refs_0_), channel_id=1, source_target_pairs={{0,2},{2,8},{4,6},{6,12},{8,10},{10,16},{12,14},{14,20},{16,18},{1... | collective-permute-start | bytes 1572872 | tf_op jit(solution)/shard_map/ppermute | solution.py:329
  86.7 22.3 %collective-permute-start.1 = (bf16[32,2,16,128]{3,2,1,0:T(8,128)(2,1)S(1)}, bf16[32,2,16,128]{3,2,1,0:T(8,128)(2,1)S(1)}, u32[]{:S(2)}, u32[]{:S(2)}) collective-permute-start(bf16[32,2,16,128]{3,2,1,0:T(8,128)(2,1)S(1)} %get-tuple-element.11.refs_0_), channel_id=1, source_target_pairs={{0,4},{2,6},{4,8},{6,10},{8,12},{10,14},{12,16},{14,18},{16,20},{1... | collective-permute-start | bytes 786440 | tf_op jit(solution)/shard_map/ppermute | solution.py:322
  88.0 35.1 %collective-permute-start.3 = (bf16[32,2,16,128]{3,2,1,0:T(8,128)(2,1)S(1)}, bf16[32,2,16,128]{3,2,1,0:T(8,128)(2,1)S(1)}, u32[]{:S(2)}, u32[]{:S(2)}) collective-permute-start(bf16[32,2,16,128]{3,2,1,0:T(8,128)(2,1)S(1)} %get-tuple-element.11.refs_0_), channel_id=1, source_target_pairs={{0,2},{2,8},{4,6},{6,12},{8,10},{10,16},{12,14},{14,20},{16,18},{1... | collective-permute-start | bytes 786440 | tf_op jit(solution)/shard_map/ppermute | solution.py:329
  91.7 18.6 %collective-permute-start.10 = (bf16[32,4,16,128]{3,2,1,0:T(8,128)(2,1)}, bf16[32,4,16,128]{3,2,1,0:T(8,128)(2,1)S(1)}, u32[]{:S(2)}, u32[]{:S(2)}) collective-permute-start(bf16[32,4,16,128]{3,2,1,0:T(8,128)(2,1)} %collective-permute-done.9.refs_2_), channel_id=1, source_target_pairs={{0,2},{2,0},{4,6},{6,4},{8,10},{10,8},{12,14},{14,12},{16,18},{18,... | collective-permute-start | bytes 1572872 | tf_op jit(solution)/shard_map/ppermute | solution.py:328
  92.4 17.8 %collective-permute-start.5 = (bf16[32,2,16,128]{3,2,1,0:T(8,128)(2,1)S(1)}, bf16[32,2,16,128]{3,2,1,0:T(8,128)(2,1)S(1)}, u32[]{:S(2)}, u32[]{:S(2)}) collective-permute-start(bf16[32,2,16,128]{3,2,1,0:T(8,128)(2,1)S(1)} %collective-permute-done.4.refs_4_), channel_id=1, source_target_pairs={{0,4},{2,6},{4,8},{6,10},{8,12},{10,14},{12,16},{14,18},{16,20},{1... | collective-permute-start | bytes 786440 | tf_op jit(solution)/shard_map/ppermute | solution.py:322
  107.5 15.6 %collective-permute-start.7 = (bf16[32,2,16,128]{3,2,1,0:T(8,128)(2,1)S(1)}, bf16[32,2,16,128]{3,2,1,0:T(8,128)(2,1)S(1)}, u32[]{:S(2)}, u32[]{:S(2)}) collective-permute-start(bf16[32,2,16,128]{3,2,1,0:T(8,128)(2,1)S(1)} %collective-permute-done.4.refs_4_), channel_id=1, source_target_pairs={{0,2},{2,8},{4,6},{6,12},{8,10},{10,16},{12,14},{14,20},{16,18},{1... | collective-permute-start | bytes 786440 | tf_op jit(solution)/shard_map/ppermute | solution.py:329
  109.0 14.1 %collective-permute-start.2 = (bf16[32,2,16,128]{3,2,1,0:T(8,128)(2,1)S(1)}, bf16[32,2,16,128]{3,2,1,0:T(8,128)(2,1)S(1)}, u32[]{:S(2)}, u32[]{:S(2)}) collective-permute-start(bf16[32,2,16,128]{3,2,1,0:T(8,128)(2,1)S(1)} %collective-permute-done.1.refs_2_), channel_id=1, source_target_pairs={{0,2},{2,0},{4,6},{6,4},{8,10},{10,8},{12,14},{14,12},{16,18},{18,... | collective-permute-start | bytes 786440 | tf_op jit(solution)/shard_map/ppermute | solution.py:328
  110.3 12.8 %collective-permute-start.6 = (bf16[32,2,16,128]{3,2,1,0:T(8,128)(2,1)S(1)}, bf16[32,2,16,128]{3,2,1,0:T(8,128)(2,1)S(1)}, u32[]{:S(2)}, u32[]{:S(2)}) collective-permute-start(bf16[32,2,16,128]{3,2,1,0:T(8,128)(2,1)S(1)} %collective-permute-done.5.refs_6_), channel_id=1, source_target_pairs={{0,2},{2,0},{4,6},{6,4},{8,10},{10,8},{12,14},{14,12},{16,18},{18,... | collective-permute-start | bytes 786440 | tf_op jit(solution)/shard_map/ppermute | solution.py:328
  110.3 1.6 %copy-start.7 = (f32[4096,128]{1,0:T(8,128)S(1)}, f32[4096,128]{1,0:T(8,128)}, u32[]{:S(2)}) copy-start(f32[4096,128]{1,0:T(8,128)} %shard_map.76.refs_4_) | copy-start | bytes 6291460

commit v4 on v3

v4 whole, which is shorter than its diff:
```python
import functools
import math

import jax
import jax.numpy as jnp
import numpy as np
from jax import lax
from jax.experimental import pallas as pl
from jax.experimental.pallas import tpu as pltpu
from jax.sharding import PartitionSpec as P

NCH = 4096
CHANS = 2048
TAPS = 16
VISITS = 4
H = 32
LANES = 128
ROWS = 2 * H
K2 = CHANS // H
STEP = 8
TILE = 16
MEMBERS = 4
PAD = 8
SUB = 8
BF16 = jnp.bfloat16
F32 = jnp.float32


def angles(rows, columns, modulus):
    turns = np.outer(rows, columns) % modulus
    return turns.astype(np.float64) * (2.0 * math.pi / modulus)


def stage_one_table():
    theta = angles(np.arange(H), np.arange(H), H)
    cosine, sine = np.cos(theta), np.sin(theta)
    table = np.zeros((2, H, H, 2))
    table[0, :, :, 0], table[0, :, :, 1] = cosine, sine
    table[1, :, :, 0], table[1, :, :, 1] = -sine, cosine
    return np.pad(table.reshape(ROWS, ROWS), ((0, 0), (0, 2 * LANES - ROWS)))


def turn_table():
    theta = angles(np.arange(H), np.arange(LANES), NCH)
    return np.concatenate([np.cos(theta), np.sin(theta)], axis=1)


def stage_two_table(groups):
    theta = angles(np.arange(K2), np.arange(LANES), LANES)
    cosine, sine = np.cos(theta) / math.sqrt(NCH), np.sin(theta) / math.sqrt(NCH)
    real = np.concatenate([cosine, sine], 1).reshape(groups, 1, K2 // groups, 2 * LANES)
    imag = np.concatenate([-sine, cosine], 1).reshape(groups, 1, K2 // groups, 2 * LANES)
    return np.concatenate([real, imag], 1).reshape(2 * K2, 2 * LANES)


def tables(groups):
    two = stage_two_table(groups)
    rolled = np.roll(two, K2, axis=0)
    return np.concatenate([stage_one_table(), turn_table(), two, rolled]).astype(np.float32)


def halves(value):
    high = value.astype(BF16)
    return high, (value - high.astype(F32)).astype(BF16)


def dot(left, right):
    return lax.dot_general(left, right, (((1,), (0,)), ((), ())), preferred_element_type=F32)


def dot_nt(left, right):
    return lax.dot_general(left, right, (((1,), (1,)), ((), ())), preferred_element_type=F32)


def spectra_kernel(groups, parts, out_frames, place, *refs):
    part_refs, refs = refs[: len(parts)], refs[len(parts) :]
    taps_ref, table_ref = refs[:2]
    outs, (taps, one, two, ext, filtered, turned, staged) = refs[2:-7], refs[-7:]
    step, steps, members = pl.program_id(0), pl.num_programs(0), part_refs[0].shape[0]
    per_group = K2 // groups
    share = LANES // out_frames
    tiles = H // share
    pairs = tiles // 2
    frame_rows, row_rows = ROWS + PAD, tiles * TILE + PAD

    @pl.when(step == 0)
    def _():
        for h in range(H):
            for half in range(TAPS // SUB):
                tile = taps_ref[pl.ds(half * SUB, SUB), pl.ds(h * LANES, LANES)]
                for r in range(2):
                    taps[pl.ds(half * SUB * ROWS + 2 * h + r, SUB, stride=ROWS), :] = tile
        high, low = halves(table_ref[:ROWS, :ROWS])
        one[...] = jnp.concatenate([high, high, low], axis=1)
        start = pl.multiple_of(ROWS + H + place[1] * 2 * K2, SUB)
        high, low = halves(table_ref[pl.ds(start, 2 * K2), :])
        two[0] = high
        two[1] = low

    def load(member):
        for number, (frames, ref) in enumerate(zip(parts, part_refs)):
            start = place[2 + 3 * number + 1]
            valid = place[2 + 3 * number + 2]

            @pl.when(valid == 1)
            def _():
                for f in range(frames):
                    ext[member, start + f] = ref[member, f].astype(F32)

            @pl.when(valid == 0)
            def _():
                for f in range(frames):
                    ext[member, start + f] = jnp.zeros((ROWS, LANES), F32)

    def filter_rows(member, q):
        rows = pl.ds(pl.multiple_of(q * SUB, SUB), SUB)
        tap = [taps[pl.ds(pl.multiple_of(m * ROWS + q * SUB, SUB), SUB), :] for m in range(TAPS)]
        for f in range(out_frames):
            total = tap[0] * ext[member, f + 1, rows]
            for m in range(1, TAPS):
                total = total + tap[m] * ext[member, f + 1 + m, rows]
            filtered[member, f, rows] = total

    def first_stage(member):
        cosine = table_ref[ROWS : ROWS + H, :LANES]
        sine = table_ref[ROWS : ROWS + H, LANES:]
        for g in range(out_frames // STEP):
            block = jnp.concatenate([filtered[member, g * STEP + f] for f in range(STEP)], axis=1)
            high, low = halves(block)
            first = dot(one[...], jnp.concatenate([high, low, high], axis=0))
            for f in range(STEP):
                real = first[:H, f * LANES : (f + 1) * LANES]
                imag = first[H:, f * LANES : (f + 1) * LANES]
                at = (g * STEP + f) * frame_rows
                turned[member, at : at + H, :] = real * cosine + imag * sine
                turned[member, at + H : at + ROWS, :] = imag * cosine - real * sine

    def second_stage(member, pair):
        rows = []
        for k1 in range(2 * pair * share, 2 * (pair + 1) * share):
            for f in range(0, out_frames, SUB):
                rows.append(
                    jnp.concatenate(
                        [turned[member, pl.ds(f * frame_rows + p * H + k1, SUB, stride=frame_rows), :] for p in range(2)],
                        axis=1,
                    )
                )
        high, low = halves(jnp.concatenate(rows, axis=0))
        spectrum = dot_nt(two[0], high) + dot_nt(two[1], high) + dot_nt(two[0], low)
        for k in range(2):
            for t in range(groups):
                for p in range(2):
                    for k2 in range(0, per_group, SUB):
                        row = (t * 2 + p) * per_group + k2
                        start = (t * per_group + k2) * row_rows + (2 * pair + k) * TILE + p * SUB
                        staged[pl.ds(start + step * members + member, SUB, stride=row_rows), :] = spectrum[
                            row : row + SUB, k * LANES : (k + 1) * LANES
                        ]

    def write():
        at = 0
        for out in outs:

            def write_row(k2, carry):
                for k in range(tiles):
                    start = pl.multiple_of((at + k2) * row_rows + k * TILE, PAD)
                    out[k2, k] = staged[pl.ds(start, TILE), :].astype(BF16)
                return carry

            lax.fori_loop(0, out.shape[0], write_row, 0, unroll=2)
            at += out.shape[0]

    @pl.when(place[0] == 1)
    def _():
        for member in range(members):
            load(member)

        def filter_one(index, carry):
            filter_rows(index // (ROWS // SUB), index % (ROWS // SUB))
            return carry

        lax.fori_loop(0, members * (ROWS // SUB), filter_one, 0)
        for member in range(members):
            first_stage(member)
        for member in range(members):
            for pair in range(pairs):
                second_stage(member, pair)

        @pl.when(step == steps - 1)
        def _():
            write()


def after(value, *others):
    return lax.optimization_barrier((value, *others))[0]


def spectra(parts, out_frames, fir_taps, groups, sizes, run=1, order=0, wait=(), cost=10**6):
    signals = parts[0][0].shape[0]
    numbers = [run, order] + [v for part in parts for v in part[2:]]
    place = jnp.stack([jnp.asarray(v, jnp.int32) for v in numbers])
    place = after(place, *wait)
    table = tables(groups)
    tiles = H * out_frames // LANES
    whole = lambda shape: pl.BlockSpec(shape, lambda s, place: (0,) * len(shape))
    in_specs = [
        pl.BlockSpec(
            (MEMBERS, part[1], ROWS, LANES), functools.partial(lambda n, s, place: (s, place[2 + 3 * n], 0, 0), n)
        )
        for n, part in enumerate(parts)
    ]
    in_specs += [whole((TAPS, NCH)), whole(table.shape)]
    shapes = [(n, tiles, TILE, LANES) for n in sizes]
    return pl.pallas_call(
        functools.partial(spectra_kernel, groups, tuple(p[1] for p in parts), out_frames),
        grid_spec=pltpu.PrefetchScalarGridSpec(
            num_scalar_prefetch=1,
            grid=(signals // MEMBERS,),
            in_specs=in_specs,
            out_specs=[whole(shape) for shape in shapes],
            scratch_shapes=[
                pltpu.VMEM((TAPS * ROWS, LANES), F32),
                pltpu.VMEM((ROWS, 3 * ROWS), BF16),
                pltpu.VMEM((2, 2 * K2, 2 * LANES), BF16),
                pltpu.VMEM((MEMBERS, TAPS + out_frames, ROWS, LANES), F32),
                pltpu.VMEM((MEMBERS, out_frames, ROWS, LANES), F32),
                pltpu.VMEM((MEMBERS, out_frames * (ROWS + PAD), LANES), F32),
                pltpu.VMEM((K2 * (tiles * TILE + PAD), LANES), F32),
            ],
        ),
        out_shape=[jax.ShapeDtypeStruct(shape, BF16) for shape in shapes],
        compiler_params=pltpu.CompilerParams(vmem_limit_bytes=32 << 20),
        cost_estimate=pl.CostEstimate(
            flops=cost, bytes_accessed=0, transcendentals=0
        ),
    )(place, *[part[0] for part in parts], fir_taps, table)


def correlate_kernel(pieces, per_group, scale, add, last, place, *refs):
    refs = list(refs)
    sums = refs.pop() if last else None
    out = refs.pop()
    before = refs.pop() if add else None
    if not last:
        sums = out
    half = per_group // 2
    lane = lax.broadcasted_iota(jnp.int32, (SUB, LANES), 1)
    first_tile = lane < LANES // 2
    real_lane = lane % TILE < SUB
    sign = jnp.where(real_lane, 1.0, -1.0).astype(F32)
    for number, piece in enumerate(pieces):
        tiles, piece = piece
        share = H // tiles
        where = lax.broadcasted_iota(jnp.int32, (TILE, LANES), 1) // (LANES // share)

        def pair(index, carry):
            k2 = index // tiles
            k1 = index % tiles
            own, other = [], []
            for position in range(len(piece[0])):
                rows = []
                for tile in range(2):
                    array, row, column = piece[0][position]
                    a = refs[array][row + tile * half + k2, column + k1]
                    rows += [jnp.where(where == c, a, jnp.zeros_like(a)) for c in range(share)]
                own.append(jnp.concatenate(rows, axis=0))
                rows = []
                for tile in range(2):
                    for visit in range(VISITS):
                        array, row, column = piece[visit][position]
                        rows.append(refs[array][row + tile * half + k2, column + k1])
                other.append(jnp.concatenate(rows, axis=0))
            product = dot_nt(jnp.concatenate(own, axis=1), jnp.concatenate(other, axis=1))
            for c in range(share):
                value = []
                for p in range(2):
                    at = [((tile * share + c) * 2 + p) * SUB for tile in range(2)]
                    value.append(
                        jnp.where(first_tile, product[at[0] : at[0] + SUB], product[at[1] : at[1] + SUB])
                    )
                turned = jnp.where(
                    real_lane, pltpu.roll(value[1], LANES - SUB, 1), pltpu.roll(value[1], SUB, 1)
                )
                total = value[0] * sign + turned
                channel = k2 // 4 * LANES + k2 % 4 * H + k1 * share + c
                rows = pl.ds(pl.multiple_of(channel * SUB, SUB), SUB)
                if number:
                    total = total + sums[rows, :]
                elif add:
                    total = total + before[rows, :]
                sums[rows, :] = total
            return carry

        lax.fori_loop(0, half * tiles, pair, 0, unroll=16)
    if not last:
        return

    def finish(index, carry):
        block = index // SUB
        signal = index % SUB
        value = sums[pl.ds(block * LANES * SUB + signal, LANES, stride=SUB), :]
        value = jnp.transpose(value * scale)
        at = 0
        for tile in range(2):
            for visit in range(VISITS):
                for part in range(2):
                    out[part, signal, place[visit], tile * (half // 4) + block] = value[at : at + SUB]
                    at += SUB
        return carry

    lax.fori_loop(0, half // 4 * SUB, finish, 0)


def correlate(arrays, pieces, per_group, place, scale, before, last, wait=()):
    signals = TILE // 2
    rows = per_group // 2 * H * SUB
    place = after(place, *wait)
    shape = (2, signals, VISITS, per_group // 4, SUB, LANES) if last else (rows, LANES)
    operands = list(arrays) + ([] if before is None else [before])
    whole = lambda shape: pl.BlockSpec(shape, lambda i, place: (0,) * len(shape))
    return pl.pallas_call(
        functools.partial(correlate_kernel, pieces, per_group, scale, before is not None, last),
        grid_spec=pltpu.PrefetchScalarGridSpec(
            num_scalar_prefetch=1,
            grid=(1,),
            in_specs=[whole(x.shape) for x in operands],
            out_specs=whole(shape),
            scratch_shapes=[pltpu.VMEM((rows, LANES), F32)] if last else [],
        ),
        out_shape=jax.ShapeDtypeStruct(shape, F32),
        compiler_params=pltpu.CompilerParams(vmem_limit_bytes=48 << 20),
        input_output_aliases={} if before is None or last else {len(operands): 0},
        cost_estimate=pl.CostEstimate(flops=6 * 10**9, bytes_accessed=0, transcendentals=0),
    )(place, *operands)


def stacked(voltage):
    s, f = voltage.shape[:2]
    return voltage.reshape(s, f, 2, H, LANES).transpose(0, 1, 3, 2, 4).reshape(s, f, ROWS, LANES)


def natural(out):
    parts, s, visits, i, t, lanes = out.shape
    return out.transpose(0, 1, 2, 4, 3, 5).reshape(parts, s, visits * t, i * lanes)


def shifted(block, axis, distance):
    size = lax.axis_size(axis)
    return lax.ppermute(block, axis, [(i, (i + distance) % size) for i in range(size)])


def farther(block):
    size = lax.axis_size("stn")
    rest = lax.ppermute(block, "stn", [(i, (i + 1 if i % 2 == 0 else i + 3) % size) for i in range(size)])
    return shifted(block, "stn", 2), rest


def exchanged(block):
    return lax.ppermute(block, "stn", [(i, i ^ 1) for i in range(lax.axis_size("stn"))])


def general(volts, fir_taps):
    groups = lax.axis_size("tm")
    frames = volts.shape[1]
    history = lax.ppermute(volts[:, frames - TAPS :], "tm", [(i, i + 1) for i in range(groups - 1)])
    parts = [(history, TAPS, 0, 0, 1)] + [(volts, TAPS, i, TAPS * (i + 1), 1) for i in range(frames // TAPS)]
    spectrum = spectra(parts, frames, fir_taps, groups, [K2])[0]
    spectrum = lax.all_to_all(spectrum, "tm", split_axis=0, concat_axis=0, tiled=True)
    tiles = spectrum.shape[1]
    return [([spectrum], [(tiles, [(0, K2 // groups * t, 0) for t in range(groups)])])]


def paired(volts, fir_taps, correlated):
    frames = volts.shape[1]
    me = lax.axis_index("tm")
    sizes = [K2 // 2, K2 // 2]
    swap = [(0, 1), (1, 0)]
    edge = TAPS // 2
    last = frames // edge
    edge_frames = lax.dynamic_slice_in_dim(volts, jnp.where(me == 0, frames - edge, 0), edge, 1)
    visiting = lax.ppermute(edge_frames, "tm", swap)
    own_a, away_a = spectra(
        [(volts, TAPS, 0, 0, me), (volts, TAPS, me, TAPS, 1)], TAPS, fir_taps, 2, sizes, 1, me, (edge_frames,)
    )
    got_a = lax.ppermute(away_a, "tm", swap)
    two_a, rest_a = farther(own_a)
    own_b, away_b = spectra(
        [(volts, TAPS, 0, 0, 1), (volts, TAPS, 1, TAPS, 1)], TAPS, fir_taps, 2, sizes, 1 - me, me, (own_a,)
    )
    got_b = lax.ppermute(away_b, "tm", [(0, 1)])
    pair_a = exchanged(two_a)
    own_c, away_c = spectra(
        [
            (volts, edge, jnp.where(me == 0, last - 2, 0), edge * me, 1),
            (volts, edge, jnp.where(me == 0, last - 1, 1), edge * me + edge, 1),
            (visiting, edge, 0, 2 * edge * (1 - me), 1),
        ],
        edge, fir_taps, 2, sizes, 1, me, (own_b, two_a, got_a), 9 * 10**9,
    )
    got_c = lax.ppermute(away_c, "tm", swap)
    two_g, rest_g = farther(got_a)
    pair_g = exchanged(two_g)
    own_c = after(own_c, two_g, pair_a, rest_a)
    rest = jnp.concatenate([jnp.where(me == 0, own_b, got_b), own_c, got_c], axis=1)
    two_r, rest_r = farther(rest)
    pair_r = exchanged(two_r)
    many, few = own_a.shape[1], own_c.shape[1]
    sums = correlated(
        [own_a, pair_a, two_a, rest_a, got_a, pair_g, two_g, rest_g], [(many, [(0, 0, 0), (1, 0, 0)])], None, False
    )
    return correlated(
        [rest, pair_r, two_r, rest_r], [(many, [(0, 0, 0)]), (few, [(0, 0, many), (0, 0, many + few)])], sums, True
    )


def general(volts, fir_taps, correlated):
    groups = lax.axis_size("tm")
    frames = volts.shape[1]
    history = lax.ppermute(volts[:, frames - TAPS :], "tm", [(i, i + 1) for i in range(groups - 1)])
    parts = [(history, TAPS, 0, 0, 1)] + [(volts, TAPS, i, TAPS * (i + 1), 1) for i in range(frames // TAPS)]
    spectrum = spectra(parts, frames, fir_taps, groups, [K2])[0]
    spectrum = lax.all_to_all(spectrum, "tm", split_axis=0, concat_axis=0, tiled=True)
    two, rest = farther(spectrum)
    spots = [(0, K2 // groups * t, 0) for t in range(groups)]
    return correlated([spectrum, exchanged(two), two, rest], [(spectrum.shape[1], spots)], None, True)


def local(voltage, fir_taps):
    groups = lax.axis_size("tm")
    even = lax.axis_index("stn") % 2 == 0
    place = jnp.where(even, jnp.array([0, 1, 2, 3]), jnp.array([0, 3, 2, 1])).astype(jnp.int32)
    scale = 1.0 / (groups * voltage.shape[1])

    def correlated(arrays, pieces, before, last, wait=()):
        laid = [
            (tiles, [[(VISITS * n + visit, row, column) for n, row, column in spots] for visit in range(VISITS)])
            for tiles, spots in pieces
        ]
        return correlate(arrays, laid, K2 // groups, place, scale, before, last, wait)

    run = paired if groups == 2 else general
    return natural(run(stacked(voltage), fir_taps, correlated))


def solution(mesh):
    return jax.shard_map(
        local,
        mesh=mesh,
        in_specs=(P("stn", "tm", None, None), P()),
        out_specs=P(None, "stn", None, "tm"),
        check_vma=False,
    )
```

time: 135 us -> 117 us (0.87)
  the two profiles are of different devices: /device:TPU:1 before, /device:TPU:2 now
where the time goes in v4:
time: 117 us; the launch traced here: 116 us
  Pallas kernels  51.9 us (44%)
  waiting for transfers between devices  38.7 us (33%)
  local copies, waits for them, and re-layouts  14.2 us (12%)
  starting transfers between devices  11.1 us (9%)
    pallas_call x3, Pallas kernels, spectra(): pl.pallas_call(functools.partial(spectra_kernel, groups, tuple((p[1] for...  33.2 us
    ppermute x3, waiting for transfers between devices, shifted(): lax.ppermute(block, axis, [(i, (i + distance) % size) for i in range(size)])  24.4 us
    pallas_call x2, Pallas kernels, correlate(): pl.pallas_call(functools.partial(correlate_kernel, pieces, per_group, sca...  18.7 us
    unnamed x28, local copies, waits for them, and re-layouts  11.7 us
    ppermute x3, waiting for transfers between devices, farther(): lax.ppermute(block, 'stn', [(i, (i + 1 if i % 2 == 0 else i + 3) % size)...  7.77 us
    ppermute x1, waiting for transfers between devices, paired(): got_c = lax.ppermute(away_c, 'tm', swap)  6.49 us
    ppermute x3, starting transfers between devices, shifted(): lax.ppermute(block, axis, [(i, (i + distance) % size) for i in range(size)])  4.67 us
  transfers between devices with their start and end apart: 13, of which 5 were waited for; matrix products, arithmetic and copies ran while one was open for 0% of the time, Pallas kernels for 34%

profile of v4, /device:TPU:2, one launch (start us, length us, event | category | flops | bytes accessed | tf_op | source)
XLA Modules:
  0.0 116.2 jit_solution(13694799231039990835)
XLA Ops:
  0.0 2.3 %constant_dynamic-slice_fusion = bf16[8,8,64,128]{3,2,1,0:T(8,128)(2,1)} fusion(bf16[8,32,64,128]{3,2,1,0:T(8,128)(2,1)} %bitcast.15, s32[]{:T(128)S(6)} %select_n.38), kind=kLoop, calls=%fused_computation.3 | loop fusion | bytes 2097156 | tf_op jit(solution)/shard_map/dynamic_slice | solution.py:380
  2.3 1.5 %collective-permute-start.3 = (bf16[8,8,64,128]{3,2,1,0:T(8,128)(2,1)}, bf16[8,8,64,128]{3,2,1,0:T(8,128)(2,1)S(1)}, u32[]{:S(2)}, u32[]{:S(2)}) collective-permute-start(bf16[8,8,64,128]{3,2,1,0:T(8,128)(2,1)} %constant_dynamic-slice_fusion), channel_id=1, source_target_pairs={{0,1},{1,0},{2,3},{3,2},{4,5},{5,4},{6,7},{7,6},{8,9},{9,8},{10,11... | collective-permute-start | bytes 3145736 | tf_op jit(solution)/shard_map/ppermute | solution.py:381
  3.8 0.1 stack.37.place
  3.9 0.0 copy-start
  3.9 2.2 %copy-done = bf16[8,32,2,4096]{3,2,1,0:T(2,128)(2,1)S(1)} copy-done((bf16[8,32,2,4096]{3,2,1,0:T(2,128)(2,1)S(1)}, bf16[8,32,2,4096]{3,2,1,0:T(2,128)(2,1)}, u32[]{:S(2)}) %copy-start) | copy-done | bytes 4194328
  6.1 0.0 copy-start.3
  6.1 1.0 copy-done.3
  7.0 0.0 copy-start.5
  7.0 0.9 copy-done.5
  8.0 0.0 copy-start.4
  8.0 0.0 copy-start.6
  8.0 12.8 %shard_map.73 = (bf16[32,4,16,128]{3,2,1,0:T(8,128)(2,1)S(1)}, bf16[32,4,16,128]{3,2,1,0:T(8,128)(2,1)}) custom-call(s32[8]{0:T(128)S(1)} %stack.37.place, bf16[8,32,64,128]{3,2,1,0:T(8,128)(2,1)S(1)} %bitcast.16, bf16[8,32,64,128]{3,2,1,0:T(8,128)(2,1)S(1)} %bitcast.17, f32[16,4096]{1,0:T(8,128)S(1)} %copy-done.5, f32[352,256]{1,0:T(8,128)S(1)} %copy-done.3), custom_call_target="tpu_custom_call" | custom-call | flops 1000000 | tf_op jit(solution)/shard_map/pallas_call | solution.py:214
  20.8 0.0 copy-start.7
  20.8 0.5 collective-permute-start.2
  21.3 1.5 %collective-permute-start.1 = (bf16[32,4,16,128]{3,2,1,0:T(8,128)(2,1)S(1)}, bf16[32,4,16,128]{3,2,1,0:T(8,128)(2,1)S(1)}, u32[]{:S(2)}, u32[]{:S(2)}) collective-permute-start(bf16[32,4,16,128]{3,2,1,0:T(8,128)(2,1)S(1)} %get-tuple-element.16.refs_0_), channel_id=1, source_target_pairs={{0,4},{2,6},{4,8},{6,10},{8,12},{10,14},{12,16},{14,18},{16,20},{1... | collective-permute-start | bytes 1572872 | tf_op jit(solution)/shard_map/ppermute | solution.py:349
  22.9 0.0 collective-permute-start.6
  22.9 0.1 stack.36.place
  23.0 0.0 copy-done.4
  23.0 0.0 copy-done.6
  23.0 0.0 copy-start.1
  23.0 2.2 %copy-done.1 = bf16[8,32,2,4096]{3,2,1,0:T(2,128)(2,1)S(1)} copy-done((bf16[8,32,2,4096]{3,2,1,0:T(2,128)(2,1)S(1)}, bf16[8,32,2,4096]{3,2,1,0:T(2,128)(2,1)}, u32[]{:S(2)}) %copy-start.1) | copy-done | bytes 4194328
  25.2 12.8 %shard_map.74 = (bf16[32,4,16,128]{3,2,1,0:T(8,128)(2,1)S(1)}, bf16[32,4,16,128]{3,2,1,0:T(8,128)(2,1)}) custom-call(s32[8]{0:T(128)S(1)} %stack.36.place, bf16[8,32,64,128]{3,2,1,0:T(8,128)(2,1)S(1)} %bitcast.18, bf16[8,32,64,128]{3,2,1,0:T(8,128)(2,1)S(1)} %bitcast.19, f32[16,4096]{1,0:T(8,128)S(1)} %copy-done.6, f32[352,256]{1,0:T(8,128)S(1)} %copy-done.4), custom_call_target="tpu_custom_call" | custom-call | flops 1000000 | tf_op jit(solution)/shard_map/pallas_call | solution.py:214
  38.0 0.0 copy-done.7
  38.0 2.1 %collective-permute-start = (bf16[32,4,16,128]{3,2,1,0:T(8,128)(2,1)}, bf16[32,4,16,128]{3,2,1,0:T(8,128)(2,1)}, u32[]{:S(2)}, u32[]{:S(2)}) collective-permute-start(bf16[32,4,16,128]{3,2,1,0:T(8,128)(2,1)} %get-tuple-element.19), channel_id=1, source_target_pairs={{0,1},{2,3},{4,5},{6,7},{8,9},{10,11},{12,13},{14,15},{16,17},{18,... | collective-permute-start | bytes 1572872 | tf_op jit(solution)/shard_map/ppermute | solution.py:390
  40.1 0.1 stack.43.place
  40.2 0.0 collective-permute-done.2.refs_4_
  40.2 0.0 collective-permute-done.1.refs_2_
  40.2 0.0 copy-start.9
  40.2 0.0 copy-start.13
  40.2 1.5 %collective-permute-start.4 = (bf16[32,4,16,128]{3,2,1,0:T(8,128)(2,1)}, bf16[32,4,16,128]{3,2,1,0:T(8,128)(2,1)}, u32[]{:S(2)}, u32[]{:S(2)}) collective-permute-start(bf16[32,4,16,128]{3,2,1,0:T(8,128)(2,1)} %collective-permute-done.2.refs_4_), channel_id=1, source_target_pairs={{0,4},{2,6},{4,8},{6,10},{8,12},{10,14},{12,16},{14,18},{16,20},{1... | collective-permute-start | bytes 1572872 | tf_op jit(solution)/shard_map/ppermute | solution.py:349
  41.8 1.4 %collective-permute-start.5 = (bf16[32,4,16,128]{3,2,1,0:T(8,128)(2,1)S(1)}, bf16[32,4,16,128]{3,2,1,0:T(8,128)(2,1)S(1)}, u32[]{:S(2)}, u32[]{:S(2)}) collective-permute-start(bf16[32,4,16,128]{3,2,1,0:T(8,128)(2,1)S(1)} %collective-permute-done.1.refs_2_), channel_id=1, source_target_pairs={{0,2},{2,0},{4,6},{6,4},{8,10},{10,8},{12,14},{14,12},{16,18},{18,... | collective-permute-start | bytes 1572872 | tf_op jit(solution)/shard_map/ppermute | solution.py:359
  43.2 0.0 collective-permute-done.3.refs_2_
  43.2 0.0 copy-start.2
  43.2 2.2 %copy-done.2 = bf16[8,32,2,4096]{3,2,1,0:T(2,128)(2,1)S(1)} copy-done((bf16[8,32,2,4096]{3,2,1,0:T(2,128)(2,1)S(1)}, bf16[8,32,2,4096]{3,2,1,0:T(2,128)(2,1)}, u32[]{:S(2)}) %copy-start.2) | copy-done | bytes 4194328
  45.4 7.5 %shard_map.75 = (bf16[32,2,16,128]{3,2,1,0:T(8,128)(2,1)S(1)}, bf16[32,2,16,128]{3,2,1,0:T(8,128)(2,1)S(1)}) custom-call(s32[11]{0:T(128)S(1)} %stack.43.place, bf16[8,32,64,128]{3,2,1,0:T(8,128)(2,1)S(1)} %bitcast.20, bf16[8,32,64,128]{3,2,1,0:T(8,128)(2,1)S(1)} %bitcast.21, bf16[8,8,64,128]{3,2,1,0:T(8,128)(2,1)S(1)} %collective-permute-done.3.refs_2_, ...), custom_call_target="tpu_custom_call" | custom-call | flops 8999999488 | tf_op jit(solution)/shard_map/pallas_call | solution.py:214
  52.9 0.0 copy-done.9
  52.9 0.1 collective-permute-start.7
  53.0 0.0 collective-permute-done
  53.0 0.1 broadcast_select_fusion
  53.1 0.0 collective-permute-done.6.refs_3_
  53.1 1.6 %collective-permute-done.4.refs_6_ = bf16[32,4,16,128]{3,2,1,0:T(8,128)(2,1)} collective-permute-done((bf16[32,4,16,128]{3,2,1,0:T(8,128)(2,1)}, bf16[32,4,16,128]{3,2,1,0:T(8,128)(2,1)}, u32[]{:S(2)}, u32[]{:S(2)}) %collective-permute-start.4) | collective-permute-done | bytes 524320 | tf_op jit(solution)/shard_map/ppermute | solution.py:349
  54.7 0.0 collective-permute-done.5.refs_1_
  54.7 0.0 copy-start.11
  54.7 6.5 %collective-permute-done.7 = bf16[32,2,16,128]{3,2,1,0:T(8,128)(2,1)S(1)} collective-permute-done((bf16[32,2,16,128]{3,2,1,0:T(8,128)(2,1)S(1)}, bf16[32,2,16,128]{3,2,1,0:T(8,128)(2,1)S(1)}, u32[]{:S(2)}, u32[]{:S(2)}) %collective-permute-start.7) | collective-permute-done | bytes 262176 | tf_op jit(solution)/shard_map/ppermute | solution.py:400
  61.2 0.1 pad_maximum_fusion.refs_0_
  61.3 1.6 %collective-permute-start.8 = (bf16[32,8,16,128]{3,2,1,0:T(8,128)(2,1)S(1)}, bf16[32,8,16,128]{3,2,1,0:T(8,128)(2,1)S(1)}, u32[]{:S(2)}, u32[]{:S(2)}) collective-permute-start(bf16[32,8,16,128]{3,2,1,0:T(8,128)(2,1)S(1)} %pad_maximum_fusion.refs_0_), channel_id=1, source_target_pairs={{0,4},{2,6},{4,8},{6,10},{8,12},{10,14},{12,16},{14,18},{16,20},{1... | collective-permute-start | bytes 3145736 | tf_op jit(solution)/shard_map/ppermute | solution.py:349
  62.9 0.0 collective-permute-start.12
  62.9 0.8 collective-permute-start.11
  63.7 0.0 collective-permute-start.10
  63.7 22.8 %collective-permute-done.8.refs_2_ = bf16[32,8,16,128]{3,2,1,0:T(8,128)(2,1)S(1)} collective-permute-done((bf16[32,8,16,128]{3,2,1,0:T(8,128)(2,1)S(1)}, bf16[32,8,16,128]{3,2,1,0:T(8,128)(2,1)S(1)}, u32[]{:S(2)}, u32[]{:S(2)}) %collective-permute-start.8) | collective-permute-done | bytes 1048608 | tf_op jit(solution)/shard_map/ppermute | solution.py:349
  86.5 0.0 copy-done.11
  86.5 0.0 collective-permute-start.9
  86.5 0.0 copy-done.13
  86.5 6.5 %collective-permute-done.12.refs_7_ = bf16[32,4,16,128]{3,2,1,0:T(8,128)(2,1)} collective-permute-done((bf16[32,4,16,128]{3,2,1,0:T(8,128)(2,1)}, bf16[32,4,16,128]{3,2,1,0:T(8,128)(2,1)}, u32[]{:S(2)}, u32[]{:S(2)}) %collective-permute-start.12) | collective-permute-done | bytes 524320 | tf_op jit(solution)/shard_map/ppermute | solution.py:354
  93.1 0.0 collective-permute-done.11.refs_5_
  93.1 0.0 copy-start.8
  93.1 1.0 copy-done.8
  94.1 1.0 copy-done.10
  95.2 0.0 copy-start.12
  95.2 1.0 copy-done.12
  96.2 6.8 %shard_map.76.refs_4_ = f32[4096,128]{1,0:T(8,128)} custom-call(s32[4]{0:T(128)S(1)} %broadcast_select_fusion.1.place, bf16[32,4,16,128]{3,2,1,0:T(8,128)(2,1)S(1)} %copy-done.8, bf16[32,4,16,128]{3,2,1,0:T(8,128)(2,1)S(1)} %copy-done.12, bf16[32,4,16,128]{3,2,1,0:T(8,128)(2,1)S(1)} %copy-done.10, bf16[32,4,16,128]{3,2,1,0:T(8,128)(2,1)} %collective-permute-done.6.refs_3_, ...), custom_call_target="tpu_custom_call" | custom-call | flops 6000000000 | tf_op jit(solution)/shard_map/pallas_call | solution.py:321
  103.0 1.2 %collective-permute-done.10.refs_3_ = bf16[32,8,16,128]{3,2,1,0:T(8,128)(2,1)S(1)} collective-permute-done((bf16[32,8,16,128]{3,2,1,0:T(8,128)(2,1)S(1)}, bf16[32,8,16,128]{3,2,1,0:T(8,128)(2,1)S(1)}, u32[]{:S(2)}, u32[]{:S(2)}) %collective-permute-start.10) | collective-permute-done | bytes 1048608 | tf_op jit(solution)/shard_map/ppermute | solution.py:354
  104.2 0.0 collective-permute-done.9.refs_1_
  104.2 12.0 %shard_map.77 = f32[2,8,4,8,8,128]{5,4,3,2,1,0:T(8,128)} custom-call(s32[4]{0:T(128)S(1)} %broadcast_select_fusion.1.place, bf16[32,8,16,128]{3,2,1,0:T(8,128)(2,1)S(1)} %pad_maximum_fusion.refs_0_, bf16[32,8,16,128]{3,2,1,0:T(8,128)(2,1)} %collective-permute-done.9.refs_1_, bf16[32,8,16,128]{3,2,1,0:T(8,128)(2,1)S(1)} %collective-permute-done.8.refs_2_, ...), custom_call_target="tpu_custom_call" | custom-call | flops 6000000000 | tf_op jit(solution)/shard_map/pallas_call | solution.py:321
  (4 shorter events, 0.0 us)
Async XLA Ops:
  2.3 40.9 %collective-permute-start.3 = (bf16[8,8,64,128]{3,2,1,0:T(8,128)(2,1)}, bf16[8,8,64,128]{3,2,1,0:T(8,128)(2,1)S(1)}, u32[]{:S(2)}, u32[]{:S(2)}) collective-permute-start(bf16[8,8,64,128]{3,2,1,0:T(8,128)(2,1)} %constant_dynamic-slice_fusion), channel_id=1, source_target_pairs={{0,1},{1,0},{2,3},{3,2},{4,5},{5,4},{6,7},{7,6},{8,9},{9,8},{10,11... | collective-permute-start | bytes 3145736 | tf_op jit(solution)/shard_map/ppermute | solution.py:381
  3.9 2.2 %copy-start = (bf16[8,32,2,4096]{3,2,1,0:T(2,128)(2,1)S(1)}, bf16[8,32,2,4096]{3,2,1,0:T(2,128)(2,1)}, u32[]{:S(2)}) copy-start(bf16[8,32,2,4096]{3,2,1,0:T(2,128)(2,1)} %param.7) | copy-start | bytes 12582916
  6.1 1.0 copy-start.3
  7.0 0.9 copy-start.5
  8.0 15.0 %copy-start.4 = (f32[352,256]{1,0:T(8,128)S(1)}, f32[352,256]{1,0:T(8,128)}, u32[]{:S(2)}) copy-start(f32[352,256]{1,0:T(8,128)} %constant.48.clone.refs_3_.refs_4_) | copy-start | bytes 1081348
  8.0 15.0 %copy-start.6 = (f32[16,4096]{1,0:T(8,128)S(1)}, f32[16,4096]{1,0:T(8,128)}, u32[]{:S(2)}) copy-start(f32[16,4096]{1,0:T(8,128)} %refs_3_.3) | copy-start | bytes 786436
  20.8 17.2 %copy-start.7 = (bf16[32,4,16,128]{3,2,1,0:T(8,128)(2,1)}, bf16[32,4,16,128]{3,2,1,0:T(8,128)(2,1)S(1)}, u32[]{:S(2)}) copy-start(bf16[32,4,16,128]{3,2,1,0:T(8,128)(2,1)S(1)} %get-tuple-element.16.refs_0_) | copy-start | bytes 1572868
  20.8 19.3 %collective-permute-start.2 = (bf16[32,4,16,128]{3,2,1,0:T(8,128)(2,1)}, bf16[32,4,16,128]{3,2,1,0:T(8,128)(2,1)}, u32[]{:S(2)}, u32[]{:S(2)}) collective-permute-start(bf16[32,4,16,128]{3,2,1,0:T(8,128)(2,1)} %get-tuple-element.20), channel_id=1, source_target_pairs={{0,1},{1,0},{2,3},{3,2},{4,5},{5,4},{6,7},{7,6},{8,9},{9,8},{10,11... | collective-permute-start | bytes 1572872 | tf_op jit(solution)/shard_map/ppermute | solution.py:385
  21.3 18.8 %collective-permute-start.1 = (bf16[32,4,16,128]{3,2,1,0:T(8,128)(2,1)S(1)}, bf16[32,4,16,128]{3,2,1,0:T(8,128)(2,1)S(1)}, u32[]{:S(2)}, u32[]{:S(2)}) collective-permute-start(bf16[32,4,16,128]{3,2,1,0:T(8,128)(2,1)S(1)} %get-tuple-element.16.refs_0_), channel_id=1, source_target_pairs={{0,4},{2,6},{4,8},{6,10},{8,12},{10,14},{12,16},{14,18},{16,20},{1... | collective-permute-start | bytes 1572872 | tf_op jit(solution)/shard_map/ppermute | solution.py:349
  22.9 30.2 %collective-permute-start.6 = (bf16[32,4,16,128]{3,2,1,0:T(8,128)(2,1)S(1)}, bf16[32,4,16,128]{3,2,1,0:T(8,128)(2,1)}, u32[]{:S(2)}, u32[]{:S(2)}) collective-permute-start(bf16[32,4,16,128]{3,2,1,0:T(8,128)(2,1)S(1)} %get-tuple-element.16.refs_0_), channel_id=1, source_target_pairs={{0,2},{2,8},{4,6},{6,12},{8,10},{10,16},{12,14},{14,20},{16,18},{1... | collective-permute-start | bytes 1572872 | tf_op jit(solution)/shard_map/ppermute | solution.py:354
  23.0 2.2 %copy-start.1 = (bf16[8,32,2,4096]{3,2,1,0:T(2,128)(2,1)S(1)}, bf16[8,32,2,4096]{3,2,1,0:T(2,128)(2,1)}, u32[]{:S(2)}) copy-start(bf16[8,32,2,4096]{3,2,1,0:T(2,128)(2,1)} %param.7) | copy-start | bytes 12582916
  38.0 15.0 %collective-permute-start = (bf16[32,4,16,128]{3,2,1,0:T(8,128)(2,1)}, bf16[32,4,16,128]{3,2,1,0:T(8,128)(2,1)}, u32[]{:S(2)}, u32[]{:S(2)}) collective-permute-start(bf16[32,4,16,128]{3,2,1,0:T(8,128)(2,1)} %get-tuple-element.19), channel_id=1, source_target_pairs={{0,1},{2,3},{4,5},{6,7},{8,9},{10,11},{12,13},{14,15},{16,17},{18,... | collective-permute-start | bytes 1572872 | tf_op jit(solution)/shard_map/ppermute | solution.py:390
  40.2 12.7 %copy-start.9 = (bf16[32,4,16,128]{3,2,1,0:T(8,128)(2,1)}, bf16[32,4,16,128]{3,2,1,0:T(8,128)(2,1)S(1)}, u32[]{:S(2)}) copy-start(bf16[32,4,16,128]{3,2,1,0:T(8,128)(2,1)S(1)} %collective-permute-done.1.refs_2_) | copy-start | bytes 1572868
  40.2 46.3 %copy-start.13 = (s32[4]{0:T(128)S(1)}, s32[4]{0:T(128)}, u32[]{:S(2)}) copy-start(s32[4]{0:T(128)} %constant.47.clone) | copy-start | bytes 52
  40.2 14.5 %collective-permute-start.4 = (bf16[32,4,16,128]{3,2,1,0:T(8,128)(2,1)}, bf16[32,4,16,128]{3,2,1,0:T(8,128)(2,1)}, u32[]{:S(2)}, u32[]{:S(2)}) collective-permute-start(bf16[32,4,16,128]{3,2,1,0:T(8,128)(2,1)} %collective-permute-done.2.refs_4_), channel_id=1, source_target_pairs={{0,4},{2,6},{4,8},{6,10},{8,12},{10,14},{12,16},{14,18},{16,20},{1... | collective-permute-start | bytes 1572872 | tf_op jit(solution)/shard_map/ppermute | solution.py:349
  41.8 12.9 %collective-permute-start.5 = (bf16[32,4,16,128]{3,2,1,0:T(8,128)(2,1)S(1)}, bf16[32,4,16,128]{3,2,1,0:T(8,128)(2,1)S(1)}, u32[]{:S(2)}, u32[]{:S(2)}) collective-permute-start(bf16[32,4,16,128]{3,2,1,0:T(8,128)(2,1)S(1)} %collective-permute-done.1.refs_2_), channel_id=1, source_target_pairs={{0,2},{2,0},{4,6},{6,4},{8,10},{10,8},{12,14},{14,12},{16,18},{18,... | collective-permute-start | bytes 1572872 | tf_op jit(solution)/shard_map/ppermute | solution.py:359
  43.2 2.2 %copy-start.2 = (bf16[8,32,2,4096]{3,2,1,0:T(2,128)(2,1)S(1)}, bf16[8,32,2,4096]{3,2,1,0:T(2,128)(2,1)}, u32[]{:S(2)}) copy-start(bf16[8,32,2,4096]{3,2,1,0:T(2,128)(2,1)} %param.7) | copy-start | bytes 12582916
  52.9 8.3 %collective-permute-start.7 = (bf16[32,2,16,128]{3,2,1,0:T(8,128)(2,1)S(1)}, bf16[32,2,16,128]{3,2,1,0:T(8,128)(2,1)S(1)}, u32[]{:S(2)}, u32[]{:S(2)}) collective-permute-start(bf16[32,2,16,128]{3,2,1,0:T(8,128)(2,1)S(1)} %get-tuple-element.24), channel_id=1, source_target_pairs={{0,1},{1,0},{2,3},{3,2},{4,5},{5,4},{6,7},{7,6},{8,9},{9,8},{10,11... | collective-permute-start | bytes 786440 | tf_op jit(solution)/shard_map/ppermute | solution.py:400
  54.7 31.8 %copy-start.11 = (bf16[32,4,16,128]{3,2,1,0:T(8,128)(2,1)}, bf16[32,4,16,128]{3,2,1,0:T(8,128)(2,1)S(1)}, u32[]{:S(2)}) copy-start(bf16[32,4,16,128]{3,2,1,0:T(8,128)(2,1)S(1)} %collective-permute-done.5.refs_1_) | copy-start | bytes 1572868
  61.3 25.2 %collective-permute-start.8 = (bf16[32,8,16,128]{3,2,1,0:T(8,128)(2,1)S(1)}, bf16[32,8,16,128]{3,2,1,0:T(8,128)(2,1)S(1)}, u32[]{:S(2)}, u32[]{:S(2)}) collective-permute-start(bf16[32,8,16,128]{3,2,1,0:T(8,128)(2,1)S(1)} %pad_maximum_fusion.refs_0_), channel_id=1, source_target_pairs={{0,4},{2,6},{4,8},{6,10},{8,12},{10,14},{12,16},{14,18},{16,20},{1... | collective-permute-start | bytes 3145736 | tf_op jit(solution)/shard_map/ppermute | solution.py:349
  62.9 30.2 %collective-permute-start.12 = (bf16[32,4,16,128]{3,2,1,0:T(8,128)(2,1)}, bf16[32,4,16,128]{3,2,1,0:T(8,128)(2,1)}, u32[]{:S(2)}, u32[]{:S(2)}) collective-permute-start(bf16[32,4,16,128]{3,2,1,0:T(8,128)(2,1)} %collective-permute-done.2.refs_4_), channel_id=1, source_target_pairs={{0,2},{2,8},{4,6},{6,12},{8,10},{10,16},{12,14},{14,20},{16,18},{1... | collective-permute-start | bytes 1572872 | tf_op jit(solution)/shard_map/ppermute | solution.py:354
  62.9 30.2 %collective-permute-start.11 = (bf16[32,4,16,128]{3,2,1,0:T(8,128)(2,1)}, bf16[32,4,16,128]{3,2,1,0:T(8,128)(2,1)}, u32[]{:S(2)}, u32[]{:S(2)}) collective-permute-start(bf16[32,4,16,128]{3,2,1,0:T(8,128)(2,1)} %collective-permute-done.4.refs_6_), channel_id=1, source_target_pairs={{0,2},{2,0},{4,6},{6,4},{8,10},{10,8},{12,14},{14,12},{16,18},{18,... | collective-permute-start | bytes 1572872 | tf_op jit(solution)/shard_map/ppermute | solution.py:359
  63.7 40.5 %collective-permute-start.10 = (bf16[32,8,16,128]{3,2,1,0:T(8,128)(2,1)S(1)}, bf16[32,8,16,128]{3,2,1,0:T(8,128)(2,1)S(1)}, u32[]{:S(2)}, u32[]{:S(2)}) collective-permute-start(bf16[32,8,16,128]{3,2,1,0:T(8,128)(2,1)S(1)} %pad_maximum_fusion.refs_0_), channel_id=1, source_target_pairs={{0,2},{2,8},{4,6},{6,12},{8,10},{10,16},{12,14},{14,20},{16,18},{1... | collective-permute-start | bytes 3145736 | tf_op jit(solution)/shard_map/ppermute | solution.py:354
  86.5 17.7 %collective-permute-start.9 = (bf16[32,8,16,128]{3,2,1,0:T(8,128)(2,1)S(1)}, bf16[32,8,16,128]{3,2,1,0:T(8,128)(2,1)}, u32[]{:S(2)}, u32[]{:S(2)}) collective-permute-start(bf16[32,8,16,128]{3,2,1,0:T(8,128)(2,1)S(1)} %collective-permute-done.8.refs_2_), channel_id=1, source_target_pairs={{0,2},{2,0},{4,6},{6,4},{8,10},{10,8},{12,14},{14,12},{16,18},{18,... | collective-permute-start | bytes 3145736 | tf_op jit(solution)/shard_map/ppermute | solution.py:359
  93.1 1.0 copy-start.8
  94.1 1.0 copy-start.10
  95.2 1.0 copy-start.12

commit v5 on v4

--- a/solution.py
+++ b/solution.py
@@ -73,18 +73,44 @@
 
 
 def spectra_kernel(groups, parts, out_frames, place, *refs):
-    part_refs, refs = refs[: len(parts)], refs[len(parts) :]
-    taps_ref, table_ref = refs[:2]
-    outs, (taps, one, two, ext, filtered, turned, staged) = refs[2:-7], refs[-7:]
-    step, steps, members = pl.program_id(0), pl.num_programs(0), part_refs[0].shape[0]
+    sources, refs = refs[: len(parts)], refs[len(parts) :]
+    taps_source, table_source = refs[:2]
+    buffers, refs = refs[-len(parts) - 2 :], refs[2 : -len(parts) - 2]
+    outs, (taps, one, two, ext, filtered, turned, staged, arrived, fixed) = refs[:-9], refs[-9:]
+    taps_ref, table_ref, part_refs = buffers[0], buffers[1], buffers[2:]
+    step, steps, members = pl.program_id(0), pl.num_programs(0), MEMBERS
     per_group = K2 // groups
     share = LANES // out_frames
     tiles = H // share
     pairs = tiles // 2
     frame_rows, row_rows = ROWS + PAD, tiles * TILE + PAD
-
-    @pl.when(step == 0)
+    signals = part_refs[0].shape[0]
+
+    def fixed_copies():
+        return [
+            pltpu.make_async_copy(taps_source, taps_ref, fixed.at[0]),
+            pltpu.make_async_copy(table_source, table_ref, fixed.at[1]),
+        ]
+
+    def copy(number, signal):
+        frames = parts[number]
+        start = pl.multiple_of(place[2 + 3 * number] * frames, frames)
+        return pltpu.make_async_copy(
+            sources[number].at[signal, pl.ds(start, frames)],
+            part_refs[number].at[signal],
+            arrived.at[number, signal],
+        )
+
+    @pl.when((step == 0) & (place[0] == 1))
     def _():
+        for one_copy in fixed_copies():
+            one_copy.start()
+        for signal in range(signals):
+            for number in range(len(parts)):
+                copy(number, signal).start()
+        for one_copy in fixed_copies():
+            one_copy.wait()
+
         for h in range(H):
             for half in range(TAPS // SUB):
                 tile = taps_ref[pl.ds(half * SUB, SUB), pl.ds(h * LANES, LANES)]
@@ -98,14 +124,16 @@
         two[1] = low
 
     def load(member):
+        signal = step * members + member
         for number, (frames, ref) in enumerate(zip(parts, part_refs)):
             start = place[2 + 3 * number + 1]
             valid = place[2 + 3 * number + 2]
+            copy(number, signal).wait()
 
             @pl.when(valid == 1)
             def _():
                 for f in range(frames):
-                    ext[member, start + f] = ref[member, f].astype(F32)
+                    ext[member, start + f] = ref[signal, f].astype(F32)
 
             @pl.when(valid == 0)
             def _():
@@ -191,6 +219,32 @@
             write()
 
 
+def in_hbm(array):
+    return pltpu.with_memory_space_constraint(array, pltpu.HBM)
+
+
+def cut_kernel(place, source, out, done):
+    count = out.shape[1]
+    start = pl.multiple_of(place[0], count)
+    copy = pltpu.make_async_copy(source.at[:, pl.ds(start, count)], out, done)
+    copy.start()
+    copy.wait()
+
+
+def cut(volts, start, count):
+    return pl.pallas_call(
+        cut_kernel,
+        grid_spec=pltpu.PrefetchScalarGridSpec(
+            num_scalar_prefetch=1,
+            grid=(1,),
+            in_specs=[pl.BlockSpec(memory_space=pl.ANY)],
+            out_specs=pl.BlockSpec(memory_space=pl.ANY),
+            scratch_shapes=[pltpu.SemaphoreType.DMA],
+        ),
+        out_shape=jax.ShapeDtypeStruct((volts.shape[0], count, ROWS, LANES), BF16),
+    )(jnp.reshape(start, (1,)).astype(jnp.int32), volts)
+
+
 def after(value, *others):
     return lax.optimization_barrier((value, *others))[0]
 
@@ -200,16 +254,10 @@
     numbers = [run, order] + [v for part in parts for v in part[2:]]
     place = jnp.stack([jnp.asarray(v, jnp.int32) for v in numbers])
     place = after(place, *wait)
-    table = tables(groups)
+    table = jnp.asarray(tables(groups))
     tiles = H * out_frames // LANES
     whole = lambda shape: pl.BlockSpec(shape, lambda s, place: (0,) * len(shape))
-    in_specs = [
-        pl.BlockSpec(
-            (MEMBERS, part[1], ROWS, LANES), functools.partial(lambda n, s, place: (s, place[2 + 3 * n], 0, 0), n)
-        )
-        for n, part in enumerate(parts)
-    ]
-    in_specs += [whole((TAPS, NCH)), whole(table.shape)]
+    in_specs = [pl.BlockSpec(memory_space=pl.ANY)] * (len(parts) + 2)
     shapes = [(n, tiles, TILE, LANES) for n in sizes]
     return pl.pallas_call(
         functools.partial(spectra_kernel, groups, tuple(p[1] for p in parts), out_frames),
@@ -226,14 +274,19 @@
                 pltpu.VMEM((MEMBERS, out_frames, ROWS, LANES), F32),
                 pltpu.VMEM((MEMBERS, out_frames * (ROWS + PAD), LANES), F32),
                 pltpu.VMEM((K2 * (tiles * TILE + PAD), LANES), F32),
-            ],
+                pltpu.SemaphoreType.DMA((len(parts), signals)),
+                pltpu.SemaphoreType.DMA((2,)),
+                pltpu.VMEM((TAPS, NCH), F32),
+                pltpu.VMEM(table.shape, F32),
+            ]
+            + [pltpu.VMEM((signals, part[1], ROWS, LANES), BF16) for part in parts],
         ),
         out_shape=[jax.ShapeDtypeStruct(shape, BF16) for shape in shapes],
         compiler_params=pltpu.CompilerParams(vmem_limit_bytes=32 << 20),
         cost_estimate=pl.CostEstimate(
             flops=cost, bytes_accessed=0, transcendentals=0
         ),
-    )(place, *[part[0] for part in parts], fir_taps, table)
+    )(place, *[part[0] for part in parts], fir_taps, in_hbm(table))
 
 
 def correlate_kernel(pieces, per_group, scale, add, last, place, *refs):
@@ -362,7 +415,7 @@
 def general(volts, fir_taps):
     groups = lax.axis_size("tm")
     frames = volts.shape[1]
-    history = lax.ppermute(volts[:, frames - TAPS :], "tm", [(i, i + 1) for i in range(groups - 1)])
+    history = lax.ppermute(cut(volts, jnp.int32(frames - TAPS), TAPS), "tm", [(i, i + 1) for i in range(groups - 1)])
     parts = [(history, TAPS, 0, 0, 1)] + [(volts, TAPS, i, TAPS * (i + 1), 1) for i in range(frames // TAPS)]
     spectrum = spectra(parts, frames, fir_taps, groups, [K2])[0]
     spectrum = lax.all_to_all(spectrum, "tm", split_axis=0, concat_axis=0, tiled=True)
@@ -377,7 +430,7 @@
     swap = [(0, 1), (1, 0)]
     edge = TAPS // 2
     last = frames // edge
-    edge_frames = lax.dynamic_slice_in_dim(volts, jnp.where(me == 0, frames - edge, 0), edge, 1)
+    edge_frames = cut(volts, jnp.where(me == 0, frames - edge, 0), edge)
     visiting = lax.ppermute(edge_frames, "tm", swap)
     own_a, away_a = spectra(
         [(volts, TAPS, 0, 0, me), (volts, TAPS, me, TAPS, 1)], TAPS, fir_taps, 2, sizes, 1, me, (edge_frames,)
@@ -403,11 +456,11 @@
     own_c = after(own_c, two_g, pair_a, rest_a)
     rest = jnp.concatenate([jnp.where(me == 0, own_b, got_b), own_c, got_c], axis=1)
     two_r, rest_r = farther(rest)
-    pair_r = exchanged(two_r)
     many, few = own_a.shape[1], own_c.shape[1]
     sums = correlated(
         [own_a, pair_a, two_a, rest_a, got_a, pair_g, two_g, rest_g], [(many, [(0, 0, 0), (1, 0, 0)])], None, False
     )
+    pair_r = exchanged(after(two_r, sums))
     return correlated(
         [rest, pair_r, two_r, rest_r], [(many, [(0, 0, 0)]), (few, [(0, 0, many), (0, 0, many + few)])], sums, True
     )
@@ -416,7 +469,7 @@
 def general(volts, fir_taps, correlated):
     groups = lax.axis_size("tm")
     frames = volts.shape[1]
-    history = lax.ppermute(volts[:, frames - TAPS :], "tm", [(i, i + 1) for i in range(groups - 1)])
+    history = lax.ppermute(cut(volts, jnp.int32(frames - TAPS), TAPS), "tm", [(i, i + 1) for i in range(groups - 1)])
     parts = [(history, TAPS, 0, 0, 1)] + [(volts, TAPS, i, TAPS * (i + 1), 1) for i in range(frames // TAPS)]
     spectrum = spectra(parts, frames, fir_taps, groups, [K2])[0]
     spectrum = lax.all_to_all(spectrum, "tm", split_axis=0, concat_axis=0, tiled=True)
@@ -439,7 +492,7 @@
         return correlate(arrays, laid, K2 // groups, place, scale, before, last, wait)
 
     run = paired if groups == 2 else general
-    return natural(run(stacked(voltage), fir_taps, correlated))
+    return natural(run(in_hbm(stacked(voltage)), in_hbm(fir_taps), correlated))
 
 
 def solution(mesh):

time: 117 us -> 143 us (1.22)
  the two profiles are of different devices: /device:TPU:2 before, /device:TPU:6 now
where the time goes in v5:
time: 143 us; the launch traced here: 142 us
  Pallas kernels  76.9 us (54%)
  waiting for transfers between devices  48.5 us (34%)
  starting transfers between devices  15.2 us (11%)
    pallas_call x1, Pallas kernels, cut(): pl.pallas_call(cut_kernel, grid_spec=pltpu.PrefetchScalarGridSpec(num_sca...  32.9 us
    pallas_call x3, Pallas kernels, spectra(): pl.pallas_call(functools.partial(spectra_kernel, groups, tuple((p[1] for...  25.6 us
    pallas_call x2, Pallas kernels, correlate(): pl.pallas_call(functools.partial(correlate_kernel, pieces, per_group, sca...  18.4 us
    ppermute x3, waiting for transfers between devices, shifted(): lax.ppermute(block, axis, [(i, (i + distance) % size) for i in range(size)])  18.1 us
    ppermute x1, waiting for transfers between devices, paired(): got_a = lax.ppermute(away_a, 'tm', swap)  14.5 us
    ppermute x3, waiting for transfers between devices, farther(): lax.ppermute(block, 'stn', [(i, (i + 1 if i % 2 == 0 else i + 3) % size)...  14.2 us
    ppermute x3, starting transfers between devices, exchanged(): lax.ppermute(block, 'stn', [(i, i ^ 1) for i in range(lax.axis_size('stn'...  6.25 us
    ppermute x3, starting transfers between devices, shifted(): lax.ppermute(block, axis, [(i, (i + distance) % size) for i in range(size)])  4.66 us
  transfers between devices with their start and end apart: 13, of which 5 were waited for; matrix products, arithmetic and copies ran while one was open for 0% of the time, Pallas kernels for 23%

profile of v5, /device:TPU:6, one launch (start us, length us, event | category | flops | bytes accessed | tf_op | source)
XLA Modules:
  0.0 142.3 jit_solution(16443594147889798607)
XLA Ops:
  0.0 32.9 %shard_map.73 = bf16[8,8,64,128]{3,2,1,0:T(8,128)(2,1)} custom-call(s32[1]{0:T(128)} %bitcast.2.place, bf16[8,32,64,128]{3,2,1,0:T(8,128)(2,1)} %bitcast.16), custom_call_target="tpu_custom_call" | custom-call | tf_op jit(solution)/shard_map/pallas_call | solution.py:235
  32.9 0.6 collective-permute-start.3
  33.5 0.1 stack.37.place
  33.5 15.1 %shard_map.74 = (bf16[32,4,16,128]{3,2,1,0:T(8,128)(2,1)S(1)}, bf16[32,4,16,128]{3,2,1,0:T(8,128)(2,1)}) custom-call(s32[8]{0:T(128)S(1)} %stack.37.place, bf16[8,32,64,128]{3,2,1,0:T(8,128)(2,1)} %bitcast.17, bf16[8,32,64,128]{3,2,1,0:T(8,128)(2,1)} %bitcast.18, f32[16,4096]{1,0:T(8,128)} %refs_3_.3, f32[352,256]{1,0:T(8,128)} %constant.46.clone.refs_3_.refs_4_), custom_call_target="tpu_custom_call" | custom-call | flops 1000000 | tf_op jit(solution)/shard_map/pallas_call | solution.py:262
  48.6 1.6 %collective-permute-start.2 = (bf16[32,4,16,128]{3,2,1,0:T(8,128)(2,1)}, bf16[32,4,16,128]{3,2,1,0:T(8,128)(2,1)S(1)}, u32[]{:S(2)}, u32[]{:S(2)}) collective-permute-start(bf16[32,4,16,128]{3,2,1,0:T(8,128)(2,1)} %get-tuple-element.21), channel_id=1, source_target_pairs={{0,1},{1,0},{2,3},{3,2},{4,5},{5,4},{6,7},{7,6},{8,9},{9,8},{10,11... | collective-permute-start | bytes 1572872 | tf_op jit(solution)/shard_map/ppermute | solution.py:438
  50.2 1.6 %collective-permute-start.1 = (bf16[32,4,16,128]{3,2,1,0:T(8,128)(2,1)S(1)}, bf16[32,4,16,128]{3,2,1,0:T(8,128)(2,1)}, u32[]{:S(2)}, u32[]{:S(2)}) collective-permute-start(bf16[32,4,16,128]{3,2,1,0:T(8,128)(2,1)S(1)} %get-tuple-element.17.refs_0_), channel_id=1, source_target_pairs={{0,4},{2,6},{4,8},{6,10},{8,12},{10,14},{12,16},{14,18},{16,20},{1... | collective-permute-start | bytes 1572872 | tf_op jit(solution)/shard_map/ppermute | solution.py:402
  51.7 0.0 collective-permute-start.6
  51.7 0.1 stack.36.place
  51.8 1.6 %shard_map.75 = (bf16[32,4,16,128]{3,2,1,0:T(8,128)(2,1)S(1)}, bf16[32,4,16,128]{3,2,1,0:T(8,128)(2,1)}) custom-call(s32[8]{0:T(128)S(1)} %stack.36.place, bf16[8,32,64,128]{3,2,1,0:T(8,128)(2,1)} %bitcast.19, bf16[8,32,64,128]{3,2,1,0:T(8,128)(2,1)} %bitcast.20, f32[16,4096]{1,0:T(8,128)} %refs_3_.3, f32[352,256]{1,0:T(8,128)} %constant.46.clone.refs_3_.refs_4_), custom_call_target="tpu_custom_call" | custom-call | flops 1000000 | tf_op jit(solution)/shard_map/pallas_call | solution.py:262
  53.4 1.3 collective-permute-start
  54.7 0.1 stack.43.place
  54.8 14.5 %collective-permute-done.2.refs_4_ = bf16[32,4,16,128]{3,2,1,0:T(8,128)(2,1)S(1)} collective-permute-done((bf16[32,4,16,128]{3,2,1,0:T(8,128)(2,1)}, bf16[32,4,16,128]{3,2,1,0:T(8,128)(2,1)S(1)}, u32[]{:S(2)}, u32[]{:S(2)}) %collective-permute-start.2) | collective-permute-done | bytes 524320 | tf_op jit(solution)/shard_map/ppermute | solution.py:438
  69.3 0.0 collective-permute-done.1.refs_2_
  69.3 0.0 collective-permute-start.10
  69.3 1.5 %collective-permute-start.4 = (bf16[32,4,16,128]{3,2,1,0:T(8,128)(2,1)S(1)}, bf16[32,4,16,128]{3,2,1,0:T(8,128)(2,1)}, u32[]{:S(2)}, u32[]{:S(2)}) collective-permute-start(bf16[32,4,16,128]{3,2,1,0:T(8,128)(2,1)S(1)} %collective-permute-done.2.refs_4_), channel_id=1, source_target_pairs={{0,4},{2,6},{4,8},{6,10},{8,12},{10,14},{12,16},{14,18},{16,20},{1... | collective-permute-start | bytes 1572872 | tf_op jit(solution)/shard_map/ppermute | solution.py:402
  70.8 0.0 collective-permute-done.3.refs_2_
  70.8 1.4 collective-permute-start.5
  72.3 9.0 %shard_map.76 = (bf16[32,2,16,128]{3,2,1,0:T(8,128)(2,1)S(1)}, bf16[32,2,16,128]{3,2,1,0:T(8,128)(2,1)S(1)}) custom-call(s32[11]{0:T(128)S(1)} %stack.43.place, bf16[8,32,64,128]{3,2,1,0:T(8,128)(2,1)} %bitcast.21, bf16[8,32,64,128]{3,2,1,0:T(8,128)(2,1)} %bitcast.22, bf16[8,8,64,128]{3,2,1,0:T(8,128)(2,1)S(1)} %collective-permute-done.3.refs_2_, ...), custom_call_target="tpu_custom_call" | custom-call | flops 8999999488 | tf_op jit(solution)/shard_map/pallas_call | solution.py:262
  81.3 0.0 copy-start.2
  81.3 0.0 collective-permute-done
  81.3 0.6 collective-permute-start.7
  81.9 0.1 broadcast_select_fusion
  82.0 0.0 collective-permute-done.6.refs_3_
  82.0 1.5 %collective-permute-done.4.refs_6_ = bf16[32,4,16,128]{3,2,1,0:T(8,128)(2,1)} collective-permute-done((bf16[32,4,16,128]{3,2,1,0:T(8,128)(2,1)S(1)}, bf16[32,4,16,128]{3,2,1,0:T(8,128)(2,1)}, u32[]{:S(2)}, u32[]{:S(2)}) %collective-permute-start.4) | collective-permute-done | bytes 524320 | tf_op jit(solution)/shard_map/ppermute | solution.py:402
  83.5 0.0 collective-permute-done.5.refs_1_
  83.5 0.0 copy-start
  83.5 4.8 %collective-permute-start.9 = (bf16[32,4,16,128]{3,2,1,0:T(8,128)(2,1)}, bf16[32,4,16,128]{3,2,1,0:T(8,128)(2,1)}, u32[]{:S(2)}, u32[]{:S(2)}) collective-permute-start(bf16[32,4,16,128]{3,2,1,0:T(8,128)(2,1)} %collective-permute-done.4.refs_6_), channel_id=1, source_target_pairs={{0,2},{2,0},{4,6},{6,4},{8,10},{10,8},{12,14},{14,12},{16,18},{18,... | collective-permute-start | bytes 1572872 | tf_op jit(solution)/shard_map/ppermute | solution.py:412
  88.4 1.7 %collective-permute-done.7 = bf16[32,2,16,128]{3,2,1,0:T(8,128)(2,1)S(1)} collective-permute-done((bf16[32,2,16,128]{3,2,1,0:T(8,128)(2,1)S(1)}, bf16[32,2,16,128]{3,2,1,0:T(8,128)(2,1)S(1)}, u32[]{:S(2)}, u32[]{:S(2)}) %collective-permute-start.7) | collective-permute-done | bytes 262176 | tf_op jit(solution)/shard_map/ppermute | solution.py:453
  90.1 0.1 pad_maximum_fusion.refs_0_
  90.2 0.0 copy-done
  90.2 1.6 %collective-permute-start.8 = (bf16[32,8,16,128]{3,2,1,0:T(8,128)(2,1)S(1)}, bf16[32,8,16,128]{3,2,1,0:T(8,128)(2,1)S(1)}, u32[]{:S(2)}, u32[]{:S(2)}) collective-permute-start(bf16[32,8,16,128]{3,2,1,0:T(8,128)(2,1)S(1)} %pad_maximum_fusion.refs_0_), channel_id=1, source_target_pairs={{0,4},{2,6},{4,8},{6,10},{8,12},{10,14},{12,16},{14,18},{16,20},{1... | collective-permute-start | bytes 3145736 | tf_op jit(solution)/shard_map/ppermute | solution.py:402
  91.7 0.0 copy-done.2
  91.8 0.3 collective-permute-start.12
  92.1 0.0 collective-permute-done.10.refs_7_
  92.1 0.0 collective-permute-done.9.refs_5_
  92.1 0.0 copy-start.1
  92.1 1.0 copy-done.1
  93.1 6.8 %shard_map.77.refs_4_ = f32[4096,128]{1,0:T(8,128)} custom-call(s32[4]{0:T(128)S(1)} %broadcast_select_fusion.1.place, bf16[32,4,16,128]{3,2,1,0:T(8,128)(2,1)S(1)} %get-tuple-element.17.refs_0_, bf16[32,4,16,128]{3,2,1,0:T(8,128)(2,1)S(1)} %copy-done.1, bf16[32,4,16,128]{3,2,1,0:T(8,128)(2,1)} %collective-permute-done.1.refs_2_, ...), custom_call_target="tpu_custom_call" | custom-call | flops 6000000000 | tf_op jit(solution)/shard_map/pallas_call | solution.py:374
  99.9 16.6 %collective-permute-done.8.refs_2_ = bf16[32,8,16,128]{3,2,1,0:T(8,128)(2,1)S(1)} collective-permute-done((bf16[32,8,16,128]{3,2,1,0:T(8,128)(2,1)S(1)}, bf16[32,8,16,128]{3,2,1,0:T(8,128)(2,1)S(1)}, u32[]{:S(2)}, u32[]{:S(2)}) %collective-permute-start.8) | collective-permute-done | bytes 1048608 | tf_op jit(solution)/shard_map/ppermute | solution.py:402
  116.4 0.0 collective-permute-start.11
  116.5 14.2 %collective-permute-done.12.refs_3_ = bf16[32,8,16,128]{3,2,1,0:T(8,128)(2,1)S(1)} collective-permute-done((bf16[32,8,16,128]{3,2,1,0:T(8,128)(2,1)S(1)}, bf16[32,8,16,128]{3,2,1,0:T(8,128)(2,1)S(1)}, u32[]{:S(2)}, u32[]{:S(2)}) %collective-permute-start.12) | collective-permute-done | bytes 1048608 | tf_op jit(solution)/shard_map/ppermute | solution.py:407
  130.7 0.0 collective-permute-done.11.refs_1_
  130.7 11.7 %shard_map.78 = f32[2,8,4,8,8,128]{5,4,3,2,1,0:T(8,128)} custom-call(s32[4]{0:T(128)S(1)} %broadcast_select_fusion.1.place, bf16[32,8,16,128]{3,2,1,0:T(8,128)(2,1)S(1)} %pad_maximum_fusion.refs_0_, bf16[32,8,16,128]{3,2,1,0:T(8,128)(2,1)S(1)} %collective-permute-done.11.refs_1_, bf16[32,8,16,128]{3,2,1,0:T(8,128)(2,1)S(1)} %collective-permute-done.8.refs_2_, ...), custom_call_target="tpu_custom_call" | custom-call | flops 6000000000 | tf_op jit(solution)/shard_map/pallas_call | solution.py:374
  (3 shorter events, 0.0 us)
Async XLA Ops:
  32.9 38.0 %collective-permute-start.3 = (bf16[8,8,64,128]{3,2,1,0:T(8,128)(2,1)}, bf16[8,8,64,128]{3,2,1,0:T(8,128)(2,1)S(1)}, u32[]{:S(2)}, u32[]{:S(2)}) collective-permute-start(bf16[8,8,64,128]{3,2,1,0:T(8,128)(2,1)} %shard_map.73), channel_id=1, source_target_pairs={{0,1},{1,0},{2,3},{3,2},{4,5},{5,4},{6,7},{7,6},{8,9},{9,8},{10,11... | collective-permute-start | bytes 3145736 | tf_op jit(solution)/shard_map/ppermute | solution.py:434
  48.6 20.7 %collective-permute-start.2 = (bf16[32,4,16,128]{3,2,1,0:T(8,128)(2,1)}, bf16[32,4,16,128]{3,2,1,0:T(8,128)(2,1)S(1)}, u32[]{:S(2)}, u32[]{:S(2)}) collective-permute-start(bf16[32,4,16,128]{3,2,1,0:T(8,128)(2,1)} %get-tuple-element.21), channel_id=1, source_target_pairs={{0,1},{1,0},{2,3},{3,2},{4,5},{5,4},{6,7},{7,6},{8,9},{9,8},{10,11... | collective-permute-start | bytes 1572872 | tf_op jit(solution)/shard_map/ppermute | solution.py:438
  50.2 19.1 %collective-permute-start.1 = (bf16[32,4,16,128]{3,2,1,0:T(8,128)(2,1)S(1)}, bf16[32,4,16,128]{3,2,1,0:T(8,128)(2,1)}, u32[]{:S(2)}, u32[]{:S(2)}) collective-permute-start(bf16[32,4,16,128]{3,2,1,0:T(8,128)(2,1)S(1)} %get-tuple-element.17.refs_0_), channel_id=1, source_target_pairs={{0,4},{2,6},{4,8},{6,10},{8,12},{10,14},{12,16},{14,18},{16,20},{1... | collective-permute-start | bytes 1572872 | tf_op jit(solution)/shard_map/ppermute | solution.py:402
  51.7 30.3 %collective-permute-start.6 = (bf16[32,4,16,128]{3,2,1,0:T(8,128)(2,1)S(1)}, bf16[32,4,16,128]{3,2,1,0:T(8,128)(2,1)}, u32[]{:S(2)}, u32[]{:S(2)}) collective-permute-start(bf16[32,4,16,128]{3,2,1,0:T(8,128)(2,1)S(1)} %get-tuple-element.17.refs_0_), channel_id=1, source_target_pairs={{0,2},{2,8},{4,6},{6,12},{8,10},{10,16},{12,14},{14,20},{16,18},{1... | collective-permute-start | bytes 1572872 | tf_op jit(solution)/shard_map/ppermute | solution.py:407
  53.4 28.0 %collective-permute-start = (bf16[32,4,16,128]{3,2,1,0:T(8,128)(2,1)}, bf16[32,4,16,128]{3,2,1,0:T(8,128)(2,1)S(1)}, u32[]{:S(2)}, u32[]{:S(2)}) collective-permute-start(bf16[32,4,16,128]{3,2,1,0:T(8,128)(2,1)} %get-tuple-element.20), channel_id=1, source_target_pairs={{0,1},{2,3},{4,5},{6,7},{8,9},{10,11},{12,13},{14,15},{16,17},{18,... | collective-permute-start | bytes 1572872 | tf_op jit(solution)/shard_map/ppermute | solution.py:443
  69.3 22.8 %collective-permute-start.10 = (bf16[32,4,16,128]{3,2,1,0:T(8,128)(2,1)S(1)}, bf16[32,4,16,128]{3,2,1,0:T(8,128)(2,1)}, u32[]{:S(2)}, u32[]{:S(2)}) collective-permute-start(bf16[32,4,16,128]{3,2,1,0:T(8,128)(2,1)S(1)} %collective-permute-done.2.refs_4_), channel_id=1, source_target_pairs={{0,2},{2,8},{4,6},{6,12},{8,10},{10,16},{12,14},{14,20},{16,18},{1... | collective-permute-start | bytes 1572872 | tf_op jit(solution)/shard_map/ppermute | solution.py:407
  69.3 14.2 %collective-permute-start.4 = (bf16[32,4,16,128]{3,2,1,0:T(8,128)(2,1)S(1)}, bf16[32,4,16,128]{3,2,1,0:T(8,128)(2,1)}, u32[]{:S(2)}, u32[]{:S(2)}) collective-permute-start(bf16[32,4,16,128]{3,2,1,0:T(8,128)(2,1)S(1)} %collective-permute-done.2.refs_4_), channel_id=1, source_target_pairs={{0,4},{2,6},{4,8},{6,10},{8,12},{10,14},{12,16},{14,18},{16,20},{1... | collective-permute-start | bytes 1572872 | tf_op jit(solution)/shard_map/ppermute | solution.py:402
  70.8 12.7 %collective-permute-start.5 = (bf16[32,4,16,128]{3,2,1,0:T(8,128)(2,1)}, bf16[32,4,16,128]{3,2,1,0:T(8,128)(2,1)S(1)}, u32[]{:S(2)}, u32[]{:S(2)}) collective-permute-start(bf16[32,4,16,128]{3,2,1,0:T(8,128)(2,1)} %collective-permute-done.1.refs_2_), channel_id=1, source_target_pairs={{0,2},{2,0},{4,6},{6,4},{8,10},{10,8},{12,14},{14,12},{16,18},{18,... | collective-permute-start | bytes 1572872 | tf_op jit(solution)/shard_map/ppermute | solution.py:412
  81.3 10.4 %copy-start.2 = (s32[4]{0:T(128)S(1)}, s32[4]{0:T(128)}, u32[]{:S(2)}) copy-start(s32[4]{0:T(128)} %constant.45.clone) | copy-start | bytes 52
  81.3 8.7 %collective-permute-start.7 = (bf16[32,2,16,128]{3,2,1,0:T(8,128)(2,1)S(1)}, bf16[32,2,16,128]{3,2,1,0:T(8,128)(2,1)S(1)}, u32[]{:S(2)}, u32[]{:S(2)}) collective-permute-start(bf16[32,2,16,128]{3,2,1,0:T(8,128)(2,1)S(1)} %get-tuple-element.25), channel_id=1, source_target_pairs={{0,1},{1,0},{2,3},{3,2},{4,5},{5,4},{6,7},{7,6},{8,9},{9,8},{10,11... | collective-permute-start | bytes 786440 | tf_op jit(solution)/shard_map/ppermute | solution.py:453
  83.5 6.7 %copy-start = (bf16[32,4,16,128]{3,2,1,0:T(8,128)(2,1)}, bf16[32,4,16,128]{3,2,1,0:T(8,128)(2,1)S(1)}, u32[]{:S(2)}) copy-start(bf16[32,4,16,128]{3,2,1,0:T(8,128)(2,1)S(1)} %collective-permute-done.5.refs_1_) | copy-start | bytes 1572868
  83.5 8.5 %collective-permute-start.9 = (bf16[32,4,16,128]{3,2,1,0:T(8,128)(2,1)}, bf16[32,4,16,128]{3,2,1,0:T(8,128)(2,1)}, u32[]{:S(2)}, u32[]{:S(2)}) collective-permute-start(bf16[32,4,16,128]{3,2,1,0:T(8,128)(2,1)} %collective-permute-done.4.refs_6_), channel_id=1, source_target_pairs={{0,2},{2,0},{4,6},{6,4},{8,10},{10,8},{12,14},{14,12},{16,18},{18,... | collective-permute-start | bytes 1572872 | tf_op jit(solution)/shard_map/ppermute | solution.py:412
  90.2 26.2 %collective-permute-start.8 = (bf16[32,8,16,128]{3,2,1,0:T(8,128)(2,1)S(1)}, bf16[32,8,16,128]{3,2,1,0:T(8,128)(2,1)S(1)}, u32[]{:S(2)}, u32[]{:S(2)}) collective-permute-start(bf16[32,8,16,128]{3,2,1,0:T(8,128)(2,1)S(1)} %pad_maximum_fusion.refs_0_), channel_id=1, source_target_pairs={{0,4},{2,6},{4,8},{6,10},{8,12},{10,14},{12,16},{14,18},{16,20},{1... | collective-permute-start | bytes 3145736 | tf_op jit(solution)/shard_map/ppermute | solution.py:402
  91.8 38.9 %collective-permute-start.12 = (bf16[32,8,16,128]{3,2,1,0:T(8,128)(2,1)S(1)}, bf16[32,8,16,128]{3,2,1,0:T(8,128)(2,1)S(1)}, u32[]{:S(2)}, u32[]{:S(2)}) collective-permute-start(bf16[32,8,16,128]{3,2,1,0:T(8,128)(2,1)S(1)} %pad_maximum_fusion.refs_0_), channel_id=1, source_target_pairs={{0,2},{2,8},{4,6},{6,12},{8,10},{10,16},{12,14},{14,20},{16,18},{1... | collective-permute-start | bytes 3145736 | tf_op jit(solution)/shard_map/ppermute | solution.py:407
  92.1 1.0 copy-start.1
  116.4 14.2 %collective-permute-start.11 = (bf16[32,8,16,128]{3,2,1,0:T(8,128)(2,1)S(1)}, bf16[32,8,16,128]{3,2,1,0:T(8,128)(2,1)S(1)}, u32[]{:S(2)}, u32[]{:S(2)}) collective-permute-start(bf16[32,8,16,128]{3,2,1,0:T(8,128)(2,1)S(1)} %collective-permute-done.8.refs_2_), channel_id=1, source_target_pairs={{0,2},{2,0},{4,6},{6,4},{8,10},{10,8},{12,14},{14,12},{16,18},{18,... | collective-permute-start | bytes 3145736 | tf_op jit(solution)/shard_map/ppermute | solution.py:412

commit v6 on v4

--- a/solution.py
+++ b/solution.py
@@ -53,12 +53,6 @@
     return np.concatenate([real, imag], 1).reshape(2 * K2, 2 * LANES)
 
 
-def tables(groups):
-    two = stage_two_table(groups)
-    rolled = np.roll(two, K2, axis=0)
-    return np.concatenate([stage_one_table(), turn_table(), two, rolled]).astype(np.float32)
-
-
 def halves(value):
     high = value.astype(BF16)
     return high, (value - high.astype(F32)).astype(BF16)
@@ -72,40 +66,88 @@
     return lax.dot_general(left, right, (((1,), (1,)), ((), ())), preferred_element_type=F32)
 
 
+def prepare_kernel(place, volts_source, taps_source, table_source, volts, edge, taps, one, two, done, taps_ref, table_ref):
+    count = edge.shape[1]
+    start = pl.multiple_of(place[1] * count, count)
+    copies = [
+        pltpu.make_async_copy(taps_source, taps_ref, done.at[0]),
+        pltpu.make_async_copy(table_source, table_ref, done.at[1]),
+        pltpu.make_async_copy(volts_source.at[:, pl.ds(start, count)], edge, done.at[2]),
+        pltpu.make_async_copy(volts_source, volts, done.at[3]),
+    ]
+    for copy in copies:
+        copy.start()
+    copies[0].wait()
+    copies[1].wait()
+    for h in range(H):
+        for half in range(TAPS // SUB):
+            tile = taps_ref[pl.ds(half * SUB, SUB), pl.ds(h * LANES, LANES)]
+            for r in range(2):
+                taps[pl.ds(half * SUB * ROWS + 2 * h + r, SUB, stride=ROWS), :] = tile
+    high, low = halves(table_ref[:ROWS, :ROWS])
+    one[...] = jnp.concatenate([high, high, low], axis=1)
+    start = pl.multiple_of(ROWS + place[0] * 2 * K2, SUB)
+    high, low = halves(table_ref[pl.ds(start, 2 * K2), :])
+    two[0] = high
+    two[1] = low
+    copies[2].wait()
+    copies[3].wait()
+
+
+def prepare(volts, fir_taps, groups, order, edge_block, edge_frames):
+    signals, frames = volts.shape[:2]
+    two = stage_two_table(groups)
+    table = np.concatenate([stage_one_table(), two, np.roll(two, K2, axis=0)]).astype(np.float32)
+    vmem = pl.BlockSpec(memory_space=pltpu.VMEM)
+    return pl.pallas_call(
+        prepare_kernel,
+        grid_spec=pltpu.PrefetchScalarGridSpec(
+            num_scalar_prefetch=1,
+            grid=(),
+            in_specs=[pl.BlockSpec(memory_space=pl.ANY)] * 3,
+            out_specs=[vmem] * 5,
+            scratch_shapes=[
+                pltpu.SemaphoreType.DMA((4,)),
+                pltpu.VMEM(fir_taps.shape, F32),
+                pltpu.VMEM(table.shape, F32),
+            ],
+        ),
+        out_shape=[
+            jax.ShapeDtypeStruct((signals, frames, ROWS, LANES), BF16),
+            jax.ShapeDtypeStruct((signals, edge_frames, ROWS, LANES), BF16),
+            jax.ShapeDtypeStruct((TAPS * ROWS, LANES), F32),
+            jax.ShapeDtypeStruct((ROWS, 3 * ROWS), BF16),
+            jax.ShapeDtypeStruct((2, 2 * K2, 2 * LANES), BF16),
+        ],
+        compiler_params=pltpu.CompilerParams(vmem_limit_bytes=24 << 20),
+    )(
+        jnp.stack([jnp.asarray(v, jnp.int32) for v in (order, edge_block)]),
+        *[pltpu.with_memory_space_constraint(x, pltpu.HBM) for x in (volts, fir_taps, jnp.asarray(table))],
+    )
+
+
 def spectra_kernel(groups, parts, out_frames, place, *refs):
     part_refs, refs = refs[: len(parts)], refs[len(parts) :]
-    taps_ref, table_ref = refs[:2]
-    outs, (taps, one, two, ext, filtered, turned, staged) = refs[2:-7], refs[-7:]
-    step, steps, members = pl.program_id(0), pl.num_programs(0), part_refs[0].shape[0]
+    taps, one, two, turn = refs[:4]
+    outs, (ext, filtered, turned, staged) = refs[4:-4], refs[-4:]
+    step, steps, members = pl.program_id(0), pl.num_programs(0), MEMBERS
     per_group = K2 // groups
     share = LANES // out_frames
     tiles = H // share
     pairs = tiles // 2
     frame_rows, row_rows = ROWS + PAD, tiles * TILE + PAD
 
-    @pl.when(step == 0)
-    def _():
-        for h in range(H):
-            for half in range(TAPS // SUB):
-                tile = taps_ref[pl.ds(half * SUB, SUB), pl.ds(h * LANES, LANES)]
-                for r in range(2):
-                    taps[pl.ds(half * SUB * ROWS + 2 * h + r, SUB, stride=ROWS), :] = tile
-        high, low = halves(table_ref[:ROWS, :ROWS])
-        one[...] = jnp.concatenate([high, high, low], axis=1)
-        start = pl.multiple_of(ROWS + H + place[1] * 2 * K2, SUB)
-        high, low = halves(table_ref[pl.ds(start, 2 * K2), :])
-        two[0] = high
-        two[1] = low
-
     def load(member):
+        signal = step * members + member
         for number, (frames, ref) in enumerate(zip(parts, part_refs)):
-            start = place[2 + 3 * number + 1]
-            valid = place[2 + 3 * number + 2]
+            first = place[1 + 3 * number] * frames
+            start = place[1 + 3 * number + 1]
+            valid = place[1 + 3 * number + 2]
 
             @pl.when(valid == 1)
             def _():
                 for f in range(frames):
-                    ext[member, start + f] = ref[member, f].astype(F32)
+                    ext[member, start + f] = ref[signal, first + f].astype(F32)
 
             @pl.when(valid == 0)
             def _():
@@ -122,8 +164,8 @@
             filtered[member, f, rows] = total
 
     def first_stage(member):
-        cosine = table_ref[ROWS : ROWS + H, :LANES]
-        sine = table_ref[ROWS : ROWS + H, LANES:]
+        cosine = turn[:, :LANES]
+        sine = turn[:, LANES:]
         for g in range(out_frames // STEP):
             block = jnp.concatenate([filtered[member, g * STEP + f] for f in range(STEP)], axis=1)
             high, low = halves(block)
@@ -195,33 +237,21 @@
     return lax.optimization_barrier((value, *others))[0]
 
 
-def spectra(parts, out_frames, fir_taps, groups, sizes, run=1, order=0, wait=(), cost=10**6):
+def spectra(parts, out_frames, fixed, groups, sizes, run=1, wait=(), cost=10**6):
     signals = parts[0][0].shape[0]
-    numbers = [run, order] + [v for part in parts for v in part[2:]]
+    numbers = [run] + [v for part in parts for v in part[2:]]
     place = jnp.stack([jnp.asarray(v, jnp.int32) for v in numbers])
     place = after(place, *wait)
-    table = tables(groups)
     tiles = H * out_frames // LANES
-    whole = lambda shape: pl.BlockSpec(shape, lambda s, place: (0,) * len(shape))
-    in_specs = [
-        pl.BlockSpec(
-            (MEMBERS, part[1], ROWS, LANES), functools.partial(lambda n, s, place: (s, place[2 + 3 * n], 0, 0), n)
-        )
-        for n, part in enumerate(parts)
-    ]
-    in_specs += [whole((TAPS, NCH)), whole(table.shape)]
     shapes = [(n, tiles, TILE, LANES) for n in sizes]
     return pl.pallas_call(
         functools.partial(spectra_kernel, groups, tuple(p[1] for p in parts), out_frames),
         grid_spec=pltpu.PrefetchScalarGridSpec(
             num_scalar_prefetch=1,
             grid=(signals // MEMBERS,),
-            in_specs=in_specs,
-            out_specs=[whole(shape) for shape in shapes],
+            in_specs=[pl.BlockSpec(memory_space=pltpu.VMEM)] * (len(parts) + 4),
+            out_specs=[pl.BlockSpec(shape, lambda s, place: (0, 0, 0, 0)) for shape in shapes],
             scratch_shapes=[
-                pltpu.VMEM((TAPS * ROWS, LANES), F32),
-                pltpu.VMEM((ROWS, 3 * ROWS), BF16),
-                pltpu.VMEM((2, 2 * K2, 2 * LANES), BF16),
                 pltpu.VMEM((MEMBERS, TAPS + out_frames, ROWS, LANES), F32),
                 pltpu.VMEM((MEMBERS, out_frames, ROWS, LANES), F32),
                 pltpu.VMEM((MEMBERS, out_frames * (ROWS + PAD), LANES), F32),
@@ -230,10 +260,12 @@
         ),
         out_shape=[jax.ShapeDtypeStruct(shape, BF16) for shape in shapes],
         compiler_params=pltpu.CompilerParams(vmem_limit_bytes=32 << 20),
-        cost_estimate=pl.CostEstimate(
-            flops=cost, bytes_accessed=0, transcendentals=0
-        ),
-    )(place, *[part[0] for part in parts], fir_taps, table)
+        cost_estimate=pl.CostEstimate(flops=cost, bytes_accessed=0, transcendentals=0),
+    )(place, *[part[0] for part in parts], *fixed, jnp.asarray(turn_table(), F32))
+
+
+def after(value, *others):
+    return lax.optimization_barrier((value, *others))[0]
 
 
 def correlate_kernel(pieces, per_group, scale, add, last, place, *refs):
@@ -362,9 +394,10 @@
 def general(volts, fir_taps):
     groups = lax.axis_size("tm")
     frames = volts.shape[1]
-    history = lax.ppermute(volts[:, frames - TAPS :], "tm", [(i, i + 1) for i in range(groups - 1)])
+    volts, edge_frames, *fixed = prepare(volts, fir_taps, groups, 0, frames // TAPS - 1, TAPS)
+    history = lax.ppermute(edge_frames, "tm", [(i, i + 1) for i in range(groups - 1)])
     parts = [(history, TAPS, 0, 0, 1)] + [(volts, TAPS, i, TAPS * (i + 1), 1) for i in range(frames // TAPS)]
-    spectrum = spectra(parts, frames, fir_taps, groups, [K2])[0]
+    spectrum = spectra(parts, frames, fixed, groups, [K2])[0]
     spectrum = lax.all_to_all(spectrum, "tm", split_axis=0, concat_axis=0, tiled=True)
     tiles = spectrum.shape[1]
     return [([spectrum], [(tiles, [(0, K2 // groups * t, 0) for t in range(groups)])])]
@@ -377,15 +410,15 @@
     swap = [(0, 1), (1, 0)]
     edge = TAPS // 2
     last = frames // edge
-    edge_frames = lax.dynamic_slice_in_dim(volts, jnp.where(me == 0, frames - edge, 0), edge, 1)
+    volts, edge_frames, *fixed = prepare(volts, fir_taps, 2, me, jnp.where(me == 0, frames // edge - 1, 0), edge)
     visiting = lax.ppermute(edge_frames, "tm", swap)
     own_a, away_a = spectra(
-        [(volts, TAPS, 0, 0, me), (volts, TAPS, me, TAPS, 1)], TAPS, fir_taps, 2, sizes, 1, me, (edge_frames,)
+        [(volts, TAPS, 0, 0, me), (volts, TAPS, me, TAPS, 1)], TAPS, fixed, 2, sizes
     )
     got_a = lax.ppermute(away_a, "tm", swap)
     two_a, rest_a = farther(own_a)
     own_b, away_b = spectra(
-        [(volts, TAPS, 0, 0, 1), (volts, TAPS, 1, TAPS, 1)], TAPS, fir_taps, 2, sizes, 1 - me, me, (own_a,)
+        [(volts, TAPS, 0, 0, 1), (volts, TAPS, 1, TAPS, 1)], TAPS, fixed, 2, sizes, 1 - me, (own_a,)
     )
     got_b = lax.ppermute(away_b, "tm", [(0, 1)])
     pair_a = exchanged(two_a)
@@ -395,7 +428,7 @@
             (volts, edge, jnp.where(me == 0, last - 1, 1), edge * me + edge, 1),
             (visiting, edge, 0, 2 * edge * (1 - me), 1),
         ],
-        edge, fir_taps, 2, sizes, 1, me, (own_b, two_a, got_a), 9 * 10**9,
+        edge, fixed, 2, sizes, 1, (own_b, two_a, got_a), 9 * 10**9,
     )
     got_c = lax.ppermute(away_c, "tm", swap)
     two_g, rest_g = farther(got_a)
@@ -403,11 +436,11 @@
     own_c = after(own_c, two_g, pair_a, rest_a)
     rest = jnp.concatenate([jnp.where(me == 0, own_b, got_b), own_c, got_c], axis=1)
     two_r, rest_r = farther(rest)
-    pair_r = exchanged(two_r)
     many, few = own_a.shape[1], own_c.shape[1]
     sums = correlated(
         [own_a, pair_a, two_a, rest_a, got_a, pair_g, two_g, rest_g], [(many, [(0, 0, 0), (1, 0, 0)])], None, False
     )
+    pair_r = exchanged(after(two_r, sums))
     return correlated(
         [rest, pair_r, two_r, rest_r], [(many, [(0, 0, 0)]), (few, [(0, 0, many), (0, 0, many + few)])], sums, True
     )
@@ -416,9 +449,10 @@
 def general(volts, fir_taps, correlated):
     groups = lax.axis_size("tm")
     frames = volts.shape[1]
-    history = lax.ppermute(volts[:, frames - TAPS :], "tm", [(i, i + 1) for i in range(groups - 1)])
+    volts, edge_frames, *fixed = prepare(volts, fir_taps, groups, 0, frames // TAPS - 1, TAPS)
+    history = lax.ppermute(edge_frames, "tm", [(i, i + 1) for i in range(groups - 1)])
     parts = [(history, TAPS, 0, 0, 1)] + [(volts, TAPS, i, TAPS * (i + 1), 1) for i in range(frames // TAPS)]
-    spectrum = spectra(parts, frames, fir_taps, groups, [K2])[0]
+    spectrum = spectra(parts, frames, fixed, groups, [K2])[0]
     spectrum = lax.all_to_all(spectrum, "tm", split_axis=0, concat_axis=0, tiled=True)
     two, rest = farther(spectrum)
     spots = [(0, K2 // groups * t, 0) for t in range(groups)]

time: 117 us -> 112 us (0.957)
  the two profiles are of different devices: /device:TPU:2 before, /device:TPU:6 now
where the time goes in v6:
time: 112 us
  waiting for transfers between devices  49.4 us (44%)
  Pallas kernels  42.5 us (38%)
  local copies, waits for them, and re-layouts  9.82 us (9%)
  starting transfers between devices  8.76 us (8%)
  other arithmetic  1.3 us (1%)
    ppermute x3, waiting for transfers between devices, shifted(): lax.ppermute(block, axis, [(i, (i + distance) % size) for i in range(size)])  23.7 us
    pallas_call x3, Pallas kernels, spectra(): pl.pallas_call(functools.partial(spectra_kernel, groups, tuple((p[1] for...  20.8 us
    pallas_call x2, Pallas kernels, correlate(): pl.pallas_call(functools.partial(correlate_kernel, pieces, per_group, sca...  18.4 us
    ppermute x3, waiting for transfers between devices, farther(): lax.ppermute(block, 'stn', [(i, (i + 1 if i % 2 == 0 else i + 3) % size)...  12.8 us
    unnamed x16, local copies, waits for them, and re-layouts  9.56 us
    ppermute x1, waiting for transfers between devices, paired(): got_a = lax.ppermute(away_a, 'tm', swap)  6.84 us
    ppermute x1, waiting for transfers between devices, paired(): got_c = lax.ppermute(away_c, 'tm', swap)  6.08 us
    ppermute x3, starting transfers between devices, shifted(): lax.ppermute(block, axis, [(i, (i + distance) % size) for i in range(size)])  4.32 us
  transfers between devices with their start and end apart: 13, of which 6 were waited for; matrix products, arithmetic and copies ran while one was open for 1% of the time, Pallas kernels for 25%

profile of v6, /device:TPU:6, one launch (start us, length us, event | category | flops | bytes accessed | tf_op | source)
XLA Modules:
  0.0 111.9 jit_solution(3517823929440776304)
XLA Ops:
  0.0 0.0 copy-start.4
  0.0 0.1 pad_add_fusion.place
  0.1 3.3 %shard_map.82 = (bf16[8,32,64,128]{3,2,1,0:T(8,128)(2,1)S(1)}, bf16[8,8,64,128]{3,2,1,0:T(8,128)(2,1)S(1)}, f32[1024,128]{1,0:T(8,128)S(1)}, bf16[64,192]{1,0:T(8,128)(2,1)S(1)}, bf16[2,128,256]{2,1,0:T(8,128)(2,1)S(1)}) custom-call(s32[2]{0:T(128)S(1)} %pad_add_fusion.place, bf16[8,32,64,128]{3,2,1,0:T(8,128)(2,1)} %bitcast.16, f32[16,4096]{1,0:T(8,128)} %taps_source.1, ...), custom_call_target="tpu_custom_call" | custom-call | tf_op jit(solution)/shard_map/pallas_call | solution.py:102
  3.4 0.0 copy-start
  3.4 1.9 %copy-done = bf16[8,32,64,128]{3,2,1,0:T(8,128)(2,1)} copy-done((bf16[8,32,64,128]{3,2,1,0:T(8,128)(2,1)}, bf16[8,32,64,128]{3,2,1,0:T(8,128)(2,1)S(1)}, u32[]{:S(2)}) %copy-start) | copy-done | bytes 4194328
  5.3 0.5 collective-permute-start.3
  5.8 0.1 stack.41.place
  5.9 0.0 copy-done.4
  5.9 0.0 copy-start.1
  5.9 2.2 %copy-done.1 = bf16[8,32,64,128]{3,2,1,0:T(8,128)(2,1)S(1)} copy-done((bf16[8,32,64,128]{3,2,1,0:T(8,128)(2,1)S(1)}, bf16[8,32,64,128]{3,2,1,0:T(8,128)(2,1)}, u32[]{:S(2)}) %copy-start.1) | copy-done | bytes 4194328
  8.1 12.4 %shard_map.83 = (bf16[32,4,16,128]{3,2,1,0:T(8,128)(2,1)}, bf16[32,4,16,128]{3,2,1,0:T(8,128)(2,1)}) custom-call(s32[7]{0:T(128)S(1)} %stack.41.place, bf16[8,32,64,128]{3,2,1,0:T(8,128)(2,1)S(1)} %copy-done.1, bf16[8,32,64,128]{3,2,1,0:T(8,128)(2,1)S(1)} %copy-done.1, f32[1024,128]{1,0:T(8,128)S(1)} %get-tuple-element.21.refs_2_.refs_3_, ...), custom_call_target="tpu_custom_call" | custom-call | flops 1000000 | tf_op jit(solution)/shard_map/pallas_call | solution.py:247
  20.5 1.6 %collective-permute-start.1 = (bf16[32,4,16,128]{3,2,1,0:T(8,128)(2,1)}, bf16[32,4,16,128]{3,2,1,0:T(8,128)(2,1)}, u32[]{:S(2)}, u32[]{:S(2)}) collective-permute-start(bf16[32,4,16,128]{3,2,1,0:T(8,128)(2,1)} %get-tuple-element.24.refs_0_), channel_id=1, source_target_pairs={{0,4},{2,6},{4,8},{6,10},{8,12},{10,14},{12,16},{14,18},{16,20},{1... | collective-permute-start | bytes 1572872 | tf_op jit(solution)/shard_map/ppermute | solution.py:381
  22.0 1.5 %collective-permute-start.2 = (bf16[32,4,16,128]{3,2,1,0:T(8,128)(2,1)}, bf16[32,4,16,128]{3,2,1,0:T(8,128)(2,1)}, u32[]{:S(2)}, u32[]{:S(2)}) collective-permute-start(bf16[32,4,16,128]{3,2,1,0:T(8,128)(2,1)} %get-tuple-element.28), channel_id=1, source_target_pairs={{0,1},{1,0},{2,3},{3,2},{4,5},{5,4},{6,7},{7,6},{8,9},{9,8},{10,11... | collective-permute-start | bytes 1572872 | tf_op jit(solution)/shard_map/ppermute | solution.py:418
  23.5 0.0 collective-permute-start.6
  23.5 0.1 stack.39.place
  23.6 0.0 copy-start.2
  23.6 2.2 %copy-done.2 = bf16[8,32,64,128]{3,2,1,0:T(8,128)(2,1)S(1)} copy-done((bf16[8,32,64,128]{3,2,1,0:T(8,128)(2,1)S(1)}, bf16[8,32,64,128]{3,2,1,0:T(8,128)(2,1)}, u32[]{:S(2)}) %copy-start.2) | copy-done | bytes 4194328
  25.8 1.4 %shard_map.84 = (bf16[32,4,16,128]{3,2,1,0:T(8,128)(2,1)S(1)}, bf16[32,4,16,128]{3,2,1,0:T(8,128)(2,1)}) custom-call(s32[7]{0:T(128)S(1)} %stack.39.place, bf16[8,32,64,128]{3,2,1,0:T(8,128)(2,1)S(1)} %copy-done.2, bf16[8,32,64,128]{3,2,1,0:T(8,128)(2,1)S(1)} %copy-done.2, f32[1024,128]{1,0:T(8,128)S(1)} %get-tuple-element.21.refs_2_.refs_3_, ...), custom_call_target="tpu_custom_call" | custom-call | flops 1000000 | tf_op jit(solution)/shard_map/pallas_call | solution.py:247
  27.2 1.3 %collective-permute-start = (bf16[32,4,16,128]{3,2,1,0:T(8,128)(2,1)}, bf16[32,4,16,128]{3,2,1,0:T(8,128)(2,1)}, u32[]{:S(2)}, u32[]{:S(2)}) collective-permute-start(bf16[32,4,16,128]{3,2,1,0:T(8,128)(2,1)} %get-tuple-element.27), channel_id=1, source_target_pairs={{0,1},{2,3},{4,5},{6,7},{8,9},{10,11},{12,13},{14,15},{16,17},{18,... | collective-permute-start | bytes 1572872 | tf_op jit(solution)/shard_map/ppermute | solution.py:423
  28.5 0.1 stack.49.place
  28.6 6.1 %collective-permute-done.1.refs_2_ = bf16[32,4,16,128]{3,2,1,0:T(8,128)(2,1)} collective-permute-done((bf16[32,4,16,128]{3,2,1,0:T(8,128)(2,1)}, bf16[32,4,16,128]{3,2,1,0:T(8,128)(2,1)}, u32[]{:S(2)}, u32[]{:S(2)}) %collective-permute-start.1) | collective-permute-done | bytes 524320 | tf_op jit(solution)/shard_map/ppermute | solution.py:381
  34.7 6.8 %collective-permute-done.2.refs_4_ = bf16[32,4,16,128]{3,2,1,0:T(8,128)(2,1)} collective-permute-done((bf16[32,4,16,128]{3,2,1,0:T(8,128)(2,1)}, bf16[32,4,16,128]{3,2,1,0:T(8,128)(2,1)}, u32[]{:S(2)}, u32[]{:S(2)}) %collective-permute-start.2) | collective-permute-done | bytes 524320 | tf_op jit(solution)/shard_map/ppermute | solution.py:418
  41.6 0.0 copy-start.7
  41.6 1.5 %collective-permute-start.4 = (bf16[32,4,16,128]{3,2,1,0:T(8,128)(2,1)}, bf16[32,4,16,128]{3,2,1,0:T(8,128)(2,1)}, u32[]{:S(2)}, u32[]{:S(2)}) collective-permute-start(bf16[32,4,16,128]{3,2,1,0:T(8,128)(2,1)} %collective-permute-done.2.refs_4_), channel_id=1, source_target_pairs={{0,4},{2,6},{4,8},{6,10},{8,12},{10,14},{12,16},{14,18},{16,20},{1... | collective-permute-start | bytes 1572872 | tf_op jit(solution)/shard_map/ppermute | solution.py:381
  43.1 0.0 collective-permute-start.5
  43.1 0.0 collective-permute-done.3.refs_2_
  43.1 0.5 collective-permute-start.10
  43.6 0.0 copy-start.3
  43.6 2.2 %copy-done.3 = bf16[8,32,64,128]{3,2,1,0:T(8,128)(2,1)S(1)} copy-done((bf16[8,32,64,128]{3,2,1,0:T(8,128)(2,1)S(1)}, bf16[8,32,64,128]{3,2,1,0:T(8,128)(2,1)}, u32[]{:S(2)}) %copy-start.3) | copy-done | bytes 4194328
  45.8 7.0 %shard_map.85 = (bf16[32,2,16,128]{3,2,1,0:T(8,128)(2,1)S(1)}, bf16[32,2,16,128]{3,2,1,0:T(8,128)(2,1)S(1)}) custom-call(s32[10]{0:T(128)S(1)} %stack.49.place, bf16[8,32,64,128]{3,2,1,0:T(8,128)(2,1)S(1)} %copy-done.3, bf16[8,32,64,128]{3,2,1,0:T(8,128)(2,1)S(1)} %copy-done.3, bf16[8,8,64,128]{3,2,1,0:T(8,128)(2,1)S(1)} %collective-permute-done.3.refs_2_, ...), custom_call_target="tpu_custom_call" | custom-call | flops 8999999488 | tf_op jit(solution)/shard_map/pallas_call | solution.py:247
  52.8 0.0 collective-permute-done
  52.8 0.6 collective-permute-start.7
  53.4 1.1 broadcast_select_fusion
  54.5 0.0 collective-permute-done.6.refs_3_
  54.5 1.3 %collective-permute-done.4.refs_6_ = bf16[32,4,16,128]{3,2,1,0:T(8,128)(2,1)} collective-permute-done((bf16[32,4,16,128]{3,2,1,0:T(8,128)(2,1)}, bf16[32,4,16,128]{3,2,1,0:T(8,128)(2,1)}, u32[]{:S(2)}, u32[]{:S(2)}) %collective-permute-start.4) | collective-permute-done | bytes 524320 | tf_op jit(solution)/shard_map/ppermute | solution.py:381
  55.8 0.0 collective-permute-done.5.refs_1_
  55.8 0.0 copy-start.5
  55.8 0.0 collective-permute-start.9
  55.8 6.1 %collective-permute-done.7 = bf16[32,2,16,128]{3,2,1,0:T(8,128)(2,1)S(1)} collective-permute-done((bf16[32,2,16,128]{3,2,1,0:T(8,128)(2,1)S(1)}, bf16[32,2,16,128]{3,2,1,0:T(8,128)(2,1)S(1)}, u32[]{:S(2)}, u32[]{:S(2)}) %collective-permute-start.7) | collective-permute-done | bytes 262176 | tf_op jit(solution)/shard_map/ppermute | solution.py:433
  61.9 0.1 pad_maximum_fusion.refs_0_
  62.0 0.0 copy-done.5
  62.0 1.2 %collective-permute-start.8 = (bf16[32,8,16,128]{3,2,1,0:T(8,128)(2,1)S(1)}, bf16[32,8,16,128]{3,2,1,0:T(8,128)(2,1)S(1)}, u32[]{:S(2)}, u32[]{:S(2)}) collective-permute-start(bf16[32,8,16,128]{3,2,1,0:T(8,128)(2,1)S(1)} %pad_maximum_fusion.refs_0_), channel_id=1, source_target_pairs={{0,4},{2,6},{4,8},{6,10},{8,12},{10,14},{12,16},{14,18},{16,20},{1... | collective-permute-start | bytes 3145736 | tf_op jit(solution)/shard_map/ppermute | solution.py:381
  63.2 0.0 copy-done.7
  63.2 0.1 collective-permute-start.12
  63.3 0.0 collective-permute-done.10.refs_7_
  63.3 0.0 collective-permute-done.9.refs_5_
  63.3 0.0 copy-start.6
  63.3 1.0 copy-done.6
  64.4 6.8 %shard_map.86.refs_4_ = f32[4096,128]{1,0:T(8,128)} custom-call(s32[4]{0:T(128)S(1)} %broadcast_select_fusion.1.place, bf16[32,4,16,128]{3,2,1,0:T(8,128)(2,1)} %get-tuple-element.24.refs_0_, bf16[32,4,16,128]{3,2,1,0:T(8,128)(2,1)S(1)} %copy-done.6, bf16[32,4,16,128]{3,2,1,0:T(8,128)(2,1)} %collective-permute-done.1.refs_2_, ...), custom_call_target="tpu_custom_call" | custom-call | flops 6000000000 | tf_op jit(solution)/shard_map/pallas_call | solution.py:353
  71.1 16.3 %collective-permute-done.8.refs_2_ = bf16[32,8,16,128]{3,2,1,0:T(8,128)(2,1)S(1)} collective-permute-done((bf16[32,8,16,128]{3,2,1,0:T(8,128)(2,1)S(1)}, bf16[32,8,16,128]{3,2,1,0:T(8,128)(2,1)S(1)}, u32[]{:S(2)}, u32[]{:S(2)}) %collective-permute-start.8) | collective-permute-done | bytes 1048608 | tf_op jit(solution)/shard_map/ppermute | solution.py:381
  87.4 0.0 collective-permute-start.11
  87.4 12.8 %collective-permute-done.12.refs_3_ = bf16[32,8,16,128]{3,2,1,0:T(8,128)(2,1)S(1)} collective-permute-done((bf16[32,8,16,128]{3,2,1,0:T(8,128)(2,1)S(1)}, bf16[32,8,16,128]{3,2,1,0:T(8,128)(2,1)S(1)}, u32[]{:S(2)}, u32[]{:S(2)}) %collective-permute-start.12) | collective-permute-done | bytes 1048608 | tf_op jit(solution)/shard_map/ppermute | solution.py:386
  100.2 0.0 collective-permute-done.11.refs_1_
  100.2 11.7 %shard_map.87 = f32[2,8,4,8,8,128]{5,4,3,2,1,0:T(8,128)} custom-call(s32[4]{0:T(128)S(1)} %broadcast_select_fusion.1.place, bf16[32,8,16,128]{3,2,1,0:T(8,128)(2,1)S(1)} %pad_maximum_fusion.refs_0_, bf16[32,8,16,128]{3,2,1,0:T(8,128)(2,1)S(1)} %collective-permute-done.11.refs_1_, bf16[32,8,16,128]{3,2,1,0:T(8,128)(2,1)S(1)} %collective-permute-done.8.refs_2_, ...), custom_call_target="tpu_custom_call" | custom-call | flops 6000000000 | tf_op jit(solution)/shard_map/pallas_call | solution.py:353
  (3 shorter events, 0.0 us)
Async XLA Ops:
  0.0 5.9 %copy-start.4 = (f32[32,256]{1,0:T(8,128)S(1)}, f32[32,256]{1,0:T(8,128)}, u32[]{:S(2)}) copy-start(f32[32,256]{1,0:T(8,128)} %constant.47.clone.refs_5_.refs_6_) | copy-start | bytes 98308
  3.4 1.9 %copy-start = (bf16[8,32,64,128]{3,2,1,0:T(8,128)(2,1)}, bf16[8,32,64,128]{3,2,1,0:T(8,128)(2,1)S(1)}, u32[]{:S(2)}) copy-start(bf16[8,32,64,128]{3,2,1,0:T(8,128)(2,1)S(1)} %get-tuple-element.20.refs_0_.refs_1_) | copy-start | bytes 12582916
  5.3 37.8 %collective-permute-start.3 = (bf16[8,8,64,128]{3,2,1,0:T(8,128)(2,1)S(1)}, bf16[8,8,64,128]{3,2,1,0:T(8,128)(2,1)S(1)}, u32[]{:S(2)}, u32[]{:S(2)}) collective-permute-start(bf16[8,8,64,128]{3,2,1,0:T(8,128)(2,1)S(1)} %get-tuple-element.30), channel_id=1, source_target_pairs={{0,1},{1,0},{2,3},{3,2},{4,5},{5,4},{6,7},{7,6},{8,9},{9,8},{10,11... | collective-permute-start | bytes 3145736 | tf_op jit(solution)/shard_map/ppermute | solution.py:414
  5.9 2.2 %copy-start.1 = (bf16[8,32,64,128]{3,2,1,0:T(8,128)(2,1)S(1)}, bf16[8,32,64,128]{3,2,1,0:T(8,128)(2,1)}, u32[]{:S(2)}) copy-start(bf16[8,32,64,128]{3,2,1,0:T(8,128)(2,1)} %copy-done) | copy-start | bytes 12582916
  20.5 14.2 %collective-permute-start.1 = (bf16[32,4,16,128]{3,2,1,0:T(8,128)(2,1)}, bf16[32,4,16,128]{3,2,1,0:T(8,128)(2,1)}, u32[]{:S(2)}, u32[]{:S(2)}) collective-permute-start(bf16[32,4,16,128]{3,2,1,0:T(8,128)(2,1)} %get-tuple-element.24.refs_0_), channel_id=1, source_target_pairs={{0,4},{2,6},{4,8},{6,10},{8,12},{10,14},{12,16},{14,18},{16,20},{1... | collective-permute-start | bytes 1572872 | tf_op jit(solution)/shard_map/ppermute | solution.py:381
  22.0 19.5 %collective-permute-start.2 = (bf16[32,4,16,128]{3,2,1,0:T(8,128)(2,1)}, bf16[32,4,16,128]{3,2,1,0:T(8,128)(2,1)}, u32[]{:S(2)}, u32[]{:S(2)}) collective-permute-start(bf16[32,4,16,128]{3,2,1,0:T(8,128)(2,1)} %get-tuple-element.28), channel_id=1, source_target_pairs={{0,1},{1,0},{2,3},{3,2},{4,5},{5,4},{6,7},{7,6},{8,9},{9,8},{10,11... | collective-permute-start | bytes 1572872 | tf_op jit(solution)/shard_map/ppermute | solution.py:418
  23.5 31.0 %collective-permute-start.6 = (bf16[32,4,16,128]{3,2,1,0:T(8,128)(2,1)}, bf16[32,4,16,128]{3,2,1,0:T(8,128)(2,1)}, u32[]{:S(2)}, u32[]{:S(2)}) collective-permute-start(bf16[32,4,16,128]{3,2,1,0:T(8,128)(2,1)} %get-tuple-element.24.refs_0_), channel_id=1, source_target_pairs={{0,2},{2,8},{4,6},{6,12},{8,10},{10,16},{12,14},{14,20},{16,18},{1... | collective-permute-start | bytes 1572872 | tf_op jit(solution)/shard_map/ppermute | solution.py:386
  23.6 2.2 %copy-start.2 = (bf16[8,32,64,128]{3,2,1,0:T(8,128)(2,1)S(1)}, bf16[8,32,64,128]{3,2,1,0:T(8,128)(2,1)}, u32[]{:S(2)}) copy-start(bf16[8,32,64,128]{3,2,1,0:T(8,128)(2,1)} %copy-done) | copy-start | bytes 12582916
  27.2 25.7 %collective-permute-start = (bf16[32,4,16,128]{3,2,1,0:T(8,128)(2,1)}, bf16[32,4,16,128]{3,2,1,0:T(8,128)(2,1)}, u32[]{:S(2)}, u32[]{:S(2)}) collective-permute-start(bf16[32,4,16,128]{3,2,1,0:T(8,128)(2,1)} %get-tuple-element.27), channel_id=1, source_target_pairs={{0,1},{2,3},{4,5},{6,7},{8,9},{10,11},{12,13},{14,15},{16,17},{18,... | collective-permute-start | bytes 1572872 | tf_op jit(solution)/shard_map/ppermute | solution.py:423
  41.6 21.7 %copy-start.7 = (s32[4]{0:T(128)S(1)}, s32[4]{0:T(128)}, u32[]{:S(2)}) copy-start(s32[4]{0:T(128)} %constant.45.clone) | copy-start | bytes 52
  41.6 14.2 %collective-permute-start.4 = (bf16[32,4,16,128]{3,2,1,0:T(8,128)(2,1)}, bf16[32,4,16,128]{3,2,1,0:T(8,128)(2,1)}, u32[]{:S(2)}, u32[]{:S(2)}) collective-permute-start(bf16[32,4,16,128]{3,2,1,0:T(8,128)(2,1)} %collective-permute-done.2.refs_4_), channel_id=1, source_target_pairs={{0,4},{2,6},{4,8},{6,10},{8,12},{10,14},{12,16},{14,18},{16,20},{1... | collective-permute-start | bytes 1572872 | tf_op jit(solution)/shard_map/ppermute | solution.py:381
  43.1 12.7 %collective-permute-start.5 = (bf16[32,4,16,128]{3,2,1,0:T(8,128)(2,1)}, bf16[32,4,16,128]{3,2,1,0:T(8,128)(2,1)S(1)}, u32[]{:S(2)}, u32[]{:S(2)}) collective-permute-start(bf16[32,4,16,128]{3,2,1,0:T(8,128)(2,1)} %collective-permute-done.1.refs_2_), channel_id=1, source_target_pairs={{0,2},{2,0},{4,6},{6,4},{8,10},{10,8},{12,14},{14,12},{16,18},{18,... | collective-permute-start | bytes 1572872 | tf_op jit(solution)/shard_map/ppermute | solution.py:391
  43.1 20.2 %collective-permute-start.10 = (bf16[32,4,16,128]{3,2,1,0:T(8,128)(2,1)}, bf16[32,4,16,128]{3,2,1,0:T(8,128)(2,1)S(1)}, u32[]{:S(2)}, u32[]{:S(2)}) collective-permute-start(bf16[32,4,16,128]{3,2,1,0:T(8,128)(2,1)} %collective-permute-done.2.refs_4_), channel_id=1, source_target_pairs={{0,2},{2,8},{4,6},{6,12},{8,10},{10,16},{12,14},{14,20},{16,18},{1... | collective-permute-start | bytes 1572872 | tf_op jit(solution)/shard_map/ppermute | solution.py:386
  43.6 2.2 %copy-start.3 = (bf16[8,32,64,128]{3,2,1,0:T(8,128)(2,1)S(1)}, bf16[8,32,64,128]{3,2,1,0:T(8,128)(2,1)}, u32[]{:S(2)}) copy-start(bf16[8,32,64,128]{3,2,1,0:T(8,128)(2,1)} %copy-done) | copy-start | bytes 12582916
  52.8 9.0 %collective-permute-start.7 = (bf16[32,2,16,128]{3,2,1,0:T(8,128)(2,1)S(1)}, bf16[32,2,16,128]{3,2,1,0:T(8,128)(2,1)S(1)}, u32[]{:S(2)}, u32[]{:S(2)}) collective-permute-start(bf16[32,2,16,128]{3,2,1,0:T(8,128)(2,1)S(1)} %get-tuple-element.33), channel_id=1, source_target_pairs={{0,1},{1,0},{2,3},{3,2},{4,5},{5,4},{6,7},{7,6},{8,9},{9,8},{10,11... | collective-permute-start | bytes 786440 | tf_op jit(solution)/shard_map/ppermute | solution.py:433
  55.8 6.2 %copy-start.5 = (bf16[32,4,16,128]{3,2,1,0:T(8,128)(2,1)}, bf16[32,4,16,128]{3,2,1,0:T(8,128)(2,1)S(1)}, u32[]{:S(2)}) copy-start(bf16[32,4,16,128]{3,2,1,0:T(8,128)(2,1)S(1)} %collective-permute-done.5.refs_1_) | copy-start | bytes 1572868
  55.8 7.5 %collective-permute-start.9 = (bf16[32,4,16,128]{3,2,1,0:T(8,128)(2,1)}, bf16[32,4,16,128]{3,2,1,0:T(8,128)(2,1)S(1)}, u32[]{:S(2)}, u32[]{:S(2)}) collective-permute-start(bf16[32,4,16,128]{3,2,1,0:T(8,128)(2,1)} %collective-permute-done.4.refs_6_), channel_id=1, source_target_pairs={{0,2},{2,0},{4,6},{6,4},{8,10},{10,8},{12,14},{14,12},{16,18},{18,... | collective-permute-start | bytes 1572872 | tf_op jit(solution)/shard_map/ppermute | solution.py:391
  62.0 25.4 %collective-permute-start.8 = (bf16[32,8,16,128]{3,2,1,0:T(8,128)(2,1)S(1)}, bf16[32,8,16,128]{3,2,1,0:T(8,128)(2,1)S(1)}, u32[]{:S(2)}, u32[]{:S(2)}) collective-permute-start(bf16[32,8,16,128]{3,2,1,0:T(8,128)(2,1)S(1)} %pad_maximum_fusion.refs_0_), channel_id=1, source_target_pairs={{0,4},{2,6},{4,8},{6,10},{8,12},{10,14},{12,16},{14,18},{16,20},{1... | collective-permute-start | bytes 3145736 | tf_op jit(solution)/shard_map/ppermute | solution.py:381
  63.2 36.9 %collective-permute-start.12 = (bf16[32,8,16,128]{3,2,1,0:T(8,128)(2,1)S(1)}, bf16[32,8,16,128]{3,2,1,0:T(8,128)(2,1)S(1)}, u32[]{:S(2)}, u32[]{:S(2)}) collective-permute-start(bf16[32,8,16,128]{3,2,1,0:T(8,128)(2,1)S(1)} %pad_maximum_fusion.refs_0_), channel_id=1, source_target_pairs={{0,2},{2,8},{4,6},{6,12},{8,10},{10,16},{12,14},{14,20},{16,18},{1... | collective-permute-start | bytes 3145736 | tf_op jit(solution)/shard_map/ppermute | solution.py:386
  63.3 1.0 copy-start.6
  87.4 12.8 %collective-permute-start.11 = (bf16[32,8,16,128]{3,2,1,0:T(8,128)(2,1)S(1)}, bf16[32,8,16,128]{3,2,1,0:T(8,128)(2,1)S(1)}, u32[]{:S(2)}, u32[]{:S(2)}) collective-permute-start(bf16[32,8,16,128]{3,2,1,0:T(8,128)(2,1)S(1)} %collective-permute-done.8.refs_2_), channel_id=1, source_target_pairs={{0,2},{2,0},{4,6},{6,4},{8,10},{10,8},{12,14},{14,12},{16,18},{18,... | collective-permute-start | bytes 3145736 | tf_op jit(solution)/shard_map/ppermute | solution.py:391

commit v7 on v6

--- a/solution.py
+++ b/solution.py
@@ -19,6 +19,7 @@
 K2 = CHANS // H
 STEP = 8
 TILE = 16
+PLACES = (0, (1, 3), 2, (3, 1))
 MEMBERS = 4
 PAD = 8
 SUB = 8
@@ -66,14 +67,21 @@
     return lax.dot_general(left, right, (((1,), (1,)), ((), ())), preferred_element_type=F32)
 
 
-def prepare_kernel(place, volts_source, taps_source, table_source, volts, edge, taps, one, two, done, taps_ref, table_ref):
+def value_of(number, group):
+    if isinstance(number, int):
+        return number
+    return number[0] + (number[1] - number[0]) * group
+
+
+def prepare_kernel(edge_block, swapped, place, volts_source, taps_source, table_source, turn_source, volts, edge, taps, one, two, turn, done, taps_ref, table_ref):
     count = edge.shape[1]
-    start = pl.multiple_of(place[1] * count, count)
+    start = pl.multiple_of(value_of(edge_block, place[0]) * count, count)
     copies = [
         pltpu.make_async_copy(taps_source, taps_ref, done.at[0]),
         pltpu.make_async_copy(table_source, table_ref, done.at[1]),
         pltpu.make_async_copy(volts_source.at[:, pl.ds(start, count)], edge, done.at[2]),
         pltpu.make_async_copy(volts_source, volts, done.at[3]),
+        pltpu.make_async_copy(turn_source, turn, done.at[4]),
     ]
     for copy in copies:
         copy.start()
@@ -86,28 +94,28 @@
                 taps[pl.ds(half * SUB * ROWS + 2 * h + r, SUB, stride=ROWS), :] = tile
     high, low = halves(table_ref[:ROWS, :ROWS])
     one[...] = jnp.concatenate([high, high, low], axis=1)
-    start = pl.multiple_of(ROWS + place[0] * 2 * K2, SUB)
+    start = pl.multiple_of(ROWS + place[0] * (2 * K2 * swapped), SUB)
     high, low = halves(table_ref[pl.ds(start, 2 * K2), :])
     two[0] = high
     two[1] = low
-    copies[2].wait()
-    copies[3].wait()
-
-
-def prepare(volts, fir_taps, groups, order, edge_block, edge_frames):
+    for copy in copies[2:]:
+        copy.wait()
+
+
+def prepare(volts, fir_taps, place, groups, edge_block, edge_frames):
     signals, frames = volts.shape[:2]
     two = stage_two_table(groups)
     table = np.concatenate([stage_one_table(), two, np.roll(two, K2, axis=0)]).astype(np.float32)
     vmem = pl.BlockSpec(memory_space=pltpu.VMEM)
     return pl.pallas_call(
-        prepare_kernel,
+        functools.partial(prepare_kernel, edge_block, int(groups == 2)),
         grid_spec=pltpu.PrefetchScalarGridSpec(
             num_scalar_prefetch=1,
             grid=(),
-            in_specs=[pl.BlockSpec(memory_space=pl.ANY)] * 3,
-            out_specs=[vmem] * 5,
+            in_specs=[pl.BlockSpec(memory_space=pl.ANY)] * 4,
+            out_specs=[vmem] * 6,
             scratch_shapes=[
-                pltpu.SemaphoreType.DMA((4,)),
+                pltpu.SemaphoreType.DMA((5,)),
                 pltpu.VMEM(fir_taps.shape, F32),
                 pltpu.VMEM(table.shape, F32),
             ],
@@ -118,15 +126,19 @@
             jax.ShapeDtypeStruct((TAPS * ROWS, LANES), F32),
             jax.ShapeDtypeStruct((ROWS, 3 * ROWS), BF16),
             jax.ShapeDtypeStruct((2, 2 * K2, 2 * LANES), BF16),
+            jax.ShapeDtypeStruct((H, 2 * LANES), F32),
         ],
         compiler_params=pltpu.CompilerParams(vmem_limit_bytes=24 << 20),
     )(
-        jnp.stack([jnp.asarray(v, jnp.int32) for v in (order, edge_block)]),
-        *[pltpu.with_memory_space_constraint(x, pltpu.HBM) for x in (volts, fir_taps, jnp.asarray(table))],
-    )
-
-
-def spectra_kernel(groups, parts, out_frames, place, *refs):
+        place,
+        *[
+            pltpu.with_memory_space_constraint(x, pltpu.HBM)
+            for x in (volts, fir_taps, jnp.asarray(table), jnp.asarray(turn_table(), F32))
+        ],
+    )
+
+
+def spectra_kernel(groups, parts, out_frames, run, place, *refs):
     part_refs, refs = refs[: len(parts)], refs[len(parts) :]
     taps, one, two, turn = refs[:4]
     outs, (ext, filtered, turned, staged) = refs[4:-4], refs[-4:]
@@ -139,20 +151,24 @@
 
     def load(member):
         signal = step * members + member
-        for number, (frames, ref) in enumerate(zip(parts, part_refs)):
-            first = place[1 + 3 * number] * frames
-            start = place[1 + 3 * number + 1]
-            valid = place[1 + 3 * number + 2]
-
-            @pl.when(valid == 1)
-            def _():
+        for (frames, block, start, valid), ref in zip(parts, part_refs):
+            first = value_of(block, place[0]) * frames
+            start = value_of(start, place[0])
+            valid = value_of(valid, place[0])
+
+            def fill(ref=ref, frames=frames, first=first, start=start):
                 for f in range(frames):
                     ext[member, start + f] = ref[signal, first + f].astype(F32)
 
-            @pl.when(valid == 0)
-            def _():
+            def clear(frames=frames, start=start):
                 for f in range(frames):
                     ext[member, start + f] = jnp.zeros((ROWS, LANES), F32)
+
+            if isinstance(valid, int):
+                fill() if valid else clear()
+            else:
+                pl.when(valid == 1)(fill)
+                pl.when(valid == 0)(clear)
 
     def filter_rows(member, q):
         rows = pl.ds(pl.multiple_of(q * SUB, SUB), SUB)
@@ -212,8 +228,7 @@
             lax.fori_loop(0, out.shape[0], write_row, 0, unroll=2)
             at += out.shape[0]
 
-    @pl.when(place[0] == 1)
-    def _():
+    def body():
         for member in range(members):
             load(member)
 
@@ -228,24 +243,25 @@
             for pair in range(pairs):
                 second_stage(member, pair)
 
-        @pl.when(step == steps - 1)
-        def _():
-            write()
+        pl.when(step == steps - 1)(write)
+
+    if isinstance(run, int):
+        body()
+    else:
+        pl.when(value_of(run, place[0]) == 1)(body)
 
 
 def after(value, *others):
     return lax.optimization_barrier((value, *others))[0]
 
 
-def spectra(parts, out_frames, fixed, groups, sizes, run=1, wait=(), cost=10**6):
+def spectra(parts, out_frames, fixed, place, groups, sizes, run=1, wait=(), cost=10**6):
     signals = parts[0][0].shape[0]
-    numbers = [run] + [v for part in parts for v in part[2:]]
-    place = jnp.stack([jnp.asarray(v, jnp.int32) for v in numbers])
     place = after(place, *wait)
     tiles = H * out_frames // LANES
     shapes = [(n, tiles, TILE, LANES) for n in sizes]
     return pl.pallas_call(
-        functools.partial(spectra_kernel, groups, tuple(p[1] for p in parts), out_frames),
+        functools.partial(spectra_kernel, groups, tuple(part[1:] for part in parts), out_frames, run),
         grid_spec=pltpu.PrefetchScalarGridSpec(
             num_scalar_prefetch=1,
             grid=(signals // MEMBERS,),
@@ -261,7 +277,7 @@
         out_shape=[jax.ShapeDtypeStruct(shape, BF16) for shape in shapes],
         compiler_params=pltpu.CompilerParams(vmem_limit_bytes=32 << 20),
         cost_estimate=pl.CostEstimate(flops=cost, bytes_accessed=0, transcendentals=0),
-    )(place, *[part[0] for part in parts], *fixed, jnp.asarray(turn_table(), F32))
+    )(place, *[part[0] for part in parts], *fixed)
 
 
 def after(value, *others):
@@ -336,7 +352,7 @@
         for tile in range(2):
             for visit in range(VISITS):
                 for part in range(2):
-                    out[part, signal, place[visit], tile * (half // 4) + block] = value[at : at + SUB]
+                    out[part, signal, value_of(PLACES[visit], place[1]), tile * (half // 4) + block] = value[at : at + SUB]
                     at += SUB
         return carry
 
@@ -394,41 +410,41 @@
 def general(volts, fir_taps):
     groups = lax.axis_size("tm")
     frames = volts.shape[1]
-    volts, edge_frames, *fixed = prepare(volts, fir_taps, groups, 0, frames // TAPS - 1, TAPS)
+    volts, edge_frames, *fixed = prepare(volts, fir_taps, place, groups, frames // TAPS - 1, TAPS)
     history = lax.ppermute(edge_frames, "tm", [(i, i + 1) for i in range(groups - 1)])
     parts = [(history, TAPS, 0, 0, 1)] + [(volts, TAPS, i, TAPS * (i + 1), 1) for i in range(frames // TAPS)]
-    spectrum = spectra(parts, frames, fixed, groups, [K2])[0]
+    spectrum = spectra(parts, frames, fixed, place, groups, [K2])[0]
     spectrum = lax.all_to_all(spectrum, "tm", split_axis=0, concat_axis=0, tiled=True)
     tiles = spectrum.shape[1]
     return [([spectrum], [(tiles, [(0, K2 // groups * t, 0) for t in range(groups)])])]
 
 
-def paired(volts, fir_taps, correlated):
+def paired(volts, fir_taps, place, correlated):
     frames = volts.shape[1]
     me = lax.axis_index("tm")
     sizes = [K2 // 2, K2 // 2]
     swap = [(0, 1), (1, 0)]
     edge = TAPS // 2
     last = frames // edge
-    volts, edge_frames, *fixed = prepare(volts, fir_taps, 2, me, jnp.where(me == 0, frames // edge - 1, 0), edge)
+    volts, edge_frames, *fixed = prepare(volts, fir_taps, place, 2, (last - 1, 0), edge)
     visiting = lax.ppermute(edge_frames, "tm", swap)
     own_a, away_a = spectra(
-        [(volts, TAPS, 0, 0, me), (volts, TAPS, me, TAPS, 1)], TAPS, fixed, 2, sizes
+        [(volts, TAPS, 0, 0, (0, 1)), (volts, TAPS, (0, 1), TAPS, 1)], TAPS, fixed, place, 2, sizes
     )
     got_a = lax.ppermute(away_a, "tm", swap)
     two_a, rest_a = farther(own_a)
     own_b, away_b = spectra(
-        [(volts, TAPS, 0, 0, 1), (volts, TAPS, 1, TAPS, 1)], TAPS, fixed, 2, sizes, 1 - me, (own_a,)
+        [(volts, TAPS, 0, 0, 1), (volts, TAPS, 1, TAPS, 1)], TAPS, fixed, place, 2, sizes, (1, 0), (own_a,)
     )
     got_b = lax.ppermute(away_b, "tm", [(0, 1)])
     pair_a = exchanged(two_a)
     own_c, away_c = spectra(
         [
-            (volts, edge, jnp.where(me == 0, last - 2, 0), edge * me, 1),
-            (volts, edge, jnp.where(me == 0, last - 1, 1), edge * me + edge, 1),
-            (visiting, edge, 0, 2 * edge * (1 - me), 1),
+            (volts, edge, (last - 2, 0), (0, edge), 1),
+            (volts, edge, (last - 1, 1), (edge, 2 * edge), 1),
+            (visiting, edge, 0, (2 * edge, 0), 1),
         ],
-        edge, fixed, 2, sizes, 1, (own_b, two_a, got_a), 9 * 10**9,
+        edge, fixed, place, 2, sizes, 1, (own_b, two_a, got_a), 9 * 10**9,
     )
     got_c = lax.ppermute(away_c, "tm", swap)
     two_g, rest_g = farther(got_a)
@@ -446,13 +462,13 @@
     )
 
 
-def general(volts, fir_taps, correlated):
+def general(volts, fir_taps, place, correlated):
     groups = lax.axis_size("tm")
     frames = volts.shape[1]
-    volts, edge_frames, *fixed = prepare(volts, fir_taps, groups, 0, frames // TAPS - 1, TAPS)
+    volts, edge_frames, *fixed = prepare(volts, fir_taps, place, groups, frames // TAPS - 1, TAPS)
     history = lax.ppermute(edge_frames, "tm", [(i, i + 1) for i in range(groups - 1)])
     parts = [(history, TAPS, 0, 0, 1)] + [(volts, TAPS, i, TAPS * (i + 1), 1) for i in range(frames // TAPS)]
-    spectrum = spectra(parts, frames, fixed, groups, [K2])[0]
+    spectrum = spectra(parts, frames, fixed, place, groups, [K2])[0]
     spectrum = lax.all_to_all(spectrum, "tm", split_axis=0, concat_axis=0, tiled=True)
     two, rest = farther(spectrum)
     spots = [(0, K2 // groups * t, 0) for t in range(groups)]
@@ -461,8 +477,7 @@
 
 def local(voltage, fir_taps):
     groups = lax.axis_size("tm")
-    even = lax.axis_index("stn") % 2 == 0
-    place = jnp.where(even, jnp.array([0, 1, 2, 3]), jnp.array([0, 3, 2, 1])).astype(jnp.int32)
+    place = jnp.stack([lax.axis_index("tm"), lax.axis_index("stn") % 2]).astype(jnp.int32)
     scale = 1.0 / (groups * voltage.shape[1])
 
     def correlated(arrays, pieces, before, last, wait=()):
@@ -473,7 +488,7 @@
         return correlate(arrays, laid, K2 // groups, place, scale, before, last, wait)
 
     run = paired if groups == 2 else general
-    return natural(run(stacked(voltage), fir_taps, correlated))
+    return natural(run(stacked(voltage), fir_taps, place, correlated))
 
 
 def solution(mesh):

time: 112 us -> 111 us (level)
  local copies, waits for them, and re-layouts: 9.82 us -> 2.19 us
  waiting for transfers between devices: 49.4 us -> 56.8 us
    unnamed x16 -> x4, local copies, waits for them, and re-layouts: 9.56 us -> 2.19 us
    ppermute x3, waiting for transfers between devices: 23.7 us -> 27.7 us  [shifted(): lax.ppermute(block, axis, [(i, (i + distance) % size) for i in range(size)])]
    ppermute x1, waiting for transfers between devices: 6.84 us -> 10.4 us  [paired(): got_a = lax.ppermute(away_a, 'tm', swap)]
  transfers between devices with their start and end apart: 13 -> 13, of which waited for: 6 -> 6; matrix products, arithmetic and copies ran while one was open for 1% -> 1% of each run, Pallas kernels for 25% -> 24%
where the time goes in v7:
time: 111 us
  waiting for transfers between devices  56.8 us (51%)
  Pallas kernels  41.9 us (38%)
  starting transfers between devices  8.56 us (8%)
  local copies, waits for them, and re-layouts  2.19 us (2%)
  other arithmetic  1.3 us (1%)
    ppermute x3, waiting for transfers between devices, shifted(): lax.ppermute(block, axis, [(i, (i + distance) % size) for i in range(size)])  27.7 us
    pallas_call x3, Pallas kernels, spectra(): pl.pallas_call(functools.partial(spectra_kernel, groups, tuple((part[1:]...  20.3 us
    pallas_call x2, Pallas kernels, correlate(): pl.pallas_call(functools.partial(correlate_kernel, pieces, per_group, sca...  18.3 us
    ppermute x3, waiting for transfers between devices, farther(): lax.ppermute(block, 'stn', [(i, (i + 1 if i % 2 == 0 else i + 3) % size)...  12.9 us
    ppermute x1, waiting for transfers between devices, paired(): got_a = lax.ppermute(away_a, 'tm', swap)  10.4 us
    ppermute x1, waiting for transfers between devices, paired(): got_c = lax.ppermute(away_c, 'tm', swap)  5.75 us
    ppermute x3, starting transfers between devices, shifted(): lax.ppermute(block, axis, [(i, (i + distance) % size) for i in range(size)])  4.63 us
    pallas_call x1, Pallas kernels, prepare(): pl.pallas_call(functools.partial(prepare_kernel, edge_block, int(groups =...  3.29 us
  transfers between devices with their start and end apart: 13, of which 6 were waited for; matrix products, arithmetic and copies ran while one was open for 1% of the time, Pallas kernels for 24%

profile of v7, /device:TPU:6, one launch (start us, length us, event | category | flops | bytes accessed | tf_op | source)
XLA Modules:
  0.0 110.8 jit_solution(5519618281182458031)
XLA Ops:
  0.0 0.1 pad_add_fusion.place
  0.1 3.3 %shard_map.46 = (bf16[8,32,64,128]{3,2,1,0:T(8,128)(2,1)S(1)}, bf16[8,8,64,128]{3,2,1,0:T(8,128)(2,1)S(1)}, f32[1024,128]{1,0:T(8,128)S(1)}, bf16[64,192]{1,0:T(...) custom-call(s32[2]{0:T(128)S(1)} %pad_add_fusion.place, bf16[8,32,64,128]{3,2,1,0:T(8,128)(2,1)} %bitcast.10, ...), custom_call_target="tpu_custom_call" | custom-call | tf_op jit(solution)/shard_map/pallas_call | solution.py:110
  3.4 0.0 copy-start
  3.4 0.6 collective-permute-start.3
  4.0 12.3 %shard_map.47 = (bf16[32,4,16,128]{3,2,1,0:T(8,128)(2,1)}, bf16[32,4,16,128]{3,2,1,0:T(8,128)(2,1)}) custom-call(s32[2]{0:T(128)S(1)} %pad_add_fusion.place, bf16[8,32,64,128]{3,2,1,0:T(8,128)(2,1)S(1)} %get-tuple-element.21.refs_0_.refs_1_, bf16[8,32,64,128]{3,2,1,0:T(8,128)(2,1)S(1)} %get-tuple-element.21.refs_0_.refs_1_, ...), custom_call_target="tpu_custom_call" | custom-call | flops 1000000 | tf_op jit(solution)/shard_map/pallas_call | solution.py:263
  16.2 1.6 %collective-permute-start.1 = (bf16[32,4,16,128]{3,2,1,0:T(8,128)(2,1)}, bf16[32,4,16,128]{3,2,1,0:T(8,128)(2,1)}, u32[]{:S(2)}, u32[]{:S(2)}) collective-permute-start(bf16[32,4,16,128]{3,2,1,0:T(8,128)(2,1)} %get-tuple-element.26.refs_0_), channel_id=1, source_target_pairs={{0,4},{2,6},{4,8},{6,10},{8,12},{10,14},{12,16},{14,18},{16,20},{1... | collective-permute-start | bytes 1572872 | tf_op jit(solution)/shard_map/ppermute | solution.py:397
  17.8 1.5 %collective-permute-start.2 = (bf16[32,4,16,128]{3,2,1,0:T(8,128)(2,1)}, bf16[32,4,16,128]{3,2,1,0:T(8,128)(2,1)}, u32[]{:S(2)}, u32[]{:S(2)}) collective-permute-start(bf16[32,4,16,128]{3,2,1,0:T(8,128)(2,1)} %get-tuple-element.30), channel_id=1, source_target_pairs={{0,1},{1,0},{2,3},{3,2},{4,5},{5,4},{6,7},{7,6},{8,9},{9,8},{10,11... | collective-permute-start | bytes 1572872 | tf_op jit(solution)/shard_map/ppermute | solution.py:434
  19.3 0.0 collective-permute-start.6
  19.3 0.0 copy-done
  19.3 1.4 %shard_map.48 = (bf16[32,4,16,128]{3,2,1,0:T(8,128)(2,1)S(1)}, bf16[32,4,16,128]{3,2,1,0:T(8,128)(2,1)}) custom-call(s32[2]{0:T(128)S(1)} %pad_add_fusion.place, bf16[8,32,64,128]{3,2,1,0:T(8,128)(2,1)S(1)} %get-tuple-element.21.refs_0_.refs_1_, bf16[8,32,64,128]{3,2,1,0:T(8,128)(2,1)S(1)} %get-tuple-element.21.refs_0_.refs_1_, ...), custom_call_target="tpu_custom_call" | custom-call | flops 1000000 | tf_op jit(solution)/shard_map/pallas_call | solution.py:263
  20.6 1.3 %collective-permute-start = (bf16[32,4,16,128]{3,2,1,0:T(8,128)(2,1)}, bf16[32,4,16,128]{3,2,1,0:T(8,128)(2,1)}, u32[]{:S(2)}, u32[]{:S(2)}) collective-permute-start(bf16[32,4,16,128]{3,2,1,0:T(8,128)(2,1)} %get-tuple-element.29), channel_id=1, source_target_pairs={{0,1},{2,3},{4,5},{6,7},{8,9},{10,11},{12,13},{14,15},{16,17},{18,... | collective-permute-start | bytes 1572872 | tf_op jit(solution)/shard_map/ppermute | solution.py:439
  21.9 8.5 %collective-permute-done.1.refs_2_ = bf16[32,4,16,128]{3,2,1,0:T(8,128)(2,1)} collective-permute-done((bf16[32,4,16,128]{3,2,1,0:T(8,128)(2,1)}, bf16[32,4,16,128]{3,2,1,0:T(8,128)(2,1)}, u32[]{:S(2)}, u32[]{:S(2)}) %collective-permute-start.1) | collective-permute-done | bytes 524320 | tf_op jit(solution)/shard_map/ppermute | solution.py:397
  30.5 10.4 %collective-permute-done.2.refs_4_ = bf16[32,4,16,128]{3,2,1,0:T(8,128)(2,1)} collective-permute-done((bf16[32,4,16,128]{3,2,1,0:T(8,128)(2,1)}, bf16[32,4,16,128]{3,2,1,0:T(8,128)(2,1)}, u32[]{:S(2)}, u32[]{:S(2)}) %collective-permute-start.2) | collective-permute-done | bytes 524320 | tf_op jit(solution)/shard_map/ppermute | solution.py:434
  40.8 1.5 %collective-permute-start.4 = (bf16[32,4,16,128]{3,2,1,0:T(8,128)(2,1)}, bf16[32,4,16,128]{3,2,1,0:T(8,128)(2,1)S(1)}, u32[]{:S(2)}, u32[]{:S(2)}) collective-permute-start(bf16[32,4,16,128]{3,2,1,0:T(8,128)(2,1)} %collective-permute-done.2.refs_4_), channel_id=1, source_target_pairs={{0,4},{2,6},{4,8},{6,10},{8,12},{10,14},{12,16},{14,18},{16,20},{1... | collective-permute-start | bytes 1572872 | tf_op jit(solution)/shard_map/ppermute | solution.py:397
  42.4 0.0 collective-permute-start.5
  42.4 0.0 collective-permute-done.3.refs_2_
  42.4 0.5 collective-permute-start.10
  42.9 0.0 copy-start.1
  42.9 2.2 %copy-done.1 = bf16[8,32,64,128]{3,2,1,0:T(8,128)(2,1)S(1)} copy-done((bf16[8,32,64,128]{3,2,1,0:T(8,128)(2,1)S(1)}, bf16[8,32,64,128]{3,2,1,0:T(8,128)(2,1)}, u32[]{:S(2)}) %copy-start.1) | copy-done | bytes 4194328
  45.1 6.7 %shard_map.49 = (bf16[32,2,16,128]{3,2,1,0:T(8,128)(2,1)S(1)}, bf16[32,2,16,128]{3,2,1,0:T(8,128)(2,1)S(1)}) custom-call(s32[2]{0:T(128)S(1)} %pad_add_fusion.place, bf16[8,32,64,128]{3,2,1,0:T(8,128)(2,1)S(1)} %copy-done.1, bf16[8,32,64,128]{3,2,1,0:T(8,128)(2,1)S(1)} %copy-done.1, bf16[8,8,64,128]{3,2,1,0:T(8,128)(2,1)S(1)} %collective-permute-done.3.refs_2_, ...), custom_call_target="tpu_custom_call" | custom-call | flops 8999999488 | tf_op jit(solution)/shard_map/pallas_call | solution.py:263
  51.8 0.0 collective-permute-done
  51.8 0.1 collective-permute-start.7
  51.9 1.1 broadcast_select_fusion
  53.0 0.0 collective-permute-done.6.refs_3_
  53.0 2.1 %collective-permute-done.4.refs_6_ = bf16[32,4,16,128]{3,2,1,0:T(8,128)(2,1)S(1)} collective-permute-done((bf16[32,4,16,128]{3,2,1,0:T(8,128)(2,1)}, bf16[32,4,16,128]{3,2,1,0:T(8,128)(2,1)S(1)}, u32[]{:S(2)}, u32[]{:S(2)}) %collective-permute-start.4) | collective-permute-done | bytes 524320 | tf_op jit(solution)/shard_map/ppermute | solution.py:397
  55.1 0.0 collective-permute-done.5.refs_1_
  55.1 0.0 collective-permute-start.9
  55.1 5.8 %collective-permute-done.7 = bf16[32,2,16,128]{3,2,1,0:T(8,128)(2,1)S(1)} collective-permute-done((bf16[32,2,16,128]{3,2,1,0:T(8,128)(2,1)S(1)}, bf16[32,2,16,128]{3,2,1,0:T(8,128)(2,1)S(1)}, u32[]{:S(2)}, u32[]{:S(2)}) %collective-permute-start.7) | collective-permute-done | bytes 262176 | tf_op jit(solution)/shard_map/ppermute | solution.py:449
  60.8 0.1 pad_maximum_fusion.refs_0_
  61.0 1.5 %collective-permute-start.8 = (bf16[32,8,16,128]{3,2,1,0:T(8,128)(2,1)S(1)}, bf16[32,8,16,128]{3,2,1,0:T(8,128)(2,1)S(1)}, u32[]{:S(2)}, u32[]{:S(2)}) collective-permute-start(bf16[32,8,16,128]{3,2,1,0:T(8,128)(2,1)S(1)} %pad_maximum_fusion.refs_0_), channel_id=1, source_target_pairs={{0,4},{2,6},{4,8},{6,10},{8,12},{10,14},{12,16},{14,18},{16,20},{1... | collective-permute-start | bytes 3145736 | tf_op jit(solution)/shard_map/ppermute | solution.py:397
  62.5 0.0 collective-permute-start.12
  62.5 0.0 collective-permute-done.10.refs_7_
  62.5 0.0 collective-permute-done.9.refs_5_
  62.5 6.6 %shard_map.50.refs_4_ = f32[4096,128]{1,0:T(8,128)} custom-call(s32[2]{0:T(128)S(1)} %pad_add_fusion.place, bf16[32,4,16,128]{3,2,1,0:T(8,128)(2,1)} %get-tuple-element.26.refs_0_, bf16[32,4,16,128]{3,2,1,0:T(8,128)(2,1)S(1)} %collective-permute-done.5.refs_1_, bf16[32,4,16,128]{3,2,1,0:T(8,128)(2,1)} %collective-permute-done.1.refs_2_, ...), custom_call_target="tpu_custom_call" | custom-call | flops 6000000000 | tf_op jit(solution)/shard_map/pallas_call | solution.py:369
  69.1 17.1 %collective-permute-done.8.refs_2_ = bf16[32,8,16,128]{3,2,1,0:T(8,128)(2,1)S(1)} collective-permute-done((bf16[32,8,16,128]{3,2,1,0:T(8,128)(2,1)S(1)}, bf16[32,8,16,128]{3,2,1,0:T(8,128)(2,1)S(1)}, u32[]{:S(2)}, u32[]{:S(2)}) %collective-permute-start.8) | collective-permute-done | bytes 1048608 | tf_op jit(solution)/shard_map/ppermute | solution.py:397
  86.2 0.0 collective-permute-start.11
  86.2 12.9 %collective-permute-done.12.refs_3_ = bf16[32,8,16,128]{3,2,1,0:T(8,128)(2,1)S(1)} collective-permute-done((bf16[32,8,16,128]{3,2,1,0:T(8,128)(2,1)S(1)}, bf16[32,8,16,128]{3,2,1,0:T(8,128)(2,1)S(1)}, u32[]{:S(2)}, u32[]{:S(2)}) %collective-permute-start.12) | collective-permute-done | bytes 1048608 | tf_op jit(solution)/shard_map/ppermute | solution.py:402
  99.1 0.0 collective-permute-done.11.refs_1_
  99.1 11.7 %shard_map.51 = f32[2,8,4,8,8,128]{5,4,3,2,1,0:T(8,128)} custom-call(s32[2]{0:T(128)S(1)} %pad_add_fusion.place, bf16[32,8,16,128]{3,2,1,0:T(8,128)(2,1)S(1)} %pad_maximum_fusion.refs_0_, bf16[32,8,16,128]{3,2,1,0:T(8,128)(2,1)S(1)} %collective-permute-done.11.refs_1_, bf16[32,8,16,128]{3,2,1,0:T(8,128)(2,1)S(1)} %collective-permute-done.8.refs_2_, ...), custom_call_target="tpu_custom_call" | custom-call | flops 6000000000 | tf_op jit(solution)/shard_map/pallas_call | solution.py:369
Async XLA Ops:
  3.4 15.9 %copy-start = (bf16[8,32,64,128]{3,2,1,0:T(8,128)(2,1)}, bf16[8,32,64,128]{3,2,1,0:T(8,128)(2,1)S(1)}, u32[]{:S(2)}) copy-start(bf16[8,32,64,128]{3,2,1,0:T(8,128)(2,1)S(1)} %get-tuple-element.21.refs_0_.refs_1_) | copy-start | bytes 12582916
  3.4 39.0 %collective-permute-start.3 = (bf16[8,8,64,128]{3,2,1,0:T(8,128)(2,1)S(1)}, bf16[8,8,64,128]{3,2,1,0:T(8,128)(2,1)S(1)}, u32[]{:S(2)}, u32[]{:S(2)}) collective-permute-start(bf16[8,8,64,128]{3,2,1,0:T(8,128)(2,1)S(1)} %get-tuple-element.32), channel_id=1, source_target_pairs={{0,1},{1,0},{2,3},{3,2},{4,5},{5,4},{6,7},{7,6},{8,9},{9,8},{10,11... | collective-permute-start | bytes 3145736 | tf_op jit(solution)/shard_map/ppermute | solution.py:430
  16.2 14.2 %collective-permute-start.1 = (bf16[32,4,16,128]{3,2,1,0:T(8,128)(2,1)}, bf16[32,4,16,128]{3,2,1,0:T(8,128)(2,1)}, u32[]{:S(2)}, u32[]{:S(2)}) collective-permute-start(bf16[32,4,16,128]{3,2,1,0:T(8,128)(2,1)} %get-tuple-element.26.refs_0_), channel_id=1, source_target_pairs={{0,4},{2,6},{4,8},{6,10},{8,12},{10,14},{12,16},{14,18},{16,20},{1... | collective-permute-start | bytes 1572872 | tf_op jit(solution)/shard_map/ppermute | solution.py:397
  17.8 23.1 %collective-permute-start.2 = (bf16[32,4,16,128]{3,2,1,0:T(8,128)(2,1)}, bf16[32,4,16,128]{3,2,1,0:T(8,128)(2,1)}, u32[]{:S(2)}, u32[]{:S(2)}) collective-permute-start(bf16[32,4,16,128]{3,2,1,0:T(8,128)(2,1)} %get-tuple-element.30), channel_id=1, source_target_pairs={{0,1},{1,0},{2,3},{3,2},{4,5},{5,4},{6,7},{7,6},{8,9},{9,8},{10,11... | collective-permute-start | bytes 1572872 | tf_op jit(solution)/shard_map/ppermute | solution.py:434
  19.3 33.7 %collective-permute-start.6 = (bf16[32,4,16,128]{3,2,1,0:T(8,128)(2,1)}, bf16[32,4,16,128]{3,2,1,0:T(8,128)(2,1)}, u32[]{:S(2)}, u32[]{:S(2)}) collective-permute-start(bf16[32,4,16,128]{3,2,1,0:T(8,128)(2,1)} %get-tuple-element.26.refs_0_), channel_id=1, source_target_pairs={{0,2},{2,8},{4,6},{6,12},{8,10},{10,16},{12,14},{14,20},{16,18},{1... | collective-permute-start | bytes 1572872 | tf_op jit(solution)/shard_map/ppermute | solution.py:402
  20.6 31.2 %collective-permute-start = (bf16[32,4,16,128]{3,2,1,0:T(8,128)(2,1)}, bf16[32,4,16,128]{3,2,1,0:T(8,128)(2,1)}, u32[]{:S(2)}, u32[]{:S(2)}) collective-permute-start(bf16[32,4,16,128]{3,2,1,0:T(8,128)(2,1)} %get-tuple-element.29), channel_id=1, source_target_pairs={{0,1},{2,3},{4,5},{6,7},{8,9},{10,11},{12,13},{14,15},{16,17},{18,... | collective-permute-start | bytes 1572872 | tf_op jit(solution)/shard_map/ppermute | solution.py:439
  40.8 14.2 %collective-permute-start.4 = (bf16[32,4,16,128]{3,2,1,0:T(8,128)(2,1)}, bf16[32,4,16,128]{3,2,1,0:T(8,128)(2,1)S(1)}, u32[]{:S(2)}, u32[]{:S(2)}) collective-permute-start(bf16[32,4,16,128]{3,2,1,0:T(8,128)(2,1)} %collective-permute-done.2.refs_4_), channel_id=1, source_target_pairs={{0,4},{2,6},{4,8},{6,10},{8,12},{10,14},{12,16},{14,18},{16,20},{1... | collective-permute-start | bytes 1572872 | tf_op jit(solution)/shard_map/ppermute | solution.py:397
  42.4 12.7 %collective-permute-start.5 = (bf16[32,4,16,128]{3,2,1,0:T(8,128)(2,1)}, bf16[32,4,16,128]{3,2,1,0:T(8,128)(2,1)S(1)}, u32[]{:S(2)}, u32[]{:S(2)}) collective-permute-start(bf16[32,4,16,128]{3,2,1,0:T(8,128)(2,1)} %collective-permute-done.1.refs_2_), channel_id=1, source_target_pairs={{0,2},{2,0},{4,6},{6,4},{8,10},{10,8},{12,14},{14,12},{16,18},{18,... | collective-permute-start | bytes 1572872 | tf_op jit(solution)/shard_map/ppermute | solution.py:407
  42.4 20.1 %collective-permute-start.10 = (bf16[32,4,16,128]{3,2,1,0:T(8,128)(2,1)}, bf16[32,4,16,128]{3,2,1,0:T(8,128)(2,1)S(1)}, u32[]{:S(2)}, u32[]{:S(2)}) collective-permute-start(bf16[32,4,16,128]{3,2,1,0:T(8,128)(2,1)} %collective-permute-done.2.refs_4_), channel_id=1, source_target_pairs={{0,2},{2,8},{4,6},{6,12},{8,10},{10,16},{12,14},{14,20},{16,18},{1... | collective-permute-start | bytes 1572872 | tf_op jit(solution)/shard_map/ppermute | solution.py:402
  42.9 2.2 %copy-start.1 = (bf16[8,32,64,128]{3,2,1,0:T(8,128)(2,1)S(1)}, bf16[8,32,64,128]{3,2,1,0:T(8,128)(2,1)}, u32[]{:S(2)}) copy-start(bf16[8,32,64,128]{3,2,1,0:T(8,128)(2,1)} %copy-done) | copy-start | bytes 12582916
  51.8 9.0 %collective-permute-start.7 = (bf16[32,2,16,128]{3,2,1,0:T(8,128)(2,1)S(1)}, bf16[32,2,16,128]{3,2,1,0:T(8,128)(2,1)S(1)}, u32[]{:S(2)}, u32[]{:S(2)}) collective-permute-start(bf16[32,2,16,128]{3,2,1,0:T(8,128)(2,1)S(1)} %get-tuple-element.35), channel_id=1, source_target_pairs={{0,1},{1,0},{2,3},{3,2},{4,5},{5,4},{6,7},{7,6},{8,9},{9,8},{10,11... | collective-permute-start | bytes 786440 | tf_op jit(solution)/shard_map/ppermute | solution.py:449
  55.1 7.4 %collective-permute-start.9 = (bf16[32,4,16,128]{3,2,1,0:T(8,128)(2,1)S(1)}, bf16[32,4,16,128]{3,2,1,0:T(8,128)(2,1)S(1)}, u32[]{:S(2)}, u32[]{:S(2)}) collective-permute-start(bf16[32,4,16,128]{3,2,1,0:T(8,128)(2,1)S(1)} %collective-permute-done.4.refs_6_), channel_id=1, source_target_pairs={{0,2},{2,0},{4,6},{6,4},{8,10},{10,8},{12,14},{14,12},{16,18},{18,... | collective-permute-start | bytes 1572872 | tf_op jit(solution)/shard_map/ppermute | solution.py:407
  61.0 25.2 %collective-permute-start.8 = (bf16[32,8,16,128]{3,2,1,0:T(8,128)(2,1)S(1)}, bf16[32,8,16,128]{3,2,1,0:T(8,128)(2,1)S(1)}, u32[]{:S(2)}, u32[]{:S(2)}) collective-permute-start(bf16[32,8,16,128]{3,2,1,0:T(8,128)(2,1)S(1)} %pad_maximum_fusion.refs_0_), channel_id=1, source_target_pairs={{0,4},{2,6},{4,8},{6,10},{8,12},{10,14},{12,16},{14,18},{16,20},{1... | collective-permute-start | bytes 3145736 | tf_op jit(solution)/shard_map/ppermute | solution.py:397
  62.5 36.6 %collective-permute-start.12 = (bf16[32,8,16,128]{3,2,1,0:T(8,128)(2,1)S(1)}, bf16[32,8,16,128]{3,2,1,0:T(8,128)(2,1)S(1)}, u32[]{:S(2)}, u32[]{:S(2)}) collective-permute-start(bf16[32,8,16,128]{3,2,1,0:T(8,128)(2,1)S(1)} %pad_maximum_fusion.refs_0_), channel_id=1, source_target_pairs={{0,2},{2,8},{4,6},{6,12},{8,10},{10,16},{12,14},{14,20},{16,18},{1... | collective-permute-start | bytes 3145736 | tf_op jit(solution)/shard_map/ppermute | solution.py:402
  86.2 13.0 %collective-permute-start.11 = (bf16[32,8,16,128]{3,2,1,0:T(8,128)(2,1)S(1)}, bf16[32,8,16,128]{3,2,1,0:T(8,128)(2,1)S(1)}, u32[]{:S(2)}, u32[]{:S(2)}) collective-permute-start(bf16[32,8,16,128]{3,2,1,0:T(8,128)(2,1)S(1)} %collective-permute-done.8.refs_2_), channel_id=1, source_target_pairs={{0,2},{2,0},{4,6},{6,4},{8,10},{10,8},{12,14},{14,12},{16,18},{18,... | collective-permute-start | bytes 3145736 | tf_op jit(solution)/shard_map/ppermute | solution.py:407

commit v8 on v7

--- a/solution.py
+++ b/solution.py
@@ -296,6 +296,12 @@
     first_tile = lane < LANES // 2
     real_lane = lane % TILE < SUB
     sign = jnp.where(real_lane, 1.0, -1.0).astype(F32)
+
+    def fetch(spot, tile, k2, k1):
+        arrays, row, column = spot
+        values = [refs[array][row + tile * half + k2, column + k1] for array in arrays]
+        return values[0] if len(values) == 1 else values[0] + values[1]
+
     for number, piece in enumerate(pieces):
         tiles, piece = piece
         share = H // tiles
@@ -308,15 +314,13 @@
             for position in range(len(piece[0])):
                 rows = []
                 for tile in range(2):
-                    array, row, column = piece[0][position]
-                    a = refs[array][row + tile * half + k2, column + k1]
+                    a = fetch(piece[0][position], tile, k2, k1)
                     rows += [jnp.where(where == c, a, jnp.zeros_like(a)) for c in range(share)]
                 own.append(jnp.concatenate(rows, axis=0))
                 rows = []
                 for tile in range(2):
                     for visit in range(VISITS):
-                        array, row, column = piece[visit][position]
-                        rows.append(refs[array][row + tile * half + k2, column + k1])
+                        rows.append(fetch(piece[visit][position], tile, k2, k1))
                 other.append(jnp.concatenate(rows, axis=0))
             product = dot_nt(jnp.concatenate(own, axis=1), jnp.concatenate(other, axis=1))
             for c in range(share):
@@ -392,31 +396,30 @@
     return out.transpose(0, 1, 2, 4, 3, 5).reshape(parts, s, visits * t, i * lanes)
 
 
-def shifted(block, axis, distance):
-    size = lax.axis_size(axis)
-    return lax.ppermute(block, axis, [(i, (i + distance) % size) for i in range(size)])
-
-
-def farther(block):
+VISIT_ARRAYS = ((0,), (4, 5), (1, 3), (2,))
+
+
+def sent(block, way):
     size = lax.axis_size("stn")
-    rest = lax.ppermute(block, "stn", [(i, (i + 1 if i % 2 == 0 else i + 3) % size) for i in range(size)])
-    return shifted(block, "stn", 2), rest
-
-
-def exchanged(block):
-    return lax.ppermute(block, "stn", [(i, i ^ 1) for i in range(lax.axis_size("stn"))])
-
-
-def general(volts, fir_taps):
-    groups = lax.axis_size("tm")
-    frames = volts.shape[1]
-    volts, edge_frames, *fixed = prepare(volts, fir_taps, place, groups, frames // TAPS - 1, TAPS)
-    history = lax.ppermute(edge_frames, "tm", [(i, i + 1) for i in range(groups - 1)])
-    parts = [(history, TAPS, 0, 0, 1)] + [(volts, TAPS, i, TAPS * (i + 1), 1) for i in range(frames // TAPS)]
-    spectrum = spectra(parts, frames, fixed, place, groups, [K2])[0]
-    spectrum = lax.all_to_all(spectrum, "tm", split_axis=0, concat_axis=0, tiled=True)
-    tiles = spectrum.shape[1]
-    return [([spectrum], [(tiles, [(0, K2 // groups * t, 0) for t in range(groups)])])]
+    pairs = [(i, way(i)) for i in range(size)]
+    return lax.ppermute(block, "stn", [(i, j % size) for i, j in pairs if j is not None])
+
+
+def direct(block):
+    two = sent(block, lambda i: i + 2 if i % 4 < 3 else None)
+    return two, sent(block, lambda i: i + 1 if i % 2 == 0 else i + 3)
+
+
+def relayed(rest):
+    return sent(rest, lambda i: i - 1 if i % 4 == 2 else None)
+
+
+def across(two):
+    return sent(two, lambda i: i ^ 1 if i % 4 != 1 else None)
+
+
+def across_relayed(relay):
+    return sent(relay, lambda i: i - 1 if i % 4 == 1 else None)
 
 
 def paired(volts, fir_taps, place, correlated):
@@ -432,33 +435,44 @@
         [(volts, TAPS, 0, 0, (0, 1)), (volts, TAPS, (0, 1), TAPS, 1)], TAPS, fixed, place, 2, sizes
     )
     got_a = lax.ppermute(away_a, "tm", swap)
-    two_a, rest_a = farther(own_a)
+    two_a, rest_a = direct(own_a)
     own_b, away_b = spectra(
         [(volts, TAPS, 0, 0, 1), (volts, TAPS, 1, TAPS, 1)], TAPS, fixed, place, 2, sizes, (1, 0), (own_a,)
     )
+    got_a = after(got_a, own_b)
     got_b = lax.ppermute(away_b, "tm", [(0, 1)])
-    pair_a = exchanged(two_a)
+    relay_a, pair_a = relayed(rest_a), across(two_a)
     own_c, away_c = spectra(
         [
             (volts, edge, (last - 2, 0), (0, edge), 1),
             (volts, edge, (last - 1, 1), (edge, 2 * edge), 1),
             (visiting, edge, 0, (2 * edge, 0), 1),
         ],
-        edge, fixed, place, 2, sizes, 1, (own_b, two_a, got_a), 9 * 10**9,
+        edge, fixed, place, 2, sizes, 1, (own_b, two_a, rest_a, got_a), 9 * 10**9,
     )
     got_c = lax.ppermute(away_c, "tm", swap)
-    two_g, rest_g = farther(got_a)
-    pair_g = exchanged(two_g)
-    own_c = after(own_c, two_g, pair_a, rest_a)
+    two_g, rest_g = direct(got_a)
+    own_c, got_c, pair_a, relay_a, two_g, rest_g = lax.optimization_barrier(
+        (own_c, got_c, pair_a, relay_a, two_g, rest_g)
+    )
     rest = jnp.concatenate([jnp.where(me == 0, own_b, got_b), own_c, got_c], axis=1)
-    two_r, rest_r = farther(rest)
+    two_r, rest_r = direct(rest)
+    relay_g, pair_g = relayed(rest_g), across(two_g)
+    last_a, last_g = across_relayed(after(relay_a, rest)), across_relayed(after(relay_g, rest))
     many, few = own_a.shape[1], own_c.shape[1]
     sums = correlated(
-        [own_a, pair_a, two_a, rest_a, got_a, pair_g, two_g, rest_g], [(many, [(0, 0, 0), (1, 0, 0)])], None, False
-    )
-    pair_r = exchanged(after(two_r, sums))
+        [own_a, two_a, rest_a, relay_a, pair_a, last_a, got_a, two_g, rest_g, relay_g, pair_g, last_g],
+        [(many, [(0, 0, 0), (1, 0, 0)])],
+        None,
+        False,
+    )
+    relay_r, pair_r = relayed(after(rest_r, sums)), across(after(two_r, sums))
+    last_r = across_relayed(relay_r)
     return correlated(
-        [rest, pair_r, two_r, rest_r], [(many, [(0, 0, 0)]), (few, [(0, 0, many), (0, 0, many + few)])], sums, True
+        [rest, two_r, rest_r, relay_r, pair_r, last_r],
+        [(many, [(0, 0, 0)]), (few, [(0, 0, many), (0, 0, many + few)])],
+        sums,
+        True,
     )
 
 
@@ -470,9 +484,12 @@
     parts = [(history, TAPS, 0, 0, 1)] + [(volts, TAPS, i, TAPS * (i + 1), 1) for i in range(frames // TAPS)]
     spectrum = spectra(parts, frames, fixed, place, groups, [K2])[0]
     spectrum = lax.all_to_all(spectrum, "tm", split_axis=0, concat_axis=0, tiled=True)
-    two, rest = farther(spectrum)
+    two, rest = direct(spectrum)
+    relay = relayed(rest)
     spots = [(0, K2 // groups * t, 0) for t in range(groups)]
-    return correlated([spectrum, exchanged(two), two, rest], [(spectrum.shape[1], spots)], None, True)
+    return correlated(
+        [spectrum, two, rest, relay, across(two), across_relayed(relay)], [(spectrum.shape[1], spots)], None, True
+    )
 
 
 def local(voltage, fir_taps):
@@ -482,7 +499,7 @@
 
     def correlated(arrays, pieces, before, last, wait=()):
         laid = [
-            (tiles, [[(VISITS * n + visit, row, column) for n, row, column in spots] for visit in range(VISITS)])
+            (tiles, [[([6 * n + k for k in visit], row, column) for n, row, column in spots] for visit in VISIT_ARRAYS])
             for tiles, spots in pieces
         ]
         return correlate(arrays, laid, K2 // groups, place, scale, before, last, wait)

time: 111 us -> 131 us (1.18)
  the two profiles are of different devices: /device:TPU:6 before, /device:TPU:1 now
where the time goes in v8:
time: 131 us; the launch traced here: 130 us
  Pallas kernels  51.7 us (39%)
  starting transfers between devices  38.3 us (29%)
  waiting for transfers between devices  32.2 us (25%)
  local copies, waits for them, and re-layouts  6.19 us (5%)
    ppermute x15, starting transfers between devices, sent(): lax.ppermute(block, 'stn', [(i, j % size) for i, j in pairs if j is not N...  31.7 us
    pallas_call x3, Pallas kernels, spectra(): pl.pallas_call(functools.partial(spectra_kernel, groups, tuple((part[1:]...  29.9 us
    ppermute x15, waiting for transfers between devices, sent(): lax.ppermute(block, 'stn', [(i, j % size) for i, j in pairs if j is not N...  29.6 us
    pallas_call x2, Pallas kernels, correlate(): pl.pallas_call(functools.partial(correlate_kernel, pieces, per_group, sca...  18.5 us
    unnamed x14, local copies, waits for them, and re-layouts  6.19 us
    pallas_call x1, Pallas kernels, prepare(): pl.pallas_call(functools.partial(prepare_kernel, edge_block, int(groups =...  3.29 us
  transfers between devices with their start and end apart: 19, of which 6 were waited for; matrix products, arithmetic and copies ran while one was open for 1% of the time, Pallas kernels for 28%

profile of v8, /device:TPU:1, one launch (start us, length us, event | category | flops | bytes accessed | tf_op | source)
XLA Modules:
  0.0 129.8 jit_solution(13027015655468497526)
XLA Ops:
  0.0 0.1 pad_add_fusion.place
  0.1 3.3 %shard_map.46 = (bf16[8,32,64,128]{3,2,1,0:T(8,128)(2,1)S(1)}, bf16[8,8,64,128]{3,2,1,0:T(8,128)(2,1)S(1)}, f32[1024,128]{1,0:T(8,128)S(1)}, bf16[64,192]{1,0:T(...) custom-call(s32[2]{0:T(128)S(1)} %pad_add_fusion.place, bf16[8,32,64,128]{3,2,1,0:T(8,128)(2,1)} %bitcast.10, ...), custom_call_target="tpu_custom_call" | custom-call | tf_op jit(solution)/shard_map/pallas_call | solution.py:110
  3.4 2.1 %collective-permute-start.4 = (bf16[8,8,64,128]{3,2,1,0:T(8,128)(2,1)S(1)}, bf16[8,8,64,128]{3,2,1,0:T(8,128)(2,1)S(1)}, u32[]{:S(2)}, u32[]{:S(2)}) collective-permute-start(bf16[8,8,64,128]{3,2,1,0:T(8,128)(2,1)S(1)} %get-tuple-element.42), channel_id=1, source_target_pairs={{0,1},{1,0},{2,3},{3,2},{4,5},{5,4},{6,7},{7,6},{8,9},{9,8},{10,11... | collective-permute-start | bytes 3145736 | tf_op jit(solution)/shard_map/ppermute | solution.py:433
  5.5 11.3 %shard_map.47 = (bf16[32,4,16,128]{3,2,1,0:T(8,128)(2,1)S(1)}, bf16[32,4,16,128]{3,2,1,0:T(8,128)(2,1)S(1)}) custom-call(s32[2]{0:T(128)S(1)} %pad_add_fusion.place, bf16[8,32,64,128]{3,2,1,0:T(8,128)(2,1)S(1)} %get-tuple-element.30.refs_0_.refs_1_, bf16[8,32,64,128]{3,2,1,0:T(8,128)(2,1)S(1)} %get-tuple-element.30.refs_0_.refs_1_, ...), custom_call_target="tpu_custom_call" | custom-call | flops 1000000 | tf_op jit(solution)/shard_map/pallas_call | solution.py:263
  16.8 0.1 collective-permute-start.3
  16.9 3.3 %collective-permute-start.1 = (bf16[32,4,16,128]{3,2,1,0:T(8,128)(2,1)S(1)}, bf16[32,4,16,128]{3,2,1,0:T(8,128)(2,1)S(1)}, u32[]{:S(2)}, u32[]{:S(2)}) collective-permute-start(bf16[32,4,16,128]{3,2,1,0:T(8,128)(2,1)S(1)} %get-tuple-element.35.refs_0_), channel_id=1, source_target_pairs={{0,4},{2,6},{4,8},{8,12},{10,14},{12,16},{16,20},{18,22},{20,24},{... | collective-permute-start | bytes 1572872 | tf_op jit(solution)/shard_map/ppermute | solution.py:405
  20.2 2.7 %collective-permute-start.2 = (bf16[32,4,16,128]{3,2,1,0:T(8,128)(2,1)S(1)}, bf16[32,4,16,128]{3,2,1,0:T(8,128)(2,1)S(1)}, u32[]{:S(2)}, u32[]{:S(2)}) collective-permute-start(bf16[32,4,16,128]{3,2,1,0:T(8,128)(2,1)S(1)} %get-tuple-element.35.refs_0_), channel_id=1, source_target_pairs={{0,2},{2,8},{4,6},{6,12},{8,10},{10,16},{12,14},{14,20},{16,18},{1... | collective-permute-start | bytes 1572872 | tf_op jit(solution)/shard_map/ppermute | solution.py:405
  23.0 12.0 %shard_map.48 = (bf16[32,4,16,128]{3,2,1,0:T(8,128)(2,1)S(1)}, bf16[32,4,16,128]{3,2,1,0:T(8,128)(2,1)}) custom-call(s32[2]{0:T(128)S(1)} %pad_add_fusion.place, bf16[8,32,64,128]{3,2,1,0:T(8,128)(2,1)S(1)} %get-tuple-element.30.refs_0_.refs_1_, bf16[8,32,64,128]{3,2,1,0:T(8,128)(2,1)S(1)} %get-tuple-element.30.refs_0_.refs_1_, ...), custom_call_target="tpu_custom_call" | custom-call | flops 1000000 | tf_op jit(solution)/shard_map/pallas_call | solution.py:263
  34.9 2.1 %collective-permute-start = (bf16[32,4,16,128]{3,2,1,0:T(8,128)(2,1)}, bf16[32,4,16,128]{3,2,1,0:T(8,128)(2,1)}, u32[]{:S(2)}, u32[]{:S(2)}) collective-permute-start(bf16[32,4,16,128]{3,2,1,0:T(8,128)(2,1)} %get-tuple-element.38), channel_id=1, source_target_pairs={{0,1},{2,3},{4,5},{6,7},{8,9},{10,11},{12,13},{14,15},{16,17},{18,... | collective-permute-start | bytes 1572872 | tf_op jit(solution)/shard_map/ppermute | solution.py:443
  37.0 2.6 %collective-permute-done.3.refs_6_ = bf16[32,4,16,128]{3,2,1,0:T(8,128)(2,1)S(1)} collective-permute-done((bf16[32,4,16,128]{3,2,1,0:T(8,128)(2,1)S(1)}, bf16[32,4,16,128]{3,2,1,0:T(8,128)(2,1)S(1)}, u32[]{:S(2)}, u32[]{:S(2)}) %collective-permute-start.3) | collective-permute-done | bytes 524320 | tf_op jit(solution)/shard_map/ppermute | solution.py:437
  39.6 3.0 %collective-permute-start.8 = (bf16[32,4,16,128]{3,2,1,0:T(8,128)(2,1)S(1)}, bf16[32,4,16,128]{3,2,1,0:T(8,128)(2,1)S(1)}, u32[]{:S(2)}, u32[]{:S(2)}) collective-permute-start(bf16[32,4,16,128]{3,2,1,0:T(8,128)(2,1)S(1)} %collective-permute-done.3.refs_6_), channel_id=1, source_target_pairs={{0,4},{2,6},{4,8},{8,12},{10,14},{12,16},{16,20},{18,22},{20,24},{... | collective-permute-start | bytes 1572872 | tf_op jit(solution)/shard_map/ppermute | solution.py:405
  42.7 0.0 collective-permute-done.1.refs_1_
  42.7 3.2 %collective-permute-start.9 = (bf16[32,4,16,128]{3,2,1,0:T(8,128)(2,1)S(1)}, bf16[32,4,16,128]{3,2,1,0:T(8,128)(2,1)}, u32[]{:S(2)}, u32[]{:S(2)}) collective-permute-start(bf16[32,4,16,128]{3,2,1,0:T(8,128)(2,1)S(1)} %collective-permute-done.3.refs_6_), channel_id=1, source_target_pairs={{0,2},{2,8},{4,6},{6,12},{8,10},{10,16},{12,14},{14,20},{16,18},{1... | collective-permute-start | bytes 1572872 | tf_op jit(solution)/shard_map/ppermute | solution.py:405
  45.9 0.0 collective-permute-done.2.refs_2_
  45.9 1.3 collective-permute-start.6
  47.2 0.0 collective-permute-done.4.refs_2_
  47.2 1.3 collective-permute-start.7
  48.5 6.7 %shard_map.49 = (bf16[32,2,16,128]{3,2,1,0:T(8,128)(2,1)S(1)}, bf16[32,2,16,128]{3,2,1,0:T(8,128)(2,1)S(1)}) custom-call(s32[2]{0:T(128)S(1)} %pad_add_fusion.place, bf16[8,32,64,128]{3,2,1,0:T(8,128)(2,1)S(1)} %get-tuple-element.30.refs_0_.refs_1_, bf16[8,32,64,128]{3,2,1,0:T(8,128)(2,1)S(1)} %get-tuple-element.30.refs_0_.refs_1_, ...), custom_call_target="tpu_custom_call" | custom-call | flops 8999999488 | tf_op jit(solution)/shard_map/pallas_call | solution.py:263
  55.2 0.0 collective-permute-done.8.refs_7_
  55.2 2.3 %collective-permute-start.5 = (bf16[32,2,16,128]{3,2,1,0:T(8,128)(2,1)S(1)}, bf16[32,2,16,128]{3,2,1,0:T(8,128)(2,1)S(1)}, u32[]{:S(2)}, u32[]{:S(2)}) collective-permute-start(bf16[32,2,16,128]{3,2,1,0:T(8,128)(2,1)S(1)} %get-tuple-element.44), channel_id=1, source_target_pairs={{0,1},{1,0},{2,3},{3,2},{4,5},{5,4},{6,7},{7,6},{8,9},{9,8},{10,11... | collective-permute-start | bytes 786440 | tf_op jit(solution)/shard_map/ppermute | solution.py:453
  57.5 0.0 collective-permute-done.9.refs_8_
  57.5 0.0 collective-permute-done.6.refs_4_
  57.5 0.0 copy-start
  57.5 0.8 copy-done
  58.3 2.8 %collective-permute-done.7.refs_3_ = bf16[32,4,16,128]{3,2,1,0:T(8,128)(2,1)S(1)} collective-permute-done((bf16[32,4,16,128]{3,2,1,0:T(8,128)(2,1)S(1)}, bf16[32,4,16,128]{3,2,1,0:T(8,128)(2,1)S(1)}, u32[]{:S(2)}, u32[]{:S(2)}) %collective-permute-start.7) | collective-permute-done | bytes 524320 | tf_op jit(solution)/shard_map/ppermute | solution.py:405
  61.1 0.0 copy-start.2
  61.1 0.8 copy-done.2
  61.9 0.0 collective-permute-done.5
  61.9 0.0 copy-start.4
  61.9 0.7 copy-done.4
  62.6 1.3 collective-permute-start.13
  63.9 0.0 collective-permute-done
  63.9 0.1 broadcast_select_fusion
  64.0 1.1 pad_maximum_fusion.refs_0_
  65.1 6.5 %collective-permute-start.12 = (bf16[32,4,16,128]{3,2,1,0:T(8,128)(2,1)}, bf16[32,4,16,128]{3,2,1,0:T(8,128)(2,1)S(1)}, u32[]{:S(2)}, u32[]{:S(2)}) collective-permute-start(bf16[32,4,16,128]{3,2,1,0:T(8,128)(2,1)} %copy-done.2), channel_id=1, source_target_pairs={{2,0},{10,8},{18,16},{26,24},{3,1},{11,9},{19,17},{27,25}} | collective-permute-start | bytes 1572872 | tf_op jit(solution)/shard_map/ppermute | solution.py:405
  71.6 1.3 collective-permute-start.14
  72.9 2.2 %collective-permute-done.13.refs_9_ = bf16[32,4,16,128]{3,2,1,0:T(8,128)(2,1)} collective-permute-done((bf16[32,4,16,128]{3,2,1,0:T(8,128)(2,1)}, bf16[32,4,16,128]{3,2,1,0:T(8,128)(2,1)}, u32[]{:S(2)}, u32[]{:S(2)}) %collective-permute-start.13) | collective-permute-done | bytes 524320 | tf_op jit(solution)/shard_map/ppermute | solution.py:405
  75.1 1.3 %collective-permute-start.15 = (bf16[32,4,16,128]{3,2,1,0:T(8,128)(2,1)}, bf16[32,4,16,128]{3,2,1,0:T(8,128)(2,1)S(1)}, u32[]{:S(2)}, u32[]{:S(2)}) collective-permute-start(bf16[32,4,16,128]{3,2,1,0:T(8,128)(2,1)} %collective-permute-done.13.refs_9_), channel_id=1, source_target_pairs={{2,0},{10,8},{18,16},{26,24},{3,1},{11,9},{19,17},{27,25}} | collective-permute-start | bytes 1572872 | tf_op jit(solution)/shard_map/ppermute | solution.py:405
  76.4 0.1 collective-permute-start.11
  76.5 2.5 %collective-permute-start.10 = (bf16[32,8,16,128]{3,2,1,0:T(8,128)(2,1)S(1)}, bf16[32,8,16,128]{3,2,1,0:T(8,128)(2,1)S(1)}, u32[]{:S(2)}, u32[]{:S(2)}) collective-permute-start(bf16[32,8,16,128]{3,2,1,0:T(8,128)(2,1)S(1)} %pad_maximum_fusion.refs_0_), channel_id=1, source_target_pairs={{0,4},{2,6},{4,8},{8,12},{10,14},{12,16},{16,20},{18,22},{20,24},{... | collective-permute-start | bytes 3145736 | tf_op jit(solution)/shard_map/ppermute | solution.py:405
  79.0 0.0 collective-permute-done.12.refs_5_
  79.0 0.0 collective-permute-done.14.refs_10_
  79.0 0.0 collective-permute-done.15.refs_11_
  79.0 0.0 copy-start.6
  79.0 0.8 copy-done.6
  79.8 0.0 copy-start.1
  79.8 1.0 copy-done.1
  80.8 0.0 copy-start.3
  80.8 1.0 copy-done.3
  81.9 6.5 %shard_map.50.refs_6_ = f32[4096,128]{1,0:T(8,128)} custom-call(s32[2]{0:T(128)S(1)} %pad_add_fusion.place, bf16[32,4,16,128]{3,2,1,0:T(8,128)(2,1)S(1)} %get-tuple-element.35.refs_0_, bf16[32,4,16,128]{3,2,1,0:T(8,128)(2,1)S(1)} %collective-permute-done.1.refs_1_, bf16[32,4,16,128]{3,2,1,0:T(8,128)(2,1)S(1)} %collective-permute-done.2.refs_2_, ...), custom_call_target="tpu_custom_call" | custom-call | flops 6000000000 | tf_op jit(solution)/shard_map/pallas_call | solution.py:373
  88.3 0.0 collective-permute-done.11.refs_2_
  88.4 1.3 collective-permute-start.16
  89.6 12.0 %collective-permute-done.10.refs_1_ = bf16[32,8,16,128]{3,2,1,0:T(8,128)(2,1)S(1)} collective-permute-done((bf16[32,8,16,128]{3,2,1,0:T(8,128)(2,1)S(1)}, bf16[32,8,16,128]{3,2,1,0:T(8,128)(2,1)S(1)}, u32[]{:S(2)}, u32[]{:S(2)}) %collective-permute-start.10) | collective-permute-done | bytes 1048608 | tf_op jit(solution)/shard_map/ppermute | solution.py:405
  101.7 1.3 collective-permute-start.17
  102.9 10.4 %collective-permute-done.16.refs_3_ = bf16[32,8,16,128]{3,2,1,0:T(8,128)(2,1)S(1)} collective-permute-done((bf16[32,8,16,128]{3,2,1,0:T(8,128)(2,1)S(1)}, bf16[32,8,16,128]{3,2,1,0:T(8,128)(2,1)S(1)}, u32[]{:S(2)}, u32[]{:S(2)}) %collective-permute-start.16) | collective-permute-done | bytes 1048608 | tf_op jit(solution)/shard_map/ppermute | solution.py:405
  113.3 1.3 %collective-permute-start.18 = (bf16[32,8,16,128]{3,2,1,0:T(8,128)(2,1)S(1)}, bf16[32,8,16,128]{3,2,1,0:T(8,128)(2,1)S(1)}, u32[]{:S(2)}, u32[]{:S(2)}) collective-permute-start(bf16[32,8,16,128]{3,2,1,0:T(8,128)(2,1)S(1)} %collective-permute-done.16.refs_3_), channel_id=1, source_target_pairs={{2,0},{10,8},{18,16},{26,24},{3,1},{11,9},{19,17},{27,25}} | collective-permute-start | bytes 3145736 | tf_op jit(solution)/shard_map/ppermute | solution.py:405
  114.7 0.0 collective-permute-done.17.refs_4_
  114.7 2.2 %collective-permute-done.18.refs_5_ = bf16[32,8,16,128]{3,2,1,0:T(8,128)(2,1)S(1)} collective-permute-done((bf16[32,8,16,128]{3,2,1,0:T(8,128)(2,1)S(1)}, bf16[32,8,16,128]{3,2,1,0:T(8,128)(2,1)S(1)}, u32[]{:S(2)}, u32[]{:S(2)}) %collective-permute-start.18) | collective-permute-done | bytes 1048608 | tf_op jit(solution)/shard_map/ppermute | solution.py:405
  116.9 0.0 copy-start.5
  116.9 1.0 copy-done.5
  117.9 12.0 %shard_map.51 = f32[2,8,4,8,8,128]{5,4,3,2,1,0:T(8,128)} custom-call(s32[2]{0:T(128)S(1)} %pad_add_fusion.place, bf16[32,8,16,128]{3,2,1,0:T(8,128)(2,1)S(1)} %pad_maximum_fusion.refs_0_, bf16[32,8,16,128]{3,2,1,0:T(8,128)(2,1)S(1)} %collective-permute-done.10.refs_1_, bf16[32,8,16,128]{3,2,1,0:T(8,128)(2,1)S(1)} %collective-permute-done.11.refs_2_, ...), custom_call_target="tpu_custom_call" | custom-call | flops 6000000000 | tf_op jit(solution)/shard_map/pallas_call | solution.py:373
Async XLA Ops:
  3.4 43.8 %collective-permute-start.4 = (bf16[8,8,64,128]{3,2,1,0:T(8,128)(2,1)S(1)}, bf16[8,8,64,128]{3,2,1,0:T(8,128)(2,1)S(1)}, u32[]{:S(2)}, u32[]{:S(2)}) collective-permute-start(bf16[8,8,64,128]{3,2,1,0:T(8,128)(2,1)S(1)} %get-tuple-element.42), channel_id=1, source_target_pairs={{0,1},{1,0},{2,3},{3,2},{4,5},{5,4},{6,7},{7,6},{8,9},{9,8},{10,11... | collective-permute-start | bytes 3145736 | tf_op jit(solution)/shard_map/ppermute | solution.py:433
  16.8 22.8 %collective-permute-start.3 = (bf16[32,4,16,128]{3,2,1,0:T(8,128)(2,1)S(1)}, bf16[32,4,16,128]{3,2,1,0:T(8,128)(2,1)S(1)}, u32[]{:S(2)}, u32[]{:S(2)}) collective-permute-start(bf16[32,4,16,128]{3,2,1,0:T(8,128)(2,1)S(1)} %get-tuple-element.39), channel_id=1, source_target_pairs={{0,1},{1,0},{2,3},{3,2},{4,5},{5,4},{6,7},{7,6},{8,9},{9,8},{10,11... | collective-permute-start | bytes 1572872 | tf_op jit(solution)/shard_map/ppermute | solution.py:437
  16.9 25.8 %collective-permute-start.1 = (bf16[32,4,16,128]{3,2,1,0:T(8,128)(2,1)S(1)}, bf16[32,4,16,128]{3,2,1,0:T(8,128)(2,1)S(1)}, u32[]{:S(2)}, u32[]{:S(2)}) collective-permute-start(bf16[32,4,16,128]{3,2,1,0:T(8,128)(2,1)S(1)} %get-tuple-element.35.refs_0_), channel_id=1, source_target_pairs={{0,4},{2,6},{4,8},{8,12},{10,14},{12,16},{16,20},{18,22},{20,24},{... | collective-permute-start | bytes 1572872 | tf_op jit(solution)/shard_map/ppermute | solution.py:405
  20.2 25.7 %collective-permute-start.2 = (bf16[32,4,16,128]{3,2,1,0:T(8,128)(2,1)S(1)}, bf16[32,4,16,128]{3,2,1,0:T(8,128)(2,1)S(1)}, u32[]{:S(2)}, u32[]{:S(2)}) collective-permute-start(bf16[32,4,16,128]{3,2,1,0:T(8,128)(2,1)S(1)} %get-tuple-element.35.refs_0_), channel_id=1, source_target_pairs={{0,2},{2,8},{4,6},{6,12},{8,10},{10,16},{12,14},{14,20},{16,18},{1... | collective-permute-start | bytes 1572872 | tf_op jit(solution)/shard_map/ppermute | solution.py:405
  34.9 29.0 %collective-permute-start = (bf16[32,4,16,128]{3,2,1,0:T(8,128)(2,1)}, bf16[32,4,16,128]{3,2,1,0:T(8,128)(2,1)}, u32[]{:S(2)}, u32[]{:S(2)}) collective-permute-start(bf16[32,4,16,128]{3,2,1,0:T(8,128)(2,1)} %get-tuple-element.38), channel_id=1, source_target_pairs={{0,1},{2,3},{4,5},{6,7},{8,9},{10,11},{12,13},{14,15},{16,17},{18,... | collective-permute-start | bytes 1572872 | tf_op jit(solution)/shard_map/ppermute | solution.py:443
  39.6 15.6 %collective-permute-start.8 = (bf16[32,4,16,128]{3,2,1,0:T(8,128)(2,1)S(1)}, bf16[32,4,16,128]{3,2,1,0:T(8,128)(2,1)S(1)}, u32[]{:S(2)}, u32[]{:S(2)}) collective-permute-start(bf16[32,4,16,128]{3,2,1,0:T(8,128)(2,1)S(1)} %collective-permute-done.3.refs_6_), channel_id=1, source_target_pairs={{0,4},{2,6},{4,8},{8,12},{10,14},{12,16},{16,20},{18,22},{20,24},{... | collective-permute-start | bytes 1572872 | tf_op jit(solution)/shard_map/ppermute | solution.py:405
  42.7 14.8 %collective-permute-start.9 = (bf16[32,4,16,128]{3,2,1,0:T(8,128)(2,1)S(1)}, bf16[32,4,16,128]{3,2,1,0:T(8,128)(2,1)}, u32[]{:S(2)}, u32[]{:S(2)}) collective-permute-start(bf16[32,4,16,128]{3,2,1,0:T(8,128)(2,1)S(1)} %collective-permute-done.3.refs_6_), channel_id=1, source_target_pairs={{0,2},{2,8},{4,6},{6,12},{8,10},{10,16},{12,14},{14,20},{16,18},{1... | collective-permute-start | bytes 1572872 | tf_op jit(solution)/shard_map/ppermute | solution.py:405
  45.9 11.6 %collective-permute-start.6 = (bf16[32,4,16,128]{3,2,1,0:T(8,128)(2,1)S(1)}, bf16[32,4,16,128]{3,2,1,0:T(8,128)(2,1)S(1)}, u32[]{:S(2)}, u32[]{:S(2)}) collective-permute-start(bf16[32,4,16,128]{3,2,1,0:T(8,128)(2,1)S(1)} %collective-permute-done.1.refs_1_), channel_id=1, source_target_pairs={{0,2},{4,6},{6,4},{8,10},{12,14},{14,12},{16,18},{20,22},{22,20},{... | collective-permute-start | bytes 1572872 | tf_op jit(solution)/shard_map/ppermute | solution.py:405
  47.2 13.9 %collective-permute-start.7 = (bf16[32,4,16,128]{3,2,1,0:T(8,128)(2,1)S(1)}, bf16[32,4,16,128]{3,2,1,0:T(8,128)(2,1)S(1)}, u32[]{:S(2)}, u32[]{:S(2)}) collective-permute-start(bf16[32,4,16,128]{3,2,1,0:T(8,128)(2,1)S(1)} %collective-permute-done.2.refs_2_), channel_id=1, source_target_pairs={{4,2},{12,10},{20,18},{28,26},{5,3},{13,11},{21,19},{29,27}} | collective-permute-start | bytes 1572872 | tf_op jit(solution)/shard_map/ppermute | solution.py:405
  55.2 6.7 %collective-permute-start.5 = (bf16[32,2,16,128]{3,2,1,0:T(8,128)(2,1)S(1)}, bf16[32,2,16,128]{3,2,1,0:T(8,128)(2,1)S(1)}, u32[]{:S(2)}, u32[]{:S(2)}) collective-permute-start(bf16[32,2,16,128]{3,2,1,0:T(8,128)(2,1)S(1)} %get-tuple-element.44), channel_id=1, source_target_pairs={{0,1},{1,0},{2,3},{3,2},{4,5},{5,4},{6,7},{7,6},{8,9},{9,8},{10,11... | collective-permute-start | bytes 786440 | tf_op jit(solution)/shard_map/ppermute | solution.py:453
  57.5 0.8 copy-start
  61.1 0.8 copy-start.2
  61.9 0.7 copy-start.4
  62.6 12.5 %collective-permute-start.13 = (bf16[32,4,16,128]{3,2,1,0:T(8,128)(2,1)}, bf16[32,4,16,128]{3,2,1,0:T(8,128)(2,1)}, u32[]{:S(2)}, u32[]{:S(2)}) collective-permute-start(bf16[32,4,16,128]{3,2,1,0:T(8,128)(2,1)} %collective-permute-done.9.refs_8_), channel_id=1, source_target_pairs={{4,2},{12,10},{20,18},{28,26},{5,3},{13,11},{21,19},{29,27}} | collective-permute-start | bytes 1572872 | tf_op jit(solution)/shard_map/ppermute | solution.py:405
  65.1 13.9 %collective-permute-start.12 = (bf16[32,4,16,128]{3,2,1,0:T(8,128)(2,1)}, bf16[32,4,16,128]{3,2,1,0:T(8,128)(2,1)S(1)}, u32[]{:S(2)}, u32[]{:S(2)}) collective-permute-start(bf16[32,4,16,128]{3,2,1,0:T(8,128)(2,1)} %copy-done.2), channel_id=1, source_target_pairs={{2,0},{10,8},{18,16},{26,24},{3,1},{11,9},{19,17},{27,25}} | collective-permute-start | bytes 1572872 | tf_op jit(solution)/shard_map/ppermute | solution.py:405
  71.6 7.3 %collective-permute-start.14 = (bf16[32,4,16,128]{3,2,1,0:T(8,128)(2,1)S(1)}, bf16[32,4,16,128]{3,2,1,0:T(8,128)(2,1)S(1)}, u32[]{:S(2)}, u32[]{:S(2)}) collective-permute-start(bf16[32,4,16,128]{3,2,1,0:T(8,128)(2,1)S(1)} %collective-permute-done.8.refs_7_), channel_id=1, source_target_pairs={{0,2},{4,6},{6,4},{8,10},{12,14},{14,12},{16,18},{20,22},{22,20},{... | collective-permute-start | bytes 1572872 | tf_op jit(solution)/shard_map/ppermute | solution.py:405
  75.1 3.9 %collective-permute-start.15 = (bf16[32,4,16,128]{3,2,1,0:T(8,128)(2,1)}, bf16[32,4,16,128]{3,2,1,0:T(8,128)(2,1)S(1)}, u32[]{:S(2)}, u32[]{:S(2)}) collective-permute-start(bf16[32,4,16,128]{3,2,1,0:T(8,128)(2,1)} %collective-permute-done.13.refs_9_), channel_id=1, source_target_pairs={{2,0},{10,8},{18,16},{26,24},{3,1},{11,9},{19,17},{27,25}} | collective-permute-start | bytes 1572872 | tf_op jit(solution)/shard_map/ppermute | solution.py:405
  76.4 11.9 %collective-permute-start.11 = (bf16[32,8,16,128]{3,2,1,0:T(8,128)(2,1)S(1)}, bf16[32,8,16,128]{3,2,1,0:T(8,128)(2,1)S(1)}, u32[]{:S(2)}, u32[]{:S(2)}) collective-permute-start(bf16[32,8,16,128]{3,2,1,0:T(8,128)(2,1)S(1)} %pad_maximum_fusion.refs_0_), channel_id=1, source_target_pairs={{0,2},{2,8},{4,6},{6,12},{8,10},{10,16},{12,14},{14,20},{16,18},{1... | collective-permute-start | bytes 3145736 | tf_op jit(solution)/shard_map/ppermute | solution.py:405
  76.5 25.2 %collective-permute-start.10 = (bf16[32,8,16,128]{3,2,1,0:T(8,128)(2,1)S(1)}, bf16[32,8,16,128]{3,2,1,0:T(8,128)(2,1)S(1)}, u32[]{:S(2)}, u32[]{:S(2)}) collective-permute-start(bf16[32,8,16,128]{3,2,1,0:T(8,128)(2,1)S(1)} %pad_maximum_fusion.refs_0_), channel_id=1, source_target_pairs={{0,4},{2,6},{4,8},{8,12},{10,14},{12,16},{16,20},{18,22},{20,24},{... | collective-permute-start | bytes 3145736 | tf_op jit(solution)/shard_map/ppermute | solution.py:405
  79.0 0.8 copy-start.6
  79.8 1.0 copy-start.1
  80.8 1.0 copy-start.3
  88.4 25.0 %collective-permute-start.16 = (bf16[32,8,16,128]{3,2,1,0:T(8,128)(2,1)S(1)}, bf16[32,8,16,128]{3,2,1,0:T(8,128)(2,1)S(1)}, u32[]{:S(2)}, u32[]{:S(2)}) collective-permute-start(bf16[32,8,16,128]{3,2,1,0:T(8,128)(2,1)S(1)} %collective-permute-done.11.refs_2_), channel_id=1, source_target_pairs={{4,2},{12,10},{20,18},{28,26},{5,3},{13,11},{21,19},{29,27}} | collective-permute-start | bytes 3145736 | tf_op jit(solution)/shard_map/ppermute | solution.py:405
  101.7 13.0 %collective-permute-start.17 = (bf16[32,8,16,128]{3,2,1,0:T(8,128)(2,1)S(1)}, bf16[32,8,16,128]{3,2,1,0:T(8,128)(2,1)S(1)}, u32[]{:S(2)}, u32[]{:S(2)}) collective-permute-start(bf16[32,8,16,128]{3,2,1,0:T(8,128)(2,1)S(1)} %collective-permute-done.10.refs_1_), channel_id=1, source_target_pairs={{0,2},{4,6},{6,4},{8,10},{12,14},{14,12},{16,18},{20,22},{22,20},{... | collective-permute-start | bytes 3145736 | tf_op jit(solution)/shard_map/ppermute | solution.py:405
  113.3 3.6 %collective-permute-start.18 = (bf16[32,8,16,128]{3,2,1,0:T(8,128)(2,1)S(1)}, bf16[32,8,16,128]{3,2,1,0:T(8,128)(2,1)S(1)}, u32[]{:S(2)}, u32[]{:S(2)}) collective-permute-start(bf16[32,8,16,128]{3,2,1,0:T(8,128)(2,1)S(1)} %collective-permute-done.16.refs_3_), channel_id=1, source_target_pairs={{2,0},{10,8},{18,16},{26,24},{3,1},{11,9},{19,17},{27,25}} | collective-permute-start | bytes 3145736 | tf_op jit(solution)/shard_map/ppermute | solution.py:405
  116.9 1.0 copy-start.5

commit v9 on v7

--- a/solution.py
+++ b/solution.py
@@ -359,26 +359,26 @@
     lax.fori_loop(0, half // 4 * SUB, finish, 0)
 
 
-def correlate(arrays, pieces, per_group, place, scale, before, last, wait=()):
+def correlate(arrays, pieces, per_group, place, scale, before, last, wait=(), cost=6 * 10**9):
     signals = TILE // 2
     rows = per_group // 2 * H * SUB
     place = after(place, *wait)
     shape = (2, signals, VISITS, per_group // 4, SUB, LANES) if last else (rows, LANES)
     operands = list(arrays) + ([] if before is None else [before])
-    whole = lambda shape: pl.BlockSpec(shape, lambda i, place: (0,) * len(shape))
+    vmem = pl.BlockSpec(memory_space=pltpu.VMEM)
     return pl.pallas_call(
         functools.partial(correlate_kernel, pieces, per_group, scale, before is not None, last),
         grid_spec=pltpu.PrefetchScalarGridSpec(
             num_scalar_prefetch=1,
-            grid=(1,),
-            in_specs=[whole(x.shape) for x in operands],
-            out_specs=whole(shape),
+            grid=(),
+            in_specs=[vmem] * len(operands),
+            out_specs=vmem,
             scratch_shapes=[pltpu.VMEM((rows, LANES), F32)] if last else [],
         ),
         out_shape=jax.ShapeDtypeStruct(shape, F32),
-        compiler_params=pltpu.CompilerParams(vmem_limit_bytes=48 << 20),
+        compiler_params=pltpu.CompilerParams(vmem_limit_bytes=24 << 20),
         input_output_aliases={} if before is None or last else {len(operands): 0},
-        cost_estimate=pl.CostEstimate(flops=6 * 10**9, bytes_accessed=0, transcendentals=0),
+        cost_estimate=pl.CostEstimate(flops=cost, bytes_accessed=0, transcendentals=0),
     )(place, *operands)
 
 
@@ -405,18 +405,6 @@
 
 def exchanged(block):
     return lax.ppermute(block, "stn", [(i, i ^ 1) for i in range(lax.axis_size("stn"))])
-
-
-def general(volts, fir_taps):
-    groups = lax.axis_size("tm")
-    frames = volts.shape[1]
-    volts, edge_frames, *fixed = prepare(volts, fir_taps, place, groups, frames // TAPS - 1, TAPS)
-    history = lax.ppermute(edge_frames, "tm", [(i, i + 1) for i in range(groups - 1)])
-    parts = [(history, TAPS, 0, 0, 1)] + [(volts, TAPS, i, TAPS * (i + 1), 1) for i in range(frames // TAPS)]
-    spectrum = spectra(parts, frames, fixed, place, groups, [K2])[0]
-    spectrum = lax.all_to_all(spectrum, "tm", split_axis=0, concat_axis=0, tiled=True)
-    tiles = spectrum.shape[1]
-    return [([spectrum], [(tiles, [(0, K2 // groups * t, 0) for t in range(groups)])])]
 
 
 def paired(volts, fir_taps, place, correlated):

time: 111 us -> 109 us (0.982)
  Pallas kernels: 41.9 us -> 39 us
  waiting for transfers between devices: 56.8 us -> 58.1 us
    pallas_call x2, Pallas kernels: 18.3 us -> 15.4 us  [correlate(): pl.pallas_call(functools.partial(correlate_kernel, pieces, per_group, sca...]
    ppermute x3, waiting for transfers between devices: 27.7 us -> 29 us  [shifted(): lax.ppermute(block, axis, [(i, (i + distance) % size) for i in range(size)])]
  transfers between devices with their start and end apart: 13 -> 13, of which waited for: 6 -> 6; matrix products, arithmetic and copies ran while one was open for 1% -> 1% of each run, Pallas kernels for 24% -> 23%
where the time goes in v9:
time: 109 us
  waiting for transfers between devices  58.1 us (53%)
  Pallas kernels  39 us (36%)
  starting transfers between devices  8.56 us (8%)
  local copies, waits for them, and re-layouts  2.19 us (2%)
  other arithmetic  1.3 us (1%)
    ppermute x3, waiting for transfers between devices, shifted(): lax.ppermute(block, axis, [(i, (i + distance) % size) for i in range(size)])  29 us
    pallas_call x3, Pallas kernels, spectra(): pl.pallas_call(functools.partial(spectra_kernel, groups, tuple((part[1:]...  20.3 us
    pallas_call x2, Pallas kernels, correlate(): pl.pallas_call(functools.partial(correlate_kernel, pieces, per_group, sca...  15.4 us
    ppermute x3, waiting for transfers between devices, farther(): lax.ppermute(block, 'stn', [(i, (i + 1 if i % 2 == 0 else i + 3) % size)...  12.9 us
    ppermute x1, waiting for transfers between devices, paired(): got_a = lax.ppermute(away_a, 'tm', swap)  10.4 us
    ppermute x1, waiting for transfers between devices, paired(): got_c = lax.ppermute(away_c, 'tm', swap)  5.75 us
    ppermute x3, starting transfers between devices, shifted(): lax.ppermute(block, axis, [(i, (i + distance) % size) for i in range(size)])  4.63 us
    pallas_call x1, Pallas kernels, prepare(): pl.pallas_call(functools.partial(prepare_kernel, edge_block, int(groups =...  3.29 us
  transfers between devices with their start and end apart: 13, of which 6 were waited for; matrix products, arithmetic and copies ran while one was open for 1% of the time, Pallas kernels for 23%

profile of v9, /device:TPU:6, one launch (start us, length us, event | category | flops | bytes accessed | tf_op | source)
XLA Modules:
  0.0 109.2 jit_solution(18055273329940759718)
XLA Ops:
  0.0 0.1 pad_add_fusion.place
  0.1 3.3 %shard_map.46 = (bf16[8,32,64,128]{3,2,1,0:T(8,128)(2,1)S(1)}, bf16[8,8,64,128]{3,2,1,0:T(8,128)(2,1)S(1)}, f32[1024,128]{1,0:T(8,128)S(1)}, bf16[64,192]{1,0:T(...) custom-call(s32[2]{0:T(128)S(1)} %pad_add_fusion.place, bf16[8,32,64,128]{3,2,1,0:T(8,128)(2,1)} %bitcast.10, ...), custom_call_target="tpu_custom_call" | custom-call | tf_op jit(solution)/shard_map/pallas_call | solution.py:110
  3.4 0.0 copy-start
  3.4 0.6 collective-permute-start.3
  4.0 12.3 %shard_map.47 = (bf16[32,4,16,128]{3,2,1,0:T(8,128)(2,1)}, bf16[32,4,16,128]{3,2,1,0:T(8,128)(2,1)}) custom-call(s32[2]{0:T(128)S(1)} %pad_add_fusion.place, bf16[8,32,64,128]{3,2,1,0:T(8,128)(2,1)S(1)} %get-tuple-element.21.refs_0_.refs_1_, bf16[8,32,64,128]{3,2,1,0:T(8,128)(2,1)S(1)} %get-tuple-element.21.refs_0_.refs_1_, ...), custom_call_target="tpu_custom_call" | custom-call | flops 1000000 | tf_op jit(solution)/shard_map/pallas_call | solution.py:263
  16.2 1.6 %collective-permute-start.1 = (bf16[32,4,16,128]{3,2,1,0:T(8,128)(2,1)}, bf16[32,4,16,128]{3,2,1,0:T(8,128)(2,1)}, u32[]{:S(2)}, u32[]{:S(2)}) collective-permute-start(bf16[32,4,16,128]{3,2,1,0:T(8,128)(2,1)} %get-tuple-element.26.refs_0_), channel_id=1, source_target_pairs={{0,4},{2,6},{4,8},{6,10},{8,12},{10,14},{12,16},{14,18},{16,20},{1... | collective-permute-start | bytes 1572872 | tf_op jit(solution)/shard_map/ppermute | solution.py:397
  17.8 1.5 %collective-permute-start.2 = (bf16[32,4,16,128]{3,2,1,0:T(8,128)(2,1)}, bf16[32,4,16,128]{3,2,1,0:T(8,128)(2,1)}, u32[]{:S(2)}, u32[]{:S(2)}) collective-permute-start(bf16[32,4,16,128]{3,2,1,0:T(8,128)(2,1)} %get-tuple-element.30), channel_id=1, source_target_pairs={{0,1},{1,0},{2,3},{3,2},{4,5},{5,4},{6,7},{7,6},{8,9},{9,8},{10,11... | collective-permute-start | bytes 1572872 | tf_op jit(solution)/shard_map/ppermute | solution.py:422
  19.3 0.0 collective-permute-start.6
  19.3 0.0 copy-done
  19.3 1.4 %shard_map.48 = (bf16[32,4,16,128]{3,2,1,0:T(8,128)(2,1)S(1)}, bf16[32,4,16,128]{3,2,1,0:T(8,128)(2,1)}) custom-call(s32[2]{0:T(128)S(1)} %pad_add_fusion.place, bf16[8,32,64,128]{3,2,1,0:T(8,128)(2,1)S(1)} %get-tuple-element.21.refs_0_.refs_1_, bf16[8,32,64,128]{3,2,1,0:T(8,128)(2,1)S(1)} %get-tuple-element.21.refs_0_.refs_1_, ...), custom_call_target="tpu_custom_call" | custom-call | flops 1000000 | tf_op jit(solution)/shard_map/pallas_call | solution.py:263
  20.6 1.3 %collective-permute-start = (bf16[32,4,16,128]{3,2,1,0:T(8,128)(2,1)}, bf16[32,4,16,128]{3,2,1,0:T(8,128)(2,1)}, u32[]{:S(2)}, u32[]{:S(2)}) collective-permute-start(bf16[32,4,16,128]{3,2,1,0:T(8,128)(2,1)} %get-tuple-element.29), channel_id=1, source_target_pairs={{0,1},{2,3},{4,5},{6,7},{8,9},{10,11},{12,13},{14,15},{16,17},{18,... | collective-permute-start | bytes 1572872 | tf_op jit(solution)/shard_map/ppermute | solution.py:427
  21.9 8.5 %collective-permute-done.1.refs_2_ = bf16[32,4,16,128]{3,2,1,0:T(8,128)(2,1)} collective-permute-done((bf16[32,4,16,128]{3,2,1,0:T(8,128)(2,1)}, bf16[32,4,16,128]{3,2,1,0:T(8,128)(2,1)}, u32[]{:S(2)}, u32[]{:S(2)}) %collective-permute-start.1) | collective-permute-done | bytes 524320 | tf_op jit(solution)/shard_map/ppermute | solution.py:397
  30.5 10.4 %collective-permute-done.2.refs_4_ = bf16[32,4,16,128]{3,2,1,0:T(8,128)(2,1)} collective-permute-done((bf16[32,4,16,128]{3,2,1,0:T(8,128)(2,1)}, bf16[32,4,16,128]{3,2,1,0:T(8,128)(2,1)}, u32[]{:S(2)}, u32[]{:S(2)}) %collective-permute-start.2) | collective-permute-done | bytes 524320 | tf_op jit(solution)/shard_map/ppermute | solution.py:422
  40.8 1.5 %collective-permute-start.4 = (bf16[32,4,16,128]{3,2,1,0:T(8,128)(2,1)}, bf16[32,4,16,128]{3,2,1,0:T(8,128)(2,1)S(1)}, u32[]{:S(2)}, u32[]{:S(2)}) collective-permute-start(bf16[32,4,16,128]{3,2,1,0:T(8,128)(2,1)} %collective-permute-done.2.refs_4_), channel_id=1, source_target_pairs={{0,4},{2,6},{4,8},{6,10},{8,12},{10,14},{12,16},{14,18},{16,20},{1... | collective-permute-start | bytes 1572872 | tf_op jit(solution)/shard_map/ppermute | solution.py:397
  42.4 0.0 collective-permute-start.5
  42.4 0.0 collective-permute-done.3.refs_2_
  42.4 0.5 collective-permute-start.10
  42.9 0.0 copy-start.1
  42.9 2.2 %copy-done.1 = bf16[8,32,64,128]{3,2,1,0:T(8,128)(2,1)S(1)} copy-done((bf16[8,32,64,128]{3,2,1,0:T(8,128)(2,1)S(1)}, bf16[8,32,64,128]{3,2,1,0:T(8,128)(2,1)}, u32[]{:S(2)}) %copy-start.1) | copy-done | bytes 4194328
  45.1 6.7 %shard_map.49 = (bf16[32,2,16,128]{3,2,1,0:T(8,128)(2,1)S(1)}, bf16[32,2,16,128]{3,2,1,0:T(8,128)(2,1)S(1)}) custom-call(s32[2]{0:T(128)S(1)} %pad_add_fusion.place, bf16[8,32,64,128]{3,2,1,0:T(8,128)(2,1)S(1)} %copy-done.1, bf16[8,32,64,128]{3,2,1,0:T(8,128)(2,1)S(1)} %copy-done.1, bf16[8,8,64,128]{3,2,1,0:T(8,128)(2,1)S(1)} %collective-permute-done.3.refs_2_, ...), custom_call_target="tpu_custom_call" | custom-call | flops 8999999488 | tf_op jit(solution)/shard_map/pallas_call | solution.py:263
  51.8 0.0 collective-permute-done
  51.8 0.1 collective-permute-start.7
  51.9 1.1 %broadcast_select_fusion = bf16[32,4,16,128]{3,2,1,0:T(8,128)(2,1)S(1)} fusion(bf16[32,4,16,128]{3,2,1,0:T(8,128)(2,1)S(1)} %get-tuple-element.28, bf16[32,4,16,128]{3,2,1,0:T(8,128)(2,1)} %collective-permute-done, pred[]{:T(512)S(6)} %eq.5), kind=kLoop, calls=%fused_computation.1 | loop fusion | flops 262144 | bytes 1572865 | tf_op jit(solution)/shard_map/jit(_where)/select_n | solution.py:441
  53.0 0.0 collective-permute-done.6.refs_3_
  53.0 2.1 %collective-permute-done.4.refs_6_ = bf16[32,4,16,128]{3,2,1,0:T(8,128)(2,1)S(1)} collective-permute-done((bf16[32,4,16,128]{3,2,1,0:T(8,128)(2,1)}, bf16[32,4,16,128]{3,2,1,0:T(8,128)(2,1)S(1)}, u32[]{:S(2)}, u32[]{:S(2)}) %collective-permute-start.4) | collective-permute-done | bytes 524320 | tf_op jit(solution)/shard_map/ppermute | solution.py:397
  55.1 0.0 collective-permute-done.5.refs_1_
  55.1 0.0 collective-permute-start.9
  55.1 5.8 %collective-permute-done.7 = bf16[32,2,16,128]{3,2,1,0:T(8,128)(2,1)S(1)} collective-permute-done((bf16[32,2,16,128]{3,2,1,0:T(8,128)(2,1)S(1)}, bf16[32,2,16,128]{3,2,1,0:T(8,128)(2,1)S(1)}, u32[]{:S(2)}, u32[]{:S(2)}) %collective-permute-start.7) | collective-permute-done | bytes 262176 | tf_op jit(solution)/shard_map/ppermute | solution.py:437
  60.8 0.1 pad_maximum_fusion.refs_0_
  61.0 1.5 %collective-permute-start.8 = (bf16[32,8,16,128]{3,2,1,0:T(8,128)(2,1)S(1)}, bf16[32,8,16,128]{3,2,1,0:T(8,128)(2,1)S(1)}, u32[]{:S(2)}, u32[]{:S(2)}) collective-permute-start(bf16[32,8,16,128]{3,2,1,0:T(8,128)(2,1)S(1)} %pad_maximum_fusion.refs_0_), channel_id=1, source_target_pairs={{0,4},{2,6},{4,8},{6,10},{8,12},{10,14},{12,16},{14,18},{16,20},{1... | collective-permute-start | bytes 3145736 | tf_op jit(solution)/shard_map/ppermute | solution.py:397
  62.5 0.0 collective-permute-start.12
  62.5 0.0 collective-permute-done.10.refs_7_
  62.5 0.0 collective-permute-done.9.refs_5_
  62.5 5.3 %shard_map.50.refs_4_ = f32[4096,128]{1,0:T(8,128)S(1)} custom-call(s32[2]{0:T(128)S(1)} %pad_add_fusion.place, bf16[32,4,16,128]{3,2,1,0:T(8,128)(2,1)} %get-tuple-element.26.refs_0_, bf16[32,4,16,128]{3,2,1,0:T(8,128)(2,1)S(1)} %collective-permute-done.5.refs_1_, bf16[32,4,16,128]{3,2,1,0:T(8,128)(2,1)} %collective-permute-done.1.refs_2_, ...), custom_call_target="tpu_custom_call" | custom-call | flops 6000000000 | tf_op jit(solution)/shard_map/pallas_call | solution.py:369
  67.8 18.4 %collective-permute-done.8.refs_2_ = bf16[32,8,16,128]{3,2,1,0:T(8,128)(2,1)S(1)} collective-permute-done((bf16[32,8,16,128]{3,2,1,0:T(8,128)(2,1)S(1)}, bf16[32,8,16,128]{3,2,1,0:T(8,128)(2,1)S(1)}, u32[]{:S(2)}, u32[]{:S(2)}) %collective-permute-start.8) | collective-permute-done | bytes 1048608 | tf_op jit(solution)/shard_map/ppermute | solution.py:397
  86.2 0.0 collective-permute-start.11
  86.2 12.9 %collective-permute-done.12.refs_3_ = bf16[32,8,16,128]{3,2,1,0:T(8,128)(2,1)S(1)} collective-permute-done((bf16[32,8,16,128]{3,2,1,0:T(8,128)(2,1)S(1)}, bf16[32,8,16,128]{3,2,1,0:T(8,128)(2,1)S(1)}, u32[]{:S(2)}, u32[]{:S(2)}) %collective-permute-start.12) | collective-permute-done | bytes 1048608 | tf_op jit(solution)/shard_map/ppermute | solution.py:402
  99.1 0.0 collective-permute-done.11.refs_1_
  99.1 10.1 %shard_map.51 = f32[2,8,4,8,8,128]{5,4,3,2,1,0:T(8,128)} custom-call(s32[2]{0:T(128)S(1)} %pad_add_fusion.place, bf16[32,8,16,128]{3,2,1,0:T(8,128)(2,1)S(1)} %pad_maximum_fusion.refs_0_, bf16[32,8,16,128]{3,2,1,0:T(8,128)(2,1)S(1)} %collective-permute-done.11.refs_1_, bf16[32,8,16,128]{3,2,1,0:T(8,128)(2,1)S(1)} %collective-permute-done.8.refs_2_, ...), custom_call_target="tpu_custom_call" | custom-call | flops 6000000000 | tf_op jit(solution)/shard_map/pallas_call | solution.py:369
Async XLA Ops:
  3.4 15.9 %copy-start = (bf16[8,32,64,128]{3,2,1,0:T(8,128)(2,1)}, bf16[8,32,64,128]{3,2,1,0:T(8,128)(2,1)S(1)}, u32[]{:S(2)}) copy-start(bf16[8,32,64,128]{3,2,1,0:T(8,128)(2,1)S(1)} %get-tuple-element.21.refs_0_.refs_1_) | copy-start | bytes 12582916
  3.4 39.0 %collective-permute-start.3 = (bf16[8,8,64,128]{3,2,1,0:T(8,128)(2,1)S(1)}, bf16[8,8,64,128]{3,2,1,0:T(8,128)(2,1)S(1)}, u32[]{:S(2)}, u32[]{:S(2)}) collective-permute-start(bf16[8,8,64,128]{3,2,1,0:T(8,128)(2,1)S(1)} %get-tuple-element.32), channel_id=1, source_target_pairs={{0,1},{1,0},{2,3},{3,2},{4,5},{5,4},{6,7},{7,6},{8,9},{9,8},{10,11... | collective-permute-start | bytes 3145736 | tf_op jit(solution)/shard_map/ppermute | solution.py:418
  16.2 14.2 %collective-permute-start.1 = (bf16[32,4,16,128]{3,2,1,0:T(8,128)(2,1)}, bf16[32,4,16,128]{3,2,1,0:T(8,128)(2,1)}, u32[]{:S(2)}, u32[]{:S(2)}) collective-permute-start(bf16[32,4,16,128]{3,2,1,0:T(8,128)(2,1)} %get-tuple-element.26.refs_0_), channel_id=1, source_target_pairs={{0,4},{2,6},{4,8},{6,10},{8,12},{10,14},{12,16},{14,18},{16,20},{1... | collective-permute-start | bytes 1572872 | tf_op jit(solution)/shard_map/ppermute | solution.py:397
  17.8 23.1 %collective-permute-start.2 = (bf16[32,4,16,128]{3,2,1,0:T(8,128)(2,1)}, bf16[32,4,16,128]{3,2,1,0:T(8,128)(2,1)}, u32[]{:S(2)}, u32[]{:S(2)}) collective-permute-start(bf16[32,4,16,128]{3,2,1,0:T(8,128)(2,1)} %get-tuple-element.30), channel_id=1, source_target_pairs={{0,1},{1,0},{2,3},{3,2},{4,5},{5,4},{6,7},{7,6},{8,9},{9,8},{10,11... | collective-permute-start | bytes 1572872 | tf_op jit(solution)/shard_map/ppermute | solution.py:422
  19.3 33.7 %collective-permute-start.6 = (bf16[32,4,16,128]{3,2,1,0:T(8,128)(2,1)}, bf16[32,4,16,128]{3,2,1,0:T(8,128)(2,1)}, u32[]{:S(2)}, u32[]{:S(2)}) collective-permute-start(bf16[32,4,16,128]{3,2,1,0:T(8,128)(2,1)} %get-tuple-element.26.refs_0_), channel_id=1, source_target_pairs={{0,2},{2,8},{4,6},{6,12},{8,10},{10,16},{12,14},{14,20},{16,18},{1... | collective-permute-start | bytes 1572872 | tf_op jit(solution)/shard_map/ppermute | solution.py:402
  20.6 31.2 %collective-permute-start = (bf16[32,4,16,128]{3,2,1,0:T(8,128)(2,1)}, bf16[32,4,16,128]{3,2,1,0:T(8,128)(2,1)}, u32[]{:S(2)}, u32[]{:S(2)}) collective-permute-start(bf16[32,4,16,128]{3,2,1,0:T(8,128)(2,1)} %get-tuple-element.29), channel_id=1, source_target_pairs={{0,1},{2,3},{4,5},{6,7},{8,9},{10,11},{12,13},{14,15},{16,17},{18,... | collective-permute-start | bytes 1572872 | tf_op jit(solution)/shard_map/ppermute | solution.py:427
  40.8 14.2 %collective-permute-start.4 = (bf16[32,4,16,128]{3,2,1,0:T(8,128)(2,1)}, bf16[32,4,16,128]{3,2,1,0:T(8,128)(2,1)S(1)}, u32[]{:S(2)}, u32[]{:S(2)}) collective-permute-start(bf16[32,4,16,128]{3,2,1,0:T(8,128)(2,1)} %collective-permute-done.2.refs_4_), channel_id=1, source_target_pairs={{0,4},{2,6},{4,8},{6,10},{8,12},{10,14},{12,16},{14,18},{16,20},{1... | collective-permute-start | bytes 1572872 | tf_op jit(solution)/shard_map/ppermute | solution.py:397
  42.4 12.7 %collective-permute-start.5 = (bf16[32,4,16,128]{3,2,1,0:T(8,128)(2,1)}, bf16[32,4,16,128]{3,2,1,0:T(8,128)(2,1)S(1)}, u32[]{:S(2)}, u32[]{:S(2)}) collective-permute-start(bf16[32,4,16,128]{3,2,1,0:T(8,128)(2,1)} %collective-permute-done.1.refs_2_), channel_id=1, source_target_pairs={{0,2},{2,0},{4,6},{6,4},{8,10},{10,8},{12,14},{14,12},{16,18},{18,... | collective-permute-start | bytes 1572872 | tf_op jit(solution)/shard_map/ppermute | solution.py:407
  42.4 20.1 %collective-permute-start.10 = (bf16[32,4,16,128]{3,2,1,0:T(8,128)(2,1)}, bf16[32,4,16,128]{3,2,1,0:T(8,128)(2,1)S(1)}, u32[]{:S(2)}, u32[]{:S(2)}) collective-permute-start(bf16[32,4,16,128]{3,2,1,0:T(8,128)(2,1)} %collective-permute-done.2.refs_4_), channel_id=1, source_target_pairs={{0,2},{2,8},{4,6},{6,12},{8,10},{10,16},{12,14},{14,20},{16,18},{1... | collective-permute-start | bytes 1572872 | tf_op jit(solution)/shard_map/ppermute | solution.py:402
  42.9 2.2 %copy-start.1 = (bf16[8,32,64,128]{3,2,1,0:T(8,128)(2,1)S(1)}, bf16[8,32,64,128]{3,2,1,0:T(8,128)(2,1)}, u32[]{:S(2)}) copy-start(bf16[8,32,64,128]{3,2,1,0:T(8,128)(2,1)} %copy-done) | copy-start | bytes 12582916
  51.8 9.0 %collective-permute-start.7 = (bf16[32,2,16,128]{3,2,1,0:T(8,128)(2,1)S(1)}, bf16[32,2,16,128]{3,2,1,0:T(8,128)(2,1)S(1)}, u32[]{:S(2)}, u32[]{:S(2)}) collective-permute-start(bf16[32,2,16,128]{3,2,1,0:T(8,128)(2,1)S(1)} %get-tuple-element.35), channel_id=1, source_target_pairs={{0,1},{1,0},{2,3},{3,2},{4,5},{5,4},{6,7},{7,6},{8,9},{9,8},{10,11... | collective-permute-start | bytes 786440 | tf_op jit(solution)/shard_map/ppermute | solution.py:437
  55.1 7.4 %collective-permute-start.9 = (bf16[32,4,16,128]{3,2,1,0:T(8,128)(2,1)S(1)}, bf16[32,4,16,128]{3,2,1,0:T(8,128)(2,1)S(1)}, u32[]{:S(2)}, u32[]{:S(2)}) collective-permute-start(bf16[32,4,16,128]{3,2,1,0:T(8,128)(2,1)S(1)} %collective-permute-done.4.refs_6_), channel_id=1, source_target_pairs={{0,2},{2,0},{4,6},{6,4},{8,10},{10,8},{12,14},{14,12},{16,18},{18,... | collective-permute-start | bytes 1572872 | tf_op jit(solution)/shard_map/ppermute | solution.py:407
  61.0 25.2 %collective-permute-start.8 = (bf16[32,8,16,128]{3,2,1,0:T(8,128)(2,1)S(1)}, bf16[32,8,16,128]{3,2,1,0:T(8,128)(2,1)S(1)}, u32[]{:S(2)}, u32[]{:S(2)}) collective-permute-start(bf16[32,8,16,128]{3,2,1,0:T(8,128)(2,1)S(1)} %pad_maximum_fusion.refs_0_), channel_id=1, source_target_pairs={{0,4},{2,6},{4,8},{6,10},{8,12},{10,14},{12,16},{14,18},{16,20},{1... | collective-permute-start | bytes 3145736 | tf_op jit(solution)/shard_map/ppermute | solution.py:397
  62.5 36.6 %collective-permute-start.12 = (bf16[32,8,16,128]{3,2,1,0:T(8,128)(2,1)S(1)}, bf16[32,8,16,128]{3,2,1,0:T(8,128)(2,1)S(1)}, u32[]{:S(2)}, u32[]{:S(2)}) collective-permute-start(bf16[32,8,16,128]{3,2,1,0:T(8,128)(2,1)S(1)} %pad_maximum_fusion.refs_0_), channel_id=1, source_target_pairs={{0,2},{2,8},{4,6},{6,12},{8,10},{10,16},{12,14},{14,20},{16,18},{1... | collective-permute-start | bytes 3145736 | tf_op jit(solution)/shard_map/ppermute | solution.py:402
  86.2 13.0 %collective-permute-start.11 = (bf16[32,8,16,128]{3,2,1,0:T(8,128)(2,1)S(1)}, bf16[32,8,16,128]{3,2,1,0:T(8,128)(2,1)S(1)}, u32[]{:S(2)}, u32[]{:S(2)}) collective-permute-start(bf16[32,8,16,128]{3,2,1,0:T(8,128)(2,1)S(1)} %collective-permute-done.8.refs_2_), channel_id=1, source_target_pairs={{0,2},{2,0},{4,6},{6,4},{8,10},{10,8},{12,14},{14,12},{16,18},{18,... | collective-permute-start | bytes 3145736 | tf_op jit(solution)/shard_map/ppermute | solution.py:407

commit v10 on v9

--- a/solution.py
+++ b/solution.py
@@ -359,7 +359,7 @@
     lax.fori_loop(0, half // 4 * SUB, finish, 0)
 
 
-def correlate(arrays, pieces, per_group, place, scale, before, last, wait=(), cost=6 * 10**9):
+def correlate(arrays, pieces, per_group, place, scale, before, last, wait=(), cost=10**3):
     signals = TILE // 2
     rows = per_group // 2 * H * SUB
     place = after(place, *wait)
@@ -414,8 +414,8 @@
     swap = [(0, 1), (1, 0)]
     edge = TAPS // 2
     last = frames // edge
+    many, few = TAPS * H // LANES, edge * H // LANES
     volts, edge_frames, *fixed = prepare(volts, fir_taps, place, 2, (last - 1, 0), edge)
-    visiting = lax.ppermute(edge_frames, "tm", swap)
     own_a, away_a = spectra(
         [(volts, TAPS, 0, 0, (0, 1)), (volts, TAPS, (0, 1), TAPS, 1)], TAPS, fixed, place, 2, sizes
     )
@@ -424,30 +424,33 @@
     own_b, away_b = spectra(
         [(volts, TAPS, 0, 0, 1), (volts, TAPS, 1, TAPS, 1)], TAPS, fixed, place, 2, sizes, (1, 0), (own_a,)
     )
+    got_a, own_b, away_b, edge_frames, two_a = lax.optimization_barrier((got_a, own_b, away_b, edge_frames, two_a))
+    two_g, rest_g = farther(got_a)
     got_b = lax.ppermute(away_b, "tm", [(0, 1)])
+    visiting = lax.ppermute(edge_frames, "tm", swap)
     pair_a = exchanged(two_a)
+    first = [(many, [(0, 0, 0)])]
+    sums = correlated([own_a, pair_a, two_a, rest_a], first, None, False)
+    two_g, rest_g, got_b, sums = lax.optimization_barrier((two_g, rest_g, got_b, sums))
+    piece_b = jnp.where(me == 0, own_b, got_b)
+    two_b, rest_b = farther(piece_b)
+    pair_g = exchanged(two_g)
     own_c, away_c = spectra(
         [
             (volts, edge, (last - 2, 0), (0, edge), 1),
             (volts, edge, (last - 1, 1), (edge, 2 * edge), 1),
             (visiting, edge, 0, (2 * edge, 0), 1),
         ],
-        edge, fixed, place, 2, sizes, 1, (own_b, two_a, got_a), 9 * 10**9,
+        edge, fixed, place, 2, sizes, 1, (piece_b, pair_g), 9 * 10**9,
     )
     got_c = lax.ppermute(away_c, "tm", swap)
-    two_g, rest_g = farther(got_a)
-    pair_g = exchanged(two_g)
-    own_c = after(own_c, two_g, pair_a, rest_a)
-    rest = jnp.concatenate([jnp.where(me == 0, own_b, got_b), own_c, got_c], axis=1)
-    two_r, rest_r = farther(rest)
-    many, few = own_a.shape[1], own_c.shape[1]
-    sums = correlated(
-        [own_a, pair_a, two_a, rest_a, got_a, pair_g, two_g, rest_g], [(many, [(0, 0, 0), (1, 0, 0)])], None, False
-    )
-    pair_r = exchanged(after(two_r, sums))
-    return correlated(
-        [rest, pair_r, two_r, rest_r], [(many, [(0, 0, 0)]), (few, [(0, 0, many), (0, 0, many + few)])], sums, True
-    )
+    piece_c = jnp.concatenate([own_c, got_c], axis=1)
+    two_c, rest_c = farther(piece_c)
+    sums = correlated([got_a, pair_g, two_g, rest_g], first, sums, False, (piece_c, two_b), 6 * 10**9)
+    pair_b = exchanged(two_b)
+    sums = correlated([piece_b, pair_b, two_b, rest_b], first, sums, False)
+    pair_c = exchanged(after(two_c, sums))
+    return correlated([piece_c, pair_c, two_c, rest_c], [(few, [(0, 0, 0), (0, 0, few)])], sums, True)
 
 
 def general(volts, fir_taps, place, correlated):
@@ -468,12 +471,12 @@
     place = jnp.stack([lax.axis_index("tm"), lax.axis_index("stn") % 2]).astype(jnp.int32)
     scale = 1.0 / (groups * voltage.shape[1])
 
-    def correlated(arrays, pieces, before, last, wait=()):
+    def correlated(arrays, pieces, before, last, wait=(), cost=10**3):
         laid = [
             (tiles, [[(VISITS * n + visit, row, column) for n, row, column in spots] for visit in range(VISITS)])
             for tiles, spots in pieces
         ]
-        return correlate(arrays, laid, K2 // groups, place, scale, before, last, wait)
+        return correlate(arrays, laid, K2 // groups, place, scale, before, last, wait, cost)
 
     run = paired if groups == 2 else general
     return natural(run(stacked(voltage), fir_taps, place, correlated))

time: 109 us -> 120 us (1.10)
  the two profiles are of different devices: /device:TPU:6 before, /device:TPU:1 now
where the time goes in v10:
time: 120 us; the launch traced here: 118 us
  Pallas kernels  54.5 us (45%)
  waiting for transfers between devices  30.4 us (25%)
  starting transfers between devices  29.2 us (24%)
  local copies, waits for them, and re-layouts  3.85 us (3%)
    pallas_call x3, Pallas kernels, spectra(): pl.pallas_call(functools.partial(spectra_kernel, groups, tuple((part[1:]...  30.5 us
    pallas_call x4, Pallas kernels, correlate(): pl.pallas_call(functools.partial(correlate_kernel, pieces, per_group, sca...  19.7 us
    ppermute x4, waiting for transfers between devices, shifted(): lax.ppermute(block, axis, [(i, (i + distance) % size) for i in range(size)])  15.1 us
    ppermute x1, waiting for transfers between devices, paired(): visiting = lax.ppermute(edge_frames, 'tm', swap)  10.6 us
    ppermute x4, starting transfers between devices, shifted(): lax.ppermute(block, axis, [(i, (i + distance) % size) for i in range(size)])  10.5 us
    ppermute x4, starting transfers between devices, farther(): lax.ppermute(block, 'stn', [(i, (i + 1 if i % 2 == 0 else i + 3) % size)...  6.64 us
    ppermute x4, starting transfers between devices, exchanged(): lax.ppermute(block, 'stn', [(i, i ^ 1) for i in range(lax.axis_size('stn'...  5.65 us
    pallas_call x1, Pallas kernels, prepare(): pl.pallas_call(functools.partial(prepare_kernel, edge_block, int(groups =...  4.26 us
  transfers between devices with their start and end apart: 16, of which 6 were waited for; matrix products, arithmetic and copies ran while one was open for 0% of the time, Pallas kernels for 26%

profile of v10, /device:TPU:1, one launch (start us, length us, event | category | flops | bytes accessed | tf_op | source)
XLA Modules:
  0.0 118.3 jit_solution(16200615951052529675)
XLA Ops:
  0.0 0.1 pad_add_fusion.place
  0.1 4.3 %shard_map.46 = (bf16[8,32,64,128]{3,2,1,0:T(8,128)(2,1)S(1)}, bf16[8,8,64,128]{3,2,1,0:T(8,128)(2,1)}, f32[1024,128]{1,0:T(8,128)S(1)}, bf16[64,192]{1,0:T(8,12...) custom-call(s32[2]{0:T(128)S(1)} %pad_add_fusion.place, bf16[8,32,64,128]{3,2,1,0:T(8,128)(2,1)} %bitcast.10, ...), custom_call_target="tpu_custom_call" | custom-call | tf_op jit(solution)/shard_map/pallas_call | solution.py:110
  4.3 0.0 copy-start
  4.3 11.3 %shard_map.47 = (bf16[32,4,16,128]{3,2,1,0:T(8,128)(2,1)S(1)}, bf16[32,4,16,128]{3,2,1,0:T(8,128)(2,1)S(1)}) custom-call(s32[2]{0:T(128)S(1)} %pad_add_fusion.place, bf16[8,32,64,128]{3,2,1,0:T(8,128)(2,1)S(1)} %get-tuple-element.30.refs_0_.refs_1_, bf16[8,32,64,128]{3,2,1,0:T(8,128)(2,1)S(1)} %get-tuple-element.30.refs_0_.refs_1_, ...), custom_call_target="tpu_custom_call" | custom-call | flops 1000000 | tf_op jit(solution)/shard_map/pallas_call | solution.py:263
  15.7 2.2 %collective-permute-start = (bf16[32,4,16,128]{3,2,1,0:T(8,128)(2,1)S(1)}, bf16[32,4,16,128]{3,2,1,0:T(8,128)(2,1)S(1)}, u32[]{:S(2)}, u32[]{:S(2)}) collective-permute-start(bf16[32,4,16,128]{3,2,1,0:T(8,128)(2,1)S(1)} %get-tuple-element.35), channel_id=1, source_target_pairs={{0,1},{1,0},{2,3},{3,2},{4,5},{5,4},{6,7},{7,6},{8,9},{9,8},{10,11... | collective-permute-start | bytes 1572872 | tf_op jit(solution)/shard_map/ppermute | solution.py:422
  17.8 1.2 %collective-permute-start.1 = (bf16[32,4,16,128]{3,2,1,0:T(8,128)(2,1)S(1)}, bf16[32,4,16,128]{3,2,1,0:T(8,128)(2,1)S(1)}, u32[]{:S(2)}, u32[]{:S(2)}) collective-permute-start(bf16[32,4,16,128]{3,2,1,0:T(8,128)(2,1)S(1)} %get-tuple-element.36.refs_0_), channel_id=1, source_target_pairs={{0,4},{2,6},{4,8},{6,10},{8,12},{10,14},{12,16},{14,18},{16,20},{1... | collective-permute-start | bytes 1572872 | tf_op jit(solution)/shard_map/ppermute | solution.py:397
  19.1 2.4 %collective-permute-start.6 = (bf16[32,4,16,128]{3,2,1,0:T(8,128)(2,1)S(1)}, bf16[32,4,16,128]{3,2,1,0:T(8,128)(2,1)S(1)}, u32[]{:S(2)}, u32[]{:S(2)}) collective-permute-start(bf16[32,4,16,128]{3,2,1,0:T(8,128)(2,1)S(1)} %get-tuple-element.36.refs_0_), channel_id=1, source_target_pairs={{0,2},{2,8},{4,6},{6,12},{8,10},{10,16},{12,14},{14,20},{16,18},{1... | collective-permute-start | bytes 1572872 | tf_op jit(solution)/shard_map/ppermute | solution.py:402
  21.5 0.0 copy-done
  21.5 11.2 %shard_map.48 = (bf16[32,4,16,128]{3,2,1,0:T(8,128)(2,1)S(1)}, bf16[32,4,16,128]{3,2,1,0:T(8,128)(2,1)S(1)}) custom-call(s32[2]{0:T(128)S(1)} %pad_add_fusion.place, bf16[8,32,64,128]{3,2,1,0:T(8,128)(2,1)S(1)} %get-tuple-element.30.refs_0_.refs_1_, bf16[8,32,64,128]{3,2,1,0:T(8,128)(2,1)S(1)} %get-tuple-element.30.refs_0_.refs_1_, ...), custom_call_target="tpu_custom_call" | custom-call | flops 1000000 | tf_op jit(solution)/shard_map/pallas_call | solution.py:263
  32.7 0.0 collective-permute-done.refs_0_
  32.7 0.0 copy-start.2
  32.7 0.5 collective-permute-done.1.refs_2_
  33.2 3.1 %collective-permute-start.5 = (bf16[32,4,16,128]{3,2,1,0:T(8,128)(2,1)S(1)}, bf16[32,4,16,128]{3,2,1,0:T(8,128)(2,1)S(1)}, u32[]{:S(2)}, u32[]{:S(2)}) collective-permute-start(bf16[32,4,16,128]{3,2,1,0:T(8,128)(2,1)S(1)} %collective-permute-done.1.refs_2_), channel_id=1, source_target_pairs={{0,2},{2,0},{4,6},{6,4},{8,10},{10,8},{12,14},{14,12},{16,18},{18,... | collective-permute-start | bytes 1572872 | tf_op jit(solution)/shard_map/ppermute | solution.py:407
  36.3 0.0 collective-permute-start.2
  36.3 0.0 collective-permute-start.3
  36.3 1.9 %collective-permute-start.4 = (bf16[32,4,16,128]{3,2,1,0:T(8,128)(2,1)S(1)}, bf16[32,4,16,128]{3,2,1,0:T(8,128)(2,1)S(1)}, u32[]{:S(2)}, u32[]{:S(2)}) collective-permute-start(bf16[32,4,16,128]{3,2,1,0:T(8,128)(2,1)S(1)} %get-tuple-element.43), channel_id=1, source_target_pairs={{0,1},{2,3},{4,5},{6,7},{8,9},{10,11},{12,13},{14,15},{16,17},{18,... | collective-permute-start | bytes 1572872 | tf_op jit(solution)/shard_map/ppermute | solution.py:429
  38.3 0.0 collective-permute-done.6.refs_3_
  38.3 0.1 collective-permute-start.8
  38.4 0.0 collective-permute-done.5.refs_1_
  38.4 2.7 %shard_map.49.refs_4_ = f32[4096,128]{1,0:T(8,128)S(1)} custom-call(s32[2]{0:T(128)S(1)} %pad_add_fusion.place, bf16[32,4,16,128]{3,2,1,0:T(8,128)(2,1)S(1)} %get-tuple-element.36.refs_0_, bf16[32,4,16,128]{3,2,1,0:T(8,128)(2,1)S(1)} %collective-permute-done.5.refs_1_, bf16[32,4,16,128]{3,2,1,0:T(8,128)(2,1)S(1)} %collective-permute-done.1.refs_2_, ...), custom_call_target="tpu_custom_call" | custom-call | flops 1000 | tf_op jit(solution)/shard_map/pallas_call | solution.py:369
  41.1 0.0 copy-done.2
  41.1 11.6 %collective-permute-done.2.refs_2_ = bf16[32,4,16,128]{3,2,1,0:T(8,128)(2,1)} collective-permute-done((bf16[32,4,16,128]{3,2,1,0:T(8,128)(2,1)S(1)}, bf16[32,4,16,128]{3,2,1,0:T(8,128)(2,1)}, u32[]{:S(2)}, u32[]{:S(2)}) %collective-permute-start.2) | collective-permute-done | bytes 524320 | tf_op jit(solution)/shard_map/ppermute | solution.py:397
  52.7 0.0 collective-permute-done.3.refs_3_
  52.7 0.0 copy-start.4
  52.7 0.8 copy-done.4
  53.5 0.0 collective-permute-done.4
  53.5 0.0 copy-start.6
  53.5 0.8 copy-done.6
  54.3 1.2 collective-permute-start.7
  55.5 0.0 copy-start.3
  55.5 0.0 copy-start.5
  55.5 0.1 broadcast_select_fusion.refs_0_
  55.5 5.5 %collective-permute-start.11 = (bf16[32,4,16,128]{3,2,1,0:T(8,128)(2,1)S(1)}, bf16[32,4,16,128]{3,2,1,0:T(8,128)(2,1)S(1)}, u32[]{:S(2)}, u32[]{:S(2)}) collective-permute-start(bf16[32,4,16,128]{3,2,1,0:T(8,128)(2,1)S(1)} %broadcast_select_fusion.refs_0_), channel_id=1, source_target_pairs={{0,4},{2,6},{4,8},{6,10},{8,12},{10,14},{12,16},{14,18},{16,20},{1... | collective-permute-start | bytes 1572872 | tf_op jit(solution)/shard_map/ppermute | solution.py:397
  61.0 0.0 collective-permute-done.7.refs_1_
  61.0 10.6 %collective-permute-done.8.refs_2_ = bf16[8,8,64,128]{3,2,1,0:T(8,128)(2,1)} collective-permute-done((bf16[8,8,64,128]{3,2,1,0:T(8,128)(2,1)}, bf16[8,8,64,128]{3,2,1,0:T(8,128)(2,1)}, u32[]{:S(2)}, u32[]{:S(2)}) %collective-permute-start.8) | collective-permute-done | bytes 1048608 | tf_op jit(solution)/shard_map/ppermute | solution.py:430
  71.6 0.0 copy-start.1
  71.6 2.2 %copy-done.1 = bf16[8,32,64,128]{3,2,1,0:T(8,128)(2,1)S(1)} copy-done((bf16[8,32,64,128]{3,2,1,0:T(8,128)(2,1)S(1)}, bf16[8,32,64,128]{3,2,1,0:T(8,128)(2,1)}, u32[]{:S(2)}) %copy-start.1) | copy-done | bytes 4194328
  73.8 8.0 %shard_map.50 = (bf16[32,2,16,128]{3,2,1,0:T(8,128)(2,1)S(1)}, bf16[32,2,16,128]{3,2,1,0:T(8,128)(2,1)S(1)}) custom-call(s32[2]{0:T(128)S(1)} %pad_add_fusion.place, bf16[8,32,64,128]{3,2,1,0:T(8,128)(2,1)S(1)} %copy-done.1, bf16[8,32,64,128]{3,2,1,0:T(8,128)(2,1)S(1)} %copy-done.1, bf16[8,8,64,128]{3,2,1,0:T(8,128)(2,1)} %collective-permute-done.8.refs_2_, ...), custom_call_target="tpu_custom_call" | custom-call | flops 8999999488 | tf_op jit(solution)/shard_map/pallas_call | solution.py:263
  81.7 2.3 %collective-permute-start.9 = (bf16[32,2,16,128]{3,2,1,0:T(8,128)(2,1)S(1)}, bf16[32,2,16,128]{3,2,1,0:T(8,128)(2,1)S(1)}, u32[]{:S(2)}, u32[]{:S(2)}) collective-permute-start(bf16[32,2,16,128]{3,2,1,0:T(8,128)(2,1)S(1)} %get-tuple-element.50), channel_id=1, source_target_pairs={{0,1},{1,0},{2,3},{3,2},{4,5},{5,4},{6,7},{7,6},{8,9},{9,8},{10,11... | collective-permute-start | bytes 786440 | tf_op jit(solution)/shard_map/ppermute | solution.py:446
  84.0 2.0 %collective-permute-start.13 = (bf16[32,4,16,128]{3,2,1,0:T(8,128)(2,1)S(1)}, bf16[32,4,16,128]{3,2,1,0:T(8,128)(2,1)S(1)}, u32[]{:S(2)}, u32[]{:S(2)}) collective-permute-start(bf16[32,4,16,128]{3,2,1,0:T(8,128)(2,1)S(1)} %broadcast_select_fusion.refs_0_), channel_id=1, source_target_pairs={{0,2},{2,8},{4,6},{6,12},{8,10},{10,16},{12,14},{14,20},{16,18},{1... | collective-permute-start | bytes 1572872 | tf_op jit(solution)/shard_map/ppermute | solution.py:402
  86.0 0.0 collective-permute-done.11.refs_2_
  86.0 0.0 collective-permute-start.12
  86.0 3.2 %collective-permute-done.9 = bf16[32,2,16,128]{3,2,1,0:T(8,128)(2,1)S(1)} collective-permute-done((bf16[32,2,16,128]{3,2,1,0:T(8,128)(2,1)S(1)}, bf16[32,2,16,128]{3,2,1,0:T(8,128)(2,1)S(1)}, u32[]{:S(2)}, u32[]{:S(2)}) %collective-permute-start.9) | collective-permute-done | bytes 262176 | tf_op jit(solution)/shard_map/ppermute | solution.py:446
  89.3 3.8 %collective-permute-start.10 = (bf16[32,4,16,128]{3,2,1,0:T(8,128)(2,1)S(1)}, bf16[32,4,16,128]{3,2,1,0:T(8,128)(2,1)S(1)}, u32[]{:S(2)}, u32[]{:S(2)}) collective-permute-start(bf16[32,4,16,128]{3,2,1,0:T(8,128)(2,1)S(1)} %constant_dynamic-update-slice_fusion.refs_0_), channel_id=1, source_target_pairs={{0,4},{2,6},{4,8},{6,10},{8,12},{10,14},{12,16},{14,18},{16,20},{1... | collective-permute-start | bytes 1572872 | tf_op jit(solution)/shard_map/ppermute | solution.py:397
  93.1 2.2 %collective-permute-start.15 = (bf16[32,4,16,128]{3,2,1,0:T(8,128)(2,1)S(1)}, bf16[32,4,16,128]{3,2,1,0:T(8,128)(2,1)S(1)}, u32[]{:S(2)}, u32[]{:S(2)}) collective-permute-start(bf16[32,4,16,128]{3,2,1,0:T(8,128)(2,1)S(1)} %constant_dynamic-update-slice_fusion.refs_0_), channel_id=1, source_target_pairs={{0,2},{2,8},{4,6},{6,12},{8,10},{10,16},{12,14},{14,20},{16,18},{1... | collective-permute-start | bytes 1572872 | tf_op jit(solution)/shard_map/ppermute | solution.py:402
  95.3 0.0 copy-done.3
  95.3 0.0 copy-done.5
  95.3 5.2 %shard_map.51.refs_4_ = f32[4096,128]{1,0:T(8,128)S(1)} custom-call(s32[2]{0:T(128)S(1)} %pad_add_fusion.place, bf16[32,4,16,128]{3,2,1,0:T(8,128)(2,1)S(1)} %copy-done.3, bf16[32,4,16,128]{3,2,1,0:T(8,128)(2,1)} %collective-permute-done.7.refs_1_, bf16[32,4,16,128]{3,2,1,0:T(8,128)(2,1)} %collective-permute-done.2.refs_2_, ...), custom_call_target="tpu_custom_call", output_to_operand_aliasing={{}: (5, {})} | custom-call | flops 6000000000 | tf_op jit(solution)/shard_map/pallas_call | solution.py:369
  100.5 0.0 collective-permute-done.13.refs_3_
  100.5 0.0 collective-permute-done.12.refs_1_
  100.5 4.0 %shard_map.52.refs_4_ = f32[4096,128]{1,0:T(8,128)S(1)} custom-call(s32[2]{0:T(128)S(1)} %pad_add_fusion.place, bf16[32,4,16,128]{3,2,1,0:T(8,128)(2,1)S(1)} %broadcast_select_fusion.refs_0_, bf16[32,4,16,128]{3,2,1,0:T(8,128)(2,1)S(1)} %collective-permute-done.12.refs_1_, ...), custom_call_target="tpu_custom_call", output_to_operand_aliasing={{}: (5, {})} | custom-call | flops 1000 | tf_op jit(solution)/shard_map/pallas_call | solution.py:369
  104.5 3.1 %collective-permute-done.10.refs_2_ = bf16[32,4,16,128]{3,2,1,0:T(8,128)(2,1)S(1)} collective-permute-done((bf16[32,4,16,128]{3,2,1,0:T(8,128)(2,1)S(1)}, bf16[32,4,16,128]{3,2,1,0:T(8,128)(2,1)S(1)}, u32[]{:S(2)}, u32[]{:S(2)}) %collective-permute-start.10) | collective-permute-done | bytes 524320 | tf_op jit(solution)/shard_map/ppermute | solution.py:397
  107.6 1.3 %collective-permute-start.14 = (bf16[32,4,16,128]{3,2,1,0:T(8,128)(2,1)S(1)}, bf16[32,4,16,128]{3,2,1,0:T(8,128)(2,1)S(1)}, u32[]{:S(2)}, u32[]{:S(2)}) collective-permute-start(bf16[32,4,16,128]{3,2,1,0:T(8,128)(2,1)S(1)} %collective-permute-done.10.refs_2_), channel_id=1, source_target_pairs={{0,2},{2,0},{4,6},{6,4},{8,10},{10,8},{12,14},{14,12},{16,18},{18,... | collective-permute-start | bytes 1572872 | tf_op jit(solution)/shard_map/ppermute | solution.py:407
  108.9 0.0 collective-permute-done.15.refs_3_
  108.9 1.5 %collective-permute-done.14.refs_1_ = bf16[32,4,16,128]{3,2,1,0:T(8,128)(2,1)S(1)} collective-permute-done((bf16[32,4,16,128]{3,2,1,0:T(8,128)(2,1)S(1)}, bf16[32,4,16,128]{3,2,1,0:T(8,128)(2,1)S(1)}, u32[]{:S(2)}, u32[]{:S(2)}) %collective-permute-start.14) | collective-permute-done | bytes 524320 | tf_op jit(solution)/shard_map/ppermute | solution.py:407
  110.4 7.9 %shard_map.53 = f32[2,8,4,8,8,128]{5,4,3,2,1,0:T(8,128)} custom-call(s32[2]{0:T(128)S(1)} %pad_add_fusion.place, bf16[32,4,16,128]{3,2,1,0:T(8,128)(2,1)S(1)} %constant_dynamic-update-slice_fusion.refs_0_, bf16[32,4,16,128]{3,2,1,0:T(8,128)(2,1)S(1)} %collective-permute-done.14.refs_1_, bf16[32,4,16,128]{3,2,1,0:T(8,128)(2,1)S(1)} %collective-permute-done.10.refs_2_, ...), custom_call_target="tpu_custom_call" | custom-call | flops 1000 | tf_op jit(solution)/shard_map/pallas_call | solution.py:369
  (2 shorter events, 0.1 us)
Async XLA Ops:
  4.3 17.1 %copy-start = (bf16[8,32,64,128]{3,2,1,0:T(8,128)(2,1)}, bf16[8,32,64,128]{3,2,1,0:T(8,128)(2,1)S(1)}, u32[]{:S(2)}) copy-start(bf16[8,32,64,128]{3,2,1,0:T(8,128)(2,1)S(1)} %get-tuple-element.30.refs_0_.refs_1_) | copy-start | bytes 12582916
  15.7 17.1 %collective-permute-start = (bf16[32,4,16,128]{3,2,1,0:T(8,128)(2,1)S(1)}, bf16[32,4,16,128]{3,2,1,0:T(8,128)(2,1)S(1)}, u32[]{:S(2)}, u32[]{:S(2)}) collective-permute-start(bf16[32,4,16,128]{3,2,1,0:T(8,128)(2,1)S(1)} %get-tuple-element.35), channel_id=1, source_target_pairs={{0,1},{1,0},{2,3},{3,2},{4,5},{5,4},{6,7},{7,6},{8,9},{9,8},{10,11... | collective-permute-start | bytes 1572872 | tf_op jit(solution)/shard_map/ppermute | solution.py:422
  17.8 15.4 %collective-permute-start.1 = (bf16[32,4,16,128]{3,2,1,0:T(8,128)(2,1)S(1)}, bf16[32,4,16,128]{3,2,1,0:T(8,128)(2,1)S(1)}, u32[]{:S(2)}, u32[]{:S(2)}) collective-permute-start(bf16[32,4,16,128]{3,2,1,0:T(8,128)(2,1)S(1)} %get-tuple-element.36.refs_0_), channel_id=1, source_target_pairs={{0,4},{2,6},{4,8},{6,10},{8,12},{10,14},{12,16},{14,18},{16,20},{1... | collective-permute-start | bytes 1572872 | tf_op jit(solution)/shard_map/ppermute | solution.py:397
  19.1 19.2 %collective-permute-start.6 = (bf16[32,4,16,128]{3,2,1,0:T(8,128)(2,1)S(1)}, bf16[32,4,16,128]{3,2,1,0:T(8,128)(2,1)S(1)}, u32[]{:S(2)}, u32[]{:S(2)}) collective-permute-start(bf16[32,4,16,128]{3,2,1,0:T(8,128)(2,1)S(1)} %get-tuple-element.36.refs_0_), channel_id=1, source_target_pairs={{0,2},{2,8},{4,6},{6,12},{8,10},{10,16},{12,14},{14,20},{16,18},{1... | collective-permute-start | bytes 1572872 | tf_op jit(solution)/shard_map/ppermute | solution.py:402
  32.7 8.4 %copy-start.2 = (bf16[32,4,16,128]{3,2,1,0:T(8,128)(2,1)}, bf16[32,4,16,128]{3,2,1,0:T(8,128)(2,1)S(1)}, u32[]{:S(2)}) copy-start(bf16[32,4,16,128]{3,2,1,0:T(8,128)(2,1)S(1)} %collective-permute-done.refs_0_) | copy-start | bytes 1572868
  33.2 5.1 %collective-permute-start.5 = (bf16[32,4,16,128]{3,2,1,0:T(8,128)(2,1)S(1)}, bf16[32,4,16,128]{3,2,1,0:T(8,128)(2,1)S(1)}, u32[]{:S(2)}, u32[]{:S(2)}) collective-permute-start(bf16[32,4,16,128]{3,2,1,0:T(8,128)(2,1)S(1)} %collective-permute-done.1.refs_2_), channel_id=1, source_target_pairs={{0,2},{2,0},{4,6},{6,4},{8,10},{10,8},{12,14},{14,12},{16,18},{18,... | collective-permute-start | bytes 1572872 | tf_op jit(solution)/shard_map/ppermute | solution.py:407
  36.3 16.4 %collective-permute-start.2 = (bf16[32,4,16,128]{3,2,1,0:T(8,128)(2,1)S(1)}, bf16[32,4,16,128]{3,2,1,0:T(8,128)(2,1)}, u32[]{:S(2)}, u32[]{:S(2)}) collective-permute-start(bf16[32,4,16,128]{3,2,1,0:T(8,128)(2,1)S(1)} %collective-permute-done.refs_0_), channel_id=1, source_target_pairs={{0,4},{2,6},{4,8},{6,10},{8,12},{10,14},{12,16},{14,18},{16,20},{1... | collective-permute-start | bytes 1572872 | tf_op jit(solution)/shard_map/ppermute | solution.py:397
  36.3 16.4 %collective-permute-start.3 = (bf16[32,4,16,128]{3,2,1,0:T(8,128)(2,1)S(1)}, bf16[32,4,16,128]{3,2,1,0:T(8,128)(2,1)S(1)}, u32[]{:S(2)}, u32[]{:S(2)}) collective-permute-start(bf16[32,4,16,128]{3,2,1,0:T(8,128)(2,1)S(1)} %collective-permute-done.refs_0_), channel_id=1, source_target_pairs={{0,2},{2,8},{4,6},{6,12},{8,10},{10,16},{12,14},{14,20},{16,18},{1... | collective-permute-start | bytes 1572872 | tf_op jit(solution)/shard_map/ppermute | solution.py:402
  36.3 17.2 %collective-permute-start.4 = (bf16[32,4,16,128]{3,2,1,0:T(8,128)(2,1)S(1)}, bf16[32,4,16,128]{3,2,1,0:T(8,128)(2,1)S(1)}, u32[]{:S(2)}, u32[]{:S(2)}) collective-permute-start(bf16[32,4,16,128]{3,2,1,0:T(8,128)(2,1)S(1)} %get-tuple-element.43), channel_id=1, source_target_pairs={{0,1},{2,3},{4,5},{6,7},{8,9},{10,11},{12,13},{14,15},{16,17},{18,... | collective-permute-start | bytes 1572872 | tf_op jit(solution)/shard_map/ppermute | solution.py:429
  38.3 33.3 %collective-permute-start.8 = (bf16[8,8,64,128]{3,2,1,0:T(8,128)(2,1)}, bf16[8,8,64,128]{3,2,1,0:T(8,128)(2,1)}, u32[]{:S(2)}, u32[]{:S(2)}) collective-permute-start(bf16[8,8,64,128]{3,2,1,0:T(8,128)(2,1)} %get-tuple-element.48), channel_id=1, source_target_pairs={{0,1},{1,0},{2,3},{3,2},{4,5},{5,4},{6,7},{7,6},{8,9},{9,8},{10,11... | collective-permute-start | bytes 3145736 | tf_op jit(solution)/shard_map/ppermute | solution.py:430
  52.7 0.8 copy-start.4
  53.5 0.8 copy-start.6
  54.3 6.7 %collective-permute-start.7 = (bf16[32,4,16,128]{3,2,1,0:T(8,128)(2,1)}, bf16[32,4,16,128]{3,2,1,0:T(8,128)(2,1)}, u32[]{:S(2)}, u32[]{:S(2)}) collective-permute-start(bf16[32,4,16,128]{3,2,1,0:T(8,128)(2,1)} %collective-permute-done.2.refs_2_), channel_id=1, source_target_pairs={{0,2},{2,0},{4,6},{6,4},{8,10},{10,8},{12,14},{14,12},{16,18},{18,... | collective-permute-start | bytes 1572872 | tf_op jit(solution)/shard_map/ppermute | solution.py:407
  55.5 39.9 %copy-start.3 = (bf16[32,4,16,128]{3,2,1,0:T(8,128)(2,1)S(1)}, bf16[32,4,16,128]{3,2,1,0:T(8,128)(2,1)}, u32[]{:S(2)}) copy-start(bf16[32,4,16,128]{3,2,1,0:T(8,128)(2,1)} %copy-done.2) | copy-start | bytes 1572868
  55.5 39.9 %copy-start.5 = (bf16[32,4,16,128]{3,2,1,0:T(8,128)(2,1)S(1)}, bf16[32,4,16,128]{3,2,1,0:T(8,128)(2,1)}, u32[]{:S(2)}) copy-start(bf16[32,4,16,128]{3,2,1,0:T(8,128)(2,1)} %copy-done.4) | copy-start | bytes 1572868
  55.5 30.4 %collective-permute-start.11 = (bf16[32,4,16,128]{3,2,1,0:T(8,128)(2,1)S(1)}, bf16[32,4,16,128]{3,2,1,0:T(8,128)(2,1)S(1)}, u32[]{:S(2)}, u32[]{:S(2)}) collective-permute-start(bf16[32,4,16,128]{3,2,1,0:T(8,128)(2,1)S(1)} %broadcast_select_fusion.refs_0_), channel_id=1, source_target_pairs={{0,4},{2,6},{4,8},{6,10},{8,12},{10,14},{12,16},{14,18},{16,20},{1... | collective-permute-start | bytes 1572872 | tf_op jit(solution)/shard_map/ppermute | solution.py:397
  71.6 2.2 %copy-start.1 = (bf16[8,32,64,128]{3,2,1,0:T(8,128)(2,1)S(1)}, bf16[8,32,64,128]{3,2,1,0:T(8,128)(2,1)}, u32[]{:S(2)}) copy-start(bf16[8,32,64,128]{3,2,1,0:T(8,128)(2,1)} %copy-done) | copy-start | bytes 12582916
  81.7 7.5 %collective-permute-start.9 = (bf16[32,2,16,128]{3,2,1,0:T(8,128)(2,1)S(1)}, bf16[32,2,16,128]{3,2,1,0:T(8,128)(2,1)S(1)}, u32[]{:S(2)}, u32[]{:S(2)}) collective-permute-start(bf16[32,2,16,128]{3,2,1,0:T(8,128)(2,1)S(1)} %get-tuple-element.50), channel_id=1, source_target_pairs={{0,1},{1,0},{2,3},{3,2},{4,5},{5,4},{6,7},{7,6},{8,9},{9,8},{10,11... | collective-permute-start | bytes 786440 | tf_op jit(solution)/shard_map/ppermute | solution.py:446
  84.0 16.5 %collective-permute-start.13 = (bf16[32,4,16,128]{3,2,1,0:T(8,128)(2,1)S(1)}, bf16[32,4,16,128]{3,2,1,0:T(8,128)(2,1)S(1)}, u32[]{:S(2)}, u32[]{:S(2)}) collective-permute-start(bf16[32,4,16,128]{3,2,1,0:T(8,128)(2,1)S(1)} %broadcast_select_fusion.refs_0_), channel_id=1, source_target_pairs={{0,2},{2,8},{4,6},{6,12},{8,10},{10,16},{12,14},{14,20},{16,18},{1... | collective-permute-start | bytes 1572872 | tf_op jit(solution)/shard_map/ppermute | solution.py:402
  86.0 14.5 %collective-permute-start.12 = (bf16[32,4,16,128]{3,2,1,0:T(8,128)(2,1)S(1)}, bf16[32,4,16,128]{3,2,1,0:T(8,128)(2,1)S(1)}, u32[]{:S(2)}, u32[]{:S(2)}) collective-permute-start(bf16[32,4,16,128]{3,2,1,0:T(8,128)(2,1)S(1)} %collective-permute-done.11.refs_2_), channel_id=1, source_target_pairs={{0,2},{2,0},{4,6},{6,4},{8,10},{10,8},{12,14},{14,12},{16,18},{18,... | collective-permute-start | bytes 1572872 | tf_op jit(solution)/shard_map/ppermute | solution.py:407
  89.3 18.3 %collective-permute-start.10 = (bf16[32,4,16,128]{3,2,1,0:T(8,128)(2,1)S(1)}, bf16[32,4,16,128]{3,2,1,0:T(8,128)(2,1)S(1)}, u32[]{:S(2)}, u32[]{:S(2)}) collective-permute-start(bf16[32,4,16,128]{3,2,1,0:T(8,128)(2,1)S(1)} %constant_dynamic-update-slice_fusion.refs_0_), channel_id=1, source_target_pairs={{0,4},{2,6},{4,8},{6,10},{8,12},{10,14},{12,16},{14,18},{16,20},{1... | collective-permute-start | bytes 1572872 | tf_op jit(solution)/shard_map/ppermute | solution.py:397
  93.1 15.8 %collective-permute-start.15 = (bf16[32,4,16,128]{3,2,1,0:T(8,128)(2,1)S(1)}, bf16[32,4,16,128]{3,2,1,0:T(8,128)(2,1)S(1)}, u32[]{:S(2)}, u32[]{:S(2)}) collective-permute-start(bf16[32,4,16,128]{3,2,1,0:T(8,128)(2,1)S(1)} %constant_dynamic-update-slice_fusion.refs_0_), channel_id=1, source_target_pairs={{0,2},{2,8},{4,6},{6,12},{8,10},{10,16},{12,14},{14,20},{16,18},{1... | collective-permute-start | bytes 1572872 | tf_op jit(solution)/shard_map/ppermute | solution.py:402
  107.6 2.9 %collective-permute-start.14 = (bf16[32,4,16,128]{3,2,1,0:T(8,128)(2,1)S(1)}, bf16[32,4,16,128]{3,2,1,0:T(8,128)(2,1)S(1)}, u32[]{:S(2)}, u32[]{:S(2)}) collective-permute-start(bf16[32,4,16,128]{3,2,1,0:T(8,128)(2,1)S(1)} %collective-permute-done.10.refs_2_), channel_id=1, source_target_pairs={{0,2},{2,0},{4,6},{6,4},{8,10},{10,8},{12,14},{14,12},{16,18},{18,... | collective-permute-start | bytes 1572872 | tf_op jit(solution)/shard_map/ppermute | solution.py:407

commit v11 on v10

--- a/solution.py
+++ b/solution.py
@@ -416,6 +416,7 @@
     last = frames // edge
     many, few = TAPS * H // LANES, edge * H // LANES
     volts, edge_frames, *fixed = prepare(volts, fir_taps, place, 2, (last - 1, 0), edge)
+    visiting = lax.ppermute(edge_frames, "tm", swap)
     own_a, away_a = spectra(
         [(volts, TAPS, 0, 0, (0, 1)), (volts, TAPS, (0, 1), TAPS, 1)], TAPS, fixed, place, 2, sizes
     )
@@ -424,29 +425,28 @@
     own_b, away_b = spectra(
         [(volts, TAPS, 0, 0, 1), (volts, TAPS, 1, TAPS, 1)], TAPS, fixed, place, 2, sizes, (1, 0), (own_a,)
     )
-    got_a, own_b, away_b, edge_frames, two_a = lax.optimization_barrier((got_a, own_b, away_b, edge_frames, two_a))
-    two_g, rest_g = farther(got_a)
-    got_b = lax.ppermute(away_b, "tm", [(0, 1)])
-    visiting = lax.ppermute(edge_frames, "tm", swap)
-    pair_a = exchanged(two_a)
-    first = [(many, [(0, 0, 0)])]
-    sums = correlated([own_a, pair_a, two_a, rest_a], first, None, False)
-    two_g, rest_g, got_b, sums = lax.optimization_barrier((two_g, rest_g, got_b, sums))
-    piece_b = jnp.where(me == 0, own_b, got_b)
-    two_b, rest_b = farther(piece_b)
-    pair_g = exchanged(two_g)
     own_c, away_c = spectra(
         [
             (volts, edge, (last - 2, 0), (0, edge), 1),
             (volts, edge, (last - 1, 1), (edge, 2 * edge), 1),
             (visiting, edge, 0, (2 * edge, 0), 1),
         ],
-        edge, fixed, place, 2, sizes, 1, (piece_b, pair_g), 9 * 10**9,
+        edge, fixed, place, 2, sizes, 1, (own_b, two_a),
     )
+    got_a, own_c, away_b, away_c, two_a = lax.optimization_barrier((got_a, own_c, away_b, away_c, two_a))
+    two_g, rest_g = farther(got_a)
+    got_b = lax.ppermute(away_b, "tm", [(0, 1)])
     got_c = lax.ppermute(away_c, "tm", swap)
+    pair_a = exchanged(two_a)
+    first = [(many, [(0, 0, 0)])]
+    sums = correlated([own_a, pair_a, two_a, rest_a], first, None, False)
+    got_b, got_c, sums = lax.optimization_barrier((got_b, got_c, sums))
+    piece_b = jnp.where(me == 0, own_b, got_b)
+    two_b, rest_b = farther(piece_b)
     piece_c = jnp.concatenate([own_c, got_c], axis=1)
     two_c, rest_c = farther(piece_c)
-    sums = correlated([got_a, pair_g, two_g, rest_g], first, sums, False, (piece_c, two_b), 6 * 10**9)
+    pair_g = exchanged(after(two_g, piece_b))
+    sums = correlated([got_a, pair_g, two_g, rest_g], first, sums, False, (piece_c,), 6 * 10**9)
     pair_b = exchanged(two_b)
     sums = correlated([piece_b, pair_b, two_b, rest_b], first, sums, False)
     pair_c = exchanged(after(two_c, sums))

time: 120 us -> 109 us (0.908)
  the two profiles are of different devices: /device:TPU:1 before, /device:TPU:6 now
where the time goes in v11:
time: 109 us
  waiting for transfers between devices  49.2 us (45%)
  Pallas kernels  43 us (39%)
  starting transfers between devices  14.6 us (13%)
  other arithmetic  1.17 us (1%)
    pallas_call x3, Pallas kernels, spectra(): pl.pallas_call(functools.partial(spectra_kernel, groups, tuple((part[1:]...  20.2 us
    pallas_call x4, Pallas kernels, correlate(): pl.pallas_call(functools.partial(correlate_kernel, pieces, per_group, sca...  19.6 us
    ppermute x4, waiting for transfers between devices, shifted(): lax.ppermute(block, axis, [(i, (i + distance) % size) for i in range(size)])  18.7 us
    ppermute x4, waiting for transfers between devices, farther(): lax.ppermute(block, 'stn', [(i, (i + 1 if i % 2 == 0 else i + 3) % size)...  14.5 us
    ppermute x1, waiting for transfers between devices, paired(): got_c = lax.ppermute(away_c, 'tm', swap)  13.1 us
    ppermute x4, starting transfers between devices, shifted(): lax.ppermute(block, axis, [(i, (i + distance) % size) for i in range(size)])  6.3 us
    ppermute x1, starting transfers between devices, paired(): got_c = lax.ppermute(away_c, 'tm', swap)  3.44 us
    pallas_call x1, Pallas kernels, prepare(): pl.pallas_call(functools.partial(prepare_kernel, edge_block, int(groups =...  3.29 us
  transfers between devices with their start and end apart: 16, of which 7 were waited for; matrix products, arithmetic and copies ran while one was open for 2% of the time, Pallas kernels for 29%

profile of v11, /device:TPU:6, one launch (start us, length us, event | category | flops | bytes accessed | tf_op | source)
XLA Modules:
  0.0 109.2 jit_solution(15690409716006331565)
XLA Ops:
  0.0 0.1 pad_add_fusion.place
  0.1 3.3 %shard_map.46 = (bf16[8,32,64,128]{3,2,1,0:T(8,128)(2,1)S(1)}, bf16[8,8,64,128]{3,2,1,0:T(8,128)(2,1)S(1)}, f32[1024,128]{1,0:T(8,128)S(1)}, bf16[64,192]{1,0:T(...) custom-call(s32[2]{0:T(128)S(1)} %pad_add_fusion.place, bf16[8,32,64,128]{3,2,1,0:T(8,128)(2,1)} %bitcast.10, ...), custom_call_target="tpu_custom_call" | custom-call | tf_op jit(solution)/shard_map/pallas_call | solution.py:110
  3.4 0.6 collective-permute-start.2
  3.9 11.4 %shard_map.47 = (bf16[32,4,16,128]{3,2,1,0:T(8,128)(2,1)S(1)}, bf16[32,4,16,128]{3,2,1,0:T(8,128)(2,1)S(1)}) custom-call(s32[2]{0:T(128)S(1)} %pad_add_fusion.place, bf16[8,32,64,128]{3,2,1,0:T(8,128)(2,1)S(1)} %get-tuple-element.30.refs_0_.refs_1_, bf16[8,32,64,128]{3,2,1,0:T(8,128)(2,1)S(1)} %get-tuple-element.30.refs_0_.refs_1_, ...), custom_call_target="tpu_custom_call" | custom-call | flops 1000000 | tf_op jit(solution)/shard_map/pallas_call | solution.py:263
  15.3 1.6 %collective-permute-start.1 = (bf16[32,4,16,128]{3,2,1,0:T(8,128)(2,1)S(1)}, bf16[32,4,16,128]{3,2,1,0:T(8,128)(2,1)S(1)}, u32[]{:S(2)}, u32[]{:S(2)}) collective-permute-start(bf16[32,4,16,128]{3,2,1,0:T(8,128)(2,1)S(1)} %get-tuple-element.36.refs_0_), channel_id=1, source_target_pairs={{0,4},{2,6},{4,8},{6,10},{8,12},{10,14},{12,16},{14,18},{16,20},{1... | collective-permute-start | bytes 1572872 | tf_op jit(solution)/shard_map/ppermute | solution.py:397
  16.9 1.5 %collective-permute-start = (bf16[32,4,16,128]{3,2,1,0:T(8,128)(2,1)S(1)}, bf16[32,4,16,128]{3,2,1,0:T(8,128)(2,1)S(1)}, u32[]{:S(2)}, u32[]{:S(2)}) collective-permute-start(bf16[32,4,16,128]{3,2,1,0:T(8,128)(2,1)S(1)} %get-tuple-element.35), channel_id=1, source_target_pairs={{0,1},{1,0},{2,3},{3,2},{4,5},{5,4},{6,7},{7,6},{8,9},{9,8},{10,11... | collective-permute-start | bytes 1572872 | tf_op jit(solution)/shard_map/ppermute | solution.py:423
  18.4 0.0 collective-permute-start.6
  18.4 1.4 %shard_map.48 = (bf16[32,4,16,128]{3,2,1,0:T(8,128)(2,1)S(1)}, bf16[32,4,16,128]{3,2,1,0:T(8,128)(2,1)}) custom-call(s32[2]{0:T(128)S(1)} %pad_add_fusion.place, bf16[8,32,64,128]{3,2,1,0:T(8,128)(2,1)S(1)} %get-tuple-element.30.refs_0_.refs_1_, bf16[8,32,64,128]{3,2,1,0:T(8,128)(2,1)S(1)} %get-tuple-element.30.refs_0_.refs_1_, ...), custom_call_target="tpu_custom_call" | custom-call | flops 1000000 | tf_op jit(solution)/shard_map/pallas_call | solution.py:263
  19.8 9.5 %collective-permute-done.1.refs_2_ = bf16[32,4,16,128]{3,2,1,0:T(8,128)(2,1)S(1)} collective-permute-done((bf16[32,4,16,128]{3,2,1,0:T(8,128)(2,1)S(1)}, bf16[32,4,16,128]{3,2,1,0:T(8,128)(2,1)S(1)}, u32[]{:S(2)}, u32[]{:S(2)}) %collective-permute-start.1) | collective-permute-done | bytes 524320 | tf_op jit(solution)/shard_map/ppermute | solution.py:397
  29.3 0.2 collective-permute-done.2.refs_2_
  29.5 7.4 %shard_map.49 = (bf16[32,2,16,128]{3,2,1,0:T(8,128)(2,1)S(1)}, bf16[32,2,16,128]{3,2,1,0:T(8,128)(2,1)}) custom-call(s32[2]{0:T(128)S(1)} %pad_add_fusion.place, bf16[8,32,64,128]{3,2,1,0:T(8,128)(2,1)S(1)} %get-tuple-element.30.refs_0_.refs_1_, bf16[8,32,64,128]{3,2,1,0:T(8,128)(2,1)S(1)} %get-tuple-element.30.refs_0_.refs_1_, ...), custom_call_target="tpu_custom_call" | custom-call | flops 1000000 | tf_op jit(solution)/shard_map/pallas_call | solution.py:263
  36.9 2.6 %collective-permute-done.refs_0_ = bf16[32,4,16,128]{3,2,1,0:T(8,128)(2,1)S(1)} collective-permute-done((bf16[32,4,16,128]{3,2,1,0:T(8,128)(2,1)S(1)}, bf16[32,4,16,128]{3,2,1,0:T(8,128)(2,1)S(1)}, u32[]{:S(2)}, u32[]{:S(2)}) %collective-permute-start) | collective-permute-done | bytes 524320 | tf_op jit(solution)/shard_map/ppermute | solution.py:423
  39.6 0.0 collective-permute-start.5
  39.6 1.3 %collective-permute-start.3 = (bf16[32,4,16,128]{3,2,1,0:T(8,128)(2,1)}, bf16[32,4,16,128]{3,2,1,0:T(8,128)(2,1)}, u32[]{:S(2)}, u32[]{:S(2)}) collective-permute-start(bf16[32,4,16,128]{3,2,1,0:T(8,128)(2,1)} %get-tuple-element.45), channel_id=1, source_target_pairs={{0,1},{2,3},{4,5},{6,7},{8,9},{10,11},{12,13},{14,15},{16,17},{18,... | collective-permute-start | bytes 1572872 | tf_op jit(solution)/shard_map/ppermute | solution.py:438
  40.9 3.4 %collective-permute-start.4 = (bf16[32,2,16,128]{3,2,1,0:T(8,128)(2,1)}, bf16[32,2,16,128]{3,2,1,0:T(8,128)(2,1)}, u32[]{:S(2)}, u32[]{:S(2)}) collective-permute-start(bf16[32,2,16,128]{3,2,1,0:T(8,128)(2,1)} %get-tuple-element.46), channel_id=1, source_target_pairs={{0,1},{1,0},{2,3},{3,2},{4,5},{5,4},{6,7},{7,6},{8,9},{9,8},{10,11... | collective-permute-start | bytes 786440 | tf_op jit(solution)/shard_map/ppermute | solution.py:439
  44.3 1.5 %collective-permute-start.11 = (bf16[32,4,16,128]{3,2,1,0:T(8,128)(2,1)S(1)}, bf16[32,4,16,128]{3,2,1,0:T(8,128)(2,1)}, u32[]{:S(2)}, u32[]{:S(2)}) collective-permute-start(bf16[32,4,16,128]{3,2,1,0:T(8,128)(2,1)S(1)} %collective-permute-done.refs_0_), channel_id=1, source_target_pairs={{0,4},{2,6},{4,8},{6,10},{8,12},{10,14},{12,16},{14,18},{16,20},{1... | collective-permute-start | bytes 1572872 | tf_op jit(solution)/shard_map/ppermute | solution.py:397
  45.9 0.0 collective-permute-done.6.refs_3_
  45.9 0.0 collective-permute-start.13
  45.9 0.0 collective-permute-done.5.refs_1_
  45.9 2.7 %shard_map.50.refs_4_ = f32[4096,128]{1,0:T(8,128)S(1)} custom-call(s32[2]{0:T(128)S(1)} %pad_add_fusion.place, bf16[32,4,16,128]{3,2,1,0:T(8,128)(2,1)S(1)} %get-tuple-element.36.refs_0_, bf16[32,4,16,128]{3,2,1,0:T(8,128)(2,1)S(1)} %collective-permute-done.5.refs_1_, bf16[32,4,16,128]{3,2,1,0:T(8,128)(2,1)S(1)} %collective-permute-done.1.refs_2_, ...), custom_call_target="tpu_custom_call" | custom-call | flops 1000 | tf_op jit(solution)/shard_map/pallas_call | solution.py:369
  48.6 13.1 %collective-permute-done.4 = bf16[32,2,16,128]{3,2,1,0:T(8,128)(2,1)} collective-permute-done((bf16[32,2,16,128]{3,2,1,0:T(8,128)(2,1)}, bf16[32,2,16,128]{3,2,1,0:T(8,128)(2,1)}, u32[]{:S(2)}, u32[]{:S(2)}) %collective-permute-start.4) | collective-permute-done | bytes 262176 | tf_op jit(solution)/shard_map/ppermute | solution.py:439
  61.7 0.0 collective-permute-done.3
  61.7 1.1 %broadcast_select_fusion.refs_0_ = bf16[32,4,16,128]{3,2,1,0:T(8,128)(2,1)S(1)} fusion(bf16[32,4,16,128]{3,2,1,0:T(8,128)(2,1)S(1)} %get-tuple-element.38, bf16[32,4,16,128]{3,2,1,0:T(8,128)(2,1)} %collective-permute-done.3, pred[]{:T(512)S(6)} %eq.5), kind=kLoop, calls=%fused_computation | loop fusion | flops 262144 | bytes 1572865 | tf_op jit(solution)/shard_map/jit(_where)/select_n | solution.py:444
  62.9 1.6 %collective-permute-start.8 = (bf16[32,4,16,128]{3,2,1,0:T(8,128)(2,1)S(1)}, bf16[32,4,16,128]{3,2,1,0:T(8,128)(2,1)S(1)}, u32[]{:S(2)}, u32[]{:S(2)}) collective-permute-start(bf16[32,4,16,128]{3,2,1,0:T(8,128)(2,1)S(1)} %broadcast_select_fusion.refs_0_), channel_id=1, source_target_pairs={{0,4},{2,6},{4,8},{6,10},{8,12},{10,14},{12,16},{14,18},{16,20},{1... | collective-permute-start | bytes 1572872 | tf_op jit(solution)/shard_map/ppermute | solution.py:397
  64.5 0.0 collective-permute-done.11.refs_2_
  64.5 0.0 collective-permute-start.12
  64.5 0.6 collective-permute-start.10
  65.0 1.0 constant_dynamic-update-slice_fusion.refs_0_
  66.0 1.5 %collective-permute-start.7 = (bf16[32,4,16,128]{3,2,1,0:T(8,128)(2,1)S(1)}, bf16[32,4,16,128]{3,2,1,0:T(8,128)(2,1)S(1)}, u32[]{:S(2)}, u32[]{:S(2)}) collective-permute-start(bf16[32,4,16,128]{3,2,1,0:T(8,128)(2,1)S(1)} %constant_dynamic-update-slice_fusion.refs_0_), channel_id=1, source_target_pairs={{0,4},{2,6},{4,8},{6,10},{8,12},{10,14},{12,16},{14,18},{16,20},{1... | collective-permute-start | bytes 1572872 | tf_op jit(solution)/shard_map/ppermute | solution.py:397
  67.6 0.0 collective-permute-done.13.refs_3_
  67.6 0.9 collective-permute-start.15
  68.5 9.2 %collective-permute-done.8.refs_2_ = bf16[32,4,16,128]{3,2,1,0:T(8,128)(2,1)S(1)} collective-permute-done((bf16[32,4,16,128]{3,2,1,0:T(8,128)(2,1)S(1)}, bf16[32,4,16,128]{3,2,1,0:T(8,128)(2,1)S(1)}, u32[]{:S(2)}, u32[]{:S(2)}) %collective-permute-start.8) | collective-permute-done | bytes 524320 | tf_op jit(solution)/shard_map/ppermute | solution.py:397
  77.7 0.0 collective-permute-start.9
  77.7 0.0 collective-permute-done.12.refs_1_
  77.7 5.0 %shard_map.51.refs_4_ = f32[4096,128]{1,0:T(8,128)S(1)} custom-call(s32[2]{0:T(128)S(1)} %pad_add_fusion.place, bf16[32,4,16,128]{3,2,1,0:T(8,128)(2,1)S(1)} %collective-permute-done.refs_0_, bf16[32,4,16,128]{3,2,1,0:T(8,128)(2,1)S(1)} %collective-permute-done.12.refs_1_, ...), custom_call_target="tpu_custom_call", output_to_operand_aliasing={{}: (5, {})} | custom-call | flops 6000000000 | tf_op jit(solution)/shard_map/pallas_call | solution.py:369
  82.7 6.1 %collective-permute-done.10.refs_3_ = bf16[32,4,16,128]{3,2,1,0:T(8,128)(2,1)S(1)} collective-permute-done((bf16[32,4,16,128]{3,2,1,0:T(8,128)(2,1)S(1)}, bf16[32,4,16,128]{3,2,1,0:T(8,128)(2,1)S(1)}, u32[]{:S(2)}, u32[]{:S(2)}) %collective-permute-start.10) | collective-permute-done | bytes 524320 | tf_op jit(solution)/shard_map/ppermute | solution.py:402
  88.8 0.0 collective-permute-done.9.refs_1_
  88.8 4.0 %shard_map.52.refs_4_ = f32[4096,128]{1,0:T(8,128)S(1)} custom-call(s32[2]{0:T(128)S(1)} %pad_add_fusion.place, bf16[32,4,16,128]{3,2,1,0:T(8,128)(2,1)S(1)} %broadcast_select_fusion.refs_0_, bf16[32,4,16,128]{3,2,1,0:T(8,128)(2,1)S(1)} %collective-permute-done.9.refs_1_, ...), custom_call_target="tpu_custom_call", output_to_operand_aliasing={{}: (5, {})} | custom-call | flops 1000 | tf_op jit(solution)/shard_map/pallas_call | solution.py:369
  92.8 0.0 collective-permute-done.7.refs_2_
  92.8 0.1 collective-permute-start.14
  92.9 8.4 %collective-permute-done.15.refs_3_ = bf16[32,4,16,128]{3,2,1,0:T(8,128)(2,1)S(1)} collective-permute-done((bf16[32,4,16,128]{3,2,1,0:T(8,128)(2,1)S(1)}, bf16[32,4,16,128]{3,2,1,0:T(8,128)(2,1)S(1)}, u32[]{:S(2)}, u32[]{:S(2)}) %collective-permute-start.15) | collective-permute-done | bytes 524320 | tf_op jit(solution)/shard_map/ppermute | solution.py:402
  101.3 0.0 collective-permute-done.14.refs_1_
  101.3 7.9 %shard_map.53 = f32[2,8,4,8,8,128]{5,4,3,2,1,0:T(8,128)} custom-call(s32[2]{0:T(128)S(1)} %pad_add_fusion.place, bf16[32,4,16,128]{3,2,1,0:T(8,128)(2,1)S(1)} %constant_dynamic-update-slice_fusion.refs_0_, bf16[32,4,16,128]{3,2,1,0:T(8,128)(2,1)S(1)} %collective-permute-done.14.refs_1_, bf16[32,4,16,128]{3,2,1,0:T(8,128)(2,1)S(1)} %collective-permute-done.7.refs_2_, ...), custom_call_target="tpu_custom_call" | custom-call | flops 1000 | tf_op jit(solution)/shard_map/pallas_call | solution.py:369
  (1 shorter events, 0.0 us)
Async XLA Ops:
  3.4 26.1 %collective-permute-start.2 = (bf16[8,8,64,128]{3,2,1,0:T(8,128)(2,1)S(1)}, bf16[8,8,64,128]{3,2,1,0:T(8,128)(2,1)S(1)}, u32[]{:S(2)}, u32[]{:S(2)}) collective-permute-start(bf16[8,8,64,128]{3,2,1,0:T(8,128)(2,1)S(1)} %get-tuple-element.40), channel_id=1, source_target_pairs={{0,1},{1,0},{2,3},{3,2},{4,5},{5,4},{6,7},{7,6},{8,9},{9,8},{10,11... | collective-permute-start | bytes 3145736 | tf_op jit(solution)/shard_map/ppermute | solution.py:419
  15.3 14.0 %collective-permute-start.1 = (bf16[32,4,16,128]{3,2,1,0:T(8,128)(2,1)S(1)}, bf16[32,4,16,128]{3,2,1,0:T(8,128)(2,1)S(1)}, u32[]{:S(2)}, u32[]{:S(2)}) collective-permute-start(bf16[32,4,16,128]{3,2,1,0:T(8,128)(2,1)S(1)} %get-tuple-element.36.refs_0_), channel_id=1, source_target_pairs={{0,4},{2,6},{4,8},{6,10},{8,12},{10,14},{12,16},{14,18},{16,20},{1... | collective-permute-start | bytes 1572872 | tf_op jit(solution)/shard_map/ppermute | solution.py:397
  16.9 22.7 %collective-permute-start = (bf16[32,4,16,128]{3,2,1,0:T(8,128)(2,1)S(1)}, bf16[32,4,16,128]{3,2,1,0:T(8,128)(2,1)S(1)}, u32[]{:S(2)}, u32[]{:S(2)}) collective-permute-start(bf16[32,4,16,128]{3,2,1,0:T(8,128)(2,1)S(1)} %get-tuple-element.35), channel_id=1, source_target_pairs={{0,1},{1,0},{2,3},{3,2},{4,5},{5,4},{6,7},{7,6},{8,9},{9,8},{10,11... | collective-permute-start | bytes 1572872 | tf_op jit(solution)/shard_map/ppermute | solution.py:423
  18.4 27.4 %collective-permute-start.6 = (bf16[32,4,16,128]{3,2,1,0:T(8,128)(2,1)S(1)}, bf16[32,4,16,128]{3,2,1,0:T(8,128)(2,1)S(1)}, u32[]{:S(2)}, u32[]{:S(2)}) collective-permute-start(bf16[32,4,16,128]{3,2,1,0:T(8,128)(2,1)S(1)} %get-tuple-element.36.refs_0_), channel_id=1, source_target_pairs={{0,2},{2,8},{4,6},{6,12},{8,10},{10,16},{12,14},{14,20},{16,18},{1... | collective-permute-start | bytes 1572872 | tf_op jit(solution)/shard_map/ppermute | solution.py:402
  39.6 6.3 %collective-permute-start.5 = (bf16[32,4,16,128]{3,2,1,0:T(8,128)(2,1)S(1)}, bf16[32,4,16,128]{3,2,1,0:T(8,128)(2,1)S(1)}, u32[]{:S(2)}, u32[]{:S(2)}) collective-permute-start(bf16[32,4,16,128]{3,2,1,0:T(8,128)(2,1)S(1)} %collective-permute-done.1.refs_2_), channel_id=1, source_target_pairs={{0,2},{2,0},{4,6},{6,4},{8,10},{10,8},{12,14},{14,12},{16,18},{18,... | collective-permute-start | bytes 1572872 | tf_op jit(solution)/shard_map/ppermute | solution.py:407
  39.6 22.2 %collective-permute-start.3 = (bf16[32,4,16,128]{3,2,1,0:T(8,128)(2,1)}, bf16[32,4,16,128]{3,2,1,0:T(8,128)(2,1)}, u32[]{:S(2)}, u32[]{:S(2)}) collective-permute-start(bf16[32,4,16,128]{3,2,1,0:T(8,128)(2,1)} %get-tuple-element.45), channel_id=1, source_target_pairs={{0,1},{2,3},{4,5},{6,7},{8,9},{10,11},{12,13},{14,15},{16,17},{18,... | collective-permute-start | bytes 1572872 | tf_op jit(solution)/shard_map/ppermute | solution.py:438
  40.9 20.9 %collective-permute-start.4 = (bf16[32,2,16,128]{3,2,1,0:T(8,128)(2,1)}, bf16[32,2,16,128]{3,2,1,0:T(8,128)(2,1)}, u32[]{:S(2)}, u32[]{:S(2)}) collective-permute-start(bf16[32,2,16,128]{3,2,1,0:T(8,128)(2,1)} %get-tuple-element.46), channel_id=1, source_target_pairs={{0,1},{1,0},{2,3},{3,2},{4,5},{5,4},{6,7},{7,6},{8,9},{9,8},{10,11... | collective-permute-start | bytes 786440 | tf_op jit(solution)/shard_map/ppermute | solution.py:439
  44.3 20.2 %collective-permute-start.11 = (bf16[32,4,16,128]{3,2,1,0:T(8,128)(2,1)S(1)}, bf16[32,4,16,128]{3,2,1,0:T(8,128)(2,1)}, u32[]{:S(2)}, u32[]{:S(2)}) collective-permute-start(bf16[32,4,16,128]{3,2,1,0:T(8,128)(2,1)S(1)} %collective-permute-done.refs_0_), channel_id=1, source_target_pairs={{0,4},{2,6},{4,8},{6,10},{8,12},{10,14},{12,16},{14,18},{16,20},{1... | collective-permute-start | bytes 1572872 | tf_op jit(solution)/shard_map/ppermute | solution.py:397
  45.9 21.7 %collective-permute-start.13 = (bf16[32,4,16,128]{3,2,1,0:T(8,128)(2,1)S(1)}, bf16[32,4,16,128]{3,2,1,0:T(8,128)(2,1)S(1)}, u32[]{:S(2)}, u32[]{:S(2)}) collective-permute-start(bf16[32,4,16,128]{3,2,1,0:T(8,128)(2,1)S(1)} %collective-permute-done.refs_0_), channel_id=1, source_target_pairs={{0,2},{2,8},{4,6},{6,12},{8,10},{10,16},{12,14},{14,20},{16,18},{1... | collective-permute-start | bytes 1572872 | tf_op jit(solution)/shard_map/ppermute | solution.py:402
  62.9 14.9 %collective-permute-start.8 = (bf16[32,4,16,128]{3,2,1,0:T(8,128)(2,1)S(1)}, bf16[32,4,16,128]{3,2,1,0:T(8,128)(2,1)S(1)}, u32[]{:S(2)}, u32[]{:S(2)}) collective-permute-start(bf16[32,4,16,128]{3,2,1,0:T(8,128)(2,1)S(1)} %broadcast_select_fusion.refs_0_), channel_id=1, source_target_pairs={{0,4},{2,6},{4,8},{6,10},{8,12},{10,14},{12,16},{14,18},{16,20},{1... | collective-permute-start | bytes 1572872 | tf_op jit(solution)/shard_map/ppermute | solution.py:397
  64.5 13.3 %collective-permute-start.12 = (bf16[32,4,16,128]{3,2,1,0:T(8,128)(2,1)}, bf16[32,4,16,128]{3,2,1,0:T(8,128)(2,1)S(1)}, u32[]{:S(2)}, u32[]{:S(2)}) collective-permute-start(bf16[32,4,16,128]{3,2,1,0:T(8,128)(2,1)} %collective-permute-done.11.refs_2_), channel_id=1, source_target_pairs={{0,2},{2,0},{4,6},{6,4},{8,10},{10,8},{12,14},{14,12},{16,18},{18,... | collective-permute-start | bytes 1572872 | tf_op jit(solution)/shard_map/ppermute | solution.py:407
  64.5 24.3 %collective-permute-start.10 = (bf16[32,4,16,128]{3,2,1,0:T(8,128)(2,1)S(1)}, bf16[32,4,16,128]{3,2,1,0:T(8,128)(2,1)S(1)}, u32[]{:S(2)}, u32[]{:S(2)}) collective-permute-start(bf16[32,4,16,128]{3,2,1,0:T(8,128)(2,1)S(1)} %broadcast_select_fusion.refs_0_), channel_id=1, source_target_pairs={{0,2},{2,8},{4,6},{6,12},{8,10},{10,16},{12,14},{14,20},{16,18},{1... | collective-permute-start | bytes 1572872 | tf_op jit(solution)/shard_map/ppermute | solution.py:402
  66.0 26.7 %collective-permute-start.7 = (bf16[32,4,16,128]{3,2,1,0:T(8,128)(2,1)S(1)}, bf16[32,4,16,128]{3,2,1,0:T(8,128)(2,1)S(1)}, u32[]{:S(2)}, u32[]{:S(2)}) collective-permute-start(bf16[32,4,16,128]{3,2,1,0:T(8,128)(2,1)S(1)} %constant_dynamic-update-slice_fusion.refs_0_), channel_id=1, source_target_pairs={{0,4},{2,6},{4,8},{6,10},{8,12},{10,14},{12,16},{14,18},{16,20},{1... | collective-permute-start | bytes 1572872 | tf_op jit(solution)/shard_map/ppermute | solution.py:397
  67.6 33.7 %collective-permute-start.15 = (bf16[32,4,16,128]{3,2,1,0:T(8,128)(2,1)S(1)}, bf16[32,4,16,128]{3,2,1,0:T(8,128)(2,1)S(1)}, u32[]{:S(2)}, u32[]{:S(2)}) collective-permute-start(bf16[32,4,16,128]{3,2,1,0:T(8,128)(2,1)S(1)} %constant_dynamic-update-slice_fusion.refs_0_), channel_id=1, source_target_pairs={{0,2},{2,8},{4,6},{6,12},{8,10},{10,16},{12,14},{14,20},{16,18},{1... | collective-permute-start | bytes 1572872 | tf_op jit(solution)/shard_map/ppermute | solution.py:402
  77.7 11.1 %collective-permute-start.9 = (bf16[32,4,16,128]{3,2,1,0:T(8,128)(2,1)S(1)}, bf16[32,4,16,128]{3,2,1,0:T(8,128)(2,1)S(1)}, u32[]{:S(2)}, u32[]{:S(2)}) collective-permute-start(bf16[32,4,16,128]{3,2,1,0:T(8,128)(2,1)S(1)} %collective-permute-done.8.refs_2_), channel_id=1, source_target_pairs={{0,2},{2,0},{4,6},{6,4},{8,10},{10,8},{12,14},{14,12},{16,18},{18,... | collective-permute-start | bytes 1572872 | tf_op jit(solution)/shard_map/ppermute | solution.py:407
  92.8 8.5 %collective-permute-start.14 = (bf16[32,4,16,128]{3,2,1,0:T(8,128)(2,1)S(1)}, bf16[32,4,16,128]{3,2,1,0:T(8,128)(2,1)S(1)}, u32[]{:S(2)}, u32[]{:S(2)}) collective-permute-start(bf16[32,4,16,128]{3,2,1,0:T(8,128)(2,1)S(1)} %collective-permute-done.7.refs_2_), channel_id=1, source_target_pairs={{0,2},{2,0},{4,6},{6,4},{8,10},{10,8},{12,14},{14,12},{16,18},{18,... | collective-permute-start | bytes 1572872 | tf_op jit(solution)/shard_map/ppermute | solution.py:407

commit v12 on v9

--- a/solution.py
+++ b/solution.py
@@ -403,6 +403,16 @@
     return shifted(block, "stn", 2), rest
 
 
+def evenly(block):
+    size = lax.axis_size("stn")
+    rest = lax.ppermute(block, "stn", [(i, (i + 1 if i % 2 == 0 else i + 3) % size) for i in range(size)])
+    return lax.ppermute(block, "stn", [(i, (i + 2) % size) for i in range(size) if i % 4 < 3]), rest
+
+
+def relayed(rest):
+    return lax.ppermute(rest, "stn", [(i, i - 1) for i in range(lax.axis_size("stn")) if i % 4 == 2])
+
+
 def exchanged(block):
     return lax.ppermute(block, "stn", [(i, i ^ 1) for i in range(lax.axis_size("stn"))])
 
@@ -439,12 +449,13 @@
     pair_g = exchanged(two_g)
     own_c = after(own_c, two_g, pair_a, rest_a)
     rest = jnp.concatenate([jnp.where(me == 0, own_b, got_b), own_c, got_c], axis=1)
-    two_r, rest_r = farther(rest)
+    two_r, rest_r = evenly(rest)
     many, few = own_a.shape[1], own_c.shape[1]
     sums = correlated(
         [own_a, pair_a, two_a, rest_a, got_a, pair_g, two_g, rest_g], [(many, [(0, 0, 0), (1, 0, 0)])], None, False
     )
-    pair_r = exchanged(after(two_r, sums))
+    two_r = two_r + relayed(after(rest_r, sums))
+    pair_r = exchanged(two_r)
     return correlated(
         [rest, pair_r, two_r, rest_r], [(many, [(0, 0, 0)]), (few, [(0, 0, many), (0, 0, many + few)])], sums, True
     )

time: 109 us -> 115 us (1.055)
  the two profiles are of different devices: /device:TPU:6 before, /device:TPU:1 now
where the time goes in v12:
time: 115 us; the launch traced here: 114 us
  Pallas kernels  49.6 us (43%)
  waiting for transfers between devices  37.1 us (32%)
  starting transfers between devices  24.8 us (22%)
  local copies, waits for them, and re-layouts  2.19 us (2%)
    pallas_call x3, Pallas kernels, spectra(): pl.pallas_call(functools.partial(spectra_kernel, groups, tuple((part[1:]...  30.9 us
    pallas_call x2, Pallas kernels, correlate(): pl.pallas_call(functools.partial(correlate_kernel, pieces, per_group, sca...  15.4 us
    ppermute x1, waiting for transfers between devices, relayed(): lax.ppermute(rest, 'stn', [(i, i - 1) for i in range(lax.axis_size('stn')...  12.6 us
    ppermute x1, waiting for transfers between devices, evenly(): lax.ppermute(block, 'stn', [(i, (i + 2) % size) for i in range(size) if i...  12.6 us
    ppermute x3, starting transfers between devices, exchanged(): lax.ppermute(block, 'stn', [(i, i ^ 1) for i in range(lax.axis_size('stn'...  5.91 us
    ppermute x2, starting transfers between devices, farther(): lax.ppermute(block, 'stn', [(i, (i + 1 if i % 2 == 0 else i + 3) % size)...  3.88 us
    ppermute x1, waiting for transfers between devices, paired(): got_a = lax.ppermute(away_a, 'tm', swap)  3.76 us
    pallas_call x1, Pallas kernels, prepare(): pl.pallas_call(functools.partial(prepare_kernel, edge_block, int(groups =...  3.29 us
  transfers between devices with their start and end apart: 14, of which 6 were waited for; matrix products, arithmetic and copies ran while one was open for 0% of the time, Pallas kernels for 32%

profile of v12, /device:TPU:1, one launch (start us, length us, event | category | flops | bytes accessed | tf_op | source)
XLA Modules:
  0.0 114.4 jit_solution(10180896619379940277)
XLA Ops:
  0.0 0.1 pad_add_fusion.place
  0.1 3.3 %shard_map.46 = (bf16[8,32,64,128]{3,2,1,0:T(8,128)(2,1)S(1)}, bf16[8,8,64,128]{3,2,1,0:T(8,128)(2,1)S(1)}, f32[1024,128]{1,0:T(8,128)S(1)}, bf16[64,192]{1,0:T(...) custom-call(s32[2]{0:T(128)S(1)} %pad_add_fusion.place, bf16[8,32,64,128]{3,2,1,0:T(8,128)(2,1)} %bitcast.10, ...), custom_call_target="tpu_custom_call" | custom-call | tf_op jit(solution)/shard_map/pallas_call | solution.py:110
  3.4 0.0 copy-start
  3.4 2.1 %collective-permute-start.3 = (bf16[8,8,64,128]{3,2,1,0:T(8,128)(2,1)S(1)}, bf16[8,8,64,128]{3,2,1,0:T(8,128)(2,1)S(1)}, u32[]{:S(2)}, u32[]{:S(2)}) collective-permute-start(bf16[8,8,64,128]{3,2,1,0:T(8,128)(2,1)S(1)} %get-tuple-element.32), channel_id=1, source_target_pairs={{0,1},{1,0},{2,3},{3,2},{4,5},{5,4},{6,7},{7,6},{8,9},{9,8},{10,11... | collective-permute-start | bytes 3145736 | tf_op jit(solution)/shard_map/ppermute | solution.py:428
  5.5 12.2 %shard_map.47 = (bf16[32,4,16,128]{3,2,1,0:T(8,128)(2,1)}, bf16[32,4,16,128]{3,2,1,0:T(8,128)(2,1)}) custom-call(s32[2]{0:T(128)S(1)} %pad_add_fusion.place, bf16[8,32,64,128]{3,2,1,0:T(8,128)(2,1)S(1)} %get-tuple-element.21.refs_0_.refs_1_, bf16[8,32,64,128]{3,2,1,0:T(8,128)(2,1)S(1)} %get-tuple-element.21.refs_0_.refs_1_, ...), custom_call_target="tpu_custom_call" | custom-call | flops 1000000 | tf_op jit(solution)/shard_map/pallas_call | solution.py:263
  17.7 1.2 %collective-permute-start.1 = (bf16[32,4,16,128]{3,2,1,0:T(8,128)(2,1)}, bf16[32,4,16,128]{3,2,1,0:T(8,128)(2,1)}, u32[]{:S(2)}, u32[]{:S(2)}) collective-permute-start(bf16[32,4,16,128]{3,2,1,0:T(8,128)(2,1)} %get-tuple-element.26.refs_0_), channel_id=1, source_target_pairs={{0,4},{2,6},{4,8},{6,10},{8,12},{10,14},{12,16},{14,18},{16,20},{1... | collective-permute-start | bytes 1572872 | tf_op jit(solution)/shard_map/ppermute | solution.py:397
  19.0 0.3 collective-permute-start.2
  19.2 2.7 %collective-permute-start.6 = (bf16[32,4,16,128]{3,2,1,0:T(8,128)(2,1)}, bf16[32,4,16,128]{3,2,1,0:T(8,128)(2,1)}, u32[]{:S(2)}, u32[]{:S(2)}) collective-permute-start(bf16[32,4,16,128]{3,2,1,0:T(8,128)(2,1)} %get-tuple-element.26.refs_0_), channel_id=1, source_target_pairs={{0,2},{2,8},{4,6},{6,12},{8,10},{10,16},{12,14},{14,20},{16,18},{1... | collective-permute-start | bytes 1572872 | tf_op jit(solution)/shard_map/ppermute | solution.py:402
  21.9 0.0 copy-done
  21.9 12.0 %shard_map.48 = (bf16[32,4,16,128]{3,2,1,0:T(8,128)(2,1)S(1)}, bf16[32,4,16,128]{3,2,1,0:T(8,128)(2,1)}) custom-call(s32[2]{0:T(128)S(1)} %pad_add_fusion.place, bf16[8,32,64,128]{3,2,1,0:T(8,128)(2,1)S(1)} %get-tuple-element.21.refs_0_.refs_1_, bf16[8,32,64,128]{3,2,1,0:T(8,128)(2,1)S(1)} %get-tuple-element.21.refs_0_.refs_1_, ...), custom_call_target="tpu_custom_call" | custom-call | flops 1000000 | tf_op jit(solution)/shard_map/pallas_call | solution.py:263
  33.9 2.1 %collective-permute-start = (bf16[32,4,16,128]{3,2,1,0:T(8,128)(2,1)}, bf16[32,4,16,128]{3,2,1,0:T(8,128)(2,1)}, u32[]{:S(2)}, u32[]{:S(2)}) collective-permute-start(bf16[32,4,16,128]{3,2,1,0:T(8,128)(2,1)} %get-tuple-element.29), channel_id=1, source_target_pairs={{0,1},{2,3},{4,5},{6,7},{8,9},{10,11},{12,13},{14,15},{16,17},{18,... | collective-permute-start | bytes 1572872 | tf_op jit(solution)/shard_map/ppermute | solution.py:437
  36.0 0.0 collective-permute-done.1.refs_2_
  36.0 3.8 %collective-permute-done.2.refs_4_ = bf16[32,4,16,128]{3,2,1,0:T(8,128)(2,1)} collective-permute-done((bf16[32,4,16,128]{3,2,1,0:T(8,128)(2,1)}, bf16[32,4,16,128]{3,2,1,0:T(8,128)(2,1)}, u32[]{:S(2)}, u32[]{:S(2)}) %collective-permute-start.2) | collective-permute-done | bytes 524320 | tf_op jit(solution)/shard_map/ppermute | solution.py:432
  39.7 1.1 collective-permute-start.4
  40.9 2.0 %collective-permute-start.5 = (bf16[32,4,16,128]{3,2,1,0:T(8,128)(2,1)}, bf16[32,4,16,128]{3,2,1,0:T(8,128)(2,1)S(1)}, u32[]{:S(2)}, u32[]{:S(2)}) collective-permute-start(bf16[32,4,16,128]{3,2,1,0:T(8,128)(2,1)} %collective-permute-done.1.refs_2_), channel_id=1, source_target_pairs={{0,2},{2,0},{4,6},{6,4},{8,10},{10,8},{12,14},{14,12},{16,18},{18,... | collective-permute-start | bytes 1572872 | tf_op jit(solution)/shard_map/ppermute | solution.py:417
  42.9 0.0 collective-permute-done.3.refs_2_
  42.9 1.2 %collective-permute-start.11 = (bf16[32,4,16,128]{3,2,1,0:T(8,128)(2,1)}, bf16[32,4,16,128]{3,2,1,0:T(8,128)(2,1)S(1)}, u32[]{:S(2)}, u32[]{:S(2)}) collective-permute-start(bf16[32,4,16,128]{3,2,1,0:T(8,128)(2,1)} %collective-permute-done.2.refs_4_), channel_id=1, source_target_pairs={{0,2},{2,8},{4,6},{6,12},{8,10},{10,16},{12,14},{14,20},{16,18},{1... | collective-permute-start | bytes 1572872 | tf_op jit(solution)/shard_map/ppermute | solution.py:402
  44.1 0.0 copy-start.1
  44.1 2.2 %copy-done.1 = bf16[8,32,64,128]{3,2,1,0:T(8,128)(2,1)S(1)} copy-done((bf16[8,32,64,128]{3,2,1,0:T(8,128)(2,1)S(1)}, bf16[8,32,64,128]{3,2,1,0:T(8,128)(2,1)}, u32[]{:S(2)}) %copy-start.1) | copy-done | bytes 4194328
  46.2 6.7 %shard_map.49 = (bf16[32,2,16,128]{3,2,1,0:T(8,128)(2,1)S(1)}, bf16[32,2,16,128]{3,2,1,0:T(8,128)(2,1)S(1)}) custom-call(s32[2]{0:T(128)S(1)} %pad_add_fusion.place, bf16[8,32,64,128]{3,2,1,0:T(8,128)(2,1)S(1)} %copy-done.1, bf16[8,32,64,128]{3,2,1,0:T(8,128)(2,1)S(1)} %copy-done.1, bf16[8,8,64,128]{3,2,1,0:T(8,128)(2,1)S(1)} %collective-permute-done.3.refs_2_, ...), custom_call_target="tpu_custom_call" | custom-call | flops 8999999488 | tf_op jit(solution)/shard_map/pallas_call | solution.py:263
  53.0 0.0 collective-permute-done
  53.0 2.3 %collective-permute-start.7 = (bf16[32,2,16,128]{3,2,1,0:T(8,128)(2,1)S(1)}, bf16[32,2,16,128]{3,2,1,0:T(8,128)(2,1)S(1)}, u32[]{:S(2)}, u32[]{:S(2)}) collective-permute-start(bf16[32,2,16,128]{3,2,1,0:T(8,128)(2,1)S(1)} %get-tuple-element.35), channel_id=1, source_target_pairs={{0,1},{1,0},{2,3},{3,2},{4,5},{5,4},{6,7},{7,6},{8,9},{9,8},{10,11... | collective-permute-start | bytes 786440 | tf_op jit(solution)/shard_map/ppermute | solution.py:447
  55.2 0.1 broadcast_select_fusion
  55.3 0.0 collective-permute-done.6.refs_3_
  55.3 0.0 collective-permute-done.4.refs_6_
  55.3 0.0 collective-permute-done.5.refs_1_
  55.3 3.8 %collective-permute-start.10 = (bf16[32,4,16,128]{3,2,1,0:T(8,128)(2,1)S(1)}, bf16[32,4,16,128]{3,2,1,0:T(8,128)(2,1)S(1)}, u32[]{:S(2)}, u32[]{:S(2)}) collective-permute-start(bf16[32,4,16,128]{3,2,1,0:T(8,128)(2,1)S(1)} %collective-permute-done.4.refs_6_), channel_id=1, source_target_pairs={{0,2},{2,0},{4,6},{6,4},{8,10},{10,8},{12,14},{14,12},{16,18},{18,... | collective-permute-start | bytes 1572872 | tf_op jit(solution)/shard_map/ppermute | solution.py:417
  59.1 2.2 %collective-permute-done.7 = bf16[32,2,16,128]{3,2,1,0:T(8,128)(2,1)S(1)} collective-permute-done((bf16[32,2,16,128]{3,2,1,0:T(8,128)(2,1)S(1)}, bf16[32,2,16,128]{3,2,1,0:T(8,128)(2,1)S(1)}, u32[]{:S(2)}, u32[]{:S(2)}) %collective-permute-start.7) | collective-permute-done | bytes 262176 | tf_op jit(solution)/shard_map/ppermute | solution.py:447
  61.3 0.1 pad_maximum_fusion.refs_0_
  61.4 1.5 %collective-permute-start.9 = (bf16[32,8,16,128]{3,2,1,0:T(8,128)(2,1)S(1)}, bf16[32,8,16,128]{3,2,1,0:T(8,128)(2,1)S(1)}, u32[]{:S(2)}, u32[]{:S(2)}) collective-permute-start(bf16[32,8,16,128]{3,2,1,0:T(8,128)(2,1)S(1)} %pad_maximum_fusion.refs_0_), channel_id=1, source_target_pairs={{0,2},{2,8},{4,6},{6,12},{8,10},{10,16},{12,14},{14,20},{16,18},{1... | collective-permute-start | bytes 3145736 | tf_op jit(solution)/shard_map/ppermute | solution.py:408
  62.9 3.2 %collective-permute-start.8 = (bf16[32,8,16,128]{3,2,1,0:T(8,128)(2,1)S(1)}, bf16[32,8,16,128]{3,2,1,0:T(8,128)(2,1)S(1)}, u32[]{:S(2)}, u32[]{:S(2)}) collective-permute-start(bf16[32,8,16,128]{3,2,1,0:T(8,128)(2,1)S(1)} %pad_maximum_fusion.refs_0_), channel_id=1, source_target_pairs={{0,4},{2,6},{4,8},{8,12},{10,14},{12,16},{16,20},{18,22},{20,24},{... | collective-permute-start | bytes 3145736 | tf_op jit(solution)/shard_map/ppermute | solution.py:409
  66.2 0.0 collective-permute-done.11.refs_7_
  66.2 0.0 collective-permute-done.10.refs_5_
  66.2 5.3 %shard_map.50.refs_4_ = f32[4096,128]{1,0:T(8,128)S(1)} custom-call(s32[2]{0:T(128)S(1)} %pad_add_fusion.place, bf16[32,4,16,128]{3,2,1,0:T(8,128)(2,1)} %get-tuple-element.26.refs_0_, bf16[32,4,16,128]{3,2,1,0:T(8,128)(2,1)S(1)} %collective-permute-done.5.refs_1_, bf16[32,4,16,128]{3,2,1,0:T(8,128)(2,1)} %collective-permute-done.1.refs_2_, ...), custom_call_target="tpu_custom_call" | custom-call | flops 6000000000 | tf_op jit(solution)/shard_map/pallas_call | solution.py:369
  71.5 3.2 %collective-permute-done.9.refs_3_ = bf16[32,8,16,128]{3,2,1,0:T(8,128)(2,1)S(1)} collective-permute-done((bf16[32,8,16,128]{3,2,1,0:T(8,128)(2,1)S(1)}, bf16[32,8,16,128]{3,2,1,0:T(8,128)(2,1)S(1)}, u32[]{:S(2)}, u32[]{:S(2)}) %collective-permute-start.9) | collective-permute-done | bytes 1048608 | tf_op jit(solution)/shard_map/ppermute | solution.py:408
  74.7 1.3 %collective-permute-start.12 = (bf16[32,8,16,128]{3,2,1,0:T(8,128)(2,1)S(1)}, bf16[32,8,16,128]{3,2,1,0:T(8,128)(2,1)S(1)}, u32[]{:S(2)}, u32[]{:S(2)}) collective-permute-start(bf16[32,8,16,128]{3,2,1,0:T(8,128)(2,1)S(1)} %collective-permute-done.9.refs_3_), channel_id=1, source_target_pairs={{4,2},{12,10},{20,18},{28,26},{5,3},{13,11},{21,19},{29,27}} | collective-permute-start | bytes 3145736 | tf_op jit(solution)/shard_map/ppermute | solution.py:413
  76.0 12.6 %collective-permute-done.8 = bf16[32,8,16,128]{3,2,1,0:T(8,128)(2,1)S(1)} collective-permute-done((bf16[32,8,16,128]{3,2,1,0:T(8,128)(2,1)S(1)}, bf16[32,8,16,128]{3,2,1,0:T(8,128)(2,1)S(1)}, u32[]{:S(2)}, u32[]{:S(2)}) %collective-permute-start.8) | collective-permute-done | bytes 1048608 | tf_op jit(solution)/shard_map/ppermute | solution.py:409
  88.6 12.6 %collective-permute-done.12 = bf16[32,8,16,128]{3,2,1,0:T(8,128)(2,1)S(1)} collective-permute-done((bf16[32,8,16,128]{3,2,1,0:T(8,128)(2,1)S(1)}, bf16[32,8,16,128]{3,2,1,0:T(8,128)(2,1)S(1)}, u32[]{:S(2)}, u32[]{:S(2)}) %collective-permute-start.12) | collective-permute-done | bytes 1048608 | tf_op jit(solution)/shard_map/ppermute | solution.py:413
  101.2 0.4 add.8.refs_2_
  101.6 0.1 collective-permute-start.13
  101.7 2.6 %collective-permute-done.13.refs_1_ = bf16[32,8,16,128]{3,2,1,0:T(8,128)(2,1)S(1)} collective-permute-done((bf16[32,8,16,128]{3,2,1,0:T(8,128)(2,1)S(1)}, bf16[32,8,16,128]{3,2,1,0:T(8,128)(2,1)S(1)}, u32[]{:S(2)}, u32[]{:S(2)}) %collective-permute-start.13) | collective-permute-done | bytes 1048608 | tf_op jit(solution)/shard_map/ppermute | solution.py:417
  104.3 10.1 %shard_map.51 = f32[2,8,4,8,8,128]{5,4,3,2,1,0:T(8,128)} custom-call(s32[2]{0:T(128)S(1)} %pad_add_fusion.place, bf16[32,8,16,128]{3,2,1,0:T(8,128)(2,1)S(1)} %pad_maximum_fusion.refs_0_, bf16[32,8,16,128]{3,2,1,0:T(8,128)(2,1)S(1)} %collective-permute-done.13.refs_1_, bf16[32,8,16,128]{3,2,1,0:T(8,128)(2,1)S(1)} %add.8.refs_2_, ...), custom_call_target="tpu_custom_call" | custom-call | flops 6000000000 | tf_op jit(solution)/shard_map/pallas_call | solution.py:369
Async XLA Ops:
  3.4 18.5 %copy-start = (bf16[8,32,64,128]{3,2,1,0:T(8,128)(2,1)}, bf16[8,32,64,128]{3,2,1,0:T(8,128)(2,1)S(1)}, u32[]{:S(2)}) copy-start(bf16[8,32,64,128]{3,2,1,0:T(8,128)(2,1)S(1)} %get-tuple-element.21.refs_0_.refs_1_) | copy-start | bytes 12582916
  3.4 39.5 %collective-permute-start.3 = (bf16[8,8,64,128]{3,2,1,0:T(8,128)(2,1)S(1)}, bf16[8,8,64,128]{3,2,1,0:T(8,128)(2,1)S(1)}, u32[]{:S(2)}, u32[]{:S(2)}) collective-permute-start(bf16[8,8,64,128]{3,2,1,0:T(8,128)(2,1)S(1)} %get-tuple-element.32), channel_id=1, source_target_pairs={{0,1},{1,0},{2,3},{3,2},{4,5},{5,4},{6,7},{7,6},{8,9},{9,8},{10,11... | collective-permute-start | bytes 3145736 | tf_op jit(solution)/shard_map/ppermute | solution.py:428
  17.7 18.2 %collective-permute-start.1 = (bf16[32,4,16,128]{3,2,1,0:T(8,128)(2,1)}, bf16[32,4,16,128]{3,2,1,0:T(8,128)(2,1)}, u32[]{:S(2)}, u32[]{:S(2)}) collective-permute-start(bf16[32,4,16,128]{3,2,1,0:T(8,128)(2,1)} %get-tuple-element.26.refs_0_), channel_id=1, source_target_pairs={{0,4},{2,6},{4,8},{6,10},{8,12},{10,14},{12,16},{14,18},{16,20},{1... | collective-permute-start | bytes 1572872 | tf_op jit(solution)/shard_map/ppermute | solution.py:397
  19.0 20.8 %collective-permute-start.2 = (bf16[32,4,16,128]{3,2,1,0:T(8,128)(2,1)}, bf16[32,4,16,128]{3,2,1,0:T(8,128)(2,1)}, u32[]{:S(2)}, u32[]{:S(2)}) collective-permute-start(bf16[32,4,16,128]{3,2,1,0:T(8,128)(2,1)} %get-tuple-element.30), channel_id=1, source_target_pairs={{0,1},{1,0},{2,3},{3,2},{4,5},{5,4},{6,7},{7,6},{8,9},{9,8},{10,11... | collective-permute-start | bytes 1572872 | tf_op jit(solution)/shard_map/ppermute | solution.py:432
  19.2 36.1 %collective-permute-start.6 = (bf16[32,4,16,128]{3,2,1,0:T(8,128)(2,1)}, bf16[32,4,16,128]{3,2,1,0:T(8,128)(2,1)}, u32[]{:S(2)}, u32[]{:S(2)}) collective-permute-start(bf16[32,4,16,128]{3,2,1,0:T(8,128)(2,1)} %get-tuple-element.26.refs_0_), channel_id=1, source_target_pairs={{0,2},{2,8},{4,6},{6,12},{8,10},{10,16},{12,14},{14,20},{16,18},{1... | collective-permute-start | bytes 1572872 | tf_op jit(solution)/shard_map/ppermute | solution.py:402
  33.9 19.1 %collective-permute-start = (bf16[32,4,16,128]{3,2,1,0:T(8,128)(2,1)}, bf16[32,4,16,128]{3,2,1,0:T(8,128)(2,1)}, u32[]{:S(2)}, u32[]{:S(2)}) collective-permute-start(bf16[32,4,16,128]{3,2,1,0:T(8,128)(2,1)} %get-tuple-element.29), channel_id=1, source_target_pairs={{0,1},{2,3},{4,5},{6,7},{8,9},{10,11},{12,13},{14,15},{16,17},{18,... | collective-permute-start | bytes 1572872 | tf_op jit(solution)/shard_map/ppermute | solution.py:437
  39.7 15.6 %collective-permute-start.4 = (bf16[32,4,16,128]{3,2,1,0:T(8,128)(2,1)}, bf16[32,4,16,128]{3,2,1,0:T(8,128)(2,1)S(1)}, u32[]{:S(2)}, u32[]{:S(2)}) collective-permute-start(bf16[32,4,16,128]{3,2,1,0:T(8,128)(2,1)} %collective-permute-done.2.refs_4_), channel_id=1, source_target_pairs={{0,4},{2,6},{4,8},{6,10},{8,12},{10,14},{12,16},{14,18},{16,20},{1... | collective-permute-start | bytes 1572872 | tf_op jit(solution)/shard_map/ppermute | solution.py:397
  40.9 14.5 %collective-permute-start.5 = (bf16[32,4,16,128]{3,2,1,0:T(8,128)(2,1)}, bf16[32,4,16,128]{3,2,1,0:T(8,128)(2,1)S(1)}, u32[]{:S(2)}, u32[]{:S(2)}) collective-permute-start(bf16[32,4,16,128]{3,2,1,0:T(8,128)(2,1)} %collective-permute-done.1.refs_2_), channel_id=1, source_target_pairs={{0,2},{2,0},{4,6},{6,4},{8,10},{10,8},{12,14},{14,12},{16,18},{18,... | collective-permute-start | bytes 1572872 | tf_op jit(solution)/shard_map/ppermute | solution.py:417
  42.9 23.3 %collective-permute-start.11 = (bf16[32,4,16,128]{3,2,1,0:T(8,128)(2,1)}, bf16[32,4,16,128]{3,2,1,0:T(8,128)(2,1)S(1)}, u32[]{:S(2)}, u32[]{:S(2)}) collective-permute-start(bf16[32,4,16,128]{3,2,1,0:T(8,128)(2,1)} %collective-permute-done.2.refs_4_), channel_id=1, source_target_pairs={{0,2},{2,8},{4,6},{6,12},{8,10},{10,16},{12,14},{14,20},{16,18},{1... | collective-permute-start | bytes 1572872 | tf_op jit(solution)/shard_map/ppermute | solution.py:402
  44.1 2.2 %copy-start.1 = (bf16[8,32,64,128]{3,2,1,0:T(8,128)(2,1)S(1)}, bf16[8,32,64,128]{3,2,1,0:T(8,128)(2,1)}, u32[]{:S(2)}) copy-start(bf16[8,32,64,128]{3,2,1,0:T(8,128)(2,1)} %copy-done) | copy-start | bytes 12582916
  53.0 8.3 %collective-permute-start.7 = (bf16[32,2,16,128]{3,2,1,0:T(8,128)(2,1)S(1)}, bf16[32,2,16,128]{3,2,1,0:T(8,128)(2,1)S(1)}, u32[]{:S(2)}, u32[]{:S(2)}) collective-permute-start(bf16[32,2,16,128]{3,2,1,0:T(8,128)(2,1)S(1)} %get-tuple-element.35), channel_id=1, source_target_pairs={{0,1},{1,0},{2,3},{3,2},{4,5},{5,4},{6,7},{7,6},{8,9},{9,8},{10,11... | collective-permute-start | bytes 786440 | tf_op jit(solution)/shard_map/ppermute | solution.py:447
  55.3 10.8 %collective-permute-start.10 = (bf16[32,4,16,128]{3,2,1,0:T(8,128)(2,1)S(1)}, bf16[32,4,16,128]{3,2,1,0:T(8,128)(2,1)S(1)}, u32[]{:S(2)}, u32[]{:S(2)}) collective-permute-start(bf16[32,4,16,128]{3,2,1,0:T(8,128)(2,1)S(1)} %collective-permute-done.4.refs_6_), channel_id=1, source_target_pairs={{0,2},{2,0},{4,6},{6,4},{8,10},{10,8},{12,14},{14,12},{16,18},{18,... | collective-permute-start | bytes 1572872 | tf_op jit(solution)/shard_map/ppermute | solution.py:417
  61.4 13.2 %collective-permute-start.9 = (bf16[32,8,16,128]{3,2,1,0:T(8,128)(2,1)S(1)}, bf16[32,8,16,128]{3,2,1,0:T(8,128)(2,1)S(1)}, u32[]{:S(2)}, u32[]{:S(2)}) collective-permute-start(bf16[32,8,16,128]{3,2,1,0:T(8,128)(2,1)S(1)} %pad_maximum_fusion.refs_0_), channel_id=1, source_target_pairs={{0,2},{2,8},{4,6},{6,12},{8,10},{10,16},{12,14},{14,20},{16,18},{1... | collective-permute-start | bytes 3145736 | tf_op jit(solution)/shard_map/ppermute | solution.py:408
  62.9 25.7 %collective-permute-start.8 = (bf16[32,8,16,128]{3,2,1,0:T(8,128)(2,1)S(1)}, bf16[32,8,16,128]{3,2,1,0:T(8,128)(2,1)S(1)}, u32[]{:S(2)}, u32[]{:S(2)}) collective-permute-start(bf16[32,8,16,128]{3,2,1,0:T(8,128)(2,1)S(1)} %pad_maximum_fusion.refs_0_), channel_id=1, source_target_pairs={{0,4},{2,6},{4,8},{8,12},{10,14},{12,16},{16,20},{18,22},{20,24},{... | collective-permute-start | bytes 3145736 | tf_op jit(solution)/shard_map/ppermute | solution.py:409
  74.7 26.6 %collective-permute-start.12 = (bf16[32,8,16,128]{3,2,1,0:T(8,128)(2,1)S(1)}, bf16[32,8,16,128]{3,2,1,0:T(8,128)(2,1)S(1)}, u32[]{:S(2)}, u32[]{:S(2)}) collective-permute-start(bf16[32,8,16,128]{3,2,1,0:T(8,128)(2,1)S(1)} %collective-permute-done.9.refs_3_), channel_id=1, source_target_pairs={{4,2},{12,10},{20,18},{28,26},{5,3},{13,11},{21,19},{29,27}} | collective-permute-start | bytes 3145736 | tf_op jit(solution)/shard_map/ppermute | solution.py:413
  101.6 2.7 %collective-permute-start.13 = (bf16[32,8,16,128]{3,2,1,0:T(8,128)(2,1)S(1)}, bf16[32,8,16,128]{3,2,1,0:T(8,128)(2,1)S(1)}, u32[]{:S(2)}, u32[]{:S(2)}) collective-permute-start(bf16[32,8,16,128]{3,2,1,0:T(8,128)(2,1)S(1)} %add.8.refs_2_), channel_id=1, source_target_pairs={{0,2},{2,0},{4,6},{6,4},{8,10},{10,8},{12,14},{14,12},{16,18},{18,... | collective-permute-start | bytes 3145736 | tf_op jit(solution)/shard_map/ppermute | solution.py:417

commit v13 on v11

--- a/solution.py
+++ b/solution.py
@@ -403,6 +403,16 @@
     return shifted(block, "stn", 2), rest
 
 
+def evenly(block):
+    size = lax.axis_size("stn")
+    rest = lax.ppermute(block, "stn", [(i, (i + 1 if i % 2 == 0 else i + 3) % size) for i in range(size)])
+    return lax.ppermute(block, "stn", [(i, (i + 2) % size) for i in range(size) if i % 4 < 3]), rest
+
+
+def relayed(rest):
+    return lax.ppermute(rest, "stn", [(i, i - 1) for i in range(lax.axis_size("stn")) if i % 4 == 2])
+
+
 def exchanged(block):
     return lax.ppermute(block, "stn", [(i, i ^ 1) for i in range(lax.axis_size("stn"))])
 
@@ -434,19 +444,20 @@
         edge, fixed, place, 2, sizes, 1, (own_b, two_a),
     )
     got_a, own_c, away_b, away_c, two_a = lax.optimization_barrier((got_a, own_c, away_b, away_c, two_a))
-    two_g, rest_g = farther(got_a)
+    two_g, rest_g = evenly(got_a)
     got_b = lax.ppermute(away_b, "tm", [(0, 1)])
-    got_c = lax.ppermute(away_c, "tm", swap)
     pair_a = exchanged(two_a)
     first = [(many, [(0, 0, 0)])]
     sums = correlated([own_a, pair_a, two_a, rest_a], first, None, False)
-    got_b, got_c, sums = lax.optimization_barrier((got_b, got_c, sums))
+    two_g = two_g + relayed(after(rest_g, two_g, sums))
+    got_b, away_c, sums = lax.optimization_barrier((got_b, away_c, sums))
+    got_c = lax.ppermute(away_c, "tm", swap)
     piece_b = jnp.where(me == 0, own_b, got_b)
     two_b, rest_b = farther(piece_b)
+    pair_g = exchanged(after(two_g, piece_b))
+    sums = correlated([got_a, pair_g, two_g, rest_g], first, sums, False)
     piece_c = jnp.concatenate([own_c, got_c], axis=1)
     two_c, rest_c = farther(piece_c)
-    pair_g = exchanged(after(two_g, piece_b))
-    sums = correlated([got_a, pair_g, two_g, rest_g], first, sums, False, (piece_c,), 6 * 10**9)
     pair_b = exchanged(two_b)
     sums = correlated([piece_b, pair_b, two_b, rest_b], first, sums, False)
     pair_c = exchanged(after(two_c, sums))

time: 109 us -> 113 us (1.037)
  the two profiles are of different devices: /device:TPU:6 before, /device:TPU:1 now
where the time goes in v13:
time: 113 us; the launch traced here: 112 us
  Pallas kernels  51.9 us (46%)
  waiting for transfers between devices  33.1 us (29%)
  starting transfers between devices  24.6 us (22%)
  other arithmetic  1.37 us (1%)
    pallas_call x3, Pallas kernels, spectra(): pl.pallas_call(functools.partial(spectra_kernel, groups, tuple((part[1:]...  30.1 us
    pallas_call x4, Pallas kernels, correlate(): pl.pallas_call(functools.partial(correlate_kernel, pieces, per_group, sca...  18.5 us
    ppermute x1, waiting for transfers between devices, relayed(): lax.ppermute(rest, 'stn', [(i, i - 1) for i in range(lax.axis_size('stn')...  17 us
    ppermute x3, waiting for transfers between devices, shifted(): lax.ppermute(block, axis, [(i, (i + distance) % size) for i in range(size)])  6.93 us
    ppermute x3, starting transfers between devices, farther(): lax.ppermute(block, 'stn', [(i, (i + 1 if i % 2 == 0 else i + 3) % size)...  6.19 us
    ppermute x4, starting transfers between devices, exchanged(): lax.ppermute(block, 'stn', [(i, i ^ 1) for i in range(lax.axis_size('stn'...  4.16 us
    ppermute x1, waiting for transfers between devices, paired(): got_b = lax.ppermute(away_b, 'tm', [(0, 1)])  3.78 us
    ppermute x3, starting transfers between devices, shifted(): lax.ppermute(block, axis, [(i, (i + distance) % size) for i in range(size)])  3.5 us
  transfers between devices with their start and end apart: 17, of which 6 were waited for; matrix products, arithmetic and copies ran while one was open for 1% of the time, Pallas kernels for 36%

profile of v13, /device:TPU:1, one launch (start us, length us, event | category | flops | bytes accessed | tf_op | source)
XLA Modules:
  0.0 112.0 jit_solution(6286791670839514966)
XLA Ops:
  0.0 0.1 pad_add_fusion.place
  0.1 3.3 %shard_map.46 = (bf16[8,32,64,128]{3,2,1,0:T(8,128)(2,1)S(1)}, bf16[8,8,64,128]{3,2,1,0:T(8,128)(2,1)S(1)}, f32[1024,128]{1,0:T(8,128)S(1)}, bf16[64,192]{1,0:T(...) custom-call(s32[2]{0:T(128)S(1)} %pad_add_fusion.place, bf16[8,32,64,128]{3,2,1,0:T(8,128)(2,1)} %bitcast.10, ...), custom_call_target="tpu_custom_call" | custom-call | tf_op jit(solution)/shard_map/pallas_call | solution.py:110
  3.4 2.1 %collective-permute-start.2 = (bf16[8,8,64,128]{3,2,1,0:T(8,128)(2,1)S(1)}, bf16[8,8,64,128]{3,2,1,0:T(8,128)(2,1)S(1)}, u32[]{:S(2)}, u32[]{:S(2)}) collective-permute-start(bf16[8,8,64,128]{3,2,1,0:T(8,128)(2,1)S(1)} %get-tuple-element.40), channel_id=1, source_target_pairs={{0,1},{1,0},{2,3},{3,2},{4,5},{5,4},{6,7},{7,6},{8,9},{9,8},{10,11... | collective-permute-start | bytes 3145736 | tf_op jit(solution)/shard_map/ppermute | solution.py:429
  5.5 11.3 %shard_map.47 = (bf16[32,4,16,128]{3,2,1,0:T(8,128)(2,1)S(1)}, bf16[32,4,16,128]{3,2,1,0:T(8,128)(2,1)S(1)}) custom-call(s32[2]{0:T(128)S(1)} %pad_add_fusion.place, bf16[8,32,64,128]{3,2,1,0:T(8,128)(2,1)S(1)} %get-tuple-element.30.refs_0_.refs_1_, bf16[8,32,64,128]{3,2,1,0:T(8,128)(2,1)S(1)} %get-tuple-element.30.refs_0_.refs_1_, ...), custom_call_target="tpu_custom_call" | custom-call | flops 1000000 | tf_op jit(solution)/shard_map/pallas_call | solution.py:263
  16.8 1.3 %collective-permute-start.1 = (bf16[32,4,16,128]{3,2,1,0:T(8,128)(2,1)S(1)}, bf16[32,4,16,128]{3,2,1,0:T(8,128)(2,1)S(1)}, u32[]{:S(2)}, u32[]{:S(2)}) collective-permute-start(bf16[32,4,16,128]{3,2,1,0:T(8,128)(2,1)S(1)} %get-tuple-element.36.refs_0_), channel_id=1, source_target_pairs={{0,4},{2,6},{4,8},{6,10},{8,12},{10,14},{12,16},{14,18},{16,20},{1... | collective-permute-start | bytes 1572872 | tf_op jit(solution)/shard_map/ppermute | solution.py:397
  18.1 0.3 collective-permute-start
  18.4 2.7 %collective-permute-start.5 = (bf16[32,4,16,128]{3,2,1,0:T(8,128)(2,1)S(1)}, bf16[32,4,16,128]{3,2,1,0:T(8,128)(2,1)S(1)}, u32[]{:S(2)}, u32[]{:S(2)}) collective-permute-start(bf16[32,4,16,128]{3,2,1,0:T(8,128)(2,1)S(1)} %get-tuple-element.36.refs_0_), channel_id=1, source_target_pairs={{0,2},{2,8},{4,6},{6,12},{8,10},{10,16},{12,14},{14,20},{16,18},{1... | collective-permute-start | bytes 1572872 | tf_op jit(solution)/shard_map/ppermute | solution.py:402
  21.1 12.0 %shard_map.48 = (bf16[32,4,16,128]{3,2,1,0:T(8,128)(2,1)S(1)}, bf16[32,4,16,128]{3,2,1,0:T(8,128)(2,1)}) custom-call(s32[2]{0:T(128)S(1)} %pad_add_fusion.place, bf16[8,32,64,128]{3,2,1,0:T(8,128)(2,1)S(1)} %get-tuple-element.30.refs_0_.refs_1_, bf16[8,32,64,128]{3,2,1,0:T(8,128)(2,1)S(1)} %get-tuple-element.30.refs_0_.refs_1_, ...), custom_call_target="tpu_custom_call" | custom-call | flops 1000000 | tf_op jit(solution)/shard_map/pallas_call | solution.py:263
  33.1 0.0 copy-start
  33.1 0.0 collective-permute-done.1.refs_2_
  33.1 0.0 collective-permute-done.2.refs_2_
  33.1 6.7 %shard_map.49 = (bf16[32,2,16,128]{3,2,1,0:T(8,128)(2,1)S(1)}, bf16[32,2,16,128]{3,2,1,0:T(8,128)(2,1)S(1)}) custom-call(s32[2]{0:T(128)S(1)} %pad_add_fusion.place, bf16[8,32,64,128]{3,2,1,0:T(8,128)(2,1)S(1)} %get-tuple-element.30.refs_0_.refs_1_, bf16[8,32,64,128]{3,2,1,0:T(8,128)(2,1)S(1)} %get-tuple-element.30.refs_0_.refs_1_, ...), custom_call_target="tpu_custom_call" | custom-call | flops 1000000 | tf_op jit(solution)/shard_map/pallas_call | solution.py:263
  39.9 0.0 copy-done
  39.9 0.0 copy-start.2
  39.9 0.7 copy-done.2
  40.6 0.0 collective-permute-done.refs_0_
  40.6 2.3 %collective-permute-start.4 = (bf16[32,4,16,128]{3,2,1,0:T(8,128)(2,1)S(1)}, bf16[32,4,16,128]{3,2,1,0:T(8,128)(2,1)S(1)}, u32[]{:S(2)}, u32[]{:S(2)}) collective-permute-start(bf16[32,4,16,128]{3,2,1,0:T(8,128)(2,1)S(1)} %collective-permute-done.1.refs_2_), channel_id=1, source_target_pairs={{0,2},{2,0},{4,6},{6,4},{8,10},{10,8},{12,14},{14,12},{16,18},{18,... | collective-permute-start | bytes 1572872 | tf_op jit(solution)/shard_map/ppermute | solution.py:417
  42.9 2.7 %collective-permute-start.3 = (bf16[32,4,16,128]{3,2,1,0:T(8,128)(2,1)}, bf16[32,4,16,128]{3,2,1,0:T(8,128)(2,1)}, u32[]{:S(2)}, u32[]{:S(2)}) collective-permute-start(bf16[32,4,16,128]{3,2,1,0:T(8,128)(2,1)} %get-tuple-element.45), channel_id=1, source_target_pairs={{0,1},{2,3},{4,5},{6,7},{8,9},{10,11},{12,13},{14,15},{16,17},{18,... | collective-permute-start | bytes 1572872 | tf_op jit(solution)/shard_map/ppermute | solution.py:448
  45.6 3.3 %collective-permute-start.11 = (bf16[32,4,16,128]{3,2,1,0:T(8,128)(2,1)S(1)}, bf16[32,4,16,128]{3,2,1,0:T(8,128)(2,1)}, u32[]{:S(2)}, u32[]{:S(2)}) collective-permute-start(bf16[32,4,16,128]{3,2,1,0:T(8,128)(2,1)S(1)} %collective-permute-done.refs_0_), channel_id=1, source_target_pairs={{0,4},{2,6},{4,8},{8,12},{10,14},{12,16},{16,20},{18,22},{20,24},{... | collective-permute-start | bytes 1572872 | tf_op jit(solution)/shard_map/ppermute | solution.py:409
  48.9 1.0 collective-permute-start.12
  49.9 0.0 copy-start.1
  49.9 0.0 copy-start.3
  49.9 0.0 collective-permute-done.5.refs_3_
  49.9 0.0 collective-permute-done.4.refs_1_
  49.9 2.7 %shard_map.50.refs_4_ = f32[4096,128]{1,0:T(8,128)S(1)} custom-call(s32[2]{0:T(128)S(1)} %pad_add_fusion.place, bf16[32,4,16,128]{3,2,1,0:T(8,128)(2,1)S(1)} %get-tuple-element.36.refs_0_, bf16[32,4,16,128]{3,2,1,0:T(8,128)(2,1)S(1)} %collective-permute-done.4.refs_1_, bf16[32,4,16,128]{3,2,1,0:T(8,128)(2,1)S(1)} %collective-permute-done.1.refs_2_, ...), custom_call_target="tpu_custom_call" | custom-call | flops 1000 | tf_op jit(solution)/shard_map/pallas_call | solution.py:369
  52.7 3.8 %collective-permute-done.3 = bf16[32,4,16,128]{3,2,1,0:T(8,128)(2,1)} collective-permute-done((bf16[32,4,16,128]{3,2,1,0:T(8,128)(2,1)}, bf16[32,4,16,128]{3,2,1,0:T(8,128)(2,1)}, u32[]{:S(2)}, u32[]{:S(2)}) %collective-permute-start.3) | collective-permute-done | bytes 524320 | tf_op jit(solution)/shard_map/ppermute | solution.py:448
  56.5 2.7 %collective-permute-done.11 = bf16[32,4,16,128]{3,2,1,0:T(8,128)(2,1)} collective-permute-done((bf16[32,4,16,128]{3,2,1,0:T(8,128)(2,1)S(1)}, bf16[32,4,16,128]{3,2,1,0:T(8,128)(2,1)}, u32[]{:S(2)}, u32[]{:S(2)}) %collective-permute-start.11) | collective-permute-done | bytes 524320 | tf_op jit(solution)/shard_map/ppermute | solution.py:409
  59.1 0.0 collective-permute-done.12.refs_3_
  59.1 1.3 %collective-permute-start.13 = (bf16[32,4,16,128]{3,2,1,0:T(8,128)(2,1)S(1)}, bf16[32,4,16,128]{3,2,1,0:T(8,128)(2,1)S(1)}, u32[]{:S(2)}, u32[]{:S(2)}) collective-permute-start(bf16[32,4,16,128]{3,2,1,0:T(8,128)(2,1)S(1)} %collective-permute-done.12.refs_3_), channel_id=1, source_target_pairs={{4,2},{12,10},{20,18},{28,26},{5,3},{13,11},{21,19},{29,27}} | collective-permute-start | bytes 1572872 | tf_op jit(solution)/shard_map/ppermute | solution.py:413
  60.4 0.0 copy-done.1
  60.4 0.1 broadcast_select_fusion.refs_0_
  60.5 2.2 %collective-permute-start.8 = (bf16[32,4,16,128]{3,2,1,0:T(8,128)(2,1)S(1)}, bf16[32,4,16,128]{3,2,1,0:T(8,128)(2,1)S(1)}, u32[]{:S(2)}, u32[]{:S(2)}) collective-permute-start(bf16[32,4,16,128]{3,2,1,0:T(8,128)(2,1)S(1)} %broadcast_select_fusion.refs_0_), channel_id=1, source_target_pairs={{0,4},{2,6},{4,8},{6,10},{8,12},{10,14},{12,16},{14,18},{16,20},{1... | collective-permute-start | bytes 1572872 | tf_op jit(solution)/shard_map/ppermute | solution.py:397
  62.7 0.0 copy-done.3
  62.7 0.0 collective-permute-start.6
  62.7 3.4 %collective-permute-start.10 = (bf16[32,4,16,128]{3,2,1,0:T(8,128)(2,1)S(1)}, bf16[32,4,16,128]{3,2,1,0:T(8,128)(2,1)S(1)}, u32[]{:S(2)}, u32[]{:S(2)}) collective-permute-start(bf16[32,4,16,128]{3,2,1,0:T(8,128)(2,1)S(1)} %broadcast_select_fusion.refs_0_), channel_id=1, source_target_pairs={{0,2},{2,8},{4,6},{6,12},{8,10},{10,16},{12,14},{14,20},{16,18},{1... | collective-permute-start | bytes 1572872 | tf_op jit(solution)/shard_map/ppermute | solution.py:402
  66.2 17.0 %collective-permute-done.13 = bf16[32,4,16,128]{3,2,1,0:T(8,128)(2,1)S(1)} collective-permute-done((bf16[32,4,16,128]{3,2,1,0:T(8,128)(2,1)S(1)}, bf16[32,4,16,128]{3,2,1,0:T(8,128)(2,1)S(1)}, u32[]{:S(2)}, u32[]{:S(2)}) %collective-permute-start.13) | collective-permute-done | bytes 524320 | tf_op jit(solution)/shard_map/ppermute | solution.py:413
  83.1 1.2 %add.8.refs_2_ = bf16[32,4,16,128]{3,2,1,0:T(8,128)(2,1)S(1)} add(bf16[32,4,16,128]{3,2,1,0:T(8,128)(2,1)} %collective-permute-done.11, bf16[32,4,16,128]{3,2,1,0:T(8,128)(2,1)S(1)} %collective-permute-done.13) | non-fusion elementwise | flops 262144 | bytes 1572864 | tf_op jit(solution)/shard_map/add | solution.py:452
  84.4 0.1 collective-permute-start.14
  84.4 0.0 collective-permute-done.8.refs_2_
  84.4 0.5 collective-permute-start.9
  84.9 0.0 collective-permute-done.6
  85.0 0.1 collective-permute-start.7
  85.0 0.1 collective-permute-start.16
  85.1 1.2 %collective-permute-done.14.refs_1_ = bf16[32,4,16,128]{3,2,1,0:T(8,128)(2,1)S(1)} collective-permute-done((bf16[32,4,16,128]{3,2,1,0:T(8,128)(2,1)S(1)}, bf16[32,4,16,128]{3,2,1,0:T(8,128)(2,1)S(1)}, u32[]{:S(2)}, u32[]{:S(2)}) %collective-permute-start.14) | collective-permute-done | bytes 524320 | tf_op jit(solution)/shard_map/ppermute | solution.py:417
  86.3 4.0 %shard_map.51.refs_4_ = f32[4096,128]{1,0:T(8,128)S(1)} custom-call(s32[2]{0:T(128)S(1)} %pad_add_fusion.place, bf16[32,4,16,128]{3,2,1,0:T(8,128)(2,1)S(1)} %collective-permute-done.refs_0_, bf16[32,4,16,128]{3,2,1,0:T(8,128)(2,1)S(1)} %collective-permute-done.14.refs_1_, bf16[32,4,16,128]{3,2,1,0:T(8,128)(2,1)S(1)} %add.8.refs_2_, ...), custom_call_target="tpu_custom_call", output_to_operand_aliasing={{}: (5, {})} | custom-call | flops 1000 | tf_op jit(solution)/shard_map/pallas_call | solution.py:369
  90.3 0.0 collective-permute-done.10.refs_3_
  90.3 0.0 collective-permute-done.9.refs_1_
  90.3 4.0 %shard_map.52.refs_4_ = f32[4096,128]{1,0:T(8,128)S(1)} custom-call(s32[2]{0:T(128)S(1)} %pad_add_fusion.place, bf16[32,4,16,128]{3,2,1,0:T(8,128)(2,1)S(1)} %broadcast_select_fusion.refs_0_, bf16[32,4,16,128]{3,2,1,0:T(8,128)(2,1)S(1)} %collective-permute-done.9.refs_1_, ...), custom_call_target="tpu_custom_call", output_to_operand_aliasing={{}: (5, {})} | custom-call | flops 1000 | tf_op jit(solution)/shard_map/pallas_call | solution.py:369
  94.3 6.9 %collective-permute-done.7.refs_2_ = bf16[32,4,16,128]{3,2,1,0:T(8,128)(2,1)S(1)} collective-permute-done((bf16[32,4,16,128]{3,2,1,0:T(8,128)(2,1)S(1)}, bf16[32,4,16,128]{3,2,1,0:T(8,128)(2,1)S(1)}, u32[]{:S(2)}, u32[]{:S(2)}) %collective-permute-start.7) | collective-permute-done | bytes 524320 | tf_op jit(solution)/shard_map/ppermute | solution.py:397
  101.2 1.3 %collective-permute-start.15 = (bf16[32,4,16,128]{3,2,1,0:T(8,128)(2,1)S(1)}, bf16[32,4,16,128]{3,2,1,0:T(8,128)(2,1)S(1)}, u32[]{:S(2)}, u32[]{:S(2)}) collective-permute-start(bf16[32,4,16,128]{3,2,1,0:T(8,128)(2,1)S(1)} %collective-permute-done.7.refs_2_), channel_id=1, source_target_pairs={{0,2},{2,0},{4,6},{6,4},{8,10},{10,8},{12,14},{14,12},{16,18},{18,... | collective-permute-start | bytes 1572872 | tf_op jit(solution)/shard_map/ppermute | solution.py:417
  102.5 0.0 collective-permute-done.16.refs_3_
  102.5 1.5 %collective-permute-done.15.refs_1_ = bf16[32,4,16,128]{3,2,1,0:T(8,128)(2,1)S(1)} collective-permute-done((bf16[32,4,16,128]{3,2,1,0:T(8,128)(2,1)S(1)}, bf16[32,4,16,128]{3,2,1,0:T(8,128)(2,1)S(1)}, u32[]{:S(2)}, u32[]{:S(2)}) %collective-permute-start.15) | collective-permute-done | bytes 524320 | tf_op jit(solution)/shard_map/ppermute | solution.py:417
  104.1 7.9 %shard_map.53 = f32[2,8,4,8,8,128]{5,4,3,2,1,0:T(8,128)} custom-call(s32[2]{0:T(128)S(1)} %pad_add_fusion.place, bf16[32,4,16,128]{3,2,1,0:T(8,128)(2,1)S(1)} %constant_dynamic-update-slice_fusion.refs_0_, bf16[32,4,16,128]{3,2,1,0:T(8,128)(2,1)S(1)} %collective-permute-done.15.refs_1_, bf16[32,4,16,128]{3,2,1,0:T(8,128)(2,1)S(1)} %collective-permute-done.7.refs_2_, ...), custom_call_target="tpu_custom_call" | custom-call | flops 1000 | tf_op jit(solution)/shard_map/pallas_call | solution.py:369
  (2 shorter events, 0.1 us)
Async XLA Ops:
  3.4 29.7 %collective-permute-start.2 = (bf16[8,8,64,128]{3,2,1,0:T(8,128)(2,1)S(1)}, bf16[8,8,64,128]{3,2,1,0:T(8,128)(2,1)S(1)}, u32[]{:S(2)}, u32[]{:S(2)}) collective-permute-start(bf16[8,8,64,128]{3,2,1,0:T(8,128)(2,1)S(1)} %get-tuple-element.40), channel_id=1, source_target_pairs={{0,1},{1,0},{2,3},{3,2},{4,5},{5,4},{6,7},{7,6},{8,9},{9,8},{10,11... | collective-permute-start | bytes 3145736 | tf_op jit(solution)/shard_map/ppermute | solution.py:429
  16.8 16.3 %collective-permute-start.1 = (bf16[32,4,16,128]{3,2,1,0:T(8,128)(2,1)S(1)}, bf16[32,4,16,128]{3,2,1,0:T(8,128)(2,1)S(1)}, u32[]{:S(2)}, u32[]{:S(2)}) collective-permute-start(bf16[32,4,16,128]{3,2,1,0:T(8,128)(2,1)S(1)} %get-tuple-element.36.refs_0_), channel_id=1, source_target_pairs={{0,4},{2,6},{4,8},{6,10},{8,12},{10,14},{12,16},{14,18},{16,20},{1... | collective-permute-start | bytes 1572872 | tf_op jit(solution)/shard_map/ppermute | solution.py:397
  18.1 22.5 %collective-permute-start = (bf16[32,4,16,128]{3,2,1,0:T(8,128)(2,1)S(1)}, bf16[32,4,16,128]{3,2,1,0:T(8,128)(2,1)S(1)}, u32[]{:S(2)}, u32[]{:S(2)}) collective-permute-start(bf16[32,4,16,128]{3,2,1,0:T(8,128)(2,1)S(1)} %get-tuple-element.35), channel_id=1, source_target_pairs={{0,1},{1,0},{2,3},{3,2},{4,5},{5,4},{6,7},{7,6},{8,9},{9,8},{10,11... | collective-permute-start | bytes 1572872 | tf_op jit(solution)/shard_map/ppermute | solution.py:433
  18.4 31.6 %collective-permute-start.5 = (bf16[32,4,16,128]{3,2,1,0:T(8,128)(2,1)S(1)}, bf16[32,4,16,128]{3,2,1,0:T(8,128)(2,1)S(1)}, u32[]{:S(2)}, u32[]{:S(2)}) collective-permute-start(bf16[32,4,16,128]{3,2,1,0:T(8,128)(2,1)S(1)} %get-tuple-element.36.refs_0_), channel_id=1, source_target_pairs={{0,2},{2,8},{4,6},{6,12},{8,10},{10,16},{12,14},{14,20},{16,18},{1... | collective-permute-start | bytes 1572872 | tf_op jit(solution)/shard_map/ppermute | solution.py:402
  33.1 6.8 %copy-start = (bf16[32,4,16,128]{3,2,1,0:T(8,128)(2,1)}, bf16[32,4,16,128]{3,2,1,0:T(8,128)(2,1)S(1)}, u32[]{:S(2)}) copy-start(bf16[32,4,16,128]{3,2,1,0:T(8,128)(2,1)S(1)} %get-tuple-element.38) | copy-start | bytes 1572868
  39.9 0.7 copy-start.2
  40.6 9.3 %collective-permute-start.4 = (bf16[32,4,16,128]{3,2,1,0:T(8,128)(2,1)S(1)}, bf16[32,4,16,128]{3,2,1,0:T(8,128)(2,1)S(1)}, u32[]{:S(2)}, u32[]{:S(2)}) collective-permute-start(bf16[32,4,16,128]{3,2,1,0:T(8,128)(2,1)S(1)} %collective-permute-done.1.refs_2_), channel_id=1, source_target_pairs={{0,2},{2,0},{4,6},{6,4},{8,10},{10,8},{12,14},{14,12},{16,18},{18,... | collective-permute-start | bytes 1572872 | tf_op jit(solution)/shard_map/ppermute | solution.py:417
  42.9 13.6 %collective-permute-start.3 = (bf16[32,4,16,128]{3,2,1,0:T(8,128)(2,1)}, bf16[32,4,16,128]{3,2,1,0:T(8,128)(2,1)}, u32[]{:S(2)}, u32[]{:S(2)}) collective-permute-start(bf16[32,4,16,128]{3,2,1,0:T(8,128)(2,1)} %get-tuple-element.45), channel_id=1, source_target_pairs={{0,1},{2,3},{4,5},{6,7},{8,9},{10,11},{12,13},{14,15},{16,17},{18,... | collective-permute-start | bytes 1572872 | tf_op jit(solution)/shard_map/ppermute | solution.py:448
  45.6 13.5 %collective-permute-start.11 = (bf16[32,4,16,128]{3,2,1,0:T(8,128)(2,1)S(1)}, bf16[32,4,16,128]{3,2,1,0:T(8,128)(2,1)}, u32[]{:S(2)}, u32[]{:S(2)}) collective-permute-start(bf16[32,4,16,128]{3,2,1,0:T(8,128)(2,1)S(1)} %collective-permute-done.refs_0_), channel_id=1, source_target_pairs={{0,4},{2,6},{4,8},{8,12},{10,14},{12,16},{16,20},{18,22},{20,24},{... | collective-permute-start | bytes 1572872 | tf_op jit(solution)/shard_map/ppermute | solution.py:409
  48.9 10.2 %collective-permute-start.12 = (bf16[32,4,16,128]{3,2,1,0:T(8,128)(2,1)S(1)}, bf16[32,4,16,128]{3,2,1,0:T(8,128)(2,1)S(1)}, u32[]{:S(2)}, u32[]{:S(2)}) collective-permute-start(bf16[32,4,16,128]{3,2,1,0:T(8,128)(2,1)S(1)} %collective-permute-done.refs_0_), channel_id=1, source_target_pairs={{0,2},{2,8},{4,6},{6,12},{8,10},{10,16},{12,14},{14,20},{16,18},{1... | collective-permute-start | bytes 1572872 | tf_op jit(solution)/shard_map/ppermute | solution.py:408
  49.9 10.5 %copy-start.1 = (bf16[32,4,16,128]{3,2,1,0:T(8,128)(2,1)S(1)}, bf16[32,4,16,128]{3,2,1,0:T(8,128)(2,1)}, u32[]{:S(2)}) copy-start(bf16[32,4,16,128]{3,2,1,0:T(8,128)(2,1)} %copy-done) | copy-start | bytes 1572868
  49.9 12.8 %copy-start.3 = (bf16[32,2,16,128]{3,2,1,0:T(8,128)(2,1)S(1)}, bf16[32,2,16,128]{3,2,1,0:T(8,128)(2,1)}, u32[]{:S(2)}) copy-start(bf16[32,2,16,128]{3,2,1,0:T(8,128)(2,1)} %copy-done.2) | copy-start | bytes 786436
  59.1 24.0 %collective-permute-start.13 = (bf16[32,4,16,128]{3,2,1,0:T(8,128)(2,1)S(1)}, bf16[32,4,16,128]{3,2,1,0:T(8,128)(2,1)S(1)}, u32[]{:S(2)}, u32[]{:S(2)}) collective-permute-start(bf16[32,4,16,128]{3,2,1,0:T(8,128)(2,1)S(1)} %collective-permute-done.12.refs_3_), channel_id=1, source_target_pairs={{4,2},{12,10},{20,18},{28,26},{5,3},{13,11},{21,19},{29,27}} | collective-permute-start | bytes 1572872 | tf_op jit(solution)/shard_map/ppermute | solution.py:413
  60.5 23.9 %collective-permute-start.8 = (bf16[32,4,16,128]{3,2,1,0:T(8,128)(2,1)S(1)}, bf16[32,4,16,128]{3,2,1,0:T(8,128)(2,1)S(1)}, u32[]{:S(2)}, u32[]{:S(2)}) collective-permute-start(bf16[32,4,16,128]{3,2,1,0:T(8,128)(2,1)S(1)} %broadcast_select_fusion.refs_0_), channel_id=1, source_target_pairs={{0,4},{2,6},{4,8},{6,10},{8,12},{10,14},{12,16},{14,18},{16,20},{1... | collective-permute-start | bytes 1572872 | tf_op jit(solution)/shard_map/ppermute | solution.py:397
  62.7 22.2 %collective-permute-start.6 = (bf16[32,2,16,128]{3,2,1,0:T(8,128)(2,1)S(1)}, bf16[32,2,16,128]{3,2,1,0:T(8,128)(2,1)S(1)}, u32[]{:S(2)}, u32[]{:S(2)}) collective-permute-start(bf16[32,2,16,128]{3,2,1,0:T(8,128)(2,1)S(1)} %copy-done.3), channel_id=1, source_target_pairs={{0,1},{1,0},{2,3},{3,2},{4,5},{5,4},{6,7},{7,6},{8,9},{9,8},{10,11... | collective-permute-start | bytes 786440 | tf_op jit(solution)/shard_map/ppermute | solution.py:454
  62.7 27.6 %collective-permute-start.10 = (bf16[32,4,16,128]{3,2,1,0:T(8,128)(2,1)S(1)}, bf16[32,4,16,128]{3,2,1,0:T(8,128)(2,1)S(1)}, u32[]{:S(2)}, u32[]{:S(2)}) collective-permute-start(bf16[32,4,16,128]{3,2,1,0:T(8,128)(2,1)S(1)} %broadcast_select_fusion.refs_0_), channel_id=1, source_target_pairs={{0,2},{2,8},{4,6},{6,12},{8,10},{10,16},{12,14},{14,20},{16,18},{1... | collective-permute-start | bytes 1572872 | tf_op jit(solution)/shard_map/ppermute | solution.py:402
  84.4 2.0 %collective-permute-start.14 = (bf16[32,4,16,128]{3,2,1,0:T(8,128)(2,1)S(1)}, bf16[32,4,16,128]{3,2,1,0:T(8,128)(2,1)S(1)}, u32[]{:S(2)}, u32[]{:S(2)}) collective-permute-start(bf16[32,4,16,128]{3,2,1,0:T(8,128)(2,1)S(1)} %add.8.refs_2_), channel_id=1, source_target_pairs={{0,2},{2,0},{4,6},{6,4},{8,10},{10,8},{12,14},{14,12},{16,18},{18,... | collective-permute-start | bytes 1572872 | tf_op jit(solution)/shard_map/ppermute | solution.py:417
  84.4 5.9 %collective-permute-start.9 = (bf16[32,4,16,128]{3,2,1,0:T(8,128)(2,1)S(1)}, bf16[32,4,16,128]{3,2,1,0:T(8,128)(2,1)S(1)}, u32[]{:S(2)}, u32[]{:S(2)}) collective-permute-start(bf16[32,4,16,128]{3,2,1,0:T(8,128)(2,1)S(1)} %collective-permute-done.8.refs_2_), channel_id=1, source_target_pairs={{0,2},{2,0},{4,6},{6,4},{8,10},{10,8},{12,14},{14,12},{16,18},{18,... | collective-permute-start | bytes 1572872 | tf_op jit(solution)/shard_map/ppermute | solution.py:417
  85.0 16.2 %collective-permute-start.7 = (bf16[32,4,16,128]{3,2,1,0:T(8,128)(2,1)S(1)}, bf16[32,4,16,128]{3,2,1,0:T(8,128)(2,1)S(1)}, u32[]{:S(2)}, u32[]{:S(2)}) collective-permute-start(bf16[32,4,16,128]{3,2,1,0:T(8,128)(2,1)S(1)} %constant_dynamic-update-slice_fusion.refs_0_), channel_id=1, source_target_pairs={{0,4},{2,6},{4,8},{6,10},{8,12},{10,14},{12,16},{14,18},{16,20},{1... | collective-permute-start | bytes 1572872 | tf_op jit(solution)/shard_map/ppermute | solution.py:397
  85.0 17.5 %collective-permute-start.16 = (bf16[32,4,16,128]{3,2,1,0:T(8,128)(2,1)S(1)}, bf16[32,4,16,128]{3,2,1,0:T(8,128)(2,1)S(1)}, u32[]{:S(2)}, u32[]{:S(2)}) collective-permute-start(bf16[32,4,16,128]{3,2,1,0:T(8,128)(2,1)S(1)} %constant_dynamic-update-slice_fusion.refs_0_), channel_id=1, source_target_pairs={{0,2},{2,8},{4,6},{6,12},{8,10},{10,16},{12,14},{14,20},{16,18},{1... | collective-permute-start | bytes 1572872 | tf_op jit(solution)/shard_map/ppermute | solution.py:402
  101.2 2.9 %collective-permute-start.15 = (bf16[32,4,16,128]{3,2,1,0:T(8,128)(2,1)S(1)}, bf16[32,4,16,128]{3,2,1,0:T(8,128)(2,1)S(1)}, u32[]{:S(2)}, u32[]{:S(2)}) collective-permute-start(bf16[32,4,16,128]{3,2,1,0:T(8,128)(2,1)S(1)} %collective-permute-done.7.refs_2_), channel_id=1, source_target_pairs={{0,2},{2,0},{4,6},{6,4},{8,10},{10,8},{12,14},{14,12},{16,18},{18,... | collective-permute-start | bytes 1572872 | tf_op jit(solution)/shard_map/ppermute | solution.py:417

commit v14 on v13

--- a/solution.py
+++ b/solution.py
@@ -296,6 +296,12 @@
     first_tile = lane < LANES // 2
     real_lane = lane % TILE < SUB
     sign = jnp.where(real_lane, 1.0, -1.0).astype(F32)
+
+    def fetch(spot, tile, k2, k1):
+        arrays, row, column = spot
+        values = [refs[array][row + tile * half + k2, column + k1] for array in arrays]
+        return values[0] if len(values) == 1 else values[0] + values[1]
+
     for number, piece in enumerate(pieces):
         tiles, piece = piece
         share = H // tiles
@@ -308,15 +314,13 @@
             for position in range(len(piece[0])):
                 rows = []
                 for tile in range(2):
-                    array, row, column = piece[0][position]
-                    a = refs[array][row + tile * half + k2, column + k1]
+                    a = fetch(piece[0][position], tile, k2, k1)
                     rows += [jnp.where(where == c, a, jnp.zeros_like(a)) for c in range(share)]
                 own.append(jnp.concatenate(rows, axis=0))
                 rows = []
                 for tile in range(2):
                     for visit in range(VISITS):
-                        array, row, column = piece[visit][position]
-                        rows.append(refs[array][row + tile * half + k2, column + k1])
+                        rows.append(fetch(piece[visit][position], tile, k2, k1))
                 other.append(jnp.concatenate(rows, axis=0))
             product = dot_nt(jnp.concatenate(own, axis=1), jnp.concatenate(other, axis=1))
             for c in range(share):
@@ -405,12 +409,12 @@
 
 def evenly(block):
     size = lax.axis_size("stn")
-    rest = lax.ppermute(block, "stn", [(i, (i + 1 if i % 2 == 0 else i + 3) % size) for i in range(size)])
-    return lax.ppermute(block, "stn", [(i, (i + 2) % size) for i in range(size) if i % 4 < 3]), rest
-
-
-def relayed(rest):
-    return lax.ppermute(rest, "stn", [(i, i - 1) for i in range(lax.axis_size("stn")) if i % 4 == 2])
+    ways = [(i, (i + 1 if i % 2 == 0 else i + 3) % size) for i in range(size) if i % 4 < 3]
+    return shifted(block, "stn", 2), lax.ppermute(block, "stn", ways)
+
+
+def relayed(two):
+    return lax.ppermute(two, "stn", [(i, i + 1) for i in range(lax.axis_size("stn")) if i % 4 == 1])
 
 
 def exchanged(block):
@@ -449,17 +453,16 @@
     pair_a = exchanged(two_a)
     first = [(many, [(0, 0, 0)])]
     sums = correlated([own_a, pair_a, two_a, rest_a], first, None, False)
-    two_g = two_g + relayed(after(rest_g, two_g, sums))
     got_b, away_c, sums = lax.optimization_barrier((got_b, away_c, sums))
     got_c = lax.ppermute(away_c, "tm", swap)
     piece_b = jnp.where(me == 0, own_b, got_b)
-    two_b, rest_b = farther(piece_b)
-    pair_g = exchanged(after(two_g, piece_b))
-    sums = correlated([got_a, pair_g, two_g, rest_g], first, sums, False)
+    two_b, rest_b = evenly(piece_b)
+    pair_g, relay_g = exchanged(two_g), relayed(two_g)
+    sums = correlated([got_a, pair_g, two_g, (rest_g, relay_g)], first, sums, False)
     piece_c = jnp.concatenate([own_c, got_c], axis=1)
     two_c, rest_c = farther(piece_c)
-    pair_b = exchanged(two_b)
-    sums = correlated([piece_b, pair_b, two_b, rest_b], first, sums, False)
+    pair_b, relay_b = exchanged(two_b), relayed(two_b)
+    sums = correlated([piece_b, pair_b, two_b, (rest_b, relay_b)], first, sums, False)
     pair_c = exchanged(after(two_c, sums))
     return correlated([piece_c, pair_c, two_c, rest_c], [(few, [(0, 0, 0), (0, 0, few)])], sums, True)
 
@@ -483,11 +486,13 @@
     scale = 1.0 / (groups * voltage.shape[1])
 
     def correlated(arrays, pieces, before, last, wait=(), cost=10**3):
-        laid = [
-            (tiles, [[(VISITS * n + visit, row, column) for n, row, column in spots] for visit in range(VISITS)])
-            for tiles, spots in pieces
-        ]
-        return correlate(arrays, laid, K2 // groups, place, scale, before, last, wait, cost)
+        flat, spots_of = [], []
+        for array in arrays:
+            parts = array if isinstance(array, tuple) else (array,)
+            spots_of.append(tuple(range(len(flat), len(flat) + len(parts))))
+            flat += parts
+        laid = [(tiles, [[(where, r, c) for _, r, c in spots] for where in spots_of]) for tiles, spots in pieces]
+        return correlate(flat, laid, K2 // groups, place, scale, before, last, wait, cost)
 
     run = paired if groups == 2 else general
     return natural(run(stacked(voltage), fir_taps, place, correlated))

time: 113 us -> 107 us (0.947)
  waiting for transfers between devices: 33.1 us -> 24.7 us
  starting transfers between devices: 24.6 us -> 27.5 us
  other arithmetic: 1.37 us -> 0.13 us
    ppermute x3 -> x4, waiting for transfers between devices: 19.6 us -> 10.9 us  [the longest x2 10.9 us: relayed(): lax.ppermute(two, 'stn', [(i, i + 1) for i in range(lax.axis_size('stn'))...]
    ppermute x3 -> x4, starting transfers between devices: 5.61 us -> 11.5 us  [the longest x2 7.94 us: evenly(): return (shifted(block, 'stn', 2), lax.ppermute(block, 'stn', ways))]
    ppermute x3 -> x4, waiting for transfers between devices: 6.93 us -> 1.91 us  [shifted(): lax.ppermute(block, axis, [(i, (i + distance) % size) for i in range(size)])]
    ppermute x1, waiting for transfers between devices: 3.78 us -> 7.45 us  [paired(): got_b = lax.ppermute(away_b, 'tm', [(0, 1)])]
    ppermute x3 -> x2, starting transfers between devices: 6.19 us -> 2.7 us  [farther(): lax.ppermute(block, 'stn', [(i, (i + 1 if i % 2 == 0 else i + 3) % size)...]
    ppermute x1, waiting for transfers between devices: 0.01 us -> 2.49 us  [paired(): got_c = lax.ppermute(away_c, 'tm', swap)]
    ppermute x1, starting transfers between devices: 0.01 us -> 1.85 us  [paired(): got_c = lax.ppermute(away_c, 'tm', swap)]
    add x1 -> x0, other arithmetic: 1.22 us -> none  [paired(): two_g = two_g + relayed(after(rest_g, two_g, sums))]
  transfers between devices with their start and end apart: 17 -> 18, of which waited for: 6 -> 7; matrix products, arithmetic and copies ran while one was open for 1% -> 0% of each run, Pallas kernels for 36% -> 39%
where the time goes in v14:
time: 107 us; the launch traced here: 106 us
  Pallas kernels  53 us (50%)
  starting transfers between devices  27.5 us (26%)
  waiting for transfers between devices  24.7 us (23%)
    pallas_call x3, Pallas kernels, spectra(): pl.pallas_call(functools.partial(spectra_kernel, groups, tuple((part[1:]...  30.1 us
    pallas_call x4, Pallas kernels, correlate(): pl.pallas_call(functools.partial(correlate_kernel, pieces, per_group, sca...  19.6 us
    ppermute x2, waiting for transfers between devices, relayed(): lax.ppermute(two, 'stn', [(i, i + 1) for i in range(lax.axis_size('stn'))...  10.9 us
    ppermute x2, starting transfers between devices, evenly(): return (shifted(block, 'stn', 2), lax.ppermute(block, 'stn', ways))  7.94 us
    ppermute x1, waiting for transfers between devices, paired(): got_b = lax.ppermute(away_b, 'tm', [(0, 1)])  7.45 us
    ppermute x4, starting transfers between devices, exchanged(): lax.ppermute(block, 'stn', [(i, i ^ 1) for i in range(lax.axis_size('stn'...  3.65 us
    ppermute x2, starting transfers between devices, relayed(): lax.ppermute(two, 'stn', [(i, i + 1) for i in range(lax.axis_size('stn'))...  3.54 us
    pallas_call x1, Pallas kernels, prepare(): pl.pallas_call(functools.partial(prepare_kernel, edge_block, int(groups =...  3.29 us
  transfers between devices with their start and end apart: 18, of which 7 were waited for; matrix products, arithmetic and copies ran while one was open for 0% of the time, Pallas kernels for 39%

profile of v14, /device:TPU:1, one launch (start us, length us, event | category | flops | bytes accessed | tf_op | source)
XLA Modules:
  0.0 106.2 jit_solution(16803706808765707891)
XLA Ops:
  0.0 0.1 pad_add_fusion.place
  0.1 3.3 %shard_map.46 = (bf16[8,32,64,128]{3,2,1,0:T(8,128)(2,1)S(1)}, bf16[8,8,64,128]{3,2,1,0:T(8,128)(2,1)S(1)}, f32[1024,128]{1,0:T(8,128)S(1)}, bf16[64,192]{1,0:T(...) custom-call(s32[2]{0:T(128)S(1)} %pad_add_fusion.place, bf16[8,32,64,128]{3,2,1,0:T(8,128)(2,1)} %bitcast.10, ...), custom_call_target="tpu_custom_call" | custom-call | tf_op jit(solution)/shard_map/pallas_call | solution.py:110
  3.4 2.1 %collective-permute-start.2 = (bf16[8,8,64,128]{3,2,1,0:T(8,128)(2,1)S(1)}, bf16[8,8,64,128]{3,2,1,0:T(8,128)(2,1)S(1)}, u32[]{:S(2)}, u32[]{:S(2)}) collective-permute-start(bf16[8,8,64,128]{3,2,1,0:T(8,128)(2,1)S(1)} %get-tuple-element.38), channel_id=1, source_target_pairs={{0,1},{1,0},{2,3},{3,2},{4,5},{5,4},{6,7},{7,6},{8,9},{9,8},{10,11... | collective-permute-start | bytes 3145736 | tf_op jit(solution)/shard_map/ppermute | solution.py:433
  5.5 11.3 %shard_map.47 = (bf16[32,4,16,128]{3,2,1,0:T(8,128)(2,1)S(1)}, bf16[32,4,16,128]{3,2,1,0:T(8,128)(2,1)S(1)}) custom-call(s32[2]{0:T(128)S(1)} %pad_add_fusion.place, bf16[8,32,64,128]{3,2,1,0:T(8,128)(2,1)S(1)} %get-tuple-element.28.refs_0_.refs_1_, bf16[8,32,64,128]{3,2,1,0:T(8,128)(2,1)S(1)} %get-tuple-element.28.refs_0_.refs_1_, ...), custom_call_target="tpu_custom_call" | custom-call | flops 1000000 | tf_op jit(solution)/shard_map/pallas_call | solution.py:263
  16.8 1.3 %collective-permute-start.1 = (bf16[32,4,16,128]{3,2,1,0:T(8,128)(2,1)S(1)}, bf16[32,4,16,128]{3,2,1,0:T(8,128)(2,1)S(1)}, u32[]{:S(2)}, u32[]{:S(2)}) collective-permute-start(bf16[32,4,16,128]{3,2,1,0:T(8,128)(2,1)S(1)} %get-tuple-element.34.refs_0_), channel_id=1, source_target_pairs={{0,4},{2,6},{4,8},{6,10},{8,12},{10,14},{12,16},{14,18},{16,20},{1... | collective-permute-start | bytes 1572872 | tf_op jit(solution)/shard_map/ppermute | solution.py:401
  18.1 0.3 collective-permute-start
  18.4 2.7 %collective-permute-start.5 = (bf16[32,4,16,128]{3,2,1,0:T(8,128)(2,1)S(1)}, bf16[32,4,16,128]{3,2,1,0:T(8,128)(2,1)S(1)}, u32[]{:S(2)}, u32[]{:S(2)}) collective-permute-start(bf16[32,4,16,128]{3,2,1,0:T(8,128)(2,1)S(1)} %get-tuple-element.34.refs_0_), channel_id=1, source_target_pairs={{0,2},{2,8},{4,6},{6,12},{8,10},{10,16},{12,14},{14,20},{16,18},{1... | collective-permute-start | bytes 1572872 | tf_op jit(solution)/shard_map/ppermute | solution.py:406
  21.1 12.0 %shard_map.48 = (bf16[32,4,16,128]{3,2,1,0:T(8,128)(2,1)S(1)}, bf16[32,4,16,128]{3,2,1,0:T(8,128)(2,1)}) custom-call(s32[2]{0:T(128)S(1)} %pad_add_fusion.place, bf16[8,32,64,128]{3,2,1,0:T(8,128)(2,1)S(1)} %get-tuple-element.28.refs_0_.refs_1_, bf16[8,32,64,128]{3,2,1,0:T(8,128)(2,1)S(1)} %get-tuple-element.28.refs_0_.refs_1_, ...), custom_call_target="tpu_custom_call" | custom-call | flops 1000000 | tf_op jit(solution)/shard_map/pallas_call | solution.py:263
  33.1 0.0 collective-permute-done.1.refs_2_
  33.1 0.0 collective-permute-done.2.refs_2_
  33.1 6.7 %shard_map.49 = (bf16[32,2,16,128]{3,2,1,0:T(8,128)(2,1)S(1)}, bf16[32,2,16,128]{3,2,1,0:T(8,128)(2,1)S(1)}) custom-call(s32[2]{0:T(128)S(1)} %pad_add_fusion.place, bf16[8,32,64,128]{3,2,1,0:T(8,128)(2,1)S(1)} %get-tuple-element.28.refs_0_.refs_1_, bf16[8,32,64,128]{3,2,1,0:T(8,128)(2,1)S(1)} %get-tuple-element.28.refs_0_.refs_1_, ...), custom_call_target="tpu_custom_call" | custom-call | flops 1000000 | tf_op jit(solution)/shard_map/pallas_call | solution.py:263
  39.9 0.0 copy-start
  39.9 0.7 copy-done
  40.5 0.0 collective-permute-done.refs_0_
  40.5 2.3 %collective-permute-start.4 = (bf16[32,4,16,128]{3,2,1,0:T(8,128)(2,1)S(1)}, bf16[32,4,16,128]{3,2,1,0:T(8,128)(2,1)S(1)}, u32[]{:S(2)}, u32[]{:S(2)}) collective-permute-start(bf16[32,4,16,128]{3,2,1,0:T(8,128)(2,1)S(1)} %collective-permute-done.1.refs_2_), channel_id=1, source_target_pairs={{0,2},{2,0},{4,6},{6,4},{8,10},{10,8},{12,14},{14,12},{16,18},{18,... | collective-permute-start | bytes 1572872 | tf_op jit(solution)/shard_map/ppermute | solution.py:421
  42.8 2.7 %collective-permute-start.3 = (bf16[32,4,16,128]{3,2,1,0:T(8,128)(2,1)}, bf16[32,4,16,128]{3,2,1,0:T(8,128)(2,1)}, u32[]{:S(2)}, u32[]{:S(2)}) collective-permute-start(bf16[32,4,16,128]{3,2,1,0:T(8,128)(2,1)} %get-tuple-element.43), channel_id=1, source_target_pairs={{0,1},{2,3},{4,5},{6,7},{8,9},{10,11},{12,13},{14,15},{16,17},{18,... | collective-permute-start | bytes 1572872 | tf_op jit(solution)/shard_map/ppermute | solution.py:452
  45.6 0.7 collective-permute-start.12
  46.2 0.0 copy-start.1
  46.2 0.0 collective-permute-done.5.refs_3_
  46.2 0.0 collective-permute-done.4.refs_1_
  46.2 2.7 %shard_map.50.refs_5_ = f32[4096,128]{1,0:T(8,128)S(1)} custom-call(s32[2]{0:T(128)S(1)} %pad_add_fusion.place, bf16[32,4,16,128]{3,2,1,0:T(8,128)(2,1)S(1)} %get-tuple-element.34.refs_0_, bf16[32,4,16,128]{3,2,1,0:T(8,128)(2,1)S(1)} %collective-permute-done.4.refs_1_, bf16[32,4,16,128]{3,2,1,0:T(8,128)(2,1)S(1)} %collective-permute-done.1.refs_2_, ...), custom_call_target="tpu_custom_call" | custom-call | flops 1000 | tf_op jit(solution)/shard_map/pallas_call | solution.py:373
  49.0 7.5 %collective-permute-done.3 = bf16[32,4,16,128]{3,2,1,0:T(8,128)(2,1)} collective-permute-done((bf16[32,4,16,128]{3,2,1,0:T(8,128)(2,1)}, bf16[32,4,16,128]{3,2,1,0:T(8,128)(2,1)}, u32[]{:S(2)}, u32[]{:S(2)}) %collective-permute-start.3) | collective-permute-done | bytes 524320 | tf_op jit(solution)/shard_map/ppermute | solution.py:452
  56.4 0.1 broadcast_select_fusion.refs_0_
  56.5 0.7 collective-permute-start.8
  57.2 4.1 %collective-permute-start.14 = (bf16[32,4,16,128]{3,2,1,0:T(8,128)(2,1)S(1)}, bf16[32,4,16,128]{3,2,1,0:T(8,128)(2,1)S(1)}, u32[]{:S(2)}, u32[]{:S(2)}) collective-permute-start(bf16[32,4,16,128]{3,2,1,0:T(8,128)(2,1)S(1)} %collective-permute-done.refs_0_), channel_id=1, source_target_pairs={{0,2},{2,8},{4,6},{8,10},{10,16},{12,14},{16,18},{18,24},{20,22},{... | collective-permute-start | bytes 1572872 | tf_op jit(solution)/shard_map/ppermute | solution.py:413
  61.3 0.3 collective-permute-done.12.refs_2_
  61.6 1.3 %collective-permute-start.13 = (bf16[32,4,16,128]{3,2,1,0:T(8,128)(2,1)}, bf16[32,4,16,128]{3,2,1,0:T(8,128)(2,1)S(1)}, u32[]{:S(2)}, u32[]{:S(2)}) collective-permute-start(bf16[32,4,16,128]{3,2,1,0:T(8,128)(2,1)} %collective-permute-done.12.refs_2_), channel_id=1, source_target_pairs={{0,2},{2,0},{4,6},{6,4},{8,10},{10,8},{12,14},{14,12},{16,18},{18,... | collective-permute-start | bytes 1572872 | tf_op jit(solution)/shard_map/ppermute | solution.py:421
  62.9 0.0 copy-done.1
  62.9 1.8 %collective-permute-start.6 = (bf16[32,2,16,128]{3,2,1,0:T(8,128)(2,1)S(1)}, bf16[32,2,16,128]{3,2,1,0:T(8,128)(2,1)S(1)}, u32[]{:S(2)}, u32[]{:S(2)}) collective-permute-start(bf16[32,2,16,128]{3,2,1,0:T(8,128)(2,1)S(1)} %copy-done.1), channel_id=1, source_target_pairs={{0,1},{1,0},{2,3},{3,2},{4,5},{5,4},{6,7},{7,6},{8,9},{9,8},{10,11... | collective-permute-start | bytes 786440 | tf_op jit(solution)/shard_map/ppermute | solution.py:457
  64.8 3.8 %collective-permute-start.10 = (bf16[32,4,16,128]{3,2,1,0:T(8,128)(2,1)S(1)}, bf16[32,4,16,128]{3,2,1,0:T(8,128)(2,1)S(1)}, u32[]{:S(2)}, u32[]{:S(2)}) collective-permute-start(bf16[32,4,16,128]{3,2,1,0:T(8,128)(2,1)S(1)} %broadcast_select_fusion.refs_0_), channel_id=1, source_target_pairs={{0,2},{2,8},{4,6},{8,10},{10,16},{12,14},{16,18},{18,24},{20,22},{... | collective-permute-start | bytes 1572872 | tf_op jit(solution)/shard_map/ppermute | solution.py:413
  68.6 2.5 %collective-permute-done.6 = bf16[32,2,16,128]{3,2,1,0:T(8,128)(2,1)S(1)} collective-permute-done((bf16[32,2,16,128]{3,2,1,0:T(8,128)(2,1)S(1)}, bf16[32,2,16,128]{3,2,1,0:T(8,128)(2,1)S(1)}, u32[]{:S(2)}, u32[]{:S(2)}) %collective-permute-start.6) | collective-permute-done | bytes 262176 | tf_op jit(solution)/shard_map/ppermute | solution.py:457
  71.1 2.2 %collective-permute-start.15 = (bf16[32,4,16,128]{3,2,1,0:T(8,128)(2,1)}, bf16[32,4,16,128]{3,2,1,0:T(8,128)(2,1)S(1)}, u32[]{:S(2)}, u32[]{:S(2)}) collective-permute-start(bf16[32,4,16,128]{3,2,1,0:T(8,128)(2,1)} %collective-permute-done.12.refs_2_), channel_id=1, source_target_pairs={{2,4},{10,12},{18,20},{26,28},{3,5},{11,13},{19,21},{27,29}} | collective-permute-start | bytes 1572872 | tf_op jit(solution)/shard_map/ppermute | solution.py:417
  73.3 0.0 collective-permute-done.8.refs_2_
  73.4 1.3 %collective-permute-start.11 = (bf16[32,4,16,128]{3,2,1,0:T(8,128)(2,1)S(1)}, bf16[32,4,16,128]{3,2,1,0:T(8,128)(2,1)S(1)}, u32[]{:S(2)}, u32[]{:S(2)}) collective-permute-start(bf16[32,4,16,128]{3,2,1,0:T(8,128)(2,1)S(1)} %collective-permute-done.8.refs_2_), channel_id=1, source_target_pairs={{2,4},{10,12},{18,20},{26,28},{3,5},{11,13},{19,21},{27,29}} | collective-permute-start | bytes 1572872 | tf_op jit(solution)/shard_map/ppermute | solution.py:417
  74.7 0.0 collective-permute-done.14.refs_3_
  74.7 0.1 collective-permute-start.9
  74.8 0.0 collective-permute-done.13.refs_1_
  74.8 0.1 collective-permute-start.7
  74.9 8.4 %collective-permute-done.15.refs_4_ = bf16[32,4,16,128]{3,2,1,0:T(8,128)(2,1)S(1)} collective-permute-done((bf16[32,4,16,128]{3,2,1,0:T(8,128)(2,1)}, bf16[32,4,16,128]{3,2,1,0:T(8,128)(2,1)S(1)}, u32[]{:S(2)}, u32[]{:S(2)}) %collective-permute-start.15) | collective-permute-done | bytes 524320 | tf_op jit(solution)/shard_map/ppermute | solution.py:417
  83.2 0.0 collective-permute-start.17
  83.2 5.0 %shard_map.51.refs_5_ = f32[4096,128]{1,0:T(8,128)S(1)} custom-call(s32[2]{0:T(128)S(1)} %pad_add_fusion.place, bf16[32,4,16,128]{3,2,1,0:T(8,128)(2,1)S(1)} %collective-permute-done.refs_0_, bf16[32,4,16,128]{3,2,1,0:T(8,128)(2,1)S(1)} %collective-permute-done.13.refs_1_, ...), custom_call_target="tpu_custom_call", output_to_operand_aliasing={{}: (6, {})} | custom-call | flops 1000 | tf_op jit(solution)/shard_map/pallas_call | solution.py:373
  88.3 0.0 collective-permute-done.10.refs_3_
  88.3 2.6 %collective-permute-done.11.refs_4_ = bf16[32,4,16,128]{3,2,1,0:T(8,128)(2,1)S(1)} collective-permute-done((bf16[32,4,16,128]{3,2,1,0:T(8,128)(2,1)S(1)}, bf16[32,4,16,128]{3,2,1,0:T(8,128)(2,1)S(1)}, u32[]{:S(2)}, u32[]{:S(2)}) %collective-permute-start.11) | collective-permute-done | bytes 524320 | tf_op jit(solution)/shard_map/ppermute | solution.py:417
  90.8 0.0 collective-permute-done.9.refs_1_
  90.8 4.0 %shard_map.52.refs_4_ = f32[4096,128]{1,0:T(8,128)S(1)} custom-call(s32[2]{0:T(128)S(1)} %pad_add_fusion.place, bf16[32,4,16,128]{3,2,1,0:T(8,128)(2,1)S(1)} %broadcast_select_fusion.refs_0_, bf16[32,4,16,128]{3,2,1,0:T(8,128)(2,1)S(1)} %collective-permute-done.9.refs_1_, ...), custom_call_target="tpu_custom_call", output_to_operand_aliasing={{}: (6, {})} | custom-call | flops 1000 | tf_op jit(solution)/shard_map/pallas_call | solution.py:373
  94.8 1.6 %collective-permute-done.7.refs_2_ = bf16[32,4,16,128]{3,2,1,0:T(8,128)(2,1)S(1)} collective-permute-done((bf16[32,4,16,128]{3,2,1,0:T(8,128)(2,1)S(1)}, bf16[32,4,16,128]{3,2,1,0:T(8,128)(2,1)S(1)}, u32[]{:S(2)}, u32[]{:S(2)}) %collective-permute-start.7) | collective-permute-done | bytes 524320 | tf_op jit(solution)/shard_map/ppermute | solution.py:401
  96.4 0.0 collective-permute-start.16
  96.4 0.0 collective-permute-done.17.refs_3_
  96.4 1.9 %collective-permute-done.16.refs_1_ = bf16[32,4,16,128]{3,2,1,0:T(8,128)(2,1)S(1)} collective-permute-done((bf16[32,4,16,128]{3,2,1,0:T(8,128)(2,1)S(1)}, bf16[32,4,16,128]{3,2,1,0:T(8,128)(2,1)S(1)}, u32[]{:S(2)}, u32[]{:S(2)}) %collective-permute-start.16) | collective-permute-done | bytes 524320 | tf_op jit(solution)/shard_map/ppermute | solution.py:421
  98.4 7.9 %shard_map.53 = f32[2,8,4,8,8,128]{5,4,3,2,1,0:T(8,128)} custom-call(s32[2]{0:T(128)S(1)} %pad_add_fusion.place, bf16[32,4,16,128]{3,2,1,0:T(8,128)(2,1)S(1)} %constant_dynamic-update-slice_fusion.refs_0_, bf16[32,4,16,128]{3,2,1,0:T(8,128)(2,1)S(1)} %collective-permute-done.16.refs_1_, bf16[32,4,16,128]{3,2,1,0:T(8,128)(2,1)S(1)} %collective-permute-done.7.refs_2_, ...), custom_call_target="tpu_custom_call" | custom-call | flops 1000 | tf_op jit(solution)/shard_map/pallas_call | solution.py:373
  (2 shorter events, 0.1 us)
Async XLA Ops:
  3.4 29.7 %collective-permute-start.2 = (bf16[8,8,64,128]{3,2,1,0:T(8,128)(2,1)S(1)}, bf16[8,8,64,128]{3,2,1,0:T(8,128)(2,1)S(1)}, u32[]{:S(2)}, u32[]{:S(2)}) collective-permute-start(bf16[8,8,64,128]{3,2,1,0:T(8,128)(2,1)S(1)} %get-tuple-element.38), channel_id=1, source_target_pairs={{0,1},{1,0},{2,3},{3,2},{4,5},{5,4},{6,7},{7,6},{8,9},{9,8},{10,11... | collective-permute-start | bytes 3145736 | tf_op jit(solution)/shard_map/ppermute | solution.py:433
  16.8 16.3 %collective-permute-start.1 = (bf16[32,4,16,128]{3,2,1,0:T(8,128)(2,1)S(1)}, bf16[32,4,16,128]{3,2,1,0:T(8,128)(2,1)S(1)}, u32[]{:S(2)}, u32[]{:S(2)}) collective-permute-start(bf16[32,4,16,128]{3,2,1,0:T(8,128)(2,1)S(1)} %get-tuple-element.34.refs_0_), channel_id=1, source_target_pairs={{0,4},{2,6},{4,8},{6,10},{8,12},{10,14},{12,16},{14,18},{16,20},{1... | collective-permute-start | bytes 1572872 | tf_op jit(solution)/shard_map/ppermute | solution.py:401
  18.1 22.4 %collective-permute-start = (bf16[32,4,16,128]{3,2,1,0:T(8,128)(2,1)S(1)}, bf16[32,4,16,128]{3,2,1,0:T(8,128)(2,1)S(1)}, u32[]{:S(2)}, u32[]{:S(2)}) collective-permute-start(bf16[32,4,16,128]{3,2,1,0:T(8,128)(2,1)S(1)} %get-tuple-element.33), channel_id=1, source_target_pairs={{0,1},{1,0},{2,3},{3,2},{4,5},{5,4},{6,7},{7,6},{8,9},{9,8},{10,11... | collective-permute-start | bytes 1572872 | tf_op jit(solution)/shard_map/ppermute | solution.py:437
  18.4 27.9 %collective-permute-start.5 = (bf16[32,4,16,128]{3,2,1,0:T(8,128)(2,1)S(1)}, bf16[32,4,16,128]{3,2,1,0:T(8,128)(2,1)S(1)}, u32[]{:S(2)}, u32[]{:S(2)}) collective-permute-start(bf16[32,4,16,128]{3,2,1,0:T(8,128)(2,1)S(1)} %get-tuple-element.34.refs_0_), channel_id=1, source_target_pairs={{0,2},{2,8},{4,6},{6,12},{8,10},{10,16},{12,14},{14,20},{16,18},{1... | collective-permute-start | bytes 1572872 | tf_op jit(solution)/shard_map/ppermute | solution.py:406
  39.9 0.7 copy-start
  40.5 5.7 %collective-permute-start.4 = (bf16[32,4,16,128]{3,2,1,0:T(8,128)(2,1)S(1)}, bf16[32,4,16,128]{3,2,1,0:T(8,128)(2,1)S(1)}, u32[]{:S(2)}, u32[]{:S(2)}) collective-permute-start(bf16[32,4,16,128]{3,2,1,0:T(8,128)(2,1)S(1)} %collective-permute-done.1.refs_2_), channel_id=1, source_target_pairs={{0,2},{2,0},{4,6},{6,4},{8,10},{10,8},{12,14},{14,12},{16,18},{18,... | collective-permute-start | bytes 1572872 | tf_op jit(solution)/shard_map/ppermute | solution.py:421
  42.8 13.6 %collective-permute-start.3 = (bf16[32,4,16,128]{3,2,1,0:T(8,128)(2,1)}, bf16[32,4,16,128]{3,2,1,0:T(8,128)(2,1)}, u32[]{:S(2)}, u32[]{:S(2)}) collective-permute-start(bf16[32,4,16,128]{3,2,1,0:T(8,128)(2,1)} %get-tuple-element.43), channel_id=1, source_target_pairs={{0,1},{2,3},{4,5},{6,7},{8,9},{10,11},{12,13},{14,15},{16,17},{18,... | collective-permute-start | bytes 1572872 | tf_op jit(solution)/shard_map/ppermute | solution.py:452
  45.6 16.0 %collective-permute-start.12 = (bf16[32,4,16,128]{3,2,1,0:T(8,128)(2,1)S(1)}, bf16[32,4,16,128]{3,2,1,0:T(8,128)(2,1)}, u32[]{:S(2)}, u32[]{:S(2)}) collective-permute-start(bf16[32,4,16,128]{3,2,1,0:T(8,128)(2,1)S(1)} %collective-permute-done.refs_0_), channel_id=1, source_target_pairs={{0,4},{2,6},{4,8},{6,10},{8,12},{10,14},{12,16},{14,18},{16,20},{1... | collective-permute-start | bytes 1572872 | tf_op jit(solution)/shard_map/ppermute | solution.py:401
  46.2 16.7 %copy-start.1 = (bf16[32,2,16,128]{3,2,1,0:T(8,128)(2,1)S(1)}, bf16[32,2,16,128]{3,2,1,0:T(8,128)(2,1)}, u32[]{:S(2)}) copy-start(bf16[32,2,16,128]{3,2,1,0:T(8,128)(2,1)} %copy-done) | copy-start | bytes 786436
  56.5 16.9 %collective-permute-start.8 = (bf16[32,4,16,128]{3,2,1,0:T(8,128)(2,1)S(1)}, bf16[32,4,16,128]{3,2,1,0:T(8,128)(2,1)S(1)}, u32[]{:S(2)}, u32[]{:S(2)}) collective-permute-start(bf16[32,4,16,128]{3,2,1,0:T(8,128)(2,1)S(1)} %broadcast_select_fusion.refs_0_), channel_id=1, source_target_pairs={{0,4},{2,6},{4,8},{6,10},{8,12},{10,14},{12,16},{14,18},{16,20},{1... | collective-permute-start | bytes 1572872 | tf_op jit(solution)/shard_map/ppermute | solution.py:401
  57.2 17.5 %collective-permute-start.14 = (bf16[32,4,16,128]{3,2,1,0:T(8,128)(2,1)S(1)}, bf16[32,4,16,128]{3,2,1,0:T(8,128)(2,1)S(1)}, u32[]{:S(2)}, u32[]{:S(2)}) collective-permute-start(bf16[32,4,16,128]{3,2,1,0:T(8,128)(2,1)S(1)} %collective-permute-done.refs_0_), channel_id=1, source_target_pairs={{0,2},{2,8},{4,6},{8,10},{10,16},{12,14},{16,18},{18,24},{20,22},{... | collective-permute-start | bytes 1572872 | tf_op jit(solution)/shard_map/ppermute | solution.py:413
  61.6 13.2 %collective-permute-start.13 = (bf16[32,4,16,128]{3,2,1,0:T(8,128)(2,1)}, bf16[32,4,16,128]{3,2,1,0:T(8,128)(2,1)S(1)}, u32[]{:S(2)}, u32[]{:S(2)}) collective-permute-start(bf16[32,4,16,128]{3,2,1,0:T(8,128)(2,1)} %collective-permute-done.12.refs_2_), channel_id=1, source_target_pairs={{0,2},{2,0},{4,6},{6,4},{8,10},{10,8},{12,14},{14,12},{16,18},{18,... | collective-permute-start | bytes 1572872 | tf_op jit(solution)/shard_map/ppermute | solution.py:421
  62.9 8.2 %collective-permute-start.6 = (bf16[32,2,16,128]{3,2,1,0:T(8,128)(2,1)S(1)}, bf16[32,2,16,128]{3,2,1,0:T(8,128)(2,1)S(1)}, u32[]{:S(2)}, u32[]{:S(2)}) collective-permute-start(bf16[32,2,16,128]{3,2,1,0:T(8,128)(2,1)S(1)} %copy-done.1), channel_id=1, source_target_pairs={{0,1},{1,0},{2,3},{3,2},{4,5},{5,4},{6,7},{7,6},{8,9},{9,8},{10,11... | collective-permute-start | bytes 786440 | tf_op jit(solution)/shard_map/ppermute | solution.py:457
  64.8 23.5 %collective-permute-start.10 = (bf16[32,4,16,128]{3,2,1,0:T(8,128)(2,1)S(1)}, bf16[32,4,16,128]{3,2,1,0:T(8,128)(2,1)S(1)}, u32[]{:S(2)}, u32[]{:S(2)}) collective-permute-start(bf16[32,4,16,128]{3,2,1,0:T(8,128)(2,1)S(1)} %broadcast_select_fusion.refs_0_), channel_id=1, source_target_pairs={{0,2},{2,8},{4,6},{8,10},{10,16},{12,14},{16,18},{18,24},{20,22},{... | collective-permute-start | bytes 1572872 | tf_op jit(solution)/shard_map/ppermute | solution.py:413
  71.1 12.2 %collective-permute-start.15 = (bf16[32,4,16,128]{3,2,1,0:T(8,128)(2,1)}, bf16[32,4,16,128]{3,2,1,0:T(8,128)(2,1)S(1)}, u32[]{:S(2)}, u32[]{:S(2)}) collective-permute-start(bf16[32,4,16,128]{3,2,1,0:T(8,128)(2,1)} %collective-permute-done.12.refs_2_), channel_id=1, source_target_pairs={{2,4},{10,12},{18,20},{26,28},{3,5},{11,13},{19,21},{27,29}} | collective-permute-start | bytes 1572872 | tf_op jit(solution)/shard_map/ppermute | solution.py:417
  73.4 17.5 %collective-permute-start.11 = (bf16[32,4,16,128]{3,2,1,0:T(8,128)(2,1)S(1)}, bf16[32,4,16,128]{3,2,1,0:T(8,128)(2,1)S(1)}, u32[]{:S(2)}, u32[]{:S(2)}) collective-permute-start(bf16[32,4,16,128]{3,2,1,0:T(8,128)(2,1)S(1)} %collective-permute-done.8.refs_2_), channel_id=1, source_target_pairs={{2,4},{10,12},{18,20},{26,28},{3,5},{11,13},{19,21},{27,29}} | collective-permute-start | bytes 1572872 | tf_op jit(solution)/shard_map/ppermute | solution.py:417
  74.7 16.1 %collective-permute-start.9 = (bf16[32,4,16,128]{3,2,1,0:T(8,128)(2,1)S(1)}, bf16[32,4,16,128]{3,2,1,0:T(8,128)(2,1)S(1)}, u32[]{:S(2)}, u32[]{:S(2)}) collective-permute-start(bf16[32,4,16,128]{3,2,1,0:T(8,128)(2,1)S(1)} %collective-permute-done.8.refs_2_), channel_id=1, source_target_pairs={{0,2},{2,0},{4,6},{6,4},{8,10},{10,8},{12,14},{14,12},{16,18},{18,... | collective-permute-start | bytes 1572872 | tf_op jit(solution)/shard_map/ppermute | solution.py:421
  74.8 21.7 %collective-permute-start.7 = (bf16[32,4,16,128]{3,2,1,0:T(8,128)(2,1)S(1)}, bf16[32,4,16,128]{3,2,1,0:T(8,128)(2,1)S(1)}, u32[]{:S(2)}, u32[]{:S(2)}) collective-permute-start(bf16[32,4,16,128]{3,2,1,0:T(8,128)(2,1)S(1)} %constant_dynamic-update-slice_fusion.refs_0_), channel_id=1, source_target_pairs={{0,4},{2,6},{4,8},{6,10},{8,12},{10,14},{12,16},{14,18},{16,20},{1... | collective-permute-start | bytes 1572872 | tf_op jit(solution)/shard_map/ppermute | solution.py:401
  83.2 13.2 %collective-permute-start.17 = (bf16[32,4,16,128]{3,2,1,0:T(8,128)(2,1)S(1)}, bf16[32,4,16,128]{3,2,1,0:T(8,128)(2,1)S(1)}, u32[]{:S(2)}, u32[]{:S(2)}) collective-permute-start(bf16[32,4,16,128]{3,2,1,0:T(8,128)(2,1)S(1)} %constant_dynamic-update-slice_fusion.refs_0_), channel_id=1, source_target_pairs={{0,2},{2,8},{4,6},{6,12},{8,10},{10,16},{12,14},{14,20},{16,18},{1... | collective-permute-start | bytes 1572872 | tf_op jit(solution)/shard_map/ppermute | solution.py:406
  96.4 1.9 %collective-permute-start.16 = (bf16[32,4,16,128]{3,2,1,0:T(8,128)(2,1)S(1)}, bf16[32,4,16,128]{3,2,1,0:T(8,128)(2,1)S(1)}, u32[]{:S(2)}, u32[]{:S(2)}) collective-permute-start(bf16[32,4,16,128]{3,2,1,0:T(8,128)(2,1)S(1)} %collective-permute-done.7.refs_2_), channel_id=1, source_target_pairs={{0,2},{2,0},{4,6},{6,4},{8,10},{10,8},{12,14},{14,12},{16,18},{18,... | collective-permute-start | bytes 1572872 | tf_op jit(solution)/shard_map/ppermute | solution.py:421

commit v15 on v14

--- a/solution.py
+++ b/solution.py
@@ -370,7 +370,7 @@
     shape = (2, signals, VISITS, per_group // 4, SUB, LANES) if last else (rows, LANES)
     operands = list(arrays) + ([] if before is None else [before])
     vmem = pl.BlockSpec(memory_space=pltpu.VMEM)
-    return pl.pallas_call(
+    result = pl.pallas_call(
         functools.partial(correlate_kernel, pieces, per_group, scale, before is not None, last),
         grid_spec=pltpu.PrefetchScalarGridSpec(
             num_scalar_prefetch=1,
@@ -384,6 +384,7 @@
         input_output_aliases={} if before is None or last else {len(operands): 0},
         cost_estimate=pl.CostEstimate(flops=cost, bytes_accessed=0, transcendentals=0),
     )(place, *operands)
+    return result if last else pltpu.with_memory_space_constraint(result, pltpu.VMEM)
 
 
 def stacked(voltage):
@@ -456,14 +457,14 @@
     got_b, away_c, sums = lax.optimization_barrier((got_b, away_c, sums))
     got_c = lax.ppermute(away_c, "tm", swap)
     piece_b = jnp.where(me == 0, own_b, got_b)
-    two_b, rest_b = evenly(piece_b)
+    two_b, rest_b = farther(piece_b)
     pair_g, relay_g = exchanged(two_g), relayed(two_g)
     sums = correlated([got_a, pair_g, two_g, (rest_g, relay_g)], first, sums, False)
-    piece_c = jnp.concatenate([own_c, got_c], axis=1)
+    piece_c = jnp.concatenate([after(own_c, relay_g), got_c], axis=1)
     two_c, rest_c = farther(piece_c)
-    pair_b, relay_b = exchanged(two_b), relayed(two_b)
-    sums = correlated([piece_b, pair_b, two_b, (rest_b, relay_b)], first, sums, False)
-    pair_c = exchanged(after(two_c, sums))
+    pair_b = exchanged(two_b)
+    sums = correlated([piece_b, pair_b, two_b, rest_b], first, sums, False)
+    pair_c = exchanged(after(two_c, rest_c, sums))
     return correlated([piece_c, pair_c, two_c, rest_c], [(few, [(0, 0, 0), (0, 0, few)])], sums, True)
 
 

time: 107 us -> 114 us (1.065)
  waiting for transfers between devices: 24.7 us -> 39 us
  starting transfers between devices: 27.5 us -> 20.7 us
    ppermute x4, waiting for transfers between devices: 1.91 us -> 22.3 us  [shifted(): lax.ppermute(block, axis, [(i, (i + distance) % size) for i in range(size)])]
    ppermute x2 -> x1, starting transfers between devices: 7.94 us -> 2.37 us  [evenly(): return (shifted(block, 'stn', 2), lax.ppermute(block, 'stn', ways))]
    ppermute x2 -> x1, waiting for transfers between devices: 10.9 us -> 7.34 us  [relayed(): lax.ppermute(two, 'stn', [(i, i + 1) for i in range(lax.axis_size('stn'))...]
    ppermute x1, waiting for transfers between devices: 2.49 us -> 0.01 us  [paired(): got_c = lax.ppermute(away_c, 'tm', swap)]
    ppermute x2 -> x1, starting transfers between devices: 3.54 us -> 1.31 us  [relayed(): lax.ppermute(two, 'stn', [(i, i + 1) for i in range(lax.axis_size('stn'))...]
    ppermute x2 -> x3, starting transfers between devices: 2.7 us -> 4.39 us  [farther(): lax.ppermute(block, 'stn', [(i, (i + 1 if i % 2 == 0 else i + 3) % size)...]
    ppermute x4, starting transfers between devices: 2.69 us -> 4.18 us  [shifted(): lax.ppermute(block, axis, [(i, (i + distance) % size) for i in range(size)])]
    ppermute x1, starting transfers between devices: 1.85 us -> 0.5 us  [paired(): got_c = lax.ppermute(away_c, 'tm', swap)]
  transfers between devices with their start and end apart: 18 -> 17, of which waited for: 7 -> 6; matrix products, arithmetic and copies ran while one was open for 0% -> 0% of each run, Pallas kernels for 39% -> 37%
where the time goes in v15:
time: 114 us
  Pallas kernels  53 us (46%)
  waiting for transfers between devices  39 us (34%)
  starting transfers between devices  20.7 us (18%)
    pallas_call x3, Pallas kernels, spectra(): pl.pallas_call(functools.partial(spectra_kernel, groups, tuple((part[1:]...  30.1 us
    ppermute x4, waiting for transfers between devices, shifted(): lax.ppermute(block, axis, [(i, (i + distance) % size) for i in range(size)])  22.3 us
    pallas_call x4, Pallas kernels, correlate(): pl.pallas_call(functools.partial(correlate_kernel, pieces, per_group, sca...  19.6 us
    ppermute x1, waiting for transfers between devices, paired(): got_b = lax.ppermute(away_b, 'tm', [(0, 1)])  7.45 us
    ppermute x1, waiting for transfers between devices, relayed(): lax.ppermute(two, 'stn', [(i, i + 1) for i in range(lax.axis_size('stn'))...  7.34 us
    ppermute x3, starting transfers between devices, farther(): lax.ppermute(block, 'stn', [(i, (i + 1 if i % 2 == 0 else i + 3) % size)...  4.39 us
    ppermute x4, starting transfers between devices, shifted(): lax.ppermute(block, axis, [(i, (i + distance) % size) for i in range(size)])  4.18 us
    pallas_call x1, Pallas kernels, prepare(): pl.pallas_call(functools.partial(prepare_kernel, edge_block, int(groups =...  3.29 us
  transfers between devices with their start and end apart: 17, of which 6 were waited for; matrix products, arithmetic and copies ran while one was open for 0% of the time, Pallas kernels for 37%

profile of v15, /device:TPU:1, one launch (start us, length us, event | category | flops | bytes accessed | tf_op | source)
XLA Modules:
  0.0 113.8 jit_solution(10538361135259361787)
XLA Ops:
  0.0 0.1 pad_add_fusion.place
  0.1 3.3 %shard_map.46 = (bf16[8,32,64,128]{3,2,1,0:T(8,128)(2,1)S(1)}, bf16[8,8,64,128]{3,2,1,0:T(8,128)(2,1)S(1)}, f32[1024,128]{1,0:T(8,128)S(1)}, bf16[64,192]{1,0:T(...) custom-call(s32[2]{0:T(128)S(1)} %pad_add_fusion.place, bf16[8,32,64,128]{3,2,1,0:T(8,128)(2,1)} %bitcast.10, ...), custom_call_target="tpu_custom_call" | custom-call | tf_op jit(solution)/shard_map/pallas_call | solution.py:110
  3.4 2.1 %collective-permute-start.2 = (bf16[8,8,64,128]{3,2,1,0:T(8,128)(2,1)S(1)}, bf16[8,8,64,128]{3,2,1,0:T(8,128)(2,1)S(1)}, u32[]{:S(2)}, u32[]{:S(2)}) collective-permute-start(bf16[8,8,64,128]{3,2,1,0:T(8,128)(2,1)S(1)} %get-tuple-element.39), channel_id=1, source_target_pairs={{0,1},{1,0},{2,3},{3,2},{4,5},{5,4},{6,7},{7,6},{8,9},{9,8},{10,11... | collective-permute-start | bytes 3145736 | tf_op jit(solution)/shard_map/ppermute | solution.py:434
  5.5 11.3 %shard_map.47 = (bf16[32,4,16,128]{3,2,1,0:T(8,128)(2,1)S(1)}, bf16[32,4,16,128]{3,2,1,0:T(8,128)(2,1)S(1)}) custom-call(s32[2]{0:T(128)S(1)} %pad_add_fusion.place, bf16[8,32,64,128]{3,2,1,0:T(8,128)(2,1)S(1)} %get-tuple-element.29.refs_0_.refs_1_, bf16[8,32,64,128]{3,2,1,0:T(8,128)(2,1)S(1)} %get-tuple-element.29.refs_0_.refs_1_, ...), custom_call_target="tpu_custom_call" | custom-call | flops 1000000 | tf_op jit(solution)/shard_map/pallas_call | solution.py:263
  16.8 1.3 %collective-permute-start.1 = (bf16[32,4,16,128]{3,2,1,0:T(8,128)(2,1)S(1)}, bf16[32,4,16,128]{3,2,1,0:T(8,128)(2,1)S(1)}, u32[]{:S(2)}, u32[]{:S(2)}) collective-permute-start(bf16[32,4,16,128]{3,2,1,0:T(8,128)(2,1)S(1)} %get-tuple-element.35.refs_0_), channel_id=1, source_target_pairs={{0,4},{2,6},{4,8},{6,10},{8,12},{10,14},{12,16},{14,18},{16,20},{1... | collective-permute-start | bytes 1572872 | tf_op jit(solution)/shard_map/ppermute | solution.py:402
  18.1 0.3 collective-permute-start
  18.4 2.7 %collective-permute-start.7 = (bf16[32,4,16,128]{3,2,1,0:T(8,128)(2,1)S(1)}, bf16[32,4,16,128]{3,2,1,0:T(8,128)(2,1)S(1)}, u32[]{:S(2)}, u32[]{:S(2)}) collective-permute-start(bf16[32,4,16,128]{3,2,1,0:T(8,128)(2,1)S(1)} %get-tuple-element.35.refs_0_), channel_id=1, source_target_pairs={{0,2},{2,8},{4,6},{6,12},{8,10},{10,16},{12,14},{14,20},{16,18},{1... | collective-permute-start | bytes 1572872 | tf_op jit(solution)/shard_map/ppermute | solution.py:407
  21.1 12.0 %shard_map.48 = (bf16[32,4,16,128]{3,2,1,0:T(8,128)(2,1)S(1)}, bf16[32,4,16,128]{3,2,1,0:T(8,128)(2,1)}) custom-call(s32[2]{0:T(128)S(1)} %pad_add_fusion.place, bf16[8,32,64,128]{3,2,1,0:T(8,128)(2,1)S(1)} %get-tuple-element.29.refs_0_.refs_1_, bf16[8,32,64,128]{3,2,1,0:T(8,128)(2,1)S(1)} %get-tuple-element.29.refs_0_.refs_1_, ...), custom_call_target="tpu_custom_call" | custom-call | flops 1000000 | tf_op jit(solution)/shard_map/pallas_call | solution.py:263
  33.1 0.0 collective-permute-done.1.refs_2_
  33.1 0.0 collective-permute-done.2.refs_2_
  33.1 6.7 %shard_map.49 = (bf16[32,2,16,128]{3,2,1,0:T(8,128)(2,1)S(1)}, bf16[32,2,16,128]{3,2,1,0:T(8,128)(2,1)S(1)}) custom-call(s32[2]{0:T(128)S(1)} %pad_add_fusion.place, bf16[8,32,64,128]{3,2,1,0:T(8,128)(2,1)S(1)} %get-tuple-element.29.refs_0_.refs_1_, bf16[8,32,64,128]{3,2,1,0:T(8,128)(2,1)S(1)} %get-tuple-element.29.refs_0_.refs_1_, ...), custom_call_target="tpu_custom_call" | custom-call | flops 1000000 | tf_op jit(solution)/shard_map/pallas_call | solution.py:263
  39.9 0.0 copy-start
  39.9 0.7 copy-done
  40.6 0.0 collective-permute-done.refs_0_
  40.6 2.3 %collective-permute-start.6 = (bf16[32,4,16,128]{3,2,1,0:T(8,128)(2,1)S(1)}, bf16[32,4,16,128]{3,2,1,0:T(8,128)(2,1)S(1)}, u32[]{:S(2)}, u32[]{:S(2)}) collective-permute-start(bf16[32,4,16,128]{3,2,1,0:T(8,128)(2,1)S(1)} %collective-permute-done.1.refs_2_), channel_id=1, source_target_pairs={{0,2},{2,0},{4,6},{6,4},{8,10},{10,8},{12,14},{14,12},{16,18},{18,... | collective-permute-start | bytes 1572872 | tf_op jit(solution)/shard_map/ppermute | solution.py:422
  42.8 2.7 %collective-permute-start.5 = (bf16[32,4,16,128]{3,2,1,0:T(8,128)(2,1)}, bf16[32,4,16,128]{3,2,1,0:T(8,128)(2,1)}, u32[]{:S(2)}, u32[]{:S(2)}) collective-permute-start(bf16[32,4,16,128]{3,2,1,0:T(8,128)(2,1)} %get-tuple-element.46), channel_id=1, source_target_pairs={{0,1},{2,3},{4,5},{6,7},{8,9},{10,11},{12,13},{14,15},{16,17},{18,... | collective-permute-start | bytes 1572872 | tf_op jit(solution)/shard_map/ppermute | solution.py:453
  45.6 0.6 collective-permute-start.3
  46.2 0.0 copy-start.1
  46.2 0.0 collective-permute-done.7.refs_3_
  46.2 0.0 collective-permute-done.6.refs_1_
  46.2 2.7 %shard_map.50.refs_5_ = f32[4096,128]{1,0:T(8,128)S(1)} custom-call(s32[2]{0:T(128)S(1)} %pad_add_fusion.place, bf16[32,4,16,128]{3,2,1,0:T(8,128)(2,1)S(1)} %get-tuple-element.35.refs_0_, bf16[32,4,16,128]{3,2,1,0:T(8,128)(2,1)S(1)} %collective-permute-done.6.refs_1_, bf16[32,4,16,128]{3,2,1,0:T(8,128)(2,1)S(1)} %collective-permute-done.1.refs_2_, ...), custom_call_target="tpu_custom_call" | custom-call | flops 1000 | tf_op jit(solution)/shard_map/pallas_call | solution.py:373
  49.0 7.4 %collective-permute-done.5 = bf16[32,4,16,128]{3,2,1,0:T(8,128)(2,1)} collective-permute-done((bf16[32,4,16,128]{3,2,1,0:T(8,128)(2,1)}, bf16[32,4,16,128]{3,2,1,0:T(8,128)(2,1)}, u32[]{:S(2)}, u32[]{:S(2)}) %collective-permute-start.5) | collective-permute-done | bytes 524320 | tf_op jit(solution)/shard_map/ppermute | solution.py:453
  56.4 5.2 %collective-permute-done.3.refs_2_ = bf16[32,4,16,128]{3,2,1,0:T(8,128)(2,1)} collective-permute-done((bf16[32,4,16,128]{3,2,1,0:T(8,128)(2,1)S(1)}, bf16[32,4,16,128]{3,2,1,0:T(8,128)(2,1)}, u32[]{:S(2)}, u32[]{:S(2)}) %collective-permute-start.3) | collective-permute-done | bytes 524320 | tf_op jit(solution)/shard_map/ppermute | solution.py:402
  61.6 1.3 %collective-permute-start.4 = (bf16[32,4,16,128]{3,2,1,0:T(8,128)(2,1)}, bf16[32,4,16,128]{3,2,1,0:T(8,128)(2,1)S(1)}, u32[]{:S(2)}, u32[]{:S(2)}) collective-permute-start(bf16[32,4,16,128]{3,2,1,0:T(8,128)(2,1)} %collective-permute-done.3.refs_2_), channel_id=1, source_target_pairs={{2,4},{10,12},{18,20},{26,28},{3,5},{11,13},{19,21},{27,29}} | collective-permute-start | bytes 1572872 | tf_op jit(solution)/shard_map/ppermute | solution.py:418
  62.9 0.1 broadcast_select_fusion.refs_0_
  63.0 0.1 collective-permute-start.11
  63.1 2.4 %collective-permute-start.15 = (bf16[32,4,16,128]{3,2,1,0:T(8,128)(2,1)S(1)}, bf16[32,4,16,128]{3,2,1,0:T(8,128)(2,1)S(1)}, u32[]{:S(2)}, u32[]{:S(2)}) collective-permute-start(bf16[32,4,16,128]{3,2,1,0:T(8,128)(2,1)S(1)} %collective-permute-done.refs_0_), channel_id=1, source_target_pairs={{0,2},{2,8},{4,6},{8,10},{10,16},{12,14},{16,18},{18,24},{20,22},{... | collective-permute-start | bytes 1572872 | tf_op jit(solution)/shard_map/ppermute | solution.py:414
  65.5 0.0 copy-done.1
  65.5 0.5 collective-permute-start.8
  66.0 1.1 collective-permute-start.13
  67.0 7.3 %collective-permute-done.4.refs_4_ = bf16[32,4,16,128]{3,2,1,0:T(8,128)(2,1)S(1)} collective-permute-done((bf16[32,4,16,128]{3,2,1,0:T(8,128)(2,1)}, bf16[32,4,16,128]{3,2,1,0:T(8,128)(2,1)S(1)}, u32[]{:S(2)}, u32[]{:S(2)}) %collective-permute-start.4) | collective-permute-done | bytes 524320 | tf_op jit(solution)/shard_map/ppermute | solution.py:418
  74.4 0.0 collective-permute-start.14
  74.4 6.1 %collective-permute-done.11.refs_2_ = bf16[32,4,16,128]{3,2,1,0:T(8,128)(2,1)S(1)} collective-permute-done((bf16[32,4,16,128]{3,2,1,0:T(8,128)(2,1)S(1)}, bf16[32,4,16,128]{3,2,1,0:T(8,128)(2,1)S(1)}, u32[]{:S(2)}, u32[]{:S(2)}) %collective-permute-start.11) | collective-permute-done | bytes 524320 | tf_op jit(solution)/shard_map/ppermute | solution.py:402
  80.5 0.6 collective-permute-start.12
  81.0 0.0 collective-permute-done.8
  81.1 0.6 collective-permute-start.10
  81.7 0.0 collective-permute-done.15.refs_3_
  81.7 2.2 %collective-permute-start.9 = (bf16[32,4,16,128]{3,2,1,0:T(8,128)(2,1)S(1)}, bf16[32,4,16,128]{3,2,1,0:T(8,128)(2,1)S(1)}, u32[]{:S(2)}, u32[]{:S(2)}) collective-permute-start(bf16[32,4,16,128]{3,2,1,0:T(8,128)(2,1)S(1)} %constant_dynamic-update-slice_fusion.refs_0_), channel_id=1, source_target_pairs={{0,4},{2,6},{4,8},{6,10},{8,12},{10,14},{12,16},{14,18},{16,20},{1... | collective-permute-start | bytes 1572872 | tf_op jit(solution)/shard_map/ppermute | solution.py:402
  83.9 0.0 collective-permute-done.14.refs_1_
  83.9 5.0 %shard_map.51.refs_4_ = f32[4096,128]{1,0:T(8,128)S(1)} custom-call(s32[2]{0:T(128)S(1)} %pad_add_fusion.place, bf16[32,4,16,128]{3,2,1,0:T(8,128)(2,1)S(1)} %collective-permute-done.refs_0_, bf16[32,4,16,128]{3,2,1,0:T(8,128)(2,1)S(1)} %collective-permute-done.14.refs_1_, ...), custom_call_target="tpu_custom_call", output_to_operand_aliasing={{}: (6, {})} | custom-call | flops 1000 | tf_op jit(solution)/shard_map/pallas_call | solution.py:373
  89.0 0.0 collective-permute-done.13.refs_3_
  89.0 0.0 collective-permute-done.12.refs_1_
  89.0 4.0 %shard_map.52.refs_4_ = f32[4096,128]{1,0:T(8,128)S(1)} custom-call(s32[2]{0:T(128)S(1)} %pad_add_fusion.place, bf16[32,4,16,128]{3,2,1,0:T(8,128)(2,1)S(1)} %broadcast_select_fusion.refs_0_, bf16[32,4,16,128]{3,2,1,0:T(8,128)(2,1)S(1)} %collective-permute-done.12.refs_1_, ...), custom_call_target="tpu_custom_call", output_to_operand_aliasing={{}: (5, {})} | custom-call | flops 1000 | tf_op jit(solution)/shard_map/pallas_call | solution.py:373
  93.0 0.0 collective-permute-done.10.refs_3_
  93.0 11.0 %collective-permute-done.9.refs_2_ = bf16[32,4,16,128]{3,2,1,0:T(8,128)(2,1)S(1)} collective-permute-done((bf16[32,4,16,128]{3,2,1,0:T(8,128)(2,1)S(1)}, bf16[32,4,16,128]{3,2,1,0:T(8,128)(2,1)S(1)}, u32[]{:S(2)}, u32[]{:S(2)}) %collective-permute-start.9) | collective-permute-done | bytes 524320 | tf_op jit(solution)/shard_map/ppermute | solution.py:402
  104.0 0.0 collective-permute-start.16
  104.0 1.9 %collective-permute-done.16.refs_1_ = bf16[32,4,16,128]{3,2,1,0:T(8,128)(2,1)S(1)} collective-permute-done((bf16[32,4,16,128]{3,2,1,0:T(8,128)(2,1)S(1)}, bf16[32,4,16,128]{3,2,1,0:T(8,128)(2,1)S(1)}, u32[]{:S(2)}, u32[]{:S(2)}) %collective-permute-start.16) | collective-permute-done | bytes 524320 | tf_op jit(solution)/shard_map/ppermute | solution.py:422
  105.9 7.9 %shard_map.53 = f32[2,8,4,8,8,128]{5,4,3,2,1,0:T(8,128)} custom-call(s32[2]{0:T(128)S(1)} %pad_add_fusion.place, bf16[32,4,16,128]{3,2,1,0:T(8,128)(2,1)S(1)} %constant_dynamic-update-slice_fusion.refs_0_, bf16[32,4,16,128]{3,2,1,0:T(8,128)(2,1)S(1)} %collective-permute-done.16.refs_1_, bf16[32,4,16,128]{3,2,1,0:T(8,128)(2,1)S(1)} %collective-permute-done.9.refs_2_, ...), custom_call_target="tpu_custom_call" | custom-call | flops 1000 | tf_op jit(solution)/shard_map/pallas_call | solution.py:373
  (2 shorter events, 0.1 us)
Async XLA Ops:
  3.4 29.7 %collective-permute-start.2 = (bf16[8,8,64,128]{3,2,1,0:T(8,128)(2,1)S(1)}, bf16[8,8,64,128]{3,2,1,0:T(8,128)(2,1)S(1)}, u32[]{:S(2)}, u32[]{:S(2)}) collective-permute-start(bf16[8,8,64,128]{3,2,1,0:T(8,128)(2,1)S(1)} %get-tuple-element.39), channel_id=1, source_target_pairs={{0,1},{1,0},{2,3},{3,2},{4,5},{5,4},{6,7},{7,6},{8,9},{9,8},{10,11... | collective-permute-start | bytes 3145736 | tf_op jit(solution)/shard_map/ppermute | solution.py:434
  16.8 16.3 %collective-permute-start.1 = (bf16[32,4,16,128]{3,2,1,0:T(8,128)(2,1)S(1)}, bf16[32,4,16,128]{3,2,1,0:T(8,128)(2,1)S(1)}, u32[]{:S(2)}, u32[]{:S(2)}) collective-permute-start(bf16[32,4,16,128]{3,2,1,0:T(8,128)(2,1)S(1)} %get-tuple-element.35.refs_0_), channel_id=1, source_target_pairs={{0,4},{2,6},{4,8},{6,10},{8,12},{10,14},{12,16},{14,18},{16,20},{1... | collective-permute-start | bytes 1572872 | tf_op jit(solution)/shard_map/ppermute | solution.py:402
  18.1 22.4 %collective-permute-start = (bf16[32,4,16,128]{3,2,1,0:T(8,128)(2,1)S(1)}, bf16[32,4,16,128]{3,2,1,0:T(8,128)(2,1)S(1)}, u32[]{:S(2)}, u32[]{:S(2)}) collective-permute-start(bf16[32,4,16,128]{3,2,1,0:T(8,128)(2,1)S(1)} %get-tuple-element.34), channel_id=1, source_target_pairs={{0,1},{1,0},{2,3},{3,2},{4,5},{5,4},{6,7},{7,6},{8,9},{9,8},{10,11... | collective-permute-start | bytes 1572872 | tf_op jit(solution)/shard_map/ppermute | solution.py:438
  18.4 27.9 %collective-permute-start.7 = (bf16[32,4,16,128]{3,2,1,0:T(8,128)(2,1)S(1)}, bf16[32,4,16,128]{3,2,1,0:T(8,128)(2,1)S(1)}, u32[]{:S(2)}, u32[]{:S(2)}) collective-permute-start(bf16[32,4,16,128]{3,2,1,0:T(8,128)(2,1)S(1)} %get-tuple-element.35.refs_0_), channel_id=1, source_target_pairs={{0,2},{2,8},{4,6},{6,12},{8,10},{10,16},{12,14},{14,20},{16,18},{1... | collective-permute-start | bytes 1572872 | tf_op jit(solution)/shard_map/ppermute | solution.py:407
  39.9 0.7 copy-start
  40.6 5.7 %collective-permute-start.6 = (bf16[32,4,16,128]{3,2,1,0:T(8,128)(2,1)S(1)}, bf16[32,4,16,128]{3,2,1,0:T(8,128)(2,1)S(1)}, u32[]{:S(2)}, u32[]{:S(2)}) collective-permute-start(bf16[32,4,16,128]{3,2,1,0:T(8,128)(2,1)S(1)} %collective-permute-done.1.refs_2_), channel_id=1, source_target_pairs={{0,2},{2,0},{4,6},{6,4},{8,10},{10,8},{12,14},{14,12},{16,18},{18,... | collective-permute-start | bytes 1572872 | tf_op jit(solution)/shard_map/ppermute | solution.py:422
  42.8 13.6 %collective-permute-start.5 = (bf16[32,4,16,128]{3,2,1,0:T(8,128)(2,1)}, bf16[32,4,16,128]{3,2,1,0:T(8,128)(2,1)}, u32[]{:S(2)}, u32[]{:S(2)}) collective-permute-start(bf16[32,4,16,128]{3,2,1,0:T(8,128)(2,1)} %get-tuple-element.46), channel_id=1, source_target_pairs={{0,1},{2,3},{4,5},{6,7},{8,9},{10,11},{12,13},{14,15},{16,17},{18,... | collective-permute-start | bytes 1572872 | tf_op jit(solution)/shard_map/ppermute | solution.py:453
  45.6 16.0 %collective-permute-start.3 = (bf16[32,4,16,128]{3,2,1,0:T(8,128)(2,1)S(1)}, bf16[32,4,16,128]{3,2,1,0:T(8,128)(2,1)}, u32[]{:S(2)}, u32[]{:S(2)}) collective-permute-start(bf16[32,4,16,128]{3,2,1,0:T(8,128)(2,1)S(1)} %collective-permute-done.refs_0_), channel_id=1, source_target_pairs={{0,4},{2,6},{4,8},{6,10},{8,12},{10,14},{12,16},{14,18},{16,20},{1... | collective-permute-start | bytes 1572872 | tf_op jit(solution)/shard_map/ppermute | solution.py:402
  46.2 19.2 %copy-start.1 = (bf16[32,2,16,128]{3,2,1,0:T(8,128)(2,1)S(1)}, bf16[32,2,16,128]{3,2,1,0:T(8,128)(2,1)}, u32[]{:S(2)}) copy-start(bf16[32,2,16,128]{3,2,1,0:T(8,128)(2,1)} %copy-done) | copy-start | bytes 786436
  61.6 12.8 %collective-permute-start.4 = (bf16[32,4,16,128]{3,2,1,0:T(8,128)(2,1)}, bf16[32,4,16,128]{3,2,1,0:T(8,128)(2,1)S(1)}, u32[]{:S(2)}, u32[]{:S(2)}) collective-permute-start(bf16[32,4,16,128]{3,2,1,0:T(8,128)(2,1)} %collective-permute-done.3.refs_2_), channel_id=1, source_target_pairs={{2,4},{10,12},{18,20},{26,28},{3,5},{11,13},{19,21},{27,29}} | collective-permute-start | bytes 1572872 | tf_op jit(solution)/shard_map/ppermute | solution.py:418
  63.0 17.4 %collective-permute-start.11 = (bf16[32,4,16,128]{3,2,1,0:T(8,128)(2,1)S(1)}, bf16[32,4,16,128]{3,2,1,0:T(8,128)(2,1)S(1)}, u32[]{:S(2)}, u32[]{:S(2)}) collective-permute-start(bf16[32,4,16,128]{3,2,1,0:T(8,128)(2,1)S(1)} %broadcast_select_fusion.refs_0_), channel_id=1, source_target_pairs={{0,4},{2,6},{4,8},{6,10},{8,12},{10,14},{12,16},{14,18},{16,20},{1... | collective-permute-start | bytes 1572872 | tf_op jit(solution)/shard_map/ppermute | solution.py:402
  63.1 18.7 %collective-permute-start.15 = (bf16[32,4,16,128]{3,2,1,0:T(8,128)(2,1)S(1)}, bf16[32,4,16,128]{3,2,1,0:T(8,128)(2,1)S(1)}, u32[]{:S(2)}, u32[]{:S(2)}) collective-permute-start(bf16[32,4,16,128]{3,2,1,0:T(8,128)(2,1)S(1)} %collective-permute-done.refs_0_), channel_id=1, source_target_pairs={{0,2},{2,8},{4,6},{8,10},{10,16},{12,14},{16,18},{18,24},{20,22},{... | collective-permute-start | bytes 1572872 | tf_op jit(solution)/shard_map/ppermute | solution.py:414
  65.5 15.6 %collective-permute-start.8 = (bf16[32,2,16,128]{3,2,1,0:T(8,128)(2,1)S(1)}, bf16[32,2,16,128]{3,2,1,0:T(8,128)(2,1)S(1)}, u32[]{:S(2)}, u32[]{:S(2)}) collective-permute-start(bf16[32,2,16,128]{3,2,1,0:T(8,128)(2,1)S(1)} %copy-done.1), channel_id=1, source_target_pairs={{0,1},{1,0},{2,3},{3,2},{4,5},{5,4},{6,7},{7,6},{8,9},{9,8},{10,11... | collective-permute-start | bytes 786440 | tf_op jit(solution)/shard_map/ppermute | solution.py:458
  66.0 23.0 %collective-permute-start.13 = (bf16[32,4,16,128]{3,2,1,0:T(8,128)(2,1)S(1)}, bf16[32,4,16,128]{3,2,1,0:T(8,128)(2,1)S(1)}, u32[]{:S(2)}, u32[]{:S(2)}) collective-permute-start(bf16[32,4,16,128]{3,2,1,0:T(8,128)(2,1)S(1)} %broadcast_select_fusion.refs_0_), channel_id=1, source_target_pairs={{0,2},{2,8},{4,6},{6,12},{8,10},{10,16},{12,14},{14,20},{16,18},{1... | collective-permute-start | bytes 1572872 | tf_op jit(solution)/shard_map/ppermute | solution.py:407
  74.4 9.6 %collective-permute-start.14 = (bf16[32,4,16,128]{3,2,1,0:T(8,128)(2,1)}, bf16[32,4,16,128]{3,2,1,0:T(8,128)(2,1)S(1)}, u32[]{:S(2)}, u32[]{:S(2)}) collective-permute-start(bf16[32,4,16,128]{3,2,1,0:T(8,128)(2,1)} %collective-permute-done.3.refs_2_), channel_id=1, source_target_pairs={{0,2},{2,0},{4,6},{6,4},{8,10},{10,8},{12,14},{14,12},{16,18},{18,... | collective-permute-start | bytes 1572872 | tf_op jit(solution)/shard_map/ppermute | solution.py:422
  80.5 8.5 %collective-permute-start.12 = (bf16[32,4,16,128]{3,2,1,0:T(8,128)(2,1)S(1)}, bf16[32,4,16,128]{3,2,1,0:T(8,128)(2,1)S(1)}, u32[]{:S(2)}, u32[]{:S(2)}) collective-permute-start(bf16[32,4,16,128]{3,2,1,0:T(8,128)(2,1)S(1)} %collective-permute-done.11.refs_2_), channel_id=1, source_target_pairs={{0,2},{2,0},{4,6},{6,4},{8,10},{10,8},{12,14},{14,12},{16,18},{18,... | collective-permute-start | bytes 1572872 | tf_op jit(solution)/shard_map/ppermute | solution.py:422
  81.1 11.9 %collective-permute-start.10 = (bf16[32,4,16,128]{3,2,1,0:T(8,128)(2,1)S(1)}, bf16[32,4,16,128]{3,2,1,0:T(8,128)(2,1)S(1)}, u32[]{:S(2)}, u32[]{:S(2)}) collective-permute-start(bf16[32,4,16,128]{3,2,1,0:T(8,128)(2,1)S(1)} %constant_dynamic-update-slice_fusion.refs_0_), channel_id=1, source_target_pairs={{0,2},{2,8},{4,6},{6,12},{8,10},{10,16},{12,14},{14,20},{16,18},{1... | collective-permute-start | bytes 1572872 | tf_op jit(solution)/shard_map/ppermute | solution.py:407
  81.7 22.2 %collective-permute-start.9 = (bf16[32,4,16,128]{3,2,1,0:T(8,128)(2,1)S(1)}, bf16[32,4,16,128]{3,2,1,0:T(8,128)(2,1)S(1)}, u32[]{:S(2)}, u32[]{:S(2)}) collective-permute-start(bf16[32,4,16,128]{3,2,1,0:T(8,128)(2,1)S(1)} %constant_dynamic-update-slice_fusion.refs_0_), channel_id=1, source_target_pairs={{0,4},{2,6},{4,8},{6,10},{8,12},{10,14},{12,16},{14,18},{16,20},{1... | collective-permute-start | bytes 1572872 | tf_op jit(solution)/shard_map/ppermute | solution.py:402
  104.0 1.9 %collective-permute-start.16 = (bf16[32,4,16,128]{3,2,1,0:T(8,128)(2,1)S(1)}, bf16[32,4,16,128]{3,2,1,0:T(8,128)(2,1)S(1)}, u32[]{:S(2)}, u32[]{:S(2)}) collective-permute-start(bf16[32,4,16,128]{3,2,1,0:T(8,128)(2,1)S(1)} %collective-permute-done.9.refs_2_), channel_id=1, source_target_pairs={{0,2},{2,0},{4,6},{6,4},{8,10},{10,8},{12,14},{14,12},{16,18},{18,... | collective-permute-start | bytes 1572872 | tf_op jit(solution)/shard_map/ppermute | solution.py:422

commit v16 on v15

--- a/solution.py
+++ b/solution.py
@@ -460,7 +460,7 @@
     two_b, rest_b = farther(piece_b)
     pair_g, relay_g = exchanged(two_g), relayed(two_g)
     sums = correlated([got_a, pair_g, two_g, (rest_g, relay_g)], first, sums, False)
-    piece_c = jnp.concatenate([after(own_c, relay_g), got_c], axis=1)
+    piece_c = jnp.concatenate([own_c, got_c], axis=1)
     two_c, rest_c = farther(piece_c)
     pair_b = exchanged(two_b)
     sums = correlated([piece_b, pair_b, two_b, rest_b], first, sums, False)

time: 114 us -> 107 us (0.939)
  the two profiles are of different devices: /device:TPU:1 before, /device:TPU:7 now
where the time goes in v16:
time: 107 us
  Pallas kernels  42.3 us (40%)
  waiting for transfers between devices  35.6 us (33%)
  starting transfers between devices  27.2 us (25%)
  other arithmetic  1.17 us (1%)
    pallas_call x4, Pallas kernels, correlate(): pl.pallas_call(functools.partial(correlate_kernel, pieces, per_group, sca...  19.6 us
    pallas_call x3, Pallas kernels, spectra(): pl.pallas_call(functools.partial(spectra_kernel, groups, tuple((part[1:]...  19.5 us
    ppermute x4, waiting for transfers between devices, shifted(): lax.ppermute(block, axis, [(i, (i + distance) % size) for i in range(size)])  11.7 us
    ppermute x1, waiting for transfers between devices, paired(): got_b = lax.ppermute(away_b, 'tm', [(0, 1)])  10.4 us
    ppermute x4, starting transfers between devices, exchanged(): lax.ppermute(block, 'stn', [(i, i ^ 1) for i in range(lax.axis_size('stn'...  9.9 us
    ppermute x4, starting transfers between devices, shifted(): lax.ppermute(block, axis, [(i, (i + distance) % size) for i in range(size)])  7.07 us
    ppermute x1, waiting for transfers between devices, paired(): got_c = lax.ppermute(away_c, 'tm', swap)  6.51 us
    ppermute x3, starting transfers between devices, farther(): lax.ppermute(block, 'stn', [(i, (i + 1 if i % 2 == 0 else i + 3) % size)...  5.5 us
  transfers between devices with their start and end apart: 17, of which 8 were waited for; matrix products, arithmetic and copies ran while one was open for 1% of the time, Pallas kernels for 29%

profile of v16, /device:TPU:7, one launch (start us, length us, event | category | flops | bytes accessed | tf_op | source)
XLA Modules:
  0.0 107.2 jit_solution(10539092619086963847)
XLA Ops:
  0.0 0.1 pad_add_fusion.place
  0.1 3.3 %shard_map.46 = (bf16[8,32,64,128]{3,2,1,0:T(8,128)(2,1)S(1)}, bf16[8,8,64,128]{3,2,1,0:T(8,128)(2,1)S(1)}, f32[1024,128]{1,0:T(8,128)S(1)}, bf16[64,192]{1,0:T(...) custom-call(s32[2]{0:T(128)S(1)} %pad_add_fusion.place, bf16[8,32,64,128]{3,2,1,0:T(8,128)(2,1)} %bitcast.10, ...), custom_call_target="tpu_custom_call" | custom-call | tf_op jit(solution)/shard_map/pallas_call | solution.py:110
  3.4 0.3 collective-permute-start.2
  3.7 11.4 %shard_map.47 = (bf16[32,4,16,128]{3,2,1,0:T(8,128)(2,1)S(1)}, bf16[32,4,16,128]{3,2,1,0:T(8,128)(2,1)S(1)}) custom-call(s32[2]{0:T(128)S(1)} %pad_add_fusion.place, bf16[8,32,64,128]{3,2,1,0:T(8,128)(2,1)S(1)} %get-tuple-element.28.refs_0_.refs_1_, bf16[8,32,64,128]{3,2,1,0:T(8,128)(2,1)S(1)} %get-tuple-element.28.refs_0_.refs_1_, ...), custom_call_target="tpu_custom_call" | custom-call | flops 1000000 | tf_op jit(solution)/shard_map/pallas_call | solution.py:263
  15.0 1.3 %collective-permute-start.1 = (bf16[32,4,16,128]{3,2,1,0:T(8,128)(2,1)S(1)}, bf16[32,4,16,128]{3,2,1,0:T(8,128)(2,1)S(1)}, u32[]{:S(2)}, u32[]{:S(2)}) collective-permute-start(bf16[32,4,16,128]{3,2,1,0:T(8,128)(2,1)S(1)} %get-tuple-element.34.refs_0_), channel_id=1, source_target_pairs={{0,4},{2,6},{4,8},{6,10},{8,12},{10,14},{12,16},{14,18},{16,20},{1... | collective-permute-start | bytes 1572872 | tf_op jit(solution)/shard_map/ppermute | solution.py:402
  16.4 1.2 %collective-permute-start = (bf16[32,4,16,128]{3,2,1,0:T(8,128)(2,1)S(1)}, bf16[32,4,16,128]{3,2,1,0:T(8,128)(2,1)S(1)}, u32[]{:S(2)}, u32[]{:S(2)}) collective-permute-start(bf16[32,4,16,128]{3,2,1,0:T(8,128)(2,1)S(1)} %get-tuple-element.33), channel_id=1, source_target_pairs={{0,1},{1,0},{2,3},{3,2},{4,5},{5,4},{6,7},{7,6},{8,9},{9,8},{10,11... | collective-permute-start | bytes 1572872 | tf_op jit(solution)/shard_map/ppermute | solution.py:438
  17.6 2.7 %collective-permute-start.5 = (bf16[32,4,16,128]{3,2,1,0:T(8,128)(2,1)S(1)}, bf16[32,4,16,128]{3,2,1,0:T(8,128)(2,1)S(1)}, u32[]{:S(2)}, u32[]{:S(2)}) collective-permute-start(bf16[32,4,16,128]{3,2,1,0:T(8,128)(2,1)S(1)} %get-tuple-element.34.refs_0_), channel_id=1, source_target_pairs={{0,2},{2,8},{4,6},{6,12},{8,10},{10,16},{12,14},{14,20},{16,18},{1... | collective-permute-start | bytes 1572872 | tf_op jit(solution)/shard_map/ppermute | solution.py:407
  20.3 1.4 %shard_map.48 = (bf16[32,4,16,128]{3,2,1,0:T(8,128)(2,1)S(1)}, bf16[32,4,16,128]{3,2,1,0:T(8,128)(2,1)}) custom-call(s32[2]{0:T(128)S(1)} %pad_add_fusion.place, bf16[8,32,64,128]{3,2,1,0:T(8,128)(2,1)S(1)} %get-tuple-element.28.refs_0_.refs_1_, bf16[8,32,64,128]{3,2,1,0:T(8,128)(2,1)S(1)} %get-tuple-element.28.refs_0_.refs_1_, ...), custom_call_target="tpu_custom_call" | custom-call | flops 1000000 | tf_op jit(solution)/shard_map/pallas_call | solution.py:263
  21.6 5.9 %collective-permute-done.1.refs_2_ = bf16[32,4,16,128]{3,2,1,0:T(8,128)(2,1)S(1)} collective-permute-done((bf16[32,4,16,128]{3,2,1,0:T(8,128)(2,1)S(1)}, bf16[32,4,16,128]{3,2,1,0:T(8,128)(2,1)S(1)}, u32[]{:S(2)}, u32[]{:S(2)}) %collective-permute-start.1) | collective-permute-done | bytes 524320 | tf_op jit(solution)/shard_map/ppermute | solution.py:402
  27.6 0.0 collective-permute-done.2.refs_2_
  27.6 6.7 %shard_map.49 = (bf16[32,2,16,128]{3,2,1,0:T(8,128)(2,1)S(1)}, bf16[32,2,16,128]{3,2,1,0:T(8,128)(2,1)S(1)}) custom-call(s32[2]{0:T(128)S(1)} %pad_add_fusion.place, bf16[8,32,64,128]{3,2,1,0:T(8,128)(2,1)S(1)} %get-tuple-element.28.refs_0_.refs_1_, bf16[8,32,64,128]{3,2,1,0:T(8,128)(2,1)S(1)} %get-tuple-element.28.refs_0_.refs_1_, ...), custom_call_target="tpu_custom_call" | custom-call | flops 1000000 | tf_op jit(solution)/shard_map/pallas_call | solution.py:263
  34.3 0.0 copy-start
  34.3 0.7 copy-done
  35.0 3.7 %collective-permute-done.refs_0_ = bf16[32,4,16,128]{3,2,1,0:T(8,128)(2,1)S(1)} collective-permute-done((bf16[32,4,16,128]{3,2,1,0:T(8,128)(2,1)S(1)}, bf16[32,4,16,128]{3,2,1,0:T(8,128)(2,1)S(1)}, u32[]{:S(2)}, u32[]{:S(2)}) %collective-permute-start) | collective-permute-done | bytes 524320 | tf_op jit(solution)/shard_map/ppermute | solution.py:438
  38.7 1.5 %collective-permute-start.4 = (bf16[32,4,16,128]{3,2,1,0:T(8,128)(2,1)S(1)}, bf16[32,4,16,128]{3,2,1,0:T(8,128)(2,1)S(1)}, u32[]{:S(2)}, u32[]{:S(2)}) collective-permute-start(bf16[32,4,16,128]{3,2,1,0:T(8,128)(2,1)S(1)} %collective-permute-done.1.refs_2_), channel_id=1, source_target_pairs={{0,2},{2,0},{4,6},{6,4},{8,10},{10,8},{12,14},{14,12},{16,18},{18,... | collective-permute-start | bytes 1572872 | tf_op jit(solution)/shard_map/ppermute | solution.py:422
  40.2 1.3 %collective-permute-start.3 = (bf16[32,4,16,128]{3,2,1,0:T(8,128)(2,1)}, bf16[32,4,16,128]{3,2,1,0:T(8,128)(2,1)}, u32[]{:S(2)}, u32[]{:S(2)}) collective-permute-start(bf16[32,4,16,128]{3,2,1,0:T(8,128)(2,1)} %get-tuple-element.43), channel_id=1, source_target_pairs={{0,1},{2,3},{4,5},{6,7},{8,9},{10,11},{12,13},{14,15},{16,17},{18,... | collective-permute-start | bytes 1572872 | tf_op jit(solution)/shard_map/ppermute | solution.py:453
  41.5 1.3 %collective-permute-start.12 = (bf16[32,4,16,128]{3,2,1,0:T(8,128)(2,1)S(1)}, bf16[32,4,16,128]{3,2,1,0:T(8,128)(2,1)}, u32[]{:S(2)}, u32[]{:S(2)}) collective-permute-start(bf16[32,4,16,128]{3,2,1,0:T(8,128)(2,1)S(1)} %collective-permute-done.refs_0_), channel_id=1, source_target_pairs={{0,4},{2,6},{4,8},{6,10},{8,12},{10,14},{12,16},{14,18},{16,20},{1... | collective-permute-start | bytes 1572872 | tf_op jit(solution)/shard_map/ppermute | solution.py:402
  42.9 0.0 copy-start.1
  42.9 0.0 collective-permute-done.5.refs_3_
  42.9 0.0 collective-permute-done.4.refs_1_
  42.9 2.7 %shard_map.50.refs_5_ = f32[4096,128]{1,0:T(8,128)S(1)} custom-call(s32[2]{0:T(128)S(1)} %pad_add_fusion.place, bf16[32,4,16,128]{3,2,1,0:T(8,128)(2,1)S(1)} %get-tuple-element.34.refs_0_, bf16[32,4,16,128]{3,2,1,0:T(8,128)(2,1)S(1)} %collective-permute-done.4.refs_1_, bf16[32,4,16,128]{3,2,1,0:T(8,128)(2,1)S(1)} %collective-permute-done.1.refs_2_, ...), custom_call_target="tpu_custom_call" | custom-call | flops 1000 | tf_op jit(solution)/shard_map/pallas_call | solution.py:373
  45.6 10.4 %collective-permute-done.3 = bf16[32,4,16,128]{3,2,1,0:T(8,128)(2,1)} collective-permute-done((bf16[32,4,16,128]{3,2,1,0:T(8,128)(2,1)}, bf16[32,4,16,128]{3,2,1,0:T(8,128)(2,1)}, u32[]{:S(2)}, u32[]{:S(2)}) %collective-permute-start.3) | collective-permute-done | bytes 524320 | tf_op jit(solution)/shard_map/ppermute | solution.py:453
  56.0 1.1 %broadcast_select_fusion.refs_0_ = bf16[32,4,16,128]{3,2,1,0:T(8,128)(2,1)S(1)} fusion(bf16[32,4,16,128]{3,2,1,0:T(8,128)(2,1)S(1)} %get-tuple-element.36, bf16[32,4,16,128]{3,2,1,0:T(8,128)(2,1)} %collective-permute-done.3, pred[]{:T(512)S(6)} %eq.5), kind=kLoop, calls=%fused_computation | loop fusion | flops 262144 | bytes 1572865 | tf_op jit(solution)/shard_map/jit(_where)/select_n | solution.py:459
  57.1 1.3 %collective-permute-start.9 = (bf16[32,4,16,128]{3,2,1,0:T(8,128)(2,1)S(1)}, bf16[32,4,16,128]{3,2,1,0:T(8,128)(2,1)S(1)}, u32[]{:S(2)}, u32[]{:S(2)}) collective-permute-start(bf16[32,4,16,128]{3,2,1,0:T(8,128)(2,1)S(1)} %broadcast_select_fusion.refs_0_), channel_id=1, source_target_pairs={{0,4},{2,6},{4,8},{6,10},{8,12},{10,14},{12,16},{14,18},{16,20},{1... | collective-permute-start | bytes 1572872 | tf_op jit(solution)/shard_map/ppermute | solution.py:402
  58.4 1.3 %collective-permute-start.14 = (bf16[32,4,16,128]{3,2,1,0:T(8,128)(2,1)S(1)}, bf16[32,4,16,128]{3,2,1,0:T(8,128)(2,1)S(1)}, u32[]{:S(2)}, u32[]{:S(2)}) collective-permute-start(bf16[32,4,16,128]{3,2,1,0:T(8,128)(2,1)S(1)} %collective-permute-done.refs_0_), channel_id=1, source_target_pairs={{0,2},{2,8},{4,6},{8,10},{10,16},{12,14},{16,18},{18,24},{20,22},{... | collective-permute-start | bytes 1572872 | tf_op jit(solution)/shard_map/ppermute | solution.py:414
  59.7 0.0 collective-permute-done.12.refs_2_
  59.7 1.2 %collective-permute-start.13 = (bf16[32,4,16,128]{3,2,1,0:T(8,128)(2,1)}, bf16[32,4,16,128]{3,2,1,0:T(8,128)(2,1)S(1)}, u32[]{:S(2)}, u32[]{:S(2)}) collective-permute-start(bf16[32,4,16,128]{3,2,1,0:T(8,128)(2,1)} %collective-permute-done.12.refs_2_), channel_id=1, source_target_pairs={{0,2},{2,0},{4,6},{6,4},{8,10},{10,8},{12,14},{14,12},{16,18},{18,... | collective-permute-start | bytes 1572872 | tf_op jit(solution)/shard_map/ppermute | solution.py:422
  60.9 0.0 copy-done.1
  60.9 0.0 collective-permute-start.6
  61.0 1.3 %collective-permute-start.11 = (bf16[32,4,16,128]{3,2,1,0:T(8,128)(2,1)S(1)}, bf16[32,4,16,128]{3,2,1,0:T(8,128)(2,1)S(1)}, u32[]{:S(2)}, u32[]{:S(2)}) collective-permute-start(bf16[32,4,16,128]{3,2,1,0:T(8,128)(2,1)S(1)} %broadcast_select_fusion.refs_0_), channel_id=1, source_target_pairs={{0,2},{2,8},{4,6},{6,12},{8,10},{10,16},{12,14},{14,20},{16,18},{1... | collective-permute-start | bytes 1572872 | tf_op jit(solution)/shard_map/ppermute | solution.py:407
  62.3 6.5 %collective-permute-done.6 = bf16[32,2,16,128]{3,2,1,0:T(8,128)(2,1)S(1)} collective-permute-done((bf16[32,2,16,128]{3,2,1,0:T(8,128)(2,1)S(1)}, bf16[32,2,16,128]{3,2,1,0:T(8,128)(2,1)S(1)}, u32[]{:S(2)}, u32[]{:S(2)}) %collective-permute-start.6) | collective-permute-done | bytes 262176 | tf_op jit(solution)/shard_map/ppermute | solution.py:458
  68.8 0.7 collective-permute-start.15
  69.6 0.3 collective-permute-done.9.refs_2_
  69.8 2.0 %collective-permute-start.10 = (bf16[32,4,16,128]{3,2,1,0:T(8,128)(2,1)S(1)}, bf16[32,4,16,128]{3,2,1,0:T(8,128)(2,1)S(1)}, u32[]{:S(2)}, u32[]{:S(2)}) collective-permute-start(bf16[32,4,16,128]{3,2,1,0:T(8,128)(2,1)S(1)} %collective-permute-done.9.refs_2_), channel_id=1, source_target_pairs={{0,2},{2,0},{4,6},{6,4},{8,10},{10,8},{12,14},{14,12},{16,18},{18,... | collective-permute-start | bytes 1572872 | tf_op jit(solution)/shard_map/ppermute | solution.py:422
  71.8 0.0 collective-permute-done.14.refs_3_
  71.8 3.1 %collective-permute-start.7 = (bf16[32,4,16,128]{3,2,1,0:T(8,128)(2,1)S(1)}, bf16[32,4,16,128]{3,2,1,0:T(8,128)(2,1)S(1)}, u32[]{:S(2)}, u32[]{:S(2)}) collective-permute-start(bf16[32,4,16,128]{3,2,1,0:T(8,128)(2,1)S(1)} %constant_dynamic-update-slice_fusion.refs_0_), channel_id=1, source_target_pairs={{0,4},{2,6},{4,8},{6,10},{8,12},{10,14},{12,16},{14,18},{16,20},{1... | collective-permute-start | bytes 1572872 | tf_op jit(solution)/shard_map/ppermute | solution.py:402
  74.9 0.0 collective-permute-done.13.refs_1_
  74.9 1.5 %collective-permute-start.8 = (bf16[32,4,16,128]{3,2,1,0:T(8,128)(2,1)S(1)}, bf16[32,4,16,128]{3,2,1,0:T(8,128)(2,1)S(1)}, u32[]{:S(2)}, u32[]{:S(2)}) collective-permute-start(bf16[32,4,16,128]{3,2,1,0:T(8,128)(2,1)S(1)} %constant_dynamic-update-slice_fusion.refs_0_), channel_id=1, source_target_pairs={{0,2},{2,8},{4,6},{6,12},{8,10},{10,16},{12,14},{14,20},{16,18},{1... | collective-permute-start | bytes 1572872 | tf_op jit(solution)/shard_map/ppermute | solution.py:407
  76.4 0.0 collective-permute-done.15.refs_4_
  76.4 5.0 %shard_map.51.refs_4_ = f32[4096,128]{1,0:T(8,128)S(1)} custom-call(s32[2]{0:T(128)S(1)} %pad_add_fusion.place, bf16[32,4,16,128]{3,2,1,0:T(8,128)(2,1)S(1)} %collective-permute-done.refs_0_, bf16[32,4,16,128]{3,2,1,0:T(8,128)(2,1)S(1)} %collective-permute-done.13.refs_1_, ...), custom_call_target="tpu_custom_call", output_to_operand_aliasing={{}: (6, {})} | custom-call | flops 1000 | tf_op jit(solution)/shard_map/pallas_call | solution.py:373
  81.4 0.0 collective-permute-done.11.refs_3_
  81.4 0.0 collective-permute-done.10.refs_1_
  81.4 4.0 %shard_map.52.refs_4_ = f32[4096,128]{1,0:T(8,128)S(1)} custom-call(s32[2]{0:T(128)S(1)} %pad_add_fusion.place, bf16[32,4,16,128]{3,2,1,0:T(8,128)(2,1)S(1)} %broadcast_select_fusion.refs_0_, bf16[32,4,16,128]{3,2,1,0:T(8,128)(2,1)S(1)} %collective-permute-done.10.refs_1_, ...), custom_call_target="tpu_custom_call", output_to_operand_aliasing={{}: (5, {})} | custom-call | flops 1000 | tf_op jit(solution)/shard_map/pallas_call | solution.py:373
  85.4 5.5 %collective-permute-done.7.refs_2_ = bf16[32,4,16,128]{3,2,1,0:T(8,128)(2,1)S(1)} collective-permute-done((bf16[32,4,16,128]{3,2,1,0:T(8,128)(2,1)S(1)}, bf16[32,4,16,128]{3,2,1,0:T(8,128)(2,1)S(1)}, u32[]{:S(2)}, u32[]{:S(2)}) %collective-permute-start.7) | collective-permute-done | bytes 524320 | tf_op jit(solution)/shard_map/ppermute | solution.py:402
  90.9 1.7 %collective-permute-done.8.refs_3_ = bf16[32,4,16,128]{3,2,1,0:T(8,128)(2,1)S(1)} collective-permute-done((bf16[32,4,16,128]{3,2,1,0:T(8,128)(2,1)S(1)}, bf16[32,4,16,128]{3,2,1,0:T(8,128)(2,1)S(1)}, u32[]{:S(2)}, u32[]{:S(2)}) %collective-permute-start.8) | collective-permute-done | bytes 524320 | tf_op jit(solution)/shard_map/ppermute | solution.py:407
  92.6 5.1 %collective-permute-start.16 = (bf16[32,4,16,128]{3,2,1,0:T(8,128)(2,1)S(1)}, bf16[32,4,16,128]{3,2,1,0:T(8,128)(2,1)S(1)}, u32[]{:S(2)}, u32[]{:S(2)}) collective-permute-start(bf16[32,4,16,128]{3,2,1,0:T(8,128)(2,1)S(1)} %collective-permute-done.7.refs_2_), channel_id=1, source_target_pairs={{0,2},{2,0},{4,6},{6,4},{8,10},{10,8},{12,14},{14,12},{16,18},{18,... | collective-permute-start | bytes 1572872 | tf_op jit(solution)/shard_map/ppermute | solution.py:422
  97.8 1.5 %collective-permute-done.16.refs_1_ = bf16[32,4,16,128]{3,2,1,0:T(8,128)(2,1)S(1)} collective-permute-done((bf16[32,4,16,128]{3,2,1,0:T(8,128)(2,1)S(1)}, bf16[32,4,16,128]{3,2,1,0:T(8,128)(2,1)S(1)}, u32[]{:S(2)}, u32[]{:S(2)}) %collective-permute-start.16) | collective-permute-done | bytes 524320 | tf_op jit(solution)/shard_map/ppermute | solution.py:422
  99.3 7.9 %shard_map.53 = f32[2,8,4,8,8,128]{5,4,3,2,1,0:T(8,128)} custom-call(s32[2]{0:T(128)S(1)} %pad_add_fusion.place, bf16[32,4,16,128]{3,2,1,0:T(8,128)(2,1)S(1)} %constant_dynamic-update-slice_fusion.refs_0_, bf16[32,4,16,128]{3,2,1,0:T(8,128)(2,1)S(1)} %collective-permute-done.16.refs_1_, bf16[32,4,16,128]{3,2,1,0:T(8,128)(2,1)S(1)} %collective-permute-done.7.refs_2_, ...), custom_call_target="tpu_custom_call" | custom-call | flops 1000 | tf_op jit(solution)/shard_map/pallas_call | solution.py:373
  (2 shorter events, 0.1 us)
Async XLA Ops:
  3.4 24.2 %collective-permute-start.2 = (bf16[8,8,64,128]{3,2,1,0:T(8,128)(2,1)S(1)}, bf16[8,8,64,128]{3,2,1,0:T(8,128)(2,1)S(1)}, u32[]{:S(2)}, u32[]{:S(2)}) collective-permute-start(bf16[8,8,64,128]{3,2,1,0:T(8,128)(2,1)S(1)} %get-tuple-element.38), channel_id=1, source_target_pairs={{0,1},{1,0},{2,3},{3,2},{4,5},{5,4},{6,7},{7,6},{8,9},{9,8},{10,11... | collective-permute-start | bytes 3145736 | tf_op jit(solution)/shard_map/ppermute | solution.py:434
  15.0 12.5 %collective-permute-start.1 = (bf16[32,4,16,128]{3,2,1,0:T(8,128)(2,1)S(1)}, bf16[32,4,16,128]{3,2,1,0:T(8,128)(2,1)S(1)}, u32[]{:S(2)}, u32[]{:S(2)}) collective-permute-start(bf16[32,4,16,128]{3,2,1,0:T(8,128)(2,1)S(1)} %get-tuple-element.34.refs_0_), channel_id=1, source_target_pairs={{0,4},{2,6},{4,8},{6,10},{8,12},{10,14},{12,16},{14,18},{16,20},{1... | collective-permute-start | bytes 1572872 | tf_op jit(solution)/shard_map/ppermute | solution.py:402
  16.4 22.3 %collective-permute-start = (bf16[32,4,16,128]{3,2,1,0:T(8,128)(2,1)S(1)}, bf16[32,4,16,128]{3,2,1,0:T(8,128)(2,1)S(1)}, u32[]{:S(2)}, u32[]{:S(2)}) collective-permute-start(bf16[32,4,16,128]{3,2,1,0:T(8,128)(2,1)S(1)} %get-tuple-element.33), channel_id=1, source_target_pairs={{0,1},{1,0},{2,3},{3,2},{4,5},{5,4},{6,7},{7,6},{8,9},{9,8},{10,11... | collective-permute-start | bytes 1572872 | tf_op jit(solution)/shard_map/ppermute | solution.py:438
  17.6 25.3 %collective-permute-start.5 = (bf16[32,4,16,128]{3,2,1,0:T(8,128)(2,1)S(1)}, bf16[32,4,16,128]{3,2,1,0:T(8,128)(2,1)S(1)}, u32[]{:S(2)}, u32[]{:S(2)}) collective-permute-start(bf16[32,4,16,128]{3,2,1,0:T(8,128)(2,1)S(1)} %get-tuple-element.34.refs_0_), channel_id=1, source_target_pairs={{0,2},{2,8},{4,6},{6,12},{8,10},{10,16},{12,14},{14,20},{16,18},{1... | collective-permute-start | bytes 1572872 | tf_op jit(solution)/shard_map/ppermute | solution.py:407
  34.3 0.7 copy-start
  38.7 4.2 %collective-permute-start.4 = (bf16[32,4,16,128]{3,2,1,0:T(8,128)(2,1)S(1)}, bf16[32,4,16,128]{3,2,1,0:T(8,128)(2,1)S(1)}, u32[]{:S(2)}, u32[]{:S(2)}) collective-permute-start(bf16[32,4,16,128]{3,2,1,0:T(8,128)(2,1)S(1)} %collective-permute-done.1.refs_2_), channel_id=1, source_target_pairs={{0,2},{2,0},{4,6},{6,4},{8,10},{10,8},{12,14},{14,12},{16,18},{18,... | collective-permute-start | bytes 1572872 | tf_op jit(solution)/shard_map/ppermute | solution.py:422
  40.2 15.8 %collective-permute-start.3 = (bf16[32,4,16,128]{3,2,1,0:T(8,128)(2,1)}, bf16[32,4,16,128]{3,2,1,0:T(8,128)(2,1)}, u32[]{:S(2)}, u32[]{:S(2)}) collective-permute-start(bf16[32,4,16,128]{3,2,1,0:T(8,128)(2,1)} %get-tuple-element.43), channel_id=1, source_target_pairs={{0,1},{2,3},{4,5},{6,7},{8,9},{10,11},{12,13},{14,15},{16,17},{18,... | collective-permute-start | bytes 1572872 | tf_op jit(solution)/shard_map/ppermute | solution.py:453
  41.5 18.2 %collective-permute-start.12 = (bf16[32,4,16,128]{3,2,1,0:T(8,128)(2,1)S(1)}, bf16[32,4,16,128]{3,2,1,0:T(8,128)(2,1)}, u32[]{:S(2)}, u32[]{:S(2)}) collective-permute-start(bf16[32,4,16,128]{3,2,1,0:T(8,128)(2,1)S(1)} %collective-permute-done.refs_0_), channel_id=1, source_target_pairs={{0,4},{2,6},{4,8},{6,10},{8,12},{10,14},{12,16},{14,18},{16,20},{1... | collective-permute-start | bytes 1572872 | tf_op jit(solution)/shard_map/ppermute | solution.py:402
  42.9 18.1 %copy-start.1 = (bf16[32,2,16,128]{3,2,1,0:T(8,128)(2,1)S(1)}, bf16[32,2,16,128]{3,2,1,0:T(8,128)(2,1)}, u32[]{:S(2)}) copy-start(bf16[32,2,16,128]{3,2,1,0:T(8,128)(2,1)} %copy-done) | copy-start | bytes 786436
  57.1 12.7 %collective-permute-start.9 = (bf16[32,4,16,128]{3,2,1,0:T(8,128)(2,1)S(1)}, bf16[32,4,16,128]{3,2,1,0:T(8,128)(2,1)S(1)}, u32[]{:S(2)}, u32[]{:S(2)}) collective-permute-start(bf16[32,4,16,128]{3,2,1,0:T(8,128)(2,1)S(1)} %broadcast_select_fusion.refs_0_), channel_id=1, source_target_pairs={{0,4},{2,6},{4,8},{6,10},{8,12},{10,14},{12,16},{14,18},{16,20},{1... | collective-permute-start | bytes 1572872 | tf_op jit(solution)/shard_map/ppermute | solution.py:402
  58.4 13.4 %collective-permute-start.14 = (bf16[32,4,16,128]{3,2,1,0:T(8,128)(2,1)S(1)}, bf16[32,4,16,128]{3,2,1,0:T(8,128)(2,1)S(1)}, u32[]{:S(2)}, u32[]{:S(2)}) collective-permute-start(bf16[32,4,16,128]{3,2,1,0:T(8,128)(2,1)S(1)} %collective-permute-done.refs_0_), channel_id=1, source_target_pairs={{0,2},{2,8},{4,6},{8,10},{10,16},{12,14},{16,18},{18,24},{20,22},{... | collective-permute-start | bytes 1572872 | tf_op jit(solution)/shard_map/ppermute | solution.py:414
  59.7 15.2 %collective-permute-start.13 = (bf16[32,4,16,128]{3,2,1,0:T(8,128)(2,1)}, bf16[32,4,16,128]{3,2,1,0:T(8,128)(2,1)S(1)}, u32[]{:S(2)}, u32[]{:S(2)}) collective-permute-start(bf16[32,4,16,128]{3,2,1,0:T(8,128)(2,1)} %collective-permute-done.12.refs_2_), channel_id=1, source_target_pairs={{0,2},{2,0},{4,6},{6,4},{8,10},{10,8},{12,14},{14,12},{16,18},{18,... | collective-permute-start | bytes 1572872 | tf_op jit(solution)/shard_map/ppermute | solution.py:422
  60.9 7.9 %collective-permute-start.6 = (bf16[32,2,16,128]{3,2,1,0:T(8,128)(2,1)S(1)}, bf16[32,2,16,128]{3,2,1,0:T(8,128)(2,1)S(1)}, u32[]{:S(2)}, u32[]{:S(2)}) collective-permute-start(bf16[32,2,16,128]{3,2,1,0:T(8,128)(2,1)S(1)} %copy-done.1), channel_id=1, source_target_pairs={{0,1},{1,0},{2,3},{3,2},{4,5},{5,4},{6,7},{7,6},{8,9},{9,8},{10,11... | collective-permute-start | bytes 786440 | tf_op jit(solution)/shard_map/ppermute | solution.py:458
  61.0 20.5 %collective-permute-start.11 = (bf16[32,4,16,128]{3,2,1,0:T(8,128)(2,1)S(1)}, bf16[32,4,16,128]{3,2,1,0:T(8,128)(2,1)S(1)}, u32[]{:S(2)}, u32[]{:S(2)}) collective-permute-start(bf16[32,4,16,128]{3,2,1,0:T(8,128)(2,1)S(1)} %broadcast_select_fusion.refs_0_), channel_id=1, source_target_pairs={{0,2},{2,8},{4,6},{6,12},{8,10},{10,16},{12,14},{14,20},{16,18},{1... | collective-permute-start | bytes 1572872 | tf_op jit(solution)/shard_map/ppermute | solution.py:407
  68.8 7.6 %collective-permute-start.15 = (bf16[32,4,16,128]{3,2,1,0:T(8,128)(2,1)}, bf16[32,4,16,128]{3,2,1,0:T(8,128)(2,1)S(1)}, u32[]{:S(2)}, u32[]{:S(2)}) collective-permute-start(bf16[32,4,16,128]{3,2,1,0:T(8,128)(2,1)} %collective-permute-done.12.refs_2_), channel_id=1, source_target_pairs={{2,4},{10,12},{18,20},{26,28},{3,5},{11,13},{19,21},{27,29}} | collective-permute-start | bytes 1572872 | tf_op jit(solution)/shard_map/ppermute | solution.py:418
  69.8 11.6 %collective-permute-start.10 = (bf16[32,4,16,128]{3,2,1,0:T(8,128)(2,1)S(1)}, bf16[32,4,16,128]{3,2,1,0:T(8,128)(2,1)S(1)}, u32[]{:S(2)}, u32[]{:S(2)}) collective-permute-start(bf16[32,4,16,128]{3,2,1,0:T(8,128)(2,1)S(1)} %collective-permute-done.9.refs_2_), channel_id=1, source_target_pairs={{0,2},{2,0},{4,6},{6,4},{8,10},{10,8},{12,14},{14,12},{16,18},{18,... | collective-permute-start | bytes 1572872 | tf_op jit(solution)/shard_map/ppermute | solution.py:422
  71.8 19.1 %collective-permute-start.7 = (bf16[32,4,16,128]{3,2,1,0:T(8,128)(2,1)S(1)}, bf16[32,4,16,128]{3,2,1,0:T(8,128)(2,1)S(1)}, u32[]{:S(2)}, u32[]{:S(2)}) collective-permute-start(bf16[32,4,16,128]{3,2,1,0:T(8,128)(2,1)S(1)} %constant_dynamic-update-slice_fusion.refs_0_), channel_id=1, source_target_pairs={{0,4},{2,6},{4,8},{6,10},{8,12},{10,14},{12,16},{14,18},{16,20},{1... | collective-permute-start | bytes 1572872 | tf_op jit(solution)/shard_map/ppermute | solution.py:402
  74.9 17.7 %collective-permute-start.8 = (bf16[32,4,16,128]{3,2,1,0:T(8,128)(2,1)S(1)}, bf16[32,4,16,128]{3,2,1,0:T(8,128)(2,1)S(1)}, u32[]{:S(2)}, u32[]{:S(2)}) collective-permute-start(bf16[32,4,16,128]{3,2,1,0:T(8,128)(2,1)S(1)} %constant_dynamic-update-slice_fusion.refs_0_), channel_id=1, source_target_pairs={{0,2},{2,8},{4,6},{6,12},{8,10},{10,16},{12,14},{14,20},{16,18},{1... | collective-permute-start | bytes 1572872 | tf_op jit(solution)/shard_map/ppermute | solution.py:407
  92.6 6.7 %collective-permute-start.16 = (bf16[32,4,16,128]{3,2,1,0:T(8,128)(2,1)S(1)}, bf16[32,4,16,128]{3,2,1,0:T(8,128)(2,1)S(1)}, u32[]{:S(2)}, u32[]{:S(2)}) collective-permute-start(bf16[32,4,16,128]{3,2,1,0:T(8,128)(2,1)S(1)} %collective-permute-done.7.refs_2_), channel_id=1, source_target_pairs={{0,2},{2,0},{4,6},{6,4},{8,10},{10,8},{12,14},{14,12},{16,18},{18,... | collective-permute-start | bytes 1572872 | tf_op jit(solution)/shard_map/ppermute | solution.py:422

commit v17 on v16

--- a/solution.py
+++ b/solution.py
@@ -450,22 +450,22 @@
     )
     got_a, own_c, away_b, away_c, two_a = lax.optimization_barrier((got_a, own_c, away_b, away_c, two_a))
     two_g, rest_g = evenly(got_a)
-    got_b = lax.ppermute(away_b, "tm", [(0, 1)])
+    got_c = lax.ppermute(away_c, "tm", swap)
     pair_a = exchanged(two_a)
     first = [(many, [(0, 0, 0)])]
     sums = correlated([own_a, pair_a, two_a, rest_a], first, None, False)
-    got_b, away_c, sums = lax.optimization_barrier((got_b, away_c, sums))
-    got_c = lax.ppermute(away_c, "tm", swap)
-    piece_b = jnp.where(me == 0, own_b, got_b)
-    two_b, rest_b = farther(piece_b)
+    got_c, away_b, sums = lax.optimization_barrier((got_c, away_b, sums))
+    got_b = lax.ppermute(away_b, "tm", [(0, 1)])
+    piece_c = jnp.concatenate([own_c, got_c], axis=1)
+    two_c, rest_c = farther(piece_c)
     pair_g, relay_g = exchanged(two_g), relayed(two_g)
     sums = correlated([got_a, pair_g, two_g, (rest_g, relay_g)], first, sums, False)
-    piece_c = jnp.concatenate([own_c, got_c], axis=1)
-    two_c, rest_c = farther(piece_c)
-    pair_b = exchanged(two_b)
-    sums = correlated([piece_b, pair_b, two_b, rest_b], first, sums, False)
-    pair_c = exchanged(after(two_c, rest_c, sums))
-    return correlated([piece_c, pair_c, two_c, rest_c], [(few, [(0, 0, 0), (0, 0, few)])], sums, True)
+    piece_b = jnp.where(me == 0, after(own_b, relay_g), got_b)
+    two_b, rest_b = farther(piece_b)
+    pair_c = exchanged(two_c)
+    sums = correlated([piece_c, pair_c, two_c, rest_c], [(few, [(0, 0, 0), (0, 0, few)])], sums, False)
+    pair_b = exchanged(after(two_b, rest_b, sums))
+    return correlated([piece_b, pair_b, two_b, rest_b], first, sums, True)
 
 
 def general(volts, fir_taps, place, correlated):

time: 107 us -> 112 us (1.047)
  the two profiles are of different devices: /device:TPU:7 before, /device:TPU:1 now
where the time goes in v17:
time: 112 us; the launch traced here: 111 us
  Pallas kernels  52.5 us (47%)
  waiting for transfers between devices  35.7 us (32%)
  starting transfers between devices  20.8 us (19%)
  other arithmetic  1.18 us (1%)
    pallas_call x3, Pallas kernels, spectra(): pl.pallas_call(functools.partial(spectra_kernel, groups, tuple((part[1:]...  30 us
    ppermute x4, waiting for transfers between devices, shifted(): lax.ppermute(block, axis, [(i, (i + distance) % size) for i in range(size)])  26.6 us
    pallas_call x4, Pallas kernels, correlate(): pl.pallas_call(functools.partial(correlate_kernel, pieces, per_group, sca...  19.2 us
    ppermute x3, starting transfers between devices, farther(): lax.ppermute(block, 'stn', [(i, (i + 1 if i % 2 == 0 else i + 3) % size)...  4.09 us
    ppermute x1, waiting for transfers between devices, paired(): got_c = lax.ppermute(away_c, 'tm', swap)  3.69 us
    ppermute x1, waiting for transfers between devices, relayed(): lax.ppermute(two, 'stn', [(i, i + 1) for i in range(lax.axis_size('stn'))...  3.5 us
    pallas_call x1, Pallas kernels, prepare(): pl.pallas_call(functools.partial(prepare_kernel, edge_block, int(groups =...  3.29 us
    ppermute x4, starting transfers between devices, shifted(): lax.ppermute(block, axis, [(i, (i + distance) % size) for i in range(size)])  3.26 us
  transfers between devices with their start and end apart: 17, of which 6 were waited for; matrix products, arithmetic and copies ran while one was open for 1% of the time, Pallas kernels for 38%

profile of v17, /device:TPU:1, one launch (start us, length us, event | category | flops | bytes accessed | tf_op | source)
XLA Modules:
  0.0 111.2 jit_solution(18229760778456115933)
XLA Ops:
  0.0 0.1 pad_add_fusion.place
  0.1 3.3 %shard_map.46 = (bf16[8,32,64,128]{3,2,1,0:T(8,128)(2,1)S(1)}, bf16[8,8,64,128]{3,2,1,0:T(8,128)(2,1)S(1)}, f32[1024,128]{1,0:T(8,128)S(1)}, bf16[64,192]{1,0:T(...) custom-call(s32[2]{0:T(128)S(1)} %pad_add_fusion.place, bf16[8,32,64,128]{3,2,1,0:T(8,128)(2,1)} %bitcast.10, ...), custom_call_target="tpu_custom_call" | custom-call | tf_op jit(solution)/shard_map/pallas_call | solution.py:110
  3.4 2.1 %collective-permute-start.2 = (bf16[8,8,64,128]{3,2,1,0:T(8,128)(2,1)S(1)}, bf16[8,8,64,128]{3,2,1,0:T(8,128)(2,1)S(1)}, u32[]{:S(2)}, u32[]{:S(2)}) collective-permute-start(bf16[8,8,64,128]{3,2,1,0:T(8,128)(2,1)S(1)} %get-tuple-element.39), channel_id=1, source_target_pairs={{0,1},{1,0},{2,3},{3,2},{4,5},{5,4},{6,7},{7,6},{8,9},{9,8},{10,11... | collective-permute-start | bytes 3145736 | tf_op jit(solution)/shard_map/ppermute | solution.py:434
  5.5 11.3 %shard_map.47 = (bf16[32,4,16,128]{3,2,1,0:T(8,128)(2,1)S(1)}, bf16[32,4,16,128]{3,2,1,0:T(8,128)(2,1)S(1)}) custom-call(s32[2]{0:T(128)S(1)} %pad_add_fusion.place, bf16[8,32,64,128]{3,2,1,0:T(8,128)(2,1)S(1)} %get-tuple-element.29.refs_0_.refs_1_, bf16[8,32,64,128]{3,2,1,0:T(8,128)(2,1)S(1)} %get-tuple-element.29.refs_0_.refs_1_, ...), custom_call_target="tpu_custom_call" | custom-call | flops 1000000 | tf_op jit(solution)/shard_map/pallas_call | solution.py:263
  16.8 1.3 %collective-permute-start.1 = (bf16[32,4,16,128]{3,2,1,0:T(8,128)(2,1)S(1)}, bf16[32,4,16,128]{3,2,1,0:T(8,128)(2,1)S(1)}, u32[]{:S(2)}, u32[]{:S(2)}) collective-permute-start(bf16[32,4,16,128]{3,2,1,0:T(8,128)(2,1)S(1)} %get-tuple-element.34.refs_0_), channel_id=1, source_target_pairs={{0,4},{2,6},{4,8},{6,10},{8,12},{10,14},{12,16},{14,18},{16,20},{1... | collective-permute-start | bytes 1572872 | tf_op jit(solution)/shard_map/ppermute | solution.py:402
  18.1 0.2 collective-permute-start
  18.3 2.7 %collective-permute-start.7 = (bf16[32,4,16,128]{3,2,1,0:T(8,128)(2,1)S(1)}, bf16[32,4,16,128]{3,2,1,0:T(8,128)(2,1)S(1)}, u32[]{:S(2)}, u32[]{:S(2)}) collective-permute-start(bf16[32,4,16,128]{3,2,1,0:T(8,128)(2,1)S(1)} %get-tuple-element.34.refs_0_), channel_id=1, source_target_pairs={{0,2},{2,8},{4,6},{6,12},{8,10},{10,16},{12,14},{14,20},{16,18},{1... | collective-permute-start | bytes 1572872 | tf_op jit(solution)/shard_map/ppermute | solution.py:407
  21.0 12.0 %shard_map.48 = (bf16[32,4,16,128]{3,2,1,0:T(8,128)(2,1)S(1)}, bf16[32,4,16,128]{3,2,1,0:T(8,128)(2,1)}) custom-call(s32[2]{0:T(128)S(1)} %pad_add_fusion.place, bf16[8,32,64,128]{3,2,1,0:T(8,128)(2,1)S(1)} %get-tuple-element.29.refs_0_.refs_1_, bf16[8,32,64,128]{3,2,1,0:T(8,128)(2,1)S(1)} %get-tuple-element.29.refs_0_.refs_1_, ...), custom_call_target="tpu_custom_call" | custom-call | flops 1000000 | tf_op jit(solution)/shard_map/pallas_call | solution.py:263
  33.0 0.0 copy-start
  33.0 0.8 copy-done
  33.8 0.0 collective-permute-done.1.refs_2_
  33.8 0.0 collective-permute-done.2.refs_2_
  33.8 6.7 %shard_map.49 = (bf16[32,2,16,128]{3,2,1,0:T(8,128)(2,1)S(1)}, bf16[32,2,16,128]{3,2,1,0:T(8,128)(2,1)S(1)}) custom-call(s32[2]{0:T(128)S(1)} %pad_add_fusion.place, bf16[8,32,64,128]{3,2,1,0:T(8,128)(2,1)S(1)} %get-tuple-element.29.refs_0_.refs_1_, bf16[8,32,64,128]{3,2,1,0:T(8,128)(2,1)S(1)} %get-tuple-element.29.refs_0_.refs_1_, ...), custom_call_target="tpu_custom_call" | custom-call | flops 1000000 | tf_op jit(solution)/shard_map/pallas_call | solution.py:263
  40.5 0.0 collective-permute-done.refs_0_
  40.6 1.6 %collective-permute-start.6 = (bf16[32,4,16,128]{3,2,1,0:T(8,128)(2,1)S(1)}, bf16[32,4,16,128]{3,2,1,0:T(8,128)(2,1)S(1)}, u32[]{:S(2)}, u32[]{:S(2)}) collective-permute-start(bf16[32,4,16,128]{3,2,1,0:T(8,128)(2,1)S(1)} %collective-permute-done.1.refs_2_), channel_id=1, source_target_pairs={{0,2},{2,0},{4,6},{6,4},{8,10},{10,8},{12,14},{14,12},{16,18},{18,... | collective-permute-start | bytes 1572872 | tf_op jit(solution)/shard_map/ppermute | solution.py:422
  42.1 0.3 collective-permute-start.3
  42.4 1.2 %collective-permute-start.5 = (bf16[32,2,16,128]{3,2,1,0:T(8,128)(2,1)S(1)}, bf16[32,2,16,128]{3,2,1,0:T(8,128)(2,1)S(1)}, u32[]{:S(2)}, u32[]{:S(2)}) collective-permute-start(bf16[32,2,16,128]{3,2,1,0:T(8,128)(2,1)S(1)} %get-tuple-element.45), channel_id=1, source_target_pairs={{0,1},{1,0},{2,3},{3,2},{4,5},{5,4},{6,7},{7,6},{8,9},{9,8},{10,11... | collective-permute-start | bytes 786440 | tf_op jit(solution)/shard_map/ppermute | solution.py:453
  43.7 0.0 collective-permute-done.7.refs_3_
  43.7 0.0 collective-permute-done.6.refs_1_
  43.7 2.7 %shard_map.50.refs_5_ = f32[4096,128]{1,0:T(8,128)S(1)} custom-call(s32[2]{0:T(128)S(1)} %pad_add_fusion.place, bf16[32,4,16,128]{3,2,1,0:T(8,128)(2,1)S(1)} %get-tuple-element.34.refs_0_, bf16[32,4,16,128]{3,2,1,0:T(8,128)(2,1)S(1)} %collective-permute-done.6.refs_1_, bf16[32,4,16,128]{3,2,1,0:T(8,128)(2,1)S(1)} %collective-permute-done.1.refs_2_, ...), custom_call_target="tpu_custom_call" | custom-call | flops 1000 | tf_op jit(solution)/shard_map/pallas_call | solution.py:373
  46.4 3.7 %collective-permute-done.5 = bf16[32,2,16,128]{3,2,1,0:T(8,128)(2,1)S(1)} collective-permute-done((bf16[32,2,16,128]{3,2,1,0:T(8,128)(2,1)S(1)}, bf16[32,2,16,128]{3,2,1,0:T(8,128)(2,1)S(1)}, u32[]{:S(2)}, u32[]{:S(2)}) %collective-permute-start.5) | collective-permute-done | bytes 262176 | tf_op jit(solution)/shard_map/ppermute | solution.py:453
  50.1 8.5 %collective-permute-done.3.refs_2_ = bf16[32,4,16,128]{3,2,1,0:T(8,128)(2,1)} collective-permute-done((bf16[32,4,16,128]{3,2,1,0:T(8,128)(2,1)}, bf16[32,4,16,128]{3,2,1,0:T(8,128)(2,1)}, u32[]{:S(2)}, u32[]{:S(2)}) %collective-permute-start.3) | collective-permute-done | bytes 524320 | tf_op jit(solution)/shard_map/ppermute | solution.py:402
  58.6 2.1 %collective-permute-start.4 = (bf16[32,4,16,128]{3,2,1,0:T(8,128)(2,1)}, bf16[32,4,16,128]{3,2,1,0:T(8,128)(2,1)}, u32[]{:S(2)}, u32[]{:S(2)}) collective-permute-start(bf16[32,4,16,128]{3,2,1,0:T(8,128)(2,1)} %collective-permute-done.3.refs_2_), channel_id=1, source_target_pairs={{2,4},{10,12},{18,20},{26,28},{3,5},{11,13},{19,21},{27,29}} | collective-permute-start | bytes 1572872 | tf_op jit(solution)/shard_map/ppermute | solution.py:418
  60.8 0.1 collective-permute-start.11
  60.8 3.3 %collective-permute-start.8 = (bf16[32,4,16,128]{3,2,1,0:T(8,128)(2,1)}, bf16[32,4,16,128]{3,2,1,0:T(8,128)(2,1)}, u32[]{:S(2)}, u32[]{:S(2)}) collective-permute-start(bf16[32,4,16,128]{3,2,1,0:T(8,128)(2,1)} %get-tuple-element.48), channel_id=1, source_target_pairs={{0,1},{2,3},{4,5},{6,7},{8,9},{10,11},{12,13},{14,15},{16,17},{18,... | collective-permute-start | bytes 1572872 | tf_op jit(solution)/shard_map/ppermute | solution.py:458
  64.1 1.9 %collective-permute-start.15 = (bf16[32,4,16,128]{3,2,1,0:T(8,128)(2,1)}, bf16[32,4,16,128]{3,2,1,0:T(8,128)(2,1)}, u32[]{:S(2)}, u32[]{:S(2)}) collective-permute-start(bf16[32,4,16,128]{3,2,1,0:T(8,128)(2,1)} %collective-permute-done.refs_0_), channel_id=1, source_target_pairs={{0,2},{2,8},{4,6},{8,10},{10,16},{12,14},{16,18},{18,24},{20,22},{... | collective-permute-start | bytes 1572872 | tf_op jit(solution)/shard_map/ppermute | solution.py:414
  66.0 1.3 %collective-permute-start.13 = (bf16[32,4,16,128]{3,2,1,0:T(8,128)(2,1)S(1)}, bf16[32,4,16,128]{3,2,1,0:T(8,128)(2,1)S(1)}, u32[]{:S(2)}, u32[]{:S(2)}) collective-permute-start(bf16[32,4,16,128]{3,2,1,0:T(8,128)(2,1)S(1)} %constant_dynamic-update-slice_fusion.refs_0_), channel_id=1, source_target_pairs={{0,2},{2,8},{4,6},{6,12},{8,10},{10,16},{12,14},{14,20},{16,18},{1... | collective-permute-start | bytes 1572872 | tf_op jit(solution)/shard_map/ppermute | solution.py:407
  67.3 3.5 %collective-permute-done.4.refs_4_ = bf16[32,4,16,128]{3,2,1,0:T(8,128)(2,1)} collective-permute-done((bf16[32,4,16,128]{3,2,1,0:T(8,128)(2,1)}, bf16[32,4,16,128]{3,2,1,0:T(8,128)(2,1)}, u32[]{:S(2)}, u32[]{:S(2)}) %collective-permute-start.4) | collective-permute-done | bytes 524320 | tf_op jit(solution)/shard_map/ppermute | solution.py:418
  70.8 0.0 collective-permute-start.14
  70.8 6.6 %collective-permute-done.11.refs_2_ = bf16[32,4,16,128]{3,2,1,0:T(8,128)(2,1)S(1)} collective-permute-done((bf16[32,4,16,128]{3,2,1,0:T(8,128)(2,1)S(1)}, bf16[32,4,16,128]{3,2,1,0:T(8,128)(2,1)S(1)}, u32[]{:S(2)}, u32[]{:S(2)}) %collective-permute-start.11) | collective-permute-done | bytes 524320 | tf_op jit(solution)/shard_map/ppermute | solution.py:402
  77.5 1.0 collective-permute-start.12
  78.5 0.0 collective-permute-done.8
  78.5 1.1 broadcast_select_fusion.refs_0_
  79.6 0.1 collective-permute-start.10
  79.7 0.0 collective-permute-done.15.refs_3_
  79.7 1.7 %collective-permute-start.9 = (bf16[32,4,16,128]{3,2,1,0:T(8,128)(2,1)S(1)}, bf16[32,4,16,128]{3,2,1,0:T(8,128)(2,1)S(1)}, u32[]{:S(2)}, u32[]{:S(2)}) collective-permute-start(bf16[32,4,16,128]{3,2,1,0:T(8,128)(2,1)S(1)} %broadcast_select_fusion.refs_0_), channel_id=1, source_target_pairs={{0,4},{2,6},{4,8},{6,10},{8,12},{10,14},{12,16},{14,18},{16,20},{1... | collective-permute-start | bytes 1572872 | tf_op jit(solution)/shard_map/ppermute | solution.py:402
  81.3 0.0 collective-permute-done.14.refs_1_
  81.3 5.5 %shard_map.51.refs_4_ = f32[4096,128]{1,0:T(8,128)S(1)} custom-call(s32[2]{0:T(128)S(1)} %pad_add_fusion.place, bf16[32,4,16,128]{3,2,1,0:T(8,128)(2,1)} %collective-permute-done.refs_0_, bf16[32,4,16,128]{3,2,1,0:T(8,128)(2,1)S(1)} %collective-permute-done.14.refs_1_, ...), custom_call_target="tpu_custom_call", output_to_operand_aliasing={{}: (6, {})} | custom-call | flops 1000 | tf_op jit(solution)/shard_map/pallas_call | solution.py:373
  86.8 0.0 collective-permute-done.13.refs_3_
  86.8 0.0 collective-permute-done.12.refs_1_
  86.8 3.7 %shard_map.52.refs_4_ = f32[4096,128]{1,0:T(8,128)S(1)} custom-call(s32[2]{0:T(128)S(1)} %pad_add_fusion.place, bf16[32,4,16,128]{3,2,1,0:T(8,128)(2,1)S(1)} %constant_dynamic-update-slice_fusion.refs_0_, bf16[32,4,16,128]{3,2,1,0:T(8,128)(2,1)S(1)} %collective-permute-done.12.refs_1_, ...), custom_call_target="tpu_custom_call", output_to_operand_aliasing={{}: (5, {})} | custom-call | flops 1000 | tf_op jit(solution)/shard_map/pallas_call | solution.py:373
  90.6 0.0 collective-permute-done.10.refs_3_
  90.6 11.4 %collective-permute-done.9.refs_2_ = bf16[32,4,16,128]{3,2,1,0:T(8,128)(2,1)S(1)} collective-permute-done((bf16[32,4,16,128]{3,2,1,0:T(8,128)(2,1)S(1)}, bf16[32,4,16,128]{3,2,1,0:T(8,128)(2,1)S(1)}, u32[]{:S(2)}, u32[]{:S(2)}) %collective-permute-start.9) | collective-permute-done | bytes 524320 | tf_op jit(solution)/shard_map/ppermute | solution.py:402
  102.0 0.0 collective-permute-start.16
  102.0 1.9 %collective-permute-done.16.refs_1_ = bf16[32,4,16,128]{3,2,1,0:T(8,128)(2,1)S(1)} collective-permute-done((bf16[32,4,16,128]{3,2,1,0:T(8,128)(2,1)S(1)}, bf16[32,4,16,128]{3,2,1,0:T(8,128)(2,1)S(1)}, u32[]{:S(2)}, u32[]{:S(2)}) %collective-permute-start.16) | collective-permute-done | bytes 524320 | tf_op jit(solution)/shard_map/ppermute | solution.py:422
  103.9 7.3 %shard_map.53 = f32[2,8,4,8,8,128]{5,4,3,2,1,0:T(8,128)} custom-call(s32[2]{0:T(128)S(1)} %pad_add_fusion.place, bf16[32,4,16,128]{3,2,1,0:T(8,128)(2,1)S(1)} %broadcast_select_fusion.refs_0_, bf16[32,4,16,128]{3,2,1,0:T(8,128)(2,1)S(1)} %collective-permute-done.16.refs_1_, bf16[32,4,16,128]{3,2,1,0:T(8,128)(2,1)S(1)} %collective-permute-done.9.refs_2_, ...), custom_call_target="tpu_custom_call" | custom-call | flops 1000 | tf_op jit(solution)/shard_map/pallas_call | solution.py:373
  (2 shorter events, 0.1 us)
Async XLA Ops:
  3.4 30.5 %collective-permute-start.2 = (bf16[8,8,64,128]{3,2,1,0:T(8,128)(2,1)S(1)}, bf16[8,8,64,128]{3,2,1,0:T(8,128)(2,1)S(1)}, u32[]{:S(2)}, u32[]{:S(2)}) collective-permute-start(bf16[8,8,64,128]{3,2,1,0:T(8,128)(2,1)S(1)} %get-tuple-element.39), channel_id=1, source_target_pairs={{0,1},{1,0},{2,3},{3,2},{4,5},{5,4},{6,7},{7,6},{8,9},{9,8},{10,11... | collective-permute-start | bytes 3145736 | tf_op jit(solution)/shard_map/ppermute | solution.py:434
  16.8 17.0 %collective-permute-start.1 = (bf16[32,4,16,128]{3,2,1,0:T(8,128)(2,1)S(1)}, bf16[32,4,16,128]{3,2,1,0:T(8,128)(2,1)S(1)}, u32[]{:S(2)}, u32[]{:S(2)}) collective-permute-start(bf16[32,4,16,128]{3,2,1,0:T(8,128)(2,1)S(1)} %get-tuple-element.34.refs_0_), channel_id=1, source_target_pairs={{0,4},{2,6},{4,8},{6,10},{8,12},{10,14},{12,16},{14,18},{16,20},{1... | collective-permute-start | bytes 1572872 | tf_op jit(solution)/shard_map/ppermute | solution.py:402
  18.1 22.5 %collective-permute-start = (bf16[32,4,16,128]{3,2,1,0:T(8,128)(2,1)S(1)}, bf16[32,4,16,128]{3,2,1,0:T(8,128)(2,1)}, u32[]{:S(2)}, u32[]{:S(2)}) collective-permute-start(bf16[32,4,16,128]{3,2,1,0:T(8,128)(2,1)S(1)} %get-tuple-element.37), channel_id=1, source_target_pairs={{0,1},{1,0},{2,3},{3,2},{4,5},{5,4},{6,7},{7,6},{8,9},{9,8},{10,11... | collective-permute-start | bytes 1572872 | tf_op jit(solution)/shard_map/ppermute | solution.py:438
  18.3 25.4 %collective-permute-start.7 = (bf16[32,4,16,128]{3,2,1,0:T(8,128)(2,1)S(1)}, bf16[32,4,16,128]{3,2,1,0:T(8,128)(2,1)S(1)}, u32[]{:S(2)}, u32[]{:S(2)}) collective-permute-start(bf16[32,4,16,128]{3,2,1,0:T(8,128)(2,1)S(1)} %get-tuple-element.34.refs_0_), channel_id=1, source_target_pairs={{0,2},{2,8},{4,6},{6,12},{8,10},{10,16},{12,14},{14,20},{16,18},{1... | collective-permute-start | bytes 1572872 | tf_op jit(solution)/shard_map/ppermute | solution.py:407
  33.0 0.8 copy-start
  40.6 3.1 %collective-permute-start.6 = (bf16[32,4,16,128]{3,2,1,0:T(8,128)(2,1)S(1)}, bf16[32,4,16,128]{3,2,1,0:T(8,128)(2,1)S(1)}, u32[]{:S(2)}, u32[]{:S(2)}) collective-permute-start(bf16[32,4,16,128]{3,2,1,0:T(8,128)(2,1)S(1)} %collective-permute-done.1.refs_2_), channel_id=1, source_target_pairs={{0,2},{2,0},{4,6},{6,4},{8,10},{10,8},{12,14},{14,12},{16,18},{18,... | collective-permute-start | bytes 1572872 | tf_op jit(solution)/shard_map/ppermute | solution.py:422
  42.1 16.5 %collective-permute-start.3 = (bf16[32,4,16,128]{3,2,1,0:T(8,128)(2,1)}, bf16[32,4,16,128]{3,2,1,0:T(8,128)(2,1)}, u32[]{:S(2)}, u32[]{:S(2)}) collective-permute-start(bf16[32,4,16,128]{3,2,1,0:T(8,128)(2,1)} %collective-permute-done.refs_0_), channel_id=1, source_target_pairs={{0,4},{2,6},{4,8},{6,10},{8,12},{10,14},{12,16},{14,18},{16,20},{1... | collective-permute-start | bytes 1572872 | tf_op jit(solution)/shard_map/ppermute | solution.py:402
  42.4 7.7 %collective-permute-start.5 = (bf16[32,2,16,128]{3,2,1,0:T(8,128)(2,1)S(1)}, bf16[32,2,16,128]{3,2,1,0:T(8,128)(2,1)S(1)}, u32[]{:S(2)}, u32[]{:S(2)}) collective-permute-start(bf16[32,2,16,128]{3,2,1,0:T(8,128)(2,1)S(1)} %get-tuple-element.45), channel_id=1, source_target_pairs={{0,1},{1,0},{2,3},{3,2},{4,5},{5,4},{6,7},{7,6},{8,9},{9,8},{10,11... | collective-permute-start | bytes 786440 | tf_op jit(solution)/shard_map/ppermute | solution.py:453
  58.6 12.2 %collective-permute-start.4 = (bf16[32,4,16,128]{3,2,1,0:T(8,128)(2,1)}, bf16[32,4,16,128]{3,2,1,0:T(8,128)(2,1)}, u32[]{:S(2)}, u32[]{:S(2)}) collective-permute-start(bf16[32,4,16,128]{3,2,1,0:T(8,128)(2,1)} %collective-permute-done.3.refs_2_), channel_id=1, source_target_pairs={{2,4},{10,12},{18,20},{26,28},{3,5},{11,13},{19,21},{27,29}} | collective-permute-start | bytes 1572872 | tf_op jit(solution)/shard_map/ppermute | solution.py:418
  60.8 16.7 %collective-permute-start.11 = (bf16[32,4,16,128]{3,2,1,0:T(8,128)(2,1)S(1)}, bf16[32,4,16,128]{3,2,1,0:T(8,128)(2,1)S(1)}, u32[]{:S(2)}, u32[]{:S(2)}) collective-permute-start(bf16[32,4,16,128]{3,2,1,0:T(8,128)(2,1)S(1)} %constant_dynamic-update-slice_fusion.refs_0_), channel_id=1, source_target_pairs={{0,4},{2,6},{4,8},{6,10},{8,12},{10,14},{12,16},{14,18},{16,20},{1... | collective-permute-start | bytes 1572872 | tf_op jit(solution)/shard_map/ppermute | solution.py:402
  60.8 17.7 %collective-permute-start.8 = (bf16[32,4,16,128]{3,2,1,0:T(8,128)(2,1)}, bf16[32,4,16,128]{3,2,1,0:T(8,128)(2,1)}, u32[]{:S(2)}, u32[]{:S(2)}) collective-permute-start(bf16[32,4,16,128]{3,2,1,0:T(8,128)(2,1)} %get-tuple-element.48), channel_id=1, source_target_pairs={{0,1},{2,3},{4,5},{6,7},{8,9},{10,11},{12,13},{14,15},{16,17},{18,... | collective-permute-start | bytes 1572872 | tf_op jit(solution)/shard_map/ppermute | solution.py:458
  64.1 15.6 %collective-permute-start.15 = (bf16[32,4,16,128]{3,2,1,0:T(8,128)(2,1)}, bf16[32,4,16,128]{3,2,1,0:T(8,128)(2,1)}, u32[]{:S(2)}, u32[]{:S(2)}) collective-permute-start(bf16[32,4,16,128]{3,2,1,0:T(8,128)(2,1)} %collective-permute-done.refs_0_), channel_id=1, source_target_pairs={{0,2},{2,8},{4,6},{8,10},{10,16},{12,14},{16,18},{18,24},{20,22},{... | collective-permute-start | bytes 1572872 | tf_op jit(solution)/shard_map/ppermute | solution.py:414
  66.0 20.8 %collective-permute-start.13 = (bf16[32,4,16,128]{3,2,1,0:T(8,128)(2,1)S(1)}, bf16[32,4,16,128]{3,2,1,0:T(8,128)(2,1)S(1)}, u32[]{:S(2)}, u32[]{:S(2)}) collective-permute-start(bf16[32,4,16,128]{3,2,1,0:T(8,128)(2,1)S(1)} %constant_dynamic-update-slice_fusion.refs_0_), channel_id=1, source_target_pairs={{0,2},{2,8},{4,6},{6,12},{8,10},{10,16},{12,14},{14,20},{16,18},{1... | collective-permute-start | bytes 1572872 | tf_op jit(solution)/shard_map/ppermute | solution.py:407
  70.8 10.5 %collective-permute-start.14 = (bf16[32,4,16,128]{3,2,1,0:T(8,128)(2,1)}, bf16[32,4,16,128]{3,2,1,0:T(8,128)(2,1)S(1)}, u32[]{:S(2)}, u32[]{:S(2)}) collective-permute-start(bf16[32,4,16,128]{3,2,1,0:T(8,128)(2,1)} %collective-permute-done.3.refs_2_), channel_id=1, source_target_pairs={{0,2},{2,0},{4,6},{6,4},{8,10},{10,8},{12,14},{14,12},{16,18},{18,... | collective-permute-start | bytes 1572872 | tf_op jit(solution)/shard_map/ppermute | solution.py:422
  77.5 9.4 %collective-permute-start.12 = (bf16[32,4,16,128]{3,2,1,0:T(8,128)(2,1)S(1)}, bf16[32,4,16,128]{3,2,1,0:T(8,128)(2,1)S(1)}, u32[]{:S(2)}, u32[]{:S(2)}) collective-permute-start(bf16[32,4,16,128]{3,2,1,0:T(8,128)(2,1)S(1)} %collective-permute-done.11.refs_2_), channel_id=1, source_target_pairs={{0,2},{2,0},{4,6},{6,4},{8,10},{10,8},{12,14},{14,12},{16,18},{18,... | collective-permute-start | bytes 1572872 | tf_op jit(solution)/shard_map/ppermute | solution.py:422
  79.6 11.0 %collective-permute-start.10 = (bf16[32,4,16,128]{3,2,1,0:T(8,128)(2,1)S(1)}, bf16[32,4,16,128]{3,2,1,0:T(8,128)(2,1)S(1)}, u32[]{:S(2)}, u32[]{:S(2)}) collective-permute-start(bf16[32,4,16,128]{3,2,1,0:T(8,128)(2,1)S(1)} %broadcast_select_fusion.refs_0_), channel_id=1, source_target_pairs={{0,2},{2,8},{4,6},{6,12},{8,10},{10,16},{12,14},{14,20},{16,18},{1... | collective-permute-start | bytes 1572872 | tf_op jit(solution)/shard_map/ppermute | solution.py:407
  79.7 22.3 %collective-permute-start.9 = (bf16[32,4,16,128]{3,2,1,0:T(8,128)(2,1)S(1)}, bf16[32,4,16,128]{3,2,1,0:T(8,128)(2,1)S(1)}, u32[]{:S(2)}, u32[]{:S(2)}) collective-permute-start(bf16[32,4,16,128]{3,2,1,0:T(8,128)(2,1)S(1)} %broadcast_select_fusion.refs_0_), channel_id=1, source_target_pairs={{0,4},{2,6},{4,8},{6,10},{8,12},{10,14},{12,16},{14,18},{16,20},{1... | collective-permute-start | bytes 1572872 | tf_op jit(solution)/shard_map/ppermute | solution.py:402
  102.0 1.9 %collective-permute-start.16 = (bf16[32,4,16,128]{3,2,1,0:T(8,128)(2,1)S(1)}, bf16[32,4,16,128]{3,2,1,0:T(8,128)(2,1)S(1)}, u32[]{:S(2)}, u32[]{:S(2)}) collective-permute-start(bf16[32,4,16,128]{3,2,1,0:T(8,128)(2,1)S(1)} %collective-permute-done.9.refs_2_), channel_id=1, source_target_pairs={{0,2},{2,0},{4,6},{6,4},{8,10},{10,8},{12,14},{14,12},{16,18},{18,... | collective-permute-start | bytes 1572872 | tf_op jit(solution)/shard_map/ppermute | solution.py:422

commit v18 on v16

--- a/solution.py
+++ b/solution.py
@@ -343,7 +343,7 @@
                 sums[rows, :] = total
             return carry
 
-        lax.fori_loop(0, half * tiles, pair, 0, unroll=16)
+        lax.fori_loop(0, half * tiles, pair, 0, unroll=32)
     if not last:
         return
 
@@ -360,7 +360,7 @@
                     at += SUB
         return carry
 
-    lax.fori_loop(0, half // 4 * SUB, finish, 0)
+    lax.fori_loop(0, half // 4 * SUB, finish, 0, unroll=8)
 
 
 def correlate(arrays, pieces, per_group, place, scale, before, last, wait=(), cost=10**3):

time: 107 us -> 105 us (0.981)
  Pallas kernels: 42.3 us -> 38.4 us
  waiting for transfers between devices: 35.6 us -> 36.8 us
    pallas_call x4, Pallas kernels: 19.6 us -> 15.7 us  [correlate(): pl.pallas_call(functools.partial(correlate_kernel, pieces, per_group, sca...]
where the time goes in v18:
time: 105 us; the launch traced here: 104 us
  Pallas kernels  38.4 us (37%)
  waiting for transfers between devices  36.8 us (35%)
  starting transfers between devices  27.2 us (26%)
  other arithmetic  1.17 us (1%)
    pallas_call x3, Pallas kernels, spectra(): pl.pallas_call(functools.partial(spectra_kernel, groups, tuple((part[1:]...  19.5 us
    pallas_call x4, Pallas kernels, correlate(): pl.pallas_call(functools.partial(correlate_kernel, pieces, per_group, sca...  15.7 us
    ppermute x4, waiting for transfers between devices, shifted(): lax.ppermute(block, axis, [(i, (i + distance) % size) for i in range(size)])  12.4 us
    ppermute x1, waiting for transfers between devices, paired(): got_b = lax.ppermute(away_b, 'tm', [(0, 1)])  10.9 us
    ppermute x4, starting transfers between devices, exchanged(): lax.ppermute(block, 'stn', [(i, i ^ 1) for i in range(lax.axis_size('stn'...  9.9 us
    ppermute x4, starting transfers between devices, shifted(): lax.ppermute(block, axis, [(i, (i + distance) % size) for i in range(size)])  7.07 us
    ppermute x1, waiting for transfers between devices, paired(): got_c = lax.ppermute(away_c, 'tm', swap)  6.51 us
    ppermute x3, starting transfers between devices, farther(): lax.ppermute(block, 'stn', [(i, (i + 1 if i % 2 == 0 else i + 3) % size)...  5.49 us
  transfers between devices with their start and end apart: 17, of which 8 were waited for; matrix products, arithmetic and copies ran while one was open for 1% of the time, Pallas kernels for 29%

profile of v18, /device:TPU:7, one launch (start us, length us, event | category | flops | bytes accessed | tf_op | source)
XLA Modules:
  0.0 104.5 jit_solution(76521605539142324)
XLA Ops:
  0.0 0.1 pad_add_fusion.place
  0.1 3.3 %shard_map.46 = (bf16[8,32,64,128]{3,2,1,0:T(8,128)(2,1)S(1)}, bf16[8,8,64,128]{3,2,1,0:T(8,128)(2,1)S(1)}, f32[1024,128]{1,0:T(8,128)S(1)}, bf16[64,192]{1,0:T(...) custom-call(s32[2]{0:T(128)S(1)} %pad_add_fusion.place, bf16[8,32,64,128]{3,2,1,0:T(8,128)(2,1)} %bitcast.10, ...), custom_call_target="tpu_custom_call" | custom-call | tf_op jit(solution)/shard_map/pallas_call | solution.py:110
  3.4 0.3 collective-permute-start.2
  3.7 11.4 %shard_map.47 = (bf16[32,4,16,128]{3,2,1,0:T(8,128)(2,1)S(1)}, bf16[32,4,16,128]{3,2,1,0:T(8,128)(2,1)S(1)}) custom-call(s32[2]{0:T(128)S(1)} %pad_add_fusion.place, bf16[8,32,64,128]{3,2,1,0:T(8,128)(2,1)S(1)} %get-tuple-element.28.refs_0_.refs_1_, bf16[8,32,64,128]{3,2,1,0:T(8,128)(2,1)S(1)} %get-tuple-element.28.refs_0_.refs_1_, ...), custom_call_target="tpu_custom_call" | custom-call | flops 1000000 | tf_op jit(solution)/shard_map/pallas_call | solution.py:263
  15.0 1.3 %collective-permute-start.1 = (bf16[32,4,16,128]{3,2,1,0:T(8,128)(2,1)S(1)}, bf16[32,4,16,128]{3,2,1,0:T(8,128)(2,1)S(1)}, u32[]{:S(2)}, u32[]{:S(2)}) collective-permute-start(bf16[32,4,16,128]{3,2,1,0:T(8,128)(2,1)S(1)} %get-tuple-element.34.refs_0_), channel_id=1, source_target_pairs={{0,4},{2,6},{4,8},{6,10},{8,12},{10,14},{12,16},{14,18},{16,20},{1... | collective-permute-start | bytes 1572872 | tf_op jit(solution)/shard_map/ppermute | solution.py:402
  16.4 1.2 %collective-permute-start = (bf16[32,4,16,128]{3,2,1,0:T(8,128)(2,1)S(1)}, bf16[32,4,16,128]{3,2,1,0:T(8,128)(2,1)S(1)}, u32[]{:S(2)}, u32[]{:S(2)}) collective-permute-start(bf16[32,4,16,128]{3,2,1,0:T(8,128)(2,1)S(1)} %get-tuple-element.33), channel_id=1, source_target_pairs={{0,1},{1,0},{2,3},{3,2},{4,5},{5,4},{6,7},{7,6},{8,9},{9,8},{10,11... | collective-permute-start | bytes 1572872 | tf_op jit(solution)/shard_map/ppermute | solution.py:438
  17.6 2.7 %collective-permute-start.5 = (bf16[32,4,16,128]{3,2,1,0:T(8,128)(2,1)S(1)}, bf16[32,4,16,128]{3,2,1,0:T(8,128)(2,1)S(1)}, u32[]{:S(2)}, u32[]{:S(2)}) collective-permute-start(bf16[32,4,16,128]{3,2,1,0:T(8,128)(2,1)S(1)} %get-tuple-element.34.refs_0_), channel_id=1, source_target_pairs={{0,2},{2,8},{4,6},{6,12},{8,10},{10,16},{12,14},{14,20},{16,18},{1... | collective-permute-start | bytes 1572872 | tf_op jit(solution)/shard_map/ppermute | solution.py:407
  20.3 1.4 %shard_map.48 = (bf16[32,4,16,128]{3,2,1,0:T(8,128)(2,1)S(1)}, bf16[32,4,16,128]{3,2,1,0:T(8,128)(2,1)}) custom-call(s32[2]{0:T(128)S(1)} %pad_add_fusion.place, bf16[8,32,64,128]{3,2,1,0:T(8,128)(2,1)S(1)} %get-tuple-element.28.refs_0_.refs_1_, bf16[8,32,64,128]{3,2,1,0:T(8,128)(2,1)S(1)} %get-tuple-element.28.refs_0_.refs_1_, ...), custom_call_target="tpu_custom_call" | custom-call | flops 1000000 | tf_op jit(solution)/shard_map/pallas_call | solution.py:263
  21.6 5.9 %collective-permute-done.1.refs_2_ = bf16[32,4,16,128]{3,2,1,0:T(8,128)(2,1)S(1)} collective-permute-done((bf16[32,4,16,128]{3,2,1,0:T(8,128)(2,1)S(1)}, bf16[32,4,16,128]{3,2,1,0:T(8,128)(2,1)S(1)}, u32[]{:S(2)}, u32[]{:S(2)}) %collective-permute-start.1) | collective-permute-done | bytes 524320 | tf_op jit(solution)/shard_map/ppermute | solution.py:402
  27.6 0.0 collective-permute-done.2.refs_2_
  27.6 6.7 %shard_map.49 = (bf16[32,2,16,128]{3,2,1,0:T(8,128)(2,1)S(1)}, bf16[32,2,16,128]{3,2,1,0:T(8,128)(2,1)S(1)}) custom-call(s32[2]{0:T(128)S(1)} %pad_add_fusion.place, bf16[8,32,64,128]{3,2,1,0:T(8,128)(2,1)S(1)} %get-tuple-element.28.refs_0_.refs_1_, bf16[8,32,64,128]{3,2,1,0:T(8,128)(2,1)S(1)} %get-tuple-element.28.refs_0_.refs_1_, ...), custom_call_target="tpu_custom_call" | custom-call | flops 1000000 | tf_op jit(solution)/shard_map/pallas_call | solution.py:263
  34.3 0.0 copy-start
  34.3 0.7 copy-done
  35.0 3.7 %collective-permute-done.refs_0_ = bf16[32,4,16,128]{3,2,1,0:T(8,128)(2,1)S(1)} collective-permute-done((bf16[32,4,16,128]{3,2,1,0:T(8,128)(2,1)S(1)}, bf16[32,4,16,128]{3,2,1,0:T(8,128)(2,1)S(1)}, u32[]{:S(2)}, u32[]{:S(2)}) %collective-permute-start) | collective-permute-done | bytes 524320 | tf_op jit(solution)/shard_map/ppermute | solution.py:438
  38.7 1.5 %collective-permute-start.4 = (bf16[32,4,16,128]{3,2,1,0:T(8,128)(2,1)S(1)}, bf16[32,4,16,128]{3,2,1,0:T(8,128)(2,1)S(1)}, u32[]{:S(2)}, u32[]{:S(2)}) collective-permute-start(bf16[32,4,16,128]{3,2,1,0:T(8,128)(2,1)S(1)} %collective-permute-done.1.refs_2_), channel_id=1, source_target_pairs={{0,2},{2,0},{4,6},{6,4},{8,10},{10,8},{12,14},{14,12},{16,18},{18,... | collective-permute-start | bytes 1572872 | tf_op jit(solution)/shard_map/ppermute | solution.py:422
  40.2 1.3 %collective-permute-start.3 = (bf16[32,4,16,128]{3,2,1,0:T(8,128)(2,1)}, bf16[32,4,16,128]{3,2,1,0:T(8,128)(2,1)}, u32[]{:S(2)}, u32[]{:S(2)}) collective-permute-start(bf16[32,4,16,128]{3,2,1,0:T(8,128)(2,1)} %get-tuple-element.43), channel_id=1, source_target_pairs={{0,1},{2,3},{4,5},{6,7},{8,9},{10,11},{12,13},{14,15},{16,17},{18,... | collective-permute-start | bytes 1572872 | tf_op jit(solution)/shard_map/ppermute | solution.py:453
  41.5 1.3 %collective-permute-start.12 = (bf16[32,4,16,128]{3,2,1,0:T(8,128)(2,1)S(1)}, bf16[32,4,16,128]{3,2,1,0:T(8,128)(2,1)}, u32[]{:S(2)}, u32[]{:S(2)}) collective-permute-start(bf16[32,4,16,128]{3,2,1,0:T(8,128)(2,1)S(1)} %collective-permute-done.refs_0_), channel_id=1, source_target_pairs={{0,4},{2,6},{4,8},{6,10},{8,12},{10,14},{12,16},{14,18},{16,20},{1... | collective-permute-start | bytes 1572872 | tf_op jit(solution)/shard_map/ppermute | solution.py:402
  42.9 0.0 copy-start.1
  42.9 0.0 collective-permute-done.5.refs_3_
  42.9 0.0 collective-permute-done.4.refs_1_
  42.9 2.2 %shard_map.50.refs_5_ = f32[4096,128]{1,0:T(8,128)S(1)} custom-call(s32[2]{0:T(128)S(1)} %pad_add_fusion.place, bf16[32,4,16,128]{3,2,1,0:T(8,128)(2,1)S(1)} %get-tuple-element.34.refs_0_, bf16[32,4,16,128]{3,2,1,0:T(8,128)(2,1)S(1)} %collective-permute-done.4.refs_1_, bf16[32,4,16,128]{3,2,1,0:T(8,128)(2,1)S(1)} %collective-permute-done.1.refs_2_, ...), custom_call_target="tpu_custom_call" | custom-call | flops 1000 | tf_op jit(solution)/shard_map/pallas_call | solution.py:373
  45.1 10.9 %collective-permute-done.3 = bf16[32,4,16,128]{3,2,1,0:T(8,128)(2,1)} collective-permute-done((bf16[32,4,16,128]{3,2,1,0:T(8,128)(2,1)}, bf16[32,4,16,128]{3,2,1,0:T(8,128)(2,1)}, u32[]{:S(2)}, u32[]{:S(2)}) %collective-permute-start.3) | collective-permute-done | bytes 524320 | tf_op jit(solution)/shard_map/ppermute | solution.py:453
  56.0 1.1 %broadcast_select_fusion.refs_0_ = bf16[32,4,16,128]{3,2,1,0:T(8,128)(2,1)S(1)} fusion(bf16[32,4,16,128]{3,2,1,0:T(8,128)(2,1)S(1)} %get-tuple-element.36, bf16[32,4,16,128]{3,2,1,0:T(8,128)(2,1)} %collective-permute-done.3, pred[]{:T(512)S(6)} %eq.5), kind=kLoop, calls=%fused_computation | loop fusion | flops 262144 | bytes 1572865 | tf_op jit(solution)/shard_map/jit(_where)/select_n | solution.py:459
  57.1 1.3 %collective-permute-start.9 = (bf16[32,4,16,128]{3,2,1,0:T(8,128)(2,1)S(1)}, bf16[32,4,16,128]{3,2,1,0:T(8,128)(2,1)S(1)}, u32[]{:S(2)}, u32[]{:S(2)}) collective-permute-start(bf16[32,4,16,128]{3,2,1,0:T(8,128)(2,1)S(1)} %broadcast_select_fusion.refs_0_), channel_id=1, source_target_pairs={{0,4},{2,6},{4,8},{6,10},{8,12},{10,14},{12,16},{14,18},{16,20},{1... | collective-permute-start | bytes 1572872 | tf_op jit(solution)/shard_map/ppermute | solution.py:402
  58.4 1.3 %collective-permute-start.14 = (bf16[32,4,16,128]{3,2,1,0:T(8,128)(2,1)S(1)}, bf16[32,4,16,128]{3,2,1,0:T(8,128)(2,1)S(1)}, u32[]{:S(2)}, u32[]{:S(2)}) collective-permute-start(bf16[32,4,16,128]{3,2,1,0:T(8,128)(2,1)S(1)} %collective-permute-done.refs_0_), channel_id=1, source_target_pairs={{0,2},{2,8},{4,6},{8,10},{10,16},{12,14},{16,18},{18,24},{20,22},{... | collective-permute-start | bytes 1572872 | tf_op jit(solution)/shard_map/ppermute | solution.py:414
  59.7 0.0 collective-permute-done.12.refs_2_
  59.7 1.2 %collective-permute-start.13 = (bf16[32,4,16,128]{3,2,1,0:T(8,128)(2,1)}, bf16[32,4,16,128]{3,2,1,0:T(8,128)(2,1)S(1)}, u32[]{:S(2)}, u32[]{:S(2)}) collective-permute-start(bf16[32,4,16,128]{3,2,1,0:T(8,128)(2,1)} %collective-permute-done.12.refs_2_), channel_id=1, source_target_pairs={{0,2},{2,0},{4,6},{6,4},{8,10},{10,8},{12,14},{14,12},{16,18},{18,... | collective-permute-start | bytes 1572872 | tf_op jit(solution)/shard_map/ppermute | solution.py:422
  60.9 0.0 copy-done.1
  60.9 0.0 collective-permute-start.6
  61.0 1.3 %collective-permute-start.11 = (bf16[32,4,16,128]{3,2,1,0:T(8,128)(2,1)S(1)}, bf16[32,4,16,128]{3,2,1,0:T(8,128)(2,1)S(1)}, u32[]{:S(2)}, u32[]{:S(2)}) collective-permute-start(bf16[32,4,16,128]{3,2,1,0:T(8,128)(2,1)S(1)} %broadcast_select_fusion.refs_0_), channel_id=1, source_target_pairs={{0,2},{2,8},{4,6},{6,12},{8,10},{10,16},{12,14},{14,20},{16,18},{1... | collective-permute-start | bytes 1572872 | tf_op jit(solution)/shard_map/ppermute | solution.py:407
  62.3 6.5 %collective-permute-done.6 = bf16[32,2,16,128]{3,2,1,0:T(8,128)(2,1)S(1)} collective-permute-done((bf16[32,2,16,128]{3,2,1,0:T(8,128)(2,1)S(1)}, bf16[32,2,16,128]{3,2,1,0:T(8,128)(2,1)S(1)}, u32[]{:S(2)}, u32[]{:S(2)}) %collective-permute-start.6) | collective-permute-done | bytes 262176 | tf_op jit(solution)/shard_map/ppermute | solution.py:458
  68.8 0.7 collective-permute-start.15
  69.6 0.3 collective-permute-done.9.refs_2_
  69.8 2.0 %collective-permute-start.10 = (bf16[32,4,16,128]{3,2,1,0:T(8,128)(2,1)S(1)}, bf16[32,4,16,128]{3,2,1,0:T(8,128)(2,1)S(1)}, u32[]{:S(2)}, u32[]{:S(2)}) collective-permute-start(bf16[32,4,16,128]{3,2,1,0:T(8,128)(2,1)S(1)} %collective-permute-done.9.refs_2_), channel_id=1, source_target_pairs={{0,2},{2,0},{4,6},{6,4},{8,10},{10,8},{12,14},{14,12},{16,18},{18,... | collective-permute-start | bytes 1572872 | tf_op jit(solution)/shard_map/ppermute | solution.py:422
  71.8 0.0 collective-permute-done.14.refs_3_
  71.8 3.1 %collective-permute-start.7 = (bf16[32,4,16,128]{3,2,1,0:T(8,128)(2,1)S(1)}, bf16[32,4,16,128]{3,2,1,0:T(8,128)(2,1)S(1)}, u32[]{:S(2)}, u32[]{:S(2)}) collective-permute-start(bf16[32,4,16,128]{3,2,1,0:T(8,128)(2,1)S(1)} %constant_dynamic-update-slice_fusion.refs_0_), channel_id=1, source_target_pairs={{0,4},{2,6},{4,8},{6,10},{8,12},{10,14},{12,16},{14,18},{16,20},{1... | collective-permute-start | bytes 1572872 | tf_op jit(solution)/shard_map/ppermute | solution.py:402
  74.9 0.0 collective-permute-done.13.refs_1_
  74.9 1.5 %collective-permute-start.8 = (bf16[32,4,16,128]{3,2,1,0:T(8,128)(2,1)S(1)}, bf16[32,4,16,128]{3,2,1,0:T(8,128)(2,1)S(1)}, u32[]{:S(2)}, u32[]{:S(2)}) collective-permute-start(bf16[32,4,16,128]{3,2,1,0:T(8,128)(2,1)S(1)} %constant_dynamic-update-slice_fusion.refs_0_), channel_id=1, source_target_pairs={{0,2},{2,8},{4,6},{6,12},{8,10},{10,16},{12,14},{14,20},{16,18},{1... | collective-permute-start | bytes 1572872 | tf_op jit(solution)/shard_map/ppermute | solution.py:407
  76.4 0.0 collective-permute-done.15.refs_4_
  76.4 4.7 %shard_map.51.refs_4_ = f32[4096,128]{1,0:T(8,128)S(1)} custom-call(s32[2]{0:T(128)S(1)} %pad_add_fusion.place, bf16[32,4,16,128]{3,2,1,0:T(8,128)(2,1)S(1)} %collective-permute-done.refs_0_, bf16[32,4,16,128]{3,2,1,0:T(8,128)(2,1)S(1)} %collective-permute-done.13.refs_1_, ...), custom_call_target="tpu_custom_call", output_to_operand_aliasing={{}: (6, {})} | custom-call | flops 1000 | tf_op jit(solution)/shard_map/pallas_call | solution.py:373
  81.1 0.0 collective-permute-done.11.refs_3_
  81.1 0.0 collective-permute-done.10.refs_1_
  81.1 3.6 %shard_map.52.refs_4_ = f32[4096,128]{1,0:T(8,128)S(1)} custom-call(s32[2]{0:T(128)S(1)} %pad_add_fusion.place, bf16[32,4,16,128]{3,2,1,0:T(8,128)(2,1)S(1)} %broadcast_select_fusion.refs_0_, bf16[32,4,16,128]{3,2,1,0:T(8,128)(2,1)S(1)} %collective-permute-done.10.refs_1_, ...), custom_call_target="tpu_custom_call", output_to_operand_aliasing={{}: (5, {})} | custom-call | flops 1000 | tf_op jit(solution)/shard_map/pallas_call | solution.py:373
  84.7 6.2 %collective-permute-done.7.refs_2_ = bf16[32,4,16,128]{3,2,1,0:T(8,128)(2,1)S(1)} collective-permute-done((bf16[32,4,16,128]{3,2,1,0:T(8,128)(2,1)S(1)}, bf16[32,4,16,128]{3,2,1,0:T(8,128)(2,1)S(1)}, u32[]{:S(2)}, u32[]{:S(2)}) %collective-permute-start.7) | collective-permute-done | bytes 524320 | tf_op jit(solution)/shard_map/ppermute | solution.py:402
  90.9 1.7 %collective-permute-done.8.refs_3_ = bf16[32,4,16,128]{3,2,1,0:T(8,128)(2,1)S(1)} collective-permute-done((bf16[32,4,16,128]{3,2,1,0:T(8,128)(2,1)S(1)}, bf16[32,4,16,128]{3,2,1,0:T(8,128)(2,1)S(1)}, u32[]{:S(2)}, u32[]{:S(2)}) %collective-permute-start.8) | collective-permute-done | bytes 524320 | tf_op jit(solution)/shard_map/ppermute | solution.py:407
  92.6 5.1 %collective-permute-start.16 = (bf16[32,4,16,128]{3,2,1,0:T(8,128)(2,1)S(1)}, bf16[32,4,16,128]{3,2,1,0:T(8,128)(2,1)S(1)}, u32[]{:S(2)}, u32[]{:S(2)}) collective-permute-start(bf16[32,4,16,128]{3,2,1,0:T(8,128)(2,1)S(1)} %collective-permute-done.7.refs_2_), channel_id=1, source_target_pairs={{0,2},{2,0},{4,6},{6,4},{8,10},{10,8},{12,14},{14,12},{16,18},{18,... | collective-permute-start | bytes 1572872 | tf_op jit(solution)/shard_map/ppermute | solution.py:422
  97.8 1.5 %collective-permute-done.16.refs_1_ = bf16[32,4,16,128]{3,2,1,0:T(8,128)(2,1)S(1)} collective-permute-done((bf16[32,4,16,128]{3,2,1,0:T(8,128)(2,1)S(1)}, bf16[32,4,16,128]{3,2,1,0:T(8,128)(2,1)S(1)}, u32[]{:S(2)}, u32[]{:S(2)}) %collective-permute-start.16) | collective-permute-done | bytes 524320 | tf_op jit(solution)/shard_map/ppermute | solution.py:422
  99.3 5.2 %shard_map.53 = f32[2,8,4,8,8,128]{5,4,3,2,1,0:T(8,128)} custom-call(s32[2]{0:T(128)S(1)} %pad_add_fusion.place, bf16[32,4,16,128]{3,2,1,0:T(8,128)(2,1)S(1)} %constant_dynamic-update-slice_fusion.refs_0_, bf16[32,4,16,128]{3,2,1,0:T(8,128)(2,1)S(1)} %collective-permute-done.16.refs_1_, bf16[32,4,16,128]{3,2,1,0:T(8,128)(2,1)S(1)} %collective-permute-done.7.refs_2_, ...), custom_call_target="tpu_custom_call" | custom-call | flops 1000 | tf_op jit(solution)/shard_map/pallas_call | solution.py:373
  (2 shorter events, 0.1 us)
Async XLA Ops:
  3.4 24.2 %collective-permute-start.2 = (bf16[8,8,64,128]{3,2,1,0:T(8,128)(2,1)S(1)}, bf16[8,8,64,128]{3,2,1,0:T(8,128)(2,1)S(1)}, u32[]{:S(2)}, u32[]{:S(2)}) collective-permute-start(bf16[8,8,64,128]{3,2,1,0:T(8,128)(2,1)S(1)} %get-tuple-element.38), channel_id=1, source_target_pairs={{0,1},{1,0},{2,3},{3,2},{4,5},{5,4},{6,7},{7,6},{8,9},{9,8},{10,11... | collective-permute-start | bytes 3145736 | tf_op jit(solution)/shard_map/ppermute | solution.py:434
  15.0 12.5 %collective-permute-start.1 = (bf16[32,4,16,128]{3,2,1,0:T(8,128)(2,1)S(1)}, bf16[32,4,16,128]{3,2,1,0:T(8,128)(2,1)S(1)}, u32[]{:S(2)}, u32[]{:S(2)}) collective-permute-start(bf16[32,4,16,128]{3,2,1,0:T(8,128)(2,1)S(1)} %get-tuple-element.34.refs_0_), channel_id=1, source_target_pairs={{0,4},{2,6},{4,8},{6,10},{8,12},{10,14},{12,16},{14,18},{16,20},{1... | collective-permute-start | bytes 1572872 | tf_op jit(solution)/shard_map/ppermute | solution.py:402
  16.4 22.3 %collective-permute-start = (bf16[32,4,16,128]{3,2,1,0:T(8,128)(2,1)S(1)}, bf16[32,4,16,128]{3,2,1,0:T(8,128)(2,1)S(1)}, u32[]{:S(2)}, u32[]{:S(2)}) collective-permute-start(bf16[32,4,16,128]{3,2,1,0:T(8,128)(2,1)S(1)} %get-tuple-element.33), channel_id=1, source_target_pairs={{0,1},{1,0},{2,3},{3,2},{4,5},{5,4},{6,7},{7,6},{8,9},{9,8},{10,11... | collective-permute-start | bytes 1572872 | tf_op jit(solution)/shard_map/ppermute | solution.py:438
  17.6 25.3 %collective-permute-start.5 = (bf16[32,4,16,128]{3,2,1,0:T(8,128)(2,1)S(1)}, bf16[32,4,16,128]{3,2,1,0:T(8,128)(2,1)S(1)}, u32[]{:S(2)}, u32[]{:S(2)}) collective-permute-start(bf16[32,4,16,128]{3,2,1,0:T(8,128)(2,1)S(1)} %get-tuple-element.34.refs_0_), channel_id=1, source_target_pairs={{0,2},{2,8},{4,6},{6,12},{8,10},{10,16},{12,14},{14,20},{16,18},{1... | collective-permute-start | bytes 1572872 | tf_op jit(solution)/shard_map/ppermute | solution.py:407
  34.3 0.7 copy-start
  38.7 4.2 %collective-permute-start.4 = (bf16[32,4,16,128]{3,2,1,0:T(8,128)(2,1)S(1)}, bf16[32,4,16,128]{3,2,1,0:T(8,128)(2,1)S(1)}, u32[]{:S(2)}, u32[]{:S(2)}) collective-permute-start(bf16[32,4,16,128]{3,2,1,0:T(8,128)(2,1)S(1)} %collective-permute-done.1.refs_2_), channel_id=1, source_target_pairs={{0,2},{2,0},{4,6},{6,4},{8,10},{10,8},{12,14},{14,12},{16,18},{18,... | collective-permute-start | bytes 1572872 | tf_op jit(solution)/shard_map/ppermute | solution.py:422
  40.2 15.8 %collective-permute-start.3 = (bf16[32,4,16,128]{3,2,1,0:T(8,128)(2,1)}, bf16[32,4,16,128]{3,2,1,0:T(8,128)(2,1)}, u32[]{:S(2)}, u32[]{:S(2)}) collective-permute-start(bf16[32,4,16,128]{3,2,1,0:T(8,128)(2,1)} %get-tuple-element.43), channel_id=1, source_target_pairs={{0,1},{2,3},{4,5},{6,7},{8,9},{10,11},{12,13},{14,15},{16,17},{18,... | collective-permute-start | bytes 1572872 | tf_op jit(solution)/shard_map/ppermute | solution.py:453
  41.5 18.2 %collective-permute-start.12 = (bf16[32,4,16,128]{3,2,1,0:T(8,128)(2,1)S(1)}, bf16[32,4,16,128]{3,2,1,0:T(8,128)(2,1)}, u32[]{:S(2)}, u32[]{:S(2)}) collective-permute-start(bf16[32,4,16,128]{3,2,1,0:T(8,128)(2,1)S(1)} %collective-permute-done.refs_0_), channel_id=1, source_target_pairs={{0,4},{2,6},{4,8},{6,10},{8,12},{10,14},{12,16},{14,18},{16,20},{1... | collective-permute-start | bytes 1572872 | tf_op jit(solution)/shard_map/ppermute | solution.py:402
  42.9 18.1 %copy-start.1 = (bf16[32,2,16,128]{3,2,1,0:T(8,128)(2,1)S(1)}, bf16[32,2,16,128]{3,2,1,0:T(8,128)(2,1)}, u32[]{:S(2)}) copy-start(bf16[32,2,16,128]{3,2,1,0:T(8,128)(2,1)} %copy-done) | copy-start | bytes 786436
  57.1 12.7 %collective-permute-start.9 = (bf16[32,4,16,128]{3,2,1,0:T(8,128)(2,1)S(1)}, bf16[32,4,16,128]{3,2,1,0:T(8,128)(2,1)S(1)}, u32[]{:S(2)}, u32[]{:S(2)}) collective-permute-start(bf16[32,4,16,128]{3,2,1,0:T(8,128)(2,1)S(1)} %broadcast_select_fusion.refs_0_), channel_id=1, source_target_pairs={{0,4},{2,6},{4,8},{6,10},{8,12},{10,14},{12,16},{14,18},{16,20},{1... | collective-permute-start | bytes 1572872 | tf_op jit(solution)/shard_map/ppermute | solution.py:402
  58.4 13.4 %collective-permute-start.14 = (bf16[32,4,16,128]{3,2,1,0:T(8,128)(2,1)S(1)}, bf16[32,4,16,128]{3,2,1,0:T(8,128)(2,1)S(1)}, u32[]{:S(2)}, u32[]{:S(2)}) collective-permute-start(bf16[32,4,16,128]{3,2,1,0:T(8,128)(2,1)S(1)} %collective-permute-done.refs_0_), channel_id=1, source_target_pairs={{0,2},{2,8},{4,6},{8,10},{10,16},{12,14},{16,18},{18,24},{20,22},{... | collective-permute-start | bytes 1572872 | tf_op jit(solution)/shard_map/ppermute | solution.py:414
  59.7 15.2 %collective-permute-start.13 = (bf16[32,4,16,128]{3,2,1,0:T(8,128)(2,1)}, bf16[32,4,16,128]{3,2,1,0:T(8,128)(2,1)S(1)}, u32[]{:S(2)}, u32[]{:S(2)}) collective-permute-start(bf16[32,4,16,128]{3,2,1,0:T(8,128)(2,1)} %collective-permute-done.12.refs_2_), channel_id=1, source_target_pairs={{0,2},{2,0},{4,6},{6,4},{8,10},{10,8},{12,14},{14,12},{16,18},{18,... | collective-permute-start | bytes 1572872 | tf_op jit(solution)/shard_map/ppermute | solution.py:422
  60.9 7.9 %collective-permute-start.6 = (bf16[32,2,16,128]{3,2,1,0:T(8,128)(2,1)S(1)}, bf16[32,2,16,128]{3,2,1,0:T(8,128)(2,1)S(1)}, u32[]{:S(2)}, u32[]{:S(2)}) collective-permute-start(bf16[32,2,16,128]{3,2,1,0:T(8,128)(2,1)S(1)} %copy-done.1), channel_id=1, source_target_pairs={{0,1},{1,0},{2,3},{3,2},{4,5},{5,4},{6,7},{7,6},{8,9},{9,8},{10,11... | collective-permute-start | bytes 786440 | tf_op jit(solution)/shard_map/ppermute | solution.py:458
  61.0 20.1 %collective-permute-start.11 = (bf16[32,4,16,128]{3,2,1,0:T(8,128)(2,1)S(1)}, bf16[32,4,16,128]{3,2,1,0:T(8,128)(2,1)S(1)}, u32[]{:S(2)}, u32[]{:S(2)}) collective-permute-start(bf16[32,4,16,128]{3,2,1,0:T(8,128)(2,1)S(1)} %broadcast_select_fusion.refs_0_), channel_id=1, source_target_pairs={{0,2},{2,8},{4,6},{6,12},{8,10},{10,16},{12,14},{14,20},{16,18},{1... | collective-permute-start | bytes 1572872 | tf_op jit(solution)/shard_map/ppermute | solution.py:407
  68.8 7.6 %collective-permute-start.15 = (bf16[32,4,16,128]{3,2,1,0:T(8,128)(2,1)}, bf16[32,4,16,128]{3,2,1,0:T(8,128)(2,1)S(1)}, u32[]{:S(2)}, u32[]{:S(2)}) collective-permute-start(bf16[32,4,16,128]{3,2,1,0:T(8,128)(2,1)} %collective-permute-done.12.refs_2_), channel_id=1, source_target_pairs={{2,4},{10,12},{18,20},{26,28},{3,5},{11,13},{19,21},{27,29}} | collective-permute-start | bytes 1572872 | tf_op jit(solution)/shard_map/ppermute | solution.py:418
  69.8 11.3 %collective-permute-start.10 = (bf16[32,4,16,128]{3,2,1,0:T(8,128)(2,1)S(1)}, bf16[32,4,16,128]{3,2,1,0:T(8,128)(2,1)S(1)}, u32[]{:S(2)}, u32[]{:S(2)}) collective-permute-start(bf16[32,4,16,128]{3,2,1,0:T(8,128)(2,1)S(1)} %collective-permute-done.9.refs_2_), channel_id=1, source_target_pairs={{0,2},{2,0},{4,6},{6,4},{8,10},{10,8},{12,14},{14,12},{16,18},{18,... | collective-permute-start | bytes 1572872 | tf_op jit(solution)/shard_map/ppermute | solution.py:422
  71.8 19.1 %collective-permute-start.7 = (bf16[32,4,16,128]{3,2,1,0:T(8,128)(2,1)S(1)}, bf16[32,4,16,128]{3,2,1,0:T(8,128)(2,1)S(1)}, u32[]{:S(2)}, u32[]{:S(2)}) collective-permute-start(bf16[32,4,16,128]{3,2,1,0:T(8,128)(2,1)S(1)} %constant_dynamic-update-slice_fusion.refs_0_), channel_id=1, source_target_pairs={{0,4},{2,6},{4,8},{6,10},{8,12},{10,14},{12,16},{14,18},{16,20},{1... | collective-permute-start | bytes 1572872 | tf_op jit(solution)/shard_map/ppermute | solution.py:402
  74.9 17.7 %collective-permute-start.8 = (bf16[32,4,16,128]{3,2,1,0:T(8,128)(2,1)S(1)}, bf16[32,4,16,128]{3,2,1,0:T(8,128)(2,1)S(1)}, u32[]{:S(2)}, u32[]{:S(2)}) collective-permute-start(bf16[32,4,16,128]{3,2,1,0:T(8,128)(2,1)S(1)} %constant_dynamic-update-slice_fusion.refs_0_), channel_id=1, source_target_pairs={{0,2},{2,8},{4,6},{6,12},{8,10},{10,16},{12,14},{14,20},{16,18},{1... | collective-permute-start | bytes 1572872 | tf_op jit(solution)/shard_map/ppermute | solution.py:407
  92.6 6.7 %collective-permute-start.16 = (bf16[32,4,16,128]{3,2,1,0:T(8,128)(2,1)S(1)}, bf16[32,4,16,128]{3,2,1,0:T(8,128)(2,1)S(1)}, u32[]{:S(2)}, u32[]{:S(2)}) collective-permute-start(bf16[32,4,16,128]{3,2,1,0:T(8,128)(2,1)S(1)} %collective-permute-done.7.refs_2_), channel_id=1, source_target_pairs={{0,2},{2,0},{4,6},{6,4},{8,10},{10,8},{12,14},{14,12},{16,18},{18,... | collective-permute-start | bytes 1572872 | tf_op jit(solution)/shard_map/ppermute | solution.py:422

commit v19 on v18

--- a/solution.py
+++ b/solution.py
@@ -461,11 +461,12 @@
     pair_g, relay_g = exchanged(two_g), relayed(two_g)
     sums = correlated([got_a, pair_g, two_g, (rest_g, relay_g)], first, sums, False)
     piece_c = jnp.concatenate([own_c, got_c], axis=1)
-    two_c, rest_c = farther(piece_c)
+    two_c, rest_c = evenly(piece_c)
     pair_b = exchanged(two_b)
     sums = correlated([piece_b, pair_b, two_b, rest_b], first, sums, False)
-    pair_c = exchanged(after(two_c, rest_c, sums))
-    return correlated([piece_c, pair_c, two_c, rest_c], [(few, [(0, 0, 0), (0, 0, few)])], sums, True)
+    two_c = after(two_c, rest_c, sums)
+    pair_c, relay_c = exchanged(two_c), relayed(two_c)
+    return correlated([piece_c, pair_c, two_c, (rest_c, relay_c)], [(few, [(0, 0, 0), (0, 0, few)])], sums, True)
 
 
 def general(volts, fir_taps, place, correlated):

time: 105 us -> 109 us (1.038)
  the two profiles are of different devices: /device:TPU:7 before, /device:TPU:1 now
where the time goes in v19:
time: 109 us; the launch traced here: 108 us
  Pallas kernels  49.1 us (45%)
  starting transfers between devices  32.4 us (30%)
  waiting for transfers between devices  25.1 us (23%)
    pallas_call x3, Pallas kernels, spectra(): pl.pallas_call(functools.partial(spectra_kernel, groups, tuple((part[1:]...  30.1 us
    pallas_call x4, Pallas kernels, correlate(): pl.pallas_call(functools.partial(correlate_kernel, pieces, per_group, sca...  15.7 us
    ppermute x2, waiting for transfers between devices, relayed(): lax.ppermute(two, 'stn', [(i, i + 1) for i in range(lax.axis_size('stn'))...  12.5 us
    ppermute x1, waiting for transfers between devices, paired(): got_b = lax.ppermute(away_b, 'tm', [(0, 1)])  7.97 us
    ppermute x2, starting transfers between devices, relayed(): lax.ppermute(two, 'stn', [(i, i + 1) for i in range(lax.axis_size('stn'))...  6.71 us
    ppermute x2, starting transfers between devices, evenly(): return (shifted(block, 'stn', 2), lax.ppermute(block, 'stn', ways))  6.32 us
    ppermute x4, starting transfers between devices, exchanged(): lax.ppermute(block, 'stn', [(i, i ^ 1) for i in range(lax.axis_size('stn'...  5.13 us
    ppermute x2, starting transfers between devices, farther(): lax.ppermute(block, 'stn', [(i, (i + 1 if i % 2 == 0 else i + 3) % size)...  4.64 us
  transfers between devices with their start and end apart: 18, of which 5 were waited for; matrix products, arithmetic and copies ran while one was open for 0% of the time, Pallas kernels for 38%

profile of v19, /device:TPU:1, one launch (start us, length us, event | category | flops | bytes accessed | tf_op | source)
XLA Modules:
  0.0 107.7 jit_solution(3532463087943221686)
XLA Ops:
  0.0 0.1 pad_add_fusion.place
  0.1 3.3 %shard_map.46 = (bf16[8,32,64,128]{3,2,1,0:T(8,128)(2,1)S(1)}, bf16[8,8,64,128]{3,2,1,0:T(8,128)(2,1)S(1)}, f32[1024,128]{1,0:T(8,128)S(1)}, bf16[64,192]{1,0:T(...) custom-call(s32[2]{0:T(128)S(1)} %pad_add_fusion.place, bf16[8,32,64,128]{3,2,1,0:T(8,128)(2,1)} %bitcast.10, ...), custom_call_target="tpu_custom_call" | custom-call | tf_op jit(solution)/shard_map/pallas_call | solution.py:110
  3.4 2.1 %collective-permute-start.2 = (bf16[8,8,64,128]{3,2,1,0:T(8,128)(2,1)S(1)}, bf16[8,8,64,128]{3,2,1,0:T(8,128)(2,1)S(1)}, u32[]{:S(2)}, u32[]{:S(2)}) collective-permute-start(bf16[8,8,64,128]{3,2,1,0:T(8,128)(2,1)S(1)} %get-tuple-element.38), channel_id=1, source_target_pairs={{0,1},{1,0},{2,3},{3,2},{4,5},{5,4},{6,7},{7,6},{8,9},{9,8},{10,11... | collective-permute-start | bytes 3145736 | tf_op jit(solution)/shard_map/ppermute | solution.py:434
  5.5 11.3 %shard_map.47 = (bf16[32,4,16,128]{3,2,1,0:T(8,128)(2,1)S(1)}, bf16[32,4,16,128]{3,2,1,0:T(8,128)(2,1)S(1)}) custom-call(s32[2]{0:T(128)S(1)} %pad_add_fusion.place, bf16[8,32,64,128]{3,2,1,0:T(8,128)(2,1)S(1)} %get-tuple-element.28.refs_0_.refs_1_, bf16[8,32,64,128]{3,2,1,0:T(8,128)(2,1)S(1)} %get-tuple-element.28.refs_0_.refs_1_, ...), custom_call_target="tpu_custom_call" | custom-call | flops 1000000 | tf_op jit(solution)/shard_map/pallas_call | solution.py:263
  16.8 1.3 %collective-permute-start.1 = (bf16[32,4,16,128]{3,2,1,0:T(8,128)(2,1)S(1)}, bf16[32,4,16,128]{3,2,1,0:T(8,128)(2,1)S(1)}, u32[]{:S(2)}, u32[]{:S(2)}) collective-permute-start(bf16[32,4,16,128]{3,2,1,0:T(8,128)(2,1)S(1)} %get-tuple-element.34.refs_0_), channel_id=1, source_target_pairs={{0,4},{2,6},{4,8},{6,10},{8,12},{10,14},{12,16},{14,18},{16,20},{1... | collective-permute-start | bytes 1572872 | tf_op jit(solution)/shard_map/ppermute | solution.py:402
  18.1 0.3 collective-permute-start
  18.4 2.7 %collective-permute-start.5 = (bf16[32,4,16,128]{3,2,1,0:T(8,128)(2,1)S(1)}, bf16[32,4,16,128]{3,2,1,0:T(8,128)(2,1)S(1)}, u32[]{:S(2)}, u32[]{:S(2)}) collective-permute-start(bf16[32,4,16,128]{3,2,1,0:T(8,128)(2,1)S(1)} %get-tuple-element.34.refs_0_), channel_id=1, source_target_pairs={{0,2},{2,8},{4,6},{6,12},{8,10},{10,16},{12,14},{14,20},{16,18},{1... | collective-permute-start | bytes 1572872 | tf_op jit(solution)/shard_map/ppermute | solution.py:407
  21.1 12.0 %shard_map.48 = (bf16[32,4,16,128]{3,2,1,0:T(8,128)(2,1)S(1)}, bf16[32,4,16,128]{3,2,1,0:T(8,128)(2,1)}) custom-call(s32[2]{0:T(128)S(1)} %pad_add_fusion.place, bf16[8,32,64,128]{3,2,1,0:T(8,128)(2,1)S(1)} %get-tuple-element.28.refs_0_.refs_1_, bf16[8,32,64,128]{3,2,1,0:T(8,128)(2,1)S(1)} %get-tuple-element.28.refs_0_.refs_1_, ...), custom_call_target="tpu_custom_call" | custom-call | flops 1000000 | tf_op jit(solution)/shard_map/pallas_call | solution.py:263
  33.1 0.0 collective-permute-done.1.refs_2_
  33.1 0.0 collective-permute-done.2.refs_2_
  33.1 6.7 %shard_map.49 = (bf16[32,2,16,128]{3,2,1,0:T(8,128)(2,1)S(1)}, bf16[32,2,16,128]{3,2,1,0:T(8,128)(2,1)S(1)}) custom-call(s32[2]{0:T(128)S(1)} %pad_add_fusion.place, bf16[8,32,64,128]{3,2,1,0:T(8,128)(2,1)S(1)} %get-tuple-element.28.refs_0_.refs_1_, bf16[8,32,64,128]{3,2,1,0:T(8,128)(2,1)S(1)} %get-tuple-element.28.refs_0_.refs_1_, ...), custom_call_target="tpu_custom_call" | custom-call | flops 1000000 | tf_op jit(solution)/shard_map/pallas_call | solution.py:263
  39.9 0.0 copy-start
  39.9 0.7 copy-done
  40.6 0.0 collective-permute-done.refs_0_
  40.6 2.3 %collective-permute-start.4 = (bf16[32,4,16,128]{3,2,1,0:T(8,128)(2,1)S(1)}, bf16[32,4,16,128]{3,2,1,0:T(8,128)(2,1)S(1)}, u32[]{:S(2)}, u32[]{:S(2)}) collective-permute-start(bf16[32,4,16,128]{3,2,1,0:T(8,128)(2,1)S(1)} %collective-permute-done.1.refs_2_), channel_id=1, source_target_pairs={{0,2},{2,0},{4,6},{6,4},{8,10},{10,8},{12,14},{14,12},{16,18},{18,... | collective-permute-start | bytes 1572872 | tf_op jit(solution)/shard_map/ppermute | solution.py:422
  42.8 2.7 %collective-permute-start.3 = (bf16[32,4,16,128]{3,2,1,0:T(8,128)(2,1)}, bf16[32,4,16,128]{3,2,1,0:T(8,128)(2,1)}, u32[]{:S(2)}, u32[]{:S(2)}) collective-permute-start(bf16[32,4,16,128]{3,2,1,0:T(8,128)(2,1)} %get-tuple-element.43), channel_id=1, source_target_pairs={{0,1},{2,3},{4,5},{6,7},{8,9},{10,11},{12,13},{14,15},{16,17},{18,... | collective-permute-start | bytes 1572872 | tf_op jit(solution)/shard_map/ppermute | solution.py:453
  45.6 0.7 collective-permute-start.12
  46.2 0.0 copy-start.1
  46.2 0.0 collective-permute-done.5.refs_3_
  46.2 0.0 collective-permute-done.4.refs_1_
  46.2 2.2 %shard_map.50.refs_5_ = f32[4096,128]{1,0:T(8,128)S(1)} custom-call(s32[2]{0:T(128)S(1)} %pad_add_fusion.place, bf16[32,4,16,128]{3,2,1,0:T(8,128)(2,1)S(1)} %get-tuple-element.34.refs_0_, bf16[32,4,16,128]{3,2,1,0:T(8,128)(2,1)S(1)} %collective-permute-done.4.refs_1_, bf16[32,4,16,128]{3,2,1,0:T(8,128)(2,1)S(1)} %collective-permute-done.1.refs_2_, ...), custom_call_target="tpu_custom_call" | custom-call | flops 1000 | tf_op jit(solution)/shard_map/pallas_call | solution.py:373
  48.5 8.0 %collective-permute-done.3 = bf16[32,4,16,128]{3,2,1,0:T(8,128)(2,1)} collective-permute-done((bf16[32,4,16,128]{3,2,1,0:T(8,128)(2,1)}, bf16[32,4,16,128]{3,2,1,0:T(8,128)(2,1)}, u32[]{:S(2)}, u32[]{:S(2)}) %collective-permute-start.3) | collective-permute-done | bytes 524320 | tf_op jit(solution)/shard_map/ppermute | solution.py:453
  56.4 0.1 broadcast_select_fusion.refs_0_
  56.5 0.7 collective-permute-start.9
  57.2 4.1 %collective-permute-start.14 = (bf16[32,4,16,128]{3,2,1,0:T(8,128)(2,1)S(1)}, bf16[32,4,16,128]{3,2,1,0:T(8,128)(2,1)S(1)}, u32[]{:S(2)}, u32[]{:S(2)}) collective-permute-start(bf16[32,4,16,128]{3,2,1,0:T(8,128)(2,1)S(1)} %collective-permute-done.refs_0_), channel_id=1, source_target_pairs={{0,2},{2,8},{4,6},{8,10},{10,16},{12,14},{16,18},{18,24},{20,22},{... | collective-permute-start | bytes 1572872 | tf_op jit(solution)/shard_map/ppermute | solution.py:414
  61.3 0.3 collective-permute-done.12.refs_2_
  61.6 1.3 %collective-permute-start.13 = (bf16[32,4,16,128]{3,2,1,0:T(8,128)(2,1)}, bf16[32,4,16,128]{3,2,1,0:T(8,128)(2,1)S(1)}, u32[]{:S(2)}, u32[]{:S(2)}) collective-permute-start(bf16[32,4,16,128]{3,2,1,0:T(8,128)(2,1)} %collective-permute-done.12.refs_2_), channel_id=1, source_target_pairs={{0,2},{2,0},{4,6},{6,4},{8,10},{10,8},{12,14},{14,12},{16,18},{18,... | collective-permute-start | bytes 1572872 | tf_op jit(solution)/shard_map/ppermute | solution.py:422
  62.9 0.0 copy-done.1
  62.9 1.8 %collective-permute-start.6 = (bf16[32,2,16,128]{3,2,1,0:T(8,128)(2,1)S(1)}, bf16[32,2,16,128]{3,2,1,0:T(8,128)(2,1)S(1)}, u32[]{:S(2)}, u32[]{:S(2)}) collective-permute-start(bf16[32,2,16,128]{3,2,1,0:T(8,128)(2,1)S(1)} %copy-done.1), channel_id=1, source_target_pairs={{0,1},{1,0},{2,3},{3,2},{4,5},{5,4},{6,7},{7,6},{8,9},{9,8},{10,11... | collective-permute-start | bytes 786440 | tf_op jit(solution)/shard_map/ppermute | solution.py:458
  64.8 1.9 %collective-permute-start.11 = (bf16[32,4,16,128]{3,2,1,0:T(8,128)(2,1)S(1)}, bf16[32,4,16,128]{3,2,1,0:T(8,128)(2,1)S(1)}, u32[]{:S(2)}, u32[]{:S(2)}) collective-permute-start(bf16[32,4,16,128]{3,2,1,0:T(8,128)(2,1)S(1)} %broadcast_select_fusion.refs_0_), channel_id=1, source_target_pairs={{0,2},{2,8},{4,6},{6,12},{8,10},{10,16},{12,14},{14,20},{16,18},{1... | collective-permute-start | bytes 1572872 | tf_op jit(solution)/shard_map/ppermute | solution.py:407
  66.7 4.4 %collective-permute-done.6 = bf16[32,2,16,128]{3,2,1,0:T(8,128)(2,1)S(1)} collective-permute-done((bf16[32,2,16,128]{3,2,1,0:T(8,128)(2,1)S(1)}, bf16[32,2,16,128]{3,2,1,0:T(8,128)(2,1)S(1)}, u32[]{:S(2)}, u32[]{:S(2)}) %collective-permute-start.6) | collective-permute-done | bytes 262176 | tf_op jit(solution)/shard_map/ppermute | solution.py:458
  71.1 2.2 %collective-permute-start.15 = (bf16[32,4,16,128]{3,2,1,0:T(8,128)(2,1)}, bf16[32,4,16,128]{3,2,1,0:T(8,128)(2,1)S(1)}, u32[]{:S(2)}, u32[]{:S(2)}) collective-permute-start(bf16[32,4,16,128]{3,2,1,0:T(8,128)(2,1)} %collective-permute-done.12.refs_2_), channel_id=1, source_target_pairs={{2,4},{10,12},{18,20},{26,28},{3,5},{11,13},{19,21},{27,29}} | collective-permute-start | bytes 1572872 | tf_op jit(solution)/shard_map/ppermute | solution.py:418
  73.3 0.0 collective-permute-done.9.refs_2_
  73.4 1.5 %collective-permute-start.10 = (bf16[32,4,16,128]{3,2,1,0:T(8,128)(2,1)S(1)}, bf16[32,4,16,128]{3,2,1,0:T(8,128)(2,1)S(1)}, u32[]{:S(2)}, u32[]{:S(2)}) collective-permute-start(bf16[32,4,16,128]{3,2,1,0:T(8,128)(2,1)S(1)} %collective-permute-done.9.refs_2_), channel_id=1, source_target_pairs={{0,2},{2,0},{4,6},{6,4},{8,10},{10,8},{12,14},{14,12},{16,18},{18,... | collective-permute-start | bytes 1572872 | tf_op jit(solution)/shard_map/ppermute | solution.py:422
  74.8 0.0 collective-permute-done.14.refs_3_
  74.8 0.0 collective-permute-start.7
  74.9 0.0 collective-permute-done.13.refs_1_
  74.9 2.2 %collective-permute-start.8 = (bf16[32,4,16,128]{3,2,1,0:T(8,128)(2,1)S(1)}, bf16[32,4,16,128]{3,2,1,0:T(8,128)(2,1)S(1)}, u32[]{:S(2)}, u32[]{:S(2)}) collective-permute-start(bf16[32,4,16,128]{3,2,1,0:T(8,128)(2,1)S(1)} %constant_dynamic-update-slice_fusion.refs_0_), channel_id=1, source_target_pairs={{0,2},{2,8},{4,6},{8,10},{10,16},{12,14},{16,18},{18,24},{20,22},{... | collective-permute-start | bytes 1572872 | tf_op jit(solution)/shard_map/ppermute | solution.py:414
  77.0 6.6 %collective-permute-done.15.refs_4_ = bf16[32,4,16,128]{3,2,1,0:T(8,128)(2,1)S(1)} collective-permute-done((bf16[32,4,16,128]{3,2,1,0:T(8,128)(2,1)}, bf16[32,4,16,128]{3,2,1,0:T(8,128)(2,1)S(1)}, u32[]{:S(2)}, u32[]{:S(2)}) %collective-permute-start.15) | collective-permute-done | bytes 524320 | tf_op jit(solution)/shard_map/ppermute | solution.py:418
  83.7 4.7 %shard_map.51.refs_4_ = f32[4096,128]{1,0:T(8,128)S(1)} custom-call(s32[2]{0:T(128)S(1)} %pad_add_fusion.place, bf16[32,4,16,128]{3,2,1,0:T(8,128)(2,1)S(1)} %collective-permute-done.refs_0_, bf16[32,4,16,128]{3,2,1,0:T(8,128)(2,1)S(1)} %collective-permute-done.13.refs_1_, ...), custom_call_target="tpu_custom_call", output_to_operand_aliasing={{}: (6, {})} | custom-call | flops 1000 | tf_op jit(solution)/shard_map/pallas_call | solution.py:373
  88.3 0.0 collective-permute-done.11.refs_3_
  88.3 0.0 collective-permute-done.10.refs_1_
  88.4 3.6 %shard_map.52.refs_5_ = f32[4096,128]{1,0:T(8,128)S(1)} custom-call(s32[2]{0:T(128)S(1)} %pad_add_fusion.place, bf16[32,4,16,128]{3,2,1,0:T(8,128)(2,1)S(1)} %broadcast_select_fusion.refs_0_, bf16[32,4,16,128]{3,2,1,0:T(8,128)(2,1)S(1)} %collective-permute-done.10.refs_1_, ...), custom_call_target="tpu_custom_call", output_to_operand_aliasing={{}: (5, {})} | custom-call | flops 1000 | tf_op jit(solution)/shard_map/pallas_call | solution.py:373
  92.0 0.0 collective-permute-done.7.refs_2_
  92.0 0.0 collective-permute-done.8.refs_3_
  92.0 0.1 collective-permute-start.16
  92.1 4.5 %collective-permute-start.17 = (bf16[32,4,16,128]{3,2,1,0:T(8,128)(2,1)S(1)}, bf16[32,4,16,128]{3,2,1,0:T(8,128)(2,1)S(1)}, u32[]{:S(2)}, u32[]{:S(2)}) collective-permute-start(bf16[32,4,16,128]{3,2,1,0:T(8,128)(2,1)S(1)} %collective-permute-done.7.refs_2_), channel_id=1, source_target_pairs={{2,4},{10,12},{18,20},{26,28},{3,5},{11,13},{19,21},{27,29}} | collective-permute-start | bytes 1572872 | tf_op jit(solution)/shard_map/ppermute | solution.py:418
  96.6 0.0 collective-permute-done.16.refs_1_
  96.6 5.9 %collective-permute-done.17.refs_4_ = bf16[32,4,16,128]{3,2,1,0:T(8,128)(2,1)S(1)} collective-permute-done((bf16[32,4,16,128]{3,2,1,0:T(8,128)(2,1)S(1)}, bf16[32,4,16,128]{3,2,1,0:T(8,128)(2,1)S(1)}, u32[]{:S(2)}, u32[]{:S(2)}) %collective-permute-start.17) | collective-permute-done | bytes 524320 | tf_op jit(solution)/shard_map/ppermute | solution.py:418
  102.5 5.2 %shard_map.53 = f32[2,8,4,8,8,128]{5,4,3,2,1,0:T(8,128)} custom-call(s32[2]{0:T(128)S(1)} %pad_add_fusion.place, bf16[32,4,16,128]{3,2,1,0:T(8,128)(2,1)S(1)} %constant_dynamic-update-slice_fusion.refs_0_, bf16[32,4,16,128]{3,2,1,0:T(8,128)(2,1)S(1)} %collective-permute-done.16.refs_1_, bf16[32,4,16,128]{3,2,1,0:T(8,128)(2,1)S(1)} %collective-permute-done.7.refs_2_, ...), custom_call_target="tpu_custom_call" | custom-call | flops 1000 | tf_op jit(solution)/shard_map/pallas_call | solution.py:373
  (2 shorter events, 0.1 us)
Async XLA Ops:
  3.4 29.7 %collective-permute-start.2 = (bf16[8,8,64,128]{3,2,1,0:T(8,128)(2,1)S(1)}, bf16[8,8,64,128]{3,2,1,0:T(8,128)(2,1)S(1)}, u32[]{:S(2)}, u32[]{:S(2)}) collective-permute-start(bf16[8,8,64,128]{3,2,1,0:T(8,128)(2,1)S(1)} %get-tuple-element.38), channel_id=1, source_target_pairs={{0,1},{1,0},{2,3},{3,2},{4,5},{5,4},{6,7},{7,6},{8,9},{9,8},{10,11... | collective-permute-start | bytes 3145736 | tf_op jit(solution)/shard_map/ppermute | solution.py:434
  16.8 16.3 %collective-permute-start.1 = (bf16[32,4,16,128]{3,2,1,0:T(8,128)(2,1)S(1)}, bf16[32,4,16,128]{3,2,1,0:T(8,128)(2,1)S(1)}, u32[]{:S(2)}, u32[]{:S(2)}) collective-permute-start(bf16[32,4,16,128]{3,2,1,0:T(8,128)(2,1)S(1)} %get-tuple-element.34.refs_0_), channel_id=1, source_target_pairs={{0,4},{2,6},{4,8},{6,10},{8,12},{10,14},{12,16},{14,18},{16,20},{1... | collective-permute-start | bytes 1572872 | tf_op jit(solution)/shard_map/ppermute | solution.py:402
  18.1 22.4 %collective-permute-start = (bf16[32,4,16,128]{3,2,1,0:T(8,128)(2,1)S(1)}, bf16[32,4,16,128]{3,2,1,0:T(8,128)(2,1)S(1)}, u32[]{:S(2)}, u32[]{:S(2)}) collective-permute-start(bf16[32,4,16,128]{3,2,1,0:T(8,128)(2,1)S(1)} %get-tuple-element.33), channel_id=1, source_target_pairs={{0,1},{1,0},{2,3},{3,2},{4,5},{5,4},{6,7},{7,6},{8,9},{9,8},{10,11... | collective-permute-start | bytes 1572872 | tf_op jit(solution)/shard_map/ppermute | solution.py:438
  18.4 27.9 %collective-permute-start.5 = (bf16[32,4,16,128]{3,2,1,0:T(8,128)(2,1)S(1)}, bf16[32,4,16,128]{3,2,1,0:T(8,128)(2,1)S(1)}, u32[]{:S(2)}, u32[]{:S(2)}) collective-permute-start(bf16[32,4,16,128]{3,2,1,0:T(8,128)(2,1)S(1)} %get-tuple-element.34.refs_0_), channel_id=1, source_target_pairs={{0,2},{2,8},{4,6},{6,12},{8,10},{10,16},{12,14},{14,20},{16,18},{1... | collective-permute-start | bytes 1572872 | tf_op jit(solution)/shard_map/ppermute | solution.py:407
  39.9 0.7 copy-start
  40.6 5.7 %collective-permute-start.4 = (bf16[32,4,16,128]{3,2,1,0:T(8,128)(2,1)S(1)}, bf16[32,4,16,128]{3,2,1,0:T(8,128)(2,1)S(1)}, u32[]{:S(2)}, u32[]{:S(2)}) collective-permute-start(bf16[32,4,16,128]{3,2,1,0:T(8,128)(2,1)S(1)} %collective-permute-done.1.refs_2_), channel_id=1, source_target_pairs={{0,2},{2,0},{4,6},{6,4},{8,10},{10,8},{12,14},{14,12},{16,18},{18,... | collective-permute-start | bytes 1572872 | tf_op jit(solution)/shard_map/ppermute | solution.py:422
  42.8 13.6 %collective-permute-start.3 = (bf16[32,4,16,128]{3,2,1,0:T(8,128)(2,1)}, bf16[32,4,16,128]{3,2,1,0:T(8,128)(2,1)}, u32[]{:S(2)}, u32[]{:S(2)}) collective-permute-start(bf16[32,4,16,128]{3,2,1,0:T(8,128)(2,1)} %get-tuple-element.43), channel_id=1, source_target_pairs={{0,1},{2,3},{4,5},{6,7},{8,9},{10,11},{12,13},{14,15},{16,17},{18,... | collective-permute-start | bytes 1572872 | tf_op jit(solution)/shard_map/ppermute | solution.py:453
  45.6 16.0 %collective-permute-start.12 = (bf16[32,4,16,128]{3,2,1,0:T(8,128)(2,1)S(1)}, bf16[32,4,16,128]{3,2,1,0:T(8,128)(2,1)}, u32[]{:S(2)}, u32[]{:S(2)}) collective-permute-start(bf16[32,4,16,128]{3,2,1,0:T(8,128)(2,1)S(1)} %collective-permute-done.refs_0_), channel_id=1, source_target_pairs={{0,4},{2,6},{4,8},{6,10},{8,12},{10,14},{12,16},{14,18},{16,20},{1... | collective-permute-start | bytes 1572872 | tf_op jit(solution)/shard_map/ppermute | solution.py:402
  46.2 16.7 %copy-start.1 = (bf16[32,2,16,128]{3,2,1,0:T(8,128)(2,1)S(1)}, bf16[32,2,16,128]{3,2,1,0:T(8,128)(2,1)}, u32[]{:S(2)}) copy-start(bf16[32,2,16,128]{3,2,1,0:T(8,128)(2,1)} %copy-done) | copy-start | bytes 786436
  56.5 16.9 %collective-permute-start.9 = (bf16[32,4,16,128]{3,2,1,0:T(8,128)(2,1)S(1)}, bf16[32,4,16,128]{3,2,1,0:T(8,128)(2,1)S(1)}, u32[]{:S(2)}, u32[]{:S(2)}) collective-permute-start(bf16[32,4,16,128]{3,2,1,0:T(8,128)(2,1)S(1)} %broadcast_select_fusion.refs_0_), channel_id=1, source_target_pairs={{0,4},{2,6},{4,8},{6,10},{8,12},{10,14},{12,16},{14,18},{16,20},{1... | collective-permute-start | bytes 1572872 | tf_op jit(solution)/shard_map/ppermute | solution.py:402
  57.2 17.7 %collective-permute-start.14 = (bf16[32,4,16,128]{3,2,1,0:T(8,128)(2,1)S(1)}, bf16[32,4,16,128]{3,2,1,0:T(8,128)(2,1)S(1)}, u32[]{:S(2)}, u32[]{:S(2)}) collective-permute-start(bf16[32,4,16,128]{3,2,1,0:T(8,128)(2,1)S(1)} %collective-permute-done.refs_0_), channel_id=1, source_target_pairs={{0,2},{2,8},{4,6},{8,10},{10,16},{12,14},{16,18},{18,24},{20,22},{... | collective-permute-start | bytes 1572872 | tf_op jit(solution)/shard_map/ppermute | solution.py:414
  61.6 13.3 %collective-permute-start.13 = (bf16[32,4,16,128]{3,2,1,0:T(8,128)(2,1)}, bf16[32,4,16,128]{3,2,1,0:T(8,128)(2,1)S(1)}, u32[]{:S(2)}, u32[]{:S(2)}) collective-permute-start(bf16[32,4,16,128]{3,2,1,0:T(8,128)(2,1)} %collective-permute-done.12.refs_2_), channel_id=1, source_target_pairs={{0,2},{2,0},{4,6},{6,4},{8,10},{10,8},{12,14},{14,12},{16,18},{18,... | collective-permute-start | bytes 1572872 | tf_op jit(solution)/shard_map/ppermute | solution.py:422
  62.9 8.2 %collective-permute-start.6 = (bf16[32,2,16,128]{3,2,1,0:T(8,128)(2,1)S(1)}, bf16[32,2,16,128]{3,2,1,0:T(8,128)(2,1)S(1)}, u32[]{:S(2)}, u32[]{:S(2)}) collective-permute-start(bf16[32,2,16,128]{3,2,1,0:T(8,128)(2,1)S(1)} %copy-done.1), channel_id=1, source_target_pairs={{0,1},{1,0},{2,3},{3,2},{4,5},{5,4},{6,7},{7,6},{8,9},{9,8},{10,11... | collective-permute-start | bytes 786440 | tf_op jit(solution)/shard_map/ppermute | solution.py:458
  64.8 23.6 %collective-permute-start.11 = (bf16[32,4,16,128]{3,2,1,0:T(8,128)(2,1)S(1)}, bf16[32,4,16,128]{3,2,1,0:T(8,128)(2,1)S(1)}, u32[]{:S(2)}, u32[]{:S(2)}) collective-permute-start(bf16[32,4,16,128]{3,2,1,0:T(8,128)(2,1)S(1)} %broadcast_select_fusion.refs_0_), channel_id=1, source_target_pairs={{0,2},{2,8},{4,6},{6,12},{8,10},{10,16},{12,14},{14,20},{16,18},{1... | collective-permute-start | bytes 1572872 | tf_op jit(solution)/shard_map/ppermute | solution.py:407
  71.1 12.6 %collective-permute-start.15 = (bf16[32,4,16,128]{3,2,1,0:T(8,128)(2,1)}, bf16[32,4,16,128]{3,2,1,0:T(8,128)(2,1)S(1)}, u32[]{:S(2)}, u32[]{:S(2)}) collective-permute-start(bf16[32,4,16,128]{3,2,1,0:T(8,128)(2,1)} %collective-permute-done.12.refs_2_), channel_id=1, source_target_pairs={{2,4},{10,12},{18,20},{26,28},{3,5},{11,13},{19,21},{27,29}} | collective-permute-start | bytes 1572872 | tf_op jit(solution)/shard_map/ppermute | solution.py:418
  73.4 15.0 %collective-permute-start.10 = (bf16[32,4,16,128]{3,2,1,0:T(8,128)(2,1)S(1)}, bf16[32,4,16,128]{3,2,1,0:T(8,128)(2,1)S(1)}, u32[]{:S(2)}, u32[]{:S(2)}) collective-permute-start(bf16[32,4,16,128]{3,2,1,0:T(8,128)(2,1)S(1)} %collective-permute-done.9.refs_2_), channel_id=1, source_target_pairs={{0,2},{2,0},{4,6},{6,4},{8,10},{10,8},{12,14},{14,12},{16,18},{18,... | collective-permute-start | bytes 1572872 | tf_op jit(solution)/shard_map/ppermute | solution.py:422
  74.8 17.1 %collective-permute-start.7 = (bf16[32,4,16,128]{3,2,1,0:T(8,128)(2,1)S(1)}, bf16[32,4,16,128]{3,2,1,0:T(8,128)(2,1)S(1)}, u32[]{:S(2)}, u32[]{:S(2)}) collective-permute-start(bf16[32,4,16,128]{3,2,1,0:T(8,128)(2,1)S(1)} %constant_dynamic-update-slice_fusion.refs_0_), channel_id=1, source_target_pairs={{0,4},{2,6},{4,8},{6,10},{8,12},{10,14},{12,16},{14,18},{16,20},{1... | collective-permute-start | bytes 1572872 | tf_op jit(solution)/shard_map/ppermute | solution.py:402
  74.9 17.1 %collective-permute-start.8 = (bf16[32,4,16,128]{3,2,1,0:T(8,128)(2,1)S(1)}, bf16[32,4,16,128]{3,2,1,0:T(8,128)(2,1)S(1)}, u32[]{:S(2)}, u32[]{:S(2)}) collective-permute-start(bf16[32,4,16,128]{3,2,1,0:T(8,128)(2,1)S(1)} %constant_dynamic-update-slice_fusion.refs_0_), channel_id=1, source_target_pairs={{0,2},{2,8},{4,6},{8,10},{10,16},{12,14},{16,18},{18,24},{20,22},{... | collective-permute-start | bytes 1572872 | tf_op jit(solution)/shard_map/ppermute | solution.py:414
  92.0 4.6 %collective-permute-start.16 = (bf16[32,4,16,128]{3,2,1,0:T(8,128)(2,1)S(1)}, bf16[32,4,16,128]{3,2,1,0:T(8,128)(2,1)S(1)}, u32[]{:S(2)}, u32[]{:S(2)}) collective-permute-start(bf16[32,4,16,128]{3,2,1,0:T(8,128)(2,1)S(1)} %collective-permute-done.7.refs_2_), channel_id=1, source_target_pairs={{0,2},{2,0},{4,6},{6,4},{8,10},{10,8},{12,14},{14,12},{16,18},{18,... | collective-permute-start | bytes 1572872 | tf_op jit(solution)/shard_map/ppermute | solution.py:422
  92.1 10.4 %collective-permute-start.17 = (bf16[32,4,16,128]{3,2,1,0:T(8,128)(2,1)S(1)}, bf16[32,4,16,128]{3,2,1,0:T(8,128)(2,1)S(1)}, u32[]{:S(2)}, u32[]{:S(2)}) collective-permute-start(bf16[32,4,16,128]{3,2,1,0:T(8,128)(2,1)S(1)} %collective-permute-done.7.refs_2_), channel_id=1, source_target_pairs={{2,4},{10,12},{18,20},{26,28},{3,5},{11,13},{19,21},{27,29}} | collective-permute-start | bytes 1572872 | tf_op jit(solution)/shard_map/ppermute | solution.py:418

commit v20 on v18

--- a/solution.py
+++ b/solution.py
@@ -457,14 +457,14 @@
     got_b, away_c, sums = lax.optimization_barrier((got_b, away_c, sums))
     got_c = lax.ppermute(away_c, "tm", swap)
     piece_b = jnp.where(me == 0, own_b, got_b)
-    two_b, rest_b = farther(piece_b)
+    two_b, rest_b = evenly(piece_b)
     pair_g, relay_g = exchanged(two_g), relayed(two_g)
     sums = correlated([got_a, pair_g, two_g, (rest_g, relay_g)], first, sums, False)
     piece_c = jnp.concatenate([own_c, got_c], axis=1)
     two_c, rest_c = farther(piece_c)
-    pair_b = exchanged(two_b)
-    sums = correlated([piece_b, pair_b, two_b, rest_b], first, sums, False)
+    pair_b, relay_b = exchanged(two_b), relayed(two_b)
     pair_c = exchanged(after(two_c, rest_c, sums))
+    sums = correlated([piece_b, pair_b, two_b, (rest_b, relay_b)], first, sums, False, (), 6 * 10**9)
     return correlated([piece_c, pair_c, two_c, rest_c], [(few, [(0, 0, 0), (0, 0, few)])], sums, True)
 
 

time: 105 us -> 106 us (level)
  the two profiles are of different devices: /device:TPU:7 before, /device:TPU:1 now
where the time goes in v20:
time: 106 us
  Pallas kernels  49.1 us (46%)
  starting transfers between devices  28.4 us (27%)
  waiting for transfers between devices  27.3 us (26%)
    pallas_call x3, Pallas kernels, spectra(): pl.pallas_call(functools.partial(spectra_kernel, groups, tuple((part[1:]...  30.1 us
    pallas_call x4, Pallas kernels, correlate(): pl.pallas_call(functools.partial(correlate_kernel, pieces, per_group, sca...  15.7 us
    ppermute x4, waiting for transfers between devices, shifted(): lax.ppermute(block, axis, [(i, (i + distance) % size) for i in range(size)])  8.34 us
    ppermute x2, waiting for transfers between devices, relayed(): lax.ppermute(two, 'stn', [(i, i + 1) for i in range(lax.axis_size('stn'))...  7.51 us
    ppermute x1, waiting for transfers between devices, paired(): got_c = lax.ppermute(away_c, 'tm', swap)  7.23 us
    ppermute x2, starting transfers between devices, relayed(): lax.ppermute(two, 'stn', [(i, i + 1) for i in range(lax.axis_size('stn'))...  6.69 us
    ppermute x2, starting transfers between devices, evenly(): return (shifted(block, 'stn', 2), lax.ppermute(block, 'stn', ways))  5.69 us
    ppermute x4, starting transfers between devices, exchanged(): lax.ppermute(block, 'stn', [(i, i ^ 1) for i in range(lax.axis_size('stn'...  4.62 us
  transfers between devices with their start and end apart: 18, of which 6 were waited for; matrix products, arithmetic and copies ran while one was open for 0% of the time, Pallas kernels for 38%

profile of v20, /device:TPU:1, one launch (start us, length us, event | category | flops | bytes accessed | tf_op | source)
XLA Modules:
  0.0 105.9 jit_solution(17914774599054111198)
XLA Ops:
  0.0 0.1 pad_add_fusion.place
  0.1 3.3 %shard_map.46 = (bf16[8,32,64,128]{3,2,1,0:T(8,128)(2,1)S(1)}, bf16[8,8,64,128]{3,2,1,0:T(8,128)(2,1)S(1)}, f32[1024,128]{1,0:T(8,128)S(1)}, bf16[64,192]{1,0:T(...) custom-call(s32[2]{0:T(128)S(1)} %pad_add_fusion.place, bf16[8,32,64,128]{3,2,1,0:T(8,128)(2,1)} %bitcast.10, ...), custom_call_target="tpu_custom_call" | custom-call | tf_op jit(solution)/shard_map/pallas_call | solution.py:110
  3.4 2.1 %collective-permute-start.2 = (bf16[8,8,64,128]{3,2,1,0:T(8,128)(2,1)S(1)}, bf16[8,8,64,128]{3,2,1,0:T(8,128)(2,1)S(1)}, u32[]{:S(2)}, u32[]{:S(2)}) collective-permute-start(bf16[8,8,64,128]{3,2,1,0:T(8,128)(2,1)S(1)} %get-tuple-element.38), channel_id=1, source_target_pairs={{0,1},{1,0},{2,3},{3,2},{4,5},{5,4},{6,7},{7,6},{8,9},{9,8},{10,11... | collective-permute-start | bytes 3145736 | tf_op jit(solution)/shard_map/ppermute | solution.py:434
  5.5 11.3 %shard_map.47 = (bf16[32,4,16,128]{3,2,1,0:T(8,128)(2,1)S(1)}, bf16[32,4,16,128]{3,2,1,0:T(8,128)(2,1)S(1)}) custom-call(s32[2]{0:T(128)S(1)} %pad_add_fusion.place, bf16[8,32,64,128]{3,2,1,0:T(8,128)(2,1)S(1)} %get-tuple-element.28.refs_0_.refs_1_, bf16[8,32,64,128]{3,2,1,0:T(8,128)(2,1)S(1)} %get-tuple-element.28.refs_0_.refs_1_, ...), custom_call_target="tpu_custom_call" | custom-call | flops 1000000 | tf_op jit(solution)/shard_map/pallas_call | solution.py:263
  16.8 1.3 %collective-permute-start.1 = (bf16[32,4,16,128]{3,2,1,0:T(8,128)(2,1)S(1)}, bf16[32,4,16,128]{3,2,1,0:T(8,128)(2,1)S(1)}, u32[]{:S(2)}, u32[]{:S(2)}) collective-permute-start(bf16[32,4,16,128]{3,2,1,0:T(8,128)(2,1)S(1)} %get-tuple-element.34.refs_0_), channel_id=1, source_target_pairs={{0,4},{2,6},{4,8},{6,10},{8,12},{10,14},{12,16},{14,18},{16,20},{1... | collective-permute-start | bytes 1572872 | tf_op jit(solution)/shard_map/ppermute | solution.py:402
  18.1 0.3 collective-permute-start
  18.4 2.7 %collective-permute-start.5 = (bf16[32,4,16,128]{3,2,1,0:T(8,128)(2,1)S(1)}, bf16[32,4,16,128]{3,2,1,0:T(8,128)(2,1)S(1)}, u32[]{:S(2)}, u32[]{:S(2)}) collective-permute-start(bf16[32,4,16,128]{3,2,1,0:T(8,128)(2,1)S(1)} %get-tuple-element.34.refs_0_), channel_id=1, source_target_pairs={{0,2},{2,8},{4,6},{6,12},{8,10},{10,16},{12,14},{14,20},{16,18},{1... | collective-permute-start | bytes 1572872 | tf_op jit(solution)/shard_map/ppermute | solution.py:407
  21.1 12.0 %shard_map.48 = (bf16[32,4,16,128]{3,2,1,0:T(8,128)(2,1)S(1)}, bf16[32,4,16,128]{3,2,1,0:T(8,128)(2,1)}) custom-call(s32[2]{0:T(128)S(1)} %pad_add_fusion.place, bf16[8,32,64,128]{3,2,1,0:T(8,128)(2,1)S(1)} %get-tuple-element.28.refs_0_.refs_1_, bf16[8,32,64,128]{3,2,1,0:T(8,128)(2,1)S(1)} %get-tuple-element.28.refs_0_.refs_1_, ...), custom_call_target="tpu_custom_call" | custom-call | flops 1000000 | tf_op jit(solution)/shard_map/pallas_call | solution.py:263
  33.1 0.0 collective-permute-done.1.refs_2_
  33.1 0.0 collective-permute-done.2.refs_2_
  33.1 6.7 %shard_map.49 = (bf16[32,2,16,128]{3,2,1,0:T(8,128)(2,1)S(1)}, bf16[32,2,16,128]{3,2,1,0:T(8,128)(2,1)S(1)}) custom-call(s32[2]{0:T(128)S(1)} %pad_add_fusion.place, bf16[8,32,64,128]{3,2,1,0:T(8,128)(2,1)S(1)} %get-tuple-element.28.refs_0_.refs_1_, bf16[8,32,64,128]{3,2,1,0:T(8,128)(2,1)S(1)} %get-tuple-element.28.refs_0_.refs_1_, ...), custom_call_target="tpu_custom_call" | custom-call | flops 1000000 | tf_op jit(solution)/shard_map/pallas_call | solution.py:263
  39.9 0.0 copy-start
  39.9 0.7 copy-done
  40.6 0.0 collective-permute-done.refs_0_
  40.6 2.3 %collective-permute-start.4 = (bf16[32,4,16,128]{3,2,1,0:T(8,128)(2,1)S(1)}, bf16[32,4,16,128]{3,2,1,0:T(8,128)(2,1)S(1)}, u32[]{:S(2)}, u32[]{:S(2)}) collective-permute-start(bf16[32,4,16,128]{3,2,1,0:T(8,128)(2,1)S(1)} %collective-permute-done.1.refs_2_), channel_id=1, source_target_pairs={{0,2},{2,0},{4,6},{6,4},{8,10},{10,8},{12,14},{14,12},{16,18},{18,... | collective-permute-start | bytes 1572872 | tf_op jit(solution)/shard_map/ppermute | solution.py:422
  42.8 2.7 %collective-permute-start.3 = (bf16[32,4,16,128]{3,2,1,0:T(8,128)(2,1)}, bf16[32,4,16,128]{3,2,1,0:T(8,128)(2,1)}, u32[]{:S(2)}, u32[]{:S(2)}) collective-permute-start(bf16[32,4,16,128]{3,2,1,0:T(8,128)(2,1)} %get-tuple-element.43), channel_id=1, source_target_pairs={{0,1},{2,3},{4,5},{6,7},{8,9},{10,11},{12,13},{14,15},{16,17},{18,... | collective-permute-start | bytes 1572872 | tf_op jit(solution)/shard_map/ppermute | solution.py:453
  45.6 0.7 collective-permute-start.9
  46.2 0.0 copy-start.1
  46.2 3.8 %collective-permute-start.11 = (bf16[32,4,16,128]{3,2,1,0:T(8,128)(2,1)S(1)}, bf16[32,4,16,128]{3,2,1,0:T(8,128)(2,1)S(1)}, u32[]{:S(2)}, u32[]{:S(2)}) collective-permute-start(bf16[32,4,16,128]{3,2,1,0:T(8,128)(2,1)S(1)} %collective-permute-done.refs_0_), channel_id=1, source_target_pairs={{0,2},{2,8},{4,6},{8,10},{10,16},{12,14},{16,18},{18,24},{20,22},{... | collective-permute-start | bytes 1572872 | tf_op jit(solution)/shard_map/ppermute | solution.py:414
  50.0 0.0 collective-permute-done.5.refs_3_
  50.0 0.0 collective-permute-done.4.refs_1_
  50.0 2.2 %shard_map.50.refs_5_ = f32[4096,128]{1,0:T(8,128)S(1)} custom-call(s32[2]{0:T(128)S(1)} %pad_add_fusion.place, bf16[32,4,16,128]{3,2,1,0:T(8,128)(2,1)S(1)} %get-tuple-element.34.refs_0_, bf16[32,4,16,128]{3,2,1,0:T(8,128)(2,1)S(1)} %collective-permute-done.4.refs_1_, bf16[32,4,16,128]{3,2,1,0:T(8,128)(2,1)S(1)} %collective-permute-done.1.refs_2_, ...), custom_call_target="tpu_custom_call" | custom-call | flops 1000 | tf_op jit(solution)/shard_map/pallas_call | solution.py:373
  52.2 4.2 %collective-permute-done.3 = bf16[32,4,16,128]{3,2,1,0:T(8,128)(2,1)} collective-permute-done((bf16[32,4,16,128]{3,2,1,0:T(8,128)(2,1)}, bf16[32,4,16,128]{3,2,1,0:T(8,128)(2,1)}, u32[]{:S(2)}, u32[]{:S(2)}) %collective-permute-start.3) | collective-permute-done | bytes 524320 | tf_op jit(solution)/shard_map/ppermute | solution.py:453
  56.4 5.2 %collective-permute-done.9.refs_2_ = bf16[32,4,16,128]{3,2,1,0:T(8,128)(2,1)} collective-permute-done((bf16[32,4,16,128]{3,2,1,0:T(8,128)(2,1)S(1)}, bf16[32,4,16,128]{3,2,1,0:T(8,128)(2,1)}, u32[]{:S(2)}, u32[]{:S(2)}) %collective-permute-start.9) | collective-permute-done | bytes 524320 | tf_op jit(solution)/shard_map/ppermute | solution.py:402
  61.6 1.1 %collective-permute-start.10 = (bf16[32,4,16,128]{3,2,1,0:T(8,128)(2,1)}, bf16[32,4,16,128]{3,2,1,0:T(8,128)(2,1)S(1)}, u32[]{:S(2)}, u32[]{:S(2)}) collective-permute-start(bf16[32,4,16,128]{3,2,1,0:T(8,128)(2,1)} %collective-permute-done.9.refs_2_), channel_id=1, source_target_pairs={{0,2},{2,0},{4,6},{6,4},{8,10},{10,8},{12,14},{14,12},{16,18},{18,... | collective-permute-start | bytes 1572872 | tf_op jit(solution)/shard_map/ppermute | solution.py:422
  62.7 0.1 broadcast_select_fusion.refs_0_
  62.8 0.1 collective-permute-start.14
  62.8 2.2 %collective-permute-start.12 = (bf16[32,4,16,128]{3,2,1,0:T(8,128)(2,1)}, bf16[32,4,16,128]{3,2,1,0:T(8,128)(2,1)S(1)}, u32[]{:S(2)}, u32[]{:S(2)}) collective-permute-start(bf16[32,4,16,128]{3,2,1,0:T(8,128)(2,1)} %collective-permute-done.9.refs_2_), channel_id=1, source_target_pairs={{2,4},{10,12},{18,20},{26,28},{3,5},{11,13},{19,21},{27,29}} | collective-permute-start | bytes 1572872 | tf_op jit(solution)/shard_map/ppermute | solution.py:418
  65.1 0.0 copy-done.1
  65.1 0.1 collective-permute-start.6
  65.2 7.2 %collective-permute-done.6 = bf16[32,2,16,128]{3,2,1,0:T(8,128)(2,1)S(1)} collective-permute-done((bf16[32,2,16,128]{3,2,1,0:T(8,128)(2,1)S(1)}, bf16[32,2,16,128]{3,2,1,0:T(8,128)(2,1)S(1)}, u32[]{:S(2)}, u32[]{:S(2)}) %collective-permute-start.6) | collective-permute-done | bytes 262176 | tf_op jit(solution)/shard_map/ppermute | solution.py:458
  72.4 0.1 collective-permute-start.7
  72.5 0.0 collective-permute-done.11.refs_3_
  72.5 1.5 %collective-permute-start.8 = (bf16[32,4,16,128]{3,2,1,0:T(8,128)(2,1)S(1)}, bf16[32,4,16,128]{3,2,1,0:T(8,128)(2,1)S(1)}, u32[]{:S(2)}, u32[]{:S(2)}) collective-permute-start(bf16[32,4,16,128]{3,2,1,0:T(8,128)(2,1)S(1)} %constant_dynamic-update-slice_fusion.refs_0_), channel_id=1, source_target_pairs={{0,2},{2,8},{4,6},{6,12},{8,10},{10,16},{12,14},{14,20},{16,18},{1... | collective-permute-start | bytes 1572872 | tf_op jit(solution)/shard_map/ppermute | solution.py:407
  74.0 0.0 collective-permute-done.10.refs_1_
  74.0 1.9 %collective-permute-start.16 = (bf16[32,4,16,128]{3,2,1,0:T(8,128)(2,1)S(1)}, bf16[32,4,16,128]{3,2,1,0:T(8,128)(2,1)S(1)}, u32[]{:S(2)}, u32[]{:S(2)}) collective-permute-start(bf16[32,4,16,128]{3,2,1,0:T(8,128)(2,1)S(1)} %broadcast_select_fusion.refs_0_), channel_id=1, source_target_pairs={{0,2},{2,8},{4,6},{8,10},{10,16},{12,14},{16,18},{18,24},{20,22},{... | collective-permute-start | bytes 1572872 | tf_op jit(solution)/shard_map/ppermute | solution.py:414
  75.9 3.2 %collective-permute-done.14.refs_2_ = bf16[32,4,16,128]{3,2,1,0:T(8,128)(2,1)S(1)} collective-permute-done((bf16[32,4,16,128]{3,2,1,0:T(8,128)(2,1)S(1)}, bf16[32,4,16,128]{3,2,1,0:T(8,128)(2,1)S(1)}, u32[]{:S(2)}, u32[]{:S(2)}) %collective-permute-start.14) | collective-permute-done | bytes 524320 | tf_op jit(solution)/shard_map/ppermute | solution.py:402
  79.1 1.2 %collective-permute-start.15 = (bf16[32,4,16,128]{3,2,1,0:T(8,128)(2,1)S(1)}, bf16[32,4,16,128]{3,2,1,0:T(8,128)(2,1)S(1)}, u32[]{:S(2)}, u32[]{:S(2)}) collective-permute-start(bf16[32,4,16,128]{3,2,1,0:T(8,128)(2,1)S(1)} %collective-permute-done.14.refs_2_), channel_id=1, source_target_pairs={{0,2},{2,0},{4,6},{6,4},{8,10},{10,8},{12,14},{14,12},{16,18},{18,... | collective-permute-start | bytes 1572872 | tf_op jit(solution)/shard_map/ppermute | solution.py:422
  80.2 5.5 %collective-permute-done.12.refs_4_ = bf16[32,4,16,128]{3,2,1,0:T(8,128)(2,1)S(1)} collective-permute-done((bf16[32,4,16,128]{3,2,1,0:T(8,128)(2,1)}, bf16[32,4,16,128]{3,2,1,0:T(8,128)(2,1)S(1)}, u32[]{:S(2)}, u32[]{:S(2)}) %collective-permute-start.12) | collective-permute-done | bytes 524320 | tf_op jit(solution)/shard_map/ppermute | solution.py:418
  85.7 4.5 %collective-permute-start.17 = (bf16[32,4,16,128]{3,2,1,0:T(8,128)(2,1)S(1)}, bf16[32,4,16,128]{3,2,1,0:T(8,128)(2,1)S(1)}, u32[]{:S(2)}, u32[]{:S(2)}) collective-permute-start(bf16[32,4,16,128]{3,2,1,0:T(8,128)(2,1)S(1)} %collective-permute-done.14.refs_2_), channel_id=1, source_target_pairs={{2,4},{10,12},{18,20},{26,28},{3,5},{11,13},{19,21},{27,29}} | collective-permute-start | bytes 1572872 | tf_op jit(solution)/shard_map/ppermute | solution.py:418
  90.2 4.7 %shard_map.51.refs_5_ = f32[4096,128]{1,0:T(8,128)S(1)} custom-call(s32[2]{0:T(128)S(1)} %pad_add_fusion.place, bf16[32,4,16,128]{3,2,1,0:T(8,128)(2,1)S(1)} %collective-permute-done.refs_0_, bf16[32,4,16,128]{3,2,1,0:T(8,128)(2,1)S(1)} %collective-permute-done.10.refs_1_, ...), custom_call_target="tpu_custom_call", output_to_operand_aliasing={{}: (6, {})} | custom-call | flops 1000 | tf_op jit(solution)/shard_map/pallas_call | solution.py:373
  94.9 0.0 collective-permute-done.7.refs_2_
  94.9 0.0 collective-permute-done.8.refs_3_
  94.9 0.1 collective-permute-start.13
  95.0 0.0 collective-permute-done.16.refs_3_
  95.0 0.0 collective-permute-done.15.refs_1_
  95.0 2.0 %collective-permute-done.17.refs_4_ = bf16[32,4,16,128]{3,2,1,0:T(8,128)(2,1)S(1)} collective-permute-done((bf16[32,4,16,128]{3,2,1,0:T(8,128)(2,1)S(1)}, bf16[32,4,16,128]{3,2,1,0:T(8,128)(2,1)S(1)}, u32[]{:S(2)}, u32[]{:S(2)}) %collective-permute-start.17) | collective-permute-done | bytes 524320 | tf_op jit(solution)/shard_map/ppermute | solution.py:418
  97.0 3.6 %shard_map.52.refs_4_ = f32[4096,128]{1,0:T(8,128)S(1)} custom-call(s32[2]{0:T(128)S(1)} %pad_add_fusion.place, bf16[32,4,16,128]{3,2,1,0:T(8,128)(2,1)S(1)} %broadcast_select_fusion.refs_0_, bf16[32,4,16,128]{3,2,1,0:T(8,128)(2,1)S(1)} %collective-permute-done.15.refs_1_, ...), custom_call_target="tpu_custom_call", output_to_operand_aliasing={{}: (6, {})} | custom-call | flops 6000000000 | tf_op jit(solution)/shard_map/pallas_call | solution.py:373
  100.7 0.0 collective-permute-done.13.refs_1_
  100.7 5.2 %shard_map.53 = f32[2,8,4,8,8,128]{5,4,3,2,1,0:T(8,128)} custom-call(s32[2]{0:T(128)S(1)} %pad_add_fusion.place, bf16[32,4,16,128]{3,2,1,0:T(8,128)(2,1)S(1)} %constant_dynamic-update-slice_fusion.refs_0_, bf16[32,4,16,128]{3,2,1,0:T(8,128)(2,1)S(1)} %collective-permute-done.13.refs_1_, bf16[32,4,16,128]{3,2,1,0:T(8,128)(2,1)S(1)} %collective-permute-done.7.refs_2_, ...), custom_call_target="tpu_custom_call" | custom-call | flops 1000 | tf_op jit(solution)/shard_map/pallas_call | solution.py:373
  (2 shorter events, 0.1 us)
Async XLA Ops:
  3.4 29.7 %collective-permute-start.2 = (bf16[8,8,64,128]{3,2,1,0:T(8,128)(2,1)S(1)}, bf16[8,8,64,128]{3,2,1,0:T(8,128)(2,1)S(1)}, u32[]{:S(2)}, u32[]{:S(2)}) collective-permute-start(bf16[8,8,64,128]{3,2,1,0:T(8,128)(2,1)S(1)} %get-tuple-element.38), channel_id=1, source_target_pairs={{0,1},{1,0},{2,3},{3,2},{4,5},{5,4},{6,7},{7,6},{8,9},{9,8},{10,11... | collective-permute-start | bytes 3145736 | tf_op jit(solution)/shard_map/ppermute | solution.py:434
  16.8 16.3 %collective-permute-start.1 = (bf16[32,4,16,128]{3,2,1,0:T(8,128)(2,1)S(1)}, bf16[32,4,16,128]{3,2,1,0:T(8,128)(2,1)S(1)}, u32[]{:S(2)}, u32[]{:S(2)}) collective-permute-start(bf16[32,4,16,128]{3,2,1,0:T(8,128)(2,1)S(1)} %get-tuple-element.34.refs_0_), channel_id=1, source_target_pairs={{0,4},{2,6},{4,8},{6,10},{8,12},{10,14},{12,16},{14,18},{16,20},{1... | collective-permute-start | bytes 1572872 | tf_op jit(solution)/shard_map/ppermute | solution.py:402
  18.1 22.4 %collective-permute-start = (bf16[32,4,16,128]{3,2,1,0:T(8,128)(2,1)S(1)}, bf16[32,4,16,128]{3,2,1,0:T(8,128)(2,1)S(1)}, u32[]{:S(2)}, u32[]{:S(2)}) collective-permute-start(bf16[32,4,16,128]{3,2,1,0:T(8,128)(2,1)S(1)} %get-tuple-element.33), channel_id=1, source_target_pairs={{0,1},{1,0},{2,3},{3,2},{4,5},{5,4},{6,7},{7,6},{8,9},{9,8},{10,11... | collective-permute-start | bytes 1572872 | tf_op jit(solution)/shard_map/ppermute | solution.py:438
  18.4 31.6 %collective-permute-start.5 = (bf16[32,4,16,128]{3,2,1,0:T(8,128)(2,1)S(1)}, bf16[32,4,16,128]{3,2,1,0:T(8,128)(2,1)S(1)}, u32[]{:S(2)}, u32[]{:S(2)}) collective-permute-start(bf16[32,4,16,128]{3,2,1,0:T(8,128)(2,1)S(1)} %get-tuple-element.34.refs_0_), channel_id=1, source_target_pairs={{0,2},{2,8},{4,6},{6,12},{8,10},{10,16},{12,14},{14,20},{16,18},{1... | collective-permute-start | bytes 1572872 | tf_op jit(solution)/shard_map/ppermute | solution.py:407
  39.9 0.7 copy-start
  40.6 9.5 %collective-permute-start.4 = (bf16[32,4,16,128]{3,2,1,0:T(8,128)(2,1)S(1)}, bf16[32,4,16,128]{3,2,1,0:T(8,128)(2,1)S(1)}, u32[]{:S(2)}, u32[]{:S(2)}) collective-permute-start(bf16[32,4,16,128]{3,2,1,0:T(8,128)(2,1)S(1)} %collective-permute-done.1.refs_2_), channel_id=1, source_target_pairs={{0,2},{2,0},{4,6},{6,4},{8,10},{10,8},{12,14},{14,12},{16,18},{18,... | collective-permute-start | bytes 1572872 | tf_op jit(solution)/shard_map/ppermute | solution.py:422
  42.8 13.6 %collective-permute-start.3 = (bf16[32,4,16,128]{3,2,1,0:T(8,128)(2,1)}, bf16[32,4,16,128]{3,2,1,0:T(8,128)(2,1)}, u32[]{:S(2)}, u32[]{:S(2)}) collective-permute-start(bf16[32,4,16,128]{3,2,1,0:T(8,128)(2,1)} %get-tuple-element.43), channel_id=1, source_target_pairs={{0,1},{2,3},{4,5},{6,7},{8,9},{10,11},{12,13},{14,15},{16,17},{18,... | collective-permute-start | bytes 1572872 | tf_op jit(solution)/shard_map/ppermute | solution.py:453
  45.6 16.0 %collective-permute-start.9 = (bf16[32,4,16,128]{3,2,1,0:T(8,128)(2,1)S(1)}, bf16[32,4,16,128]{3,2,1,0:T(8,128)(2,1)}, u32[]{:S(2)}, u32[]{:S(2)}) collective-permute-start(bf16[32,4,16,128]{3,2,1,0:T(8,128)(2,1)S(1)} %collective-permute-done.refs_0_), channel_id=1, source_target_pairs={{0,4},{2,6},{4,8},{6,10},{8,12},{10,14},{12,16},{14,18},{16,20},{1... | collective-permute-start | bytes 1572872 | tf_op jit(solution)/shard_map/ppermute | solution.py:402
  46.2 18.8 %copy-start.1 = (bf16[32,2,16,128]{3,2,1,0:T(8,128)(2,1)S(1)}, bf16[32,2,16,128]{3,2,1,0:T(8,128)(2,1)}, u32[]{:S(2)}) copy-start(bf16[32,2,16,128]{3,2,1,0:T(8,128)(2,1)} %copy-done) | copy-start | bytes 786436
  46.2 26.3 %collective-permute-start.11 = (bf16[32,4,16,128]{3,2,1,0:T(8,128)(2,1)S(1)}, bf16[32,4,16,128]{3,2,1,0:T(8,128)(2,1)S(1)}, u32[]{:S(2)}, u32[]{:S(2)}) collective-permute-start(bf16[32,4,16,128]{3,2,1,0:T(8,128)(2,1)S(1)} %collective-permute-done.refs_0_), channel_id=1, source_target_pairs={{0,2},{2,8},{4,6},{8,10},{10,16},{12,14},{16,18},{18,24},{20,22},{... | collective-permute-start | bytes 1572872 | tf_op jit(solution)/shard_map/ppermute | solution.py:414
  61.6 12.4 %collective-permute-start.10 = (bf16[32,4,16,128]{3,2,1,0:T(8,128)(2,1)}, bf16[32,4,16,128]{3,2,1,0:T(8,128)(2,1)S(1)}, u32[]{:S(2)}, u32[]{:S(2)}) collective-permute-start(bf16[32,4,16,128]{3,2,1,0:T(8,128)(2,1)} %collective-permute-done.9.refs_2_), channel_id=1, source_target_pairs={{0,2},{2,0},{4,6},{6,4},{8,10},{10,8},{12,14},{14,12},{16,18},{18,... | collective-permute-start | bytes 1572872 | tf_op jit(solution)/shard_map/ppermute | solution.py:422
  62.8 16.3 %collective-permute-start.14 = (bf16[32,4,16,128]{3,2,1,0:T(8,128)(2,1)S(1)}, bf16[32,4,16,128]{3,2,1,0:T(8,128)(2,1)S(1)}, u32[]{:S(2)}, u32[]{:S(2)}) collective-permute-start(bf16[32,4,16,128]{3,2,1,0:T(8,128)(2,1)S(1)} %broadcast_select_fusion.refs_0_), channel_id=1, source_target_pairs={{0,4},{2,6},{4,8},{6,10},{8,12},{10,14},{12,16},{14,18},{16,20},{1... | collective-permute-start | bytes 1572872 | tf_op jit(solution)/shard_map/ppermute | solution.py:402
  62.8 22.9 %collective-permute-start.12 = (bf16[32,4,16,128]{3,2,1,0:T(8,128)(2,1)}, bf16[32,4,16,128]{3,2,1,0:T(8,128)(2,1)S(1)}, u32[]{:S(2)}, u32[]{:S(2)}) collective-permute-start(bf16[32,4,16,128]{3,2,1,0:T(8,128)(2,1)} %collective-permute-done.9.refs_2_), channel_id=1, source_target_pairs={{2,4},{10,12},{18,20},{26,28},{3,5},{11,13},{19,21},{27,29}} | collective-permute-start | bytes 1572872 | tf_op jit(solution)/shard_map/ppermute | solution.py:418
  65.1 7.3 %collective-permute-start.6 = (bf16[32,2,16,128]{3,2,1,0:T(8,128)(2,1)S(1)}, bf16[32,2,16,128]{3,2,1,0:T(8,128)(2,1)S(1)}, u32[]{:S(2)}, u32[]{:S(2)}) collective-permute-start(bf16[32,2,16,128]{3,2,1,0:T(8,128)(2,1)S(1)} %copy-done.1), channel_id=1, source_target_pairs={{0,1},{1,0},{2,3},{3,2},{4,5},{5,4},{6,7},{7,6},{8,9},{9,8},{10,11... | collective-permute-start | bytes 786440 | tf_op jit(solution)/shard_map/ppermute | solution.py:458
  72.4 22.5 %collective-permute-start.7 = (bf16[32,4,16,128]{3,2,1,0:T(8,128)(2,1)S(1)}, bf16[32,4,16,128]{3,2,1,0:T(8,128)(2,1)S(1)}, u32[]{:S(2)}, u32[]{:S(2)}) collective-permute-start(bf16[32,4,16,128]{3,2,1,0:T(8,128)(2,1)S(1)} %constant_dynamic-update-slice_fusion.refs_0_), channel_id=1, source_target_pairs={{0,4},{2,6},{4,8},{6,10},{8,12},{10,14},{12,16},{14,18},{16,20},{1... | collective-permute-start | bytes 1572872 | tf_op jit(solution)/shard_map/ppermute | solution.py:402
  72.5 22.4 %collective-permute-start.8 = (bf16[32,4,16,128]{3,2,1,0:T(8,128)(2,1)S(1)}, bf16[32,4,16,128]{3,2,1,0:T(8,128)(2,1)S(1)}, u32[]{:S(2)}, u32[]{:S(2)}) collective-permute-start(bf16[32,4,16,128]{3,2,1,0:T(8,128)(2,1)S(1)} %constant_dynamic-update-slice_fusion.refs_0_), channel_id=1, source_target_pairs={{0,2},{2,8},{4,6},{6,12},{8,10},{10,16},{12,14},{14,20},{16,18},{1... | collective-permute-start | bytes 1572872 | tf_op jit(solution)/shard_map/ppermute | solution.py:407
  74.0 21.0 %collective-permute-start.16 = (bf16[32,4,16,128]{3,2,1,0:T(8,128)(2,1)S(1)}, bf16[32,4,16,128]{3,2,1,0:T(8,128)(2,1)S(1)}, u32[]{:S(2)}, u32[]{:S(2)}) collective-permute-start(bf16[32,4,16,128]{3,2,1,0:T(8,128)(2,1)S(1)} %broadcast_select_fusion.refs_0_), channel_id=1, source_target_pairs={{0,2},{2,8},{4,6},{8,10},{10,16},{12,14},{16,18},{18,24},{20,22},{... | collective-permute-start | bytes 1572872 | tf_op jit(solution)/shard_map/ppermute | solution.py:414
  79.1 15.9 %collective-permute-start.15 = (bf16[32,4,16,128]{3,2,1,0:T(8,128)(2,1)S(1)}, bf16[32,4,16,128]{3,2,1,0:T(8,128)(2,1)S(1)}, u32[]{:S(2)}, u32[]{:S(2)}) collective-permute-start(bf16[32,4,16,128]{3,2,1,0:T(8,128)(2,1)S(1)} %collective-permute-done.14.refs_2_), channel_id=1, source_target_pairs={{0,2},{2,0},{4,6},{6,4},{8,10},{10,8},{12,14},{14,12},{16,18},{18,... | collective-permute-start | bytes 1572872 | tf_op jit(solution)/shard_map/ppermute | solution.py:422
  85.7 11.3 %collective-permute-start.17 = (bf16[32,4,16,128]{3,2,1,0:T(8,128)(2,1)S(1)}, bf16[32,4,16,128]{3,2,1,0:T(8,128)(2,1)S(1)}, u32[]{:S(2)}, u32[]{:S(2)}) collective-permute-start(bf16[32,4,16,128]{3,2,1,0:T(8,128)(2,1)S(1)} %collective-permute-done.14.refs_2_), channel_id=1, source_target_pairs={{2,4},{10,12},{18,20},{26,28},{3,5},{11,13},{19,21},{27,29}} | collective-permute-start | bytes 1572872 | tf_op jit(solution)/shard_map/ppermute | solution.py:418
  94.9 5.8 %collective-permute-start.13 = (bf16[32,4,16,128]{3,2,1,0:T(8,128)(2,1)S(1)}, bf16[32,4,16,128]{3,2,1,0:T(8,128)(2,1)S(1)}, u32[]{:S(2)}, u32[]{:S(2)}) collective-permute-start(bf16[32,4,16,128]{3,2,1,0:T(8,128)(2,1)S(1)} %collective-permute-done.7.refs_2_), channel_id=1, source_target_pairs={{0,2},{2,0},{4,6},{6,4},{8,10},{10,8},{12,14},{14,12},{16,18},{18,... | collective-permute-start | bytes 1572872 | tf_op jit(solution)/shard_map/ppermute | solution.py:422

commit v21 on v18

--- a/solution.py
+++ b/solution.py
@@ -464,7 +464,8 @@
     two_c, rest_c = farther(piece_c)
     pair_b = exchanged(two_b)
     sums = correlated([piece_b, pair_b, two_b, rest_b], first, sums, False)
-    pair_c = exchanged(after(two_c, rest_c, sums))
+    rest_c, two_c, sums = lax.optimization_barrier((rest_c, two_c, sums))
+    pair_c = exchanged(two_c)
     return correlated([piece_c, pair_c, two_c, rest_c], [(few, [(0, 0, 0), (0, 0, few)])], sums, True)
 
 

time: 105 us -> 104 us (level)
  the two profiles are of different devices: /device:TPU:7 before, /device:TPU:1 now
where the time goes in v21:
time: 104 us; the launch traced here: 103 us
  Pallas kernels  49.1 us (47%)
  waiting for transfers between devices  26.7 us (26%)
  starting transfers between devices  25.9 us (25%)
    pallas_call x3, Pallas kernels, spectra(): pl.pallas_call(functools.partial(spectra_kernel, groups, tuple((part[1:]...  30.1 us
    pallas_call x4, Pallas kernels, correlate(): pl.pallas_call(functools.partial(correlate_kernel, pieces, per_group, sca...  15.7 us
    ppermute x1, waiting for transfers between devices, relayed(): lax.ppermute(two, 'stn', [(i, i + 1) for i in range(lax.axis_size('stn'))...  8.02 us
    ppermute x1, waiting for transfers between devices, paired(): got_b = lax.ppermute(away_b, 'tm', [(0, 1)])  7.98 us
    ppermute x4, starting transfers between devices, exchanged(): lax.ppermute(block, 'stn', [(i, i ^ 1) for i in range(lax.axis_size('stn'...  5.08 us
    ppermute x3, starting transfers between devices, farther(): lax.ppermute(block, 'stn', [(i, (i + 1 if i % 2 == 0 else i + 3) % size)...  4.9 us
    ppermute x4, waiting for transfers between devices, shifted(): lax.ppermute(block, axis, [(i, (i + distance) % size) for i in range(size)])  4.42 us
    ppermute x1, waiting for transfers between devices, paired(): got_c = lax.ppermute(away_c, 'tm', swap)  4.36 us
  transfers between devices with their start and end apart: 17, of which 6 were waited for; matrix products, arithmetic and copies ran while one was open for 0% of the time, Pallas kernels for 40%

profile of v21, /device:TPU:1, one launch (start us, length us, event | category | flops | bytes accessed | tf_op | source)
XLA Modules:
  0.0 102.7 jit_solution(736223590228200039)
XLA Ops:
  0.0 0.1 pad_add_fusion.place
  0.1 3.3 %shard_map.46 = (bf16[8,32,64,128]{3,2,1,0:T(8,128)(2,1)S(1)}, bf16[8,8,64,128]{3,2,1,0:T(8,128)(2,1)S(1)}, f32[1024,128]{1,0:T(8,128)S(1)}, bf16[64,192]{1,0:T(...) custom-call(s32[2]{0:T(128)S(1)} %pad_add_fusion.place, bf16[8,32,64,128]{3,2,1,0:T(8,128)(2,1)} %bitcast.10, ...), custom_call_target="tpu_custom_call" | custom-call | tf_op jit(solution)/shard_map/pallas_call | solution.py:110
  3.4 2.1 %collective-permute-start.2 = (bf16[8,8,64,128]{3,2,1,0:T(8,128)(2,1)S(1)}, bf16[8,8,64,128]{3,2,1,0:T(8,128)(2,1)S(1)}, u32[]{:S(2)}, u32[]{:S(2)}) collective-permute-start(bf16[8,8,64,128]{3,2,1,0:T(8,128)(2,1)S(1)} %get-tuple-element.40), channel_id=1, source_target_pairs={{0,1},{1,0},{2,3},{3,2},{4,5},{5,4},{6,7},{7,6},{8,9},{9,8},{10,11... | collective-permute-start | bytes 3145736 | tf_op jit(solution)/shard_map/ppermute | solution.py:434
  5.5 11.3 %shard_map.47 = (bf16[32,4,16,128]{3,2,1,0:T(8,128)(2,1)S(1)}, bf16[32,4,16,128]{3,2,1,0:T(8,128)(2,1)S(1)}) custom-call(s32[2]{0:T(128)S(1)} %pad_add_fusion.place, bf16[8,32,64,128]{3,2,1,0:T(8,128)(2,1)S(1)} %get-tuple-element.30.refs_0_.refs_1_, bf16[8,32,64,128]{3,2,1,0:T(8,128)(2,1)S(1)} %get-tuple-element.30.refs_0_.refs_1_, ...), custom_call_target="tpu_custom_call" | custom-call | flops 1000000 | tf_op jit(solution)/shard_map/pallas_call | solution.py:263
  16.8 1.3 %collective-permute-start.1 = (bf16[32,4,16,128]{3,2,1,0:T(8,128)(2,1)S(1)}, bf16[32,4,16,128]{3,2,1,0:T(8,128)(2,1)S(1)}, u32[]{:S(2)}, u32[]{:S(2)}) collective-permute-start(bf16[32,4,16,128]{3,2,1,0:T(8,128)(2,1)S(1)} %get-tuple-element.36.refs_0_), channel_id=1, source_target_pairs={{0,4},{2,6},{4,8},{6,10},{8,12},{10,14},{12,16},{14,18},{16,20},{1... | collective-permute-start | bytes 1572872 | tf_op jit(solution)/shard_map/ppermute | solution.py:402
  18.1 0.3 collective-permute-start
  18.4 2.7 %collective-permute-start.5 = (bf16[32,4,16,128]{3,2,1,0:T(8,128)(2,1)S(1)}, bf16[32,4,16,128]{3,2,1,0:T(8,128)(2,1)S(1)}, u32[]{:S(2)}, u32[]{:S(2)}) collective-permute-start(bf16[32,4,16,128]{3,2,1,0:T(8,128)(2,1)S(1)} %get-tuple-element.36.refs_0_), channel_id=1, source_target_pairs={{0,2},{2,8},{4,6},{6,12},{8,10},{10,16},{12,14},{14,20},{16,18},{1... | collective-permute-start | bytes 1572872 | tf_op jit(solution)/shard_map/ppermute | solution.py:407
  21.1 12.0 %shard_map.48 = (bf16[32,4,16,128]{3,2,1,0:T(8,128)(2,1)S(1)}, bf16[32,4,16,128]{3,2,1,0:T(8,128)(2,1)}) custom-call(s32[2]{0:T(128)S(1)} %pad_add_fusion.place, bf16[8,32,64,128]{3,2,1,0:T(8,128)(2,1)S(1)} %get-tuple-element.30.refs_0_.refs_1_, bf16[8,32,64,128]{3,2,1,0:T(8,128)(2,1)S(1)} %get-tuple-element.30.refs_0_.refs_1_, ...), custom_call_target="tpu_custom_call" | custom-call | flops 1000000 | tf_op jit(solution)/shard_map/pallas_call | solution.py:263
  33.1 0.0 collective-permute-done.1.refs_2_
  33.1 0.0 collective-permute-done.2.refs_2_
  33.1 6.7 %shard_map.49 = (bf16[32,2,16,128]{3,2,1,0:T(8,128)(2,1)S(1)}, bf16[32,2,16,128]{3,2,1,0:T(8,128)(2,1)S(1)}) custom-call(s32[2]{0:T(128)S(1)} %pad_add_fusion.place, bf16[8,32,64,128]{3,2,1,0:T(8,128)(2,1)S(1)} %get-tuple-element.30.refs_0_.refs_1_, bf16[8,32,64,128]{3,2,1,0:T(8,128)(2,1)S(1)} %get-tuple-element.30.refs_0_.refs_1_, ...), custom_call_target="tpu_custom_call" | custom-call | flops 1000000 | tf_op jit(solution)/shard_map/pallas_call | solution.py:263
  39.9 0.0 copy-start
  39.9 0.7 copy-done
  40.6 0.0 collective-permute-done.refs_0_
  40.6 2.3 %collective-permute-start.4 = (bf16[32,4,16,128]{3,2,1,0:T(8,128)(2,1)S(1)}, bf16[32,4,16,128]{3,2,1,0:T(8,128)(2,1)S(1)}, u32[]{:S(2)}, u32[]{:S(2)}) collective-permute-start(bf16[32,4,16,128]{3,2,1,0:T(8,128)(2,1)S(1)} %collective-permute-done.1.refs_2_), channel_id=1, source_target_pairs={{0,2},{2,0},{4,6},{6,4},{8,10},{10,8},{12,14},{14,12},{16,18},{18,... | collective-permute-start | bytes 1572872 | tf_op jit(solution)/shard_map/ppermute | solution.py:422
  42.8 2.7 %collective-permute-start.3 = (bf16[32,4,16,128]{3,2,1,0:T(8,128)(2,1)}, bf16[32,4,16,128]{3,2,1,0:T(8,128)(2,1)}, u32[]{:S(2)}, u32[]{:S(2)}) collective-permute-start(bf16[32,4,16,128]{3,2,1,0:T(8,128)(2,1)} %get-tuple-element.45), channel_id=1, source_target_pairs={{0,1},{2,3},{4,5},{6,7},{8,9},{10,11},{12,13},{14,15},{16,17},{18,... | collective-permute-start | bytes 1572872 | tf_op jit(solution)/shard_map/ppermute | solution.py:453
  45.6 0.7 collective-permute-start.12
  46.2 0.0 copy-start.1
  46.2 0.0 collective-permute-done.5.refs_3_
  46.2 0.0 collective-permute-done.4.refs_1_
  46.2 2.2 %shard_map.50.refs_5_ = f32[4096,128]{1,0:T(8,128)S(1)} custom-call(s32[2]{0:T(128)S(1)} %pad_add_fusion.place, bf16[32,4,16,128]{3,2,1,0:T(8,128)(2,1)S(1)} %get-tuple-element.36.refs_0_, bf16[32,4,16,128]{3,2,1,0:T(8,128)(2,1)S(1)} %collective-permute-done.4.refs_1_, bf16[32,4,16,128]{3,2,1,0:T(8,128)(2,1)S(1)} %collective-permute-done.1.refs_2_, ...), custom_call_target="tpu_custom_call" | custom-call | flops 1000 | tf_op jit(solution)/shard_map/pallas_call | solution.py:373
  48.4 8.0 %collective-permute-done.3 = bf16[32,4,16,128]{3,2,1,0:T(8,128)(2,1)} collective-permute-done((bf16[32,4,16,128]{3,2,1,0:T(8,128)(2,1)}, bf16[32,4,16,128]{3,2,1,0:T(8,128)(2,1)}, u32[]{:S(2)}, u32[]{:S(2)}) %collective-permute-start.3) | collective-permute-done | bytes 524320 | tf_op jit(solution)/shard_map/ppermute | solution.py:453
  56.4 0.1 broadcast_select_fusion.refs_0_
  56.5 0.7 collective-permute-start.9
  57.2 4.1 %collective-permute-start.14 = (bf16[32,4,16,128]{3,2,1,0:T(8,128)(2,1)S(1)}, bf16[32,4,16,128]{3,2,1,0:T(8,128)(2,1)S(1)}, u32[]{:S(2)}, u32[]{:S(2)}) collective-permute-start(bf16[32,4,16,128]{3,2,1,0:T(8,128)(2,1)S(1)} %collective-permute-done.refs_0_), channel_id=1, source_target_pairs={{0,2},{2,8},{4,6},{8,10},{10,16},{12,14},{16,18},{18,24},{20,22},{... | collective-permute-start | bytes 1572872 | tf_op jit(solution)/shard_map/ppermute | solution.py:414
  61.3 0.3 collective-permute-done.12.refs_2_
  61.6 1.3 %collective-permute-start.13 = (bf16[32,4,16,128]{3,2,1,0:T(8,128)(2,1)}, bf16[32,4,16,128]{3,2,1,0:T(8,128)(2,1)S(1)}, u32[]{:S(2)}, u32[]{:S(2)}) collective-permute-start(bf16[32,4,16,128]{3,2,1,0:T(8,128)(2,1)} %collective-permute-done.12.refs_2_), channel_id=1, source_target_pairs={{0,2},{2,0},{4,6},{6,4},{8,10},{10,8},{12,14},{14,12},{16,18},{18,... | collective-permute-start | bytes 1572872 | tf_op jit(solution)/shard_map/ppermute | solution.py:422
  62.9 0.0 copy-done.1
  62.9 1.8 %collective-permute-start.6 = (bf16[32,2,16,128]{3,2,1,0:T(8,128)(2,1)S(1)}, bf16[32,2,16,128]{3,2,1,0:T(8,128)(2,1)S(1)}, u32[]{:S(2)}, u32[]{:S(2)}) collective-permute-start(bf16[32,2,16,128]{3,2,1,0:T(8,128)(2,1)S(1)} %copy-done.1), channel_id=1, source_target_pairs={{0,1},{1,0},{2,3},{3,2},{4,5},{5,4},{6,7},{7,6},{8,9},{9,8},{10,11... | collective-permute-start | bytes 786440 | tf_op jit(solution)/shard_map/ppermute | solution.py:458
  64.8 1.9 %collective-permute-start.11 = (bf16[32,4,16,128]{3,2,1,0:T(8,128)(2,1)S(1)}, bf16[32,4,16,128]{3,2,1,0:T(8,128)(2,1)S(1)}, u32[]{:S(2)}, u32[]{:S(2)}) collective-permute-start(bf16[32,4,16,128]{3,2,1,0:T(8,128)(2,1)S(1)} %broadcast_select_fusion.refs_0_), channel_id=1, source_target_pairs={{0,2},{2,8},{4,6},{6,12},{8,10},{10,16},{12,14},{14,20},{16,18},{1... | collective-permute-start | bytes 1572872 | tf_op jit(solution)/shard_map/ppermute | solution.py:407
  66.7 4.4 %collective-permute-done.6 = bf16[32,2,16,128]{3,2,1,0:T(8,128)(2,1)S(1)} collective-permute-done((bf16[32,2,16,128]{3,2,1,0:T(8,128)(2,1)S(1)}, bf16[32,2,16,128]{3,2,1,0:T(8,128)(2,1)S(1)}, u32[]{:S(2)}, u32[]{:S(2)}) %collective-permute-start.6) | collective-permute-done | bytes 262176 | tf_op jit(solution)/shard_map/ppermute | solution.py:458
  71.1 2.2 %collective-permute-start.15 = (bf16[32,4,16,128]{3,2,1,0:T(8,128)(2,1)}, bf16[32,4,16,128]{3,2,1,0:T(8,128)(2,1)S(1)}, u32[]{:S(2)}, u32[]{:S(2)}) collective-permute-start(bf16[32,4,16,128]{3,2,1,0:T(8,128)(2,1)} %collective-permute-done.12.refs_2_), channel_id=1, source_target_pairs={{2,4},{10,12},{18,20},{26,28},{3,5},{11,13},{19,21},{27,29}} | collective-permute-start | bytes 1572872 | tf_op jit(solution)/shard_map/ppermute | solution.py:418
  73.3 0.0 collective-permute-done.9.refs_2_
  73.4 1.5 %collective-permute-start.10 = (bf16[32,4,16,128]{3,2,1,0:T(8,128)(2,1)S(1)}, bf16[32,4,16,128]{3,2,1,0:T(8,128)(2,1)S(1)}, u32[]{:S(2)}, u32[]{:S(2)}) collective-permute-start(bf16[32,4,16,128]{3,2,1,0:T(8,128)(2,1)S(1)} %collective-permute-done.9.refs_2_), channel_id=1, source_target_pairs={{0,2},{2,0},{4,6},{6,4},{8,10},{10,8},{12,14},{14,12},{16,18},{18,... | collective-permute-start | bytes 1572872 | tf_op jit(solution)/shard_map/ppermute | solution.py:422
  74.9 0.0 collective-permute-done.14.refs_3_
  74.9 0.3 collective-permute-start.7
  75.1 0.0 collective-permute-done.13.refs_1_
  75.1 0.0 collective-permute-start.8
  75.1 8.0 %collective-permute-done.15.refs_4_ = bf16[32,4,16,128]{3,2,1,0:T(8,128)(2,1)S(1)} collective-permute-done((bf16[32,4,16,128]{3,2,1,0:T(8,128)(2,1)}, bf16[32,4,16,128]{3,2,1,0:T(8,128)(2,1)S(1)}, u32[]{:S(2)}, u32[]{:S(2)}) %collective-permute-start.15) | collective-permute-done | bytes 524320 | tf_op jit(solution)/shard_map/ppermute | solution.py:418
  83.1 4.7 %shard_map.51.refs_4_ = f32[4096,128]{1,0:T(8,128)S(1)} custom-call(s32[2]{0:T(128)S(1)} %pad_add_fusion.place, bf16[32,4,16,128]{3,2,1,0:T(8,128)(2,1)S(1)} %collective-permute-done.refs_0_, bf16[32,4,16,128]{3,2,1,0:T(8,128)(2,1)S(1)} %collective-permute-done.13.refs_1_, ...), custom_call_target="tpu_custom_call", output_to_operand_aliasing={{}: (6, {})} | custom-call | flops 1000 | tf_op jit(solution)/shard_map/pallas_call | solution.py:373
  87.8 0.0 collective-permute-done.11.refs_3_
  87.8 0.0 collective-permute-done.10.refs_1_
  87.8 3.6 %shard_map.52.refs_4_ = f32[4096,128]{1,0:T(8,128)S(1)} custom-call(s32[2]{0:T(128)S(1)} %pad_add_fusion.place, bf16[32,4,16,128]{3,2,1,0:T(8,128)(2,1)S(1)} %broadcast_select_fusion.refs_0_, bf16[32,4,16,128]{3,2,1,0:T(8,128)(2,1)S(1)} %collective-permute-done.10.refs_1_, ...), custom_call_target="tpu_custom_call", output_to_operand_aliasing={{}: (5, {})} | custom-call | flops 1000 | tf_op jit(solution)/shard_map/pallas_call | solution.py:373
  91.5 0.0 collective-permute-done.7.refs_3_
  91.5 4.1 %collective-permute-done.8.refs_2_ = bf16[32,4,16,128]{3,2,1,0:T(8,128)(2,1)S(1)} collective-permute-done((bf16[32,4,16,128]{3,2,1,0:T(8,128)(2,1)S(1)}, bf16[32,4,16,128]{3,2,1,0:T(8,128)(2,1)S(1)}, u32[]{:S(2)}, u32[]{:S(2)}) %collective-permute-start.8) | collective-permute-done | bytes 524320 | tf_op jit(solution)/shard_map/ppermute | solution.py:402
  95.6 0.0 collective-permute-start.16
  95.6 1.9 %collective-permute-done.16.refs_1_ = bf16[32,4,16,128]{3,2,1,0:T(8,128)(2,1)S(1)} collective-permute-done((bf16[32,4,16,128]{3,2,1,0:T(8,128)(2,1)S(1)}, bf16[32,4,16,128]{3,2,1,0:T(8,128)(2,1)S(1)}, u32[]{:S(2)}, u32[]{:S(2)}) %collective-permute-start.16) | collective-permute-done | bytes 524320 | tf_op jit(solution)/shard_map/ppermute | solution.py:422
  97.5 5.2 %shard_map.53 = f32[2,8,4,8,8,128]{5,4,3,2,1,0:T(8,128)} custom-call(s32[2]{0:T(128)S(1)} %pad_add_fusion.place, bf16[32,4,16,128]{3,2,1,0:T(8,128)(2,1)S(1)} %constant_dynamic-update-slice_fusion.refs_0_, bf16[32,4,16,128]{3,2,1,0:T(8,128)(2,1)S(1)} %collective-permute-done.16.refs_1_, bf16[32,4,16,128]{3,2,1,0:T(8,128)(2,1)S(1)} %collective-permute-done.8.refs_2_, ...), custom_call_target="tpu_custom_call" | custom-call | flops 1000 | tf_op jit(solution)/shard_map/pallas_call | solution.py:373
  (2 shorter events, 0.1 us)
Async XLA Ops:
  3.4 29.7 %collective-permute-start.2 = (bf16[8,8,64,128]{3,2,1,0:T(8,128)(2,1)S(1)}, bf16[8,8,64,128]{3,2,1,0:T(8,128)(2,1)S(1)}, u32[]{:S(2)}, u32[]{:S(2)}) collective-permute-start(bf16[8,8,64,128]{3,2,1,0:T(8,128)(2,1)S(1)} %get-tuple-element.40), channel_id=1, source_target_pairs={{0,1},{1,0},{2,3},{3,2},{4,5},{5,4},{6,7},{7,6},{8,9},{9,8},{10,11... | collective-permute-start | bytes 3145736 | tf_op jit(solution)/shard_map/ppermute | solution.py:434
  16.8 16.3 %collective-permute-start.1 = (bf16[32,4,16,128]{3,2,1,0:T(8,128)(2,1)S(1)}, bf16[32,4,16,128]{3,2,1,0:T(8,128)(2,1)S(1)}, u32[]{:S(2)}, u32[]{:S(2)}) collective-permute-start(bf16[32,4,16,128]{3,2,1,0:T(8,128)(2,1)S(1)} %get-tuple-element.36.refs_0_), channel_id=1, source_target_pairs={{0,4},{2,6},{4,8},{6,10},{8,12},{10,14},{12,16},{14,18},{16,20},{1... | collective-permute-start | bytes 1572872 | tf_op jit(solution)/shard_map/ppermute | solution.py:402
  18.1 22.5 %collective-permute-start = (bf16[32,4,16,128]{3,2,1,0:T(8,128)(2,1)S(1)}, bf16[32,4,16,128]{3,2,1,0:T(8,128)(2,1)S(1)}, u32[]{:S(2)}, u32[]{:S(2)}) collective-permute-start(bf16[32,4,16,128]{3,2,1,0:T(8,128)(2,1)S(1)} %get-tuple-element.35), channel_id=1, source_target_pairs={{0,1},{1,0},{2,3},{3,2},{4,5},{5,4},{6,7},{7,6},{8,9},{9,8},{10,11... | collective-permute-start | bytes 1572872 | tf_op jit(solution)/shard_map/ppermute | solution.py:438
  18.4 27.9 %collective-permute-start.5 = (bf16[32,4,16,128]{3,2,1,0:T(8,128)(2,1)S(1)}, bf16[32,4,16,128]{3,2,1,0:T(8,128)(2,1)S(1)}, u32[]{:S(2)}, u32[]{:S(2)}) collective-permute-start(bf16[32,4,16,128]{3,2,1,0:T(8,128)(2,1)S(1)} %get-tuple-element.36.refs_0_), channel_id=1, source_target_pairs={{0,2},{2,8},{4,6},{6,12},{8,10},{10,16},{12,14},{14,20},{16,18},{1... | collective-permute-start | bytes 1572872 | tf_op jit(solution)/shard_map/ppermute | solution.py:407
  39.9 0.7 copy-start
  40.6 5.7 %collective-permute-start.4 = (bf16[32,4,16,128]{3,2,1,0:T(8,128)(2,1)S(1)}, bf16[32,4,16,128]{3,2,1,0:T(8,128)(2,1)S(1)}, u32[]{:S(2)}, u32[]{:S(2)}) collective-permute-start(bf16[32,4,16,128]{3,2,1,0:T(8,128)(2,1)S(1)} %collective-permute-done.1.refs_2_), channel_id=1, source_target_pairs={{0,2},{2,0},{4,6},{6,4},{8,10},{10,8},{12,14},{14,12},{16,18},{18,... | collective-permute-start | bytes 1572872 | tf_op jit(solution)/shard_map/ppermute | solution.py:422
  42.8 13.6 %collective-permute-start.3 = (bf16[32,4,16,128]{3,2,1,0:T(8,128)(2,1)}, bf16[32,4,16,128]{3,2,1,0:T(8,128)(2,1)}, u32[]{:S(2)}, u32[]{:S(2)}) collective-permute-start(bf16[32,4,16,128]{3,2,1,0:T(8,128)(2,1)} %get-tuple-element.45), channel_id=1, source_target_pairs={{0,1},{2,3},{4,5},{6,7},{8,9},{10,11},{12,13},{14,15},{16,17},{18,... | collective-permute-start | bytes 1572872 | tf_op jit(solution)/shard_map/ppermute | solution.py:453
  45.6 16.0 %collective-permute-start.12 = (bf16[32,4,16,128]{3,2,1,0:T(8,128)(2,1)S(1)}, bf16[32,4,16,128]{3,2,1,0:T(8,128)(2,1)}, u32[]{:S(2)}, u32[]{:S(2)}) collective-permute-start(bf16[32,4,16,128]{3,2,1,0:T(8,128)(2,1)S(1)} %collective-permute-done.refs_0_), channel_id=1, source_target_pairs={{0,4},{2,6},{4,8},{6,10},{8,12},{10,14},{12,16},{14,18},{16,20},{1... | collective-permute-start | bytes 1572872 | tf_op jit(solution)/shard_map/ppermute | solution.py:402
  46.2 16.7 %copy-start.1 = (bf16[32,2,16,128]{3,2,1,0:T(8,128)(2,1)S(1)}, bf16[32,2,16,128]{3,2,1,0:T(8,128)(2,1)}, u32[]{:S(2)}) copy-start(bf16[32,2,16,128]{3,2,1,0:T(8,128)(2,1)} %copy-done) | copy-start | bytes 786436
  56.5 16.9 %collective-permute-start.9 = (bf16[32,4,16,128]{3,2,1,0:T(8,128)(2,1)S(1)}, bf16[32,4,16,128]{3,2,1,0:T(8,128)(2,1)S(1)}, u32[]{:S(2)}, u32[]{:S(2)}) collective-permute-start(bf16[32,4,16,128]{3,2,1,0:T(8,128)(2,1)S(1)} %broadcast_select_fusion.refs_0_), channel_id=1, source_target_pairs={{0,4},{2,6},{4,8},{6,10},{8,12},{10,14},{12,16},{14,18},{16,20},{1... | collective-permute-start | bytes 1572872 | tf_op jit(solution)/shard_map/ppermute | solution.py:402
  57.2 17.7 %collective-permute-start.14 = (bf16[32,4,16,128]{3,2,1,0:T(8,128)(2,1)S(1)}, bf16[32,4,16,128]{3,2,1,0:T(8,128)(2,1)S(1)}, u32[]{:S(2)}, u32[]{:S(2)}) collective-permute-start(bf16[32,4,16,128]{3,2,1,0:T(8,128)(2,1)S(1)} %collective-permute-done.refs_0_), channel_id=1, source_target_pairs={{0,2},{2,8},{4,6},{8,10},{10,16},{12,14},{16,18},{18,24},{20,22},{... | collective-permute-start | bytes 1572872 | tf_op jit(solution)/shard_map/ppermute | solution.py:414
  61.6 13.5 %collective-permute-start.13 = (bf16[32,4,16,128]{3,2,1,0:T(8,128)(2,1)}, bf16[32,4,16,128]{3,2,1,0:T(8,128)(2,1)S(1)}, u32[]{:S(2)}, u32[]{:S(2)}) collective-permute-start(bf16[32,4,16,128]{3,2,1,0:T(8,128)(2,1)} %collective-permute-done.12.refs_2_), channel_id=1, source_target_pairs={{0,2},{2,0},{4,6},{6,4},{8,10},{10,8},{12,14},{14,12},{16,18},{18,... | collective-permute-start | bytes 1572872 | tf_op jit(solution)/shard_map/ppermute | solution.py:422
  62.9 8.2 %collective-permute-start.6 = (bf16[32,2,16,128]{3,2,1,0:T(8,128)(2,1)S(1)}, bf16[32,2,16,128]{3,2,1,0:T(8,128)(2,1)S(1)}, u32[]{:S(2)}, u32[]{:S(2)}) collective-permute-start(bf16[32,2,16,128]{3,2,1,0:T(8,128)(2,1)S(1)} %copy-done.1), channel_id=1, source_target_pairs={{0,1},{1,0},{2,3},{3,2},{4,5},{5,4},{6,7},{7,6},{8,9},{9,8},{10,11... | collective-permute-start | bytes 786440 | tf_op jit(solution)/shard_map/ppermute | solution.py:458
  64.8 23.0 %collective-permute-start.11 = (bf16[32,4,16,128]{3,2,1,0:T(8,128)(2,1)S(1)}, bf16[32,4,16,128]{3,2,1,0:T(8,128)(2,1)S(1)}, u32[]{:S(2)}, u32[]{:S(2)}) collective-permute-start(bf16[32,4,16,128]{3,2,1,0:T(8,128)(2,1)S(1)} %broadcast_select_fusion.refs_0_), channel_id=1, source_target_pairs={{0,2},{2,8},{4,6},{6,12},{8,10},{10,16},{12,14},{14,20},{16,18},{1... | collective-permute-start | bytes 1572872 | tf_op jit(solution)/shard_map/ppermute | solution.py:407
  71.1 12.1 %collective-permute-start.15 = (bf16[32,4,16,128]{3,2,1,0:T(8,128)(2,1)}, bf16[32,4,16,128]{3,2,1,0:T(8,128)(2,1)S(1)}, u32[]{:S(2)}, u32[]{:S(2)}) collective-permute-start(bf16[32,4,16,128]{3,2,1,0:T(8,128)(2,1)} %collective-permute-done.12.refs_2_), channel_id=1, source_target_pairs={{2,4},{10,12},{18,20},{26,28},{3,5},{11,13},{19,21},{27,29}} | collective-permute-start | bytes 1572872 | tf_op jit(solution)/shard_map/ppermute | solution.py:418
  73.4 14.5 %collective-permute-start.10 = (bf16[32,4,16,128]{3,2,1,0:T(8,128)(2,1)S(1)}, bf16[32,4,16,128]{3,2,1,0:T(8,128)(2,1)S(1)}, u32[]{:S(2)}, u32[]{:S(2)}) collective-permute-start(bf16[32,4,16,128]{3,2,1,0:T(8,128)(2,1)S(1)} %collective-permute-done.9.refs_2_), channel_id=1, source_target_pairs={{0,2},{2,0},{4,6},{6,4},{8,10},{10,8},{12,14},{14,12},{16,18},{18,... | collective-permute-start | bytes 1572872 | tf_op jit(solution)/shard_map/ppermute | solution.py:422
  74.9 16.6 %collective-permute-start.7 = (bf16[32,4,16,128]{3,2,1,0:T(8,128)(2,1)S(1)}, bf16[32,4,16,128]{3,2,1,0:T(8,128)(2,1)S(1)}, u32[]{:S(2)}, u32[]{:S(2)}) collective-permute-start(bf16[32,4,16,128]{3,2,1,0:T(8,128)(2,1)S(1)} %constant_dynamic-update-slice_fusion.refs_0_), channel_id=1, source_target_pairs={{0,2},{2,8},{4,6},{6,12},{8,10},{10,16},{12,14},{14,20},{16,18},{1... | collective-permute-start | bytes 1572872 | tf_op jit(solution)/shard_map/ppermute | solution.py:407
  75.1 20.5 %collective-permute-start.8 = (bf16[32,4,16,128]{3,2,1,0:T(8,128)(2,1)S(1)}, bf16[32,4,16,128]{3,2,1,0:T(8,128)(2,1)S(1)}, u32[]{:S(2)}, u32[]{:S(2)}) collective-permute-start(bf16[32,4,16,128]{3,2,1,0:T(8,128)(2,1)S(1)} %constant_dynamic-update-slice_fusion.refs_0_), channel_id=1, source_target_pairs={{0,4},{2,6},{4,8},{6,10},{8,12},{10,14},{12,16},{14,18},{16,20},{1... | collective-permute-start | bytes 1572872 | tf_op jit(solution)/shard_map/ppermute | solution.py:402
  95.6 1.9 %collective-permute-start.16 = (bf16[32,4,16,128]{3,2,1,0:T(8,128)(2,1)S(1)}, bf16[32,4,16,128]{3,2,1,0:T(8,128)(2,1)S(1)}, u32[]{:S(2)}, u32[]{:S(2)}) collective-permute-start(bf16[32,4,16,128]{3,2,1,0:T(8,128)(2,1)S(1)} %collective-permute-done.8.refs_2_), channel_id=1, source_target_pairs={{0,2},{2,0},{4,6},{6,4},{8,10},{10,8},{12,14},{14,12},{16,18},{18,... | collective-permute-start | bytes 1572872 | tf_op jit(solution)/shard_map/ppermute | solution.py:422

commit v22 on v21

--- a/solution.py
+++ b/solution.py
@@ -73,15 +73,35 @@
     return number[0] + (number[1] - number[0]) * group
 
 
-def prepare_kernel(edge_block, swapped, place, volts_source, taps_source, table_source, turn_source, volts, edge, taps, one, two, turn, done, taps_ref, table_ref):
+def cut_kernel(edge_block, place, source, edge, done):
     count = edge.shape[1]
     start = pl.multiple_of(value_of(edge_block, place[0]) * count, count)
+    copy = pltpu.make_async_copy(source.at[:, pl.ds(start, count)], edge, done)
+    copy.start()
+    copy.wait()
+
+
+def cut(volts, place, edge_block, edge_frames):
+    return pl.pallas_call(
+        functools.partial(cut_kernel, edge_block),
+        grid_spec=pltpu.PrefetchScalarGridSpec(
+            num_scalar_prefetch=1,
+            grid=(),
+            in_specs=[pl.BlockSpec(memory_space=pl.ANY)],
+            out_specs=pl.BlockSpec(memory_space=pltpu.VMEM),
+            scratch_shapes=[pltpu.SemaphoreType.DMA],
+        ),
+        out_shape=jax.ShapeDtypeStruct((volts.shape[0], edge_frames, ROWS, LANES), BF16),
+        compiler_params=pltpu.CompilerParams(vmem_limit_bytes=24 << 20),
+    )(place, pltpu.with_memory_space_constraint(volts, pltpu.HBM))
+
+
+def prepare_kernel(swapped, place, volts_source, taps_source, table_source, turn_source, volts, taps, one, two, turn, done, taps_ref, table_ref):
     copies = [
         pltpu.make_async_copy(taps_source, taps_ref, done.at[0]),
         pltpu.make_async_copy(table_source, table_ref, done.at[1]),
-        pltpu.make_async_copy(volts_source.at[:, pl.ds(start, count)], edge, done.at[2]),
-        pltpu.make_async_copy(volts_source, volts, done.at[3]),
-        pltpu.make_async_copy(turn_source, turn, done.at[4]),
+        pltpu.make_async_copy(volts_source, volts, done.at[2]),
+        pltpu.make_async_copy(turn_source, turn, done.at[3]),
     ]
     for copy in copies:
         copy.start()
@@ -102,27 +122,26 @@
         copy.wait()
 
 
-def prepare(volts, fir_taps, place, groups, edge_block, edge_frames):
+def prepare(volts, fir_taps, place, groups):
     signals, frames = volts.shape[:2]
     two = stage_two_table(groups)
     table = np.concatenate([stage_one_table(), two, np.roll(two, K2, axis=0)]).astype(np.float32)
     vmem = pl.BlockSpec(memory_space=pltpu.VMEM)
     return pl.pallas_call(
-        functools.partial(prepare_kernel, edge_block, int(groups == 2)),
+        functools.partial(prepare_kernel, int(groups == 2)),
         grid_spec=pltpu.PrefetchScalarGridSpec(
             num_scalar_prefetch=1,
             grid=(),
             in_specs=[pl.BlockSpec(memory_space=pl.ANY)] * 4,
-            out_specs=[vmem] * 6,
+            out_specs=[vmem] * 5,
             scratch_shapes=[
-                pltpu.SemaphoreType.DMA((5,)),
+                pltpu.SemaphoreType.DMA((4,)),
                 pltpu.VMEM(fir_taps.shape, F32),
                 pltpu.VMEM(table.shape, F32),
             ],
         ),
         out_shape=[
             jax.ShapeDtypeStruct((signals, frames, ROWS, LANES), BF16),
-            jax.ShapeDtypeStruct((signals, edge_frames, ROWS, LANES), BF16),
             jax.ShapeDtypeStruct((TAPS * ROWS, LANES), F32),
             jax.ShapeDtypeStruct((ROWS, 3 * ROWS), BF16),
             jax.ShapeDtypeStruct((2, 2 * K2, 2 * LANES), BF16),
@@ -430,8 +449,9 @@
     edge = TAPS // 2
     last = frames // edge
     many, few = TAPS * H // LANES, edge * H // LANES
-    volts, edge_frames, *fixed = prepare(volts, fir_taps, place, 2, (last - 1, 0), edge)
+    edge_frames = cut(volts, place, (last - 1, 0), edge)
     visiting = lax.ppermute(edge_frames, "tm", swap)
+    volts, *fixed = prepare(volts, fir_taps, after(place, edge_frames), 2)
     own_a, away_a = spectra(
         [(volts, TAPS, 0, 0, (0, 1)), (volts, TAPS, (0, 1), TAPS, 1)], TAPS, fixed, place, 2, sizes
     )
@@ -472,7 +492,8 @@
 def general(volts, fir_taps, place, correlated):
     groups = lax.axis_size("tm")
     frames = volts.shape[1]
-    volts, edge_frames, *fixed = prepare(volts, fir_taps, place, groups, frames // TAPS - 1, TAPS)
+    edge_frames = cut(volts, place, frames // TAPS - 1, TAPS)
+    volts, *fixed = prepare(volts, fir_taps, place, groups)
     history = lax.ppermute(edge_frames, "tm", [(i, i + 1) for i in range(groups - 1)])
     parts = [(history, TAPS, 0, 0, 1)] + [(volts, TAPS, i, TAPS * (i + 1), 1) for i in range(frames // TAPS)]
     spectrum = spectra(parts, frames, fixed, place, groups, [K2])[0]

time: 104 us -> 105 us (level)
  waiting for transfers between devices: 26.7 us -> 32 us
  starting transfers between devices: 25.9 us -> 20.6 us
  Pallas kernels: 49.1 us -> 50.5 us
    ppermute x4, waiting for transfers between devices: 4.42 us -> 8.85 us  [shifted(): lax.ppermute(block, axis, [(i, (i + distance) % size) for i in range(size)])]
    ppermute x1, waiting for transfers between devices: 4.36 us -> 6.62 us  [paired(): got_c = lax.ppermute(away_c, 'tm', swap)]
    ppermute x1, waiting for transfers between devices: 8.02 us -> 6.01 us  [relayed(): lax.ppermute(two, 'stn', [(i, i + 1) for i in range(lax.axis_size('stn'))...]
    ppermute x1, starting transfers between devices: 1.83 us -> 0.01 us  [paired(): got_c = lax.ppermute(away_c, 'tm', swap)]
    ppermute x1, starting transfers between devices: 4.14 us -> 2.47 us  [evenly(): return (shifted(block, 'stn', 2), lax.ppermute(block, 'stn', ways))]
    pallas_call x1 -> x2, Pallas kernels: 3.29 us -> 4.73 us  [the longest x1 2.95 us: prepare(): pl.pallas_call(functools.partial(prepare_kernel, int(groups == 2)), grid_...]
    ppermute x4, starting transfers between devices: 2.62 us -> 1.57 us  [shifted(): lax.ppermute(block, axis, [(i, (i + distance) % size) for i in range(size)])]
  transfers between devices with their start and end apart: 17 -> 17, of which waited for: 6 -> 7; matrix products, arithmetic and copies ran while one was open for 0% -> 0% of each run, Pallas kernels for 40% -> 42%
where the time goes in v22:
time: 105 us; the launch traced here: 104 us
  Pallas kernels  50.5 us (48%)
  waiting for transfers between devices  32 us (30%)
  starting transfers between devices  20.6 us (20%)
    pallas_call x3, Pallas kernels, spectra(): pl.pallas_call(functools.partial(spectra_kernel, groups, tuple((part[1:]...  30.1 us
    pallas_call x4, Pallas kernels, correlate(): pl.pallas_call(functools.partial(correlate_kernel, pieces, per_group, sca...  15.7 us
    ppermute x4, waiting for transfers between devices, shifted(): lax.ppermute(block, axis, [(i, (i + distance) % size) for i in range(size)])  8.85 us
    ppermute x1, waiting for transfers between devices, paired(): got_b = lax.ppermute(away_b, 'tm', [(0, 1)])  8.63 us
    ppermute x1, waiting for transfers between devices, paired(): got_c = lax.ppermute(away_c, 'tm', swap)  6.62 us
    ppermute x1, waiting for transfers between devices, relayed(): lax.ppermute(two, 'stn', [(i, i + 1) for i in range(lax.axis_size('stn'))...  6.01 us
    ppermute x4, starting transfers between devices, exchanged(): lax.ppermute(block, 'stn', [(i, i ^ 1) for i in range(lax.axis_size('stn'...  6 us
    ppermute x3, starting transfers between devices, farther(): lax.ppermute(block, 'stn', [(i, (i + 1 if i % 2 == 0 else i + 3) % size)...  3.99 us
  transfers between devices with their start and end apart: 17, of which 7 were waited for; matrix products, arithmetic and copies ran while one was open for 0% of the time, Pallas kernels for 42%

profile of v22, /device:TPU:1, one launch (start us, length us, event | category | flops | bytes accessed | tf_op | source)
XLA Modules:
  0.0 104.2 jit_solution(9592724226556716240)
XLA Ops:
  0.0 0.1 pad_add_fusion.place
  0.1 1.8 %shard_map.46 = bf16[8,8,64,128]{3,2,1,0:T(8,128)(2,1)S(1)} custom-call(s32[2]{0:T(128)S(1)} %pad_add_fusion.place, bf16[8,32,64,128]{3,2,1,0:T(8,128)(2,1)} %bitcast.10), custom_call_target="tpu_custom_call" | custom-call | tf_op jit(solution)/shard_map/pallas_call | solution.py:85
  1.9 2.1 %collective-permute-start.2 = (bf16[8,8,64,128]{3,2,1,0:T(8,128)(2,1)S(1)}, bf16[8,8,64,128]{3,2,1,0:T(8,128)(2,1)S(1)}, u32[]{:S(2)}, u32[]{:S(2)}) collective-permute-start(bf16[8,8,64,128]{3,2,1,0:T(8,128)(2,1)S(1)} %shard_map.46), channel_id=1, source_target_pairs={{0,1},{1,0},{2,3},{3,2},{4,5},{5,4},{6,7},{7,6},{8,9},{9,8},{10,11... | collective-permute-start | bytes 3145736 | tf_op jit(solution)/shard_map/ppermute | solution.py:453
  4.0 3.0 %shard_map.47 = (bf16[8,32,64,128]{3,2,1,0:T(8,128)(2,1)S(1)}, f32[1024,128]{1,0:T(8,128)S(1)}, bf16[64,192]{1,0:T(8,128)(2,1)S(1)}, bf16[2,128,256]{2,1,0:T(8,128)(2,1)S(1)}, f32[32,256]{1,0:T(8,128)S(1)}) custom-call(s32[2]{0:T(128)S(1)} %pad_add_fusion.place, bf16[8,32,64,128]{3,2,1,0:T(8,128)(2,1)} %bitcast.11, f32[16,4096]{1,0:T(8,128)} %taps_source.1, ...), custom_call_target="tpu_custom_call" | custom-call | tf_op jit(solution)/shard_map/pallas_call | solution.py:130
  7.0 11.3 %shard_map.48 = (bf16[32,4,16,128]{3,2,1,0:T(8,128)(2,1)S(1)}, bf16[32,4,16,128]{3,2,1,0:T(8,128)(2,1)S(1)}) custom-call(s32[2]{0:T(128)S(1)} %pad_add_fusion.place, bf16[8,32,64,128]{3,2,1,0:T(8,128)(2,1)S(1)} %get-tuple-element.31.refs_0_.refs_1_, bf16[8,32,64,128]{3,2,1,0:T(8,128)(2,1)S(1)} %get-tuple-element.31.refs_0_.refs_1_, ...), custom_call_target="tpu_custom_call" | custom-call | flops 1000000 | tf_op jit(solution)/shard_map/pallas_call | solution.py:282
  18.3 1.3 %collective-permute-start.1 = (bf16[32,4,16,128]{3,2,1,0:T(8,128)(2,1)S(1)}, bf16[32,4,16,128]{3,2,1,0:T(8,128)(2,1)S(1)}, u32[]{:S(2)}, u32[]{:S(2)}) collective-permute-start(bf16[32,4,16,128]{3,2,1,0:T(8,128)(2,1)S(1)} %get-tuple-element.37.refs_0_), channel_id=1, source_target_pairs={{0,4},{2,6},{4,8},{6,10},{8,12},{10,14},{12,16},{14,18},{16,20},{1... | collective-permute-start | bytes 1572872 | tf_op jit(solution)/shard_map/ppermute | solution.py:421
  19.6 0.3 collective-permute-start
  19.8 2.7 %collective-permute-start.5 = (bf16[32,4,16,128]{3,2,1,0:T(8,128)(2,1)S(1)}, bf16[32,4,16,128]{3,2,1,0:T(8,128)(2,1)S(1)}, u32[]{:S(2)}, u32[]{:S(2)}) collective-permute-start(bf16[32,4,16,128]{3,2,1,0:T(8,128)(2,1)S(1)} %get-tuple-element.37.refs_0_), channel_id=1, source_target_pairs={{0,2},{2,8},{4,6},{6,12},{8,10},{10,16},{12,14},{14,20},{16,18},{1... | collective-permute-start | bytes 1572872 | tf_op jit(solution)/shard_map/ppermute | solution.py:426
  22.5 12.0 %shard_map.49 = (bf16[32,4,16,128]{3,2,1,0:T(8,128)(2,1)S(1)}, bf16[32,4,16,128]{3,2,1,0:T(8,128)(2,1)}) custom-call(s32[2]{0:T(128)S(1)} %pad_add_fusion.place, bf16[8,32,64,128]{3,2,1,0:T(8,128)(2,1)S(1)} %get-tuple-element.31.refs_0_.refs_1_, bf16[8,32,64,128]{3,2,1,0:T(8,128)(2,1)S(1)} %get-tuple-element.31.refs_0_.refs_1_, ...), custom_call_target="tpu_custom_call" | custom-call | flops 1000000 | tf_op jit(solution)/shard_map/pallas_call | solution.py:282
  34.6 0.0 collective-permute-done.1.refs_2_
  34.6 0.0 collective-permute-done.2.refs_2_
  34.6 6.7 %shard_map.50 = (bf16[32,2,16,128]{3,2,1,0:T(8,128)(2,1)S(1)}, bf16[32,2,16,128]{3,2,1,0:T(8,128)(2,1)S(1)}) custom-call(s32[2]{0:T(128)S(1)} %pad_add_fusion.place, bf16[8,32,64,128]{3,2,1,0:T(8,128)(2,1)S(1)} %get-tuple-element.31.refs_0_.refs_1_, bf16[8,32,64,128]{3,2,1,0:T(8,128)(2,1)S(1)} %get-tuple-element.31.refs_0_.refs_1_, ...), custom_call_target="tpu_custom_call" | custom-call | flops 1000000 | tf_op jit(solution)/shard_map/pallas_call | solution.py:282
  41.3 0.0 copy-start
  41.3 0.7 copy-done
  42.0 0.0 collective-permute-done.refs_0_
  42.0 2.3 %collective-permute-start.4 = (bf16[32,4,16,128]{3,2,1,0:T(8,128)(2,1)S(1)}, bf16[32,4,16,128]{3,2,1,0:T(8,128)(2,1)S(1)}, u32[]{:S(2)}, u32[]{:S(2)}) collective-permute-start(bf16[32,4,16,128]{3,2,1,0:T(8,128)(2,1)S(1)} %collective-permute-done.1.refs_2_), channel_id=1, source_target_pairs={{0,2},{2,0},{4,6},{6,4},{8,10},{10,8},{12,14},{14,12},{16,18},{18,... | collective-permute-start | bytes 1572872 | tf_op jit(solution)/shard_map/ppermute | solution.py:441
  44.3 2.7 %collective-permute-start.3 = (bf16[32,4,16,128]{3,2,1,0:T(8,128)(2,1)}, bf16[32,4,16,128]{3,2,1,0:T(8,128)(2,1)}, u32[]{:S(2)}, u32[]{:S(2)}) collective-permute-start(bf16[32,4,16,128]{3,2,1,0:T(8,128)(2,1)} %get-tuple-element.45), channel_id=1, source_target_pairs={{0,1},{2,3},{4,5},{6,7},{8,9},{10,11},{12,13},{14,15},{16,17},{18,... | collective-permute-start | bytes 1572872 | tf_op jit(solution)/shard_map/ppermute | solution.py:473
  47.0 0.0 collective-permute-start.12
  47.0 0.0 copy-start.1
  47.0 0.0 collective-permute-done.5.refs_3_
  47.0 0.0 collective-permute-done.4.refs_1_
  47.0 2.2 %shard_map.51.refs_5_ = f32[4096,128]{1,0:T(8,128)S(1)} custom-call(s32[2]{0:T(128)S(1)} %pad_add_fusion.place, bf16[32,4,16,128]{3,2,1,0:T(8,128)(2,1)S(1)} %get-tuple-element.37.refs_0_, bf16[32,4,16,128]{3,2,1,0:T(8,128)(2,1)S(1)} %collective-permute-done.4.refs_1_, bf16[32,4,16,128]{3,2,1,0:T(8,128)(2,1)S(1)} %collective-permute-done.1.refs_2_, ...), custom_call_target="tpu_custom_call" | custom-call | flops 1000 | tf_op jit(solution)/shard_map/pallas_call | solution.py:392
  49.3 8.6 %collective-permute-done.3 = bf16[32,4,16,128]{3,2,1,0:T(8,128)(2,1)} collective-permute-done((bf16[32,4,16,128]{3,2,1,0:T(8,128)(2,1)}, bf16[32,4,16,128]{3,2,1,0:T(8,128)(2,1)}, u32[]{:S(2)}, u32[]{:S(2)}) %collective-permute-start.3) | collective-permute-done | bytes 524320 | tf_op jit(solution)/shard_map/ppermute | solution.py:473
  57.9 0.1 broadcast_select_fusion.refs_0_
  57.9 0.1 collective-permute-start.9
  58.0 2.5 %collective-permute-start.14 = (bf16[32,4,16,128]{3,2,1,0:T(8,128)(2,1)S(1)}, bf16[32,4,16,128]{3,2,1,0:T(8,128)(2,1)S(1)}, u32[]{:S(2)}, u32[]{:S(2)}) collective-permute-start(bf16[32,4,16,128]{3,2,1,0:T(8,128)(2,1)S(1)} %collective-permute-done.refs_0_), channel_id=1, source_target_pairs={{0,2},{2,8},{4,6},{8,10},{10,16},{12,14},{16,18},{18,24},{20,22},{... | collective-permute-start | bytes 1572872 | tf_op jit(solution)/shard_map/ppermute | solution.py:433
  60.5 2.6 %collective-permute-done.12.refs_2_ = bf16[32,4,16,128]{3,2,1,0:T(8,128)(2,1)} collective-permute-done((bf16[32,4,16,128]{3,2,1,0:T(8,128)(2,1)S(1)}, bf16[32,4,16,128]{3,2,1,0:T(8,128)(2,1)}, u32[]{:S(2)}, u32[]{:S(2)}) %collective-permute-start.12) | collective-permute-done | bytes 524320 | tf_op jit(solution)/shard_map/ppermute | solution.py:421
  63.1 1.3 %collective-permute-start.13 = (bf16[32,4,16,128]{3,2,1,0:T(8,128)(2,1)}, bf16[32,4,16,128]{3,2,1,0:T(8,128)(2,1)S(1)}, u32[]{:S(2)}, u32[]{:S(2)}) collective-permute-start(bf16[32,4,16,128]{3,2,1,0:T(8,128)(2,1)} %collective-permute-done.12.refs_2_), channel_id=1, source_target_pairs={{0,2},{2,0},{4,6},{6,4},{8,10},{10,8},{12,14},{14,12},{16,18},{18,... | collective-permute-start | bytes 1572872 | tf_op jit(solution)/shard_map/ppermute | solution.py:441
  64.4 0.0 copy-done.1
  64.4 0.0 collective-permute-start.6
  64.4 1.3 %collective-permute-start.11 = (bf16[32,4,16,128]{3,2,1,0:T(8,128)(2,1)S(1)}, bf16[32,4,16,128]{3,2,1,0:T(8,128)(2,1)S(1)}, u32[]{:S(2)}, u32[]{:S(2)}) collective-permute-start(bf16[32,4,16,128]{3,2,1,0:T(8,128)(2,1)S(1)} %broadcast_select_fusion.refs_0_), channel_id=1, source_target_pairs={{0,2},{2,8},{4,6},{6,12},{8,10},{10,16},{12,14},{14,20},{16,18},{1... | collective-permute-start | bytes 1572872 | tf_op jit(solution)/shard_map/ppermute | solution.py:426
  65.7 6.6 %collective-permute-done.6 = bf16[32,2,16,128]{3,2,1,0:T(8,128)(2,1)S(1)} collective-permute-done((bf16[32,2,16,128]{3,2,1,0:T(8,128)(2,1)S(1)}, bf16[32,2,16,128]{3,2,1,0:T(8,128)(2,1)S(1)}, u32[]{:S(2)}, u32[]{:S(2)}) %collective-permute-start.6) | collective-permute-done | bytes 262176 | tf_op jit(solution)/shard_map/ppermute | solution.py:478
  72.3 1.4 %collective-permute-start.15 = (bf16[32,4,16,128]{3,2,1,0:T(8,128)(2,1)}, bf16[32,4,16,128]{3,2,1,0:T(8,128)(2,1)S(1)}, u32[]{:S(2)}, u32[]{:S(2)}) collective-permute-start(bf16[32,4,16,128]{3,2,1,0:T(8,128)(2,1)} %collective-permute-done.12.refs_2_), channel_id=1, source_target_pairs={{2,4},{10,12},{18,20},{26,28},{3,5},{11,13},{19,21},{27,29}} | collective-permute-start | bytes 1572872 | tf_op jit(solution)/shard_map/ppermute | solution.py:437
  73.8 0.1 collective-permute-done.9.refs_2_
  73.9 2.4 %collective-permute-start.10 = (bf16[32,4,16,128]{3,2,1,0:T(8,128)(2,1)S(1)}, bf16[32,4,16,128]{3,2,1,0:T(8,128)(2,1)S(1)}, u32[]{:S(2)}, u32[]{:S(2)}) collective-permute-start(bf16[32,4,16,128]{3,2,1,0:T(8,128)(2,1)S(1)} %collective-permute-done.9.refs_2_), channel_id=1, source_target_pairs={{0,2},{2,0},{4,6},{6,4},{8,10},{10,8},{12,14},{14,12},{16,18},{18,... | collective-permute-start | bytes 1572872 | tf_op jit(solution)/shard_map/ppermute | solution.py:441
  76.3 0.0 collective-permute-done.14.refs_3_
  76.3 0.0 collective-permute-start.7
  76.3 0.0 collective-permute-done.13.refs_1_
  76.3 0.2 collective-permute-start.8
  76.6 6.0 %collective-permute-done.15.refs_4_ = bf16[32,4,16,128]{3,2,1,0:T(8,128)(2,1)S(1)} collective-permute-done((bf16[32,4,16,128]{3,2,1,0:T(8,128)(2,1)}, bf16[32,4,16,128]{3,2,1,0:T(8,128)(2,1)S(1)}, u32[]{:S(2)}, u32[]{:S(2)}) %collective-permute-start.15) | collective-permute-done | bytes 524320 | tf_op jit(solution)/shard_map/ppermute | solution.py:437
  82.6 4.7 %shard_map.52.refs_4_ = f32[4096,128]{1,0:T(8,128)S(1)} custom-call(s32[2]{0:T(128)S(1)} %pad_add_fusion.place, bf16[32,4,16,128]{3,2,1,0:T(8,128)(2,1)S(1)} %collective-permute-done.refs_0_, bf16[32,4,16,128]{3,2,1,0:T(8,128)(2,1)S(1)} %collective-permute-done.13.refs_1_, ...), custom_call_target="tpu_custom_call", output_to_operand_aliasing={{}: (6, {})} | custom-call | flops 1000 | tf_op jit(solution)/shard_map/pallas_call | solution.py:392
  87.3 0.0 collective-permute-done.11.refs_3_
  87.3 0.0 collective-permute-done.10.refs_1_
  87.3 3.6 %shard_map.53.refs_4_ = f32[4096,128]{1,0:T(8,128)S(1)} custom-call(s32[2]{0:T(128)S(1)} %pad_add_fusion.place, bf16[32,4,16,128]{3,2,1,0:T(8,128)(2,1)S(1)} %broadcast_select_fusion.refs_0_, bf16[32,4,16,128]{3,2,1,0:T(8,128)(2,1)S(1)} %collective-permute-done.10.refs_1_, ...), custom_call_target="tpu_custom_call", output_to_operand_aliasing={{}: (5, {})} | custom-call | flops 1000 | tf_op jit(solution)/shard_map/pallas_call | solution.py:392
  90.9 0.0 collective-permute-done.7.refs_3_
  90.9 6.2 %collective-permute-done.8.refs_2_ = bf16[32,4,16,128]{3,2,1,0:T(8,128)(2,1)S(1)} collective-permute-done((bf16[32,4,16,128]{3,2,1,0:T(8,128)(2,1)S(1)}, bf16[32,4,16,128]{3,2,1,0:T(8,128)(2,1)S(1)}, u32[]{:S(2)}, u32[]{:S(2)}) %collective-permute-start.8) | collective-permute-done | bytes 524320 | tf_op jit(solution)/shard_map/ppermute | solution.py:421
  97.1 0.0 collective-permute-start.16
  97.1 1.9 %collective-permute-done.16.refs_1_ = bf16[32,4,16,128]{3,2,1,0:T(8,128)(2,1)S(1)} collective-permute-done((bf16[32,4,16,128]{3,2,1,0:T(8,128)(2,1)S(1)}, bf16[32,4,16,128]{3,2,1,0:T(8,128)(2,1)S(1)}, u32[]{:S(2)}, u32[]{:S(2)}) %collective-permute-start.16) | collective-permute-done | bytes 524320 | tf_op jit(solution)/shard_map/ppermute | solution.py:441
  99.0 5.2 %shard_map.54 = f32[2,8,4,8,8,128]{5,4,3,2,1,0:T(8,128)} custom-call(s32[2]{0:T(128)S(1)} %pad_add_fusion.place, bf16[32,4,16,128]{3,2,1,0:T(8,128)(2,1)S(1)} %constant_dynamic-update-slice_fusion.refs_0_, bf16[32,4,16,128]{3,2,1,0:T(8,128)(2,1)S(1)} %collective-permute-done.16.refs_1_, bf16[32,4,16,128]{3,2,1,0:T(8,128)(2,1)S(1)} %collective-permute-done.8.refs_2_, ...), custom_call_target="tpu_custom_call" | custom-call | flops 1000 | tf_op jit(solution)/shard_map/pallas_call | solution.py:392
  (2 shorter events, 0.1 us)
Async XLA Ops:
  1.9 32.7 %collective-permute-start.2 = (bf16[8,8,64,128]{3,2,1,0:T(8,128)(2,1)S(1)}, bf16[8,8,64,128]{3,2,1,0:T(8,128)(2,1)S(1)}, u32[]{:S(2)}, u32[]{:S(2)}) collective-permute-start(bf16[8,8,64,128]{3,2,1,0:T(8,128)(2,1)S(1)} %shard_map.46), channel_id=1, source_target_pairs={{0,1},{1,0},{2,3},{3,2},{4,5},{5,4},{6,7},{7,6},{8,9},{9,8},{10,11... | collective-permute-start | bytes 3145736 | tf_op jit(solution)/shard_map/ppermute | solution.py:453
  18.3 16.3 %collective-permute-start.1 = (bf16[32,4,16,128]{3,2,1,0:T(8,128)(2,1)S(1)}, bf16[32,4,16,128]{3,2,1,0:T(8,128)(2,1)S(1)}, u32[]{:S(2)}, u32[]{:S(2)}) collective-permute-start(bf16[32,4,16,128]{3,2,1,0:T(8,128)(2,1)S(1)} %get-tuple-element.37.refs_0_), channel_id=1, source_target_pairs={{0,4},{2,6},{4,8},{6,10},{8,12},{10,14},{12,16},{14,18},{16,20},{1... | collective-permute-start | bytes 1572872 | tf_op jit(solution)/shard_map/ppermute | solution.py:421
  19.6 22.4 %collective-permute-start = (bf16[32,4,16,128]{3,2,1,0:T(8,128)(2,1)S(1)}, bf16[32,4,16,128]{3,2,1,0:T(8,128)(2,1)S(1)}, u32[]{:S(2)}, u32[]{:S(2)}) collective-permute-start(bf16[32,4,16,128]{3,2,1,0:T(8,128)(2,1)S(1)} %get-tuple-element.36), channel_id=1, source_target_pairs={{0,1},{1,0},{2,3},{3,2},{4,5},{5,4},{6,7},{7,6},{8,9},{9,8},{10,11... | collective-permute-start | bytes 1572872 | tf_op jit(solution)/shard_map/ppermute | solution.py:458
  19.8 27.2 %collective-permute-start.5 = (bf16[32,4,16,128]{3,2,1,0:T(8,128)(2,1)S(1)}, bf16[32,4,16,128]{3,2,1,0:T(8,128)(2,1)S(1)}, u32[]{:S(2)}, u32[]{:S(2)}) collective-permute-start(bf16[32,4,16,128]{3,2,1,0:T(8,128)(2,1)S(1)} %get-tuple-element.37.refs_0_), channel_id=1, source_target_pairs={{0,2},{2,8},{4,6},{6,12},{8,10},{10,16},{12,14},{14,20},{16,18},{1... | collective-permute-start | bytes 1572872 | tf_op jit(solution)/shard_map/ppermute | solution.py:426
  41.3 0.7 copy-start
  42.0 5.0 %collective-permute-start.4 = (bf16[32,4,16,128]{3,2,1,0:T(8,128)(2,1)S(1)}, bf16[32,4,16,128]{3,2,1,0:T(8,128)(2,1)S(1)}, u32[]{:S(2)}, u32[]{:S(2)}) collective-permute-start(bf16[32,4,16,128]{3,2,1,0:T(8,128)(2,1)S(1)} %collective-permute-done.1.refs_2_), channel_id=1, source_target_pairs={{0,2},{2,0},{4,6},{6,4},{8,10},{10,8},{12,14},{14,12},{16,18},{18,... | collective-permute-start | bytes 1572872 | tf_op jit(solution)/shard_map/ppermute | solution.py:441
  44.3 13.6 %collective-permute-start.3 = (bf16[32,4,16,128]{3,2,1,0:T(8,128)(2,1)}, bf16[32,4,16,128]{3,2,1,0:T(8,128)(2,1)}, u32[]{:S(2)}, u32[]{:S(2)}) collective-permute-start(bf16[32,4,16,128]{3,2,1,0:T(8,128)(2,1)} %get-tuple-element.45), channel_id=1, source_target_pairs={{0,1},{2,3},{4,5},{6,7},{8,9},{10,11},{12,13},{14,15},{16,17},{18,... | collective-permute-start | bytes 1572872 | tf_op jit(solution)/shard_map/ppermute | solution.py:473
  47.0 16.0 %collective-permute-start.12 = (bf16[32,4,16,128]{3,2,1,0:T(8,128)(2,1)S(1)}, bf16[32,4,16,128]{3,2,1,0:T(8,128)(2,1)}, u32[]{:S(2)}, u32[]{:S(2)}) collective-permute-start(bf16[32,4,16,128]{3,2,1,0:T(8,128)(2,1)S(1)} %collective-permute-done.refs_0_), channel_id=1, source_target_pairs={{0,4},{2,6},{4,8},{6,10},{8,12},{10,14},{12,16},{14,18},{16,20},{1... | collective-permute-start | bytes 1572872 | tf_op jit(solution)/shard_map/ppermute | solution.py:421
  47.0 17.3 %copy-start.1 = (bf16[32,2,16,128]{3,2,1,0:T(8,128)(2,1)S(1)}, bf16[32,2,16,128]{3,2,1,0:T(8,128)(2,1)}, u32[]{:S(2)}) copy-start(bf16[32,2,16,128]{3,2,1,0:T(8,128)(2,1)} %copy-done) | copy-start | bytes 786436
  57.9 15.9 %collective-permute-start.9 = (bf16[32,4,16,128]{3,2,1,0:T(8,128)(2,1)S(1)}, bf16[32,4,16,128]{3,2,1,0:T(8,128)(2,1)S(1)}, u32[]{:S(2)}, u32[]{:S(2)}) collective-permute-start(bf16[32,4,16,128]{3,2,1,0:T(8,128)(2,1)S(1)} %broadcast_select_fusion.refs_0_), channel_id=1, source_target_pairs={{0,4},{2,6},{4,8},{6,10},{8,12},{10,14},{12,16},{14,18},{16,20},{1... | collective-permute-start | bytes 1572872 | tf_op jit(solution)/shard_map/ppermute | solution.py:421
  58.0 18.3 %collective-permute-start.14 = (bf16[32,4,16,128]{3,2,1,0:T(8,128)(2,1)S(1)}, bf16[32,4,16,128]{3,2,1,0:T(8,128)(2,1)S(1)}, u32[]{:S(2)}, u32[]{:S(2)}) collective-permute-start(bf16[32,4,16,128]{3,2,1,0:T(8,128)(2,1)S(1)} %collective-permute-done.refs_0_), channel_id=1, source_target_pairs={{0,2},{2,8},{4,6},{8,10},{10,16},{12,14},{16,18},{18,24},{20,22},{... | collective-permute-start | bytes 1572872 | tf_op jit(solution)/shard_map/ppermute | solution.py:433
  63.1 13.3 %collective-permute-start.13 = (bf16[32,4,16,128]{3,2,1,0:T(8,128)(2,1)}, bf16[32,4,16,128]{3,2,1,0:T(8,128)(2,1)S(1)}, u32[]{:S(2)}, u32[]{:S(2)}) collective-permute-start(bf16[32,4,16,128]{3,2,1,0:T(8,128)(2,1)} %collective-permute-done.12.refs_2_), channel_id=1, source_target_pairs={{0,2},{2,0},{4,6},{6,4},{8,10},{10,8},{12,14},{14,12},{16,18},{18,... | collective-permute-start | bytes 1572872 | tf_op jit(solution)/shard_map/ppermute | solution.py:441
  64.4 7.9 %collective-permute-start.6 = (bf16[32,2,16,128]{3,2,1,0:T(8,128)(2,1)S(1)}, bf16[32,2,16,128]{3,2,1,0:T(8,128)(2,1)S(1)}, u32[]{:S(2)}, u32[]{:S(2)}) collective-permute-start(bf16[32,2,16,128]{3,2,1,0:T(8,128)(2,1)S(1)} %copy-done.1), channel_id=1, source_target_pairs={{0,1},{1,0},{2,3},{3,2},{4,5},{5,4},{6,7},{7,6},{8,9},{9,8},{10,11... | collective-permute-start | bytes 786440 | tf_op jit(solution)/shard_map/ppermute | solution.py:478
  64.4 22.9 %collective-permute-start.11 = (bf16[32,4,16,128]{3,2,1,0:T(8,128)(2,1)S(1)}, bf16[32,4,16,128]{3,2,1,0:T(8,128)(2,1)S(1)}, u32[]{:S(2)}, u32[]{:S(2)}) collective-permute-start(bf16[32,4,16,128]{3,2,1,0:T(8,128)(2,1)S(1)} %broadcast_select_fusion.refs_0_), channel_id=1, source_target_pairs={{0,2},{2,8},{4,6},{6,12},{8,10},{10,16},{12,14},{14,20},{16,18},{1... | collective-permute-start | bytes 1572872 | tf_op jit(solution)/shard_map/ppermute | solution.py:426
  72.3 10.3 %collective-permute-start.15 = (bf16[32,4,16,128]{3,2,1,0:T(8,128)(2,1)}, bf16[32,4,16,128]{3,2,1,0:T(8,128)(2,1)S(1)}, u32[]{:S(2)}, u32[]{:S(2)}) collective-permute-start(bf16[32,4,16,128]{3,2,1,0:T(8,128)(2,1)} %collective-permute-done.12.refs_2_), channel_id=1, source_target_pairs={{2,4},{10,12},{18,20},{26,28},{3,5},{11,13},{19,21},{27,29}} | collective-permute-start | bytes 1572872 | tf_op jit(solution)/shard_map/ppermute | solution.py:437
  73.9 13.4 %collective-permute-start.10 = (bf16[32,4,16,128]{3,2,1,0:T(8,128)(2,1)S(1)}, bf16[32,4,16,128]{3,2,1,0:T(8,128)(2,1)S(1)}, u32[]{:S(2)}, u32[]{:S(2)}) collective-permute-start(bf16[32,4,16,128]{3,2,1,0:T(8,128)(2,1)S(1)} %collective-permute-done.9.refs_2_), channel_id=1, source_target_pairs={{0,2},{2,0},{4,6},{6,4},{8,10},{10,8},{12,14},{14,12},{16,18},{18,... | collective-permute-start | bytes 1572872 | tf_op jit(solution)/shard_map/ppermute | solution.py:441
  76.3 14.6 %collective-permute-start.7 = (bf16[32,4,16,128]{3,2,1,0:T(8,128)(2,1)S(1)}, bf16[32,4,16,128]{3,2,1,0:T(8,128)(2,1)S(1)}, u32[]{:S(2)}, u32[]{:S(2)}) collective-permute-start(bf16[32,4,16,128]{3,2,1,0:T(8,128)(2,1)S(1)} %constant_dynamic-update-slice_fusion.refs_0_), channel_id=1, source_target_pairs={{0,2},{2,8},{4,6},{6,12},{8,10},{10,16},{12,14},{14,20},{16,18},{1... | collective-permute-start | bytes 1572872 | tf_op jit(solution)/shard_map/ppermute | solution.py:426
  76.3 20.8 %collective-permute-start.8 = (bf16[32,4,16,128]{3,2,1,0:T(8,128)(2,1)S(1)}, bf16[32,4,16,128]{3,2,1,0:T(8,128)(2,1)S(1)}, u32[]{:S(2)}, u32[]{:S(2)}) collective-permute-start(bf16[32,4,16,128]{3,2,1,0:T(8,128)(2,1)S(1)} %constant_dynamic-update-slice_fusion.refs_0_), channel_id=1, source_target_pairs={{0,4},{2,6},{4,8},{6,10},{8,12},{10,14},{12,16},{14,18},{16,20},{1... | collective-permute-start | bytes 1572872 | tf_op jit(solution)/shard_map/ppermute | solution.py:421
  97.1 1.9 %collective-permute-start.16 = (bf16[32,4,16,128]{3,2,1,0:T(8,128)(2,1)S(1)}, bf16[32,4,16,128]{3,2,1,0:T(8,128)(2,1)S(1)}, u32[]{:S(2)}, u32[]{:S(2)}) collective-permute-start(bf16[32,4,16,128]{3,2,1,0:T(8,128)(2,1)S(1)} %collective-permute-done.8.refs_2_), channel_id=1, source_target_pairs={{0,2},{2,0},{4,6},{6,4},{8,10},{10,8},{12,14},{14,12},{16,18},{18,... | collective-permute-start | bytes 1572872 | tf_op jit(solution)/shard_map/ppermute | solution.py:441

commit v23 on v21

--- a/solution.py
+++ b/solution.py
@@ -123,7 +123,7 @@
         out_shape=[
             jax.ShapeDtypeStruct((signals, frames, ROWS, LANES), BF16),
             jax.ShapeDtypeStruct((signals, edge_frames, ROWS, LANES), BF16),
-            jax.ShapeDtypeStruct((TAPS * ROWS, LANES), F32),
+            jax.ShapeDtypeStruct(((TAPS + 1) * ROWS, LANES), F32),
             jax.ShapeDtypeStruct((ROWS, 3 * ROWS), BF16),
             jax.ShapeDtypeStruct((2, 2 * K2, 2 * LANES), BF16),
             jax.ShapeDtypeStruct((H, 2 * LANES), F32),
@@ -270,8 +270,8 @@
             scratch_shapes=[
                 pltpu.VMEM((MEMBERS, TAPS + out_frames, ROWS, LANES), F32),
                 pltpu.VMEM((MEMBERS, out_frames, ROWS, LANES), F32),
-                pltpu.VMEM((MEMBERS, out_frames * (ROWS + PAD), LANES), F32),
-                pltpu.VMEM((K2 * (tiles * TILE + PAD), LANES), F32),
+                pltpu.VMEM((MEMBERS, (out_frames + 1) * (ROWS + PAD), LANES), F32),
+                pltpu.VMEM(((K2 + 1) * (tiles * TILE + PAD), LANES), F32),
             ],
         ),
         out_shape=[jax.ShapeDtypeStruct(shape, BF16) for shape in shapes],
@@ -365,7 +365,7 @@
 
 def correlate(arrays, pieces, per_group, place, scale, before, last, wait=(), cost=10**3):
     signals = TILE // 2
-    rows = per_group // 2 * H * SUB
+    rows = per_group // 2 * H * SUB + SUB
     place = after(place, *wait)
     shape = (2, signals, VISITS, per_group // 4, SUB, LANES) if last else (rows, LANES)
     operands = list(arrays) + ([] if before is None else [before])

time: 104 us -> 104 us (level)
  transfers between devices with their start and end apart: 17 -> 17, of which waited for: 6 -> 6; matrix products, arithmetic and copies ran while one was open for 0% -> 0% of each run, Pallas kernels for 40% -> 39%
where the time goes in v23:
time: 104 us; the launch traced here: 103 us
  Pallas kernels  49.1 us (47%)
  waiting for transfers between devices  26.7 us (26%)
  starting transfers between devices  25.9 us (25%)
    pallas_call x3, Pallas kernels, spectra(): pl.pallas_call(functools.partial(spectra_kernel, groups, tuple((part[1:]...  30.1 us
    pallas_call x4, Pallas kernels, correlate(): pl.pallas_call(functools.partial(correlate_kernel, pieces, per_group, sca...  15.7 us
    ppermute x1, waiting for transfers between devices, relayed(): lax.ppermute(two, 'stn', [(i, i + 1) for i in range(lax.axis_size('stn'))...  8.02 us
    ppermute x1, waiting for transfers between devices, paired(): got_b = lax.ppermute(away_b, 'tm', [(0, 1)])  7.98 us
    ppermute x4, starting transfers between devices, exchanged(): lax.ppermute(block, 'stn', [(i, i ^ 1) for i in range(lax.axis_size('stn'...  5.08 us
    ppermute x3, starting transfers between devices, farther(): lax.ppermute(block, 'stn', [(i, (i + 1 if i % 2 == 0 else i + 3) % size)...  4.91 us
    ppermute x4, waiting for transfers between devices, shifted(): lax.ppermute(block, axis, [(i, (i + distance) % size) for i in range(size)])  4.41 us
    ppermute x1, waiting for transfers between devices, paired(): got_c = lax.ppermute(away_c, 'tm', swap)  4.36 us
  transfers between devices with their start and end apart: 17, of which 6 were waited for; matrix products, arithmetic and copies ran while one was open for 0% of the time, Pallas kernels for 39%

profile of v23, /device:TPU:1, one launch (start us, length us, event | category | flops | bytes accessed | tf_op | source)
XLA Modules:
  0.0 102.8 jit_solution(2158704634509089451)
XLA Ops:
  0.0 0.1 pad_add_fusion.place
  0.1 3.3 %shard_map.46 = (bf16[8,32,64,128]{3,2,1,0:T(8,128)(2,1)S(1)}, bf16[8,8,64,128]{3,2,1,0:T(8,128)(2,1)S(1)}, f32[1088,128]{1,0:T(8,128)S(1)}, bf16[64,192]{1,0:T(...) custom-call(s32[2]{0:T(128)S(1)} %pad_add_fusion.place, bf16[8,32,64,128]{3,2,1,0:T(8,128)(2,1)} %bitcast.10, ...), custom_call_target="tpu_custom_call" | custom-call | tf_op jit(solution)/shard_map/pallas_call | solution.py:110
  3.4 2.1 %collective-permute-start.2 = (bf16[8,8,64,128]{3,2,1,0:T(8,128)(2,1)S(1)}, bf16[8,8,64,128]{3,2,1,0:T(8,128)(2,1)S(1)}, u32[]{:S(2)}, u32[]{:S(2)}) collective-permute-start(bf16[8,8,64,128]{3,2,1,0:T(8,128)(2,1)S(1)} %get-tuple-element.40), channel_id=1, source_target_pairs={{0,1},{1,0},{2,3},{3,2},{4,5},{5,4},{6,7},{7,6},{8,9},{9,8},{10,11... | collective-permute-start | bytes 3145736 | tf_op jit(solution)/shard_map/ppermute | solution.py:434
  5.5 11.3 %shard_map.47 = (bf16[32,4,16,128]{3,2,1,0:T(8,128)(2,1)S(1)}, bf16[32,4,16,128]{3,2,1,0:T(8,128)(2,1)S(1)}) custom-call(s32[2]{0:T(128)S(1)} %pad_add_fusion.place, bf16[8,32,64,128]{3,2,1,0:T(8,128)(2,1)S(1)} %get-tuple-element.30.refs_0_.refs_1_, bf16[8,32,64,128]{3,2,1,0:T(8,128)(2,1)S(1)} %get-tuple-element.30.refs_0_.refs_1_, ...), custom_call_target="tpu_custom_call" | custom-call | flops 1000000 | tf_op jit(solution)/shard_map/pallas_call | solution.py:263
  16.8 1.3 %collective-permute-start.1 = (bf16[32,4,16,128]{3,2,1,0:T(8,128)(2,1)S(1)}, bf16[32,4,16,128]{3,2,1,0:T(8,128)(2,1)S(1)}, u32[]{:S(2)}, u32[]{:S(2)}) collective-permute-start(bf16[32,4,16,128]{3,2,1,0:T(8,128)(2,1)S(1)} %get-tuple-element.36.refs_0_), channel_id=1, source_target_pairs={{0,4},{2,6},{4,8},{6,10},{8,12},{10,14},{12,16},{14,18},{16,20},{1... | collective-permute-start | bytes 1572872 | tf_op jit(solution)/shard_map/ppermute | solution.py:402
  18.1 0.2 collective-permute-start
  18.3 2.7 %collective-permute-start.5 = (bf16[32,4,16,128]{3,2,1,0:T(8,128)(2,1)S(1)}, bf16[32,4,16,128]{3,2,1,0:T(8,128)(2,1)S(1)}, u32[]{:S(2)}, u32[]{:S(2)}) collective-permute-start(bf16[32,4,16,128]{3,2,1,0:T(8,128)(2,1)S(1)} %get-tuple-element.36.refs_0_), channel_id=1, source_target_pairs={{0,2},{2,8},{4,6},{6,12},{8,10},{10,16},{12,14},{14,20},{16,18},{1... | collective-permute-start | bytes 1572872 | tf_op jit(solution)/shard_map/ppermute | solution.py:407
  21.1 12.0 %shard_map.48 = (bf16[32,4,16,128]{3,2,1,0:T(8,128)(2,1)S(1)}, bf16[32,4,16,128]{3,2,1,0:T(8,128)(2,1)}) custom-call(s32[2]{0:T(128)S(1)} %pad_add_fusion.place, bf16[8,32,64,128]{3,2,1,0:T(8,128)(2,1)S(1)} %get-tuple-element.30.refs_0_.refs_1_, bf16[8,32,64,128]{3,2,1,0:T(8,128)(2,1)S(1)} %get-tuple-element.30.refs_0_.refs_1_, ...), custom_call_target="tpu_custom_call" | custom-call | flops 1000000 | tf_op jit(solution)/shard_map/pallas_call | solution.py:263
  33.1 0.0 collective-permute-done.1.refs_2_
  33.1 0.0 collective-permute-done.2.refs_2_
  33.1 6.7 %shard_map.49 = (bf16[32,2,16,128]{3,2,1,0:T(8,128)(2,1)S(1)}, bf16[32,2,16,128]{3,2,1,0:T(8,128)(2,1)S(1)}) custom-call(s32[2]{0:T(128)S(1)} %pad_add_fusion.place, bf16[8,32,64,128]{3,2,1,0:T(8,128)(2,1)S(1)} %get-tuple-element.30.refs_0_.refs_1_, bf16[8,32,64,128]{3,2,1,0:T(8,128)(2,1)S(1)} %get-tuple-element.30.refs_0_.refs_1_, ...), custom_call_target="tpu_custom_call" | custom-call | flops 1000000 | tf_op jit(solution)/shard_map/pallas_call | solution.py:263
  39.8 0.0 copy-start
  39.9 0.7 copy-done
  40.5 0.0 collective-permute-done.refs_0_
  40.5 2.3 %collective-permute-start.4 = (bf16[32,4,16,128]{3,2,1,0:T(8,128)(2,1)S(1)}, bf16[32,4,16,128]{3,2,1,0:T(8,128)(2,1)S(1)}, u32[]{:S(2)}, u32[]{:S(2)}) collective-permute-start(bf16[32,4,16,128]{3,2,1,0:T(8,128)(2,1)S(1)} %collective-permute-done.1.refs_2_), channel_id=1, source_target_pairs={{0,2},{2,0},{4,6},{6,4},{8,10},{10,8},{12,14},{14,12},{16,18},{18,... | collective-permute-start | bytes 1572872 | tf_op jit(solution)/shard_map/ppermute | solution.py:422
  42.8 2.7 %collective-permute-start.3 = (bf16[32,4,16,128]{3,2,1,0:T(8,128)(2,1)}, bf16[32,4,16,128]{3,2,1,0:T(8,128)(2,1)}, u32[]{:S(2)}, u32[]{:S(2)}) collective-permute-start(bf16[32,4,16,128]{3,2,1,0:T(8,128)(2,1)} %get-tuple-element.45), channel_id=1, source_target_pairs={{0,1},{2,3},{4,5},{6,7},{8,9},{10,11},{12,13},{14,15},{16,17},{18,... | collective-permute-start | bytes 1572872 | tf_op jit(solution)/shard_map/ppermute | solution.py:453
  45.6 0.7 collective-permute-start.12
  46.2 0.0 copy-start.1
  46.2 0.0 collective-permute-done.5.refs_3_
  46.2 0.0 collective-permute-done.4.refs_1_
  46.2 2.2 %shard_map.50.refs_5_ = f32[4104,128]{1,0:T(8,128)S(1)} custom-call(s32[2]{0:T(128)S(1)} %pad_add_fusion.place, bf16[32,4,16,128]{3,2,1,0:T(8,128)(2,1)S(1)} %get-tuple-element.36.refs_0_, bf16[32,4,16,128]{3,2,1,0:T(8,128)(2,1)S(1)} %collective-permute-done.4.refs_1_, bf16[32,4,16,128]{3,2,1,0:T(8,128)(2,1)S(1)} %collective-permute-done.1.refs_2_, ...), custom_call_target="tpu_custom_call" | custom-call | flops 1000 | tf_op jit(solution)/shard_map/pallas_call | solution.py:373
  48.4 8.0 %collective-permute-done.3 = bf16[32,4,16,128]{3,2,1,0:T(8,128)(2,1)} collective-permute-done((bf16[32,4,16,128]{3,2,1,0:T(8,128)(2,1)}, bf16[32,4,16,128]{3,2,1,0:T(8,128)(2,1)}, u32[]{:S(2)}, u32[]{:S(2)}) %collective-permute-start.3) | collective-permute-done | bytes 524320 | tf_op jit(solution)/shard_map/ppermute | solution.py:453
  56.4 0.1 broadcast_select_fusion.refs_0_
  56.5 0.7 collective-permute-start.9
  57.2 4.1 %collective-permute-start.14 = (bf16[32,4,16,128]{3,2,1,0:T(8,128)(2,1)S(1)}, bf16[32,4,16,128]{3,2,1,0:T(8,128)(2,1)S(1)}, u32[]{:S(2)}, u32[]{:S(2)}) collective-permute-start(bf16[32,4,16,128]{3,2,1,0:T(8,128)(2,1)S(1)} %collective-permute-done.refs_0_), channel_id=1, source_target_pairs={{0,2},{2,8},{4,6},{8,10},{10,16},{12,14},{16,18},{18,24},{20,22},{... | collective-permute-start | bytes 1572872 | tf_op jit(solution)/shard_map/ppermute | solution.py:414
  61.3 0.3 collective-permute-done.12.refs_2_
  61.6 1.3 %collective-permute-start.13 = (bf16[32,4,16,128]{3,2,1,0:T(8,128)(2,1)}, bf16[32,4,16,128]{3,2,1,0:T(8,128)(2,1)S(1)}, u32[]{:S(2)}, u32[]{:S(2)}) collective-permute-start(bf16[32,4,16,128]{3,2,1,0:T(8,128)(2,1)} %collective-permute-done.12.refs_2_), channel_id=1, source_target_pairs={{0,2},{2,0},{4,6},{6,4},{8,10},{10,8},{12,14},{14,12},{16,18},{18,... | collective-permute-start | bytes 1572872 | tf_op jit(solution)/shard_map/ppermute | solution.py:422
  62.9 0.0 copy-done.1
  62.9 1.8 %collective-permute-start.6 = (bf16[32,2,16,128]{3,2,1,0:T(8,128)(2,1)S(1)}, bf16[32,2,16,128]{3,2,1,0:T(8,128)(2,1)S(1)}, u32[]{:S(2)}, u32[]{:S(2)}) collective-permute-start(bf16[32,2,16,128]{3,2,1,0:T(8,128)(2,1)S(1)} %copy-done.1), channel_id=1, source_target_pairs={{0,1},{1,0},{2,3},{3,2},{4,5},{5,4},{6,7},{7,6},{8,9},{9,8},{10,11... | collective-permute-start | bytes 786440 | tf_op jit(solution)/shard_map/ppermute | solution.py:458
  64.8 1.9 %collective-permute-start.11 = (bf16[32,4,16,128]{3,2,1,0:T(8,128)(2,1)S(1)}, bf16[32,4,16,128]{3,2,1,0:T(8,128)(2,1)S(1)}, u32[]{:S(2)}, u32[]{:S(2)}) collective-permute-start(bf16[32,4,16,128]{3,2,1,0:T(8,128)(2,1)S(1)} %broadcast_select_fusion.refs_0_), channel_id=1, source_target_pairs={{0,2},{2,8},{4,6},{6,12},{8,10},{10,16},{12,14},{14,20},{16,18},{1... | collective-permute-start | bytes 1572872 | tf_op jit(solution)/shard_map/ppermute | solution.py:407
  66.7 4.4 %collective-permute-done.6 = bf16[32,2,16,128]{3,2,1,0:T(8,128)(2,1)S(1)} collective-permute-done((bf16[32,2,16,128]{3,2,1,0:T(8,128)(2,1)S(1)}, bf16[32,2,16,128]{3,2,1,0:T(8,128)(2,1)S(1)}, u32[]{:S(2)}, u32[]{:S(2)}) %collective-permute-start.6) | collective-permute-done | bytes 262176 | tf_op jit(solution)/shard_map/ppermute | solution.py:458
  71.1 2.2 %collective-permute-start.15 = (bf16[32,4,16,128]{3,2,1,0:T(8,128)(2,1)}, bf16[32,4,16,128]{3,2,1,0:T(8,128)(2,1)S(1)}, u32[]{:S(2)}, u32[]{:S(2)}) collective-permute-start(bf16[32,4,16,128]{3,2,1,0:T(8,128)(2,1)} %collective-permute-done.12.refs_2_), channel_id=1, source_target_pairs={{2,4},{10,12},{18,20},{26,28},{3,5},{11,13},{19,21},{27,29}} | collective-permute-start | bytes 1572872 | tf_op jit(solution)/shard_map/ppermute | solution.py:418
  73.3 0.0 collective-permute-done.9.refs_2_
  73.4 1.5 %collective-permute-start.10 = (bf16[32,4,16,128]{3,2,1,0:T(8,128)(2,1)S(1)}, bf16[32,4,16,128]{3,2,1,0:T(8,128)(2,1)S(1)}, u32[]{:S(2)}, u32[]{:S(2)}) collective-permute-start(bf16[32,4,16,128]{3,2,1,0:T(8,128)(2,1)S(1)} %collective-permute-done.9.refs_2_), channel_id=1, source_target_pairs={{0,2},{2,0},{4,6},{6,4},{8,10},{10,8},{12,14},{14,12},{16,18},{18,... | collective-permute-start | bytes 1572872 | tf_op jit(solution)/shard_map/ppermute | solution.py:422
  74.9 0.0 collective-permute-done.14.refs_3_
  74.9 0.3 collective-permute-start.7
  75.1 0.0 collective-permute-done.13.refs_1_
  75.1 0.0 collective-permute-start.8
  75.1 8.0 %collective-permute-done.15.refs_4_ = bf16[32,4,16,128]{3,2,1,0:T(8,128)(2,1)S(1)} collective-permute-done((bf16[32,4,16,128]{3,2,1,0:T(8,128)(2,1)}, bf16[32,4,16,128]{3,2,1,0:T(8,128)(2,1)S(1)}, u32[]{:S(2)}, u32[]{:S(2)}) %collective-permute-start.15) | collective-permute-done | bytes 524320 | tf_op jit(solution)/shard_map/ppermute | solution.py:418
  83.2 4.7 %shard_map.51.refs_4_ = f32[4104,128]{1,0:T(8,128)S(1)} custom-call(s32[2]{0:T(128)S(1)} %pad_add_fusion.place, bf16[32,4,16,128]{3,2,1,0:T(8,128)(2,1)S(1)} %collective-permute-done.refs_0_, bf16[32,4,16,128]{3,2,1,0:T(8,128)(2,1)S(1)} %collective-permute-done.13.refs_1_, ...), custom_call_target="tpu_custom_call", output_to_operand_aliasing={{}: (6, {})} | custom-call | flops 1000 | tf_op jit(solution)/shard_map/pallas_call | solution.py:373
  87.8 0.0 collective-permute-done.11.refs_3_
  87.8 0.0 collective-permute-done.10.refs_1_
  87.8 3.6 %shard_map.52.refs_4_ = f32[4104,128]{1,0:T(8,128)S(1)} custom-call(s32[2]{0:T(128)S(1)} %pad_add_fusion.place, bf16[32,4,16,128]{3,2,1,0:T(8,128)(2,1)S(1)} %broadcast_select_fusion.refs_0_, bf16[32,4,16,128]{3,2,1,0:T(8,128)(2,1)S(1)} %collective-permute-done.10.refs_1_, ...), custom_call_target="tpu_custom_call", output_to_operand_aliasing={{}: (5, {})} | custom-call | flops 1000 | tf_op jit(solution)/shard_map/pallas_call | solution.py:373
  91.5 0.0 collective-permute-done.7.refs_3_
  91.5 4.1 %collective-permute-done.8.refs_2_ = bf16[32,4,16,128]{3,2,1,0:T(8,128)(2,1)S(1)} collective-permute-done((bf16[32,4,16,128]{3,2,1,0:T(8,128)(2,1)S(1)}, bf16[32,4,16,128]{3,2,1,0:T(8,128)(2,1)S(1)}, u32[]{:S(2)}, u32[]{:S(2)}) %collective-permute-start.8) | collective-permute-done | bytes 524320 | tf_op jit(solution)/shard_map/ppermute | solution.py:402
  95.6 0.0 collective-permute-start.16
  95.6 1.9 %collective-permute-done.16.refs_1_ = bf16[32,4,16,128]{3,2,1,0:T(8,128)(2,1)S(1)} collective-permute-done((bf16[32,4,16,128]{3,2,1,0:T(8,128)(2,1)S(1)}, bf16[32,4,16,128]{3,2,1,0:T(8,128)(2,1)S(1)}, u32[]{:S(2)}, u32[]{:S(2)}) %collective-permute-start.16) | collective-permute-done | bytes 524320 | tf_op jit(solution)/shard_map/ppermute | solution.py:422
  97.5 5.2 %shard_map.53 = f32[2,8,4,8,8,128]{5,4,3,2,1,0:T(8,128)} custom-call(s32[2]{0:T(128)S(1)} %pad_add_fusion.place, bf16[32,4,16,128]{3,2,1,0:T(8,128)(2,1)S(1)} %constant_dynamic-update-slice_fusion.refs_0_, bf16[32,4,16,128]{3,2,1,0:T(8,128)(2,1)S(1)} %collective-permute-done.16.refs_1_, bf16[32,4,16,128]{3,2,1,0:T(8,128)(2,1)S(1)} %collective-permute-done.8.refs_2_, ...), custom_call_target="tpu_custom_call" | custom-call | flops 1000 | tf_op jit(solution)/shard_map/pallas_call | solution.py:373
  (2 shorter events, 0.1 us)
Async XLA Ops:
  3.4 29.7 %collective-permute-start.2 = (bf16[8,8,64,128]{3,2,1,0:T(8,128)(2,1)S(1)}, bf16[8,8,64,128]{3,2,1,0:T(8,128)(2,1)S(1)}, u32[]{:S(2)}, u32[]{:S(2)}) collective-permute-start(bf16[8,8,64,128]{3,2,1,0:T(8,128)(2,1)S(1)} %get-tuple-element.40), channel_id=1, source_target_pairs={{0,1},{1,0},{2,3},{3,2},{4,5},{5,4},{6,7},{7,6},{8,9},{9,8},{10,11... | collective-permute-start | bytes 3145736 | tf_op jit(solution)/shard_map/ppermute | solution.py:434
  16.8 16.3 %collective-permute-start.1 = (bf16[32,4,16,128]{3,2,1,0:T(8,128)(2,1)S(1)}, bf16[32,4,16,128]{3,2,1,0:T(8,128)(2,1)S(1)}, u32[]{:S(2)}, u32[]{:S(2)}) collective-permute-start(bf16[32,4,16,128]{3,2,1,0:T(8,128)(2,1)S(1)} %get-tuple-element.36.refs_0_), channel_id=1, source_target_pairs={{0,4},{2,6},{4,8},{6,10},{8,12},{10,14},{12,16},{14,18},{16,20},{1... | collective-permute-start | bytes 1572872 | tf_op jit(solution)/shard_map/ppermute | solution.py:402
  18.1 22.4 %collective-permute-start = (bf16[32,4,16,128]{3,2,1,0:T(8,128)(2,1)S(1)}, bf16[32,4,16,128]{3,2,1,0:T(8,128)(2,1)S(1)}, u32[]{:S(2)}, u32[]{:S(2)}) collective-permute-start(bf16[32,4,16,128]{3,2,1,0:T(8,128)(2,1)S(1)} %get-tuple-element.35), channel_id=1, source_target_pairs={{0,1},{1,0},{2,3},{3,2},{4,5},{5,4},{6,7},{7,6},{8,9},{9,8},{10,11... | collective-permute-start | bytes 1572872 | tf_op jit(solution)/shard_map/ppermute | solution.py:438
  18.3 27.9 %collective-permute-start.5 = (bf16[32,4,16,128]{3,2,1,0:T(8,128)(2,1)S(1)}, bf16[32,4,16,128]{3,2,1,0:T(8,128)(2,1)S(1)}, u32[]{:S(2)}, u32[]{:S(2)}) collective-permute-start(bf16[32,4,16,128]{3,2,1,0:T(8,128)(2,1)S(1)} %get-tuple-element.36.refs_0_), channel_id=1, source_target_pairs={{0,2},{2,8},{4,6},{6,12},{8,10},{10,16},{12,14},{14,20},{16,18},{1... | collective-permute-start | bytes 1572872 | tf_op jit(solution)/shard_map/ppermute | solution.py:407
  39.8 0.7 copy-start
  40.5 5.7 %collective-permute-start.4 = (bf16[32,4,16,128]{3,2,1,0:T(8,128)(2,1)S(1)}, bf16[32,4,16,128]{3,2,1,0:T(8,128)(2,1)S(1)}, u32[]{:S(2)}, u32[]{:S(2)}) collective-permute-start(bf16[32,4,16,128]{3,2,1,0:T(8,128)(2,1)S(1)} %collective-permute-done.1.refs_2_), channel_id=1, source_target_pairs={{0,2},{2,0},{4,6},{6,4},{8,10},{10,8},{12,14},{14,12},{16,18},{18,... | collective-permute-start | bytes 1572872 | tf_op jit(solution)/shard_map/ppermute | solution.py:422
  42.8 13.6 %collective-permute-start.3 = (bf16[32,4,16,128]{3,2,1,0:T(8,128)(2,1)}, bf16[32,4,16,128]{3,2,1,0:T(8,128)(2,1)}, u32[]{:S(2)}, u32[]{:S(2)}) collective-permute-start(bf16[32,4,16,128]{3,2,1,0:T(8,128)(2,1)} %get-tuple-element.45), channel_id=1, source_target_pairs={{0,1},{2,3},{4,5},{6,7},{8,9},{10,11},{12,13},{14,15},{16,17},{18,... | collective-permute-start | bytes 1572872 | tf_op jit(solution)/shard_map/ppermute | solution.py:453
  45.6 16.0 %collective-permute-start.12 = (bf16[32,4,16,128]{3,2,1,0:T(8,128)(2,1)S(1)}, bf16[32,4,16,128]{3,2,1,0:T(8,128)(2,1)}, u32[]{:S(2)}, u32[]{:S(2)}) collective-permute-start(bf16[32,4,16,128]{3,2,1,0:T(8,128)(2,1)S(1)} %collective-permute-done.refs_0_), channel_id=1, source_target_pairs={{0,4},{2,6},{4,8},{6,10},{8,12},{10,14},{12,16},{14,18},{16,20},{1... | collective-permute-start | bytes 1572872 | tf_op jit(solution)/shard_map/ppermute | solution.py:402
  46.2 16.7 %copy-start.1 = (bf16[32,2,16,128]{3,2,1,0:T(8,128)(2,1)S(1)}, bf16[32,2,16,128]{3,2,1,0:T(8,128)(2,1)}, u32[]{:S(2)}) copy-start(bf16[32,2,16,128]{3,2,1,0:T(8,128)(2,1)} %copy-done) | copy-start | bytes 786436
  56.5 16.9 %collective-permute-start.9 = (bf16[32,4,16,128]{3,2,1,0:T(8,128)(2,1)S(1)}, bf16[32,4,16,128]{3,2,1,0:T(8,128)(2,1)S(1)}, u32[]{:S(2)}, u32[]{:S(2)}) collective-permute-start(bf16[32,4,16,128]{3,2,1,0:T(8,128)(2,1)S(1)} %broadcast_select_fusion.refs_0_), channel_id=1, source_target_pairs={{0,4},{2,6},{4,8},{6,10},{8,12},{10,14},{12,16},{14,18},{16,20},{1... | collective-permute-start | bytes 1572872 | tf_op jit(solution)/shard_map/ppermute | solution.py:402
  57.2 17.7 %collective-permute-start.14 = (bf16[32,4,16,128]{3,2,1,0:T(8,128)(2,1)S(1)}, bf16[32,4,16,128]{3,2,1,0:T(8,128)(2,1)S(1)}, u32[]{:S(2)}, u32[]{:S(2)}) collective-permute-start(bf16[32,4,16,128]{3,2,1,0:T(8,128)(2,1)S(1)} %collective-permute-done.refs_0_), channel_id=1, source_target_pairs={{0,2},{2,8},{4,6},{8,10},{10,16},{12,14},{16,18},{18,24},{20,22},{... | collective-permute-start | bytes 1572872 | tf_op jit(solution)/shard_map/ppermute | solution.py:414
  61.6 13.5 %collective-permute-start.13 = (bf16[32,4,16,128]{3,2,1,0:T(8,128)(2,1)}, bf16[32,4,16,128]{3,2,1,0:T(8,128)(2,1)S(1)}, u32[]{:S(2)}, u32[]{:S(2)}) collective-permute-start(bf16[32,4,16,128]{3,2,1,0:T(8,128)(2,1)} %collective-permute-done.12.refs_2_), channel_id=1, source_target_pairs={{0,2},{2,0},{4,6},{6,4},{8,10},{10,8},{12,14},{14,12},{16,18},{18,... | collective-permute-start | bytes 1572872 | tf_op jit(solution)/shard_map/ppermute | solution.py:422
  62.9 8.2 %collective-permute-start.6 = (bf16[32,2,16,128]{3,2,1,0:T(8,128)(2,1)S(1)}, bf16[32,2,16,128]{3,2,1,0:T(8,128)(2,1)S(1)}, u32[]{:S(2)}, u32[]{:S(2)}) collective-permute-start(bf16[32,2,16,128]{3,2,1,0:T(8,128)(2,1)S(1)} %copy-done.1), channel_id=1, source_target_pairs={{0,1},{1,0},{2,3},{3,2},{4,5},{5,4},{6,7},{7,6},{8,9},{9,8},{10,11... | collective-permute-start | bytes 786440 | tf_op jit(solution)/shard_map/ppermute | solution.py:458
  64.8 23.0 %collective-permute-start.11 = (bf16[32,4,16,128]{3,2,1,0:T(8,128)(2,1)S(1)}, bf16[32,4,16,128]{3,2,1,0:T(8,128)(2,1)S(1)}, u32[]{:S(2)}, u32[]{:S(2)}) collective-permute-start(bf16[32,4,16,128]{3,2,1,0:T(8,128)(2,1)S(1)} %broadcast_select_fusion.refs_0_), channel_id=1, source_target_pairs={{0,2},{2,8},{4,6},{6,12},{8,10},{10,16},{12,14},{14,20},{16,18},{1... | collective-permute-start | bytes 1572872 | tf_op jit(solution)/shard_map/ppermute | solution.py:407
  71.1 12.1 %collective-permute-start.15 = (bf16[32,4,16,128]{3,2,1,0:T(8,128)(2,1)}, bf16[32,4,16,128]{3,2,1,0:T(8,128)(2,1)S(1)}, u32[]{:S(2)}, u32[]{:S(2)}) collective-permute-start(bf16[32,4,16,128]{3,2,1,0:T(8,128)(2,1)} %collective-permute-done.12.refs_2_), channel_id=1, source_target_pairs={{2,4},{10,12},{18,20},{26,28},{3,5},{11,13},{19,21},{27,29}} | collective-permute-start | bytes 1572872 | tf_op jit(solution)/shard_map/ppermute | solution.py:418
  73.4 14.5 %collective-permute-start.10 = (bf16[32,4,16,128]{3,2,1,0:T(8,128)(2,1)S(1)}, bf16[32,4,16,128]{3,2,1,0:T(8,128)(2,1)S(1)}, u32[]{:S(2)}, u32[]{:S(2)}) collective-permute-start(bf16[32,4,16,128]{3,2,1,0:T(8,128)(2,1)S(1)} %collective-permute-done.9.refs_2_), channel_id=1, source_target_pairs={{0,2},{2,0},{4,6},{6,4},{8,10},{10,8},{12,14},{14,12},{16,18},{18,... | collective-permute-start | bytes 1572872 | tf_op jit(solution)/shard_map/ppermute | solution.py:422
  74.9 16.6 %collective-permute-start.7 = (bf16[32,4,16,128]{3,2,1,0:T(8,128)(2,1)S(1)}, bf16[32,4,16,128]{3,2,1,0:T(8,128)(2,1)S(1)}, u32[]{:S(2)}, u32[]{:S(2)}) collective-permute-start(bf16[32,4,16,128]{3,2,1,0:T(8,128)(2,1)S(1)} %constant_dynamic-update-slice_fusion.refs_0_), channel_id=1, source_target_pairs={{0,2},{2,8},{4,6},{6,12},{8,10},{10,16},{12,14},{14,20},{16,18},{1... | collective-permute-start | bytes 1572872 | tf_op jit(solution)/shard_map/ppermute | solution.py:407
  75.1 20.5 %collective-permute-start.8 = (bf16[32,4,16,128]{3,2,1,0:T(8,128)(2,1)S(1)}, bf16[32,4,16,128]{3,2,1,0:T(8,128)(2,1)S(1)}, u32[]{:S(2)}, u32[]{:S(2)}) collective-permute-start(bf16[32,4,16,128]{3,2,1,0:T(8,128)(2,1)S(1)} %constant_dynamic-update-slice_fusion.refs_0_), channel_id=1, source_target_pairs={{0,4},{2,6},{4,8},{6,10},{8,12},{10,14},{12,16},{14,18},{16,20},{1... | collective-permute-start | bytes 1572872 | tf_op jit(solution)/shard_map/ppermute | solution.py:402
  95.6 1.9 %collective-permute-start.16 = (bf16[32,4,16,128]{3,2,1,0:T(8,128)(2,1)S(1)}, bf16[32,4,16,128]{3,2,1,0:T(8,128)(2,1)S(1)}, u32[]{:S(2)}, u32[]{:S(2)}) collective-permute-start(bf16[32,4,16,128]{3,2,1,0:T(8,128)(2,1)S(1)} %collective-permute-done.8.refs_2_), channel_id=1, source_target_pairs={{0,2},{2,0},{4,6},{6,4},{8,10},{10,8},{12,14},{14,12},{16,18},{18,... | collective-permute-start | bytes 1572872 | tf_op jit(solution)/shard_map/ppermute | solution.py:422

commit v24 on v23

--- a/solution.py
+++ b/solution.py
@@ -408,16 +408,6 @@
     return shifted(block, "stn", 2), rest
 
 
-def evenly(block):
-    size = lax.axis_size("stn")
-    ways = [(i, (i + 1 if i % 2 == 0 else i + 3) % size) for i in range(size) if i % 4 < 3]
-    return shifted(block, "stn", 2), lax.ppermute(block, "stn", ways)
-
-
-def relayed(two):
-    return lax.ppermute(two, "stn", [(i, i + 1) for i in range(lax.axis_size("stn")) if i % 4 == 1])
-
-
 def exchanged(block):
     return lax.ppermute(block, "stn", [(i, i ^ 1) for i in range(lax.axis_size("stn"))])
 
@@ -449,7 +439,7 @@
         edge, fixed, place, 2, sizes, 1, (own_b, two_a),
     )
     got_a, own_c, away_b, away_c, two_a = lax.optimization_barrier((got_a, own_c, away_b, away_c, two_a))
-    two_g, rest_g = evenly(got_a)
+    two_g, rest_g = farther(got_a)
     got_b = lax.ppermute(away_b, "tm", [(0, 1)])
     pair_a = exchanged(two_a)
     first = [(many, [(0, 0, 0)])]
@@ -458,8 +448,8 @@
     got_c = lax.ppermute(away_c, "tm", swap)
     piece_b = jnp.where(me == 0, own_b, got_b)
     two_b, rest_b = farther(piece_b)
-    pair_g, relay_g = exchanged(two_g), relayed(two_g)
-    sums = correlated([got_a, pair_g, two_g, (rest_g, relay_g)], first, sums, False)
+    pair_g = exchanged(two_g)
+    sums = correlated([got_a, pair_g, two_g, rest_g], first, sums, False)
     piece_c = jnp.concatenate([own_c, got_c], axis=1)
     two_c, rest_c = farther(piece_c)
     pair_b = exchanged(two_b)

time: 104 us -> 109 us (1.048)
  waiting for transfers between devices: 26.7 us -> 36.9 us
  starting transfers between devices: 25.9 us -> 22.4 us
  Pallas kernels: 49.1 us -> 48 us
    ppermute x4, waiting for transfers between devices: 4.41 us -> 21.7 us  [shifted(): lax.ppermute(block, axis, [(i, (i + distance) % size) for i in range(size)])]
    ppermute x2 -> x0, waiting for transfers between devices: 8.03 us -> none  [the longest x1 8.02 us: relayed(): lax.ppermute(two, 'stn', [(i, i + 1) for i in range(lax.axis_size('stn'))...]
    ppermute x2 -> x0, starting transfers between devices: 6.36 us -> none  [the longest x1 4.14 us: evenly(): return (shifted(block, 'stn', 2), lax.ppermute(block, 'stn', ways))]
    ppermute x1, starting transfers between devices: 1.84 us -> 3.24 us  [paired(): got_c = lax.ppermute(away_c, 'tm', swap)]
    ppermute x4, starting transfers between devices: 2.63 us -> 3.86 us  [shifted(): lax.ppermute(block, axis, [(i, (i + distance) % size) for i in range(size)])]
    ppermute x3 -> x4, starting transfers between devices: 4.91 us -> 5.29 us  [farther(): lax.ppermute(block, 'stn', [(i, (i + 1 if i % 2 == 0 else i + 3) % size)...]
  transfers between devices with their start and end apart: 17 -> 16, of which waited for: 6 -> 5; matrix products, arithmetic and copies ran while one was open for 0% -> 0% of each run, Pallas kernels for 39% -> 36%
where the time goes in v24:
time: 109 us; the launch traced here: 108 us
  Pallas kernels  48 us (44%)
  waiting for transfers between devices  36.9 us (34%)
  starting transfers between devices  22.4 us (21%)
    pallas_call x3, Pallas kernels, spectra(): pl.pallas_call(functools.partial(spectra_kernel, groups, tuple((part[1:]...  30.1 us
    ppermute x4, waiting for transfers between devices, shifted(): lax.ppermute(block, axis, [(i, (i + distance) % size) for i in range(size)])  21.7 us
    pallas_call x4, Pallas kernels, correlate(): pl.pallas_call(functools.partial(correlate_kernel, pieces, per_group, sca...  14.7 us
    ppermute x1, waiting for transfers between devices, paired(): got_b = lax.ppermute(away_b, 'tm', [(0, 1)])  7.97 us
    ppermute x4, starting transfers between devices, farther(): lax.ppermute(block, 'stn', [(i, (i + 1 if i % 2 == 0 else i + 3) % size)...  5.29 us
    ppermute x1, waiting for transfers between devices, paired(): got_c = lax.ppermute(away_c, 'tm', swap)  5.27 us
    ppermute x4, starting transfers between devices, exchanged(): lax.ppermute(block, 'stn', [(i, i ^ 1) for i in range(lax.axis_size('stn'...  4.91 us
    ppermute x4, starting transfers between devices, shifted(): lax.ppermute(block, axis, [(i, (i + distance) % size) for i in range(size)])  3.86 us
  transfers between devices with their start and end apart: 16, of which 5 were waited for; matrix products, arithmetic and copies ran while one was open for 0% of the time, Pallas kernels for 36%

profile of v24, /device:TPU:1, one launch (start us, length us, event | category | flops | bytes accessed | tf_op | source)
XLA Modules:
  0.0 108.4 jit_solution(9900842626088161583)
XLA Ops:
  0.0 0.1 pad_add_fusion.place
  0.1 3.3 %shard_map.46 = (bf16[8,32,64,128]{3,2,1,0:T(8,128)(2,1)S(1)}, bf16[8,8,64,128]{3,2,1,0:T(8,128)(2,1)S(1)}, f32[1088,128]{1,0:T(8,128)S(1)}, bf16[64,192]{1,0:T(...) custom-call(s32[2]{0:T(128)S(1)} %pad_add_fusion.place, bf16[8,32,64,128]{3,2,1,0:T(8,128)(2,1)} %bitcast.10, ...), custom_call_target="tpu_custom_call" | custom-call | tf_op jit(solution)/shard_map/pallas_call | solution.py:110
  3.4 2.1 %collective-permute-start.2 = (bf16[8,8,64,128]{3,2,1,0:T(8,128)(2,1)S(1)}, bf16[8,8,64,128]{3,2,1,0:T(8,128)(2,1)S(1)}, u32[]{:S(2)}, u32[]{:S(2)}) collective-permute-start(bf16[8,8,64,128]{3,2,1,0:T(8,128)(2,1)S(1)} %get-tuple-element.40), channel_id=1, source_target_pairs={{0,1},{1,0},{2,3},{3,2},{4,5},{5,4},{6,7},{7,6},{8,9},{9,8},{10,11... | collective-permute-start | bytes 3145736 | tf_op jit(solution)/shard_map/ppermute | solution.py:424
  5.5 11.3 %shard_map.47 = (bf16[32,4,16,128]{3,2,1,0:T(8,128)(2,1)S(1)}, bf16[32,4,16,128]{3,2,1,0:T(8,128)(2,1)S(1)}) custom-call(s32[2]{0:T(128)S(1)} %pad_add_fusion.place, bf16[8,32,64,128]{3,2,1,0:T(8,128)(2,1)S(1)} %get-tuple-element.30.refs_0_.refs_1_, bf16[8,32,64,128]{3,2,1,0:T(8,128)(2,1)S(1)} %get-tuple-element.30.refs_0_.refs_1_, ...), custom_call_target="tpu_custom_call" | custom-call | flops 1000000 | tf_op jit(solution)/shard_map/pallas_call | solution.py:263
  16.8 1.3 %collective-permute-start.1 = (bf16[32,4,16,128]{3,2,1,0:T(8,128)(2,1)S(1)}, bf16[32,4,16,128]{3,2,1,0:T(8,128)(2,1)S(1)}, u32[]{:S(2)}, u32[]{:S(2)}) collective-permute-start(bf16[32,4,16,128]{3,2,1,0:T(8,128)(2,1)S(1)} %get-tuple-element.36.refs_0_), channel_id=1, source_target_pairs={{0,4},{2,6},{4,8},{6,10},{8,12},{10,14},{12,16},{14,18},{16,20},{1... | collective-permute-start | bytes 1572872 | tf_op jit(solution)/shard_map/ppermute | solution.py:402
  18.1 0.2 collective-permute-start
  18.3 2.7 %collective-permute-start.5 = (bf16[32,4,16,128]{3,2,1,0:T(8,128)(2,1)S(1)}, bf16[32,4,16,128]{3,2,1,0:T(8,128)(2,1)S(1)}, u32[]{:S(2)}, u32[]{:S(2)}) collective-permute-start(bf16[32,4,16,128]{3,2,1,0:T(8,128)(2,1)S(1)} %get-tuple-element.36.refs_0_), channel_id=1, source_target_pairs={{0,2},{2,8},{4,6},{6,12},{8,10},{10,16},{12,14},{14,20},{16,18},{1... | collective-permute-start | bytes 1572872 | tf_op jit(solution)/shard_map/ppermute | solution.py:407
  21.1 12.0 %shard_map.48 = (bf16[32,4,16,128]{3,2,1,0:T(8,128)(2,1)S(1)}, bf16[32,4,16,128]{3,2,1,0:T(8,128)(2,1)}) custom-call(s32[2]{0:T(128)S(1)} %pad_add_fusion.place, bf16[8,32,64,128]{3,2,1,0:T(8,128)(2,1)S(1)} %get-tuple-element.30.refs_0_.refs_1_, bf16[8,32,64,128]{3,2,1,0:T(8,128)(2,1)S(1)} %get-tuple-element.30.refs_0_.refs_1_, ...), custom_call_target="tpu_custom_call" | custom-call | flops 1000000 | tf_op jit(solution)/shard_map/pallas_call | solution.py:263
  33.1 0.0 collective-permute-done.1.refs_2_
  33.1 0.0 collective-permute-done.2.refs_2_
  33.1 6.7 %shard_map.49 = (bf16[32,2,16,128]{3,2,1,0:T(8,128)(2,1)S(1)}, bf16[32,2,16,128]{3,2,1,0:T(8,128)(2,1)S(1)}) custom-call(s32[2]{0:T(128)S(1)} %pad_add_fusion.place, bf16[8,32,64,128]{3,2,1,0:T(8,128)(2,1)S(1)} %get-tuple-element.30.refs_0_.refs_1_, bf16[8,32,64,128]{3,2,1,0:T(8,128)(2,1)S(1)} %get-tuple-element.30.refs_0_.refs_1_, ...), custom_call_target="tpu_custom_call" | custom-call | flops 1000000 | tf_op jit(solution)/shard_map/pallas_call | solution.py:263
  39.8 0.0 copy-start
  39.9 0.7 copy-done
  40.5 0.0 collective-permute-done.refs_0_
  40.6 2.3 %collective-permute-start.4 = (bf16[32,4,16,128]{3,2,1,0:T(8,128)(2,1)S(1)}, bf16[32,4,16,128]{3,2,1,0:T(8,128)(2,1)S(1)}, u32[]{:S(2)}, u32[]{:S(2)}) collective-permute-start(bf16[32,4,16,128]{3,2,1,0:T(8,128)(2,1)S(1)} %collective-permute-done.1.refs_2_), channel_id=1, source_target_pairs={{0,2},{2,0},{4,6},{6,4},{8,10},{10,8},{12,14},{14,12},{16,18},{18,... | collective-permute-start | bytes 1572872 | tf_op jit(solution)/shard_map/ppermute | solution.py:412
  42.8 2.7 %collective-permute-start.3 = (bf16[32,4,16,128]{3,2,1,0:T(8,128)(2,1)}, bf16[32,4,16,128]{3,2,1,0:T(8,128)(2,1)}, u32[]{:S(2)}, u32[]{:S(2)}) collective-permute-start(bf16[32,4,16,128]{3,2,1,0:T(8,128)(2,1)} %get-tuple-element.45), channel_id=1, source_target_pairs={{0,1},{2,3},{4,5},{6,7},{8,9},{10,11},{12,13},{14,15},{16,17},{18,... | collective-permute-start | bytes 1572872 | tf_op jit(solution)/shard_map/ppermute | solution.py:443
  45.6 0.0 copy-start.1
  45.6 0.7 collective-permute-start.12
  46.2 0.0 collective-permute-done.5.refs_3_
  46.2 0.0 collective-permute-done.4.refs_1_
  46.2 2.2 %shard_map.50.refs_4_ = f32[4104,128]{1,0:T(8,128)S(1)} custom-call(s32[2]{0:T(128)S(1)} %pad_add_fusion.place, bf16[32,4,16,128]{3,2,1,0:T(8,128)(2,1)S(1)} %get-tuple-element.36.refs_0_, bf16[32,4,16,128]{3,2,1,0:T(8,128)(2,1)S(1)} %collective-permute-done.4.refs_1_, bf16[32,4,16,128]{3,2,1,0:T(8,128)(2,1)S(1)} %collective-permute-done.1.refs_2_, ...), custom_call_target="tpu_custom_call" | custom-call | flops 1000 | tf_op jit(solution)/shard_map/pallas_call | solution.py:373
  48.5 8.0 %collective-permute-done.3 = bf16[32,4,16,128]{3,2,1,0:T(8,128)(2,1)} collective-permute-done((bf16[32,4,16,128]{3,2,1,0:T(8,128)(2,1)}, bf16[32,4,16,128]{3,2,1,0:T(8,128)(2,1)}, u32[]{:S(2)}, u32[]{:S(2)}) %collective-permute-start.3) | collective-permute-done | bytes 524320 | tf_op jit(solution)/shard_map/ppermute | solution.py:443
  56.4 0.1 broadcast_select_fusion.refs_0_
  56.5 0.7 collective-permute-start.9
  57.2 2.2 %collective-permute-start.14 = (bf16[32,4,16,128]{3,2,1,0:T(8,128)(2,1)S(1)}, bf16[32,4,16,128]{3,2,1,0:T(8,128)(2,1)S(1)}, u32[]{:S(2)}, u32[]{:S(2)}) collective-permute-start(bf16[32,4,16,128]{3,2,1,0:T(8,128)(2,1)S(1)} %collective-permute-done.refs_0_), channel_id=1, source_target_pairs={{0,2},{2,8},{4,6},{6,12},{8,10},{10,16},{12,14},{14,20},{16,18},{1... | collective-permute-start | bytes 1572872 | tf_op jit(solution)/shard_map/ppermute | solution.py:407
  59.4 0.0 copy-done.1
  59.4 3.2 %collective-permute-start.6 = (bf16[32,2,16,128]{3,2,1,0:T(8,128)(2,1)S(1)}, bf16[32,2,16,128]{3,2,1,0:T(8,128)(2,1)S(1)}, u32[]{:S(2)}, u32[]{:S(2)}) collective-permute-start(bf16[32,2,16,128]{3,2,1,0:T(8,128)(2,1)S(1)} %copy-done.1), channel_id=1, source_target_pairs={{0,1},{1,0},{2,3},{3,2},{4,5},{5,4},{6,7},{7,6},{8,9},{9,8},{10,11... | collective-permute-start | bytes 786440 | tf_op jit(solution)/shard_map/ppermute | solution.py:448
  62.7 0.3 collective-permute-start.11
  63.0 0.0 collective-permute-done.12.refs_2_
  63.1 0.2 collective-permute-start.13
  63.3 5.3 %collective-permute-done.6 = bf16[32,2,16,128]{3,2,1,0:T(8,128)(2,1)S(1)} collective-permute-done((bf16[32,2,16,128]{3,2,1,0:T(8,128)(2,1)S(1)}, bf16[32,2,16,128]{3,2,1,0:T(8,128)(2,1)S(1)}, u32[]{:S(2)}, u32[]{:S(2)}) %collective-permute-start.6) | collective-permute-done | bytes 262176 | tf_op jit(solution)/shard_map/ppermute | solution.py:448
  68.6 3.9 %collective-permute-done.9.refs_2_ = bf16[32,4,16,128]{3,2,1,0:T(8,128)(2,1)S(1)} collective-permute-done((bf16[32,4,16,128]{3,2,1,0:T(8,128)(2,1)S(1)}, bf16[32,4,16,128]{3,2,1,0:T(8,128)(2,1)S(1)}, u32[]{:S(2)}, u32[]{:S(2)}) %collective-permute-start.9) | collective-permute-done | bytes 524320 | tf_op jit(solution)/shard_map/ppermute | solution.py:402
  72.5 2.4 %collective-permute-start.10 = (bf16[32,4,16,128]{3,2,1,0:T(8,128)(2,1)S(1)}, bf16[32,4,16,128]{3,2,1,0:T(8,128)(2,1)S(1)}, u32[]{:S(2)}, u32[]{:S(2)}) collective-permute-start(bf16[32,4,16,128]{3,2,1,0:T(8,128)(2,1)S(1)} %collective-permute-done.9.refs_2_), channel_id=1, source_target_pairs={{0,2},{2,0},{4,6},{6,4},{8,10},{10,8},{12,14},{14,12},{16,18},{18,... | collective-permute-start | bytes 1572872 | tf_op jit(solution)/shard_map/ppermute | solution.py:412
  74.9 0.0 collective-permute-start.7
  74.9 0.0 collective-permute-done.14.refs_3_
  74.9 1.2 %collective-permute-start.8 = (bf16[32,4,16,128]{3,2,1,0:T(8,128)(2,1)S(1)}, bf16[32,4,16,128]{3,2,1,0:T(8,128)(2,1)S(1)}, u32[]{:S(2)}, u32[]{:S(2)}) collective-permute-start(bf16[32,4,16,128]{3,2,1,0:T(8,128)(2,1)S(1)} %constant_dynamic-update-slice_fusion.refs_0_), channel_id=1, source_target_pairs={{0,4},{2,6},{4,8},{6,10},{8,12},{10,14},{12,16},{14,18},{16,20},{1... | collective-permute-start | bytes 1572872 | tf_op jit(solution)/shard_map/ppermute | solution.py:402
  76.1 0.0 collective-permute-done.13.refs_1_
  76.1 3.6 %shard_map.51.refs_4_ = f32[4104,128]{1,0:T(8,128)S(1)} custom-call(s32[2]{0:T(128)S(1)} %pad_add_fusion.place, bf16[32,4,16,128]{3,2,1,0:T(8,128)(2,1)S(1)} %collective-permute-done.refs_0_, bf16[32,4,16,128]{3,2,1,0:T(8,128)(2,1)S(1)} %collective-permute-done.13.refs_1_, ...), custom_call_target="tpu_custom_call", output_to_operand_aliasing={{}: (5, {})} | custom-call | flops 1000 | tf_op jit(solution)/shard_map/pallas_call | solution.py:373
  79.7 0.0 collective-permute-done.11.refs_3_
  79.7 0.0 collective-permute-done.10.refs_1_
  79.8 3.6 %shard_map.52.refs_4_ = f32[4104,128]{1,0:T(8,128)S(1)} custom-call(s32[2]{0:T(128)S(1)} %pad_add_fusion.place, bf16[32,4,16,128]{3,2,1,0:T(8,128)(2,1)S(1)} %broadcast_select_fusion.refs_0_, bf16[32,4,16,128]{3,2,1,0:T(8,128)(2,1)S(1)} %collective-permute-done.10.refs_1_, ...), custom_call_target="tpu_custom_call", output_to_operand_aliasing={{}: (5, {})} | custom-call | flops 1000 | tf_op jit(solution)/shard_map/pallas_call | solution.py:373
  83.4 0.0 collective-permute-done.7.refs_3_
  83.4 17.9 %collective-permute-done.8.refs_2_ = bf16[32,4,16,128]{3,2,1,0:T(8,128)(2,1)S(1)} collective-permute-done((bf16[32,4,16,128]{3,2,1,0:T(8,128)(2,1)S(1)}, bf16[32,4,16,128]{3,2,1,0:T(8,128)(2,1)S(1)}, u32[]{:S(2)}, u32[]{:S(2)}) %collective-permute-start.8) | collective-permute-done | bytes 524320 | tf_op jit(solution)/shard_map/ppermute | solution.py:402
  101.3 0.0 collective-permute-start.15
  101.3 1.9 %collective-permute-done.15.refs_1_ = bf16[32,4,16,128]{3,2,1,0:T(8,128)(2,1)S(1)} collective-permute-done((bf16[32,4,16,128]{3,2,1,0:T(8,128)(2,1)S(1)}, bf16[32,4,16,128]{3,2,1,0:T(8,128)(2,1)S(1)}, u32[]{:S(2)}, u32[]{:S(2)}) %collective-permute-start.15) | collective-permute-done | bytes 524320 | tf_op jit(solution)/shard_map/ppermute | solution.py:412
  103.2 5.2 %shard_map.53 = f32[2,8,4,8,8,128]{5,4,3,2,1,0:T(8,128)} custom-call(s32[2]{0:T(128)S(1)} %pad_add_fusion.place, bf16[32,4,16,128]{3,2,1,0:T(8,128)(2,1)S(1)} %constant_dynamic-update-slice_fusion.refs_0_, bf16[32,4,16,128]{3,2,1,0:T(8,128)(2,1)S(1)} %collective-permute-done.15.refs_1_, bf16[32,4,16,128]{3,2,1,0:T(8,128)(2,1)S(1)} %collective-permute-done.8.refs_2_, ...), custom_call_target="tpu_custom_call" | custom-call | flops 1000 | tf_op jit(solution)/shard_map/pallas_call | solution.py:373
  (2 shorter events, 0.1 us)
Async XLA Ops:
  3.4 29.7 %collective-permute-start.2 = (bf16[8,8,64,128]{3,2,1,0:T(8,128)(2,1)S(1)}, bf16[8,8,64,128]{3,2,1,0:T(8,128)(2,1)S(1)}, u32[]{:S(2)}, u32[]{:S(2)}) collective-permute-start(bf16[8,8,64,128]{3,2,1,0:T(8,128)(2,1)S(1)} %get-tuple-element.40), channel_id=1, source_target_pairs={{0,1},{1,0},{2,3},{3,2},{4,5},{5,4},{6,7},{7,6},{8,9},{9,8},{10,11... | collective-permute-start | bytes 3145736 | tf_op jit(solution)/shard_map/ppermute | solution.py:424
  16.8 16.3 %collective-permute-start.1 = (bf16[32,4,16,128]{3,2,1,0:T(8,128)(2,1)S(1)}, bf16[32,4,16,128]{3,2,1,0:T(8,128)(2,1)S(1)}, u32[]{:S(2)}, u32[]{:S(2)}) collective-permute-start(bf16[32,4,16,128]{3,2,1,0:T(8,128)(2,1)S(1)} %get-tuple-element.36.refs_0_), channel_id=1, source_target_pairs={{0,4},{2,6},{4,8},{6,10},{8,12},{10,14},{12,16},{14,18},{16,20},{1... | collective-permute-start | bytes 1572872 | tf_op jit(solution)/shard_map/ppermute | solution.py:402
  18.1 22.4 %collective-permute-start = (bf16[32,4,16,128]{3,2,1,0:T(8,128)(2,1)S(1)}, bf16[32,4,16,128]{3,2,1,0:T(8,128)(2,1)S(1)}, u32[]{:S(2)}, u32[]{:S(2)}) collective-permute-start(bf16[32,4,16,128]{3,2,1,0:T(8,128)(2,1)S(1)} %get-tuple-element.35), channel_id=1, source_target_pairs={{0,1},{1,0},{2,3},{3,2},{4,5},{5,4},{6,7},{7,6},{8,9},{9,8},{10,11... | collective-permute-start | bytes 1572872 | tf_op jit(solution)/shard_map/ppermute | solution.py:428
  18.3 27.9 %collective-permute-start.5 = (bf16[32,4,16,128]{3,2,1,0:T(8,128)(2,1)S(1)}, bf16[32,4,16,128]{3,2,1,0:T(8,128)(2,1)S(1)}, u32[]{:S(2)}, u32[]{:S(2)}) collective-permute-start(bf16[32,4,16,128]{3,2,1,0:T(8,128)(2,1)S(1)} %get-tuple-element.36.refs_0_), channel_id=1, source_target_pairs={{0,2},{2,8},{4,6},{6,12},{8,10},{10,16},{12,14},{14,20},{16,18},{1... | collective-permute-start | bytes 1572872 | tf_op jit(solution)/shard_map/ppermute | solution.py:407
  39.8 0.7 copy-start
  40.6 5.7 %collective-permute-start.4 = (bf16[32,4,16,128]{3,2,1,0:T(8,128)(2,1)S(1)}, bf16[32,4,16,128]{3,2,1,0:T(8,128)(2,1)S(1)}, u32[]{:S(2)}, u32[]{:S(2)}) collective-permute-start(bf16[32,4,16,128]{3,2,1,0:T(8,128)(2,1)S(1)} %collective-permute-done.1.refs_2_), channel_id=1, source_target_pairs={{0,2},{2,0},{4,6},{6,4},{8,10},{10,8},{12,14},{14,12},{16,18},{18,... | collective-permute-start | bytes 1572872 | tf_op jit(solution)/shard_map/ppermute | solution.py:412
  42.8 13.6 %collective-permute-start.3 = (bf16[32,4,16,128]{3,2,1,0:T(8,128)(2,1)}, bf16[32,4,16,128]{3,2,1,0:T(8,128)(2,1)}, u32[]{:S(2)}, u32[]{:S(2)}) collective-permute-start(bf16[32,4,16,128]{3,2,1,0:T(8,128)(2,1)} %get-tuple-element.45), channel_id=1, source_target_pairs={{0,1},{2,3},{4,5},{6,7},{8,9},{10,11},{12,13},{14,15},{16,17},{18,... | collective-permute-start | bytes 1572872 | tf_op jit(solution)/shard_map/ppermute | solution.py:443
  45.6 13.9 %copy-start.1 = (bf16[32,2,16,128]{3,2,1,0:T(8,128)(2,1)S(1)}, bf16[32,2,16,128]{3,2,1,0:T(8,128)(2,1)}, u32[]{:S(2)}) copy-start(bf16[32,2,16,128]{3,2,1,0:T(8,128)(2,1)} %copy-done) | copy-start | bytes 786436
  45.6 17.5 %collective-permute-start.12 = (bf16[32,4,16,128]{3,2,1,0:T(8,128)(2,1)S(1)}, bf16[32,4,16,128]{3,2,1,0:T(8,128)(2,1)S(1)}, u32[]{:S(2)}, u32[]{:S(2)}) collective-permute-start(bf16[32,4,16,128]{3,2,1,0:T(8,128)(2,1)S(1)} %collective-permute-done.refs_0_), channel_id=1, source_target_pairs={{0,4},{2,6},{4,8},{6,10},{8,12},{10,14},{12,16},{14,18},{16,20},{1... | collective-permute-start | bytes 1572872 | tf_op jit(solution)/shard_map/ppermute | solution.py:402
  56.5 16.0 %collective-permute-start.9 = (bf16[32,4,16,128]{3,2,1,0:T(8,128)(2,1)S(1)}, bf16[32,4,16,128]{3,2,1,0:T(8,128)(2,1)S(1)}, u32[]{:S(2)}, u32[]{:S(2)}) collective-permute-start(bf16[32,4,16,128]{3,2,1,0:T(8,128)(2,1)S(1)} %broadcast_select_fusion.refs_0_), channel_id=1, source_target_pairs={{0,4},{2,6},{4,8},{6,10},{8,12},{10,14},{12,16},{14,18},{16,20},{1... | collective-permute-start | bytes 1572872 | tf_op jit(solution)/shard_map/ppermute | solution.py:402
  57.2 17.7 %collective-permute-start.14 = (bf16[32,4,16,128]{3,2,1,0:T(8,128)(2,1)S(1)}, bf16[32,4,16,128]{3,2,1,0:T(8,128)(2,1)S(1)}, u32[]{:S(2)}, u32[]{:S(2)}) collective-permute-start(bf16[32,4,16,128]{3,2,1,0:T(8,128)(2,1)S(1)} %collective-permute-done.refs_0_), channel_id=1, source_target_pairs={{0,2},{2,8},{4,6},{6,12},{8,10},{10,16},{12,14},{14,20},{16,18},{1... | collective-permute-start | bytes 1572872 | tf_op jit(solution)/shard_map/ppermute | solution.py:407
  59.4 9.1 %collective-permute-start.6 = (bf16[32,2,16,128]{3,2,1,0:T(8,128)(2,1)S(1)}, bf16[32,2,16,128]{3,2,1,0:T(8,128)(2,1)S(1)}, u32[]{:S(2)}, u32[]{:S(2)}) collective-permute-start(bf16[32,2,16,128]{3,2,1,0:T(8,128)(2,1)S(1)} %copy-done.1), channel_id=1, source_target_pairs={{0,1},{1,0},{2,3},{3,2},{4,5},{5,4},{6,7},{7,6},{8,9},{9,8},{10,11... | collective-permute-start | bytes 786440 | tf_op jit(solution)/shard_map/ppermute | solution.py:448
  62.7 17.0 %collective-permute-start.11 = (bf16[32,4,16,128]{3,2,1,0:T(8,128)(2,1)S(1)}, bf16[32,4,16,128]{3,2,1,0:T(8,128)(2,1)S(1)}, u32[]{:S(2)}, u32[]{:S(2)}) collective-permute-start(bf16[32,4,16,128]{3,2,1,0:T(8,128)(2,1)S(1)} %broadcast_select_fusion.refs_0_), channel_id=1, source_target_pairs={{0,2},{2,8},{4,6},{6,12},{8,10},{10,16},{12,14},{14,20},{16,18},{1... | collective-permute-start | bytes 1572872 | tf_op jit(solution)/shard_map/ppermute | solution.py:407
  63.1 13.1 %collective-permute-start.13 = (bf16[32,4,16,128]{3,2,1,0:T(8,128)(2,1)S(1)}, bf16[32,4,16,128]{3,2,1,0:T(8,128)(2,1)S(1)}, u32[]{:S(2)}, u32[]{:S(2)}) collective-permute-start(bf16[32,4,16,128]{3,2,1,0:T(8,128)(2,1)S(1)} %collective-permute-done.12.refs_2_), channel_id=1, source_target_pairs={{0,2},{2,0},{4,6},{6,4},{8,10},{10,8},{12,14},{14,12},{16,18},{18,... | collective-permute-start | bytes 1572872 | tf_op jit(solution)/shard_map/ppermute | solution.py:412
  72.5 7.3 %collective-permute-start.10 = (bf16[32,4,16,128]{3,2,1,0:T(8,128)(2,1)S(1)}, bf16[32,4,16,128]{3,2,1,0:T(8,128)(2,1)S(1)}, u32[]{:S(2)}, u32[]{:S(2)}) collective-permute-start(bf16[32,4,16,128]{3,2,1,0:T(8,128)(2,1)S(1)} %collective-permute-done.9.refs_2_), channel_id=1, source_target_pairs={{0,2},{2,0},{4,6},{6,4},{8,10},{10,8},{12,14},{14,12},{16,18},{18,... | collective-permute-start | bytes 1572872 | tf_op jit(solution)/shard_map/ppermute | solution.py:412
  74.9 8.5 %collective-permute-start.7 = (bf16[32,4,16,128]{3,2,1,0:T(8,128)(2,1)S(1)}, bf16[32,4,16,128]{3,2,1,0:T(8,128)(2,1)S(1)}, u32[]{:S(2)}, u32[]{:S(2)}) collective-permute-start(bf16[32,4,16,128]{3,2,1,0:T(8,128)(2,1)S(1)} %constant_dynamic-update-slice_fusion.refs_0_), channel_id=1, source_target_pairs={{0,2},{2,8},{4,6},{6,12},{8,10},{10,16},{12,14},{14,20},{16,18},{1... | collective-permute-start | bytes 1572872 | tf_op jit(solution)/shard_map/ppermute | solution.py:407
  74.9 26.4 %collective-permute-start.8 = (bf16[32,4,16,128]{3,2,1,0:T(8,128)(2,1)S(1)}, bf16[32,4,16,128]{3,2,1,0:T(8,128)(2,1)S(1)}, u32[]{:S(2)}, u32[]{:S(2)}) collective-permute-start(bf16[32,4,16,128]{3,2,1,0:T(8,128)(2,1)S(1)} %constant_dynamic-update-slice_fusion.refs_0_), channel_id=1, source_target_pairs={{0,4},{2,6},{4,8},{6,10},{8,12},{10,14},{12,16},{14,18},{16,20},{1... | collective-permute-start | bytes 1572872 | tf_op jit(solution)/shard_map/ppermute | solution.py:402
  101.3 1.9 %collective-permute-start.15 = (bf16[32,4,16,128]{3,2,1,0:T(8,128)(2,1)S(1)}, bf16[32,4,16,128]{3,2,1,0:T(8,128)(2,1)S(1)}, u32[]{:S(2)}, u32[]{:S(2)}) collective-permute-start(bf16[32,4,16,128]{3,2,1,0:T(8,128)(2,1)S(1)} %collective-permute-done.8.refs_2_), channel_id=1, source_target_pairs={{0,2},{2,0},{4,6},{6,4},{8,10},{10,8},{12,14},{14,12},{16,18},{18,... | collective-permute-start | bytes 1572872 | tf_op jit(solution)/shard_map/ppermute | solution.py:412
